TPU v7x, 32 devices: a whole 2x2x4 slice. The times are simulated.
32 devices in a mesh: lat: 4 (over z), lon: 8 (over y, x, core).
Axes of the slice: x: 2, y: 2, z: 4, core: 2. Of those that a mesh axis runs over, the one named last changes fastest.
Arguments:
- tokens: bfloat16 [72, 192, 1024], P('lat', 'lon'), may hold values from -6 to 6
- qkv_weight: bfloat16 [1024, 3072], replicated, may hold values from -1 to 1
- out_weight: bfloat16 [1024, 1024], replicated, may hold values from -0.1875 to 0.1875
- merge_weight: bfloat16 [4096, 2048], P(None, 'lon'), may hold values from -0.09375 to 0.09375
- up_weight: bfloat16 [2048, 8192], P(None, 'lon'), may hold values from -0.125 to 0.125
- down_weight: bfloat16 [8192, 2048], P('lon'), may hold values from -0.0625 to 0.0625
Outputs:
- middle_out: bfloat16 [72, 192, 1024], P('lat', 'lon')
- coarse_out: bfloat16 [36, 96, 2048], P('lat', 'lon')
All inputs are finite; a program needn't handle non-finite values.
Results may differ from a plain program's by a relative error of at most 0.013.
Values may be sent and summed in bfloat16 or wider, within the bound.
No kernel may reach another device: no remote copies, remote signals or barrier semaphores. Data moves between devices by JAX's collectives and lax.ppermute only.
A program may use at most 128 MiB of HBM per device.

v0:
```python
import jax
import jax.numpy as jnp
from jax import lax
from jax.sharding import PartitionSpec as P

HEADS = 16
WLAT = 6
WLON = 12


def extended(value, sides, width, wrap):
    for axis, dim in sides:
        peers, length = (lax.axis_size(axis), value.shape[dim])
        up = [(i, (i + 1) % peers) for i in range(peers if wrap else peers - 1)]
        down = [(j, i) for i, j in up]
        last = lax.slice_in_dim(value, length - width, length, axis=dim)
        first = lax.slice_in_dim(value, 0, width, axis=dim)
        before = lax.ppermute(last, axis, up)
        after = lax.ppermute(first, axis, down)
        value = jnp.concatenate([before, value, after], axis=dim)
    return value


def normalize(values):
    center = values - jnp.mean(values, axis=-1, keepdims=True)
    spread = jnp.mean(center * center, axis=-1, keepdims=True)
    return center * lax.rsqrt(spread + 1e-05)


def to_windows(grid):
    height, breadth, depth = grid.shape
    shaped = grid.reshape(height // WLAT, WLAT, breadth // WLON, WLON, depth)
    return shaped.transpose(0, 2, 1, 3, 4).reshape(-1, WLAT * WLON, depth)


def from_windows(windows, height, breadth):
    depth = windows.shape[-1]
    shaped = windows.reshape(height // WLAT, breadth // WLON, WLAT, WLON, depth)
    return shaped.transpose(0, 2, 1, 3, 4).reshape(height, breadth, depth)


def attend(query, keys, values, key_valid):
    scale = 1.0 / query.shape[-1] ** 0.5
    scores = jnp.einsum("wqhd,wkhd->whqk", query, keys, preferred_element_type=jnp.float32) * scale
    scores = jnp.where(key_valid[:, None, None, :], scores, jnp.float32(-1e30))
    top = jnp.max(scores, axis=-1, keepdims=True)
    raised = jnp.exp(scores - top)
    weights = (raised / jnp.sum(raised, axis=-1, keepdims=True)).astype(jnp.bfloat16)
    summed = jnp.einsum("whqk,wkhd->wqhd", weights, values, preferred_element_type=jnp.float32)
    return summed.astype(jnp.bfloat16)


def extend(field, rim_lat, rim_lon):
    widened = extended(field, (("lon", 1),), rim_lon, True)
    return extended(widened, (("lat", 0),), rim_lat, False)


def per_device(tokens, qkv_weight, out_weight, merge_weight, up_weight, down_weight):
    rows, columns, width = tokens.shape
    rim_lat = WLAT // 2
    rim_lon = WLON // 2
    head_size = width // HEADS
    tall = rows + 2 * rim_lat
    broad = columns + 2 * rim_lon
    normed = normalize(tokens.astype(jnp.float32)).astype(jnp.bfloat16)
    projected = jnp.dot(normed.reshape(-1, width), qkv_weight, preferred_element_type=jnp.float32)
    projected = projected.astype(jnp.bfloat16).reshape(rows, columns, 3 * width)
    query = jnp.pad(projected[:, :, :width], ((rim_lat, rim_lat), (rim_lon, rim_lon), (0, 0)))
    keyval = extend(projected[:, :, width:], rim_lat, rim_lon)
    position = lax.axis_index("lat") * rows - rim_lat + jnp.arange(tall, dtype=jnp.int32)
    row_valid = (position >= 0) & (position < rows * lax.axis_size("lat"))
    flags = to_windows(jnp.broadcast_to(row_valid[:, None, None], (tall, broad, 1)))[..., 0]
    query_windows = to_windows(query)
    count = query_windows.shape[0]
    query_windows = query_windows.reshape(count, WLAT * WLON, HEADS, head_size)
    pair_windows = to_windows(keyval).reshape(count, WLAT * WLON, 2, HEADS, head_size)
    result = attend(query_windows, pair_windows[:, :, 0], pair_windows[:, :, 1], flags)
    attended = from_windows(result.reshape(count, WLAT * WLON, width), tall, broad)
    attended = attended[rim_lat : rim_lat + rows, rim_lon : rim_lon + columns]
    mixed = jnp.dot(attended.reshape(-1, width), out_weight, preferred_element_type=jnp.float32)
    middle_out = (tokens.reshape(-1, width).astype(jnp.float32) + mixed).astype(jnp.bfloat16)
    middle_out = middle_out.reshape(rows, columns, width)
    patches = middle_out.reshape(rows // 2, 2, columns // 2, 2, width).transpose(0, 2, 1, 3, 4)
    merged = normalize(patches.reshape(-1, 4 * width).astype(jnp.float32)).astype(jnp.bfloat16)
    coarse_own = jnp.dot(
        merged,
        lax.all_gather(merge_weight, "lon", axis=1, tiled=True),
        preferred_element_type=jnp.float32,
    ).astype(jnp.bfloat16)
    coarse_band = None
    coarse_band = lax.all_gather(coarse_own, "lon", axis=0, tiled=True)
    coarse_normed = normalize(coarse_band.astype(jnp.float32)).astype(jnp.bfloat16)
    hidden = jax.nn.gelu(
        jnp.dot(coarse_normed, up_weight, preferred_element_type=jnp.float32), approximate=False
    )
    hidden = hidden.astype(jnp.bfloat16)
    summed = lax.psum_scatter(
        jnp.dot(hidden, down_weight, preferred_element_type=jnp.float32).astype(jnp.bfloat16),
        "lon",
        scatter_dimension=0,
        tiled=True,
    ).astype(jnp.float32)
    coarse_out = (coarse_own.astype(jnp.float32) + summed).astype(jnp.bfloat16)
    return (middle_out, coarse_out.reshape(rows // 2, columns // 2, -1))


def solution(mesh):
    return jax.shard_map(
        per_device,
        mesh=mesh,
        in_specs=(P("lat", "lon", None), P(), P(), P(None, "lon"), P(None, "lon"), P("lon", None)),
        out_specs=(P("lat", "lon", None), P("lat", "lon", None)),
        check_vma=False,
    )
```

profile of v0, /device:TPU:4, one launch (start us, length us, event | category | flops | bytes accessed | tf_op | source)
XLA Modules:
  0.0 307.7 jit_solution(10318063664104592539)
XLA Ops:
  7.2 0.0 all-gather.4.cloned.1.call-start
  7.2 0.7 all-gather.4.cloned.1.call-update
  7.9 0.0 all-gather.6.cloned.1.call-start
  8.0 1.4 convert_reduce_fusion.1
  9.4 0.4 multiply_reduce_fusion.2
  9.8 0.3 multiply_convert_fusion.7
  10.1 5.9 %convolution_convert_fusion = bf16[432,3072]{1,0:T(8,128)(2,1)S(1)} fusion(bf16[432,1024]{1,0:T(8,128)(2,1)S(1)} %bitcast.55, bf16[1024,3072]{1,0:T(8,128)(2,1)} %param.7), kind=kOutput, calls=%fused_computation.8 | convolution fusion | flops 2719236096 | bytes 9830400 | tf_op jit(solution)/shard_map/dot_general | solution.py:66
  16.0 0.2 fusion.96
  16.2 0.1 collective-permute-start
  16.2 2.6 collective-permute-start.1
  18.9 0.1 slice.39
  19.0 21.9 %collective-permute-done = bf16[18,6,2048]{2,1,0:T(8,128)(2,1)S(1)} collective-permute-done((bf16[18,6,2048]{2,1,0:T(8,128)(2,1)S(1)}, bf16[18,6,2048]{2,1,0:T(8,128)(2,1)S(1)}, u32[]{:S(2)}, u32[]{:S(2)}) %collective-permute-start) | collective-permute-done | bytes 442400 | tf_op jit(solution)/shard_map/ppermute | solution.py:18
  40.9 1.7 collective-permute-done.1
  42.6 1.1 pad_maximum_fusion.3
  43.7 4.4 %collective-permute-start.2 = (bf16[3,36,2048]{2,1,0:T(8,128)(2,1)}, bf16[3,36,2048]{2,1,0:T(8,128)(2,1)}, u32[]{:S(2)}, u32[]{:S(2)}) collective-permute-start(bf16[3,36,2048]{2,1,0:T(8,128)(2,1)} %get-tuple-element.4), channel_id=1, source_target_pairs={{0,8},{8,16},{16,24},{1,9},{9,17},{17,25},{2,10},{10,18},{18,26},{... | collective-permute-start | bytes 1327112 | tf_op jit(solution)/shard_map/ppermute | solution.py:18
  48.0 1.3 collective-permute-start.3
  49.3 0.1 slice.42
  49.4 0.5 copy.52
  50.0 1.7 pad.4.clone
  51.7 4.1 %reshape.113 = bf16[4,6,3,12,1024]{4,1,0,3,2:T(8,128)(2,1)} reshape(bf16[24,36,1024]{2,0,1:T(8,128)(2,1)} %pad.4.clone) | data formatting | bytes 3538944 | tf_op jit(solution)/shard_map/reshape | solution.py:32
  55.8 4.3 %copy.41 = bf16[4,3,6,12,1024]{4,3,2,1,0:T(8,128)(2,1)} copy(bf16[4,3,6,12,1024]{4,2,0,3,1:T(8,128)(2,1)} %bitcast.48) | data formatting | bytes 3538944 | tf_op jit(solution)/shard_map/transpose | solution.py:33
  60.0 6.2 %reshape_reshape.11 = bf16[12,72,16,64]{3,2,1,0:T(8,128)(2,1)} reshape(bf16[4,3,6,12,1024]{4,3,2,1,0:T(8,128)(2,1)} %copy.41) | data formatting | bytes 3538944 | tf_op jit(solution)/shard_map/reshape;reshape | solution.py:75
  66.3 0.1 transpose.38
  66.3 0.1 transpose.39
  66.5 3.2 %pad_maximum_fusion = bf16[24,36,2048]{2,1,0:T(8,128)(2,1)S(1)} fusion(bf16[3,36,2048]{2,1,0:T(8,128)(2,1)} %collective-permute-done.3, bf16[18,6,2048]{2,1,0:T(8,128)(2,1)} %copy-done.7, bf16[18,24,2048]{2,1,0:T(8,128)(2,1)} %copy-done.2, bf16[18,6,2048]{2,1,0:T(8,128)(2,1)} %copy-done.6, bf16[3,36,2048]{2,1,0:T(8,128)(2,1)} %collective-permute-done.2), kind=kLoop, calls=%fused_computation.9 | loop fusion | flops 17694720 | bytes 7077888 | tf_op jit(solution)/shard_map/concatenate | solution.py:20
  69.6 3.7 %copy.37 = bf16[24,36,2048]{2,0,1:T(8,128)(2,1)} copy(bf16[24,36,2048]{2,1,0:T(8,128)(2,1)S(1)} %pad_maximum_fusion) | data formatting | bytes 7077888 | tf_op jit(solution)/shard_map/concatenate | solution.py:20
  73.3 6.7 %reshape.112 = bf16[4,6,3,12,2048]{4,1,0,3,2:T(8,128)(2,1)} reshape(bf16[24,36,2048]{2,0,1:T(8,128)(2,1)} %copy.37) | data formatting | bytes 7077888 | tf_op jit(solution)/shard_map/reshape | solution.py:32
  80.0 7.3 %copy.38 = bf16[4,3,6,12,2048]{4,3,2,1,0:T(8,128)(2,1)} copy(bf16[4,3,6,12,2048]{4,2,0,3,1:T(8,128)(2,1)} %bitcast.47) | data formatting | bytes 7077888 | tf_op jit(solution)/shard_map/transpose | solution.py:33
  87.4 11.6 %reshape_reshape.10 = bf16[12,72,2,16,64]{4,3,2,1,0:T(8,128)(2,1)} reshape(bf16[4,3,6,12,2048]{4,3,2,1,0:T(8,128)(2,1)} %copy.38) | data formatting | bytes 7077888 | tf_op jit(solution)/shard_map/reshape;reshape | solution.py:76
  99.0 7.9 %fusion.95 = (bf16[12,72,1,16,64]{4,3,2,1,0:T(8,128)(2,1)}, bf16[12,72,1,16,64]{4,3,2,1,0:T(8,128)(2,1)}) fusion(bf16[12,72,2,16,64]{4,3,2,1,0:T(8,128)(2,1)} %reshape_reshape.10), kind=kLoop, calls=%fused_computation.130 | loop fusion | bytes 7077888 | tf_op jit(solution)/shard_map/slice | solution.py:77
  106.9 6.6 %copy.51 = bf16[12,72,1,16,64]{1,4,3,0,2:T(8,128)(2,1)} copy(bf16[12,72,1,16,64]{4,3,2,1,0:T(8,128)(2,1)} %get-tuple-element.3) | data formatting | bytes 3538944
  113.5 6.8 %copy.50 = bf16[12,72,1,16,64]{1,4,3,0,2:T(8,128)(2,1)} copy(bf16[12,72,1,16,64]{4,3,2,1,0:T(8,128)(2,1)} %get-tuple-element.2) | data formatting | bytes 3538944
  120.3 5.0 %fusion.7 = f32[12,16,72,72]{2,3,1,0:T(8,128)S(1)} fusion(bf16[12,72,16,64]{3,2,1,0:T(8,128)(2,1)} %reshape_reshape.11, bf16[12,72,1,16,64]{1,4,3,0,2:T(8,128)(2,1)} %copy.51), kind=kOutput, calls=%fused_computation.14 | convolution fusion | flops 127401984 | bytes 7520256 | tf_op jit(solution)/shard_map/wqhd,wkhd->whqk/dot_general | solution.py:44
  125.3 3.7 %fusion.97 = (f32[12,16,72]{2,1,0:T(8,128)S(1)}, f32[12,16,72,72]{2,3,1,0:T(8,128)S(1)}) fusion(f32[12,16,72,72]{2,3,1,0:T(8,128)S(1)} %fusion.7, pred[12,72]{1,0:T(8,128)(4,1)S(1)} %transpose.39), kind=kOutput, calls=%fused_computation.132 | output fusion | flops 5972039 | bytes 8018784 | tf_op jit(solution)/shard_map/sub | solution.py:47
  129.1 2.8 convert_bitcast_fusion
  131.9 6.4 %copy.45 = bf16[12,72,16,64]{3,2,1,0:T(8,128)(2,1)} copy(bf16[12,72,16,64]{1,3,2,0:T(8,128)(2,1)} %convert_bitcast_fusion) | data formatting | bytes 3538944 | tf_op jit(solution)/shard_map/convert_element_type | solution.py:50
  138.2 6.2 %reshape_reshape.12 = bf16[4,3,6,12,1024]{4,3,2,1,0:T(8,128)(2,1)} reshape(bf16[12,72,16,64]{3,2,1,0:T(8,128)(2,1)} %copy.45) | data formatting | bytes 3538944 | tf_op jit(solution)/shard_map/reshape;reshape | solution.py:38
  144.4 4.1 %copy.46 = bf16[4,6,3,12,1024]{4,1,0,3,2:T(8,128)(2,1)} copy(bf16[4,6,3,12,1024]{4,3,1,2,0:T(8,128)(2,1)} %bitcast.49) | data formatting | bytes 3538944 | tf_op jit(solution)/shard_map/transpose | solution.py:39
  148.5 3.9 %reshape.114 = bf16[24,36,1024]{2,0,1:T(8,128)(2,1)} reshape(bf16[4,6,3,12,1024]{4,1,0,3,2:T(8,128)(2,1)} %copy.46) | data formatting | bytes 3538944 | tf_op jit(solution)/shard_map/reshape | solution.py:39
  152.4 1.7 slice.44
  154.1 0.5 copy.47
  154.6 2.0 fusion.26
  156.6 2.3 reshape.121
  158.9 2.4 copy.60
  161.3 0.5 fusion.94
  161.8 0.1 div.33
  161.9 1.2 multiply_reduce_fusion.1
  163.0 0.1 rsqrt.29
  163.1 3.0 reshape.119
  166.1 0.0 all-gather.4.cloned.1.call-done
  166.1 9.1 %convolution_convert_fusion.2 = bf16[108,2048]{1,0:T(8,128)(2,1)} fusion(bf16[4096,2048]{1,0:T(8,128)(2,1)} %all-gather.4.cloned.1.call-done, f32[108,4096]{1,0:T(8,128)S(1)} %reshape.119, f32[108]{0:T(128)S(1)} %rsqrt.29, f32[108]{0:T(128)S(1)} %div.33), kind=kOutput, calls=%fused_computation.41 | convolution fusion | flops 1813487616 | bytes 18989920 | tf_op jit(solution)/shard_map/dot_general | solution.py:85
  175.3 37.4 %all-gather.6.cloned.1.call-done = bf16[8,108,2048]{2,1,0:T(8,128)(2,1)} async-done(((bf16[1,108,2048]{2,1,0:T(8,128)(2,1)}), bf16[8,108,2048]{2,1,0:T(8,128)(2,1)}) %all-gather.6.cloned.1.call-update) | async-done | bytes 3538960 | tf_op jit(solution)/shard_map/all_gather | solution.py:91
  212.7 2.6 convert_reduce_fusion
  215.3 0.1 reshape.127
  215.4 5.6 %reshape.124 = f32[864,2048]{1,0:T(8,128)} reshape(bf16[8,108,2048]{2,1,0:T(8,128)(2,1)} %all-gather.6.cloned.1.call-done) | data formatting | bytes 10616832 | tf_op jit(solution)/shard_map/convert_element_type | solution.py:92
  220.9 3.8 %multiply_reduce_fusion = f32[864]{0:T(1024)S(1)} fusion(f32[864,2048]{1,0:T(8,128)} %reshape.124, f32[864]{0:T(1024)S(1)} %reshape.127), kind=kLoop, calls=%fused_computation.2 | loop fusion | flops 5307552 | bytes 7084800 | tf_op jit(solution)/shard_map/reduce_sum | solution.py:26
  224.8 20.9 %convolution_convert_fusion.1 = bf16[864,2048]{1,0:T(8,128)(2,1)} fusion(bf16[1024,2048]{1,0:T(8,128)(2,1)} %param.11, bf16[2048,1024]{1,0:T(8,128)(2,1)} %param.10, f32[864,2048]{1,0:T(8,128)} %reshape.124, f32[864]{0:T(1024)S(1)} %add_rsqrt_fusion.2, f32[864]{0:T(1024)S(1)} %reshape.127), kind=kOutput, calls=%fused_computation.37 | convolution fusion | flops 7312343040 | bytes 19012352 | tf_op jit(solution)/shard_map/dot_general | solution.py:98
  245.7 41.7 %fusion = bf16[112,2048]{1,0:T(8,128)(2,1)S(1)} fusion(bf16[864,2048]{1,0:T(8,128)(2,1)} %convolution_convert_fusion.1), kind=kCustom, calls=%all-reduce-scatter | all-reduce-scatter fusion | flops 1835009 | bytes 3998208
  287.5 1.9 collective-permute-start.4
  289.5 0.6 dynamic-slice.4
  290.7 4.0 %collective-permute-done.4 = bf16[28,2048]{1,0:T(8,128)(2,1)S(1)} collective-permute-done((bf16[28,2048]{1,0:T(8,128)(2,1)S(1)}, bf16[28,2048]{1,0:T(8,128)(2,1)S(1)}, u32[]{:S(2)}, u32[]{:S(2)}) %collective-permute-start.4) | collective-permute-done | bytes 114720
  294.7 3.8 %concatenate.8 = bf16[140,2048]{1,0:T(8,128)(2,1)} concatenate(bf16[28,2048]{1,0:T(8,128)(2,1)S(1)} %collective-permute-done.4, bf16[112,2048]{1,0:T(8,128)(2,1)S(1)} %fusion), dimensions={0} | concatenate | bytes 1146880
  298.5 1.2 add_convert_fusion
  299.7 0.9 reshape.117
  (29 shorter events, 0.2 us)
Async XLA Ops:
  7.2 147.4 %copy-start = (bf16[1024,1024]{1,0:T(8,128)(2,1)S(1)}, bf16[1024,1024]{1,0:T(8,128)(2,1)}, u32[]{:S(2)}) copy-start(bf16[1024,1024]{1,0:T(8,128)(2,1)} %param.8) | copy-start | bytes 6291460
  7.2 2.2 copy-start.3
  7.2 158.9 %all-gather.4.cloned.1.call-start = ((), (), s32[]{:S(2)}) async-start(), calls=%async_computation | async-start | bytes 18874368 | tf_op jit(solution)/shard_map/all_gather | solution.py:87
  7.9 204.8 %all-gather.6.cloned.1.call-start = ((), (), s32[]{:S(2)}) async-start(), calls=%async_computation.1 | async-start | bytes 4128768 | tf_op jit(solution)/shard_map/all_gather | solution.py:91
  16.2 24.7 %collective-permute-start = (bf16[18,6,2048]{2,1,0:T(8,128)(2,1)S(1)}, bf16[18,6,2048]{2,1,0:T(8,128)(2,1)S(1)}, u32[]{:S(2)}, u32[]{:S(2)}) collective-permute-start(bf16[18,6,2048]{2,1,0:T(8,128)(2,1)S(1)} %get-tuple-element.6), channel_id=1, source_target_pairs={{0,1},{1,2},{2,3},{3,4},{4,5},{5,6},{6,7},{7,0},{8,9},{9,10},{10,1... | collective-permute-start | bytes 1327112 | tf_op jit(solution)/shard_map/ppermute | solution.py:18
  16.2 26.4 %collective-permute-start.1 = (bf16[18,6,2048]{2,1,0:T(8,128)(2,1)S(1)}, bf16[18,6,2048]{2,1,0:T(8,128)(2,1)S(1)}, u32[]{:S(2)}, u32[]{:S(2)}) collective-permute-start(bf16[18,6,2048]{2,1,0:T(8,128)(2,1)S(1)} %get-tuple-element.7), channel_id=1, source_target_pairs={{1,0},{2,1},{3,2},{4,3},{5,4},{6,5},{7,6},{0,7},{9,8},{10,9},{11,1... | collective-permute-start | bytes 1327112 | tf_op jit(solution)/shard_map/ppermute | solution.py:19
  19.0 31.0 %copy-start.2 = (bf16[18,24,2048]{2,1,0:T(8,128)(2,1)}, bf16[18,24,2048]{2,1,0:T(8,128)(2,1)S(1)}, u32[]{:S(2)}) copy-start(bf16[18,24,2048]{2,1,0:T(8,128)(2,1)S(1)} %slice.39) | copy-start | bytes 5308420
  40.9 8.5 %copy-start.6 = (bf16[18,6,2048]{2,1,0:T(8,128)(2,1)}, bf16[18,6,2048]{2,1,0:T(8,128)(2,1)S(1)}, u32[]{:S(2)}) copy-start(bf16[18,6,2048]{2,1,0:T(8,128)(2,1)S(1)} %collective-permute-done) | copy-start | bytes 1327108
  42.6 6.8 %copy-start.7 = (bf16[18,6,2048]{2,1,0:T(8,128)(2,1)}, bf16[18,6,2048]{2,1,0:T(8,128)(2,1)S(1)}, u32[]{:S(2)}) copy-start(bf16[18,6,2048]{2,1,0:T(8,128)(2,1)S(1)} %collective-permute-done.1) | copy-start | bytes 1327108
  43.7 22.8 %collective-permute-start.2 = (bf16[3,36,2048]{2,1,0:T(8,128)(2,1)}, bf16[3,36,2048]{2,1,0:T(8,128)(2,1)}, u32[]{:S(2)}, u32[]{:S(2)}) collective-permute-start(bf16[3,36,2048]{2,1,0:T(8,128)(2,1)} %get-tuple-element.4), channel_id=1, source_target_pairs={{0,8},{8,16},{16,24},{1,9},{9,17},{17,25},{2,10},{10,18},{18,26},{... | collective-permute-start | bytes 1327112 | tf_op jit(solution)/shard_map/ppermute | solution.py:18
  48.0 18.4 %collective-permute-start.3 = (bf16[3,36,2048]{2,1,0:T(8,128)(2,1)S(1)}, bf16[3,36,2048]{2,1,0:T(8,128)(2,1)}, u32[]{:S(2)}, u32[]{:S(2)}) collective-permute-start(bf16[3,36,2048]{2,1,0:T(8,128)(2,1)S(1)} %get-tuple-element.5), channel_id=1, source_target_pairs={{8,0},{16,8},{24,16},{9,1},{17,9},{25,17},{10,2},{18,10},{26,18},{... | collective-permute-start | bytes 1327112 | tf_op jit(solution)/shard_map/ppermute | solution.py:19
  125.3 3.7 %copy-start.5 = (bf16[12,72,1,16,64]{1,4,3,0,2:T(8,128)(2,1)S(1)}, bf16[12,72,1,16,64]{1,4,3,0,2:T(8,128)(2,1)}, u32[]{:S(2)}) copy-start(bf16[12,72,1,16,64]{1,4,3,0,2:T(8,128)(2,1)} %copy.50) | copy-start | bytes 5308420
  224.8 75.8 %copy-start.1 = (bf16[1024,1024]{1,0:T(8,128)(2,1)S(1)}, bf16[1024,1024]{1,0:T(8,128)(2,1)}, u32[]{:S(2)}) copy-start(bf16[1024,1024]{1,0:T(8,128)(2,1)} %param.8) | copy-start | bytes 6291460
  245.7 43.7 %copy-start.8 = (u32[32]{0:T(128)S(1)}, u32[32]{0:T(128)}, u32[]{:S(2)}) copy-start(u32[32]{0:T(128)} %constant.107) | copy-start | bytes 388
  245.7 52.8 %copy-start.4 = (bf16[108,2048]{1,0:T(8,128)(2,1)S(1)}, bf16[108,2048]{1,0:T(8,128)(2,1)}, u32[]{:S(2)}) copy-start(bf16[108,2048]{1,0:T(8,128)(2,1)} %convolution_convert_fusion.2) | copy-start | bytes 1327108
  287.5 7.2 %collective-permute-start.4 = (bf16[28,2048]{1,0:T(8,128)(2,1)S(1)}, bf16[28,2048]{1,0:T(8,128)(2,1)S(1)}, u32[]{:S(2)}, u32[]{:S(2)}) collective-permute-start(bf16[28,2048]{1,0:T(8,128)(2,1)S(1)} %slice.45), channel_id=1, source_target_pairs={{0,1},{1,2},{2,3},{3,4},{4,5},{5,6},{6,7},{8,9},{9,10},{10,11},{11... | collective-permute-start | bytes 344072
Sparse Core Ops, SparseCore 0:
  9.9 102.8 all-gather.3
  175.4 37.2 all-gather.5
where the time goes:
time: 313 us; the launch traced here: 308 us
  local copies, waits for them, and re-layouts  110 us (35%)
  waiting for transfers between devices  65.7 us (21%)
  matrix products  45.8 us (15%)
  blocking collectives  41.7 us (13%)
  other arithmetic  19.3 us (6%)
  between operations  15.2 us (5%)
  starting transfers between devices  10.3 us (3%)
    unnamed x1, blocking collectives  41.7 us
    all_gather x1, waiting for transfers between devices, per_device(): coarse_band = lax.all_gather(coarse_own, 'lon', axis=0, tiled=True)  37.4 us
    ppermute x2, waiting for transfers between devices, extended(): before = lax.ppermute(last, axis, up)  21.9 us
    dot_general x1, matrix products, per_device(): jnp.dot(hidden, down_weight, preferred_element_type=jnp.float32)  20.9 us
    unnamed x24, local copies, waits for them, and re-layouts  18.4 us
    transpose x4, local copies, waits for them, and re-layouts, to_windows(): return shaped.transpose(0, 2, 1, 3, 4).reshape(-1, WLAT * WLON, depth)  11.8 us
    another operation x1, local copies, waits for them, and re-layouts, per_device(): to_windows(keyval).reshape(count, WLAT * WLON, 2, HEADS, head_size)  11.6 us
    reshape x2, local copies, waits for them, and re-layouts, to_windows(): shaped = grid.reshape(height // WLAT, WLAT, breadth // WLON, WLON, depth)  10.8 us
  transfers between devices with their start and end apart: 7, of which 4 were waited for; matrix products, arithmetic and copies ran while one was open for 41% of the time, Pallas kernels for 0%

commit v1 on v0

v1 whole, which is shorter than its diff:
```python
import functools

import jax
import jax.numpy as jnp
import numpy as np
from jax import lax
from jax.experimental import pallas as pl
from jax.experimental.pallas import tpu as pltpu
from jax.sharding import PartitionSpec as P

HEADS = 16
WLAT = 6
WLON = 12
RIM_LAT = WLAT // 2
RIM_LON = WLON // 2
SIDE = 8
GROUP = 4
F32 = jnp.float32
BF16 = jnp.bfloat16


def up16(n):
    return -(-n // 16) * 16


def params(mib=48, **kw):
    return pltpu.CompilerParams(vmem_limit_bytes=mib * 2**20, **kw)


class Bands:
    def __init__(self, rows, columns):
        assert (rows - WLAT) % WLAT == 0 and (columns - WLON) % WLON == 0
        self.rows, self.columns = rows, columns
        inner = (rows - WLAT) // WLAT
        self.height = [RIM_LAT] + [WLAT] * inner + [RIM_LAT]
        self.count = len(self.height)
        self.first = [sum(self.height[:b]) for b in range(self.count)]
        self.widths = [RIM_LON] + [WLON] * ((columns - WLON) // WLON) + [RIM_LON]
        self.own = [h * columns for h in self.height]
        self.own_padded = [up16(n) for n in self.own]
        self.own_at = [sum(self.own_padded[:b]) for b in range(self.count)]
        self.own_total = sum(self.own_padded)
        edge = RIM_LAT * (columns + 2 * SIDE)
        self.halo = [
            2 * h * SIDE + (edge if b in (0, self.count - 1) else 0)
            for b, h in enumerate(self.height)
        ]
        self.halo_padded = [up16(n) for n in self.halo]
        self.halo_at = [sum(self.halo_padded[:b]) for b in range(self.count)]
        self.halo_total = sum(self.halo_padded)
        self.keys = len(self.widths) * WLAT * WLON

    def source(self, b, i, j):
        columns, h, first = self.columns, self.height[b], self.first[b]
        if 0 <= i < self.rows:
            if 0 <= j < columns:
                return (i - first) * columns + j
            at = self.own_padded[b] + (i - first) * SIDE
            return at + (j + SIDE if j < 0 else h * SIDE + j - columns)
        at = self.own_padded[b] + 2 * h * SIDE
        i = i + RIM_LAT if i < 0 else i - self.rows
        if 0 <= j < columns:
            return at + i * columns + j
        at += RIM_LAT * columns + i * SIDE
        return at + (j + SIDE if j < 0 else RIM_LAT * SIDE + j - columns)

    def key_matrix(self, b):
        g = np.zeros((self.keys, self.own_padded[b] + self.halo_padded[b]), np.float32)
        top = self.first[b] - (RIM_LAT if b == 0 else 0)
        at = 0
        for c in range(len(self.widths)):
            for i in range(WLAT):
                for j in range(WLON):
                    g[at, self.source(b, top + i, c * WLON - RIM_LON + j)] = 1
                    at += 1
        return g.astype(BF16)

    def query_matrix(self, b):
        g = np.zeros((GROUP * self.own[b], self.own_padded[b]), np.float32)
        head = np.zeros((GROUP * self.own[b],), np.int32)
        at = left = 0
        for width in self.widths:
            for k in range(GROUP):
                for i in range(self.height[b]):
                    for j in range(width):
                        g[at, i * self.columns + left + j] = 1
                        head[at] = k
                        at += 1
            left += width
        return g.astype(BF16), head

    def patch_matrix(self):
        cells = self.rows * self.columns // 4
        padded = up16(cells)
        g = np.zeros((4 * padded, self.rows * self.columns), np.float32)
        for r in range(self.rows // 2):
            for c in range(self.columns // 2):
                for k in range(4):
                    to = k * padded + r * (self.columns // 2) + c
                    g[to, (2 * r + k // 2) * self.columns + 2 * c + k % 2] = 1
        return g.astype(BF16)


def normalize(values):
    center = values - jnp.mean(values, axis=-1, keepdims=True)
    spread = jnp.mean(center * center, axis=-1, keepdims=True)
    return center * lax.rsqrt(spread + 1e-05)


def own_kernel(bands, tokens_ref, weight_ref, out_ref, normed_ref):
    @pl.when(pl.program_id(0) == 0)
    def _():
        values = tokens_ref[...].astype(F32)
        normed = normalize(values.reshape(-1, values.shape[-1]))
        pieces = []
        for b in range(bands.count):
            at = bands.first[b] * bands.columns
            pieces.append(normed[at : at + bands.own[b]])
            if bands.own_padded[b] > bands.own[b]:
                pieces.append(jnp.zeros((bands.own_padded[b] - bands.own[b], normed.shape[1]), F32))
        normed_ref[...] = jnp.concatenate(pieces, axis=0).astype(BF16)

    out_ref[...] = jnp.dot(normed_ref[...], weight_ref[...], preferred_element_type=F32).astype(BF16)


def own_projection(bands, tokens, weight):
    rows, columns, width = tokens.shape
    out = weight.shape[1]
    block = 512
    return pl.pallas_call(
        functools.partial(own_kernel, bands),
        grid=(out // block,),
        in_specs=[
            pl.BlockSpec((rows, columns, width), lambda n: (0, 0, 0)),
            pl.BlockSpec((width, block), lambda n: (0, n)),
        ],
        out_specs=pl.BlockSpec((bands.own_total, block), lambda n: (0, n)),
        out_shape=jax.ShapeDtypeStruct((bands.own_total, out), BF16),
        scratch_shapes=[pltpu.VMEM((bands.own_total, width), BF16)],
        compiler_params=params(),
        cost_estimate=pl.CostEstimate(
            flops=2 * bands.own_total * width * out, bytes_accessed=2 * width * out, transcendentals=0
        ),
        name="own_projection",
    )(tokens, weight)


def halo_kernel(bands, *refs):
    *parts, weight_ref, out_ref, normed_ref = refs

    @pl.when(pl.program_id(0) == 0)
    def _():
        west, east, north, south, nw, ne, sw, se = [
            normalize(p[...].astype(F32).reshape(-1, p.shape[-1])) for p in parts
        ]
        pieces = []
        for b in range(bands.count):
            at, size = bands.first[b] * SIDE, bands.height[b] * SIDE
            pieces += [west[at : at + size], east[at : at + size]]
            if b == 0:
                pieces += [north, nw, ne]
            if b == bands.count - 1:
                pieces += [south, sw, se]
            if bands.halo_padded[b] > bands.halo[b]:
                pieces.append(jnp.zeros((bands.halo_padded[b] - bands.halo[b], west.shape[1]), F32))
        normed_ref[...] = jnp.concatenate(pieces, axis=0).astype(BF16)

    out_ref[...] = jnp.dot(normed_ref[...], weight_ref[...], preferred_element_type=F32).astype(BF16)


def halo_projection(bands, parts, weight):
    width, out = weight.shape
    block = 512
    skip = width // block
    return pl.pallas_call(
        functools.partial(halo_kernel, bands),
        grid=((out - width) // block,),
        in_specs=[pl.BlockSpec(p.shape, lambda n: (0, 0, 0)) for p in parts]
        + [pl.BlockSpec((width, block), lambda n: (0, n + skip))],
        out_specs=pl.BlockSpec((bands.halo_total, block), lambda n: (0, n)),
        out_shape=jax.ShapeDtypeStruct((bands.halo_total, out - width), BF16),
        scratch_shapes=[pltpu.VMEM((bands.halo_total, width), BF16)],
        compiler_params=params(),
        cost_estimate=pl.CostEstimate(
            flops=2 * bands.halo_total * width * (out - width),
            bytes_accessed=2 * width * (out - width),
            transcendentals=0,
        ),
        name="halo_projection",
    )(*parts, weight)


def dot(a, b, dims=((1,), (0,))):
    return lax.dot_general(a, b, (dims, ((), ())), preferred_element_type=F32)


def attention_kernel(bands, kinds, tokens_ref, bias_ref, q_ref, k_ref, v_ref, hk_ref, hv_ref, out_w_ref, patch_ref, *rest):
    consts, (middle_ref, merged_ref, attended_ref) = rest[:-3], rest[-3:]
    group = pl.program_id(0)
    width = q_ref.shape[1]
    size = width // GROUP
    window = WLAT * WLON
    for b in range(bands.count):
        key_ref, query_ref, mask_ref, back_ref = consts[4 * kinds[b] : 4 * kinds[b] + 4]
        own = pl.ds(bands.own_at[b], bands.own_padded[b])
        halo = pl.ds(bands.halo_at[b], bands.halo_padded[b])
        keys = dot(key_ref[...], jnp.concatenate([k_ref[own, :], hk_ref[halo, :]], axis=0))
        values = dot(key_ref[...], jnp.concatenate([v_ref[own, :], hv_ref[halo, :]], axis=0))
        mask = mask_ref[...]
        query = dot(query_ref[...], q_ref[own, :]) * mask
        at = 0
        mixed = []
        for c, w in enumerate(bands.widths):
            count = GROUP * bands.height[b] * w
            part = slice(c * window, (c + 1) * window)
            scores = dot(
                (query[at : at + count] * (1.0 / size**0.5)).astype(BF16),
                keys[part].astype(BF16),
                ((1,), (1,)),
            )
            if b == 0:
                scores = scores + bias_ref[0:1, :window]
            if b == bands.count - 1:
                scores = scores + bias_ref[1:2, :window]
            top = jnp.max(scores, axis=-1, keepdims=True)
            raised = jnp.exp(scores - top)
            weights = (raised * (1.0 / jnp.sum(raised, axis=-1, keepdims=True))).astype(BF16)
            mixed.append(dot(weights, values[part].astype(BF16)) * mask[at : at + count])
            at += count
        mixed = jnp.concatenate(mixed, axis=0).astype(BF16)
        attended_ref[group, own, :] = dot(back_ref[...], mixed).astype(BF16)

    @pl.when(group == pl.num_programs(0) - 1)
    def _():
        rows, columns, depth = tokens_ref.shape
        groups = attended_ref.shape[0]
        mixed = sum(
            dot(attended_ref[g], out_w_ref[g * width : (g + 1) * width, :]) for g in range(groups)
        )
        mixed = jnp.concatenate(
            [mixed[at : at + n] for at, n in zip(bands.own_at, bands.own)], axis=0
        )
        middle = tokens_ref[...].astype(F32) + mixed.reshape(rows, columns, depth)
        middle_ref[...] = middle.astype(BF16)
        middle = middle.reshape(rows * columns, depth).astype(BF16)
        cells = rows * columns // 4
        padded = patch_ref.shape[0] // 4
        parts = [dot(patch_ref[k * padded : (k + 1) * padded, :], middle) for k in range(4)]
        total = sum(jnp.sum(p, axis=-1, keepdims=True) for p in parts)
        mean = total * (1.0 / (4 * depth))
        parts = [p - mean for p in parts]
        spread = sum(jnp.sum(p * p, axis=-1, keepdims=True) for p in parts)
        factor = lax.rsqrt(spread * (1.0 / (4 * depth)) + 1e-05)
        for k in range(4):
            merged_ref[:, k * depth : (k + 1) * depth] = (parts[k] * factor).astype(BF16)


def attention(bands, tokens, bias, own, halo, out_weight):
    rows, columns, width = tokens.shape
    groups = HEADS // GROUP
    block = width // groups
    distinct, kinds, consts = [], [], []
    for b in range(bands.count):
        kind = (bands.height[b], b == 0, b == bands.count - 1)
        if kind not in distinct:
            distinct.append(kind)
            query, head = bands.query_matrix(b)
            mask = head[:, None] == (np.arange(block) // (block // GROUP))[None, :]
            consts += [bands.key_matrix(b), query, mask.astype(np.float32), np.ascontiguousarray(query.T)]
        kinds.append(distinct.index(kind))
    patch = bands.patch_matrix()
    padded = patch.shape[0] // 4

    def whole(a):
        return pl.BlockSpec(a.shape, lambda g: (0,) * len(a.shape))

    own_total, halo_total = own.shape[0], halo.shape[0]
    return pl.pallas_call(
        functools.partial(attention_kernel, bands, kinds),
        grid=(groups,),
        in_specs=[
            whole(tokens),
            whole(bias),
            pl.BlockSpec((own_total, block), lambda g: (0, g)),
            pl.BlockSpec((own_total, block), lambda g: (0, groups + g)),
            pl.BlockSpec((own_total, block), lambda g: (0, 2 * groups + g)),
            pl.BlockSpec((halo_total, block), lambda g: (0, g)),
            pl.BlockSpec((halo_total, block), lambda g: (0, groups + g)),
            whole(out_weight),
            whole(patch),
        ]
        + [whole(c) for c in consts],
        out_specs=[whole(tokens), pl.BlockSpec((padded, 4 * width), lambda g: (0, 0))],
        out_shape=[
            jax.ShapeDtypeStruct(tokens.shape, BF16),
            jax.ShapeDtypeStruct((padded, 4 * width), BF16),
        ],
        scratch_shapes=[pltpu.VMEM((groups, own_total, block), BF16)],
        compiler_params=params(),
        cost_estimate=pl.CostEstimate(flops=8 * 10**9, bytes_accessed=10**7, transcendentals=10**6),
        name="attention",
    )(tokens, bias, own, own, own, halo, halo, out_weight, patch, *consts)


def halos(tokens):
    lat, lon = lax.axis_size("lat"), lax.axis_size("lon")
    rows, columns, _ = tokens.shape

    def send(part, south, east):
        pairs = []
        for i in range(lat):
            for j in range(lon):
                if 0 <= i + south < lat:
                    pairs.append((i * lon + j, (i + south) * lon + (j + east) % lon))
        return lax.ppermute(part, ("lat", "lon"), pairs)

    lasts, firsts = slice(rows - RIM_LAT, rows), slice(0, RIM_LAT)
    right, left = slice(columns - SIDE, columns), slice(0, SIDE)
    return [
        send(tokens[:, right], 0, 1),
        send(tokens[:, left], 0, -1),
        send(tokens[lasts], 1, 0),
        send(tokens[firsts], -1, 0),
        send(tokens[lasts, right], 1, 1),
        send(tokens[lasts, left], 1, -1),
        send(tokens[firsts, right], -1, 1),
        send(tokens[firsts, left], -1, -1),
    ]


def key_bias():
    row = jnp.arange(8, dtype=jnp.int32)[:, None]
    key = jnp.arange(128, dtype=jnp.int32)[None, :] // WLON
    north = (row == 0) & (key < RIM_LAT) & (lax.axis_index("lat") == 0)
    south = (row == 1) & (key >= RIM_LAT) & (lax.axis_index("lat") == lax.axis_size("lat") - 1)
    return jnp.where(north | south, F32(-1e30), F32(0.0))


def ffn_kernel(mine_ref, theirs_ref, up_ref, down_ref, out_mine_ref, out_theirs_ref, normed_ref, hidden_ref):
    count = mine_ref.shape[0]
    for k, ref in enumerate((mine_ref, theirs_ref)):
        normed_ref[k * count : (k + 1) * count, :] = normalize(ref[...].astype(F32)).astype(BF16)
    hidden = hidden_ref.shape[1]
    step = 256
    for at in range(0, hidden, step):
        raw = dot(normed_ref[...], up_ref[:, at : at + step])
        active = 0.5 * raw * (1.0 + lax.erf(raw * np.float32(np.sqrt(0.5))))
        hidden_ref[:, at : at + step] = active.astype(BF16)
    for at in range(0, down_ref.shape[1], step):
        out = dot(hidden_ref[...], down_ref[:, at : at + step]).astype(BF16)
        out_mine_ref[:, at : at + step] = out[:count]
        out_theirs_ref[:, at : at + step] = out[count:]


def feed_forward(mine, theirs, up, down):
    count, width = mine.shape
    hidden = up.shape[1]
    vmem = pl.BlockSpec(memory_space=pltpu.VMEM)
    return pl.pallas_call(
        ffn_kernel,
        in_specs=[vmem] * 4,
        out_specs=[vmem] * 2,
        out_shape=[jax.ShapeDtypeStruct((count, width), BF16)] * 2,
        scratch_shapes=[pltpu.VMEM((2 * count, width), BF16), pltpu.VMEM((2 * count, hidden), BF16)],
        compiler_params=params(24),
        cost_estimate=pl.CostEstimate(
            flops=8 * count * width * hidden, bytes_accessed=4 * width * hidden, transcendentals=2 * count * hidden
        ),
        name="feed_forward",
    )(mine, theirs, up, down)


def core_swap(value):
    size = lax.axis_size("lon")
    return lax.ppermute(value, "lon", [(i, i ^ 1) for i in range(size)])


def chip_swap(value, offset):
    size = lax.axis_size("lon")
    return lax.ppermute(value, "lon", [(i, i ^ (2 * offset)) for i in range(size)])


def per_device(tokens, qkv_weight, out_weight, merge_weight, up_weight, down_weight):
    rows, columns, width = tokens.shape
    bands = Bands(rows, columns)
    cells = rows * columns // 4
    parts = halos(tokens)
    own = own_projection(bands, tokens, qkv_weight)
    halo = halo_projection(bands, parts, qkv_weight)
    middle_out, merged = attention(bands, tokens, key_bias(), own, halo, out_weight)
    coarse = jnp.dot(
        merged,
        lax.all_gather(merge_weight, "lon", axis=1, tiled=True),
        preferred_element_type=jnp.float32,
    ).astype(jnp.bfloat16)
    chips = lax.axis_size("lon") // 2
    arrived = [coarse] + [chip_swap(coarse, m) for m in range(1, chips)]
    total = coarse.astype(F32)
    for m in range(chips):
        mine, theirs = feed_forward(arrived[m], core_swap(arrived[m]), up_weight, down_weight)
        summed = mine.astype(F32) + core_swap(theirs).astype(F32)
        if m:
            summed = chip_swap(summed.astype(BF16), m).astype(F32)
        total = total + summed
    coarse_out = total[:cells].astype(jnp.bfloat16)
    return (middle_out, coarse_out.reshape(rows // 2, columns // 2, -1))


def solution(mesh):
    return jax.shard_map(
        per_device,
        mesh=mesh,
        in_specs=(P("lat", "lon", None), P(), P(), P(None, "lon"), P(None, "lon"), P("lon", None)),
        out_specs=(P("lat", "lon", None), P("lat", "lon", None)),
        check_vma=False,
    )
```

time: 313 us -> 182 us (0.58)
  the two profiles are of different devices: /device:TPU:4 before, /device:TPU:0 now
where the time goes in v1:
time: 182 us
  waiting for transfers between devices  75.5 us (41%)
  Pallas kernels  45.4 us (25%)
  starting transfers between devices  30.2 us (17%)
  between operations  14.4 us (8%)
  matrix products  8.35 us (5%)
  local copies, waits for them, and re-layouts  6.88 us (4%)
    ppermute x6, waiting for transfers between devices, chip_swap(): lax.ppermute(value, 'lon', [(i, i ^ 2 * offset) for i in range(size)])  38.6 us
    all_gather x1, waiting for transfers between devices, per_device(): lax.all_gather(merge_weight, 'lon', axis=1, tiled=True)  31.4 us
    pallas_call x1, Pallas kernels, attention(): pl.pallas_call(functools.partial(attention_kernel, bands, kinds), grid=(g...  22.1 us
    ppermute x8, starting transfers between devices, send(): return lax.ppermute(part, ('lat', 'lon'), pairs)  20.6 us
    pallas_call x4, Pallas kernels, feed_forward(): pl.pallas_call(ffn_kernel, in_specs=[vmem] * 4, out_specs=[vmem] * 2, out...  10.7 us
    dot_general x1, matrix products, per_device(): jnp.dot(merged, lax.all_gather(merge_weight, 'lon', axis=1, tiled=True),...  8.35 us
    ppermute x6, starting transfers between devices, chip_swap(): lax.ppermute(value, 'lon', [(i, i ^ 2 * offset) for i in range(size)])  7.24 us
    pallas_call x1, Pallas kernels, own_projection(): pl.pallas_call(functools.partial(own_kernel, bands), grid=(out // block,)...  7.07 us
  transfers between devices with their start and end apart: 23, of which 7 were waited for; matrix products, arithmetic and copies ran while one was open for 2% of the time, Pallas kernels for 25%

profile of v1, /device:TPU:0, one launch (start us, length us, event | category | flops | bytes accessed | tf_op | source)
XLA Modules:
  0.0 181.7 jit_solution(8514528695705565924)
XLA Ops:
  7.2 0.0 copy-start.3
  7.2 0.0 all-gather.2.cloned.1.call-start
  7.2 0.7 all-gather.2.cloned.1.call-update
  7.9 1.1 fusion.7
  9.0 0.5 collective-permute-start
  9.5 2.9 %collective-permute-start.1 = (bf16[18,8,1024]{2,1,0:T(8,128)(2,1)S(1)}, bf16[18,8,1024]{2,1,0:T(8,128)(2,1)S(1)}, u32[]{:S(2)}, u32[]{:S(2)}) collective-permute-start(bf16[18,8,1024]{2,1,0:T(8,128)(2,1)S(1)} %get-tuple-element.28), channel_id=1, source_target_pairs={{0,7},{1,0},{2,1},{3,2},{4,3},{5,4},{6,5},{7,6},{8,15},{9,8},{10,9... | collective-permute-start | bytes 884744 | tf_op jit(solution)/shard_map/ppermute | solution.py:315
  12.5 0.9 fusion.5
  13.3 2.7 %collective-permute-start.4 = (bf16[3,8,1024]{2,1,0:T(8,128)(2,1)S(1)}, bf16[3,8,1024]{2,1,0:T(8,128)(2,1)S(1)}, u32[]{:S(2)}, u32[]{:S(2)}) collective-permute-start(bf16[3,8,1024]{2,1,0:T(8,128)(2,1)S(1)} %get-tuple-element.25), channel_id=1, source_target_pairs={{0,9},{1,10},{2,11},{3,12},{4,13},{5,14},{6,15},{7,8},{8,17},{9,18... | collective-permute-start | bytes 147464 | tf_op jit(solution)/shard_map/ppermute | solution.py:315
  16.1 6.4 %collective-permute-start.5 = (bf16[3,8,1024]{2,1,0:T(8,128)(2,1)S(1)}, bf16[3,8,1024]{2,1,0:T(8,128)(2,1)S(1)}, u32[]{:S(2)}, u32[]{:S(2)}) collective-permute-start(bf16[3,8,1024]{2,1,0:T(8,128)(2,1)S(1)} %get-tuple-element.24), channel_id=1, source_target_pairs={{0,15},{1,8},{2,9},{3,10},{4,11},{5,12},{6,13},{7,14},{8,23},{9,16... | collective-permute-start | bytes 147464 | tf_op jit(solution)/shard_map/ppermute | solution.py:315
  22.5 1.3 collective-permute-start.6
  23.9 1.0 fusion.6
  24.9 7.1 %own_projection.1.q_ref.k_ref.v_ref = bf16[448,3072]{1,0:T(8,128)(2,1)S(1)} custom-call(bf16[18,24,1024]{2,1,0:T(8,128)(2,1)S(1)} %copy-done.3, bf16[1024,3072]{1,0:T(8,128)(2,1)} %refs_8_.1), custom_call_target="tpu_custom_call" | custom-call | flops 2818572288 | bytes 6291456 | tf_op jit(solution)/shard_map/own_projection/pallas_call | solution.py:130
  32.0 1.5 copy-done.15
  33.5 0.0 collective-permute-done.4.refs_4_
  33.5 4.1 %collective-permute-start.2 = (bf16[3,24,1024]{2,1,0:T(8,128)(2,1)S(1)}, bf16[3,24,1024]{2,1,0:T(8,128)(2,1)S(1)}, u32[]{:S(2)}, u32[]{:S(2)}) collective-permute-start(bf16[3,24,1024]{2,1,0:T(8,128)(2,1)S(1)} %get-tuple-element.27), channel_id=1, source_target_pairs={{0,8},{1,9},{2,10},{3,11},{4,12},{5,13},{6,14},{7,15},{8,16},{9,17... | collective-permute-start | bytes 442376 | tf_op jit(solution)/shard_map/ppermute | solution.py:315
  37.6 1.3 collective-permute-start.3
  38.9 0.0 collective-permute-done.6.refs_6_
  38.9 1.3 collective-permute-start.7
  40.2 0.1 or_select_fusion.bias_ref
  40.3 0.0 copy-start.7
  40.3 0.0 copy-start.8
  40.3 0.0 copy-start.9
  40.4 0.0 copy-start.10
  40.4 0.0 copy-start.11
  40.4 0.0 copy-start.12
  40.4 0.0 copy-start.13
  40.4 0.0 copy-start.14
  40.4 4.4 %collective-permute-done.7.refs_7_ = bf16[3,8,1024]{2,1,0:T(8,128)(2,1)S(1)} collective-permute-done((bf16[3,8,1024]{2,1,0:T(8,128)(2,1)S(1)}, bf16[3,8,1024]{2,1,0:T(8,128)(2,1)S(1)}, u32[]{:S(2)}, u32[]{:S(2)}) %collective-permute-start.7) | collective-permute-done | bytes 49184 | tf_op jit(solution)/shard_map/ppermute | solution.py:315
  44.8 0.0 collective-permute-done.2.refs_2_
  44.8 0.4 collective-permute-done.3.refs_3_
  45.2 0.0 collective-permute-done.refs_0_
  45.2 5.5 %halo_projection.1.hk_ref.hv_ref = bf16[544,2048]{1,0:T(8,128)(2,1)S(1)} custom-call(bf16[18,8,1024]{2,1,0:T(8,128)(2,1)S(1)} %collective-permute-done.refs_0_, bf16[18,8,1024]{2,1,0:T(8,128)(2,1)S(1)} %collective-permute-done.1.refs_1_, bf16[3,24,1024]{2,1,0:T(8,128)(2,1)S(1)} %collective-permute-done.2.refs_2_, ...), custom_call_target="tpu_custom_call" | custom-call | flops 2281701376 | bytes 4194304 | tf_op jit(solution)/shard_map/halo_projection/pallas_call | solution.py:175
  50.7 1.4 copy-done.2
  52.2 22.1 %attention.1 = (bf16[18,24,1024]{2,1,0:T(8,128)(2,1)}, bf16[112,4096]{1,0:T(8,128)(2,1)S(1)}) custom-call(bf16[18,24,1024]{2,1,0:T(8,128)(2,1)S(1)} %copy-done.3, f32[8,128]{1,0:T(8,128)S(1)} %or_select_fusion.bias_ref, bf16[448,3072]{1,0:T(8,128)(2,1)} %copy-done.15, bf16[448,3072]{1,0:T(8,128)(2,1)} %copy-done.15, bf16[448,3072]{1,0:T(8,128)(2,1)} %copy-done.15, ...), custom_call_target="tpu_custom_call" | custom-call | flops 8000000000 | bytes 10000000 | tf_op jit(solution)/shard_map/attention/pallas_call | solution.py:278
  74.3 31.4 %all-gather.2.cloned.1.call-done = bf16[4096,2048]{1,0:T(8,128)(2,1)} async-done(((bf16[4096,256]{1,0:T(8,128)(2,1)}), bf16[4096,2048]{1,0:T(8,128)(2,1)}) %all-gather.2.cloned.1.call-update) | async-done | bytes 16777232 | tf_op jit(solution)/shard_map/all_gather | solution.py:393
  105.7 8.4 %convolution_convert_fusion.mine_ref = bf16[112,2048]{1,0:T(8,128)(2,1)S(1)} fusion(bf16[112,4096]{1,0:T(8,128)(2,1)S(1)} %get-tuple-element.13, bf16[4096,2048]{1,0:T(8,128)(2,1)} %all-gather.2.cloned.1.call-done), kind=kOutput, calls=%fused_computation | convolution fusion | flops 1879277568 | bytes 18153472 | tf_op jit(solution)/shard_map/dot_general | solution.py:391
  114.1 1.4 collective-permute-start.18
  115.5 1.5 collective-permute-start.14
  117.0 0.6 collective-permute-start.10
  117.7 10.8 %collective-permute-done.18.mine_ref = bf16[112,2048]{1,0:T(8,128)(2,1)S(1)} collective-permute-done((bf16[112,2048]{1,0:T(8,128)(2,1)S(1)}, bf16[112,2048]{1,0:T(8,128)(2,1)S(1)}, u32[]{:S(2)}, u32[]{:S(2)}) %collective-permute-start.18) | collective-permute-done | bytes 458784 | tf_op jit(solution)/shard_map/ppermute | solution.py:380
  128.5 0.5 collective-permute-start.8
  129.0 8.6 %collective-permute-done.14.mine_ref = bf16[112,2048]{1,0:T(8,128)(2,1)S(1)} collective-permute-done((bf16[112,2048]{1,0:T(8,128)(2,1)S(1)}, bf16[112,2048]{1,0:T(8,128)(2,1)S(1)}, u32[]{:S(2)}, u32[]{:S(2)}) %collective-permute-start.14) | collective-permute-done | bytes 458784 | tf_op jit(solution)/shard_map/ppermute | solution.py:380
  137.5 0.0 collective-permute-start.15
  137.6 0.5 collective-permute-start.11
  138.1 2.7 %feed_forward.7 = (bf16[112,2048]{1,0:T(8,128)(2,1)S(1)}, bf16[112,2048]{1,0:T(8,128)(2,1)S(1)}) custom-call(bf16[112,2048]{1,0:T(8,128)(2,1)S(1)} %collective-permute-done.18.mine_ref, bf16[112,2048]{1,0:T(8,128)(2,1)S(1)} %collective-permute-done.19.theirs_ref, bf16[2048,1024]{1,0:T(8,128)(2,1)S(1)} %copy-done, bf16[1024,2048]{1,0:T(8,128)(2,1)S(1)} %copy-done.1), custom_call_target="tpu_custom_call" | custom-call | flops 1879048192 | bytes 8388608 | tf_op jit(solution)/shard_map/feed_forward/pallas_call | solution.py:359
  140.7 0.1 collective-permute-start.20
  140.9 2.7 %feed_forward.4 = (bf16[112,2048]{1,0:T(8,128)(2,1)S(1)}, bf16[112,2048]{1,0:T(8,128)(2,1)S(1)}) custom-call(bf16[112,2048]{1,0:T(8,128)(2,1)S(1)} %convolution_convert_fusion.mine_ref, bf16[112,2048]{1,0:T(8,128)(2,1)S(1)} %collective-permute-done.8.theirs_ref, bf16[2048,1024]{1,0:T(8,128)(2,1)S(1)} %copy-done, bf16[1024,2048]{1,0:T(8,128)(2,1)S(1)} %copy-done.1), custom_call_target="tpu_custom_call" | custom-call | flops 1879048192 | bytes 8388608 | tf_op jit(solution)/shard_map/feed_forward/pallas_call | solution.py:359
  143.6 0.5 collective-permute-start.9
  144.1 2.7 %feed_forward.6 = (bf16[112,2048]{1,0:T(8,128)(2,1)S(1)}, bf16[112,2048]{1,0:T(8,128)(2,1)S(1)}) custom-call(bf16[112,2048]{1,0:T(8,128)(2,1)S(1)} %collective-permute-done.14.mine_ref, bf16[112,2048]{1,0:T(8,128)(2,1)S(1)} %collective-permute-done.15.theirs_ref, bf16[2048,1024]{1,0:T(8,128)(2,1)S(1)} %copy-done, bf16[1024,2048]{1,0:T(8,128)(2,1)S(1)} %copy-done.1), custom_call_target="tpu_custom_call" | custom-call | flops 1879048192 | bytes 8388608 | tf_op jit(solution)/shard_map/feed_forward/pallas_call | solution.py:359
  146.8 0.1 collective-permute-start.16
  146.9 2.7 %feed_forward.5 = (bf16[112,2048]{1,0:T(8,128)(2,1)S(1)}, bf16[112,2048]{1,0:T(8,128)(2,1)S(1)}) custom-call(bf16[112,2048]{1,0:T(8,128)(2,1)S(1)} %collective-permute-done.10.mine_ref, bf16[112,2048]{1,0:T(8,128)(2,1)S(1)} %collective-permute-done.11.theirs_ref, bf16[2048,1024]{1,0:T(8,128)(2,1)S(1)} %copy-done, bf16[1024,2048]{1,0:T(8,128)(2,1)S(1)} %copy-done.1), custom_call_target="tpu_custom_call" | custom-call | flops 1879048192 | bytes 8388608 | tf_op jit(solution)/shard_map/feed_forward/pallas_call | solution.py:359
  149.6 0.5 collective-permute-start.12
  150.1 0.1 add_convert_fusion
  150.2 1.6 collective-permute-start.21
  151.9 0.1 add_convert_fusion.1
  152.0 0.7 collective-permute-start.17
  152.6 0.1 add_convert_fusion.2
  152.7 1.4 collective-permute-start.13
  154.1 0.1 convert_element_type.51
  154.2 0.1 convert_element_type.52
  154.3 10.3 %collective-permute-done.21 = bf16[112,2048]{1,0:T(8,128)(2,1)S(1)} collective-permute-done((bf16[112,2048]{1,0:T(8,128)(2,1)S(1)}, bf16[112,2048]{1,0:T(8,128)(2,1)S(1)}, u32[]{:S(2)}, u32[]{:S(2)}) %collective-permute-start.21) | collective-permute-done | bytes 458784 | tf_op jit(solution)/shard_map/ppermute | solution.py:380
  164.6 8.9 %collective-permute-done.17 = bf16[112,2048]{1,0:T(8,128)(2,1)S(1)} collective-permute-done((bf16[112,2048]{1,0:T(8,128)(2,1)S(1)}, bf16[112,2048]{1,0:T(8,128)(2,1)S(1)}, u32[]{:S(2)}, u32[]{:S(2)}) %collective-permute-start.17) | collective-permute-done | bytes 458784 | tf_op jit(solution)/shard_map/ppermute | solution.py:380
  173.5 0.4 fusion.4
  173.9 0.9 reshape.45
  (36 shorter events, 0.1 us)
Async XLA Ops:
  7.2 17.7 %copy-start.3 = (bf16[18,24,1024]{2,1,0:T(8,128)(2,1)S(1)}, bf16[18,24,1024]{2,1,0:T(8,128)(2,1)}, u32[]{:S(2)}) copy-start(bf16[18,24,1024]{2,1,0:T(8,128)(2,1)} %tokens_ref.3) | copy-start | bytes 2654212
  7.2 98.6 %all-gather.2.cloned.1.call-start = ((), (), s32[]{:S(2)}) async-start(), calls=%async_computation | async-start | bytes 18874368 | tf_op jit(solution)/shard_map/all_gather | solution.py:393
  9.0 36.2 %collective-permute-start = (bf16[18,8,1024]{2,1,0:T(8,128)(2,1)S(1)}, bf16[18,8,1024]{2,1,0:T(8,128)(2,1)S(1)}, u32[]{:S(2)}, u32[]{:S(2)}) collective-permute-start(bf16[18,8,1024]{2,1,0:T(8,128)(2,1)S(1)} %get-tuple-element.29), channel_id=1, source_target_pairs={{0,1},{1,2},{2,3},{3,4},{4,5},{5,6},{6,7},{7,0},{8,9},{9,10},{10,1... | collective-permute-start | bytes 884744 | tf_op jit(solution)/shard_map/ppermute | solution.py:315
  9.5 35.7 %collective-permute-start.1 = (bf16[18,8,1024]{2,1,0:T(8,128)(2,1)S(1)}, bf16[18,8,1024]{2,1,0:T(8,128)(2,1)S(1)}, u32[]{:S(2)}, u32[]{:S(2)}) collective-permute-start(bf16[18,8,1024]{2,1,0:T(8,128)(2,1)S(1)} %get-tuple-element.28), channel_id=1, source_target_pairs={{0,7},{1,0},{2,1},{3,2},{4,3},{5,4},{6,5},{7,6},{8,15},{9,8},{10,9... | collective-permute-start | bytes 884744 | tf_op jit(solution)/shard_map/ppermute | solution.py:315
  13.3 20.1 %collective-permute-start.4 = (bf16[3,8,1024]{2,1,0:T(8,128)(2,1)S(1)}, bf16[3,8,1024]{2,1,0:T(8,128)(2,1)S(1)}, u32[]{:S(2)}, u32[]{:S(2)}) collective-permute-start(bf16[3,8,1024]{2,1,0:T(8,128)(2,1)S(1)} %get-tuple-element.25), channel_id=1, source_target_pairs={{0,9},{1,10},{2,11},{3,12},{4,13},{5,14},{6,15},{7,8},{8,17},{9,18... | collective-permute-start | bytes 147464 | tf_op jit(solution)/shard_map/ppermute | solution.py:315
  16.1 21.5 %collective-permute-start.5 = (bf16[3,8,1024]{2,1,0:T(8,128)(2,1)S(1)}, bf16[3,8,1024]{2,1,0:T(8,128)(2,1)S(1)}, u32[]{:S(2)}, u32[]{:S(2)}) collective-permute-start(bf16[3,8,1024]{2,1,0:T(8,128)(2,1)S(1)} %get-tuple-element.24), channel_id=1, source_target_pairs={{0,15},{1,8},{2,9},{3,10},{4,11},{5,12},{6,13},{7,14},{8,23},{9,16... | collective-permute-start | bytes 147464 | tf_op jit(solution)/shard_map/ppermute | solution.py:315
  22.5 16.4 %collective-permute-start.6 = (bf16[3,8,1024]{2,1,0:T(8,128)(2,1)S(1)}, bf16[3,8,1024]{2,1,0:T(8,128)(2,1)S(1)}, u32[]{:S(2)}, u32[]{:S(2)}) collective-permute-start(bf16[3,8,1024]{2,1,0:T(8,128)(2,1)S(1)} %get-tuple-element.23), channel_id=1, source_target_pairs={{8,1},{9,2},{10,3},{11,4},{12,5},{13,6},{14,7},{15,0},{16,9},{17,1... | collective-permute-start | bytes 147464 | tf_op jit(solution)/shard_map/ppermute | solution.py:315
  32.0 1.5 copy-start.15
  33.5 11.3 %collective-permute-start.2 = (bf16[3,24,1024]{2,1,0:T(8,128)(2,1)S(1)}, bf16[3,24,1024]{2,1,0:T(8,128)(2,1)S(1)}, u32[]{:S(2)}, u32[]{:S(2)}) collective-permute-start(bf16[3,24,1024]{2,1,0:T(8,128)(2,1)S(1)} %get-tuple-element.27), channel_id=1, source_target_pairs={{0,8},{1,9},{2,10},{3,11},{4,12},{5,13},{6,14},{7,15},{8,16},{9,17... | collective-permute-start | bytes 442376 | tf_op jit(solution)/shard_map/ppermute | solution.py:315
  37.6 7.6 %collective-permute-start.3 = (bf16[3,24,1024]{2,1,0:T(8,128)(2,1)S(1)}, bf16[3,24,1024]{2,1,0:T(8,128)(2,1)S(1)}, u32[]{:S(2)}, u32[]{:S(2)}) collective-permute-start(bf16[3,24,1024]{2,1,0:T(8,128)(2,1)S(1)} %get-tuple-element.26), channel_id=1, source_target_pairs={{8,0},{9,1},{10,2},{11,3},{12,4},{13,5},{14,6},{15,7},{16,8},{17,9... | collective-permute-start | bytes 442376 | tf_op jit(solution)/shard_map/ppermute | solution.py:315
  38.9 5.9 %collective-permute-start.7 = (bf16[3,8,1024]{2,1,0:T(8,128)(2,1)S(1)}, bf16[3,8,1024]{2,1,0:T(8,128)(2,1)S(1)}, u32[]{:S(2)}, u32[]{:S(2)}) collective-permute-start(bf16[3,8,1024]{2,1,0:T(8,128)(2,1)S(1)} %get-tuple-element.22), channel_id=1, source_target_pairs={{8,7},{9,0},{10,1},{11,2},{12,3},{13,4},{14,5},{15,6},{16,15},{17,... | collective-permute-start | bytes 147464 | tf_op jit(solution)/shard_map/ppermute | solution.py:315
  40.3 11.8 %copy-start.4 = (bf16[1024,1024]{1,0:T(8,128)(2,1)S(1)}, bf16[1024,1024]{1,0:T(8,128)(2,1)}, u32[]{:S(2)}) copy-start(bf16[1024,1024]{1,0:T(8,128)(2,1)} %out_w_ref.1) | copy-start | bytes 6291460
  40.3 11.8 %copy-start.5 = (f32[576,256]{1,0:T(8,128)S(1)}, f32[576,256]{1,0:T(8,128)}, u32[]{:S(2)}) copy-start(f32[576,256]{1,0:T(8,128)} %constant.53.clone.rest_6_) | copy-start | bytes 1769476
  40.3 11.8 %copy-start.6 = (bf16[448,432]{1,0:T(8,128)(2,1)S(1)}, bf16[448,432]{1,0:T(8,128)(2,1)}, u32[]{:S(2)}) copy-start(bf16[448,432]{1,0:T(8,128)(2,1)} %constant.46.clone.patch_ref) | copy-start | bytes 1161220
  40.3 11.8 %copy-start.7 = (f32[288,256]{1,0:T(8,128)S(1)}, f32[288,256]{1,0:T(8,128)}, u32[]{:S(2)}) copy-start(f32[288,256]{1,0:T(8,128)} %constant.49.clone.rest_2_.rest_10_) | copy-start | bytes 884740
  40.3 11.8 %copy-start.8 = (bf16[576,144]{1,0:T(8,128)(2,1)S(1)}, bf16[576,144]{1,0:T(8,128)(2,1)}, u32[]{:S(2)}) copy-start(bf16[576,144]{1,0:T(8,128)(2,1)} %constant.52.clone.rest_5_) | copy-start | bytes 497668
  40.3 11.8 %copy-start.9 = (bf16[144,576]{1,0:T(8,128)(2,1)S(1)}, bf16[144,576]{1,0:T(8,128)(2,1)}, u32[]{:S(2)}) copy-start(bf16[144,576]{1,0:T(8,128)(2,1)} %constant.54.clone.rest_7_) | copy-start | bytes 497668
  40.4 11.8 %copy-start.10 = (bf16[216,256]{1,0:T(8,128)(2,1)S(1)}, bf16[216,256]{1,0:T(8,128)(2,1)}, u32[]{:S(2)}) copy-start(bf16[216,256]{1,0:T(8,128)(2,1)} %constant.47.clone.rest_0_) | copy-start | bytes 331780
  40.4 11.8 %copy-start.11 = (bf16[216,240]{1,0:T(8,128)(2,1)S(1)}, bf16[216,240]{1,0:T(8,128)(2,1)}, u32[]{:S(2)}) copy-start(bf16[216,240]{1,0:T(8,128)(2,1)} %constant.51.clone.rest_4_) | copy-start | bytes 311044
  40.4 11.8 %copy-start.12 = (bf16[216,256]{1,0:T(8,128)(2,1)S(1)}, bf16[216,256]{1,0:T(8,128)(2,1)}, u32[]{:S(2)}) copy-start(bf16[216,256]{1,0:T(8,128)(2,1)} %constant.55.clone.rest_8_) | copy-start | bytes 331780
  40.4 11.8 %copy-start.13 = (bf16[288,80]{1,0:T(8,128)(2,1)S(1)}, bf16[288,80]{1,0:T(8,128)(2,1)}, u32[]{:S(2)}) copy-start(bf16[288,80]{1,0:T(8,128)(2,1)} %constant.48.clone.rest_1_.rest_9_) | copy-start | bytes 138244
  40.4 11.8 %copy-start.14 = (bf16[80,288]{1,0:T(8,128)(2,1)S(1)}, bf16[80,288]{1,0:T(8,128)(2,1)}, u32[]{:S(2)}) copy-start(bf16[80,288]{1,0:T(8,128)(2,1)} %constant.50.clone.rest_3_.rest_11_) | copy-start | bytes 138244
  50.7 1.4 copy-start.2
  105.7 32.3 %copy-start = (bf16[2048,1024]{1,0:T(8,128)(2,1)S(1)}, bf16[2048,1024]{1,0:T(8,128)(2,1)}, u32[]{:S(2)}) copy-start(bf16[2048,1024]{1,0:T(8,128)(2,1)} %up_ref.7) | copy-start | bytes 12582916
  105.7 32.3 %copy-start.1 = (bf16[1024,2048]{1,0:T(8,128)(2,1)S(1)}, bf16[1024,2048]{1,0:T(8,128)(2,1)}, u32[]{:S(2)}) copy-start(bf16[1024,2048]{1,0:T(8,128)(2,1)} %down_ref.7) | copy-start | bytes 12582916
  114.1 14.4 %collective-permute-start.18 = (bf16[112,2048]{1,0:T(8,128)(2,1)S(1)}, bf16[112,2048]{1,0:T(8,128)(2,1)S(1)}, u32[]{:S(2)}, u32[]{:S(2)}) collective-permute-start(bf16[112,2048]{1,0:T(8,128)(2,1)S(1)} %convolution_convert_fusion.mine_ref), channel_id=1, source_target_pairs={{0,6},{1,7},{2,4},{3,5},{4,2},{5,3},{6,0},{7,1},{8,14},{9,15},{10,... | collective-permute-start | bytes 1376264 | tf_op jit(solution)/shard_map/ppermute | solution.py:380
  115.5 22.0 %collective-permute-start.14 = (bf16[112,2048]{1,0:T(8,128)(2,1)S(1)}, bf16[112,2048]{1,0:T(8,128)(2,1)S(1)}, u32[]{:S(2)}, u32[]{:S(2)}) collective-permute-start(bf16[112,2048]{1,0:T(8,128)(2,1)S(1)} %convolution_convert_fusion.mine_ref), channel_id=1, source_target_pairs={{0,4},{1,5},{2,6},{3,7},{4,0},{5,1},{6,2},{7,3},{8,12},{9,13},{10,... | collective-permute-start | bytes 1376264 | tf_op jit(solution)/shard_map/ppermute | solution.py:380
  117.0 20.5 %collective-permute-start.10 = (bf16[112,2048]{1,0:T(8,128)(2,1)S(1)}, bf16[112,2048]{1,0:T(8,128)(2,1)S(1)}, u32[]{:S(2)}, u32[]{:S(2)}) collective-permute-start(bf16[112,2048]{1,0:T(8,128)(2,1)S(1)} %convolution_convert_fusion.mine_ref), channel_id=1, source_target_pairs={{0,2},{1,3},{2,0},{3,1},{4,6},{5,7},{6,4},{7,5},{8,10},{9,11},{10,... | collective-permute-start | bytes 1376264 | tf_op jit(solution)/shard_map/ppermute | solution.py:380
  128.5 9.6 %collective-permute-start.19 = (bf16[112,2048]{1,0:T(8,128)(2,1)S(1)}, bf16[112,2048]{1,0:T(8,128)(2,1)S(1)}, u32[]{:S(2)}, u32[]{:S(2)}) collective-permute-start(bf16[112,2048]{1,0:T(8,128)(2,1)S(1)} %collective-permute-done.18.mine_ref), channel_id=1, source_target_pairs={{0,1},{1,0},{2,3},{3,2},{4,5},{5,4},{6,7},{7,6},{8,9},{9,8},{10,11... | collective-permute-start | bytes 1376264 | tf_op jit(solution)/shard_map/ppermute | solution.py:375
  128.5 12.4 %collective-permute-start.8 = (bf16[112,2048]{1,0:T(8,128)(2,1)S(1)}, bf16[112,2048]{1,0:T(8,128)(2,1)S(1)}, u32[]{:S(2)}, u32[]{:S(2)}) collective-permute-start(bf16[112,2048]{1,0:T(8,128)(2,1)S(1)} %convolution_convert_fusion.mine_ref), channel_id=1, source_target_pairs={{0,1},{1,0},{2,3},{3,2},{4,5},{5,4},{6,7},{7,6},{8,9},{9,8},{10,11... | collective-permute-start | bytes 1376264 | tf_op jit(solution)/shard_map/ppermute | solution.py:375
  137.5 6.5 %collective-permute-start.15 = (bf16[112,2048]{1,0:T(8,128)(2,1)S(1)}, bf16[112,2048]{1,0:T(8,128)(2,1)S(1)}, u32[]{:S(2)}, u32[]{:S(2)}) collective-permute-start(bf16[112,2048]{1,0:T(8,128)(2,1)S(1)} %collective-permute-done.14.mine_ref), channel_id=1, source_target_pairs={{0,1},{1,0},{2,3},{3,2},{4,5},{5,4},{6,7},{7,6},{8,9},{9,8},{10,11... | collective-permute-start | bytes 1376264 | tf_op jit(solution)/shard_map/ppermute | solution.py:375
  137.6 9.3 %collective-permute-start.11 = (bf16[112,2048]{1,0:T(8,128)(2,1)S(1)}, bf16[112,2048]{1,0:T(8,128)(2,1)S(1)}, u32[]{:S(2)}, u32[]{:S(2)}) collective-permute-start(bf16[112,2048]{1,0:T(8,128)(2,1)S(1)} %collective-permute-done.10.mine_ref), channel_id=1, source_target_pairs={{0,1},{1,0},{2,3},{3,2},{4,5},{5,4},{6,7},{7,6},{8,9},{9,8},{10,11... | collective-permute-start | bytes 1376264 | tf_op jit(solution)/shard_map/ppermute | solution.py:375
  140.7 9.4 %collective-permute-start.20 = (bf16[112,2048]{1,0:T(8,128)(2,1)S(1)}, bf16[112,2048]{1,0:T(8,128)(2,1)S(1)}, u32[]{:S(2)}, u32[]{:S(2)}) collective-permute-start(bf16[112,2048]{1,0:T(8,128)(2,1)S(1)} %get-tuple-element.21), channel_id=1, source_target_pairs={{0,1},{1,0},{2,3},{3,2},{4,5},{5,4},{6,7},{7,6},{8,9},{9,8},{10,11... | collective-permute-start | bytes 1376264 | tf_op jit(solution)/shard_map/ppermute | solution.py:375
  143.6 10.7 %collective-permute-start.9 = (bf16[112,2048]{1,0:T(8,128)(2,1)S(1)}, bf16[112,2048]{1,0:T(8,128)(2,1)S(1)}, u32[]{:S(2)}, u32[]{:S(2)}) collective-permute-start(bf16[112,2048]{1,0:T(8,128)(2,1)S(1)} %get-tuple-element.15), channel_id=1, source_target_pairs={{0,1},{1,0},{2,3},{3,2},{4,5},{5,4},{6,7},{7,6},{8,9},{9,8},{10,11... | collective-permute-start | bytes 1376264 | tf_op jit(solution)/shard_map/ppermute | solution.py:375
  146.8 5.1 %collective-permute-start.16 = (bf16[112,2048]{1,0:T(8,128)(2,1)S(1)}, bf16[112,2048]{1,0:T(8,128)(2,1)S(1)}, u32[]{:S(2)}, u32[]{:S(2)}) collective-permute-start(bf16[112,2048]{1,0:T(8,128)(2,1)S(1)} %get-tuple-element.19), channel_id=1, source_target_pairs={{0,1},{1,0},{2,3},{3,2},{4,5},{5,4},{6,7},{7,6},{8,9},{9,8},{10,11... | collective-permute-start | bytes 1376264 | tf_op jit(solution)/shard_map/ppermute | solution.py:375
  149.6 3.0 %collective-permute-start.12 = (bf16[112,2048]{1,0:T(8,128)(2,1)S(1)}, bf16[112,2048]{1,0:T(8,128)(2,1)S(1)}, u32[]{:S(2)}, u32[]{:S(2)}) collective-permute-start(bf16[112,2048]{1,0:T(8,128)(2,1)S(1)} %get-tuple-element.17), channel_id=1, source_target_pairs={{0,1},{1,0},{2,3},{3,2},{4,5},{5,4},{6,7},{7,6},{8,9},{9,8},{10,11... | collective-permute-start | bytes 1376264 | tf_op jit(solution)/shard_map/ppermute | solution.py:375
  150.2 14.4 %collective-permute-start.21 = (bf16[112,2048]{1,0:T(8,128)(2,1)S(1)}, bf16[112,2048]{1,0:T(8,128)(2,1)S(1)}, u32[]{:S(2)}, u32[]{:S(2)}) collective-permute-start(bf16[112,2048]{1,0:T(8,128)(2,1)S(1)} %add_convert_fusion), channel_id=1, source_target_pairs={{0,6},{1,7},{2,4},{3,5},{4,2},{5,3},{6,0},{7,1},{8,14},{9,15},{10,... | collective-permute-start | bytes 1376264 | tf_op jit(solution)/shard_map/ppermute | solution.py:380
  152.0 21.5 %collective-permute-start.17 = (bf16[112,2048]{1,0:T(8,128)(2,1)S(1)}, bf16[112,2048]{1,0:T(8,128)(2,1)S(1)}, u32[]{:S(2)}, u32[]{:S(2)}) collective-permute-start(bf16[112,2048]{1,0:T(8,128)(2,1)S(1)} %add_convert_fusion.1), channel_id=1, source_target_pairs={{0,4},{1,5},{2,6},{3,7},{4,0},{5,1},{6,2},{7,3},{8,12},{9,13},{10,... | collective-permute-start | bytes 1376264 | tf_op jit(solution)/shard_map/ppermute | solution.py:380
  152.7 20.8 %collective-permute-start.13 = (bf16[112,2048]{1,0:T(8,128)(2,1)S(1)}, bf16[112,2048]{1,0:T(8,128)(2,1)S(1)}, u32[]{:S(2)}, u32[]{:S(2)}) collective-permute-start(bf16[112,2048]{1,0:T(8,128)(2,1)S(1)} %add_convert_fusion.2), channel_id=1, source_target_pairs={{0,2},{1,3},{2,0},{3,1},{4,6},{5,7},{6,4},{7,5},{8,10},{9,11},{10,... | collective-permute-start | bytes 1376264 | tf_op jit(solution)/shard_map/ppermute | solution.py:380
Sparse Core Ops, SparseCore 0:
  9.9 95.8 all-gather.1

commit v2 on v0

v2 whole, which is shorter than its diff:
```python
import functools

import jax
import jax.numpy as jnp
import numpy as np
from jax import lax
from jax.experimental import pallas as pl
from jax.experimental.pallas import tpu as pltpu
from jax.sharding import PartitionSpec as P

HEADS = 16
WLAT = 6
WLON = 12
RIM_LAT = WLAT // 2
RIM_LON = WLON // 2
SIDE = 8
GROUP = 4
F32 = jnp.float32
BF16 = jnp.bfloat16


def up16(n):
    return -(-n // 16) * 16


def params(mib=48, **kw):
    return pltpu.CompilerParams(vmem_limit_bytes=mib * 2**20, **kw)


class Bands:
    def __init__(self, rows, columns):
        assert (rows - WLAT) % WLAT == 0 and (columns - WLON) % WLON == 0
        self.rows, self.columns = rows, columns
        inner = (rows - WLAT) // WLAT
        self.height = [RIM_LAT] + [WLAT] * inner + [RIM_LAT]
        self.count = len(self.height)
        self.first = [sum(self.height[:b]) for b in range(self.count)]
        self.widths = [RIM_LON] + [WLON] * ((columns - WLON) // WLON) + [RIM_LON]
        self.own = [h * columns for h in self.height]
        self.own_padded = [up16(n) for n in self.own]
        self.own_at = [sum(self.own_padded[:b]) for b in range(self.count)]
        self.own_total = sum(self.own_padded)
        self.side = [2 * h * SIDE for h in self.height]
        assert all(n % 16 == 0 for n in self.side)
        self.side_at = [sum(self.side[:b]) for b in range(self.count)]
        self.side_total = sum(self.side)
        self.slab = columns + 2 * SIDE
        self.slab_padded = up16(RIM_LAT * self.slab)
        self.window = up16(WLAT * WLON)
        self.counts = [[GROUP * h * w for w in self.widths] for h in self.height]
        self.counts_padded = [[up16(n) for n in row] for row in self.counts]

    def edge(self, b):
        return b in (0, self.count - 1)

    def sources(self, b):
        return self.own_padded[b] + self.side[b] + (self.slab_padded if self.edge(b) else 0)

    def source(self, b, i, j):
        columns, h, first = self.columns, self.height[b], self.first[b]
        at = self.own_padded[b]
        if not 0 <= i < self.rows:
            i = i + RIM_LAT if i < 0 else i - self.rows
            return at + self.side[b] + i * self.slab + j + SIDE
        if 0 <= j < columns:
            return (i - first) * columns + j
        at += (i - first) * SIDE
        return at + (j + SIDE if j < 0 else h * SIDE + j - columns)

    def key_matrix(self, b):
        g = np.zeros((len(self.widths) * self.window, self.sources(b)), np.float32)
        top = self.first[b] - (RIM_LAT if b == 0 else 0)
        for c in range(len(self.widths)):
            for i in range(WLAT):
                for j in range(WLON):
                    at = c * self.window + i * WLON + j
                    g[at, self.source(b, top + i, c * WLON - RIM_LON + j)] = 1
        return g.astype(BF16)

    def query_matrix(self, b):
        total = sum(self.counts_padded[b])
        g = np.zeros((total, self.own_padded[b]), np.float32)
        head = np.zeros((total,), np.int32)
        start = left = 0
        for width, padded in zip(self.widths, self.counts_padded[b]):
            at = start
            for k in range(GROUP):
                for i in range(self.height[b]):
                    for j in range(width):
                        g[at, i * self.columns + left + j] = 1
                        head[at] = k
                        at += 1
            left += width
            start += padded
        return g.astype(BF16), head

    def patch_matrix(self):
        cells = self.rows * self.columns // 4
        padded = up16(cells)
        g = np.zeros((4 * padded, self.rows * self.columns), np.float32)
        for r in range(self.rows // 2):
            for c in range(self.columns // 2):
                for k in range(4):
                    to = k * padded + r * (self.columns // 2) + c
                    g[to, (2 * r + k // 2) * self.columns + 2 * c + k % 2] = 1
        return g.astype(BF16)

    def constants(self, some, block):
        distinct, kinds, consts = [], [], []
        for b in some:
            kind = (self.height[b], b == 0, b == self.count - 1)
            if kind not in distinct:
                distinct.append(kind)
                query, head = self.query_matrix(b)
                mask = head[:, None] == (np.arange(block) // (block // GROUP))[None, :]
                scale = np.float32((block // GROUP) ** -0.5)
                scaled = (query.astype(np.float32) * scale).astype(BF16)
                consts += [self.key_matrix(b), scaled, mask.astype(BF16), np.ascontiguousarray(query.T)]
            kinds.append(4 * distinct.index(kind))
        return kinds, consts


def normalize(values):
    center = values - jnp.mean(values, axis=-1, keepdims=True)
    spread = jnp.mean(center * center, axis=-1, keepdims=True)
    return center * lax.rsqrt(spread + 1e-05)


def dot(a, b, dims=((1,), (0,))):
    return lax.dot_general(a, b, (dims, ((), ())), preferred_element_type=F32)


def flat_normed(ref):
    values = ref[...].astype(F32)
    return normalize(values.reshape(-1, values.shape[-1]))


def padded_rows(values, total):
    if values.shape[0] == total:
        return values
    return jnp.concatenate([values, jnp.zeros((total - values.shape[0], values.shape[1]), values.dtype)], axis=0)


def project(normed_ref, weight_ref, out_ref, first):
    step = 256
    for at in range(0, out_ref.shape[1], step):
        part = weight_ref[:, first + at : first + at + step]
        out_ref[:, at : at + step] = dot(normed_ref[...], part).astype(BF16)


def own_kernel(bands, tokens_ref, weight_ref, out_ref, normed_ref):
    normed = flat_normed(tokens_ref)
    for b in range(bands.count):
        at = bands.first[b] * bands.columns
        part = padded_rows(normed[at : at + bands.own[b]], bands.own_padded[b])
        normed_ref[bands.own_at[b] : bands.own_at[b] + bands.own_padded[b], :] = part.astype(BF16)
    project(normed_ref, weight_ref, out_ref, 0)


def attend(bands, some, kinds, consts, own_ref, outer, bias_ref, put, scratch):
    k_ref, v_ref, q_ref, p_ref, r_ref = scratch
    width = own_ref.shape[1] // 3
    block = width * GROUP // HEADS
    window = WLAT * WLON
    units = [(n, b, g) for n, b in enumerate(some) for g in range(HEADS // GROUP)]
    for u, (n, b, g) in enumerate(units):
        keys, query, mask, _ = consts[kinds[n] : kinds[n] + 4]
        own = slice(bands.own_at[b], bands.own_at[b] + bands.own_padded[b])
        for ref, skip in ((k_ref, 0), (v_ref, width)):
            parts = [own_ref[own, width + skip + g * block : width + skip + (g + 1) * block]]
            for out_ref, at, size in outer(b):
                parts.append(out_ref[at : at + size, skip + g * block : skip + (g + 1) * block])
            ref[u] = dot(keys[...], jnp.concatenate(parts, axis=0)).astype(BF16)
        total = query.shape[0]
        q_ref[u, :total] = dot(query[...], own_ref[own, g * block : (g + 1) * block]).astype(BF16) * mask[...]
    for u, (n, b, g) in enumerate(units):
        at = 0
        for c, count in enumerate(bands.counts_padded[b]):
            scores = dot(
                q_ref[u, at : at + count], k_ref[u, c * bands.window : c * bands.window + window], ((1,), (1,))
            )
            if b == 0:
                scores = scores + bias_ref[0:1, :window]
            if b == bands.count - 1:
                scores = scores + bias_ref[1:2, :window]
            raised = jnp.exp(scores - jnp.max(scores, axis=-1, keepdims=True))
            weights = raised * (1.0 / jnp.sum(raised, axis=-1, keepdims=True))
            p_ref[u, at : at + count, :window] = weights.astype(BF16)
            at += count
    for u, (n, b, g) in enumerate(units):
        mask = consts[kinds[n] + 2]
        at = 0
        for c, count in enumerate(bands.counts_padded[b]):
            mixed = dot(
                p_ref[u, at : at + count, :window], v_ref[u, c * bands.window : c * bands.window + window]
            )
            r_ref[u, at : at + count] = mixed.astype(BF16) * mask[at : at + count]
            at += count
    for u, (n, b, g) in enumerate(units):
        back = consts[kinds[n] + 3]
        put(b, g, dot(back[...], r_ref[u, : back.shape[1]]).astype(BF16))


def attend_scratch(bands, some, block):
    units = len(some) * HEADS // GROUP
    keys = len(bands.widths) * bands.window
    rows = max(sum(bands.counts_padded[b]) for b in some)
    return [
        pltpu.VMEM((units, keys, block), BF16),
        pltpu.VMEM((units, keys, block), BF16),
        pltpu.VMEM((units, rows, block), BF16),
        pltpu.VMEM((units, rows, 128), BF16),
        pltpu.VMEM((units, rows, block), BF16),
    ]


def middle_kernel(bands, some, kinds, west_ref, east_ref, own_ref, weight_ref, *rest):
    consts, (side_ref, out_ref, normed_ref, *scratch) = rest[:-8], rest[-8:]
    width = weight_ref.shape[0]
    west, east = flat_normed(west_ref), flat_normed(east_ref)
    for b in range(bands.count):
        at, size = bands.first[b] * SIDE, bands.height[b] * SIDE
        part = jnp.concatenate([west[at : at + size], east[at : at + size]], axis=0)
        normed_ref[bands.side_at[b] : bands.side_at[b] + bands.side[b], :] = part.astype(BF16)
    project(normed_ref, weight_ref, side_ref, width)

    def outer(b):
        return [(side_ref, bands.side_at[b], bands.side[b])]

    def put(b, g, value):
        at = bands.own_at[b] - bands.own_at[1]
        block = value.shape[1]
        out_ref[at : at + bands.own_padded[b], g * block : (g + 1) * block] = value

    attend(bands, some, kinds, consts, own_ref, outer, None, put, scratch)


def edge_kernel(bands, some, kinds, tokens_ref, north_ref, south_ref, bias_ref, own_ref, side_ref, inner_ref, weight_ref, out_w_ref, patch_ref, *rest):
    consts, rest = rest[:-11], rest[-11:]
    middle_ref, upper_ref, lower_ref, normed_ref, slab_ref, attended_ref, *scratch = rest
    rows, columns, width = tokens_ref.shape
    slab = bands.slab_padded
    for k, ref in enumerate((north_ref, south_ref)):
        normed_ref[k * slab : (k + 1) * slab, :] = padded_rows(flat_normed(ref), slab).astype(BF16)
    project(normed_ref, weight_ref, slab_ref, width)

    def outer(b):
        return [
            (side_ref, bands.side_at[b], bands.side[b]),
            (slab_ref, 0 if b == 0 else slab, slab),
        ]

    def put(b, g, value):
        block = value.shape[1]
        attended_ref[bands.own_at[b] : bands.own_at[b] + bands.own_padded[b], g * block : (g + 1) * block] = value

    attended_ref[bands.own_at[1] : bands.own_at[-1], :] = inner_ref[...]
    attend(bands, some, kinds, consts, own_ref, outer, bias_ref, put, scratch)
    mixed = dot(attended_ref[...], out_w_ref[...])
    mixed = jnp.concatenate([mixed[at : at + n] for at, n in zip(bands.own_at, bands.own)], axis=0)
    middle = tokens_ref[...].astype(F32) + mixed.reshape(rows, columns, width)
    middle_ref[...] = middle.astype(BF16)
    middle = middle.reshape(rows * columns, width).astype(BF16)
    padded = patch_ref.shape[0] // 4
    parts = [dot(patch_ref[k * padded : (k + 1) * padded, :], middle) for k in range(4)]
    total = sum(jnp.sum(p, axis=-1, keepdims=True) for p in parts)
    mean = total * (1.0 / (4 * width))
    parts = [p - mean for p in parts]
    spread = sum(jnp.sum(p * p, axis=-1, keepdims=True) for p in parts)
    factor = lax.rsqrt(spread * (1.0 / (4 * width)) + 1e-05)
    for k in range(4):
        ref = (upper_ref, lower_ref)[k // 2]
        ref[:, k % 2 * width : (k % 2 + 1) * width] = (parts[k] * factor).astype(BF16)


def vmem_call(kernel, out, args, scratch, flops, name, mib=40, exps=0):
    vmem = pl.BlockSpec(memory_space=pltpu.VMEM)
    return pl.pallas_call(
        kernel,
        in_specs=[vmem] * len(args),
        out_specs=[vmem] * len(out),
        out_shape=[jax.ShapeDtypeStruct(shape, BF16) for shape in out],
        scratch_shapes=scratch,
        compiler_params=params(mib),
        cost_estimate=pl.CostEstimate(flops=flops, bytes_accessed=2**20, transcendentals=exps),
        name=name,
    )(*args)


def attention(bands, tokens, qkv_weight, out_weight):
    rows, columns, width = tokens.shape
    block = width * GROUP // HEADS
    west = shift(tokens[:, columns - SIDE :], "lon", 1, True)
    east = shift(tokens[:, :SIDE], "lon", -1, True)
    own = vmem_call(
        functools.partial(own_kernel, bands),
        [(bands.own_total, 3 * width)],
        [tokens, qkv_weight],
        [pltpu.VMEM((bands.own_total, width), BF16)],
        6 * bands.own_total * width * width,
        "own_projection",
    )[0]

    def slab(part):
        return jnp.concatenate([west[part], tokens[part], east[part]], axis=1)

    north = shift(slab(slice(rows - RIM_LAT, rows)), "lat", 1, False)
    south = shift(slab(slice(0, RIM_LAT)), "lat", -1, False)
    inner = list(range(1, bands.count - 1))
    edges = [0, bands.count - 1]
    kinds, consts = bands.constants(inner, block)
    side, attended = vmem_call(
        functools.partial(middle_kernel, bands, inner, kinds),
        [(bands.side_total, 2 * width), (bands.own_at[-1] - bands.own_at[1], width)],
        [west, east, own, qkv_weight] + consts,
        [pltpu.VMEM((bands.side_total, width), BF16)] + attend_scratch(bands, inner, block),
        5 * 10**9,
        "middle_attention",
        exps=500000,
    )
    kinds, consts = bands.constants(edges, block)
    padded = up16(rows * columns // 4)
    return vmem_call(
        functools.partial(edge_kernel, bands, edges, kinds),
        [tokens.shape, (padded, 2 * width), (padded, 2 * width)],
        [tokens, north, south, key_bias(), own, side, attended, qkv_weight, out_weight, bands.patch_matrix()] + consts,
        [
            pltpu.VMEM((2 * bands.slab_padded, width), BF16),
            pltpu.VMEM((2 * bands.slab_padded, 2 * width), BF16),
            pltpu.VMEM((bands.own_total, width), BF16),
        ]
        + attend_scratch(bands, edges, block),
        6 * 10**9,
        "edge_attention",
        exps=300000,
    )


def shift(part, axis, step, wrap):
    size = lax.axis_size(axis)
    pairs = [(i, (i + step) % size) for i in range(size) if wrap or 0 <= i + step < size]
    return lax.ppermute(part, axis, pairs)


def key_bias():
    row = jnp.arange(8, dtype=jnp.int32)[:, None]
    key = jnp.arange(128, dtype=jnp.int32)[None, :] // WLON
    north = (row == 0) & (key < RIM_LAT) & (lax.axis_index("lat") == 0)
    south = (row == 1) & (key >= RIM_LAT) & (lax.axis_index("lat") == lax.axis_size("lat") - 1)
    return jnp.where(north | south, F32(-1e30), F32(0.0))


def place_index():
    me = lax.axis_index("lon")
    return jnp.stack([me // 2, me % 2]).astype(jnp.int32)


def merge_dots(place_ref, upper, lower, mine_ref, pair_ref, x_ref, x_pair_ref, y_ref, y_pair_ref, refs):
    half, block = x_ref.shape
    at = [pl.ds(pl.multiple_of((place_ref[1] + k) % 2 * block, block), block) for k in range(2)]
    own, x, y = refs
    for k, ref in enumerate((mine_ref, pair_ref)):
        own(at[k], dot(upper, ref[:half, :]), dot(lower, ref[half:, :]))
    for k, ref in enumerate((x_ref, x_pair_ref)):
        x(at[k], dot(upper, ref[...]))
    for k, ref in enumerate((y_ref, y_pair_ref)):
        y(at[k], dot(lower, ref[...]))


def merge_own_kernel(place_ref, upper_ref, lower_ref, *refs):
    weights, (own_ref, x_ref, y_ref) = refs[:6], refs[6:]

    def own(at, a, b):
        own_ref[:, at] = a + b

    def x(at, a):
        x_ref[:, at] = a

    def y(at, b):
        y_ref[:, at] = b

    merge_dots(place_ref, upper_ref[...], lower_ref[...], *weights, (own, x, y))


def merge_other_kernel(place_ref, upper_ref, lower_ref, *refs):
    weights, (to_y_ref, to_x_ref) = refs[:6], refs[6:]
    wide = to_x_ref.shape[1] // 2

    def own(at, a, b):
        to_y_ref[:, at] = a.astype(BF16)
        to_x_ref[:, at] = b.astype(BF16)

    def x(at, a):
        to_y_ref[:, pl.ds(pl.multiple_of(wide + at.start, at.size), at.size)] = a.astype(BF16)

    def y(at, b):
        to_x_ref[:, pl.ds(pl.multiple_of(wide + at.start, at.size), at.size)] = b.astype(BF16)

    merge_dots(place_ref, upper_ref[...], lower_ref[...], *weights, (own, x, y))


def combine_kernel(place_ref, own_ref, x_ref, y_ref, from_y_ref, from_x_ref, out_ref):
    wide = own_ref.shape[1]
    chip = place_ref[0]
    from_x, from_y = from_x_ref[...].astype(F32), from_y_ref[...].astype(F32)
    parts = [
        own_ref[...],
        x_ref[...] + from_x[:, :wide],
        y_ref[...] + from_y[:, :wide],
        from_x[:, wide:] + from_y[:, wide:],
    ]
    for m, part in enumerate(parts):
        out_ref[:, pl.ds(pl.multiple_of((chip ^ m) * wide, wide), wide)] = part.astype(BF16)


def local_call(kernel, out, place, args, flops, name, mib=24):
    vmem = pl.BlockSpec(memory_space=pltpu.VMEM)
    return pl.pallas_call(
        kernel,
        in_specs=[pl.BlockSpec(memory_space=pltpu.SMEM)] + [vmem] * len(args),
        out_specs=[vmem] * len(out),
        out_shape=out,
        compiler_params=params(mib),
        cost_estimate=pl.CostEstimate(flops=flops, bytes_accessed=2**20, transcendentals=0),
        name=name,
    )(place, *args)


def merge_by_squares(upper, lower, merge_weight):
    half = merge_weight.shape[0] // 2
    block = merge_weight.shape[1]
    count = upper.shape[0]
    x = chip_swap(merge_weight[:half], 1)
    y = chip_swap(merge_weight[half:], 2)
    weights = [merge_weight, core_swap(merge_weight), x, core_swap(x), y, core_swap(y)]
    place = place_index()
    from_y = chip_swap(upper, 2)
    from_x = chip_swap(lower, 1)
    flops = 16 * count * half * block
    wide = jax.ShapeDtypeStruct((count, 2 * block), F32)
    own = local_call(merge_own_kernel, [wide] * 3, place, [upper, lower] + weights, flops, "merge_own")
    pair = jax.ShapeDtypeStruct((count, 4 * block), BF16)
    to_y, to_x = local_call(merge_other_kernel, [pair] * 2, place, [from_y, from_x] + weights, flops, "merge_other")
    back_y, back_x = chip_swap(to_y, 2), chip_swap(to_x, 1)
    out = jax.ShapeDtypeStruct((count, 8 * block), BF16)
    return local_call(combine_kernel, [out], place, [*own, back_y, back_x], 0, "combine")[0]


def merge(upper, lower, merge_weight):
    if lax.axis_size("lon") == 8:
        return merge_by_squares(upper, lower, merge_weight)
    weight = lax.all_gather(merge_weight, "lon", axis=1, tiled=True)
    return jnp.dot(jnp.concatenate([upper, lower], axis=1), weight, preferred_element_type=F32).astype(BF16)


def ffn_kernel(mine_ref, theirs_ref, up_ref, down_ref, out_mine_ref, out_theirs_ref, normed_ref, hidden_ref):
    count = mine_ref.shape[0]
    for k, ref in enumerate((mine_ref, theirs_ref)):
        normed_ref[k * count : (k + 1) * count, :] = normalize(ref[...].astype(F32)).astype(BF16)
    hidden = hidden_ref.shape[1]
    step = 256
    for at in range(0, hidden, step):
        raw = dot(normed_ref[...], up_ref[:, at : at + step])
        active = 0.5 * raw * (1.0 + lax.erf(raw * np.float32(np.sqrt(0.5))))
        hidden_ref[:, at : at + step] = active.astype(BF16)
    for at in range(0, down_ref.shape[1], step):
        out = dot(hidden_ref[...], down_ref[:, at : at + step]).astype(BF16)
        out_mine_ref[:, at : at + step] = out[:count]
        out_theirs_ref[:, at : at + step] = out[count:]


def feed_forward(mine, theirs, up, down):
    count, width = mine.shape
    hidden = up.shape[1]
    vmem = pl.BlockSpec(memory_space=pltpu.VMEM)
    return pl.pallas_call(
        ffn_kernel,
        in_specs=[vmem] * 4,
        out_specs=[vmem] * 2,
        out_shape=[jax.ShapeDtypeStruct((count, width), BF16)] * 2,
        scratch_shapes=[pltpu.VMEM((2 * count, width), BF16), pltpu.VMEM((2 * count, hidden), BF16)],
        compiler_params=params(24),
        cost_estimate=pl.CostEstimate(
            flops=8 * count * width * hidden, bytes_accessed=4 * width * hidden, transcendentals=2 * count * hidden
        ),
        name="feed_forward",
    )(mine, theirs, up, down)


def core_swap(value):
    size = lax.axis_size("lon")
    return lax.ppermute(value, "lon", [(i, i ^ 1) for i in range(size)])


def chip_swap(value, offset):
    size = lax.axis_size("lon")
    return lax.ppermute(value, "lon", [(i, i ^ (2 * offset)) for i in range(size)])


def per_device(tokens, qkv_weight, out_weight, merge_weight, up_weight, down_weight):
    rows, columns, width = tokens.shape
    bands = Bands(rows, columns)
    cells = rows * columns // 4
    middle_out, upper, lower = attention(bands, tokens, qkv_weight, out_weight)
    coarse = merge(upper, lower, merge_weight)
    chips = lax.axis_size("lon") // 2
    arrived = [coarse] + [chip_swap(coarse, m) for m in range(1, chips)]
    total = coarse.astype(F32)
    for m in range(chips):
        mine, theirs = feed_forward(arrived[m], core_swap(arrived[m]), up_weight, down_weight)
        summed = mine.astype(F32) + core_swap(theirs).astype(F32)
        if m:
            summed = chip_swap(summed.astype(BF16), m).astype(F32)
        total = total + summed
    coarse_out = total[:cells].astype(jnp.bfloat16)
    return (middle_out, coarse_out.reshape(rows // 2, columns // 2, -1))


def solution(mesh):
    return jax.shard_map(
        per_device,
        mesh=mesh,
        in_specs=(P("lat", "lon", None), P(), P(), P(None, "lon"), P(None, "lon"), P("lon", None)),
        out_specs=(P("lat", "lon", None), P("lat", "lon", None)),
        check_vma=False,
    )
```

time: 313 us -> 140 us (0.45)
  the two profiles are of different devices: /device:TPU:4 before, /device:TPU:0 now
where the time goes in v2:
time: 140 us
  waiting for transfers between devices  59.8 us (43%)
  Pallas kernels  37.7 us (27%)
  starting transfers between devices  26.4 us (19%)
  local copies, waits for them, and re-layouts  14 us (10%)
    ppermute x12, waiting for transfers between devices, chip_swap(): lax.ppermute(value, 'lon', [(i, i ^ 2 * offset) for i in range(size)])  59.7 us
    pallas_call x3, Pallas kernels, vmem_call(): pl.pallas_call(kernel, in_specs=[vmem] * len(args), out_specs=[vmem] * le...  18.1 us
    ppermute x12, starting transfers between devices, chip_swap(): lax.ppermute(value, 'lon', [(i, i ^ 2 * offset) for i in range(size)])  14.8 us
    pallas_call x4, Pallas kernels, feed_forward(): pl.pallas_call(ffn_kernel, in_specs=[vmem] * 4, out_specs=[vmem] * 2, out...  10.4 us
    pallas_call x3, Pallas kernels, local_call(): pl.pallas_call(kernel, in_specs=[pl.BlockSpec(memory_space=pltpu.SMEM)] +...  9.18 us
    unnamed x42, local copies, waits for them, and re-layouts  8.91 us
    ppermute x4, starting transfers between devices, shift(): return lax.ppermute(part, axis, pairs)  8.49 us
    ppermute x11, starting transfers between devices, core_swap(): return lax.ppermute(value, 'lon', [(i, i ^ 1) for i in range(size)])  3.08 us
  transfers between devices with their start and end apart: 27, of which 10 were waited for; matrix products, arithmetic and copies ran while one was open for 3% of the time, Pallas kernels for 24%

profile of v2, /device:TPU:0, one launch (start us, length us, event | category | flops | bytes accessed | tf_op | source)
XLA Modules:
  0.0 140.0 jit_solution(8571456773051293637)
XLA Ops:
  0.6 1.1 fusion.7
  1.7 3.4 %collective-permute-start.1 = (bf16[18,8,1024]{2,1,0:T(8,128)(2,1)S(1)}, bf16[18,8,1024]{2,1,0:T(8,128)(2,1)S(1)}, u32[]{:S(2)}, u32[]{:S(2)}) collective-permute-start(bf16[18,8,1024]{2,1,0:T(8,128)(2,1)S(1)} %get-tuple-element.43), channel_id=1, source_target_pairs={{0,7},{1,0},{2,1},{3,2},{4,3},{5,4},{6,5},{7,6},{8,15},{9,8},{10,9... | collective-permute-start | bytes 884744 | tf_op jit(solution)/shard_map/ppermute | solution.py:342
  5.1 3.1 %fusion.5 = (bf16[2048,256]{1,0:T(8,128)(2,1)}, bf16[2048,256]{1,0:T(8,128)(2,1)}) fusion(bf16[4096,256]{1,0:T(8,128)(2,1)} %refs_0_.3), kind=kLoop, calls=%fused_computation.21 | loop fusion | bytes 4194304 | tf_op jit(solution)/shard_map/slice | solution.py:434
  8.2 2.0 %collective-permute-start.5 = (bf16[2048,256]{1,0:T(8,128)(2,1)}, bf16[2048,256]{1,0:T(8,128)(2,1)S(1)}, u32[]{:S(2)}, u32[]{:S(2)}) collective-permute-start(bf16[2048,256]{1,0:T(8,128)(2,1)} %get-tuple-element.39), channel_id=1, source_target_pairs={{0,2},{1,3},{2,0},{3,1},{4,6},{5,7},{6,4},{7,5},{8,10},{9,11},{10,... | collective-permute-start | bytes 3145736 | tf_op jit(solution)/shard_map/ppermute | solution.py:497
  10.2 1.5 %collective-permute-start.7 = (bf16[2048,256]{1,0:T(8,128)(2,1)}, bf16[2048,256]{1,0:T(8,128)(2,1)}, u32[]{:S(2)}, u32[]{:S(2)}) collective-permute-start(bf16[2048,256]{1,0:T(8,128)(2,1)} %get-tuple-element.38), channel_id=1, source_target_pairs={{0,4},{1,5},{2,6},{3,7},{4,0},{5,1},{6,2},{7,3},{8,12},{9,13},{10,... | collective-permute-start | bytes 3145736 | tf_op jit(solution)/shard_map/ppermute | solution.py:497
  11.7 0.0 copy-start.5
  11.7 2.8 %copy-done.5 = bf16[1024,3072]{1,0:T(8,128)(2,1)S(1)} copy-done((bf16[1024,3072]{1,0:T(8,128)(2,1)S(1)}, bf16[1024,3072]{1,0:T(8,128)(2,1)}, u32[]{:S(2)}) %copy-start.5) | copy-done | bytes 6291480
  14.5 3.4 %own_projection.1.own_ref = bf16[448,3072]{1,0:T(8,128)(2,1)S(1)} custom-call(bf16[18,24,1024]{2,1,0:T(8,128)(2,1)S(1)} %copy-done.3, bf16[1024,3072]{1,0:T(8,128)(2,1)S(1)} %copy-done.5), custom_call_target="tpu_custom_call" | custom-call | flops 2818572288 | bytes 1048576 | tf_op jit(solution)/shard_map/own_projection/pallas_call | solution.py:278
  18.0 1.5 %copy-done.18 = bf16[448,3072]{1,0:T(8,128)(2,1)} copy-done((bf16[448,3072]{1,0:T(8,128)(2,1)}, bf16[448,3072]{1,0:T(8,128)(2,1)S(1)}, u32[]{:S(2)}) %copy-start.18) | copy-done | bytes 2752536
  19.5 0.1 or_select_fusion.bias_ref
  19.6 3.5 %collective-permute-start.2 = (bf16[3,40,1024]{2,1,0:T(8,128)(2,1)S(1)}, bf16[3,40,1024]{2,1,0:T(8,128)(2,1)S(1)}, u32[]{:S(2)}, u32[]{:S(2)}) collective-permute-start(bf16[3,40,1024]{2,1,0:T(8,128)(2,1)S(1)} %pad_maximum_fusion), channel_id=1, source_target_pairs={{0,8},{8,16},{16,24},{1,9},{9,17},{17,25},{2,10},{10,18},{18,26},{... | collective-permute-start | bytes 737288 | tf_op jit(solution)/shard_map/ppermute | solution.py:342
  23.1 0.0 copy-start.8
  23.2 0.0 copy-start.4
  23.2 1.6 %collective-permute-start.3 = (bf16[3,40,1024]{2,1,0:T(8,128)(2,1)S(1)}, bf16[3,40,1024]{2,1,0:T(8,128)(2,1)S(1)}, u32[]{:S(2)}, u32[]{:S(2)}) collective-permute-start(bf16[3,40,1024]{2,1,0:T(8,128)(2,1)S(1)} %pad_maximum_fusion.1), channel_id=1, source_target_pairs={{8,0},{16,8},{24,16},{9,1},{17,9},{25,17},{10,2},{18,10},{26,18},{... | collective-permute-start | bytes 737288 | tf_op jit(solution)/shard_map/ppermute | solution.py:342
  24.8 9.7 %collective-permute-done.5.refs_2_ = bf16[2048,256]{1,0:T(8,128)(2,1)S(1)} collective-permute-done((bf16[2048,256]{1,0:T(8,128)(2,1)}, bf16[2048,256]{1,0:T(8,128)(2,1)S(1)}, u32[]{:S(2)}, u32[]{:S(2)}) %collective-permute-start.5) | collective-permute-done | bytes 1048608 | tf_op jit(solution)/shard_map/ppermute | solution.py:497
  34.5 0.8 collective-permute-start.6
  35.3 0.8 collective-permute-done.7.refs_4_
  36.1 0.0 copy-start.6
  36.2 2.8 %copy-done.6 = bf16[1024,3072]{1,0:T(8,128)(2,1)S(1)} copy-done((bf16[1024,3072]{1,0:T(8,128)(2,1)S(1)}, bf16[1024,3072]{1,0:T(8,128)(2,1)}, u32[]{:S(2)}) %copy-start.6) | copy-done | bytes 6291480
  38.9 1.8 %copy-done.19 = bf16[448,3072]{1,0:T(8,128)(2,1)S(1)} copy-done((bf16[448,3072]{1,0:T(8,128)(2,1)S(1)}, bf16[448,3072]{1,0:T(8,128)(2,1)}, u32[]{:S(2)}) %copy-start.19) | copy-done | bytes 2752536
  40.7 0.0 copy-start.16
  40.7 0.0 copy-start.17
  40.8 5.0 %middle_attention.1 = (bf16[288,2048]{1,0:T(8,128)(2,1)S(1)}, bf16[288,1024]{1,0:T(8,128)(2,1)S(1)}) custom-call(bf16[18,8,1024]{2,1,0:T(8,128)(2,1)S(1)} %collective-permute-done.west_ref, bf16[18,8,1024]{2,1,0:T(8,128)(2,1)S(1)} %collective-permute-done.1.east_ref, bf16[448,3072]{1,0:T(8,128)(2,1)S(1)} %copy-done.19, bf16[1024,3072]{1,0:T(8,128)(2,1)S(1)} %copy-done.6, ...), custom_call_target="tpu_custom_call" | custom-call | flops 5000000000 | bytes 1048576 | tf_op jit(solution)/shard_map/middle_attention/pallas_call | solution.py:278
  45.9 0.0 copy-start.2
  45.9 9.6 %edge_attention.1 = (bf16[18,24,1024]{2,1,0:T(8,128)(2,1)}, bf16[112,2048]{1,0:T(8,128)(2,1)}, bf16[112,2048]{1,0:T(8,128)(2,1)}) custom-call(bf16[18,24,1024]{2,1,0:T(8,128)(2,1)S(1)} %copy-done.4, bf16[3,40,1024]{2,1,0:T(8,128)(2,1)S(1)} %collective-permute-done.2.north_ref, bf16[3,40,1024]{2,1,0:T(8,128)(2,1)S(1)} %collective-permute-done.3.south_ref, ...), custom_call_target="tpu_custom_call" | custom-call | flops 6000000000 | bytes 1048576 | tf_op jit(solution)/shard_map/edge_attention/pallas_call | solution.py:278
  55.5 0.9 collective-permute-start.9
  56.4 1.5 %collective-permute-start.10 = (bf16[112,2048]{1,0:T(8,128)(2,1)}, bf16[112,2048]{1,0:T(8,128)(2,1)}, u32[]{:S(2)}, u32[]{:S(2)}) collective-permute-start(bf16[112,2048]{1,0:T(8,128)(2,1)} %get-tuple-element.24.lower_ref), channel_id=1, source_target_pairs={{0,2},{1,3},{2,0},{3,1},{4,6},{5,7},{6,4},{7,5},{8,10},{9,11},{10,... | collective-permute-start | bytes 1376264 | tf_op jit(solution)/shard_map/ppermute | solution.py:497
  57.9 0.1 pad_add_fusion.place_ref
  58.0 10.8 %collective-permute-done.9.upper_ref = bf16[112,2048]{1,0:T(8,128)(2,1)} collective-permute-done((bf16[112,2048]{1,0:T(8,128)(2,1)}, bf16[112,2048]{1,0:T(8,128)(2,1)}, u32[]{:S(2)}, u32[]{:S(2)}) %collective-permute-start.9) | collective-permute-done | bytes 458784 | tf_op jit(solution)/shard_map/ppermute | solution.py:497
  68.8 0.6 collective-permute-done.10.lower_ref
  69.4 4.1 %merge_other.1 = (bf16[112,1024]{1,0:T(8,128)(2,1)S(1)}, bf16[112,1024]{1,0:T(8,128)(2,1)S(1)}) custom-call(s32[2]{0:T(128)S(1)} %pad_add_fusion.place_ref, bf16[112,2048]{1,0:T(8,128)(2,1)} %collective-permute-done.9.upper_ref, bf16[112,2048]{1,0:T(8,128)(2,1)} %collective-permute-done.10.lower_ref, bf16[4096,256]{1,0:T(8,128)(2,1)S(1)} %copy-done.2, ...), custom_call_target="tpu_custom_call" | custom-call | flops 939524096 | bytes 1048576 | tf_op jit(solution)/shard_map/merge_other/pallas_call | solution.py:418
  73.5 1.2 collective-permute-start.11
  74.7 0.5 collective-permute-start.12
  75.2 4.4 %merge_own.1 = (f32[112,512]{1,0:T(8,128)S(1)}, f32[112,512]{1,0:T(8,128)S(1)}, f32[112,512]{1,0:T(8,128)S(1)}) custom-call(s32[2]{0:T(128)S(1)} %pad_add_fusion.place_ref, bf16[112,2048]{1,0:T(8,128)(2,1)} %get-tuple-element.23.upper_ref, bf16[112,2048]{1,0:T(8,128)(2,1)} %get-tuple-element.24.lower_ref, bf16[4096,256]{1,0:T(8,128)(2,1)S(1)} %copy-done.2, ...), custom_call_target="tpu_custom_call" | custom-call | flops 939524096 | bytes 1048576 | tf_op jit(solution)/shard_map/merge_own/pallas_call | solution.py:418
  79.7 0.8 collective-permute-done.11.from_y_ref
  80.4 0.9 collective-permute-done.12.from_x_ref
  81.3 0.6 combine.1.mine_ref
  82.0 1.2 collective-permute-start.23
  83.1 0.7 collective-permute-start.19
  83.8 1.7 %collective-permute-start.15 = (bf16[112,2048]{1,0:T(8,128)(2,1)S(1)}, bf16[112,2048]{1,0:T(8,128)(2,1)S(1)}, u32[]{:S(2)}, u32[]{:S(2)}) collective-permute-start(bf16[112,2048]{1,0:T(8,128)(2,1)S(1)} %combine.1.mine_ref), channel_id=1, source_target_pairs={{0,2},{1,3},{2,0},{3,1},{4,6},{5,7},{6,4},{7,5},{8,10},{9,11},{10,... | collective-permute-start | bytes 1376264 | tf_op jit(solution)/shard_map/ppermute | solution.py:497
  85.5 10.9 %collective-permute-done.23.mine_ref = bf16[112,2048]{1,0:T(8,128)(2,1)S(1)} collective-permute-done((bf16[112,2048]{1,0:T(8,128)(2,1)S(1)}, bf16[112,2048]{1,0:T(8,128)(2,1)S(1)}, u32[]{:S(2)}, u32[]{:S(2)}) %collective-permute-start.23) | collective-permute-done | bytes 458784 | tf_op jit(solution)/shard_map/ppermute | solution.py:497
  96.4 0.5 collective-permute-start.13
  96.9 6.1 %collective-permute-done.19.mine_ref = bf16[112,2048]{1,0:T(8,128)(2,1)S(1)} collective-permute-done((bf16[112,2048]{1,0:T(8,128)(2,1)S(1)}, bf16[112,2048]{1,0:T(8,128)(2,1)S(1)}, u32[]{:S(2)}, u32[]{:S(2)}) %collective-permute-start.19) | collective-permute-done | bytes 458784 | tf_op jit(solution)/shard_map/ppermute | solution.py:497
  103.0 0.5 collective-permute-start.16
  103.5 2.6 %feed_forward.7 = (bf16[112,2048]{1,0:T(8,128)(2,1)S(1)}, bf16[112,2048]{1,0:T(8,128)(2,1)S(1)}) custom-call(bf16[112,2048]{1,0:T(8,128)(2,1)S(1)} %collective-permute-done.23.mine_ref, bf16[112,2048]{1,0:T(8,128)(2,1)S(1)} %collective-permute-done.24.theirs_ref, bf16[2048,1024]{1,0:T(8,128)(2,1)S(1)} %copy-done, bf16[1024,2048]{1,0:T(8,128)(2,1)S(1)} %copy-done.1), custom_call_target="tpu_custom_call" | custom-call | flops 1879048192 | bytes 8388608 | tf_op jit(solution)/shard_map/feed_forward/pallas_call | solution.py:476
  106.2 0.1 collective-permute-start.25
  106.3 2.6 %feed_forward.4 = (bf16[112,2048]{1,0:T(8,128)(2,1)S(1)}, bf16[112,2048]{1,0:T(8,128)(2,1)S(1)}) custom-call(bf16[112,2048]{1,0:T(8,128)(2,1)S(1)} %combine.1.mine_ref, bf16[112,2048]{1,0:T(8,128)(2,1)S(1)} %collective-permute-done.13.theirs_ref, bf16[2048,1024]{1,0:T(8,128)(2,1)S(1)} %copy-done, bf16[1024,2048]{1,0:T(8,128)(2,1)S(1)} %copy-done.1), custom_call_target="tpu_custom_call" | custom-call | flops 1879048192 | bytes 8388608 | tf_op jit(solution)/shard_map/feed_forward/pallas_call | solution.py:476
  108.9 0.5 collective-permute-start.14
  109.4 2.6 %feed_forward.6 = (bf16[112,2048]{1,0:T(8,128)(2,1)S(1)}, bf16[112,2048]{1,0:T(8,128)(2,1)S(1)}) custom-call(bf16[112,2048]{1,0:T(8,128)(2,1)S(1)} %collective-permute-done.19.mine_ref, bf16[112,2048]{1,0:T(8,128)(2,1)S(1)} %collective-permute-done.20.theirs_ref, bf16[2048,1024]{1,0:T(8,128)(2,1)S(1)} %copy-done, bf16[1024,2048]{1,0:T(8,128)(2,1)S(1)} %copy-done.1), custom_call_target="tpu_custom_call" | custom-call | flops 1879048192 | bytes 8388608 | tf_op jit(solution)/shard_map/feed_forward/pallas_call | solution.py:476
  112.0 0.1 collective-permute-start.21
  112.1 2.6 %feed_forward.5 = (bf16[112,2048]{1,0:T(8,128)(2,1)S(1)}, bf16[112,2048]{1,0:T(8,128)(2,1)S(1)}) custom-call(bf16[112,2048]{1,0:T(8,128)(2,1)S(1)} %collective-permute-done.15.mine_ref, bf16[112,2048]{1,0:T(8,128)(2,1)S(1)} %collective-permute-done.16.theirs_ref, bf16[2048,1024]{1,0:T(8,128)(2,1)S(1)} %copy-done, bf16[1024,2048]{1,0:T(8,128)(2,1)S(1)} %copy-done.1), custom_call_target="tpu_custom_call" | custom-call | flops 1879048192 | bytes 8388608 | tf_op jit(solution)/shard_map/feed_forward/pallas_call | solution.py:476
  114.7 0.6 collective-permute-start.17
  115.3 0.1 add_convert_fusion
  115.4 1.2 collective-permute-start.26
  116.7 0.1 add_convert_fusion.1
  116.8 1.2 collective-permute-start.22
  118.0 0.1 add_convert_fusion.2
  118.1 1.2 collective-permute-start.18
  119.3 0.1 convert_element_type.47
  119.4 0.1 convert_element_type.48
  119.5 10.3 %collective-permute-done.26 = bf16[112,2048]{1,0:T(8,128)(2,1)S(1)} collective-permute-done((bf16[112,2048]{1,0:T(8,128)(2,1)S(1)}, bf16[112,2048]{1,0:T(8,128)(2,1)S(1)}, u32[]{:S(2)}, u32[]{:S(2)}) %collective-permute-start.26) | collective-permute-done | bytes 458784 | tf_op jit(solution)/shard_map/ppermute | solution.py:497
  129.8 8.9 %collective-permute-done.22 = bf16[112,2048]{1,0:T(8,128)(2,1)S(1)} collective-permute-done((bf16[112,2048]{1,0:T(8,128)(2,1)S(1)}, bf16[112,2048]{1,0:T(8,128)(2,1)S(1)}, u32[]{:S(2)}, u32[]{:S(2)}) %collective-permute-start.22) | collective-permute-done | bytes 458784 | tf_op jit(solution)/shard_map/ppermute | solution.py:497
  138.7 0.4 fusion.4
  139.1 0.9 reshape.45
  (60 shorter events, 0.2 us)
Async XLA Ops:
  1.7 17.8 %collective-permute-start.1 = (bf16[18,8,1024]{2,1,0:T(8,128)(2,1)S(1)}, bf16[18,8,1024]{2,1,0:T(8,128)(2,1)S(1)}, u32[]{:S(2)}, u32[]{:S(2)}) collective-permute-start(bf16[18,8,1024]{2,1,0:T(8,128)(2,1)S(1)} %get-tuple-element.43), channel_id=1, source_target_pairs={{0,7},{1,0},{2,1},{3,2},{4,3},{5,4},{6,5},{7,6},{8,15},{9,8},{10,9... | collective-permute-start | bytes 884744 | tf_op jit(solution)/shard_map/ppermute | solution.py:342
  5.1 6.6 %copy-start.3 = (bf16[18,24,1024]{2,1,0:T(8,128)(2,1)S(1)}, bf16[18,24,1024]{2,1,0:T(8,128)(2,1)}, u32[]{:S(2)}) copy-start(bf16[18,24,1024]{2,1,0:T(8,128)(2,1)} %tokens_ref.3) | copy-start | bytes 2654212
  5.1 14.5 %collective-permute-start = (bf16[18,8,1024]{2,1,0:T(8,128)(2,1)S(1)}, bf16[18,8,1024]{2,1,0:T(8,128)(2,1)S(1)}, u32[]{:S(2)}, u32[]{:S(2)}) collective-permute-start(bf16[18,8,1024]{2,1,0:T(8,128)(2,1)S(1)} %get-tuple-element.42), channel_id=1, source_target_pairs={{0,1},{1,2},{2,3},{3,4},{4,5},{5,6},{6,7},{7,0},{8,9},{9,10},{10,1... | collective-permute-start | bytes 884744 | tf_op jit(solution)/shard_map/ppermute | solution.py:342
  5.1 64.2 %collective-permute-start.4 = (bf16[4096,256]{1,0:T(8,128)(2,1)}, bf16[4096,256]{1,0:T(8,128)(2,1)}, u32[]{:S(2)}, u32[]{:S(2)}) collective-permute-start(bf16[4096,256]{1,0:T(8,128)(2,1)} %refs_0_.3), channel_id=1, source_target_pairs={{0,1},{1,0},{2,3},{3,2},{4,5},{5,4},{6,7},{7,6},{8,9},{9,8},{10,11... | collective-permute-start | bytes 6291464 | tf_op jit(solution)/shard_map/ppermute | solution.py:492
  8.2 26.3 %collective-permute-start.5 = (bf16[2048,256]{1,0:T(8,128)(2,1)}, bf16[2048,256]{1,0:T(8,128)(2,1)S(1)}, u32[]{:S(2)}, u32[]{:S(2)}) collective-permute-start(bf16[2048,256]{1,0:T(8,128)(2,1)} %get-tuple-element.39), channel_id=1, source_target_pairs={{0,2},{1,3},{2,0},{3,1},{4,6},{5,7},{6,4},{7,5},{8,10},{9,11},{10,... | collective-permute-start | bytes 3145736 | tf_op jit(solution)/shard_map/ppermute | solution.py:497
  10.2 25.9 %collective-permute-start.7 = (bf16[2048,256]{1,0:T(8,128)(2,1)}, bf16[2048,256]{1,0:T(8,128)(2,1)}, u32[]{:S(2)}, u32[]{:S(2)}) collective-permute-start(bf16[2048,256]{1,0:T(8,128)(2,1)} %get-tuple-element.38), channel_id=1, source_target_pairs={{0,4},{1,5},{2,6},{3,7},{4,0},{5,1},{6,2},{7,3},{8,12},{9,13},{10,... | collective-permute-start | bytes 3145736 | tf_op jit(solution)/shard_map/ppermute | solution.py:497
  11.7 2.8 %copy-start.5 = (bf16[1024,3072]{1,0:T(8,128)(2,1)S(1)}, bf16[1024,3072]{1,0:T(8,128)(2,1)}, u32[]{:S(2)}) copy-start(bf16[1024,3072]{1,0:T(8,128)(2,1)} %weight_ref.5) | copy-start | bytes 18874372
  14.5 21.6 %copy-start.9 = (bf16[576,144]{1,0:T(8,128)(2,1)S(1)}, bf16[576,144]{1,0:T(8,128)(2,1)}, u32[]{:S(2)}) copy-start(bf16[576,144]{1,0:T(8,128)(2,1)} %constant.71.clone.rest_1_) | copy-start | bytes 497668
  14.5 21.6 %copy-start.10 = (bf16[576,256]{1,0:T(8,128)(2,1)S(1)}, bf16[576,256]{1,0:T(8,128)(2,1)}, u32[]{:S(2)}) copy-start(bf16[576,256]{1,0:T(8,128)(2,1)} %constant.72.clone.rest_2_) | copy-start | bytes 884740
  14.5 21.6 %copy-start.11 = (bf16[144,576]{1,0:T(8,128)(2,1)S(1)}, bf16[144,576]{1,0:T(8,128)(2,1)}, u32[]{:S(2)}) copy-start(bf16[144,576]{1,0:T(8,128)(2,1)} %constant.73.clone.rest_3_) | copy-start | bytes 497668
  14.5 21.6 %copy-start.15 = (bf16[240,240]{1,0:T(8,128)(2,1)S(1)}, bf16[240,240]{1,0:T(8,128)(2,1)}, u32[]{:S(2)}) copy-start(bf16[240,240]{1,0:T(8,128)(2,1)} %constant.70.clone.rest_0_) | copy-start | bytes 345604
  17.9 1.5 %copy-start.18 = (bf16[448,3072]{1,0:T(8,128)(2,1)}, bf16[448,3072]{1,0:T(8,128)(2,1)S(1)}, u32[]{:S(2)}) copy-start(bf16[448,3072]{1,0:T(8,128)(2,1)S(1)} %own_projection.1.own_ref) | copy-start | bytes 8257540
  19.6 26.2 %collective-permute-start.2 = (bf16[3,40,1024]{2,1,0:T(8,128)(2,1)S(1)}, bf16[3,40,1024]{2,1,0:T(8,128)(2,1)S(1)}, u32[]{:S(2)}, u32[]{:S(2)}) collective-permute-start(bf16[3,40,1024]{2,1,0:T(8,128)(2,1)S(1)} %pad_maximum_fusion), channel_id=1, source_target_pairs={{0,8},{8,16},{16,24},{1,9},{9,17},{17,25},{2,10},{10,18},{18,26},{... | collective-permute-start | bytes 737288 | tf_op jit(solution)/shard_map/ppermute | solution.py:342
  23.1 22.7 %copy-start.8 = (bf16[448,432]{1,0:T(8,128)(2,1)S(1)}, bf16[448,432]{1,0:T(8,128)(2,1)}, u32[]{:S(2)}) copy-start(bf16[448,432]{1,0:T(8,128)(2,1)} %constant.74.clone.patch_ref) | copy-start | bytes 1161220
  23.2 22.7 %copy-start.4 = (bf16[18,24,1024]{2,1,0:T(8,128)(2,1)S(1)}, bf16[18,24,1024]{2,1,0:T(8,128)(2,1)}, u32[]{:S(2)}) copy-start(bf16[18,24,1024]{2,1,0:T(8,128)(2,1)} %tokens_ref.3) | copy-start | bytes 2654212
  23.2 22.6 %collective-permute-start.3 = (bf16[3,40,1024]{2,1,0:T(8,128)(2,1)S(1)}, bf16[3,40,1024]{2,1,0:T(8,128)(2,1)S(1)}, u32[]{:S(2)}, u32[]{:S(2)}) collective-permute-start(bf16[3,40,1024]{2,1,0:T(8,128)(2,1)S(1)} %pad_maximum_fusion.1), channel_id=1, source_target_pairs={{8,0},{16,8},{24,16},{9,1},{17,9},{25,17},{10,2},{18,10},{26,18},{... | collective-permute-start | bytes 737288 | tf_op jit(solution)/shard_map/ppermute | solution.py:342
  34.5 34.9 %collective-permute-start.6 = (bf16[2048,256]{1,0:T(8,128)(2,1)S(1)}, bf16[2048,256]{1,0:T(8,128)(2,1)}, u32[]{:S(2)}, u32[]{:S(2)}) collective-permute-start(bf16[2048,256]{1,0:T(8,128)(2,1)S(1)} %collective-permute-done.5.refs_2_), channel_id=1, source_target_pairs={{0,1},{1,0},{2,3},{3,2},{4,5},{5,4},{6,7},{7,6},{8,9},{9,8},{10,11... | collective-permute-start | bytes 3145736 | tf_op jit(solution)/shard_map/ppermute | solution.py:492
  36.1 33.3 %collective-permute-start.8 = (bf16[2048,256]{1,0:T(8,128)(2,1)}, bf16[2048,256]{1,0:T(8,128)(2,1)}, u32[]{:S(2)}, u32[]{:S(2)}) collective-permute-start(bf16[2048,256]{1,0:T(8,128)(2,1)} %collective-permute-done.7.refs_4_), channel_id=1, source_target_pairs={{0,1},{1,0},{2,3},{3,2},{4,5},{5,4},{6,7},{7,6},{8,9},{9,8},{10,11... | collective-permute-start | bytes 3145736 | tf_op jit(solution)/shard_map/ppermute | solution.py:492
  36.1 2.8 %copy-start.6 = (bf16[1024,3072]{1,0:T(8,128)(2,1)S(1)}, bf16[1024,3072]{1,0:T(8,128)(2,1)}, u32[]{:S(2)}) copy-start(bf16[1024,3072]{1,0:T(8,128)(2,1)} %weight_ref.5) | copy-start | bytes 18874372
  38.9 1.8 %copy-start.19 = (bf16[448,3072]{1,0:T(8,128)(2,1)S(1)}, bf16[448,3072]{1,0:T(8,128)(2,1)}, u32[]{:S(2)}) copy-start(bf16[448,3072]{1,0:T(8,128)(2,1)} %copy-done.18) | copy-start | bytes 8257540
  40.7 5.1 %copy-start.7 = (bf16[1024,1024]{1,0:T(8,128)(2,1)S(1)}, bf16[1024,1024]{1,0:T(8,128)(2,1)}, u32[]{:S(2)}) copy-start(bf16[1024,1024]{1,0:T(8,128)(2,1)} %out_w_ref.1) | copy-start | bytes 6291460
  40.7 5.1 %copy-start.12 = (bf16[304,256]{1,0:T(8,128)(2,1)S(1)}, bf16[304,256]{1,0:T(8,128)(2,1)}, u32[]{:S(2)}) copy-start(bf16[304,256]{1,0:T(8,128)(2,1)} %constant.77.clone.rest_2_.rest_6_) | copy-start | bytes 466948
  40.7 5.1 %copy-start.13 = (bf16[240,256]{1,0:T(8,128)(2,1)S(1)}, bf16[240,256]{1,0:T(8,128)(2,1)}, u32[]{:S(2)}) copy-start(bf16[240,256]{1,0:T(8,128)(2,1)} %constant.75.clone.rest_0_) | copy-start | bytes 368644
  40.7 5.2 %copy-start.14 = (bf16[240,256]{1,0:T(8,128)(2,1)S(1)}, bf16[240,256]{1,0:T(8,128)(2,1)}, u32[]{:S(2)}) copy-start(bf16[240,256]{1,0:T(8,128)(2,1)} %constant.79.clone.rest_4_) | copy-start | bytes 368644
  40.7 5.2 %copy-start.16 = (bf16[304,80]{1,0:T(8,128)(2,1)S(1)}, bf16[304,80]{1,0:T(8,128)(2,1)}, u32[]{:S(2)}) copy-start(bf16[304,80]{1,0:T(8,128)(2,1)} %constant.76.clone.rest_1_.rest_5_) | copy-start | bytes 145924
  40.7 5.2 %copy-start.17 = (bf16[80,304]{1,0:T(8,128)(2,1)S(1)}, bf16[80,304]{1,0:T(8,128)(2,1)}, u32[]{:S(2)}) copy-start(bf16[80,304]{1,0:T(8,128)(2,1)} %constant.78.clone.rest_3_.rest_7_) | copy-start | bytes 145924
  40.7 5.2 %copy-start.20 = (bf16[448,3072]{1,0:T(8,128)(2,1)S(1)}, bf16[448,3072]{1,0:T(8,128)(2,1)}, u32[]{:S(2)}) copy-start(bf16[448,3072]{1,0:T(8,128)(2,1)} %copy-done.18) | copy-start | bytes 8257540
  45.9 23.5 %copy-start.2 = (bf16[4096,256]{1,0:T(8,128)(2,1)S(1)}, bf16[4096,256]{1,0:T(8,128)(2,1)}, u32[]{:S(2)}) copy-start(bf16[4096,256]{1,0:T(8,128)(2,1)} %refs_0_.3) | copy-start | bytes 6291460
  55.5 13.2 %collective-permute-start.9 = (bf16[112,2048]{1,0:T(8,128)(2,1)}, bf16[112,2048]{1,0:T(8,128)(2,1)}, u32[]{:S(2)}, u32[]{:S(2)}) collective-permute-start(bf16[112,2048]{1,0:T(8,128)(2,1)} %get-tuple-element.23.upper_ref), channel_id=1, source_target_pairs={{0,4},{1,5},{2,6},{3,7},{4,0},{5,1},{6,2},{7,3},{8,12},{9,13},{10,... | collective-permute-start | bytes 1376264 | tf_op jit(solution)/shard_map/ppermute | solution.py:497
  56.4 13.0 %collective-permute-start.10 = (bf16[112,2048]{1,0:T(8,128)(2,1)}, bf16[112,2048]{1,0:T(8,128)(2,1)}, u32[]{:S(2)}, u32[]{:S(2)}) collective-permute-start(bf16[112,2048]{1,0:T(8,128)(2,1)} %get-tuple-element.24.lower_ref), channel_id=1, source_target_pairs={{0,2},{1,3},{2,0},{3,1},{4,6},{5,7},{6,4},{7,5},{8,10},{9,11},{10,... | collective-permute-start | bytes 1376264 | tf_op jit(solution)/shard_map/ppermute | solution.py:497
  73.5 6.9 %collective-permute-start.11 = (bf16[112,1024]{1,0:T(8,128)(2,1)S(1)}, bf16[112,1024]{1,0:T(8,128)(2,1)S(1)}, u32[]{:S(2)}, u32[]{:S(2)}) collective-permute-start(bf16[112,1024]{1,0:T(8,128)(2,1)S(1)} %get-tuple-element.28), channel_id=1, source_target_pairs={{0,4},{1,5},{2,6},{3,7},{4,0},{5,1},{6,2},{7,3},{8,12},{9,13},{10,... | collective-permute-start | bytes 688136 | tf_op jit(solution)/shard_map/ppermute | solution.py:497
  74.7 6.7 %collective-permute-start.12 = (bf16[112,1024]{1,0:T(8,128)(2,1)S(1)}, bf16[112,1024]{1,0:T(8,128)(2,1)S(1)}, u32[]{:S(2)}, u32[]{:S(2)}) collective-permute-start(bf16[112,1024]{1,0:T(8,128)(2,1)S(1)} %get-tuple-element.29), channel_id=1, source_target_pairs={{0,2},{1,3},{2,0},{3,1},{4,6},{5,7},{6,4},{7,5},{8,10},{9,11},{10,... | collective-permute-start | bytes 688136 | tf_op jit(solution)/shard_map/ppermute | solution.py:497
  75.2 28.3 %copy-start = (bf16[2048,1024]{1,0:T(8,128)(2,1)S(1)}, bf16[2048,1024]{1,0:T(8,128)(2,1)}, u32[]{:S(2)}) copy-start(bf16[2048,1024]{1,0:T(8,128)(2,1)} %up_ref.7) | copy-start | bytes 12582916
  75.2 28.3 %copy-start.1 = (bf16[1024,2048]{1,0:T(8,128)(2,1)S(1)}, bf16[1024,2048]{1,0:T(8,128)(2,1)}, u32[]{:S(2)}) copy-start(bf16[1024,2048]{1,0:T(8,128)(2,1)} %down_ref.7) | copy-start | bytes 12582916
  82.0 14.4 %collective-permute-start.23 = (bf16[112,2048]{1,0:T(8,128)(2,1)S(1)}, bf16[112,2048]{1,0:T(8,128)(2,1)S(1)}, u32[]{:S(2)}, u32[]{:S(2)}) collective-permute-start(bf16[112,2048]{1,0:T(8,128)(2,1)S(1)} %combine.1.mine_ref), channel_id=1, source_target_pairs={{0,6},{1,7},{2,4},{3,5},{4,2},{5,3},{6,0},{7,1},{8,14},{9,15},{10,... | collective-permute-start | bytes 1376264 | tf_op jit(solution)/shard_map/ppermute | solution.py:497
  83.1 19.9 %collective-permute-start.19 = (bf16[112,2048]{1,0:T(8,128)(2,1)S(1)}, bf16[112,2048]{1,0:T(8,128)(2,1)S(1)}, u32[]{:S(2)}, u32[]{:S(2)}) collective-permute-start(bf16[112,2048]{1,0:T(8,128)(2,1)S(1)} %combine.1.mine_ref), channel_id=1, source_target_pairs={{0,4},{1,5},{2,6},{3,7},{4,0},{5,1},{6,2},{7,3},{8,12},{9,13},{10,... | collective-permute-start | bytes 1376264 | tf_op jit(solution)/shard_map/ppermute | solution.py:497
  83.8 19.2 %collective-permute-start.15 = (bf16[112,2048]{1,0:T(8,128)(2,1)S(1)}, bf16[112,2048]{1,0:T(8,128)(2,1)S(1)}, u32[]{:S(2)}, u32[]{:S(2)}) collective-permute-start(bf16[112,2048]{1,0:T(8,128)(2,1)S(1)} %combine.1.mine_ref), channel_id=1, source_target_pairs={{0,2},{1,3},{2,0},{3,1},{4,6},{5,7},{6,4},{7,5},{8,10},{9,11},{10,... | collective-permute-start | bytes 1376264 | tf_op jit(solution)/shard_map/ppermute | solution.py:497
  96.4 7.1 %collective-permute-start.24 = (bf16[112,2048]{1,0:T(8,128)(2,1)S(1)}, bf16[112,2048]{1,0:T(8,128)(2,1)S(1)}, u32[]{:S(2)}, u32[]{:S(2)}) collective-permute-start(bf16[112,2048]{1,0:T(8,128)(2,1)S(1)} %collective-permute-done.23.mine_ref), channel_id=1, source_target_pairs={{0,1},{1,0},{2,3},{3,2},{4,5},{5,4},{6,7},{7,6},{8,9},{9,8},{10,11... | collective-permute-start | bytes 1376264 | tf_op jit(solution)/shard_map/ppermute | solution.py:492
  96.4 9.9 %collective-permute-start.13 = (bf16[112,2048]{1,0:T(8,128)(2,1)S(1)}, bf16[112,2048]{1,0:T(8,128)(2,1)S(1)}, u32[]{:S(2)}, u32[]{:S(2)}) collective-permute-start(bf16[112,2048]{1,0:T(8,128)(2,1)S(1)} %combine.1.mine_ref), channel_id=1, source_target_pairs={{0,1},{1,0},{2,3},{3,2},{4,5},{5,4},{6,7},{7,6},{8,9},{9,8},{10,11... | collective-permute-start | bytes 1376264 | tf_op jit(solution)/shard_map/ppermute | solution.py:492
  103.0 6.4 %collective-permute-start.20 = (bf16[112,2048]{1,0:T(8,128)(2,1)S(1)}, bf16[112,2048]{1,0:T(8,128)(2,1)S(1)}, u32[]{:S(2)}, u32[]{:S(2)}) collective-permute-start(bf16[112,2048]{1,0:T(8,128)(2,1)S(1)} %collective-permute-done.19.mine_ref), channel_id=1, source_target_pairs={{0,1},{1,0},{2,3},{3,2},{4,5},{5,4},{6,7},{7,6},{8,9},{9,8},{10,11... | collective-permute-start | bytes 1376264 | tf_op jit(solution)/shard_map/ppermute | solution.py:492
  103.0 9.1 %collective-permute-start.16 = (bf16[112,2048]{1,0:T(8,128)(2,1)S(1)}, bf16[112,2048]{1,0:T(8,128)(2,1)S(1)}, u32[]{:S(2)}, u32[]{:S(2)}) collective-permute-start(bf16[112,2048]{1,0:T(8,128)(2,1)S(1)} %collective-permute-done.15.mine_ref), channel_id=1, source_target_pairs={{0,1},{1,0},{2,3},{3,2},{4,5},{5,4},{6,7},{7,6},{8,9},{9,8},{10,11... | collective-permute-start | bytes 1376264 | tf_op jit(solution)/shard_map/ppermute | solution.py:492
  106.2 9.1 %collective-permute-start.25 = (bf16[112,2048]{1,0:T(8,128)(2,1)S(1)}, bf16[112,2048]{1,0:T(8,128)(2,1)S(1)}, u32[]{:S(2)}, u32[]{:S(2)}) collective-permute-start(bf16[112,2048]{1,0:T(8,128)(2,1)S(1)} %get-tuple-element.37), channel_id=1, source_target_pairs={{0,1},{1,0},{2,3},{3,2},{4,5},{5,4},{6,7},{7,6},{8,9},{9,8},{10,11... | collective-permute-start | bytes 1376264 | tf_op jit(solution)/shard_map/ppermute | solution.py:492
  108.9 10.6 %collective-permute-start.14 = (bf16[112,2048]{1,0:T(8,128)(2,1)S(1)}, bf16[112,2048]{1,0:T(8,128)(2,1)S(1)}, u32[]{:S(2)}, u32[]{:S(2)}) collective-permute-start(bf16[112,2048]{1,0:T(8,128)(2,1)S(1)} %get-tuple-element.31), channel_id=1, source_target_pairs={{0,1},{1,0},{2,3},{3,2},{4,5},{5,4},{6,7},{7,6},{8,9},{9,8},{10,11... | collective-permute-start | bytes 1376264 | tf_op jit(solution)/shard_map/ppermute | solution.py:492
  112.0 4.6 %collective-permute-start.21 = (bf16[112,2048]{1,0:T(8,128)(2,1)S(1)}, bf16[112,2048]{1,0:T(8,128)(2,1)S(1)}, u32[]{:S(2)}, u32[]{:S(2)}) collective-permute-start(bf16[112,2048]{1,0:T(8,128)(2,1)S(1)} %get-tuple-element.35), channel_id=1, source_target_pairs={{0,1},{1,0},{2,3},{3,2},{4,5},{5,4},{6,7},{7,6},{8,9},{9,8},{10,11... | collective-permute-start | bytes 1376264 | tf_op jit(solution)/shard_map/ppermute | solution.py:492
  114.7 3.3 %collective-permute-start.17 = (bf16[112,2048]{1,0:T(8,128)(2,1)S(1)}, bf16[112,2048]{1,0:T(8,128)(2,1)S(1)}, u32[]{:S(2)}, u32[]{:S(2)}) collective-permute-start(bf16[112,2048]{1,0:T(8,128)(2,1)S(1)} %get-tuple-element.33), channel_id=1, source_target_pairs={{0,1},{1,0},{2,3},{3,2},{4,5},{5,4},{6,7},{7,6},{8,9},{9,8},{10,11... | collective-permute-start | bytes 1376264 | tf_op jit(solution)/shard_map/ppermute | solution.py:492
  115.4 14.4 %collective-permute-start.26 = (bf16[112,2048]{1,0:T(8,128)(2,1)S(1)}, bf16[112,2048]{1,0:T(8,128)(2,1)S(1)}, u32[]{:S(2)}, u32[]{:S(2)}) collective-permute-start(bf16[112,2048]{1,0:T(8,128)(2,1)S(1)} %add_convert_fusion), channel_id=1, source_target_pairs={{0,6},{1,7},{2,4},{3,5},{4,2},{5,3},{6,0},{7,1},{8,14},{9,15},{10,... | collective-permute-start | bytes 1376264 | tf_op jit(solution)/shard_map/ppermute | solution.py:497
  116.8 21.9 %collective-permute-start.22 = (bf16[112,2048]{1,0:T(8,128)(2,1)S(1)}, bf16[112,2048]{1,0:T(8,128)(2,1)S(1)}, u32[]{:S(2)}, u32[]{:S(2)}) collective-permute-start(bf16[112,2048]{1,0:T(8,128)(2,1)S(1)} %add_convert_fusion.1), channel_id=1, source_target_pairs={{0,4},{1,5},{2,6},{3,7},{4,0},{5,1},{6,2},{7,3},{8,12},{9,13},{10,... | collective-permute-start | bytes 1376264 | tf_op jit(solution)/shard_map/ppermute | solution.py:497
  118.1 20.5 %collective-permute-start.18 = (bf16[112,2048]{1,0:T(8,128)(2,1)S(1)}, bf16[112,2048]{1,0:T(8,128)(2,1)S(1)}, u32[]{:S(2)}, u32[]{:S(2)}) collective-permute-start(bf16[112,2048]{1,0:T(8,128)(2,1)S(1)} %add_convert_fusion.2), channel_id=1, source_target_pairs={{0,2},{1,3},{2,0},{3,1},{4,6},{5,7},{6,4},{7,5},{8,10},{9,11},{10,... | collective-permute-start | bytes 1376264 | tf_op jit(solution)/shard_map/ppermute | solution.py:497

commit v3 on v2

--- a/solution.py
+++ b/solution.py
@@ -273,7 +273,7 @@
         ref[:, k % 2 * width : (k % 2 + 1) * width] = (parts[k] * factor).astype(BF16)
 
 
-def vmem_call(kernel, out, args, scratch, flops, name, mib=40, exps=0):
+def vmem_call(kernel, out, args, scratch, flops, name, mib=24, exps=0):
     vmem = pl.BlockSpec(memory_space=pltpu.VMEM)
     return pl.pallas_call(
         kernel,
@@ -299,6 +299,7 @@
         [pltpu.VMEM((bands.own_total, width), BF16)],
         6 * bands.own_total * width * width,
         "own_projection",
+        mib=16,
     )[0]
 
     def slab(part):
@@ -413,7 +414,7 @@
         out_ref[:, pl.ds(pl.multiple_of((chip ^ m) * wide, wide), wide)] = part.astype(BF16)
 
 
-def local_call(kernel, out, place, args, flops, name, mib=24):
+def local_call(kernel, out, place, args, flops, name, mib=16):
     vmem = pl.BlockSpec(memory_space=pltpu.VMEM)
     return pl.pallas_call(
         kernel,
@@ -432,7 +433,8 @@
     count = upper.shape[0]
     x = chip_swap(merge_weight[:half], 1)
     y = chip_swap(merge_weight[half:], 2)
-    weights = [merge_weight, core_swap(merge_weight), x, core_swap(x), y, core_swap(y)]
+    x_pair, y_pair, _ = lax.optimization_barrier((x, y, upper))
+    weights = [merge_weight, core_swap(merge_weight), x, core_swap(x_pair), y, core_swap(y_pair)]
     place = place_index()
     from_y = chip_swap(upper, 2)
     from_x = chip_swap(lower, 1)
@@ -479,7 +481,7 @@
         out_specs=[vmem] * 2,
         out_shape=[jax.ShapeDtypeStruct((count, width), BF16)] * 2,
         scratch_shapes=[pltpu.VMEM((2 * count, width), BF16), pltpu.VMEM((2 * count, hidden), BF16)],
-        compiler_params=params(24),
+        compiler_params=params(20),
         cost_estimate=pl.CostEstimate(
             flops=8 * count * width * hidden, bytes_accessed=4 * width * hidden, transcendentals=2 * count * hidden
         ),

time: 140 us -> 123 us (0.88)
  waiting for transfers between devices: 59.8 us -> 49.8 us
  Pallas kernels: 37.7 us -> 35.2 us
  local copies, waits for them, and re-layouts: 14 us -> 11.5 us
  starting transfers between devices: 26.4 us -> 24.4 us
    ppermute x12, waiting for transfers between devices: 59.7 us -> 49.8 us  [chip_swap(): lax.ppermute(value, 'lon', [(i, i ^ 2 * offset) for i in range(size)])]
    unnamed x42 -> x36, local copies, waits for them, and re-layouts: 8.91 us -> 5.63 us
    pallas_call x3, Pallas kernels: 18.1 us -> 15.6 us  [vmem_call(): pl.pallas_call(kernel, in_specs=[vmem] * len(args), out_specs=[vmem] * le...]
    ppermute x12, starting transfers between devices: 14.8 us -> 13.1 us  [chip_swap(): lax.ppermute(value, 'lon', [(i, i ^ 2 * offset) for i in range(size)])]
  transfers between devices with their start and end apart: 27 -> 27, of which waited for: 10 -> 8; matrix products, arithmetic and copies ran while one was open for 3% -> 3% of each run, Pallas kernels for 24% -> 25%
where the time goes in v3:
time: 123 us
  waiting for transfers between devices  49.8 us (40%)
  Pallas kernels  35.2 us (29%)
  starting transfers between devices  24.4 us (20%)
  local copies, waits for them, and re-layouts  11.5 us (9%)
    ppermute x12, waiting for transfers between devices, chip_swap(): lax.ppermute(value, 'lon', [(i, i ^ 2 * offset) for i in range(size)])  49.8 us
    pallas_call x3, Pallas kernels, vmem_call(): pl.pallas_call(kernel, in_specs=[vmem] * len(args), out_specs=[vmem] * le...  15.6 us
    ppermute x12, starting transfers between devices, chip_swap(): lax.ppermute(value, 'lon', [(i, i ^ 2 * offset) for i in range(size)])  13.1 us
    pallas_call x4, Pallas kernels, feed_forward(): pl.pallas_call(ffn_kernel, in_specs=[vmem] * 4, out_specs=[vmem] * 2, out...  10.4 us
    pallas_call x3, Pallas kernels, local_call(): pl.pallas_call(kernel, in_specs=[pl.BlockSpec(memory_space=pltpu.SMEM)] +...  9.2 us
    ppermute x4, starting transfers between devices, shift(): return lax.ppermute(part, axis, pairs)  8.44 us
    unnamed x36, local copies, waits for them, and re-layouts  5.63 us
    slice x1, local copies, waits for them, and re-layouts, merge_by_squares(): y = chip_swap(merge_weight[half:], 2)  3.09 us
  transfers between devices with their start and end apart: 27, of which 8 were waited for; matrix products, arithmetic and copies ran while one was open for 3% of the time, Pallas kernels for 25%

profile of v3, /device:TPU:0, one launch (start us, length us, event | category | flops | bytes accessed | tf_op | source)
XLA Modules:
  0.0 123.0 jit_solution(3258261192474771128)
XLA Ops:
  0.6 1.8 %fusion.7 = (bf16[18,8,1024]{2,1,0:T(8,128)(2,1)S(1)}, bf16[18,8,1024]{2,1,0:T(8,128)(2,1)}) fusion(bf16[18,24,1024]{2,1,0:T(8,128)(2,1)} %tokens_ref.3), kind=kLoop, calls=%fused_computation.23 | loop fusion | bytes 1179648 | tf_op jit(solution)/shard_map/slice | solution.py:293
  2.4 3.3 %collective-permute-start.1 = (bf16[18,8,1024]{2,1,0:T(8,128)(2,1)}, bf16[18,8,1024]{2,1,0:T(8,128)(2,1)S(1)}, u32[]{:S(2)}, u32[]{:S(2)}) collective-permute-start(bf16[18,8,1024]{2,1,0:T(8,128)(2,1)} %get-tuple-element.47), channel_id=1, source_target_pairs={{0,7},{1,0},{2,1},{3,2},{4,3},{5,4},{6,5},{7,6},{8,15},{9,8},{10,9... | collective-permute-start | bytes 884744 | tf_op jit(solution)/shard_map/ppermute | solution.py:343
  5.8 0.0 collective-permute-start.4
  5.8 3.1 %fusion.5 = (bf16[2048,256]{1,0:T(8,128)(2,1)}, bf16[2048,256]{1,0:T(8,128)(2,1)}) fusion(bf16[4096,256]{1,0:T(8,128)(2,1)} %refs_0_.3), kind=kLoop, calls=%fused_computation.21 | loop fusion | bytes 4194304 | tf_op jit(solution)/shard_map/slice | solution.py:435
  8.9 2.0 %collective-permute-start.5 = (bf16[2048,256]{1,0:T(8,128)(2,1)}, bf16[2048,256]{1,0:T(8,128)(2,1)S(1)}, u32[]{:S(2)}, u32[]{:S(2)}) collective-permute-start(bf16[2048,256]{1,0:T(8,128)(2,1)} %get-tuple-element.43), channel_id=1, source_target_pairs={{0,2},{1,3},{2,0},{3,1},{4,6},{5,7},{6,4},{7,5},{8,10},{9,11},{10,... | collective-permute-start | bytes 3145736 | tf_op jit(solution)/shard_map/ppermute | solution.py:499
  10.9 1.5 %collective-permute-start.6 = (bf16[2048,256]{1,0:T(8,128)(2,1)}, bf16[2048,256]{1,0:T(8,128)(2,1)}, u32[]{:S(2)}, u32[]{:S(2)}) collective-permute-start(bf16[2048,256]{1,0:T(8,128)(2,1)} %get-tuple-element.42), channel_id=1, source_target_pairs={{0,4},{1,5},{2,6},{3,7},{4,0},{5,1},{6,2},{7,3},{8,12},{9,13},{10,... | collective-permute-start | bytes 3145736 | tf_op jit(solution)/shard_map/ppermute | solution.py:499
  12.4 0.0 copy-start.5
  12.5 2.8 %copy-done.5 = bf16[1024,3072]{1,0:T(8,128)(2,1)S(1)} copy-done((bf16[1024,3072]{1,0:T(8,128)(2,1)S(1)}, bf16[1024,3072]{1,0:T(8,128)(2,1)}, u32[]{:S(2)}) %copy-start.5) | copy-done | bytes 6291480
  15.2 3.4 %own_projection.1.own_ref = bf16[448,3072]{1,0:T(8,128)(2,1)S(1)} custom-call(bf16[18,24,1024]{2,1,0:T(8,128)(2,1)S(1)} %copy-done.3, bf16[1024,3072]{1,0:T(8,128)(2,1)S(1)} %copy-done.5), custom_call_target="tpu_custom_call" | custom-call | flops 2818572288 | bytes 1048576 | tf_op jit(solution)/shard_map/own_projection/pallas_call | solution.py:278
  18.7 0.1 or_select_fusion.bias_ref
  18.8 0.0 collective-permute-done.west_ref
  18.8 3.5 %collective-permute-start.2 = (bf16[3,40,1024]{2,1,0:T(8,128)(2,1)S(1)}, bf16[3,40,1024]{2,1,0:T(8,128)(2,1)S(1)}, u32[]{:S(2)}, u32[]{:S(2)}) collective-permute-start(bf16[3,40,1024]{2,1,0:T(8,128)(2,1)S(1)} %pad_maximum_fusion), channel_id=1, source_target_pairs={{0,8},{8,16},{16,24},{1,9},{9,17},{17,25},{2,10},{10,18},{18,26},{... | collective-permute-start | bytes 737288 | tf_op jit(solution)/shard_map/ppermute | solution.py:343
  22.4 0.0 copy-start.4
  22.4 1.6 %collective-permute-start.3 = (bf16[3,40,1024]{2,1,0:T(8,128)(2,1)S(1)}, bf16[3,40,1024]{2,1,0:T(8,128)(2,1)S(1)}, u32[]{:S(2)}, u32[]{:S(2)}) collective-permute-start(bf16[3,40,1024]{2,1,0:T(8,128)(2,1)S(1)} %pad_maximum_fusion.1), channel_id=1, source_target_pairs={{8,0},{16,8},{24,16},{9,1},{17,9},{25,17},{10,2},{18,10},{26,18},{... | collective-permute-start | bytes 737288 | tf_op jit(solution)/shard_map/ppermute | solution.py:343
  24.0 0.0 copy-start.6
  24.0 2.8 %copy-done.6 = bf16[1024,3072]{1,0:T(8,128)(2,1)S(1)} copy-done((bf16[1024,3072]{1,0:T(8,128)(2,1)S(1)}, bf16[1024,3072]{1,0:T(8,128)(2,1)}, u32[]{:S(2)}) %copy-start.6) | copy-done | bytes 6291480
  26.8 0.0 copy-start.14
  26.8 0.0 copy-start.16
  26.8 0.0 copy-start.17
  26.9 5.4 %middle_attention.1 = (bf16[288,2048]{1,0:T(8,128)(2,1)S(1)}, bf16[288,1024]{1,0:T(8,128)(2,1)S(1)}) custom-call(bf16[18,8,1024]{2,1,0:T(8,128)(2,1)S(1)} %collective-permute-done.west_ref, bf16[18,8,1024]{2,1,0:T(8,128)(2,1)S(1)} %collective-permute-done.1.east_ref, bf16[448,3072]{1,0:T(8,128)(2,1)S(1)} %own_projection.1.own_ref, ...), custom_call_target="tpu_custom_call" | custom-call | flops 5000000000 | bytes 1048576 | tf_op jit(solution)/shard_map/middle_attention/pallas_call | solution.py:278
  32.2 0.0 collective-permute-done.2.north_ref
  32.3 0.0 copy-start.2
  32.3 6.8 %edge_attention.1 = (bf16[18,24,1024]{2,1,0:T(8,128)(2,1)}, bf16[112,2048]{1,0:T(8,128)(2,1)}, bf16[112,2048]{1,0:T(8,128)(2,1)}) custom-call(bf16[18,24,1024]{2,1,0:T(8,128)(2,1)S(1)} %copy-done.4, bf16[3,40,1024]{2,1,0:T(8,128)(2,1)S(1)} %collective-permute-done.2.north_ref, bf16[3,40,1024]{2,1,0:T(8,128)(2,1)S(1)} %collective-permute-done.3.south_ref, ...), custom_call_target="tpu_custom_call" | custom-call | flops 6000000000 | bytes 1048576 | tf_op jit(solution)/shard_map/edge_attention/pallas_call | solution.py:278
  39.1 0.5 collective-permute-start.8
  39.6 0.5 collective-permute-start.9
  40.2 0.0 collective-permute-start.10
  40.2 0.1 pad_add_fusion.place_ref
  40.3 12.2 %collective-permute-done.9.upper_ref = bf16[112,2048]{1,0:T(8,128)(2,1)} collective-permute-done((bf16[112,2048]{1,0:T(8,128)(2,1)}, bf16[112,2048]{1,0:T(8,128)(2,1)}, u32[]{:S(2)}, u32[]{:S(2)}) %collective-permute-start.9) | collective-permute-done | bytes 458784 | tf_op jit(solution)/shard_map/ppermute | solution.py:499
  52.5 0.2 collective-permute-done.10.lower_ref
  52.7 4.1 %merge_other.1 = (bf16[112,1024]{1,0:T(8,128)(2,1)S(1)}, bf16[112,1024]{1,0:T(8,128)(2,1)S(1)}) custom-call(s32[2]{0:T(128)S(1)} %pad_add_fusion.place_ref, bf16[112,2048]{1,0:T(8,128)(2,1)} %collective-permute-done.9.upper_ref, bf16[112,2048]{1,0:T(8,128)(2,1)} %collective-permute-done.10.lower_ref, bf16[4096,256]{1,0:T(8,128)(2,1)S(1)} %copy-done.2, ...), custom_call_target="tpu_custom_call" | custom-call | flops 939524096 | bytes 1048576 | tf_op jit(solution)/shard_map/merge_other/pallas_call | solution.py:419
  56.8 1.6 %collective-permute-start.11 = (bf16[112,1024]{1,0:T(8,128)(2,1)S(1)}, bf16[112,1024]{1,0:T(8,128)(2,1)S(1)}, u32[]{:S(2)}, u32[]{:S(2)}) collective-permute-start(bf16[112,1024]{1,0:T(8,128)(2,1)S(1)} %get-tuple-element.32), channel_id=1, source_target_pairs={{0,4},{1,5},{2,6},{3,7},{4,0},{5,1},{6,2},{7,3},{8,12},{9,13},{10,... | collective-permute-start | bytes 688136 | tf_op jit(solution)/shard_map/ppermute | solution.py:499
  58.4 0.2 collective-permute-start.12
  58.6 4.5 %merge_own.1 = (f32[112,512]{1,0:T(8,128)S(1)}, f32[112,512]{1,0:T(8,128)S(1)}, f32[112,512]{1,0:T(8,128)S(1)}) custom-call(s32[2]{0:T(128)S(1)} %pad_add_fusion.place_ref, bf16[112,2048]{1,0:T(8,128)(2,1)} %get-tuple-element.25.upper_ref, bf16[112,2048]{1,0:T(8,128)(2,1)} %get-tuple-element.26.lower_ref, bf16[4096,256]{1,0:T(8,128)(2,1)S(1)} %copy-done.2, ...), custom_call_target="tpu_custom_call" | custom-call | flops 939524096 | bytes 1048576 | tf_op jit(solution)/shard_map/merge_own/pallas_call | solution.py:419
  63.1 0.3 collective-permute-done.11.from_y_ref
  63.4 1.1 collective-permute-done.12.from_x_ref
  64.5 0.6 combine.1.mine_ref
  65.1 0.7 collective-permute-start.23
  65.8 1.5 %collective-permute-start.19 = (bf16[112,2048]{1,0:T(8,128)(2,1)S(1)}, bf16[112,2048]{1,0:T(8,128)(2,1)S(1)}, u32[]{:S(2)}, u32[]{:S(2)}) collective-permute-start(bf16[112,2048]{1,0:T(8,128)(2,1)S(1)} %combine.1.mine_ref), channel_id=1, source_target_pairs={{0,4},{1,5},{2,6},{3,7},{4,0},{5,1},{6,2},{7,3},{8,12},{9,13},{10,... | collective-permute-start | bytes 1376264 | tf_op jit(solution)/shard_map/ppermute | solution.py:499
  67.3 1.4 %collective-permute-start.15 = (bf16[112,2048]{1,0:T(8,128)(2,1)S(1)}, bf16[112,2048]{1,0:T(8,128)(2,1)S(1)}, u32[]{:S(2)}, u32[]{:S(2)}) collective-permute-start(bf16[112,2048]{1,0:T(8,128)(2,1)S(1)} %combine.1.mine_ref), channel_id=1, source_target_pairs={{0,2},{1,3},{2,0},{3,1},{4,6},{5,7},{6,4},{7,5},{8,10},{9,11},{10,... | collective-permute-start | bytes 1376264 | tf_op jit(solution)/shard_map/ppermute | solution.py:499
  68.7 10.9 %collective-permute-done.23.mine_ref = bf16[112,2048]{1,0:T(8,128)(2,1)S(1)} collective-permute-done((bf16[112,2048]{1,0:T(8,128)(2,1)S(1)}, bf16[112,2048]{1,0:T(8,128)(2,1)S(1)}, u32[]{:S(2)}, u32[]{:S(2)}) %collective-permute-start.23) | collective-permute-done | bytes 458784 | tf_op jit(solution)/shard_map/ppermute | solution.py:499
  79.6 0.5 collective-permute-start.13
  80.1 5.9 %collective-permute-done.19.mine_ref = bf16[112,2048]{1,0:T(8,128)(2,1)S(1)} collective-permute-done((bf16[112,2048]{1,0:T(8,128)(2,1)S(1)}, bf16[112,2048]{1,0:T(8,128)(2,1)S(1)}, u32[]{:S(2)}, u32[]{:S(2)}) %collective-permute-start.19) | collective-permute-done | bytes 458784 | tf_op jit(solution)/shard_map/ppermute | solution.py:499
  86.0 0.0 collective-permute-start.20
  86.0 0.5 collective-permute-start.16
  86.5 2.6 %feed_forward.7 = (bf16[112,2048]{1,0:T(8,128)(2,1)S(1)}, bf16[112,2048]{1,0:T(8,128)(2,1)S(1)}) custom-call(bf16[112,2048]{1,0:T(8,128)(2,1)S(1)} %collective-permute-done.23.mine_ref, bf16[112,2048]{1,0:T(8,128)(2,1)S(1)} %collective-permute-done.24.theirs_ref, bf16[2048,1024]{1,0:T(8,128)(2,1)S(1)} %copy-done, bf16[1024,2048]{1,0:T(8,128)(2,1)S(1)} %copy-done.1), custom_call_target="tpu_custom_call" | custom-call | flops 1879048192 | bytes 8388608 | tf_op jit(solution)/shard_map/feed_forward/pallas_call | solution.py:478
  89.1 0.1 collective-permute-start.25
  89.2 2.6 %feed_forward.4 = (bf16[112,2048]{1,0:T(8,128)(2,1)S(1)}, bf16[112,2048]{1,0:T(8,128)(2,1)S(1)}) custom-call(bf16[112,2048]{1,0:T(8,128)(2,1)S(1)} %combine.1.mine_ref, bf16[112,2048]{1,0:T(8,128)(2,1)S(1)} %collective-permute-done.13.theirs_ref, bf16[2048,1024]{1,0:T(8,128)(2,1)S(1)} %copy-done, bf16[1024,2048]{1,0:T(8,128)(2,1)S(1)} %copy-done.1), custom_call_target="tpu_custom_call" | custom-call | flops 1879048192 | bytes 8388608 | tf_op jit(solution)/shard_map/feed_forward/pallas_call | solution.py:478
  91.8 0.6 collective-permute-start.14
  92.4 2.6 %feed_forward.6 = (bf16[112,2048]{1,0:T(8,128)(2,1)S(1)}, bf16[112,2048]{1,0:T(8,128)(2,1)S(1)}) custom-call(bf16[112,2048]{1,0:T(8,128)(2,1)S(1)} %collective-permute-done.19.mine_ref, bf16[112,2048]{1,0:T(8,128)(2,1)S(1)} %collective-permute-done.20.theirs_ref, bf16[2048,1024]{1,0:T(8,128)(2,1)S(1)} %copy-done, bf16[1024,2048]{1,0:T(8,128)(2,1)S(1)} %copy-done.1), custom_call_target="tpu_custom_call" | custom-call | flops 1879048192 | bytes 8388608 | tf_op jit(solution)/shard_map/feed_forward/pallas_call | solution.py:478
  95.0 0.1 collective-permute-start.21
  95.1 2.6 %feed_forward.5 = (bf16[112,2048]{1,0:T(8,128)(2,1)S(1)}, bf16[112,2048]{1,0:T(8,128)(2,1)S(1)}) custom-call(bf16[112,2048]{1,0:T(8,128)(2,1)S(1)} %collective-permute-done.15.mine_ref, bf16[112,2048]{1,0:T(8,128)(2,1)S(1)} %collective-permute-done.16.theirs_ref, bf16[2048,1024]{1,0:T(8,128)(2,1)S(1)} %copy-done, bf16[1024,2048]{1,0:T(8,128)(2,1)S(1)} %copy-done.1), custom_call_target="tpu_custom_call" | custom-call | flops 1879048192 | bytes 8388608 | tf_op jit(solution)/shard_map/feed_forward/pallas_call | solution.py:478
  97.7 0.5 collective-permute-start.17
  98.3 0.1 add_convert_fusion
  98.4 1.3 %collective-permute-start.26 = (bf16[112,2048]{1,0:T(8,128)(2,1)S(1)}, bf16[112,2048]{1,0:T(8,128)(2,1)S(1)}, u32[]{:S(2)}, u32[]{:S(2)}) collective-permute-start(bf16[112,2048]{1,0:T(8,128)(2,1)S(1)} %add_convert_fusion), channel_id=1, source_target_pairs={{0,6},{1,7},{2,4},{3,5},{4,2},{5,3},{6,0},{7,1},{8,14},{9,15},{10,... | collective-permute-start | bytes 1376264 | tf_op jit(solution)/shard_map/ppermute | solution.py:499
  99.6 0.1 add_convert_fusion.1
  99.8 1.4 %collective-permute-start.22 = (bf16[112,2048]{1,0:T(8,128)(2,1)S(1)}, bf16[112,2048]{1,0:T(8,128)(2,1)S(1)}, u32[]{:S(2)}, u32[]{:S(2)}) collective-permute-start(bf16[112,2048]{1,0:T(8,128)(2,1)S(1)} %add_convert_fusion.1), channel_id=1, source_target_pairs={{0,4},{1,5},{2,6},{3,7},{4,0},{5,1},{6,2},{7,3},{8,12},{9,13},{10,... | collective-permute-start | bytes 1376264 | tf_op jit(solution)/shard_map/ppermute | solution.py:499
  101.2 0.1 add_convert_fusion.2
  101.3 1.0 collective-permute-start.18
  102.3 0.1 convert_element_type.47
  102.4 0.1 convert_element_type.48
  102.5 10.3 %collective-permute-done.26 = bf16[112,2048]{1,0:T(8,128)(2,1)S(1)} collective-permute-done((bf16[112,2048]{1,0:T(8,128)(2,1)S(1)}, bf16[112,2048]{1,0:T(8,128)(2,1)S(1)}, u32[]{:S(2)}, u32[]{:S(2)}) %collective-permute-start.26) | collective-permute-done | bytes 458784 | tf_op jit(solution)/shard_map/ppermute | solution.py:499
  112.8 8.9 %collective-permute-done.22 = bf16[112,2048]{1,0:T(8,128)(2,1)S(1)} collective-permute-done((bf16[112,2048]{1,0:T(8,128)(2,1)S(1)}, bf16[112,2048]{1,0:T(8,128)(2,1)S(1)}, u32[]{:S(2)}, u32[]{:S(2)}) %collective-permute-start.22) | collective-permute-done | bytes 458784 | tf_op jit(solution)/shard_map/ppermute | solution.py:499
  121.6 0.4 fusion.4
  122.1 0.9 reshape.45
  (54 shorter events, 0.2 us)
Async XLA Ops:
  2.4 16.3 %collective-permute-start.1 = (bf16[18,8,1024]{2,1,0:T(8,128)(2,1)}, bf16[18,8,1024]{2,1,0:T(8,128)(2,1)S(1)}, u32[]{:S(2)}, u32[]{:S(2)}) collective-permute-start(bf16[18,8,1024]{2,1,0:T(8,128)(2,1)} %get-tuple-element.47), channel_id=1, source_target_pairs={{0,7},{1,0},{2,1},{3,2},{4,3},{5,4},{6,5},{7,6},{8,15},{9,8},{10,9... | collective-permute-start | bytes 884744 | tf_op jit(solution)/shard_map/ppermute | solution.py:343
  5.8 6.6 %copy-start.3 = (bf16[18,24,1024]{2,1,0:T(8,128)(2,1)S(1)}, bf16[18,24,1024]{2,1,0:T(8,128)(2,1)}, u32[]{:S(2)}) copy-start(bf16[18,24,1024]{2,1,0:T(8,128)(2,1)} %tokens_ref.3) | copy-start | bytes 2654212
  5.8 13.0 %collective-permute-start = (bf16[18,8,1024]{2,1,0:T(8,128)(2,1)S(1)}, bf16[18,8,1024]{2,1,0:T(8,128)(2,1)S(1)}, u32[]{:S(2)}, u32[]{:S(2)}) collective-permute-start(bf16[18,8,1024]{2,1,0:T(8,128)(2,1)S(1)} %get-tuple-element.46), channel_id=1, source_target_pairs={{0,1},{1,2},{2,3},{3,4},{4,5},{5,6},{6,7},{7,0},{8,9},{9,10},{10,1... | collective-permute-start | bytes 884744 | tf_op jit(solution)/shard_map/ppermute | solution.py:343
  5.8 46.9 %collective-permute-start.4 = (bf16[4096,256]{1,0:T(8,128)(2,1)}, bf16[4096,256]{1,0:T(8,128)(2,1)}, u32[]{:S(2)}, u32[]{:S(2)}) collective-permute-start(bf16[4096,256]{1,0:T(8,128)(2,1)} %refs_0_.3), channel_id=1, source_target_pairs={{0,1},{1,0},{2,3},{3,2},{4,5},{5,4},{6,7},{7,6},{8,9},{9,8},{10,11... | collective-permute-start | bytes 6291464 | tf_op jit(solution)/shard_map/ppermute | solution.py:494
  8.9 30.3 %collective-permute-start.5 = (bf16[2048,256]{1,0:T(8,128)(2,1)}, bf16[2048,256]{1,0:T(8,128)(2,1)S(1)}, u32[]{:S(2)}, u32[]{:S(2)}) collective-permute-start(bf16[2048,256]{1,0:T(8,128)(2,1)} %get-tuple-element.43), channel_id=1, source_target_pairs={{0,2},{1,3},{2,0},{3,1},{4,6},{5,7},{6,4},{7,5},{8,10},{9,11},{10,... | collective-permute-start | bytes 3145736 | tf_op jit(solution)/shard_map/ppermute | solution.py:499
  10.9 28.3 %collective-permute-start.6 = (bf16[2048,256]{1,0:T(8,128)(2,1)}, bf16[2048,256]{1,0:T(8,128)(2,1)}, u32[]{:S(2)}, u32[]{:S(2)}) collective-permute-start(bf16[2048,256]{1,0:T(8,128)(2,1)} %get-tuple-element.42), channel_id=1, source_target_pairs={{0,4},{1,5},{2,6},{3,7},{4,0},{5,1},{6,2},{7,3},{8,12},{9,13},{10,... | collective-permute-start | bytes 3145736 | tf_op jit(solution)/shard_map/ppermute | solution.py:499
  12.4 2.8 %copy-start.5 = (bf16[1024,3072]{1,0:T(8,128)(2,1)S(1)}, bf16[1024,3072]{1,0:T(8,128)(2,1)}, u32[]{:S(2)}) copy-start(bf16[1024,3072]{1,0:T(8,128)(2,1)} %weight_ref.5) | copy-start | bytes 18874372
  15.2 8.7 %copy-start.9 = (bf16[576,144]{1,0:T(8,128)(2,1)S(1)}, bf16[576,144]{1,0:T(8,128)(2,1)}, u32[]{:S(2)}) copy-start(bf16[576,144]{1,0:T(8,128)(2,1)} %constant.71.clone.rest_1_) | copy-start | bytes 497668
  15.2 8.7 %copy-start.10 = (bf16[576,256]{1,0:T(8,128)(2,1)S(1)}, bf16[576,256]{1,0:T(8,128)(2,1)}, u32[]{:S(2)}) copy-start(bf16[576,256]{1,0:T(8,128)(2,1)} %constant.72.clone.rest_2_) | copy-start | bytes 884740
  15.2 8.8 %copy-start.11 = (bf16[144,576]{1,0:T(8,128)(2,1)S(1)}, bf16[144,576]{1,0:T(8,128)(2,1)}, u32[]{:S(2)}) copy-start(bf16[144,576]{1,0:T(8,128)(2,1)} %constant.73.clone.rest_3_) | copy-start | bytes 497668
  15.2 8.8 %copy-start.15 = (bf16[240,240]{1,0:T(8,128)(2,1)S(1)}, bf16[240,240]{1,0:T(8,128)(2,1)}, u32[]{:S(2)}) copy-start(bf16[240,240]{1,0:T(8,128)(2,1)} %constant.70.clone.rest_0_) | copy-start | bytes 345604
  18.8 13.4 %collective-permute-start.2 = (bf16[3,40,1024]{2,1,0:T(8,128)(2,1)S(1)}, bf16[3,40,1024]{2,1,0:T(8,128)(2,1)S(1)}, u32[]{:S(2)}, u32[]{:S(2)}) collective-permute-start(bf16[3,40,1024]{2,1,0:T(8,128)(2,1)S(1)} %pad_maximum_fusion), channel_id=1, source_target_pairs={{0,8},{8,16},{16,24},{1,9},{9,17},{17,25},{2,10},{10,18},{18,26},{... | collective-permute-start | bytes 737288 | tf_op jit(solution)/shard_map/ppermute | solution.py:343
  22.4 9.9 %copy-start.4 = (bf16[18,24,1024]{2,1,0:T(8,128)(2,1)S(1)}, bf16[18,24,1024]{2,1,0:T(8,128)(2,1)}, u32[]{:S(2)}) copy-start(bf16[18,24,1024]{2,1,0:T(8,128)(2,1)} %tokens_ref.3) | copy-start | bytes 2654212
  22.4 9.9 %collective-permute-start.3 = (bf16[3,40,1024]{2,1,0:T(8,128)(2,1)S(1)}, bf16[3,40,1024]{2,1,0:T(8,128)(2,1)S(1)}, u32[]{:S(2)}, u32[]{:S(2)}) collective-permute-start(bf16[3,40,1024]{2,1,0:T(8,128)(2,1)S(1)} %pad_maximum_fusion.1), channel_id=1, source_target_pairs={{8,0},{16,8},{24,16},{9,1},{17,9},{25,17},{10,2},{18,10},{26,18},{... | collective-permute-start | bytes 737288 | tf_op jit(solution)/shard_map/ppermute | solution.py:343
  24.0 2.8 %copy-start.6 = (bf16[1024,3072]{1,0:T(8,128)(2,1)S(1)}, bf16[1024,3072]{1,0:T(8,128)(2,1)}, u32[]{:S(2)}) copy-start(bf16[1024,3072]{1,0:T(8,128)(2,1)} %weight_ref.5) | copy-start | bytes 18874372
  26.8 5.5 %copy-start.7 = (bf16[1024,1024]{1,0:T(8,128)(2,1)S(1)}, bf16[1024,1024]{1,0:T(8,128)(2,1)}, u32[]{:S(2)}) copy-start(bf16[1024,1024]{1,0:T(8,128)(2,1)} %out_w_ref.1) | copy-start | bytes 6291460
  26.8 5.5 %copy-start.8 = (bf16[448,432]{1,0:T(8,128)(2,1)S(1)}, bf16[448,432]{1,0:T(8,128)(2,1)}, u32[]{:S(2)}) copy-start(bf16[448,432]{1,0:T(8,128)(2,1)} %constant.74.clone.patch_ref) | copy-start | bytes 1161220
  26.8 5.5 %copy-start.12 = (bf16[304,256]{1,0:T(8,128)(2,1)S(1)}, bf16[304,256]{1,0:T(8,128)(2,1)}, u32[]{:S(2)}) copy-start(bf16[304,256]{1,0:T(8,128)(2,1)} %constant.77.clone.rest_2_.rest_6_) | copy-start | bytes 466948
  26.8 5.5 %copy-start.13 = (bf16[240,256]{1,0:T(8,128)(2,1)S(1)}, bf16[240,256]{1,0:T(8,128)(2,1)}, u32[]{:S(2)}) copy-start(bf16[240,256]{1,0:T(8,128)(2,1)} %constant.75.clone.rest_0_) | copy-start | bytes 368644
  26.8 5.5 %copy-start.14 = (bf16[240,256]{1,0:T(8,128)(2,1)S(1)}, bf16[240,256]{1,0:T(8,128)(2,1)}, u32[]{:S(2)}) copy-start(bf16[240,256]{1,0:T(8,128)(2,1)} %constant.79.clone.rest_4_) | copy-start | bytes 368644
  26.8 5.5 %copy-start.16 = (bf16[304,80]{1,0:T(8,128)(2,1)S(1)}, bf16[304,80]{1,0:T(8,128)(2,1)}, u32[]{:S(2)}) copy-start(bf16[304,80]{1,0:T(8,128)(2,1)} %constant.76.clone.rest_1_.rest_5_) | copy-start | bytes 145924
  26.8 5.5 %copy-start.17 = (bf16[80,304]{1,0:T(8,128)(2,1)S(1)}, bf16[80,304]{1,0:T(8,128)(2,1)}, u32[]{:S(2)}) copy-start(bf16[80,304]{1,0:T(8,128)(2,1)} %constant.78.clone.rest_3_.rest_7_) | copy-start | bytes 145924
  32.3 20.4 %copy-start.2 = (bf16[4096,256]{1,0:T(8,128)(2,1)S(1)}, bf16[4096,256]{1,0:T(8,128)(2,1)}, u32[]{:S(2)}) copy-start(bf16[4096,256]{1,0:T(8,128)(2,1)} %refs_0_.3) | copy-start | bytes 6291460
  39.1 13.6 %collective-permute-start.7 = (bf16[2048,256]{1,0:T(8,128)(2,1)S(1)}, bf16[2048,256]{1,0:T(8,128)(2,1)}, u32[]{:S(2)}, u32[]{:S(2)}) collective-permute-start(bf16[2048,256]{1,0:T(8,128)(2,1)S(1)} %collective-permute-done.5.refs_2_), channel_id=1, source_target_pairs={{0,1},{1,0},{2,3},{3,2},{4,5},{5,4},{6,7},{7,6},{8,9},{9,8},{10,11... | collective-permute-start | bytes 3145736 | tf_op jit(solution)/shard_map/ppermute | solution.py:494
  39.1 13.6 %collective-permute-start.8 = (bf16[2048,256]{1,0:T(8,128)(2,1)}, bf16[2048,256]{1,0:T(8,128)(2,1)}, u32[]{:S(2)}, u32[]{:S(2)}) collective-permute-start(bf16[2048,256]{1,0:T(8,128)(2,1)} %collective-permute-done.6.refs_4_), channel_id=1, source_target_pairs={{0,1},{1,0},{2,3},{3,2},{4,5},{5,4},{6,7},{7,6},{8,9},{9,8},{10,11... | collective-permute-start | bytes 3145736 | tf_op jit(solution)/shard_map/ppermute | solution.py:494
  39.6 12.8 %collective-permute-start.9 = (bf16[112,2048]{1,0:T(8,128)(2,1)}, bf16[112,2048]{1,0:T(8,128)(2,1)}, u32[]{:S(2)}, u32[]{:S(2)}) collective-permute-start(bf16[112,2048]{1,0:T(8,128)(2,1)} %get-tuple-element.25.upper_ref), channel_id=1, source_target_pairs={{0,4},{1,5},{2,6},{3,7},{4,0},{5,1},{6,2},{7,3},{8,12},{9,13},{10,... | collective-permute-start | bytes 1376264 | tf_op jit(solution)/shard_map/ppermute | solution.py:499
  40.2 12.5 %collective-permute-start.10 = (bf16[112,2048]{1,0:T(8,128)(2,1)}, bf16[112,2048]{1,0:T(8,128)(2,1)}, u32[]{:S(2)}, u32[]{:S(2)}) collective-permute-start(bf16[112,2048]{1,0:T(8,128)(2,1)} %get-tuple-element.26.lower_ref), channel_id=1, source_target_pairs={{0,2},{1,3},{2,0},{3,1},{4,6},{5,7},{6,4},{7,5},{8,10},{9,11},{10,... | collective-permute-start | bytes 1376264 | tf_op jit(solution)/shard_map/ppermute | solution.py:499
  56.8 6.6 %collective-permute-start.11 = (bf16[112,1024]{1,0:T(8,128)(2,1)S(1)}, bf16[112,1024]{1,0:T(8,128)(2,1)S(1)}, u32[]{:S(2)}, u32[]{:S(2)}) collective-permute-start(bf16[112,1024]{1,0:T(8,128)(2,1)S(1)} %get-tuple-element.32), channel_id=1, source_target_pairs={{0,4},{1,5},{2,6},{3,7},{4,0},{5,1},{6,2},{7,3},{8,12},{9,13},{10,... | collective-permute-start | bytes 688136 | tf_op jit(solution)/shard_map/ppermute | solution.py:499
  58.4 6.1 %collective-permute-start.12 = (bf16[112,1024]{1,0:T(8,128)(2,1)S(1)}, bf16[112,1024]{1,0:T(8,128)(2,1)S(1)}, u32[]{:S(2)}, u32[]{:S(2)}) collective-permute-start(bf16[112,1024]{1,0:T(8,128)(2,1)S(1)} %get-tuple-element.33), channel_id=1, source_target_pairs={{0,2},{1,3},{2,0},{3,1},{4,6},{5,7},{6,4},{7,5},{8,10},{9,11},{10,... | collective-permute-start | bytes 688136 | tf_op jit(solution)/shard_map/ppermute | solution.py:499
  58.6 27.9 %copy-start = (bf16[2048,1024]{1,0:T(8,128)(2,1)S(1)}, bf16[2048,1024]{1,0:T(8,128)(2,1)}, u32[]{:S(2)}) copy-start(bf16[2048,1024]{1,0:T(8,128)(2,1)} %up_ref.7) | copy-start | bytes 12582916
  58.6 27.9 %copy-start.1 = (bf16[1024,2048]{1,0:T(8,128)(2,1)S(1)}, bf16[1024,2048]{1,0:T(8,128)(2,1)}, u32[]{:S(2)}) copy-start(bf16[1024,2048]{1,0:T(8,128)(2,1)} %down_ref.7) | copy-start | bytes 12582916
  65.1 14.4 %collective-permute-start.23 = (bf16[112,2048]{1,0:T(8,128)(2,1)S(1)}, bf16[112,2048]{1,0:T(8,128)(2,1)S(1)}, u32[]{:S(2)}, u32[]{:S(2)}) collective-permute-start(bf16[112,2048]{1,0:T(8,128)(2,1)S(1)} %combine.1.mine_ref), channel_id=1, source_target_pairs={{0,6},{1,7},{2,4},{3,5},{4,2},{5,3},{6,0},{7,1},{8,14},{9,15},{10,... | collective-permute-start | bytes 1376264 | tf_op jit(solution)/shard_map/ppermute | solution.py:499
  65.8 20.2 %collective-permute-start.19 = (bf16[112,2048]{1,0:T(8,128)(2,1)S(1)}, bf16[112,2048]{1,0:T(8,128)(2,1)S(1)}, u32[]{:S(2)}, u32[]{:S(2)}) collective-permute-start(bf16[112,2048]{1,0:T(8,128)(2,1)S(1)} %combine.1.mine_ref), channel_id=1, source_target_pairs={{0,4},{1,5},{2,6},{3,7},{4,0},{5,1},{6,2},{7,3},{8,12},{9,13},{10,... | collective-permute-start | bytes 1376264 | tf_op jit(solution)/shard_map/ppermute | solution.py:499
  67.3 18.7 %collective-permute-start.15 = (bf16[112,2048]{1,0:T(8,128)(2,1)S(1)}, bf16[112,2048]{1,0:T(8,128)(2,1)S(1)}, u32[]{:S(2)}, u32[]{:S(2)}) collective-permute-start(bf16[112,2048]{1,0:T(8,128)(2,1)S(1)} %combine.1.mine_ref), channel_id=1, source_target_pairs={{0,2},{1,3},{2,0},{3,1},{4,6},{5,7},{6,4},{7,5},{8,10},{9,11},{10,... | collective-permute-start | bytes 1376264 | tf_op jit(solution)/shard_map/ppermute | solution.py:499
  79.6 7.0 %collective-permute-start.24 = (bf16[112,2048]{1,0:T(8,128)(2,1)S(1)}, bf16[112,2048]{1,0:T(8,128)(2,1)S(1)}, u32[]{:S(2)}, u32[]{:S(2)}) collective-permute-start(bf16[112,2048]{1,0:T(8,128)(2,1)S(1)} %collective-permute-done.23.mine_ref), channel_id=1, source_target_pairs={{0,1},{1,0},{2,3},{3,2},{4,5},{5,4},{6,7},{7,6},{8,9},{9,8},{10,11... | collective-permute-start | bytes 1376264 | tf_op jit(solution)/shard_map/ppermute | solution.py:494
  79.6 9.7 %collective-permute-start.13 = (bf16[112,2048]{1,0:T(8,128)(2,1)S(1)}, bf16[112,2048]{1,0:T(8,128)(2,1)S(1)}, u32[]{:S(2)}, u32[]{:S(2)}) collective-permute-start(bf16[112,2048]{1,0:T(8,128)(2,1)S(1)} %combine.1.mine_ref), channel_id=1, source_target_pairs={{0,1},{1,0},{2,3},{3,2},{4,5},{5,4},{6,7},{7,6},{8,9},{9,8},{10,11... | collective-permute-start | bytes 1376264 | tf_op jit(solution)/shard_map/ppermute | solution.py:494
  86.0 6.4 %collective-permute-start.20 = (bf16[112,2048]{1,0:T(8,128)(2,1)S(1)}, bf16[112,2048]{1,0:T(8,128)(2,1)S(1)}, u32[]{:S(2)}, u32[]{:S(2)}) collective-permute-start(bf16[112,2048]{1,0:T(8,128)(2,1)S(1)} %collective-permute-done.19.mine_ref), channel_id=1, source_target_pairs={{0,1},{1,0},{2,3},{3,2},{4,5},{5,4},{6,7},{7,6},{8,9},{9,8},{10,11... | collective-permute-start | bytes 1376264 | tf_op jit(solution)/shard_map/ppermute | solution.py:494
  86.0 9.1 %collective-permute-start.16 = (bf16[112,2048]{1,0:T(8,128)(2,1)S(1)}, bf16[112,2048]{1,0:T(8,128)(2,1)S(1)}, u32[]{:S(2)}, u32[]{:S(2)}) collective-permute-start(bf16[112,2048]{1,0:T(8,128)(2,1)S(1)} %collective-permute-done.15.mine_ref), channel_id=1, source_target_pairs={{0,1},{1,0},{2,3},{3,2},{4,5},{5,4},{6,7},{7,6},{8,9},{9,8},{10,11... | collective-permute-start | bytes 1376264 | tf_op jit(solution)/shard_map/ppermute | solution.py:494
  89.1 9.1 %collective-permute-start.25 = (bf16[112,2048]{1,0:T(8,128)(2,1)S(1)}, bf16[112,2048]{1,0:T(8,128)(2,1)S(1)}, u32[]{:S(2)}, u32[]{:S(2)}) collective-permute-start(bf16[112,2048]{1,0:T(8,128)(2,1)S(1)} %get-tuple-element.41), channel_id=1, source_target_pairs={{0,1},{1,0},{2,3},{3,2},{4,5},{5,4},{6,7},{7,6},{8,9},{9,8},{10,11... | collective-permute-start | bytes 1376264 | tf_op jit(solution)/shard_map/ppermute | solution.py:494
  91.8 10.5 %collective-permute-start.14 = (bf16[112,2048]{1,0:T(8,128)(2,1)S(1)}, bf16[112,2048]{1,0:T(8,128)(2,1)S(1)}, u32[]{:S(2)}, u32[]{:S(2)}) collective-permute-start(bf16[112,2048]{1,0:T(8,128)(2,1)S(1)} %get-tuple-element.35), channel_id=1, source_target_pairs={{0,1},{1,0},{2,3},{3,2},{4,5},{5,4},{6,7},{7,6},{8,9},{9,8},{10,11... | collective-permute-start | bytes 1376264 | tf_op jit(solution)/shard_map/ppermute | solution.py:494
  95.0 4.6 %collective-permute-start.21 = (bf16[112,2048]{1,0:T(8,128)(2,1)S(1)}, bf16[112,2048]{1,0:T(8,128)(2,1)S(1)}, u32[]{:S(2)}, u32[]{:S(2)}) collective-permute-start(bf16[112,2048]{1,0:T(8,128)(2,1)S(1)} %get-tuple-element.39), channel_id=1, source_target_pairs={{0,1},{1,0},{2,3},{3,2},{4,5},{5,4},{6,7},{7,6},{8,9},{9,8},{10,11... | collective-permute-start | bytes 1376264 | tf_op jit(solution)/shard_map/ppermute | solution.py:494
  97.7 3.5 %collective-permute-start.17 = (bf16[112,2048]{1,0:T(8,128)(2,1)S(1)}, bf16[112,2048]{1,0:T(8,128)(2,1)S(1)}, u32[]{:S(2)}, u32[]{:S(2)}) collective-permute-start(bf16[112,2048]{1,0:T(8,128)(2,1)S(1)} %get-tuple-element.37), channel_id=1, source_target_pairs={{0,1},{1,0},{2,3},{3,2},{4,5},{5,4},{6,7},{7,6},{8,9},{9,8},{10,11... | collective-permute-start | bytes 1376264 | tf_op jit(solution)/shard_map/ppermute | solution.py:494
  98.4 14.4 %collective-permute-start.26 = (bf16[112,2048]{1,0:T(8,128)(2,1)S(1)}, bf16[112,2048]{1,0:T(8,128)(2,1)S(1)}, u32[]{:S(2)}, u32[]{:S(2)}) collective-permute-start(bf16[112,2048]{1,0:T(8,128)(2,1)S(1)} %add_convert_fusion), channel_id=1, source_target_pairs={{0,6},{1,7},{2,4},{3,5},{4,2},{5,3},{6,0},{7,1},{8,14},{9,15},{10,... | collective-permute-start | bytes 1376264 | tf_op jit(solution)/shard_map/ppermute | solution.py:499
  99.8 21.9 %collective-permute-start.22 = (bf16[112,2048]{1,0:T(8,128)(2,1)S(1)}, bf16[112,2048]{1,0:T(8,128)(2,1)S(1)}, u32[]{:S(2)}, u32[]{:S(2)}) collective-permute-start(bf16[112,2048]{1,0:T(8,128)(2,1)S(1)} %add_convert_fusion.1), channel_id=1, source_target_pairs={{0,4},{1,5},{2,6},{3,7},{4,0},{5,1},{6,2},{7,3},{8,12},{9,13},{10,... | collective-permute-start | bytes 1376264 | tf_op jit(solution)/shard_map/ppermute | solution.py:499
  101.3 20.3 %collective-permute-start.18 = (bf16[112,2048]{1,0:T(8,128)(2,1)S(1)}, bf16[112,2048]{1,0:T(8,128)(2,1)S(1)}, u32[]{:S(2)}, u32[]{:S(2)}) collective-permute-start(bf16[112,2048]{1,0:T(8,128)(2,1)S(1)} %add_convert_fusion.2), channel_id=1, source_target_pairs={{0,2},{1,3},{2,0},{3,1},{4,6},{5,7},{6,4},{7,5},{8,10},{9,11},{10,... | collective-permute-start | bytes 1376264 | tf_op jit(solution)/shard_map/ppermute | solution.py:499

commit v4 on v3

--- a/solution.py
+++ b/solution.py
@@ -400,7 +400,7 @@
     merge_dots(place_ref, upper_ref[...], lower_ref[...], *weights, (own, x, y))
 
 
-def combine_kernel(place_ref, own_ref, x_ref, y_ref, from_y_ref, from_x_ref, out_ref):
+def combine_kernel(place_ref, own_ref, x_ref, y_ref, from_y_ref, from_x_ref, out_ref, low_ref, high_ref):
     wide = own_ref.shape[1]
     chip = place_ref[0]
     from_x, from_y = from_x_ref[...].astype(F32), from_y_ref[...].astype(F32)
@@ -412,6 +412,8 @@
     ]
     for m, part in enumerate(parts):
         out_ref[:, pl.ds(pl.multiple_of((chip ^ m) * wide, wide), wide)] = part.astype(BF16)
+    low_ref[...] = out_ref[:, : 2 * wide]
+    high_ref[...] = out_ref[:, 2 * wide :]
 
 
 def local_call(kernel, out, place, args, flops, name, mib=16):
@@ -444,21 +446,17 @@
     pair = jax.ShapeDtypeStruct((count, 4 * block), BF16)
     to_y, to_x = local_call(merge_other_kernel, [pair] * 2, place, [from_y, from_x] + weights, flops, "merge_other")
     back_y, back_x = chip_swap(to_y, 2), chip_swap(to_x, 1)
-    out = jax.ShapeDtypeStruct((count, 8 * block), BF16)
-    return local_call(combine_kernel, [out], place, [*own, back_y, back_x], 0, "combine")[0]
-
-
-def merge(upper, lower, merge_weight):
-    if lax.axis_size("lon") == 8:
-        return merge_by_squares(upper, lower, merge_weight)
-    weight = lax.all_gather(merge_weight, "lon", axis=1, tiled=True)
-    return jnp.dot(jnp.concatenate([upper, lower], axis=1), weight, preferred_element_type=F32).astype(BF16)
-
-
-def ffn_kernel(mine_ref, theirs_ref, up_ref, down_ref, out_mine_ref, out_theirs_ref, normed_ref, hidden_ref):
-    count = mine_ref.shape[0]
-    for k, ref in enumerate((mine_ref, theirs_ref)):
-        normed_ref[k * count : (k + 1) * count, :] = normalize(ref[...].astype(F32)).astype(BF16)
+    outs = [jax.ShapeDtypeStruct((count, n * block), BF16) for n in (8, 4, 4)]
+    return local_call(combine_kernel, outs, place, [*own, back_y, back_x], 0, "combine")
+
+
+def ffn_kernel(pieces, *refs):
+    inputs, (up_ref, down_ref, out_mine_ref, out_theirs_ref, normed_ref, hidden_ref) = refs[:-6], refs[-6:]
+    count = out_mine_ref.shape[0]
+    for k in range(2):
+        parts = [ref[...].astype(F32) for ref in inputs[k * pieces : (k + 1) * pieces]]
+        values = jnp.concatenate(parts, axis=1) if pieces > 1 else parts[0]
+        normed_ref[k * count : (k + 1) * count, :] = normalize(values).astype(BF16)
     hidden = hidden_ref.shape[1]
     step = 256
     for at in range(0, hidden, step):
@@ -472,21 +470,19 @@
 
 
 def feed_forward(mine, theirs, up, down):
-    count, width = mine.shape
-    hidden = up.shape[1]
+    count = mine[0].shape[0]
+    width, hidden = up.shape
     vmem = pl.BlockSpec(memory_space=pltpu.VMEM)
     return pl.pallas_call(
-        ffn_kernel,
-        in_specs=[vmem] * 4,
+        functools.partial(ffn_kernel, len(mine)),
+        in_specs=[vmem] * (2 * len(mine) + 2),
         out_specs=[vmem] * 2,
         out_shape=[jax.ShapeDtypeStruct((count, width), BF16)] * 2,
         scratch_shapes=[pltpu.VMEM((2 * count, width), BF16), pltpu.VMEM((2 * count, hidden), BF16)],
         compiler_params=params(20),
-        cost_estimate=pl.CostEstimate(
-            flops=8 * count * width * hidden, bytes_accessed=4 * width * hidden, transcendentals=2 * count * hidden
-        ),
+        cost_estimate=pl.CostEstimate(flops=2**10, bytes_accessed=2**10, transcendentals=0),
         name="feed_forward",
-    )(mine, theirs, up, down)
+    )(*mine, *theirs, up, down)
 
 
 def core_swap(value):
@@ -497,6 +493,42 @@
 def chip_swap(value, offset):
     size = lax.axis_size("lon")
     return lax.ppermute(value, "lon", [(i, i ^ (2 * offset)) for i in range(size)])
+
+
+def coarse_by_squares(upper, lower, merge_weight, up, down):
+    whole, low, high = merge_by_squares(upper, lower, merge_weight)
+    y_low, x_high = chip_swap(low, 2), chip_swap(high, 1)
+    y_high, x_low = chip_swap(high, 2), chip_swap(low, 1)
+    first = feed_forward([whole], [core_swap(whole)], up, down)
+    y_low, x_high, mine, theirs = lax.optimization_barrier((y_low, x_high, *first))
+    d_low, d_high = chip_swap(y_low, 1), chip_swap(x_high, 2)
+    total = whole.astype(F32) + mine.astype(F32) + core_swap(theirs).astype(F32)
+    sums = []
+    for m, pieces in ((1, [x_low, x_high]), (2, [y_low, y_high]), (3, [d_low, d_high])):
+        pairs = [core_swap(p) for p in pieces]
+        if m == 3:
+            *pairs, sums[0], sums[1] = lax.optimization_barrier((*pairs, *sums))
+        mine, theirs = feed_forward(pieces, pairs, up, down)
+        sums.append((mine.astype(F32) + core_swap(theirs).astype(F32)).astype(BF16))
+    for m in (1, 2, 3):
+        total = total + chip_swap(sums[m - 1], m).astype(F32)
+    return total
+
+
+def coarse_by_chips(upper, lower, merge_weight, up, down):
+    weight = lax.all_gather(merge_weight, "lon", axis=1, tiled=True)
+    patches = jnp.concatenate([upper, lower], axis=1)
+    coarse = jnp.dot(patches, weight, preferred_element_type=F32).astype(BF16)
+    chips = lax.axis_size("lon") // 2
+    arrived = [coarse] + [chip_swap(coarse, m) for m in range(1, chips)]
+    total = coarse.astype(F32)
+    for m in range(chips):
+        mine, theirs = feed_forward([arrived[m]], [core_swap(arrived[m])], up, down)
+        summed = mine.astype(F32) + core_swap(theirs).astype(F32)
+        if m:
+            summed = chip_swap(summed.astype(BF16), m).astype(F32)
+        total = total + summed
+    return total
 
 
 def per_device(tokens, qkv_weight, out_weight, merge_weight, up_weight, down_weight):
@@ -504,16 +536,8 @@
     bands = Bands(rows, columns)
     cells = rows * columns // 4
     middle_out, upper, lower = attention(bands, tokens, qkv_weight, out_weight)
-    coarse = merge(upper, lower, merge_weight)
-    chips = lax.axis_size("lon") // 2
-    arrived = [coarse] + [chip_swap(coarse, m) for m in range(1, chips)]
-    total = coarse.astype(F32)
-    for m in range(chips):
-        mine, theirs = feed_forward(arrived[m], core_swap(arrived[m]), up_weight, down_weight)
-        summed = mine.astype(F32) + core_swap(theirs).astype(F32)
-        if m:
-            summed = chip_swap(summed.astype(BF16), m).astype(F32)
-        total = total + summed
+    coarse = coarse_by_squares if lax.axis_size("lon") == 8 else coarse_by_chips
+    total = coarse(upper, lower, merge_weight, up_weight, down_weight)
     coarse_out = total[:cells].astype(jnp.bfloat16)
     return (middle_out, coarse_out.reshape(rows // 2, columns // 2, -1))
 

time: 123 us -> 124 us (level)
    ppermute x11 -> x14, waiting for transfers between devices: 0.03 us -> 2.26 us  [core_swap(): return lax.ppermute(value, 'lon', [(i, i ^ 1) for i in range(size)])]
    ppermute x12 -> x15, waiting for transfers between devices: 49.8 us -> 48.5 us  [chip_swap(): lax.ppermute(value, 'lon', [(i, i ^ 2 * offset) for i in range(size)])]
    ppermute x12 -> x15, starting transfers between devices: 13.1 us -> 13.8 us  [chip_swap(): lax.ppermute(value, 'lon', [(i, i ^ 2 * offset) for i in range(size)])]
    ppermute x11 -> x14, starting transfers between devices: 2.8 us -> 2.28 us  [core_swap(): return lax.ppermute(value, 'lon', [(i, i ^ 1) for i in range(size)])]
  transfers between devices with their start and end apart: 27 -> 33, of which waited for: 8 -> 16; matrix products, arithmetic and copies ran while one was open for 3% -> 3% of each run, Pallas kernels for 25% -> 22%
where the time goes in v4:
time: 124 us
  waiting for transfers between devices  50.8 us (41%)
  Pallas kernels  35.3 us (28%)
  starting transfers between devices  24.5 us (20%)
  local copies, waits for them, and re-layouts  11.5 us (9%)
    ppermute x15, waiting for transfers between devices, chip_swap(): lax.ppermute(value, 'lon', [(i, i ^ 2 * offset) for i in range(size)])  48.5 us
    pallas_call x3, Pallas kernels, vmem_call(): pl.pallas_call(kernel, in_specs=[vmem] * len(args), out_specs=[vmem] * le...  15.5 us
    ppermute x15, starting transfers between devices, chip_swap(): lax.ppermute(value, 'lon', [(i, i ^ 2 * offset) for i in range(size)])  13.8 us
    pallas_call x4, Pallas kernels, feed_forward(): pl.pallas_call(functools.partial(ffn_kernel, len(mine)), in_specs=[vmem]...  10.4 us
    pallas_call x3, Pallas kernels, local_call(): pl.pallas_call(kernel, in_specs=[pl.BlockSpec(memory_space=pltpu.SMEM)] +...  9.3 us
    ppermute x4, starting transfers between devices, shift(): return lax.ppermute(part, axis, pairs)  8.43 us
    unnamed x36, local copies, waits for them, and re-layouts  5.63 us
    slice x1, local copies, waits for them, and re-layouts, merge_by_squares(): y = chip_swap(merge_weight[half:], 2)  3.07 us
  transfers between devices with their start and end apart: 33, of which 16 were waited for; matrix products, arithmetic and copies ran while one was open for 3% of the time, Pallas kernels for 22%

profile of v4, /device:TPU:0, one launch (start us, length us, event | category | flops | bytes accessed | tf_op | source)
XLA Modules:
  0.0 124.2 jit_solution(17539110361493539613)
XLA Ops:
  0.6 1.8 %fusion.7 = (bf16[18,8,1024]{2,1,0:T(8,128)(2,1)S(1)}, bf16[18,8,1024]{2,1,0:T(8,128)(2,1)}) fusion(bf16[18,24,1024]{2,1,0:T(8,128)(2,1)} %tokens_ref.3), kind=kLoop, calls=%fused_computation.23 | loop fusion | bytes 1179648 | tf_op jit(solution)/shard_map/slice | solution.py:293
  2.4 3.3 %collective-permute-start.1 = (bf16[18,8,1024]{2,1,0:T(8,128)(2,1)}, bf16[18,8,1024]{2,1,0:T(8,128)(2,1)S(1)}, u32[]{:S(2)}, u32[]{:S(2)}) collective-permute-start(bf16[18,8,1024]{2,1,0:T(8,128)(2,1)} %get-tuple-element.69), channel_id=1, source_target_pairs={{0,7},{1,0},{2,1},{3,2},{4,3},{5,4},{6,5},{7,6},{8,15},{9,8},{10,9... | collective-permute-start | bytes 884744 | tf_op jit(solution)/shard_map/ppermute | solution.py:343
  5.8 3.1 %fusion.5 = (bf16[2048,256]{1,0:T(8,128)(2,1)}, bf16[2048,256]{1,0:T(8,128)(2,1)}) fusion(bf16[4096,256]{1,0:T(8,128)(2,1)} %refs_0_.3), kind=kLoop, calls=%fused_computation.21 | loop fusion | bytes 4194304 | tf_op jit(solution)/shard_map/slice | solution.py:437
  8.9 2.0 %collective-permute-start.5 = (bf16[2048,256]{1,0:T(8,128)(2,1)}, bf16[2048,256]{1,0:T(8,128)(2,1)S(1)}, u32[]{:S(2)}, u32[]{:S(2)}) collective-permute-start(bf16[2048,256]{1,0:T(8,128)(2,1)} %get-tuple-element.65), channel_id=1, source_target_pairs={{0,2},{1,3},{2,0},{3,1},{4,6},{5,7},{6,4},{7,5},{8,10},{9,11},{10,... | collective-permute-start | bytes 3145736 | tf_op jit(solution)/shard_map/ppermute | solution.py:495
  10.8 1.5 %collective-permute-start.6 = (bf16[2048,256]{1,0:T(8,128)(2,1)}, bf16[2048,256]{1,0:T(8,128)(2,1)}, u32[]{:S(2)}, u32[]{:S(2)}) collective-permute-start(bf16[2048,256]{1,0:T(8,128)(2,1)} %get-tuple-element.64), channel_id=1, source_target_pairs={{0,4},{1,5},{2,6},{3,7},{4,0},{5,1},{6,2},{7,3},{8,12},{9,13},{10,... | collective-permute-start | bytes 3145736 | tf_op jit(solution)/shard_map/ppermute | solution.py:495
  12.4 2.8 %copy-done.5 = bf16[1024,3072]{1,0:T(8,128)(2,1)S(1)} copy-done((bf16[1024,3072]{1,0:T(8,128)(2,1)S(1)}, bf16[1024,3072]{1,0:T(8,128)(2,1)}, u32[]{:S(2)}) %copy-start.5) | copy-done | bytes 6291480
  15.2 3.4 %own_projection.1.own_ref = bf16[448,3072]{1,0:T(8,128)(2,1)S(1)} custom-call(bf16[18,24,1024]{2,1,0:T(8,128)(2,1)S(1)} %copy-done.3, bf16[1024,3072]{1,0:T(8,128)(2,1)S(1)} %copy-done.5), custom_call_target="tpu_custom_call" | custom-call | flops 2818572288 | bytes 1048576 | tf_op jit(solution)/shard_map/own_projection/pallas_call | solution.py:278
  18.6 0.1 or_select_fusion.bias_ref
  18.8 3.5 %collective-permute-start.2 = (bf16[3,40,1024]{2,1,0:T(8,128)(2,1)S(1)}, bf16[3,40,1024]{2,1,0:T(8,128)(2,1)S(1)}, u32[]{:S(2)}, u32[]{:S(2)}) collective-permute-start(bf16[3,40,1024]{2,1,0:T(8,128)(2,1)S(1)} %pad_maximum_fusion), channel_id=1, source_target_pairs={{0,8},{8,16},{16,24},{1,9},{9,17},{17,25},{2,10},{10,18},{18,26},{... | collective-permute-start | bytes 737288 | tf_op jit(solution)/shard_map/ppermute | solution.py:343
  22.3 1.6 %collective-permute-start.3 = (bf16[3,40,1024]{2,1,0:T(8,128)(2,1)S(1)}, bf16[3,40,1024]{2,1,0:T(8,128)(2,1)S(1)}, u32[]{:S(2)}, u32[]{:S(2)}) collective-permute-start(bf16[3,40,1024]{2,1,0:T(8,128)(2,1)S(1)} %pad_maximum_fusion.1), channel_id=1, source_target_pairs={{8,0},{16,8},{24,16},{9,1},{17,9},{25,17},{10,2},{18,10},{26,18},{... | collective-permute-start | bytes 737288 | tf_op jit(solution)/shard_map/ppermute | solution.py:343
  24.0 2.8 %copy-done.6 = bf16[1024,3072]{1,0:T(8,128)(2,1)S(1)} copy-done((bf16[1024,3072]{1,0:T(8,128)(2,1)S(1)}, bf16[1024,3072]{1,0:T(8,128)(2,1)}, u32[]{:S(2)}) %copy-start.6) | copy-done | bytes 6291480
  26.8 5.4 %middle_attention.1 = (bf16[288,2048]{1,0:T(8,128)(2,1)S(1)}, bf16[288,1024]{1,0:T(8,128)(2,1)S(1)}) custom-call(bf16[18,8,1024]{2,1,0:T(8,128)(2,1)S(1)} %collective-permute-done.west_ref, bf16[18,8,1024]{2,1,0:T(8,128)(2,1)S(1)} %collective-permute-done.1.east_ref, bf16[448,3072]{1,0:T(8,128)(2,1)S(1)} %own_projection.1.own_ref, ...), custom_call_target="tpu_custom_call" | custom-call | flops 5000000000 | bytes 1048576 | tf_op jit(solution)/shard_map/middle_attention/pallas_call | solution.py:278
  32.3 6.8 %edge_attention.1 = (bf16[18,24,1024]{2,1,0:T(8,128)(2,1)}, bf16[112,2048]{1,0:T(8,128)(2,1)}, bf16[112,2048]{1,0:T(8,128)(2,1)}) custom-call(bf16[18,24,1024]{2,1,0:T(8,128)(2,1)S(1)} %copy-done.4, bf16[3,40,1024]{2,1,0:T(8,128)(2,1)S(1)} %collective-permute-done.2.north_ref, bf16[3,40,1024]{2,1,0:T(8,128)(2,1)S(1)} %collective-permute-done.3.south_ref, ...), custom_call_target="tpu_custom_call" | custom-call | flops 6000000000 | bytes 1048576 | tf_op jit(solution)/shard_map/edge_attention/pallas_call | solution.py:278
  39.1 0.5 collective-permute-start.8
  39.6 0.5 collective-permute-start.9
  40.2 0.1 pad_add_fusion.place_ref
  40.2 12.2 %collective-permute-done.9.upper_ref = bf16[112,2048]{1,0:T(8,128)(2,1)} collective-permute-done((bf16[112,2048]{1,0:T(8,128)(2,1)}, bf16[112,2048]{1,0:T(8,128)(2,1)}, u32[]{:S(2)}, u32[]{:S(2)}) %collective-permute-start.9) | collective-permute-done | bytes 458784 | tf_op jit(solution)/shard_map/ppermute | solution.py:495
  52.4 0.2 collective-permute-done.10.lower_ref
  52.7 4.1 %merge_other.1 = (bf16[112,1024]{1,0:T(8,128)(2,1)S(1)}, bf16[112,1024]{1,0:T(8,128)(2,1)S(1)}) custom-call(s32[2]{0:T(128)S(1)} %pad_add_fusion.place_ref, bf16[112,2048]{1,0:T(8,128)(2,1)} %collective-permute-done.9.upper_ref, bf16[112,2048]{1,0:T(8,128)(2,1)} %collective-permute-done.10.lower_ref, bf16[4096,256]{1,0:T(8,128)(2,1)S(1)} %copy-done.2, ...), custom_call_target="tpu_custom_call" | custom-call | flops 939524096 | bytes 1048576 | tf_op jit(solution)/shard_map/merge_other/pallas_call | solution.py:421
  56.8 1.6 %collective-permute-start.11 = (bf16[112,1024]{1,0:T(8,128)(2,1)S(1)}, bf16[112,1024]{1,0:T(8,128)(2,1)S(1)}, u32[]{:S(2)}, u32[]{:S(2)}) collective-permute-start(bf16[112,1024]{1,0:T(8,128)(2,1)S(1)} %get-tuple-element.43), channel_id=1, source_target_pairs={{0,4},{1,5},{2,6},{3,7},{4,0},{5,1},{6,2},{7,3},{8,12},{9,13},{10,... | collective-permute-start | bytes 688136 | tf_op jit(solution)/shard_map/ppermute | solution.py:495
  58.4 0.3 collective-permute-start.12
  58.7 4.5 %merge_own.1 = (f32[112,512]{1,0:T(8,128)S(1)}, f32[112,512]{1,0:T(8,128)S(1)}, f32[112,512]{1,0:T(8,128)S(1)}) custom-call(s32[2]{0:T(128)S(1)} %pad_add_fusion.place_ref, bf16[112,2048]{1,0:T(8,128)(2,1)} %get-tuple-element.36.upper_ref, bf16[112,2048]{1,0:T(8,128)(2,1)} %get-tuple-element.37.lower_ref, bf16[4096,256]{1,0:T(8,128)(2,1)S(1)} %copy-done.2, ...), custom_call_target="tpu_custom_call" | custom-call | flops 939524096 | bytes 1048576 | tf_op jit(solution)/shard_map/merge_own/pallas_call | solution.py:421
  63.1 0.2 collective-permute-done.11.from_y_ref
  63.3 1.2 collective-permute-done.12.from_x_ref
  64.5 0.7 combine.1
  65.2 0.1 collective-permute-start.15
  65.3 0.7 collective-permute-start.21
  66.0 0.4 collective-permute-start.13
  66.4 1.6 %collective-permute-start.14 = (bf16[112,1024]{1,0:T(8,128)(2,1)S(1)}, bf16[112,1024]{1,0:T(8,128)(2,1)S(1)}, u32[]{:S(2)}, u32[]{:S(2)}) collective-permute-start(bf16[112,1024]{1,0:T(8,128)(2,1)S(1)} %get-tuple-element.47), channel_id=1, source_target_pairs={{0,2},{1,3},{2,0},{3,1},{4,6},{5,7},{6,4},{7,5},{8,10},{9,11},{10,... | collective-permute-start | bytes 688136 | tf_op jit(solution)/shard_map/ppermute | solution.py:495
  67.9 5.8 %collective-permute-done.21.refs_0_ = bf16[112,1024]{1,0:T(8,128)(2,1)S(1)} collective-permute-done((bf16[112,1024]{1,0:T(8,128)(2,1)S(1)}, bf16[112,1024]{1,0:T(8,128)(2,1)S(1)}, u32[]{:S(2)}, u32[]{:S(2)}) %collective-permute-start.21) | collective-permute-done | bytes 229408 | tf_op jit(solution)/shard_map/ppermute | solution.py:495
  73.8 2.6 %feed_forward.4 = (bf16[112,2048]{1,0:T(8,128)(2,1)S(1)}, bf16[112,2048]{1,0:T(8,128)(2,1)S(1)}) custom-call(bf16[112,2048]{1,0:T(8,128)(2,1)S(1)} %get-tuple-element.45.refs_0_, bf16[112,2048]{1,0:T(8,128)(2,1)S(1)} %collective-permute-done.15.refs_1_, bf16[2048,1024]{1,0:T(8,128)(2,1)S(1)} %copy-done, bf16[1024,2048]{1,0:T(8,128)(2,1)S(1)} %copy-done.1), custom_call_target="tpu_custom_call" | custom-call | flops 1024 | bytes 1024 | tf_op jit(solution)/shard_map/feed_forward/pallas_call | solution.py:476
  76.4 1.8 %collective-permute-done.14.refs_1_ = bf16[112,1024]{1,0:T(8,128)(2,1)S(1)} collective-permute-done((bf16[112,1024]{1,0:T(8,128)(2,1)S(1)}, bf16[112,1024]{1,0:T(8,128)(2,1)S(1)}, u32[]{:S(2)}, u32[]{:S(2)}) %collective-permute-start.14) | collective-permute-done | bytes 229408 | tf_op jit(solution)/shard_map/ppermute | solution.py:495
  78.2 0.6 collective-permute-start.25
  78.8 0.9 collective-permute-done.23.refs_3_
  79.7 2.6 %feed_forward.5 = (bf16[112,2048]{1,0:T(8,128)(2,1)S(1)}, bf16[112,2048]{1,0:T(8,128)(2,1)S(1)}) custom-call(bf16[112,1024]{1,0:T(8,128)(2,1)S(1)} %collective-permute-done.21.refs_0_, bf16[112,1024]{1,0:T(8,128)(2,1)S(1)} %collective-permute-done.14.refs_1_, bf16[112,1024]{1,0:T(8,128)(2,1)S(1)} %collective-permute-done.22.refs_2_, ...), custom_call_target="tpu_custom_call" | custom-call | flops 1024 | bytes 1024 | tf_op jit(solution)/shard_map/feed_forward/pallas_call | solution.py:476
  82.3 0.2 collective-permute-start.24
  82.5 3.7 %collective-permute-done.25.refs_1_ = bf16[112,1024]{1,0:T(8,128)(2,1)S(1)} collective-permute-done((bf16[112,1024]{1,0:T(8,128)(2,1)S(1)}, bf16[112,1024]{1,0:T(8,128)(2,1)S(1)}, u32[]{:S(2)}, u32[]{:S(2)}) %collective-permute-start.25) | collective-permute-done | bytes 229408 | tf_op jit(solution)/shard_map/ppermute | solution.py:495
  86.2 0.5 collective-permute-start.26
  86.7 0.7 collective-permute-start.17
  87.4 0.4 collective-permute-start.19
  87.8 0.2 collective-permute-done.26.refs_2_
  88.0 2.6 %feed_forward.6 = (bf16[112,2048]{1,0:T(8,128)(2,1)S(1)}, bf16[112,2048]{1,0:T(8,128)(2,1)S(1)}) custom-call(bf16[112,1024]{1,0:T(8,128)(2,1)S(1)} %collective-permute-done.13.refs_0_, bf16[112,1024]{1,0:T(8,128)(2,1)S(1)} %collective-permute-done.25.refs_1_, bf16[112,1024]{1,0:T(8,128)(2,1)S(1)} %collective-permute-done.26.refs_2_, ...), custom_call_target="tpu_custom_call" | custom-call | flops 1024 | bytes 1024 | tf_op jit(solution)/shard_map/feed_forward/pallas_call | solution.py:476
  90.6 0.3 collective-permute-start.28
  90.9 3.3 %collective-permute-done.17.refs_0_ = bf16[112,1024]{1,0:T(8,128)(2,1)S(1)} collective-permute-done((bf16[112,1024]{1,0:T(8,128)(2,1)S(1)}, bf16[112,1024]{1,0:T(8,128)(2,1)S(1)}, u32[]{:S(2)}, u32[]{:S(2)}) %collective-permute-start.17) | collective-permute-done | bytes 229408 | tf_op jit(solution)/shard_map/ppermute | solution.py:495
  94.2 0.4 collective-permute-done.19.refs_1_
  94.6 0.1 collective-permute-start.20
  94.8 0.1 add_convert_fusion.2
  94.9 0.1 add_convert_fusion.1
  95.0 0.7 collective-permute-done.18.refs_2_
  95.7 0.4 collective-permute-done.20.refs_3_
  96.1 2.6 %feed_forward.7 = (bf16[112,2048]{1,0:T(8,128)(2,1)S(1)}, bf16[112,2048]{1,0:T(8,128)(2,1)S(1)}) custom-call(bf16[112,1024]{1,0:T(8,128)(2,1)S(1)} %collective-permute-done.17.refs_0_, bf16[112,1024]{1,0:T(8,128)(2,1)S(1)} %collective-permute-done.19.refs_1_, bf16[112,1024]{1,0:T(8,128)(2,1)S(1)} %collective-permute-done.18.refs_2_, ...), custom_call_target="tpu_custom_call" | custom-call | flops 1024 | bytes 1024 | tf_op jit(solution)/shard_map/feed_forward/pallas_call | solution.py:476
  98.7 0.2 collective-permute-start.31
  98.9 0.4 collective-permute-start.16
  99.3 0.6 collective-permute-start.30
  99.9 1.4 %collective-permute-start.29 = (bf16[112,2048]{1,0:T(8,128)(2,1)S(1)}, bf16[112,2048]{1,0:T(8,128)(2,1)S(1)}, u32[]{:S(2)}, u32[]{:S(2)}) collective-permute-start(bf16[112,2048]{1,0:T(8,128)(2,1)S(1)} %add_convert_fusion.2), channel_id=1, source_target_pairs={{0,2},{1,3},{2,0},{3,1},{4,6},{5,7},{6,4},{7,5},{8,10},{9,11},{10,... | collective-permute-start | bytes 1376264 | tf_op jit(solution)/shard_map/ppermute | solution.py:495
  101.3 0.1 add_convert_fusion
  101.4 1.6 %collective-permute-start.32 = (bf16[112,2048]{1,0:T(8,128)(2,1)S(1)}, bf16[112,2048]{1,0:T(8,128)(2,1)S(1)}, u32[]{:S(2)}, u32[]{:S(2)}) collective-permute-start(bf16[112,2048]{1,0:T(8,128)(2,1)S(1)} %add_convert_fusion), channel_id=1, source_target_pairs={{0,6},{1,7},{2,4},{3,5},{4,2},{5,3},{6,0},{7,1},{8,14},{9,15},{10,... | collective-permute-start | bytes 1376264 | tf_op jit(solution)/shard_map/ppermute | solution.py:495
  103.0 0.1 convert_element_type.46
  103.1 0.1 convert_element_type.47
  103.2 8.7 %collective-permute-done.30 = bf16[112,2048]{1,0:T(8,128)(2,1)S(1)} collective-permute-done((bf16[112,2048]{1,0:T(8,128)(2,1)S(1)}, bf16[112,2048]{1,0:T(8,128)(2,1)S(1)}, u32[]{:S(2)}, u32[]{:S(2)}) %collective-permute-start.30) | collective-permute-done | bytes 458784 | tf_op jit(solution)/shard_map/ppermute | solution.py:495
  111.9 1.4 %collective-permute-done.29 = bf16[112,2048]{1,0:T(8,128)(2,1)S(1)} collective-permute-done((bf16[112,2048]{1,0:T(8,128)(2,1)S(1)}, bf16[112,2048]{1,0:T(8,128)(2,1)S(1)}, u32[]{:S(2)}, u32[]{:S(2)}) %collective-permute-start.29) | collective-permute-done | bytes 458784 | tf_op jit(solution)/shard_map/ppermute | solution.py:495
  113.3 9.6 %collective-permute-done.32 = bf16[112,2048]{1,0:T(8,128)(2,1)S(1)} collective-permute-done((bf16[112,2048]{1,0:T(8,128)(2,1)S(1)}, bf16[112,2048]{1,0:T(8,128)(2,1)S(1)}, u32[]{:S(2)}, u32[]{:S(2)}) %collective-permute-start.32) | collective-permute-done | bytes 458784 | tf_op jit(solution)/shard_map/ppermute | solution.py:495
  122.9 0.4 fusion.4
  123.3 0.9 reshape.45
  (66 shorter events, 0.3 us)
Async XLA Ops:
  2.4 16.3 %collective-permute-start.1 = (bf16[18,8,1024]{2,1,0:T(8,128)(2,1)}, bf16[18,8,1024]{2,1,0:T(8,128)(2,1)S(1)}, u32[]{:S(2)}, u32[]{:S(2)}) collective-permute-start(bf16[18,8,1024]{2,1,0:T(8,128)(2,1)} %get-tuple-element.69), channel_id=1, source_target_pairs={{0,7},{1,0},{2,1},{3,2},{4,3},{5,4},{6,5},{7,6},{8,15},{9,8},{10,9... | collective-permute-start | bytes 884744 | tf_op jit(solution)/shard_map/ppermute | solution.py:343
  5.8 6.6 %copy-start.3 = (bf16[18,24,1024]{2,1,0:T(8,128)(2,1)S(1)}, bf16[18,24,1024]{2,1,0:T(8,128)(2,1)}, u32[]{:S(2)}) copy-start(bf16[18,24,1024]{2,1,0:T(8,128)(2,1)} %tokens_ref.3) | copy-start | bytes 2654212
  5.8 13.0 %collective-permute-start = (bf16[18,8,1024]{2,1,0:T(8,128)(2,1)S(1)}, bf16[18,8,1024]{2,1,0:T(8,128)(2,1)S(1)}, u32[]{:S(2)}, u32[]{:S(2)}) collective-permute-start(bf16[18,8,1024]{2,1,0:T(8,128)(2,1)S(1)} %get-tuple-element.68), channel_id=1, source_target_pairs={{0,1},{1,2},{2,3},{3,4},{4,5},{5,6},{6,7},{7,0},{8,9},{9,10},{10,1... | collective-permute-start | bytes 884744 | tf_op jit(solution)/shard_map/ppermute | solution.py:343
  5.8 46.9 %collective-permute-start.4 = (bf16[4096,256]{1,0:T(8,128)(2,1)}, bf16[4096,256]{1,0:T(8,128)(2,1)}, u32[]{:S(2)}, u32[]{:S(2)}) collective-permute-start(bf16[4096,256]{1,0:T(8,128)(2,1)} %refs_0_.3), channel_id=1, source_target_pairs={{0,1},{1,0},{2,3},{3,2},{4,5},{5,4},{6,7},{7,6},{8,9},{9,8},{10,11... | collective-permute-start | bytes 6291464 | tf_op jit(solution)/shard_map/ppermute | solution.py:490
  8.9 30.2 %collective-permute-start.5 = (bf16[2048,256]{1,0:T(8,128)(2,1)}, bf16[2048,256]{1,0:T(8,128)(2,1)S(1)}, u32[]{:S(2)}, u32[]{:S(2)}) collective-permute-start(bf16[2048,256]{1,0:T(8,128)(2,1)} %get-tuple-element.65), channel_id=1, source_target_pairs={{0,2},{1,3},{2,0},{3,1},{4,6},{5,7},{6,4},{7,5},{8,10},{9,11},{10,... | collective-permute-start | bytes 3145736 | tf_op jit(solution)/shard_map/ppermute | solution.py:495
  10.8 28.2 %collective-permute-start.6 = (bf16[2048,256]{1,0:T(8,128)(2,1)}, bf16[2048,256]{1,0:T(8,128)(2,1)}, u32[]{:S(2)}, u32[]{:S(2)}) collective-permute-start(bf16[2048,256]{1,0:T(8,128)(2,1)} %get-tuple-element.64), channel_id=1, source_target_pairs={{0,4},{1,5},{2,6},{3,7},{4,0},{5,1},{6,2},{7,3},{8,12},{9,13},{10,... | collective-permute-start | bytes 3145736 | tf_op jit(solution)/shard_map/ppermute | solution.py:495
  12.4 2.8 %copy-start.5 = (bf16[1024,3072]{1,0:T(8,128)(2,1)S(1)}, bf16[1024,3072]{1,0:T(8,128)(2,1)}, u32[]{:S(2)}) copy-start(bf16[1024,3072]{1,0:T(8,128)(2,1)} %weight_ref.5) | copy-start | bytes 18874372
  15.2 8.7 %copy-start.9 = (bf16[576,144]{1,0:T(8,128)(2,1)S(1)}, bf16[576,144]{1,0:T(8,128)(2,1)}, u32[]{:S(2)}) copy-start(bf16[576,144]{1,0:T(8,128)(2,1)} %constant.71.clone.rest_1_) | copy-start | bytes 497668
  15.2 8.7 %copy-start.10 = (bf16[576,256]{1,0:T(8,128)(2,1)S(1)}, bf16[576,256]{1,0:T(8,128)(2,1)}, u32[]{:S(2)}) copy-start(bf16[576,256]{1,0:T(8,128)(2,1)} %constant.72.clone.rest_2_) | copy-start | bytes 884740
  15.2 8.8 %copy-start.11 = (bf16[144,576]{1,0:T(8,128)(2,1)S(1)}, bf16[144,576]{1,0:T(8,128)(2,1)}, u32[]{:S(2)}) copy-start(bf16[144,576]{1,0:T(8,128)(2,1)} %constant.73.clone.rest_3_) | copy-start | bytes 497668
  15.2 8.8 %copy-start.15 = (bf16[240,240]{1,0:T(8,128)(2,1)S(1)}, bf16[240,240]{1,0:T(8,128)(2,1)}, u32[]{:S(2)}) copy-start(bf16[240,240]{1,0:T(8,128)(2,1)} %constant.70.clone.rest_0_) | copy-start | bytes 345604
  18.8 13.4 %collective-permute-start.2 = (bf16[3,40,1024]{2,1,0:T(8,128)(2,1)S(1)}, bf16[3,40,1024]{2,1,0:T(8,128)(2,1)S(1)}, u32[]{:S(2)}, u32[]{:S(2)}) collective-permute-start(bf16[3,40,1024]{2,1,0:T(8,128)(2,1)S(1)} %pad_maximum_fusion), channel_id=1, source_target_pairs={{0,8},{8,16},{16,24},{1,9},{9,17},{17,25},{2,10},{10,18},{18,26},{... | collective-permute-start | bytes 737288 | tf_op jit(solution)/shard_map/ppermute | solution.py:343
  22.3 9.9 %copy-start.4 = (bf16[18,24,1024]{2,1,0:T(8,128)(2,1)S(1)}, bf16[18,24,1024]{2,1,0:T(8,128)(2,1)}, u32[]{:S(2)}) copy-start(bf16[18,24,1024]{2,1,0:T(8,128)(2,1)} %tokens_ref.3) | copy-start | bytes 2654212
  22.3 9.9 %collective-permute-start.3 = (bf16[3,40,1024]{2,1,0:T(8,128)(2,1)S(1)}, bf16[3,40,1024]{2,1,0:T(8,128)(2,1)S(1)}, u32[]{:S(2)}, u32[]{:S(2)}) collective-permute-start(bf16[3,40,1024]{2,1,0:T(8,128)(2,1)S(1)} %pad_maximum_fusion.1), channel_id=1, source_target_pairs={{8,0},{16,8},{24,16},{9,1},{17,9},{25,17},{10,2},{18,10},{26,18},{... | collective-permute-start | bytes 737288 | tf_op jit(solution)/shard_map/ppermute | solution.py:343
  24.0 2.8 %copy-start.6 = (bf16[1024,3072]{1,0:T(8,128)(2,1)S(1)}, bf16[1024,3072]{1,0:T(8,128)(2,1)}, u32[]{:S(2)}) copy-start(bf16[1024,3072]{1,0:T(8,128)(2,1)} %weight_ref.5) | copy-start | bytes 18874372
  26.8 5.5 %copy-start.7 = (bf16[1024,1024]{1,0:T(8,128)(2,1)S(1)}, bf16[1024,1024]{1,0:T(8,128)(2,1)}, u32[]{:S(2)}) copy-start(bf16[1024,1024]{1,0:T(8,128)(2,1)} %out_w_ref.1) | copy-start | bytes 6291460
  26.8 5.5 %copy-start.8 = (bf16[448,432]{1,0:T(8,128)(2,1)S(1)}, bf16[448,432]{1,0:T(8,128)(2,1)}, u32[]{:S(2)}) copy-start(bf16[448,432]{1,0:T(8,128)(2,1)} %constant.74.clone.patch_ref) | copy-start | bytes 1161220
  26.8 5.5 %copy-start.12 = (bf16[304,256]{1,0:T(8,128)(2,1)S(1)}, bf16[304,256]{1,0:T(8,128)(2,1)}, u32[]{:S(2)}) copy-start(bf16[304,256]{1,0:T(8,128)(2,1)} %constant.77.clone.rest_2_.rest_6_) | copy-start | bytes 466948
  26.8 5.5 %copy-start.13 = (bf16[240,256]{1,0:T(8,128)(2,1)S(1)}, bf16[240,256]{1,0:T(8,128)(2,1)}, u32[]{:S(2)}) copy-start(bf16[240,256]{1,0:T(8,128)(2,1)} %constant.75.clone.rest_0_) | copy-start | bytes 368644
  26.8 5.5 %copy-start.14 = (bf16[240,256]{1,0:T(8,128)(2,1)S(1)}, bf16[240,256]{1,0:T(8,128)(2,1)}, u32[]{:S(2)}) copy-start(bf16[240,256]{1,0:T(8,128)(2,1)} %constant.79.clone.rest_4_) | copy-start | bytes 368644
  26.8 5.5 %copy-start.16 = (bf16[304,80]{1,0:T(8,128)(2,1)S(1)}, bf16[304,80]{1,0:T(8,128)(2,1)}, u32[]{:S(2)}) copy-start(bf16[304,80]{1,0:T(8,128)(2,1)} %constant.76.clone.rest_1_.rest_5_) | copy-start | bytes 145924
  26.8 5.5 %copy-start.17 = (bf16[80,304]{1,0:T(8,128)(2,1)S(1)}, bf16[80,304]{1,0:T(8,128)(2,1)}, u32[]{:S(2)}) copy-start(bf16[80,304]{1,0:T(8,128)(2,1)} %constant.78.clone.rest_3_.rest_7_) | copy-start | bytes 145924
  32.3 20.4 %copy-start.2 = (bf16[4096,256]{1,0:T(8,128)(2,1)S(1)}, bf16[4096,256]{1,0:T(8,128)(2,1)}, u32[]{:S(2)}) copy-start(bf16[4096,256]{1,0:T(8,128)(2,1)} %refs_0_.3) | copy-start | bytes 6291460
  39.1 13.6 %collective-permute-start.7 = (bf16[2048,256]{1,0:T(8,128)(2,1)S(1)}, bf16[2048,256]{1,0:T(8,128)(2,1)}, u32[]{:S(2)}, u32[]{:S(2)}) collective-permute-start(bf16[2048,256]{1,0:T(8,128)(2,1)S(1)} %collective-permute-done.5.refs_2_), channel_id=1, source_target_pairs={{0,1},{1,0},{2,3},{3,2},{4,5},{5,4},{6,7},{7,6},{8,9},{9,8},{10,11... | collective-permute-start | bytes 3145736 | tf_op jit(solution)/shard_map/ppermute | solution.py:490
  39.1 13.6 %collective-permute-start.8 = (bf16[2048,256]{1,0:T(8,128)(2,1)}, bf16[2048,256]{1,0:T(8,128)(2,1)}, u32[]{:S(2)}, u32[]{:S(2)}) collective-permute-start(bf16[2048,256]{1,0:T(8,128)(2,1)} %collective-permute-done.6.refs_4_), channel_id=1, source_target_pairs={{0,1},{1,0},{2,3},{3,2},{4,5},{5,4},{6,7},{7,6},{8,9},{9,8},{10,11... | collective-permute-start | bytes 3145736 | tf_op jit(solution)/shard_map/ppermute | solution.py:490
  39.6 12.8 %collective-permute-start.9 = (bf16[112,2048]{1,0:T(8,128)(2,1)}, bf16[112,2048]{1,0:T(8,128)(2,1)}, u32[]{:S(2)}, u32[]{:S(2)}) collective-permute-start(bf16[112,2048]{1,0:T(8,128)(2,1)} %get-tuple-element.36.upper_ref), channel_id=1, source_target_pairs={{0,4},{1,5},{2,6},{3,7},{4,0},{5,1},{6,2},{7,3},{8,12},{9,13},{10,... | collective-permute-start | bytes 1376264 | tf_op jit(solution)/shard_map/ppermute | solution.py:495
  40.1 12.5 %collective-permute-start.10 = (bf16[112,2048]{1,0:T(8,128)(2,1)}, bf16[112,2048]{1,0:T(8,128)(2,1)}, u32[]{:S(2)}, u32[]{:S(2)}) collective-permute-start(bf16[112,2048]{1,0:T(8,128)(2,1)} %get-tuple-element.37.lower_ref), channel_id=1, source_target_pairs={{0,2},{1,3},{2,0},{3,1},{4,6},{5,7},{6,4},{7,5},{8,10},{9,11},{10,... | collective-permute-start | bytes 1376264 | tf_op jit(solution)/shard_map/ppermute | solution.py:495
  56.8 6.5 %collective-permute-start.11 = (bf16[112,1024]{1,0:T(8,128)(2,1)S(1)}, bf16[112,1024]{1,0:T(8,128)(2,1)S(1)}, u32[]{:S(2)}, u32[]{:S(2)}) collective-permute-start(bf16[112,1024]{1,0:T(8,128)(2,1)S(1)} %get-tuple-element.43), channel_id=1, source_target_pairs={{0,4},{1,5},{2,6},{3,7},{4,0},{5,1},{6,2},{7,3},{8,12},{9,13},{10,... | collective-permute-start | bytes 688136 | tf_op jit(solution)/shard_map/ppermute | solution.py:495
  58.4 6.1 %collective-permute-start.12 = (bf16[112,1024]{1,0:T(8,128)(2,1)S(1)}, bf16[112,1024]{1,0:T(8,128)(2,1)S(1)}, u32[]{:S(2)}, u32[]{:S(2)}) collective-permute-start(bf16[112,1024]{1,0:T(8,128)(2,1)S(1)} %get-tuple-element.44), channel_id=1, source_target_pairs={{0,2},{1,3},{2,0},{3,1},{4,6},{5,7},{6,4},{7,5},{8,10},{9,11},{10,... | collective-permute-start | bytes 688136 | tf_op jit(solution)/shard_map/ppermute | solution.py:495
  58.6 15.1 %copy-start = (bf16[2048,1024]{1,0:T(8,128)(2,1)S(1)}, bf16[2048,1024]{1,0:T(8,128)(2,1)}, u32[]{:S(2)}) copy-start(bf16[2048,1024]{1,0:T(8,128)(2,1)} %refs_4_.5) | copy-start | bytes 12582916
  58.7 15.1 %copy-start.1 = (bf16[1024,2048]{1,0:T(8,128)(2,1)S(1)}, bf16[1024,2048]{1,0:T(8,128)(2,1)}, u32[]{:S(2)}) copy-start(bf16[1024,2048]{1,0:T(8,128)(2,1)} %refs_5_.5) | copy-start | bytes 12582916
  65.2 8.6 %collective-permute-start.15 = (bf16[112,2048]{1,0:T(8,128)(2,1)S(1)}, bf16[112,2048]{1,0:T(8,128)(2,1)S(1)}, u32[]{:S(2)}, u32[]{:S(2)}) collective-permute-start(bf16[112,2048]{1,0:T(8,128)(2,1)S(1)} %get-tuple-element.45.refs_0_), channel_id=1, source_target_pairs={{0,1},{1,0},{2,3},{3,2},{4,5},{5,4},{6,7},{7,6},{8,9},{9,8},{10,11... | collective-permute-start | bytes 1376264 | tf_op jit(solution)/shard_map/ppermute | solution.py:490
  65.3 8.5 %collective-permute-start.21 = (bf16[112,1024]{1,0:T(8,128)(2,1)S(1)}, bf16[112,1024]{1,0:T(8,128)(2,1)S(1)}, u32[]{:S(2)}, u32[]{:S(2)}) collective-permute-start(bf16[112,1024]{1,0:T(8,128)(2,1)S(1)} %get-tuple-element.46), channel_id=1, source_target_pairs={{0,2},{1,3},{2,0},{3,1},{4,6},{5,7},{6,4},{7,5},{8,10},{9,11},{10,... | collective-permute-start | bytes 688136 | tf_op jit(solution)/shard_map/ppermute | solution.py:495
  66.0 10.4 %collective-permute-start.13 = (bf16[112,1024]{1,0:T(8,128)(2,1)S(1)}, bf16[112,1024]{1,0:T(8,128)(2,1)S(1)}, u32[]{:S(2)}, u32[]{:S(2)}) collective-permute-start(bf16[112,1024]{1,0:T(8,128)(2,1)S(1)} %get-tuple-element.46), channel_id=1, source_target_pairs={{0,4},{1,5},{2,6},{3,7},{4,0},{5,1},{6,2},{7,3},{8,12},{9,13},{10,... | collective-permute-start | bytes 688136 | tf_op jit(solution)/shard_map/ppermute | solution.py:495
  66.4 11.8 %collective-permute-start.14 = (bf16[112,1024]{1,0:T(8,128)(2,1)S(1)}, bf16[112,1024]{1,0:T(8,128)(2,1)S(1)}, u32[]{:S(2)}, u32[]{:S(2)}) collective-permute-start(bf16[112,1024]{1,0:T(8,128)(2,1)S(1)} %get-tuple-element.47), channel_id=1, source_target_pairs={{0,2},{1,3},{2,0},{3,1},{4,6},{5,7},{6,4},{7,5},{8,10},{9,11},{10,... | collective-permute-start | bytes 688136 | tf_op jit(solution)/shard_map/ppermute | solution.py:495
  73.7 5.1 %collective-permute-start.22 = (bf16[112,1024]{1,0:T(8,128)(2,1)S(1)}, bf16[112,1024]{1,0:T(8,128)(2,1)S(1)}, u32[]{:S(2)}, u32[]{:S(2)}) collective-permute-start(bf16[112,1024]{1,0:T(8,128)(2,1)S(1)} %collective-permute-done.21.refs_0_), channel_id=1, source_target_pairs={{0,1},{1,0},{2,3},{3,2},{4,5},{5,4},{6,7},{7,6},{8,9},{9,8},{10,11... | collective-permute-start | bytes 688136 | tf_op jit(solution)/shard_map/ppermute | solution.py:490
  78.2 1.5 %collective-permute-start.23 = (bf16[112,1024]{1,0:T(8,128)(2,1)S(1)}, bf16[112,1024]{1,0:T(8,128)(2,1)S(1)}, u32[]{:S(2)}, u32[]{:S(2)}) collective-permute-start(bf16[112,1024]{1,0:T(8,128)(2,1)S(1)} %collective-permute-done.14.refs_1_), channel_id=1, source_target_pairs={{0,1},{1,0},{2,3},{3,2},{4,5},{5,4},{6,7},{7,6},{8,9},{9,8},{10,11... | collective-permute-start | bytes 688136 | tf_op jit(solution)/shard_map/ppermute | solution.py:490
  78.2 8.0 %collective-permute-start.25 = (bf16[112,1024]{1,0:T(8,128)(2,1)S(1)}, bf16[112,1024]{1,0:T(8,128)(2,1)S(1)}, u32[]{:S(2)}, u32[]{:S(2)}) collective-permute-start(bf16[112,1024]{1,0:T(8,128)(2,1)S(1)} %get-tuple-element.47), channel_id=1, source_target_pairs={{0,4},{1,5},{2,6},{3,7},{4,0},{5,1},{6,2},{7,3},{8,12},{9,13},{10,... | collective-permute-start | bytes 688136 | tf_op jit(solution)/shard_map/ppermute | solution.py:495
  82.3 12.5 %collective-permute-start.24 = (bf16[112,2048]{1,0:T(8,128)(2,1)S(1)}, bf16[112,2048]{1,0:T(8,128)(2,1)S(1)}, u32[]{:S(2)}, u32[]{:S(2)}) collective-permute-start(bf16[112,2048]{1,0:T(8,128)(2,1)S(1)} %get-tuple-element.55), channel_id=1, source_target_pairs={{0,1},{1,0},{2,3},{3,2},{4,5},{5,4},{6,7},{7,6},{8,9},{9,8},{10,11... | collective-permute-start | bytes 1376264 | tf_op jit(solution)/shard_map/ppermute | solution.py:490
  86.2 1.6 %collective-permute-start.27 = (bf16[112,1024]{1,0:T(8,128)(2,1)S(1)}, bf16[112,1024]{1,0:T(8,128)(2,1)S(1)}, u32[]{:S(2)}, u32[]{:S(2)}) collective-permute-start(bf16[112,1024]{1,0:T(8,128)(2,1)S(1)} %collective-permute-done.25.refs_1_), channel_id=1, source_target_pairs={{0,1},{1,0},{2,3},{3,2},{4,5},{5,4},{6,7},{7,6},{8,9},{9,8},{10,11... | collective-permute-start | bytes 688136 | tf_op jit(solution)/shard_map/ppermute | solution.py:490
  86.2 1.8 %collective-permute-start.26 = (bf16[112,1024]{1,0:T(8,128)(2,1)S(1)}, bf16[112,1024]{1,0:T(8,128)(2,1)S(1)}, u32[]{:S(2)}, u32[]{:S(2)}) collective-permute-start(bf16[112,1024]{1,0:T(8,128)(2,1)S(1)} %collective-permute-done.13.refs_0_), channel_id=1, source_target_pairs={{0,1},{1,0},{2,3},{3,2},{4,5},{5,4},{6,7},{7,6},{8,9},{9,8},{10,11... | collective-permute-start | bytes 688136 | tf_op jit(solution)/shard_map/ppermute | solution.py:490
  86.7 7.5 %collective-permute-start.17 = (bf16[112,1024]{1,0:T(8,128)(2,1)S(1)}, bf16[112,1024]{1,0:T(8,128)(2,1)S(1)}, u32[]{:S(2)}, u32[]{:S(2)}) collective-permute-start(bf16[112,1024]{1,0:T(8,128)(2,1)S(1)} %collective-permute-done.13.refs_0_), channel_id=1, source_target_pairs={{0,2},{1,3},{2,0},{3,1},{4,6},{5,7},{6,4},{7,5},{8,10},{9,11},{10,... | collective-permute-start | bytes 688136 | tf_op jit(solution)/shard_map/ppermute | solution.py:495
  87.4 7.2 %collective-permute-start.19 = (bf16[112,1024]{1,0:T(8,128)(2,1)S(1)}, bf16[112,1024]{1,0:T(8,128)(2,1)S(1)}, u32[]{:S(2)}, u32[]{:S(2)}) collective-permute-start(bf16[112,1024]{1,0:T(8,128)(2,1)S(1)} %collective-permute-done.14.refs_1_), channel_id=1, source_target_pairs={{0,4},{1,5},{2,6},{3,7},{4,0},{5,1},{6,2},{7,3},{8,12},{9,13},{10,... | collective-permute-start | bytes 688136 | tf_op jit(solution)/shard_map/ppermute | solution.py:495
  90.6 4.2 %collective-permute-start.28 = (bf16[112,2048]{1,0:T(8,128)(2,1)S(1)}, bf16[112,2048]{1,0:T(8,128)(2,1)S(1)}, u32[]{:S(2)}, u32[]{:S(2)}) collective-permute-start(bf16[112,2048]{1,0:T(8,128)(2,1)S(1)} %get-tuple-element.57), channel_id=1, source_target_pairs={{0,1},{1,0},{2,3},{3,2},{4,5},{5,4},{6,7},{7,6},{8,9},{9,8},{10,11... | collective-permute-start | bytes 1376264 | tf_op jit(solution)/shard_map/ppermute | solution.py:490
  94.2 1.5 %collective-permute-start.18 = (bf16[112,1024]{1,0:T(8,128)(2,1)S(1)}, bf16[112,1024]{1,0:T(8,128)(2,1)S(1)}, u32[]{:S(2)}, u32[]{:S(2)}) collective-permute-start(bf16[112,1024]{1,0:T(8,128)(2,1)S(1)} %collective-permute-done.17.refs_0_), channel_id=1, source_target_pairs={{0,1},{1,0},{2,3},{3,2},{4,5},{5,4},{6,7},{7,6},{8,9},{9,8},{10,11... | collective-permute-start | bytes 688136 | tf_op jit(solution)/shard_map/ppermute | solution.py:490
  94.6 1.5 %collective-permute-start.20 = (bf16[112,1024]{1,0:T(8,128)(2,1)S(1)}, bf16[112,1024]{1,0:T(8,128)(2,1)S(1)}, u32[]{:S(2)}, u32[]{:S(2)}) collective-permute-start(bf16[112,1024]{1,0:T(8,128)(2,1)S(1)} %collective-permute-done.19.refs_1_), channel_id=1, source_target_pairs={{0,1},{1,0},{2,3},{3,2},{4,5},{5,4},{6,7},{7,6},{8,9},{9,8},{10,11... | collective-permute-start | bytes 688136 | tf_op jit(solution)/shard_map/ppermute | solution.py:490
  98.7 2.5 %collective-permute-start.31 = (bf16[112,2048]{1,0:T(8,128)(2,1)S(1)}, bf16[112,2048]{1,0:T(8,128)(2,1)S(1)}, u32[]{:S(2)}, u32[]{:S(2)}) collective-permute-start(bf16[112,2048]{1,0:T(8,128)(2,1)S(1)} %get-tuple-element.63), channel_id=1, source_target_pairs={{0,1},{1,0},{2,3},{3,2},{4,5},{5,4},{6,7},{7,6},{8,9},{9,8},{10,11... | collective-permute-start | bytes 1376264 | tf_op jit(solution)/shard_map/ppermute | solution.py:490
  98.9 4.2 %collective-permute-start.16 = (bf16[112,2048]{1,0:T(8,128)(2,1)S(1)}, bf16[112,2048]{1,0:T(8,128)(2,1)S(1)}, u32[]{:S(2)}, u32[]{:S(2)}) collective-permute-start(bf16[112,2048]{1,0:T(8,128)(2,1)S(1)} %get-tuple-element.51), channel_id=1, source_target_pairs={{0,1},{1,0},{2,3},{3,2},{4,5},{5,4},{6,7},{7,6},{8,9},{9,8},{10,11... | collective-permute-start | bytes 1376264 | tf_op jit(solution)/shard_map/ppermute | solution.py:490
  99.3 12.6 %collective-permute-start.30 = (bf16[112,2048]{1,0:T(8,128)(2,1)S(1)}, bf16[112,2048]{1,0:T(8,128)(2,1)S(1)}, u32[]{:S(2)}, u32[]{:S(2)}) collective-permute-start(bf16[112,2048]{1,0:T(8,128)(2,1)S(1)} %add_convert_fusion.1), channel_id=1, source_target_pairs={{0,4},{1,5},{2,6},{3,7},{4,0},{5,1},{6,2},{7,3},{8,12},{9,13},{10,... | collective-permute-start | bytes 1376264 | tf_op jit(solution)/shard_map/ppermute | solution.py:495
  99.9 13.4 %collective-permute-start.29 = (bf16[112,2048]{1,0:T(8,128)(2,1)S(1)}, bf16[112,2048]{1,0:T(8,128)(2,1)S(1)}, u32[]{:S(2)}, u32[]{:S(2)}) collective-permute-start(bf16[112,2048]{1,0:T(8,128)(2,1)S(1)} %add_convert_fusion.2), channel_id=1, source_target_pairs={{0,2},{1,3},{2,0},{3,1},{4,6},{5,7},{6,4},{7,5},{8,10},{9,11},{10,... | collective-permute-start | bytes 1376264 | tf_op jit(solution)/shard_map/ppermute | solution.py:495
  101.4 21.5 %collective-permute-start.32 = (bf16[112,2048]{1,0:T(8,128)(2,1)S(1)}, bf16[112,2048]{1,0:T(8,128)(2,1)S(1)}, u32[]{:S(2)}, u32[]{:S(2)}) collective-permute-start(bf16[112,2048]{1,0:T(8,128)(2,1)S(1)} %add_convert_fusion), channel_id=1, source_target_pairs={{0,6},{1,7},{2,4},{3,5},{4,2},{5,3},{6,0},{7,1},{8,14},{9,15},{10,... | collective-permute-start | bytes 1376264 | tf_op jit(solution)/shard_map/ppermute | solution.py:495

commit v5 on v3

--- a/solution.py
+++ b/solution.py
@@ -448,14 +448,7 @@
     return local_call(combine_kernel, [out], place, [*own, back_y, back_x], 0, "combine")[0]
 
 
-def merge(upper, lower, merge_weight):
-    if lax.axis_size("lon") == 8:
-        return merge_by_squares(upper, lower, merge_weight)
-    weight = lax.all_gather(merge_weight, "lon", axis=1, tiled=True)
-    return jnp.dot(jnp.concatenate([upper, lower], axis=1), weight, preferred_element_type=F32).astype(BF16)
-
-
-def ffn_kernel(mine_ref, theirs_ref, up_ref, down_ref, out_mine_ref, out_theirs_ref, normed_ref, hidden_ref):
+def ffn_kernel(mine_ref, theirs_ref, up_ref, down_ref, out_mine_ref, low_ref, high_ref, normed_ref, hidden_ref):
     count = mine_ref.shape[0]
     for k, ref in enumerate((mine_ref, theirs_ref)):
         normed_ref[k * count : (k + 1) * count, :] = normalize(ref[...].astype(F32)).astype(BF16)
@@ -465,21 +458,23 @@
         raw = dot(normed_ref[...], up_ref[:, at : at + step])
         active = 0.5 * raw * (1.0 + lax.erf(raw * np.float32(np.sqrt(0.5))))
         hidden_ref[:, at : at + step] = active.astype(BF16)
-    for at in range(0, down_ref.shape[1], step):
+    half = low_ref.shape[1]
+    for at in range(0, 2 * half, step):
         out = dot(hidden_ref[...], down_ref[:, at : at + step]).astype(BF16)
         out_mine_ref[:, at : at + step] = out[:count]
-        out_theirs_ref[:, at : at + step] = out[count:]
+        ref = low_ref if at < half else high_ref
+        ref[:, at % half : at % half + step] = out[count:]
 
 
 def feed_forward(mine, theirs, up, down):
-    count, width = mine.shape
-    hidden = up.shape[1]
+    count = mine.shape[0]
+    width, hidden = up.shape
     vmem = pl.BlockSpec(memory_space=pltpu.VMEM)
     return pl.pallas_call(
         ffn_kernel,
         in_specs=[vmem] * 4,
-        out_specs=[vmem] * 2,
-        out_shape=[jax.ShapeDtypeStruct((count, width), BF16)] * 2,
+        out_specs=[vmem] * 3,
+        out_shape=[jax.ShapeDtypeStruct((count, width // n), BF16) for n in (1, 2, 2)],
         scratch_shapes=[pltpu.VMEM((2 * count, width), BF16), pltpu.VMEM((2 * count, hidden), BF16)],
         compiler_params=params(20),
         cost_estimate=pl.CostEstimate(
@@ -489,6 +484,14 @@
     )(mine, theirs, up, down)
 
 
+def added(mine, low, high):
+    return (mine.astype(F32) + jnp.concatenate([low, high], axis=1).astype(F32)).astype(BF16)
+
+
+def summed(mine, low, high):
+    return added(mine, core_swap(low), core_swap(high))
+
+
 def core_swap(value):
     size = lax.axis_size("lon")
     return lax.ppermute(value, "lon", [(i, i ^ 1) for i in range(size)])
@@ -497,6 +500,42 @@
 def chip_swap(value, offset):
     size = lax.axis_size("lon")
     return lax.ppermute(value, "lon", [(i, i ^ (2 * offset)) for i in range(size)])
+
+
+def cross(value, first, second):
+    size = lax.axis_size("lon")
+    return lax.ppermute(value, "lon", [(i, i ^ (2 * (second if i % 2 else first))) for i in range(size)])
+
+
+def coarse_by_squares(upper, lower, merge_weight, up, down):
+    own = merge_by_squares(upper, lower, merge_weight)
+    near = cross(own, 1, 2)
+    next_near = cross(own, 2, 1)
+    first = feed_forward(own, core_swap(own), up, down)
+    near, next_near, *first = lax.optimization_barrier((near, next_near, *first))
+    far = cross(near, 2, 1)
+    sums = [summed(*first)]
+    for chunk in (near, next_near):
+        sums.append(summed(*feed_forward(chunk, core_swap(chunk), up, down)))
+    pair, *sums = lax.optimization_barrier((core_swap(far), *sums))
+    back = [cross(sums[1], 1, 2), cross(sums[2], 2, 1)]
+    mine, low, high = feed_forward(far, pair, up, down)
+    low, high, *back = lax.optimization_barrier((core_swap(low), core_swap(high), *back))
+    back.append(chip_swap(added(mine, low, high), 3))
+    return sum(part.astype(F32) for part in (own, sums[0], *back))
+
+
+def coarse_by_chips(upper, lower, merge_weight, up, down):
+    weight = lax.all_gather(merge_weight, "lon", axis=1, tiled=True)
+    patches = jnp.concatenate([upper, lower], axis=1)
+    coarse = jnp.dot(patches, weight, preferred_element_type=F32).astype(BF16)
+    chips = lax.axis_size("lon") // 2
+    arrived = [coarse] + [chip_swap(coarse, m) for m in range(1, chips)]
+    total = coarse.astype(F32)
+    for m in range(chips):
+        part = summed(*feed_forward(arrived[m], core_swap(arrived[m]), up, down))
+        total = total + (chip_swap(part, m) if m else part).astype(F32)
+    return total
 
 
 def per_device(tokens, qkv_weight, out_weight, merge_weight, up_weight, down_weight):
@@ -504,16 +543,8 @@
     bands = Bands(rows, columns)
     cells = rows * columns // 4
     middle_out, upper, lower = attention(bands, tokens, qkv_weight, out_weight)
-    coarse = merge(upper, lower, merge_weight)
-    chips = lax.axis_size("lon") // 2
-    arrived = [coarse] + [chip_swap(coarse, m) for m in range(1, chips)]
-    total = coarse.astype(F32)
-    for m in range(chips):
-        mine, theirs = feed_forward(arrived[m], core_swap(arrived[m]), up_weight, down_weight)
-        summed = mine.astype(F32) + core_swap(theirs).astype(F32)
-        if m:
-            summed = chip_swap(summed.astype(BF16), m).astype(F32)
-        total = total + summed
+    coarse = coarse_by_squares if lax.axis_size("lon") == 8 else coarse_by_chips
+    total = coarse(upper, lower, merge_weight, up_weight, down_weight)
     coarse_out = total[:cells].astype(jnp.bfloat16)
     return (middle_out, coarse_out.reshape(rows // 2, columns // 2, -1))
 

time: 123 us -> 117 us (0.951)
  starting transfers between devices: 24.4 us -> 20.8 us
  waiting for transfers between devices: 49.8 us -> 47.2 us
    ppermute x12 -> x7, waiting for transfers between devices: 49.8 us -> 26.2 us  [chip_swap(): lax.ppermute(value, 'lon', [(i, i ^ 2 * offset) for i in range(size)])]
    ppermute x0 -> x5, waiting for transfers between devices: none -> 16.8 us  [cross(): lax.ppermute(value, 'lon', [(i, i ^ 2 * (second if i % 2 else first)) for...]
    ppermute x12 -> x7, starting transfers between devices: 13.1 us -> 6.68 us  [chip_swap(): lax.ppermute(value, 'lon', [(i, i ^ 2 * offset) for i in range(size)])]
    ppermute x11 -> x15, waiting for transfers between devices: 0.03 us -> 4.21 us  [core_swap(): return lax.ppermute(value, 'lon', [(i, i ^ 1) for i in range(size)])]
    ppermute x0 -> x5, starting transfers between devices: none -> 2.82 us  [cross(): lax.ppermute(value, 'lon', [(i, i ^ 2 * (second if i % 2 else first)) for...]
    ppermute x11 -> x15, starting transfers between devices: 2.8 us -> 2.88 us  [core_swap(): return lax.ppermute(value, 'lon', [(i, i ^ 1) for i in range(size)])]
  transfers between devices with their start and end apart: 27 -> 31, of which waited for: 8 -> 15; matrix products, arithmetic and copies ran while one was open for 3% -> 3% of each run, Pallas kernels for 25% -> 26%
where the time goes in v5:
time: 117 us
  waiting for transfers between devices  47.2 us (40%)
  Pallas kernels  35.1 us (30%)
  starting transfers between devices  20.8 us (18%)
  local copies, waits for them, and re-layouts  11.5 us (10%)
    ppermute x7, waiting for transfers between devices, chip_swap(): lax.ppermute(value, 'lon', [(i, i ^ 2 * offset) for i in range(size)])  26.2 us
    ppermute x5, waiting for transfers between devices, cross(): lax.ppermute(value, 'lon', [(i, i ^ 2 * (second if i % 2 else first)) for...  16.8 us
    pallas_call x3, Pallas kernels, vmem_call(): pl.pallas_call(kernel, in_specs=[vmem] * len(args), out_specs=[vmem] * le...  15.5 us
    pallas_call x4, Pallas kernels, feed_forward(): pl.pallas_call(ffn_kernel, in_specs=[vmem] * 4, out_specs=[vmem] * 3, out...  10.4 us
    pallas_call x3, Pallas kernels, local_call(): pl.pallas_call(kernel, in_specs=[pl.BlockSpec(memory_space=pltpu.SMEM)] +...  9.17 us
    ppermute x4, starting transfers between devices, shift(): return lax.ppermute(part, axis, pairs)  8.44 us
    ppermute x7, starting transfers between devices, chip_swap(): lax.ppermute(value, 'lon', [(i, i ^ 2 * offset) for i in range(size)])  6.68 us
    unnamed x36, local copies, waits for them, and re-layouts  5.63 us
  transfers between devices with their start and end apart: 31, of which 15 were waited for; matrix products, arithmetic and copies ran while one was open for 3% of the time, Pallas kernels for 26%

profile of v5, /device:TPU:0, one launch (start us, length us, event | category | flops | bytes accessed | tf_op | source)
XLA Modules:
  0.0 116.7 jit_solution(8781084096566290696)
XLA Ops:
  0.6 1.8 %fusion.2 = (bf16[18,8,1024]{2,1,0:T(8,128)(2,1)S(1)}, bf16[18,8,1024]{2,1,0:T(8,128)(2,1)}) fusion(bf16[18,24,1024]{2,1,0:T(8,128)(2,1)} %tokens_ref.3), kind=kLoop, calls=%fused_computation.19 | loop fusion | bytes 1179648 | tf_op jit(solution)/shard_map/slice | solution.py:293
  2.4 3.3 %collective-permute-start.1 = (bf16[18,8,1024]{2,1,0:T(8,128)(2,1)}, bf16[18,8,1024]{2,1,0:T(8,128)(2,1)S(1)}, u32[]{:S(2)}, u32[]{:S(2)}) collective-permute-start(bf16[18,8,1024]{2,1,0:T(8,128)(2,1)} %get-tuple-element.81), channel_id=1, source_target_pairs={{0,7},{1,0},{2,1},{3,2},{4,3},{5,4},{6,5},{7,6},{8,15},{9,8},{10,9... | collective-permute-start | bytes 884744 | tf_op jit(solution)/shard_map/ppermute | solution.py:343
  5.8 3.1 %fusion = (bf16[2048,256]{1,0:T(8,128)(2,1)}, bf16[2048,256]{1,0:T(8,128)(2,1)}) fusion(bf16[4096,256]{1,0:T(8,128)(2,1)} %refs_0_.3), kind=kLoop, calls=%fused_computation.17 | loop fusion | bytes 4194304 | tf_op jit(solution)/shard_map/slice | solution.py:435
  8.9 2.0 %collective-permute-start.5 = (bf16[2048,256]{1,0:T(8,128)(2,1)}, bf16[2048,256]{1,0:T(8,128)(2,1)S(1)}, u32[]{:S(2)}, u32[]{:S(2)}) collective-permute-start(bf16[2048,256]{1,0:T(8,128)(2,1)} %get-tuple-element.77), channel_id=1, source_target_pairs={{0,2},{1,3},{2,0},{3,1},{4,6},{5,7},{6,4},{7,5},{8,10},{9,11},{10,... | collective-permute-start | bytes 3145736 | tf_op jit(solution)/shard_map/ppermute | solution.py:502
  10.9 1.5 %collective-permute-start.6 = (bf16[2048,256]{1,0:T(8,128)(2,1)}, bf16[2048,256]{1,0:T(8,128)(2,1)}, u32[]{:S(2)}, u32[]{:S(2)}) collective-permute-start(bf16[2048,256]{1,0:T(8,128)(2,1)} %get-tuple-element.76), channel_id=1, source_target_pairs={{0,4},{1,5},{2,6},{3,7},{4,0},{5,1},{6,2},{7,3},{8,12},{9,13},{10,... | collective-permute-start | bytes 3145736 | tf_op jit(solution)/shard_map/ppermute | solution.py:502
  12.5 2.8 %copy-done.5 = bf16[1024,3072]{1,0:T(8,128)(2,1)S(1)} copy-done((bf16[1024,3072]{1,0:T(8,128)(2,1)S(1)}, bf16[1024,3072]{1,0:T(8,128)(2,1)}, u32[]{:S(2)}) %copy-start.5) | copy-done | bytes 6291480
  15.2 3.4 %own_projection.1.own_ref = bf16[448,3072]{1,0:T(8,128)(2,1)S(1)} custom-call(bf16[18,24,1024]{2,1,0:T(8,128)(2,1)S(1)} %copy-done.3, bf16[1024,3072]{1,0:T(8,128)(2,1)S(1)} %copy-done.5), custom_call_target="tpu_custom_call" | custom-call | flops 2818572288 | bytes 1048576 | tf_op jit(solution)/shard_map/own_projection/pallas_call | solution.py:278
  18.7 0.1 or_select_fusion.bias_ref
  18.8 3.5 %collective-permute-start.2 = (bf16[3,40,1024]{2,1,0:T(8,128)(2,1)S(1)}, bf16[3,40,1024]{2,1,0:T(8,128)(2,1)S(1)}, u32[]{:S(2)}, u32[]{:S(2)}) collective-permute-start(bf16[3,40,1024]{2,1,0:T(8,128)(2,1)S(1)} %pad_maximum_fusion), channel_id=1, source_target_pairs={{0,8},{8,16},{16,24},{1,9},{9,17},{17,25},{2,10},{10,18},{18,26},{... | collective-permute-start | bytes 737288 | tf_op jit(solution)/shard_map/ppermute | solution.py:343
  22.4 1.6 %collective-permute-start.3 = (bf16[3,40,1024]{2,1,0:T(8,128)(2,1)S(1)}, bf16[3,40,1024]{2,1,0:T(8,128)(2,1)S(1)}, u32[]{:S(2)}, u32[]{:S(2)}) collective-permute-start(bf16[3,40,1024]{2,1,0:T(8,128)(2,1)S(1)} %pad_maximum_fusion.1), channel_id=1, source_target_pairs={{8,0},{16,8},{24,16},{9,1},{17,9},{25,17},{10,2},{18,10},{26,18},{... | collective-permute-start | bytes 737288 | tf_op jit(solution)/shard_map/ppermute | solution.py:343
  24.0 2.8 %copy-done.6 = bf16[1024,3072]{1,0:T(8,128)(2,1)S(1)} copy-done((bf16[1024,3072]{1,0:T(8,128)(2,1)S(1)}, bf16[1024,3072]{1,0:T(8,128)(2,1)}, u32[]{:S(2)}) %copy-start.6) | copy-done | bytes 6291480
  26.8 0.0 copy-start.14
  26.8 0.0 copy-start.16
  26.8 5.4 %middle_attention.1 = (bf16[288,2048]{1,0:T(8,128)(2,1)S(1)}, bf16[288,1024]{1,0:T(8,128)(2,1)S(1)}) custom-call(bf16[18,8,1024]{2,1,0:T(8,128)(2,1)S(1)} %collective-permute-done.west_ref, bf16[18,8,1024]{2,1,0:T(8,128)(2,1)S(1)} %collective-permute-done.1.east_ref, bf16[448,3072]{1,0:T(8,128)(2,1)S(1)} %own_projection.1.own_ref, ...), custom_call_target="tpu_custom_call" | custom-call | flops 5000000000 | bytes 1048576 | tf_op jit(solution)/shard_map/middle_attention/pallas_call | solution.py:278
  32.3 6.8 %edge_attention.1 = (bf16[18,24,1024]{2,1,0:T(8,128)(2,1)}, bf16[112,2048]{1,0:T(8,128)(2,1)}, bf16[112,2048]{1,0:T(8,128)(2,1)}) custom-call(bf16[18,24,1024]{2,1,0:T(8,128)(2,1)S(1)} %copy-done.4, bf16[3,40,1024]{2,1,0:T(8,128)(2,1)S(1)} %collective-permute-done.2.north_ref, bf16[3,40,1024]{2,1,0:T(8,128)(2,1)S(1)} %collective-permute-done.3.south_ref, ...), custom_call_target="tpu_custom_call" | custom-call | flops 6000000000 | bytes 1048576 | tf_op jit(solution)/shard_map/edge_attention/pallas_call | solution.py:278
  39.1 0.5 collective-permute-start.8
  39.6 0.5 collective-permute-start.9
  40.1 0.0 collective-permute-start.10
  40.1 0.1 pad_add_fusion.place_ref
  40.2 12.2 %collective-permute-done.9.upper_ref = bf16[112,2048]{1,0:T(8,128)(2,1)} collective-permute-done((bf16[112,2048]{1,0:T(8,128)(2,1)}, bf16[112,2048]{1,0:T(8,128)(2,1)}, u32[]{:S(2)}, u32[]{:S(2)}) %collective-permute-start.9) | collective-permute-done | bytes 458784 | tf_op jit(solution)/shard_map/ppermute | solution.py:502
  52.4 0.2 collective-permute-done.10.lower_ref
  52.7 4.0 %merge_other.1 = (bf16[112,1024]{1,0:T(8,128)(2,1)S(1)}, bf16[112,1024]{1,0:T(8,128)(2,1)S(1)}) custom-call(s32[2]{0:T(128)S(1)} %pad_add_fusion.place_ref, bf16[112,2048]{1,0:T(8,128)(2,1)} %collective-permute-done.9.upper_ref, bf16[112,2048]{1,0:T(8,128)(2,1)} %collective-permute-done.10.lower_ref, bf16[4096,256]{1,0:T(8,128)(2,1)S(1)} %copy-done.2, ...), custom_call_target="tpu_custom_call" | custom-call | flops 939524096 | bytes 1048576 | tf_op jit(solution)/shard_map/merge_other/pallas_call | solution.py:419
  56.7 1.6 %collective-permute-start.11 = (bf16[112,1024]{1,0:T(8,128)(2,1)S(1)}, bf16[112,1024]{1,0:T(8,128)(2,1)S(1)}, u32[]{:S(2)}, u32[]{:S(2)}) collective-permute-start(bf16[112,1024]{1,0:T(8,128)(2,1)S(1)} %get-tuple-element.49), channel_id=1, source_target_pairs={{0,4},{1,5},{2,6},{3,7},{4,0},{5,1},{6,2},{7,3},{8,12},{9,13},{10,... | collective-permute-start | bytes 688136 | tf_op jit(solution)/shard_map/ppermute | solution.py:502
  58.3 0.3 collective-permute-start.12
  58.6 4.5 %merge_own.1 = (f32[112,512]{1,0:T(8,128)S(1)}, f32[112,512]{1,0:T(8,128)S(1)}, f32[112,512]{1,0:T(8,128)S(1)}) custom-call(s32[2]{0:T(128)S(1)} %pad_add_fusion.place_ref, bf16[112,2048]{1,0:T(8,128)(2,1)} %get-tuple-element.42.upper_ref, bf16[112,2048]{1,0:T(8,128)(2,1)} %get-tuple-element.43.lower_ref, bf16[4096,256]{1,0:T(8,128)(2,1)S(1)} %copy-done.2, ...), custom_call_target="tpu_custom_call" | custom-call | flops 939524096 | bytes 1048576 | tf_op jit(solution)/shard_map/merge_own/pallas_call | solution.py:419
  63.1 0.2 collective-permute-done.11.from_y_ref
  63.3 1.2 %collective-permute-done.12.from_x_ref = bf16[112,1024]{1,0:T(8,128)(2,1)S(1)} collective-permute-done((bf16[112,1024]{1,0:T(8,128)(2,1)S(1)}, bf16[112,1024]{1,0:T(8,128)(2,1)S(1)}, u32[]{:S(2)}, u32[]{:S(2)}) %collective-permute-start.12) | collective-permute-done | bytes 229408 | tf_op jit(solution)/shard_map/ppermute | solution.py:502
  64.5 0.6 combine.1.mine_ref
  65.2 0.1 collective-permute-start.15
  65.3 0.6 collective-permute-start.13
  65.9 0.5 collective-permute-start.14
  66.3 0.7 collective-permute-done.15.theirs_ref
  67.1 2.6 %feed_forward.4 = (bf16[112,2048]{1,0:T(8,128)(2,1)S(1)}, bf16[112,1024]{1,0:T(8,128)(2,1)S(1)}, bf16[112,1024]{1,0:T(8,128)(2,1)S(1)}) custom-call(bf16[112,2048]{1,0:T(8,128)(2,1)S(1)} %combine.1.mine_ref, bf16[112,2048]{1,0:T(8,128)(2,1)S(1)} %collective-permute-done.15.theirs_ref, bf16[2048,1024]{1,0:T(8,128)(2,1)S(1)} %copy-done, ...), custom_call_target="tpu_custom_call" | custom-call | flops 1879048192 | bytes 8388608 | tf_op jit(solution)/shard_map/feed_forward/pallas_call | solution.py:473
  69.7 8.8 %collective-permute-done.13.mine_ref = bf16[112,2048]{1,0:T(8,128)(2,1)S(1)} collective-permute-done((bf16[112,2048]{1,0:T(8,128)(2,1)S(1)}, bf16[112,2048]{1,0:T(8,128)(2,1)S(1)}, u32[]{:S(2)}, u32[]{:S(2)}) %collective-permute-start.13) | collective-permute-done | bytes 458784 | tf_op jit(solution)/shard_map/ppermute | solution.py:507
  78.5 0.5 collective-permute-start.19
  79.0 0.6 collective-permute-start.16
  79.6 0.1 collective-permute-start.23
  79.7 0.6 collective-permute-done.20.theirs_ref
  80.3 2.6 %feed_forward.5 = (bf16[112,2048]{1,0:T(8,128)(2,1)S(1)}, bf16[112,1024]{1,0:T(8,128)(2,1)S(1)}, bf16[112,1024]{1,0:T(8,128)(2,1)S(1)}) custom-call(bf16[112,2048]{1,0:T(8,128)(2,1)S(1)} %collective-permute-done.13.mine_ref, bf16[112,2048]{1,0:T(8,128)(2,1)S(1)} %collective-permute-done.20.theirs_ref, bf16[2048,1024]{1,0:T(8,128)(2,1)S(1)} %copy-done, ...), custom_call_target="tpu_custom_call" | custom-call | flops 1879048192 | bytes 8388608 | tf_op jit(solution)/shard_map/feed_forward/pallas_call | solution.py:473
  82.9 0.2 collective-permute-start.22
  83.1 0.4 collective-permute-start.21
  83.5 0.1 add_convert_fusion.4
  83.6 2.6 %feed_forward.6 = (bf16[112,2048]{1,0:T(8,128)(2,1)S(1)}, bf16[112,1024]{1,0:T(8,128)(2,1)S(1)}, bf16[112,1024]{1,0:T(8,128)(2,1)S(1)}) custom-call(bf16[112,2048]{1,0:T(8,128)(2,1)S(1)} %collective-permute-done.14.mine_ref, bf16[112,2048]{1,0:T(8,128)(2,1)S(1)} %collective-permute-done.23.theirs_ref, bf16[2048,1024]{1,0:T(8,128)(2,1)S(1)} %copy-done, ...), custom_call_target="tpu_custom_call" | custom-call | flops 1879048192 | bytes 8388608 | tf_op jit(solution)/shard_map/feed_forward/pallas_call | solution.py:473
  86.2 0.2 collective-permute-start.25
  86.4 0.4 collective-permute-start.24
  86.8 0.7 collective-permute-done.16.mine_ref
  87.5 0.1 add_convert_fusion.3
  87.6 0.2 collective-permute-done.25
  87.8 0.3 collective-permute-done.24
  88.1 0.1 add_convert_fusion.2
  88.2 1.0 collective-permute-done.17.theirs_ref
  89.3 0.5 collective-permute-start.28
  89.7 0.6 collective-permute-start.29
  90.4 2.6 %feed_forward.7 = (bf16[112,2048]{1,0:T(8,128)(2,1)S(1)}, bf16[112,1024]{1,0:T(8,128)(2,1)S(1)}, bf16[112,1024]{1,0:T(8,128)(2,1)S(1)}) custom-call(bf16[112,2048]{1,0:T(8,128)(2,1)S(1)} %collective-permute-done.16.mine_ref, bf16[112,2048]{1,0:T(8,128)(2,1)S(1)} %collective-permute-done.17.theirs_ref, bf16[2048,1024]{1,0:T(8,128)(2,1)S(1)} %copy-done, ...), custom_call_target="tpu_custom_call" | custom-call | flops 1879048192 | bytes 8388608 | tf_op jit(solution)/shard_map/feed_forward/pallas_call | solution.py:473
  93.0 0.1 collective-permute-start.26
  93.0 0.5 collective-permute-start.27
  93.5 1.0 collective-permute-done.26
  94.5 0.3 collective-permute-done.27
  94.9 7.3 %collective-permute-done.28 = bf16[112,2048]{1,0:T(8,128)(2,1)S(1)} collective-permute-done((bf16[112,2048]{1,0:T(8,128)(2,1)S(1)}, bf16[112,2048]{1,0:T(8,128)(2,1)S(1)}, u32[]{:S(2)}, u32[]{:S(2)}) %collective-permute-start.28) | collective-permute-done | bytes 458784 | tf_op jit(solution)/shard_map/ppermute | solution.py:507
  102.2 0.1 add_convert_fusion.1
  102.3 0.8 collective-permute-start.30
  103.1 12.3 %collective-permute-done.30 = bf16[112,2048]{1,0:T(8,128)(2,1)S(1)} collective-permute-done((bf16[112,2048]{1,0:T(8,128)(2,1)S(1)}, bf16[112,2048]{1,0:T(8,128)(2,1)S(1)}, u32[]{:S(2)}, u32[]{:S(2)}) %collective-permute-start.30) | collective-permute-done | bytes 458784 | tf_op jit(solution)/shard_map/ppermute | solution.py:502
  115.4 0.4 add_convert_fusion
  115.8 0.9 reshape.45
  (61 shorter events, 0.2 us)
Async XLA Ops:
  2.4 16.3 %collective-permute-start.1 = (bf16[18,8,1024]{2,1,0:T(8,128)(2,1)}, bf16[18,8,1024]{2,1,0:T(8,128)(2,1)S(1)}, u32[]{:S(2)}, u32[]{:S(2)}) collective-permute-start(bf16[18,8,1024]{2,1,0:T(8,128)(2,1)} %get-tuple-element.81), channel_id=1, source_target_pairs={{0,7},{1,0},{2,1},{3,2},{4,3},{5,4},{6,5},{7,6},{8,15},{9,8},{10,9... | collective-permute-start | bytes 884744 | tf_op jit(solution)/shard_map/ppermute | solution.py:343
  5.8 6.6 %copy-start.3 = (bf16[18,24,1024]{2,1,0:T(8,128)(2,1)S(1)}, bf16[18,24,1024]{2,1,0:T(8,128)(2,1)}, u32[]{:S(2)}) copy-start(bf16[18,24,1024]{2,1,0:T(8,128)(2,1)} %tokens_ref.3) | copy-start | bytes 2654212
  5.8 13.0 %collective-permute-start = (bf16[18,8,1024]{2,1,0:T(8,128)(2,1)S(1)}, bf16[18,8,1024]{2,1,0:T(8,128)(2,1)S(1)}, u32[]{:S(2)}, u32[]{:S(2)}) collective-permute-start(bf16[18,8,1024]{2,1,0:T(8,128)(2,1)S(1)} %get-tuple-element.80), channel_id=1, source_target_pairs={{0,1},{1,2},{2,3},{3,4},{4,5},{5,6},{6,7},{7,0},{8,9},{9,10},{10,1... | collective-permute-start | bytes 884744 | tf_op jit(solution)/shard_map/ppermute | solution.py:343
  5.8 46.9 %collective-permute-start.4 = (bf16[4096,256]{1,0:T(8,128)(2,1)}, bf16[4096,256]{1,0:T(8,128)(2,1)}, u32[]{:S(2)}, u32[]{:S(2)}) collective-permute-start(bf16[4096,256]{1,0:T(8,128)(2,1)} %refs_0_.3), channel_id=1, source_target_pairs={{0,1},{1,0},{2,3},{3,2},{4,5},{5,4},{6,7},{7,6},{8,9},{9,8},{10,11... | collective-permute-start | bytes 6291464 | tf_op jit(solution)/shard_map/ppermute | solution.py:497
  8.9 30.2 %collective-permute-start.5 = (bf16[2048,256]{1,0:T(8,128)(2,1)}, bf16[2048,256]{1,0:T(8,128)(2,1)S(1)}, u32[]{:S(2)}, u32[]{:S(2)}) collective-permute-start(bf16[2048,256]{1,0:T(8,128)(2,1)} %get-tuple-element.77), channel_id=1, source_target_pairs={{0,2},{1,3},{2,0},{3,1},{4,6},{5,7},{6,4},{7,5},{8,10},{9,11},{10,... | collective-permute-start | bytes 3145736 | tf_op jit(solution)/shard_map/ppermute | solution.py:502
  10.9 28.2 %collective-permute-start.6 = (bf16[2048,256]{1,0:T(8,128)(2,1)}, bf16[2048,256]{1,0:T(8,128)(2,1)}, u32[]{:S(2)}, u32[]{:S(2)}) collective-permute-start(bf16[2048,256]{1,0:T(8,128)(2,1)} %get-tuple-element.76), channel_id=1, source_target_pairs={{0,4},{1,5},{2,6},{3,7},{4,0},{5,1},{6,2},{7,3},{8,12},{9,13},{10,... | collective-permute-start | bytes 3145736 | tf_op jit(solution)/shard_map/ppermute | solution.py:502
  12.4 2.8 %copy-start.5 = (bf16[1024,3072]{1,0:T(8,128)(2,1)S(1)}, bf16[1024,3072]{1,0:T(8,128)(2,1)}, u32[]{:S(2)}) copy-start(bf16[1024,3072]{1,0:T(8,128)(2,1)} %weight_ref.5) | copy-start | bytes 18874372
  15.2 8.7 %copy-start.9 = (bf16[576,144]{1,0:T(8,128)(2,1)S(1)}, bf16[576,144]{1,0:T(8,128)(2,1)}, u32[]{:S(2)}) copy-start(bf16[576,144]{1,0:T(8,128)(2,1)} %constant.71.clone.rest_1_) | copy-start | bytes 497668
  15.2 8.8 %copy-start.10 = (bf16[576,256]{1,0:T(8,128)(2,1)S(1)}, bf16[576,256]{1,0:T(8,128)(2,1)}, u32[]{:S(2)}) copy-start(bf16[576,256]{1,0:T(8,128)(2,1)} %constant.72.clone.rest_2_) | copy-start | bytes 884740
  15.2 8.8 %copy-start.11 = (bf16[144,576]{1,0:T(8,128)(2,1)S(1)}, bf16[144,576]{1,0:T(8,128)(2,1)}, u32[]{:S(2)}) copy-start(bf16[144,576]{1,0:T(8,128)(2,1)} %constant.73.clone.rest_3_) | copy-start | bytes 497668
  15.2 8.8 %copy-start.15 = (bf16[240,240]{1,0:T(8,128)(2,1)S(1)}, bf16[240,240]{1,0:T(8,128)(2,1)}, u32[]{:S(2)}) copy-start(bf16[240,240]{1,0:T(8,128)(2,1)} %constant.70.clone.rest_0_) | copy-start | bytes 345604
  18.8 13.4 %collective-permute-start.2 = (bf16[3,40,1024]{2,1,0:T(8,128)(2,1)S(1)}, bf16[3,40,1024]{2,1,0:T(8,128)(2,1)S(1)}, u32[]{:S(2)}, u32[]{:S(2)}) collective-permute-start(bf16[3,40,1024]{2,1,0:T(8,128)(2,1)S(1)} %pad_maximum_fusion), channel_id=1, source_target_pairs={{0,8},{8,16},{16,24},{1,9},{9,17},{17,25},{2,10},{10,18},{18,26},{... | collective-permute-start | bytes 737288 | tf_op jit(solution)/shard_map/ppermute | solution.py:343
  22.3 9.9 %copy-start.4 = (bf16[18,24,1024]{2,1,0:T(8,128)(2,1)S(1)}, bf16[18,24,1024]{2,1,0:T(8,128)(2,1)}, u32[]{:S(2)}) copy-start(bf16[18,24,1024]{2,1,0:T(8,128)(2,1)} %tokens_ref.3) | copy-start | bytes 2654212
  22.4 9.9 %collective-permute-start.3 = (bf16[3,40,1024]{2,1,0:T(8,128)(2,1)S(1)}, bf16[3,40,1024]{2,1,0:T(8,128)(2,1)S(1)}, u32[]{:S(2)}, u32[]{:S(2)}) collective-permute-start(bf16[3,40,1024]{2,1,0:T(8,128)(2,1)S(1)} %pad_maximum_fusion.1), channel_id=1, source_target_pairs={{8,0},{16,8},{24,16},{9,1},{17,9},{25,17},{10,2},{18,10},{26,18},{... | collective-permute-start | bytes 737288 | tf_op jit(solution)/shard_map/ppermute | solution.py:343
  24.0 2.8 %copy-start.6 = (bf16[1024,3072]{1,0:T(8,128)(2,1)S(1)}, bf16[1024,3072]{1,0:T(8,128)(2,1)}, u32[]{:S(2)}) copy-start(bf16[1024,3072]{1,0:T(8,128)(2,1)} %weight_ref.5) | copy-start | bytes 18874372
  26.8 5.5 %copy-start.7 = (bf16[1024,1024]{1,0:T(8,128)(2,1)S(1)}, bf16[1024,1024]{1,0:T(8,128)(2,1)}, u32[]{:S(2)}) copy-start(bf16[1024,1024]{1,0:T(8,128)(2,1)} %out_w_ref.1) | copy-start | bytes 6291460
  26.8 5.5 %copy-start.8 = (bf16[448,432]{1,0:T(8,128)(2,1)S(1)}, bf16[448,432]{1,0:T(8,128)(2,1)}, u32[]{:S(2)}) copy-start(bf16[448,432]{1,0:T(8,128)(2,1)} %constant.74.clone.patch_ref) | copy-start | bytes 1161220
  26.8 5.5 %copy-start.12 = (bf16[304,256]{1,0:T(8,128)(2,1)S(1)}, bf16[304,256]{1,0:T(8,128)(2,1)}, u32[]{:S(2)}) copy-start(bf16[304,256]{1,0:T(8,128)(2,1)} %constant.77.clone.rest_2_.rest_6_) | copy-start | bytes 466948
  26.8 5.5 %copy-start.13 = (bf16[240,256]{1,0:T(8,128)(2,1)S(1)}, bf16[240,256]{1,0:T(8,128)(2,1)}, u32[]{:S(2)}) copy-start(bf16[240,256]{1,0:T(8,128)(2,1)} %constant.75.clone.rest_0_) | copy-start | bytes 368644
  26.8 5.5 %copy-start.14 = (bf16[240,256]{1,0:T(8,128)(2,1)S(1)}, bf16[240,256]{1,0:T(8,128)(2,1)}, u32[]{:S(2)}) copy-start(bf16[240,256]{1,0:T(8,128)(2,1)} %constant.79.clone.rest_4_) | copy-start | bytes 368644
  26.8 5.5 %copy-start.16 = (bf16[304,80]{1,0:T(8,128)(2,1)S(1)}, bf16[304,80]{1,0:T(8,128)(2,1)}, u32[]{:S(2)}) copy-start(bf16[304,80]{1,0:T(8,128)(2,1)} %constant.76.clone.rest_1_.rest_5_) | copy-start | bytes 145924
  26.8 5.5 %copy-start.17 = (bf16[80,304]{1,0:T(8,128)(2,1)S(1)}, bf16[80,304]{1,0:T(8,128)(2,1)}, u32[]{:S(2)}) copy-start(bf16[80,304]{1,0:T(8,128)(2,1)} %constant.78.clone.rest_3_.rest_7_) | copy-start | bytes 145924
  32.3 20.4 %copy-start.2 = (bf16[4096,256]{1,0:T(8,128)(2,1)S(1)}, bf16[4096,256]{1,0:T(8,128)(2,1)}, u32[]{:S(2)}) copy-start(bf16[4096,256]{1,0:T(8,128)(2,1)} %refs_0_.3) | copy-start | bytes 6291460
  39.1 13.6 %collective-permute-start.7 = (bf16[2048,256]{1,0:T(8,128)(2,1)S(1)}, bf16[2048,256]{1,0:T(8,128)(2,1)}, u32[]{:S(2)}, u32[]{:S(2)}) collective-permute-start(bf16[2048,256]{1,0:T(8,128)(2,1)S(1)} %collective-permute-done.5.refs_2_), channel_id=1, source_target_pairs={{0,1},{1,0},{2,3},{3,2},{4,5},{5,4},{6,7},{7,6},{8,9},{9,8},{10,11... | collective-permute-start | bytes 3145736 | tf_op jit(solution)/shard_map/ppermute | solution.py:497
  39.1 13.6 %collective-permute-start.8 = (bf16[2048,256]{1,0:T(8,128)(2,1)}, bf16[2048,256]{1,0:T(8,128)(2,1)}, u32[]{:S(2)}, u32[]{:S(2)}) collective-permute-start(bf16[2048,256]{1,0:T(8,128)(2,1)} %collective-permute-done.6.refs_4_), channel_id=1, source_target_pairs={{0,1},{1,0},{2,3},{3,2},{4,5},{5,4},{6,7},{7,6},{8,9},{9,8},{10,11... | collective-permute-start | bytes 3145736 | tf_op jit(solution)/shard_map/ppermute | solution.py:497
  39.6 12.8 %collective-permute-start.9 = (bf16[112,2048]{1,0:T(8,128)(2,1)}, bf16[112,2048]{1,0:T(8,128)(2,1)}, u32[]{:S(2)}, u32[]{:S(2)}) collective-permute-start(bf16[112,2048]{1,0:T(8,128)(2,1)} %get-tuple-element.42.upper_ref), channel_id=1, source_target_pairs={{0,4},{1,5},{2,6},{3,7},{4,0},{5,1},{6,2},{7,3},{8,12},{9,13},{10,... | collective-permute-start | bytes 1376264 | tf_op jit(solution)/shard_map/ppermute | solution.py:502
  40.1 12.5 %collective-permute-start.10 = (bf16[112,2048]{1,0:T(8,128)(2,1)}, bf16[112,2048]{1,0:T(8,128)(2,1)}, u32[]{:S(2)}, u32[]{:S(2)}) collective-permute-start(bf16[112,2048]{1,0:T(8,128)(2,1)} %get-tuple-element.43.lower_ref), channel_id=1, source_target_pairs={{0,2},{1,3},{2,0},{3,1},{4,6},{5,7},{6,4},{7,5},{8,10},{9,11},{10,... | collective-permute-start | bytes 1376264 | tf_op jit(solution)/shard_map/ppermute | solution.py:502
  56.7 6.6 %collective-permute-start.11 = (bf16[112,1024]{1,0:T(8,128)(2,1)S(1)}, bf16[112,1024]{1,0:T(8,128)(2,1)S(1)}, u32[]{:S(2)}, u32[]{:S(2)}) collective-permute-start(bf16[112,1024]{1,0:T(8,128)(2,1)S(1)} %get-tuple-element.49), channel_id=1, source_target_pairs={{0,4},{1,5},{2,6},{3,7},{4,0},{5,1},{6,2},{7,3},{8,12},{9,13},{10,... | collective-permute-start | bytes 688136 | tf_op jit(solution)/shard_map/ppermute | solution.py:502
  58.3 6.2 %collective-permute-start.12 = (bf16[112,1024]{1,0:T(8,128)(2,1)S(1)}, bf16[112,1024]{1,0:T(8,128)(2,1)S(1)}, u32[]{:S(2)}, u32[]{:S(2)}) collective-permute-start(bf16[112,1024]{1,0:T(8,128)(2,1)S(1)} %get-tuple-element.50), channel_id=1, source_target_pairs={{0,2},{1,3},{2,0},{3,1},{4,6},{5,7},{6,4},{7,5},{8,10},{9,11},{10,... | collective-permute-start | bytes 688136 | tf_op jit(solution)/shard_map/ppermute | solution.py:502
  58.6 8.5 %copy-start = (bf16[2048,1024]{1,0:T(8,128)(2,1)S(1)}, bf16[2048,1024]{1,0:T(8,128)(2,1)}, u32[]{:S(2)}) copy-start(bf16[2048,1024]{1,0:T(8,128)(2,1)} %up_ref.7) | copy-start | bytes 12582916
  58.6 8.5 %copy-start.1 = (bf16[1024,2048]{1,0:T(8,128)(2,1)S(1)}, bf16[1024,2048]{1,0:T(8,128)(2,1)}, u32[]{:S(2)}) copy-start(bf16[1024,2048]{1,0:T(8,128)(2,1)} %down_ref.7) | copy-start | bytes 12582916
  65.2 1.9 %collective-permute-start.15 = (bf16[112,2048]{1,0:T(8,128)(2,1)S(1)}, bf16[112,2048]{1,0:T(8,128)(2,1)S(1)}, u32[]{:S(2)}, u32[]{:S(2)}) collective-permute-start(bf16[112,2048]{1,0:T(8,128)(2,1)S(1)} %combine.1.mine_ref), channel_id=1, source_target_pairs={{0,1},{1,0},{2,3},{3,2},{4,5},{5,4},{6,7},{7,6},{8,9},{9,8},{10,11... | collective-permute-start | bytes 1376264 | tf_op jit(solution)/shard_map/ppermute | solution.py:497
  65.3 13.2 %collective-permute-start.13 = (bf16[112,2048]{1,0:T(8,128)(2,1)S(1)}, bf16[112,2048]{1,0:T(8,128)(2,1)S(1)}, u32[]{:S(2)}, u32[]{:S(2)}) collective-permute-start(bf16[112,2048]{1,0:T(8,128)(2,1)S(1)} %combine.1.mine_ref), channel_id=1, source_target_pairs={{0,2},{1,5},{2,0},{3,7},{4,6},{5,1},{6,4},{7,3},{8,10},{9,13},{10,... | collective-permute-start | bytes 1376264 | tf_op jit(solution)/shard_map/ppermute | solution.py:507
  65.9 12.6 %collective-permute-start.14 = (bf16[112,2048]{1,0:T(8,128)(2,1)S(1)}, bf16[112,2048]{1,0:T(8,128)(2,1)S(1)}, u32[]{:S(2)}, u32[]{:S(2)}) collective-permute-start(bf16[112,2048]{1,0:T(8,128)(2,1)S(1)} %combine.1.mine_ref), channel_id=1, source_target_pairs={{0,4},{1,3},{2,6},{3,1},{4,0},{5,7},{6,2},{7,5},{8,12},{9,11},{10,... | collective-permute-start | bytes 1376264 | tf_op jit(solution)/shard_map/ppermute | solution.py:507
  78.5 1.8 %collective-permute-start.20 = (bf16[112,2048]{1,0:T(8,128)(2,1)S(1)}, bf16[112,2048]{1,0:T(8,128)(2,1)S(1)}, u32[]{:S(2)}, u32[]{:S(2)}) collective-permute-start(bf16[112,2048]{1,0:T(8,128)(2,1)S(1)} %collective-permute-done.13.mine_ref), channel_id=1, source_target_pairs={{0,1},{1,0},{2,3},{3,2},{4,5},{5,4},{6,7},{7,6},{8,9},{9,8},{10,11... | collective-permute-start | bytes 1376264 | tf_op jit(solution)/shard_map/ppermute | solution.py:497
  78.5 4.6 %collective-permute-start.19 = (bf16[112,1024]{1,0:T(8,128)(2,1)S(1)}, bf16[112,1024]{1,0:T(8,128)(2,1)S(1)}, u32[]{:S(2)}, u32[]{:S(2)}) collective-permute-start(bf16[112,1024]{1,0:T(8,128)(2,1)S(1)} %get-tuple-element.57), channel_id=1, source_target_pairs={{0,1},{1,0},{2,3},{3,2},{4,5},{5,4},{6,7},{7,6},{8,9},{9,8},{10,11... | collective-permute-start | bytes 688136 | tf_op jit(solution)/shard_map/ppermute | solution.py:497
  79.0 4.5 %collective-permute-start.18 = (bf16[112,1024]{1,0:T(8,128)(2,1)S(1)}, bf16[112,1024]{1,0:T(8,128)(2,1)S(1)}, u32[]{:S(2)}, u32[]{:S(2)}) collective-permute-start(bf16[112,1024]{1,0:T(8,128)(2,1)S(1)} %get-tuple-element.56), channel_id=1, source_target_pairs={{0,1},{1,0},{2,3},{3,2},{4,5},{5,4},{6,7},{7,6},{8,9},{9,8},{10,11... | collective-permute-start | bytes 688136 | tf_op jit(solution)/shard_map/ppermute | solution.py:497
  79.0 8.5 %collective-permute-start.16 = (bf16[112,2048]{1,0:T(8,128)(2,1)S(1)}, bf16[112,2048]{1,0:T(8,128)(2,1)S(1)}, u32[]{:S(2)}, u32[]{:S(2)}) collective-permute-start(bf16[112,2048]{1,0:T(8,128)(2,1)S(1)} %collective-permute-done.13.mine_ref), channel_id=1, source_target_pairs={{0,4},{1,3},{2,6},{3,1},{4,0},{5,7},{6,2},{7,5},{8,12},{9,11},{10,... | collective-permute-start | bytes 1376264 | tf_op jit(solution)/shard_map/ppermute | solution.py:507
  79.6 4.0 %collective-permute-start.23 = (bf16[112,2048]{1,0:T(8,128)(2,1)S(1)}, bf16[112,2048]{1,0:T(8,128)(2,1)S(1)}, u32[]{:S(2)}, u32[]{:S(2)}) collective-permute-start(bf16[112,2048]{1,0:T(8,128)(2,1)S(1)} %collective-permute-done.14.mine_ref), channel_id=1, source_target_pairs={{0,1},{1,0},{2,3},{3,2},{4,5},{5,4},{6,7},{7,6},{8,9},{9,8},{10,11... | collective-permute-start | bytes 1376264 | tf_op jit(solution)/shard_map/ppermute | solution.py:497
  82.9 4.6 %collective-permute-start.22 = (bf16[112,1024]{1,0:T(8,128)(2,1)S(1)}, bf16[112,1024]{1,0:T(8,128)(2,1)S(1)}, u32[]{:S(2)}, u32[]{:S(2)}) collective-permute-start(bf16[112,1024]{1,0:T(8,128)(2,1)S(1)} %get-tuple-element.60), channel_id=1, source_target_pairs={{0,1},{1,0},{2,3},{3,2},{4,5},{5,4},{6,7},{7,6},{8,9},{9,8},{10,11... | collective-permute-start | bytes 688136 | tf_op jit(solution)/shard_map/ppermute | solution.py:497
  83.1 4.4 %collective-permute-start.21 = (bf16[112,1024]{1,0:T(8,128)(2,1)S(1)}, bf16[112,1024]{1,0:T(8,128)(2,1)S(1)}, u32[]{:S(2)}, u32[]{:S(2)}) collective-permute-start(bf16[112,1024]{1,0:T(8,128)(2,1)S(1)} %get-tuple-element.59), channel_id=1, source_target_pairs={{0,1},{1,0},{2,3},{3,2},{4,5},{5,4},{6,7},{7,6},{8,9},{9,8},{10,11... | collective-permute-start | bytes 688136 | tf_op jit(solution)/shard_map/ppermute | solution.py:497
  86.2 1.6 %collective-permute-start.25 = (bf16[112,1024]{1,0:T(8,128)(2,1)S(1)}, bf16[112,1024]{1,0:T(8,128)(2,1)S(1)}, u32[]{:S(2)}, u32[]{:S(2)}) collective-permute-start(bf16[112,1024]{1,0:T(8,128)(2,1)S(1)} %get-tuple-element.64), channel_id=1, source_target_pairs={{0,1},{1,0},{2,3},{3,2},{4,5},{5,4},{6,7},{7,6},{8,9},{9,8},{10,11... | collective-permute-start | bytes 688136 | tf_op jit(solution)/shard_map/ppermute | solution.py:497
  86.4 1.7 %collective-permute-start.24 = (bf16[112,1024]{1,0:T(8,128)(2,1)S(1)}, bf16[112,1024]{1,0:T(8,128)(2,1)S(1)}, u32[]{:S(2)}, u32[]{:S(2)}) collective-permute-start(bf16[112,1024]{1,0:T(8,128)(2,1)S(1)} %get-tuple-element.63), channel_id=1, source_target_pairs={{0,1},{1,0},{2,3},{3,2},{4,5},{5,4},{6,7},{7,6},{8,9},{9,8},{10,11... | collective-permute-start | bytes 688136 | tf_op jit(solution)/shard_map/ppermute | solution.py:497
  87.4 1.8 %collective-permute-start.17 = (bf16[112,2048]{1,0:T(8,128)(2,1)S(1)}, bf16[112,2048]{1,0:T(8,128)(2,1)S(1)}, u32[]{:S(2)}, u32[]{:S(2)}) collective-permute-start(bf16[112,2048]{1,0:T(8,128)(2,1)S(1)} %collective-permute-done.16.mine_ref), channel_id=1, source_target_pairs={{0,1},{1,0},{2,3},{3,2},{4,5},{5,4},{6,7},{7,6},{8,9},{9,8},{10,11... | collective-permute-start | bytes 1376264 | tf_op jit(solution)/shard_map/ppermute | solution.py:497
  89.3 12.9 %collective-permute-start.28 = (bf16[112,2048]{1,0:T(8,128)(2,1)S(1)}, bf16[112,2048]{1,0:T(8,128)(2,1)S(1)}, u32[]{:S(2)}, u32[]{:S(2)}) collective-permute-start(bf16[112,2048]{1,0:T(8,128)(2,1)S(1)} %add_convert_fusion.3), channel_id=1, source_target_pairs={{0,2},{1,5},{2,0},{3,7},{4,6},{5,1},{6,4},{7,3},{8,10},{9,13},{10,... | collective-permute-start | bytes 1376264 | tf_op jit(solution)/shard_map/ppermute | solution.py:507
  89.7 12.4 %collective-permute-start.29 = (bf16[112,2048]{1,0:T(8,128)(2,1)S(1)}, bf16[112,2048]{1,0:T(8,128)(2,1)S(1)}, u32[]{:S(2)}, u32[]{:S(2)}) collective-permute-start(bf16[112,2048]{1,0:T(8,128)(2,1)S(1)} %add_convert_fusion.2), channel_id=1, source_target_pairs={{0,4},{1,3},{2,6},{3,1},{4,0},{5,7},{6,2},{7,5},{8,12},{9,11},{10,... | collective-permute-start | bytes 1376264 | tf_op jit(solution)/shard_map/ppermute | solution.py:507
  93.0 1.6 %collective-permute-start.26 = (bf16[112,1024]{1,0:T(8,128)(2,1)S(1)}, bf16[112,1024]{1,0:T(8,128)(2,1)S(1)}, u32[]{:S(2)}, u32[]{:S(2)}) collective-permute-start(bf16[112,1024]{1,0:T(8,128)(2,1)S(1)} %get-tuple-element.67), channel_id=1, source_target_pairs={{0,1},{1,0},{2,3},{3,2},{4,5},{5,4},{6,7},{7,6},{8,9},{9,8},{10,11... | collective-permute-start | bytes 688136 | tf_op jit(solution)/shard_map/ppermute | solution.py:497
  93.0 1.8 %collective-permute-start.27 = (bf16[112,1024]{1,0:T(8,128)(2,1)S(1)}, bf16[112,1024]{1,0:T(8,128)(2,1)S(1)}, u32[]{:S(2)}, u32[]{:S(2)}) collective-permute-start(bf16[112,1024]{1,0:T(8,128)(2,1)S(1)} %get-tuple-element.68), channel_id=1, source_target_pairs={{0,1},{1,0},{2,3},{3,2},{4,5},{5,4},{6,7},{7,6},{8,9},{9,8},{10,11... | collective-permute-start | bytes 688136 | tf_op jit(solution)/shard_map/ppermute | solution.py:497
  102.3 13.1 %collective-permute-start.30 = (bf16[112,2048]{1,0:T(8,128)(2,1)S(1)}, bf16[112,2048]{1,0:T(8,128)(2,1)S(1)}, u32[]{:S(2)}, u32[]{:S(2)}) collective-permute-start(bf16[112,2048]{1,0:T(8,128)(2,1)S(1)} %add_convert_fusion.1), channel_id=1, source_target_pairs={{0,6},{1,7},{2,4},{3,5},{4,2},{5,3},{6,0},{7,1},{8,14},{9,15},{10,... | collective-permute-start | bytes 1376264 | tf_op jit(solution)/shard_map/ppermute | solution.py:502

commit v6 on v5

--- a/solution.py
+++ b/solution.py
@@ -135,26 +135,97 @@
     return normalize(values.reshape(-1, values.shape[-1]))
 
 
+def project(normed_ref, weight_ref, out_ref):
+    step = 256
+    for at in range(0, out_ref.shape[1], step):
+        out_ref[:, at : at + step] = dot(normed_ref[...], weight_ref[:, at : at + step]).astype(BF16)
+
+
 def padded_rows(values, total):
     if values.shape[0] == total:
         return values
     return jnp.concatenate([values, jnp.zeros((total - values.shape[0], values.shape[1]), values.dtype)], axis=0)
 
 
-def project(normed_ref, weight_ref, out_ref, first):
-    step = 256
-    for at in range(0, out_ref.shape[1], step):
-        part = weight_ref[:, first + at : first + at + step]
-        out_ref[:, at : at + step] = dot(normed_ref[...], part).astype(BF16)
-
-
-def own_kernel(bands, tokens_ref, weight_ref, out_ref, normed_ref):
+def prepare_kernel(tokens_ref, weight_ref, east_ref, west_ref, upper_ref, lower_ref, sems):
+    half = upper_ref.shape[0]
+    copies = [
+        pltpu.make_async_copy(weight_ref.at[k * half : (k + 1) * half], ref, sems.at[k])
+        for k, ref in enumerate((upper_ref, lower_ref))
+    ]
+    for copy in copies:
+        copy.start()
+    columns = tokens_ref.shape[1]
+    east_ref[...] = tokens_ref[:, columns - SIDE :]
+    west_ref[...] = tokens_ref[:, :SIDE]
+    for copy in copies:
+        copy.wait()
+
+
+def prepare(tokens, merge_weight):
+    rows, _, width = tokens.shape
+    depth, block = merge_weight.shape
+    vmem, anywhere = pl.BlockSpec(memory_space=pltpu.VMEM), pl.BlockSpec(memory_space=pl.ANY)
+    return pl.pallas_call(
+        prepare_kernel,
+        in_specs=[vmem, anywhere],
+        out_specs=[vmem] * 4,
+        out_shape=[jax.ShapeDtypeStruct((rows, SIDE, width), BF16)] * 2
+        + [jax.ShapeDtypeStruct((depth // 2, block), BF16)] * 2,
+        scratch_shapes=[pltpu.SemaphoreType.DMA((2,))],
+        compiler_params=params(52),
+        name="prepare",
+    )(tokens, merge_weight)
+
+
+def own_kernel(bands, tokens_ref, weight_ref, out_ref, kv_ref, normed_ref, q_ref, sems):
+    width = q_ref.shape[1]
+    chunk = weight_ref.shape[1] // sems.shape[0]
+    places = []
+    for n in range(sems.shape[0]):
+        at = n * chunk
+        places.append((q_ref, at) if at < width else (kv_ref, at - width))
+    copies = [
+        pltpu.make_async_copy(weight_ref.at[:, pl.ds(n * chunk, chunk)], ref.at[:, pl.ds(at, chunk)], sems.at[n])
+        for n, (ref, at) in enumerate(places)
+    ]
+    for copy in copies:
+        copy.start()
     normed = flat_normed(tokens_ref)
     for b in range(bands.count):
         at = bands.first[b] * bands.columns
         part = padded_rows(normed[at : at + bands.own[b]], bands.own_padded[b])
         normed_ref[bands.own_at[b] : bands.own_at[b] + bands.own_padded[b], :] = part.astype(BF16)
-    project(normed_ref, weight_ref, out_ref, 0)
+    step = 256
+    for n, (ref, first) in enumerate(places):
+        copies[n].wait()
+        for at in range(0, chunk, step):
+            part = ref[:, first + at : first + at + step]
+            out_ref[:, n * chunk + at : n * chunk + at + step] = dot(normed_ref[...], part).astype(BF16)
+
+
+def own_projection(bands, tokens, weight):
+    width, out = weight.shape
+    vmem = pl.BlockSpec(memory_space=pltpu.VMEM)
+    return pl.pallas_call(
+        functools.partial(own_kernel, bands),
+        in_specs=[vmem, pl.BlockSpec(memory_space=pl.ANY)],
+        out_specs=[vmem, vmem],
+        out_shape=[
+            jax.ShapeDtypeStruct((bands.own_total, out), BF16),
+            jax.ShapeDtypeStruct((width, out - width), BF16),
+        ],
+        scratch_shapes=[
+            pltpu.VMEM((bands.own_total, width), BF16),
+            pltpu.VMEM((width, width), BF16),
+            pltpu.SemaphoreType.DMA((6,)),
+        ],
+        compiler_params=params(42),
+        cost_estimate=pl.CostEstimate(
+            flops=2 * bands.own_total * width * out, bytes_accessed=2 * width * out, transcendentals=0
+        ),
+        name="own_projection",
+    )(tokens, weight)
 
 
 def attend(bands, some, kinds, consts, own_ref, outer, bias_ref, put, scratch):
@@ -216,13 +287,12 @@
 
 def middle_kernel(bands, some, kinds, west_ref, east_ref, own_ref, weight_ref, *rest):
     consts, (side_ref, out_ref, normed_ref, *scratch) = rest[:-8], rest[-8:]
-    width = weight_ref.shape[0]
     west, east = flat_normed(west_ref), flat_normed(east_ref)
     for b in range(bands.count):
         at, size = bands.first[b] * SIDE, bands.height[b] * SIDE
         part = jnp.concatenate([west[at : at + size], east[at : at + size]], axis=0)
         normed_ref[bands.side_at[b] : bands.side_at[b] + bands.side[b], :] = part.astype(BF16)
-    project(normed_ref, weight_ref, side_ref, width)
+    project(normed_ref, weight_ref, side_ref)
 
     def outer(b):
         return [(side_ref, bands.side_at[b], bands.side[b])]
@@ -242,7 +312,7 @@
     slab = bands.slab_padded
     for k, ref in enumerate((north_ref, south_ref)):
         normed_ref[k * slab : (k + 1) * slab, :] = padded_rows(flat_normed(ref), slab).astype(BF16)
-    project(normed_ref, weight_ref, slab_ref, width)
+    project(normed_ref, weight_ref, slab_ref)
 
     def outer(b):
         return [
@@ -287,20 +357,12 @@
     )(*args)
 
 
-def attention(bands, tokens, qkv_weight, out_weight):
+def attention(bands, tokens, rims, qkv_weight, out_weight):
     rows, columns, width = tokens.shape
     block = width * GROUP // HEADS
-    west = shift(tokens[:, columns - SIDE :], "lon", 1, True)
-    east = shift(tokens[:, :SIDE], "lon", -1, True)
-    own = vmem_call(
-        functools.partial(own_kernel, bands),
-        [(bands.own_total, 3 * width)],
-        [tokens, qkv_weight],
-        [pltpu.VMEM((bands.own_total, width), BF16)],
-        6 * bands.own_total * width * width,
-        "own_projection",
-        mib=16,
-    )[0]
+    west = shift(rims[0], "lon", 1, True)
+    east = shift(rims[1], "lon", -1, True)
+    own, kv_weight = own_projection(bands, tokens, qkv_weight)
 
     def slab(part):
         return jnp.concatenate([west[part], tokens[part], east[part]], axis=1)
@@ -313,7 +375,7 @@
     side, attended = vmem_call(
         functools.partial(middle_kernel, bands, inner, kinds),
         [(bands.side_total, 2 * width), (bands.own_at[-1] - bands.own_at[1], width)],
-        [west, east, own, qkv_weight] + consts,
+        [west, east, own, kv_weight] + consts,
         [pltpu.VMEM((bands.side_total, width), BF16)] + attend_scratch(bands, inner, block),
         5 * 10**9,
         "middle_attention",
@@ -324,7 +386,7 @@
     return vmem_call(
         functools.partial(edge_kernel, bands, edges, kinds),
         [tokens.shape, (padded, 2 * width), (padded, 2 * width)],
-        [tokens, north, south, key_bias(), own, side, attended, qkv_weight, out_weight, bands.patch_matrix()] + consts,
+        [tokens, north, south, key_bias(), own, side, attended, kv_weight, out_weight, bands.patch_matrix()] + consts,
         [
             pltpu.VMEM((2 * bands.slab_padded, width), BF16),
             pltpu.VMEM((2 * bands.slab_padded, 2 * width), BF16),
@@ -369,7 +431,9 @@
 
 
 def merge_own_kernel(place_ref, upper_ref, lower_ref, *refs):
-    weights, (own_ref, x_ref, y_ref) = refs[:6], refs[6:]
+    weights, (own_ref, x_ref, y_ref), kept = refs[:6], refs[6:9], refs[9:]
+    for ref, to in zip(weights, kept):
+        to[...] = ref[...]
 
     def own(at, a, b):
         own_ref[:, at] = a + b
@@ -427,12 +491,12 @@
     )(place, *args)
 
 
-def merge_by_squares(upper, lower, merge_weight):
+def merge_by_squares(upper, lower, merge_weight, halves):
     half = merge_weight.shape[0] // 2
     block = merge_weight.shape[1]
     count = upper.shape[0]
-    x = chip_swap(merge_weight[:half], 1)
-    y = chip_swap(merge_weight[half:], 2)
+    x = chip_swap(halves[0], 1)
+    y = chip_swap(halves[1], 2)
     x_pair, y_pair, _ = lax.optimization_barrier((x, y, upper))
     weights = [merge_weight, core_swap(merge_weight), x, core_swap(x_pair), y, core_swap(y_pair)]
     place = place_index()
@@ -440,7 +504,11 @@
     from_x = chip_swap(lower, 1)
     flops = 16 * count * half * block
     wide = jax.ShapeDtypeStruct((count, 2 * block), F32)
-    own = local_call(merge_own_kernel, [wide] * 3, place, [upper, lower] + weights, flops, "merge_own")
+    kept = [jax.ShapeDtypeStruct(w.shape, BF16) for w in weights]
+    *own, a, b, c, d, e, f = local_call(
+        merge_own_kernel, [wide] * 3 + kept, place, [upper, lower] + weights, flops, "merge_own", 28
+    )
+    weights = [a, b, c, d, e, f]
     pair = jax.ShapeDtypeStruct((count, 4 * block), BF16)
     to_y, to_x = local_call(merge_other_kernel, [pair] * 2, place, [from_y, from_x] + weights, flops, "merge_other")
     back_y, back_x = chip_swap(to_y, 2), chip_swap(to_x, 1)
@@ -507,8 +575,8 @@
     return lax.ppermute(value, "lon", [(i, i ^ (2 * (second if i % 2 else first))) for i in range(size)])
 
 
-def coarse_by_squares(upper, lower, merge_weight, up, down):
-    own = merge_by_squares(upper, lower, merge_weight)
+def coarse_by_squares(upper, lower, merge_weight, halves, up, down):
+    own = merge_by_squares(upper, lower, merge_weight, halves)
     near = cross(own, 1, 2)
     next_near = cross(own, 2, 1)
     first = feed_forward(own, core_swap(own), up, down)
@@ -525,7 +593,7 @@
     return sum(part.astype(F32) for part in (own, sums[0], *back))
 
 
-def coarse_by_chips(upper, lower, merge_weight, up, down):
+def coarse_by_chips(upper, lower, merge_weight, halves, up, down):
     weight = lax.all_gather(merge_weight, "lon", axis=1, tiled=True)
     patches = jnp.concatenate([upper, lower], axis=1)
     coarse = jnp.dot(patches, weight, preferred_element_type=F32).astype(BF16)
@@ -542,9 +610,11 @@
     rows, columns, width = tokens.shape
     bands = Bands(rows, columns)
     cells = rows * columns // 4
-    middle_out, upper, lower = attention(bands, tokens, qkv_weight, out_weight)
+    *rims, upper_weight, lower_weight = prepare(tokens, merge_weight)
+    middle_out, upper, lower = attention(bands, tokens, rims, qkv_weight, out_weight)
     coarse = coarse_by_squares if lax.axis_size("lon") == 8 else coarse_by_chips
-    total = coarse(upper, lower, merge_weight, up_weight, down_weight)
+    halves = [upper_weight, lower_weight]
+    total = coarse(upper, lower, merge_weight, halves, up_weight, down_weight)
     coarse_out = total[:cells].astype(jnp.bfloat16)
     return (middle_out, coarse_out.reshape(rows // 2, columns // 2, -1))
 

time: 117 us -> 116 us (level)
  local copies, waits for them, and re-layouts: 11.5 us -> 2.2 us
  starting transfers between devices: 20.8 us -> 28.1 us
  Pallas kernels: 35.1 us -> 38.7 us
  waiting for transfers between devices: 47.2 us -> 45.1 us
    pallas_call x0 -> x2, Pallas kernels: none -> 8.34 us  [the longest x1 5.35 us: own_projection(): pl.pallas_call(functools.partial(own_kernel, bands), in_specs=[vmem, pl.B...]
    ppermute x4, waiting for transfers between devices: 0.01 us -> 5 us  [shift(): return lax.ppermute(part, axis, pairs)]
    slice x2 -> x0, local copies, waits for them, and re-layouts: 4.89 us -> none  [the longest x1 3.08 us: merge_by_squares(): y = chip_swap(merge_weight[half:], 2)]
    unnamed x36 -> x32, local copies, waits for them, and re-layouts: 5.63 us -> 1.26 us
    ppermute x5, starting transfers between devices: 2.82 us -> 6.81 us  [cross(): lax.ppermute(value, 'lon', [(i, i ^ 2 * (second if i % 2 else first)) for...]
    pallas_call x3 -> x2, Pallas kernels: 15.5 us -> 11.8 us  [vmem_call(): pl.pallas_call(kernel, in_specs=[vmem] * len(args), out_specs=[vmem] * le...]
    ppermute x7, waiting for transfers between devices: 26.2 us -> 23.2 us  [chip_swap(): lax.ppermute(value, 'lon', [(i, i ^ 2 * offset) for i in range(size)])]
    ppermute x5, waiting for transfers between devices: 16.8 us -> 14 us  [cross(): lax.ppermute(value, 'lon', [(i, i ^ 2 * (second if i % 2 else first)) for...]
  transfers between devices with their start and end apart: 31 -> 31, of which waited for: 15 -> 17; matrix products, arithmetic and copies ran while one was open for 3% -> 0% of each run, Pallas kernels for 26% -> 30%
where the time goes in v6:
time: 116 us
  waiting for transfers between devices  45.1 us (39%)
  Pallas kernels  38.7 us (33%)
  starting transfers between devices  28.1 us (24%)
  local copies, waits for them, and re-layouts  2.2 us (2%)
    ppermute x7, waiting for transfers between devices, chip_swap(): lax.ppermute(value, 'lon', [(i, i ^ 2 * offset) for i in range(size)])  23.2 us
    ppermute x5, waiting for transfers between devices, cross(): lax.ppermute(value, 'lon', [(i, i ^ 2 * (second if i % 2 else first)) for...  14 us
    pallas_call x2, Pallas kernels, vmem_call(): pl.pallas_call(kernel, in_specs=[vmem] * len(args), out_specs=[vmem] * le...  11.8 us
    pallas_call x4, Pallas kernels, feed_forward(): pl.pallas_call(ffn_kernel, in_specs=[vmem] * 4, out_specs=[vmem] * 3, out...  10.5 us
    ppermute x7, starting transfers between devices, chip_swap(): lax.ppermute(value, 'lon', [(i, i ^ 2 * offset) for i in range(size)])  9.04 us
    ppermute x4, starting transfers between devices, shift(): return lax.ppermute(part, axis, pairs)  8.58 us
    pallas_call x3, Pallas kernels, local_call(): pl.pallas_call(kernel, in_specs=[pl.BlockSpec(memory_space=pltpu.SMEM)] +...  8.15 us
    ppermute x5, starting transfers between devices, cross(): lax.ppermute(value, 'lon', [(i, i ^ 2 * (second if i % 2 else first)) for...  6.81 us
  transfers between devices with their start and end apart: 31, of which 17 were waited for; matrix products, arithmetic and copies ran while one was open for 0% of the time, Pallas kernels for 30%

profile of v6, /device:TPU:0, one launch (start us, length us, event | category | flops | bytes accessed | tf_op | source)
XLA Modules:
  0.0 116.2 jit_solution(7846311331941691003)
XLA Ops:
  0.6 0.5 collective-permute-start.4
  1.1 1.2 %copy-done.3 = bf16[18,24,1024]{2,1,0:T(8,128)(2,1)S(1)} copy-done((bf16[18,24,1024]{2,1,0:T(8,128)(2,1)S(1)}, bf16[18,24,1024]{2,1,0:T(8,128)(2,1)}, u32[]{:S(2)}) %copy-start.3) | copy-done | bytes 884760
  2.3 3.0 %prepare.1 = (bf16[18,8,1024]{2,1,0:T(8,128)(2,1)S(1)}, bf16[18,8,1024]{2,1,0:T(8,128)(2,1)S(1)}, bf16[2048,256]{1,0:T(8,128)(2,1)}, bf16[2048,256]{1,0:T(8,128)(2,1)}) custom-call(bf16[18,24,1024]{2,1,0:T(8,128)(2,1)S(1)} %copy-done.3, bf16[4096,256]{1,0:T(8,128)(2,1)} %refs_0_.1), custom_call_target="tpu_custom_call" | custom-call | tf_op jit(solution)/shard_map/prepare/pallas_call | solution.py:169
  5.3 3.6 %collective-permute-start.1 = (bf16[18,8,1024]{2,1,0:T(8,128)(2,1)S(1)}, bf16[18,8,1024]{2,1,0:T(8,128)(2,1)S(1)}, u32[]{:S(2)}, u32[]{:S(2)}) collective-permute-start(bf16[18,8,1024]{2,1,0:T(8,128)(2,1)S(1)} %get-tuple-element.52), channel_id=1, source_target_pairs={{0,7},{1,0},{2,1},{3,2},{4,3},{5,4},{6,5},{7,6},{8,15},{9,8},{10,9... | collective-permute-start | bytes 884744 | tf_op jit(solution)/shard_map/ppermute | solution.py:405
  8.9 1.1 collective-permute-start.6
  10.2 5.4 %own_projection.1 = (bf16[448,3072]{1,0:T(8,128)(2,1)S(1)}, bf16[1024,2048]{1,0:T(8,128)(2,1)S(1)}) custom-call(bf16[18,24,1024]{2,1,0:T(8,128)(2,1)S(1)} %copy-done.4, bf16[1024,3072]{1,0:T(8,128)(2,1)} %weight_ref.3), custom_call_target="tpu_custom_call" | custom-call | flops 2818572288 | bytes 6291456 | tf_op jit(solution)/shard_map/own_projection/pallas_call | solution.py:210
  15.5 0.1 or_select_fusion.bias_ref
  15.6 0.8 collective-permute-done.1.east_ref
  16.4 2.8 %collective-permute-done.west_ref = bf16[18,8,1024]{2,1,0:T(8,128)(2,1)S(1)} collective-permute-done((bf16[18,8,1024]{2,1,0:T(8,128)(2,1)S(1)}, bf16[18,8,1024]{2,1,0:T(8,128)(2,1)S(1)}, u32[]{:S(2)}, u32[]{:S(2)}) %collective-permute-start) | collective-permute-done | bytes 294944 | tf_op jit(solution)/shard_map/ppermute | solution.py:405
  19.2 3.5 %collective-permute-start.2 = (bf16[3,40,1024]{2,1,0:T(8,128)(2,1)S(1)}, bf16[3,40,1024]{2,1,0:T(8,128)(2,1)S(1)}, u32[]{:S(2)}, u32[]{:S(2)}) collective-permute-start(bf16[3,40,1024]{2,1,0:T(8,128)(2,1)S(1)} %pad_maximum_fusion), channel_id=1, source_target_pairs={{0,8},{8,16},{16,24},{1,9},{9,17},{17,25},{2,10},{10,18},{18,26},{... | collective-permute-start | bytes 737288 | tf_op jit(solution)/shard_map/ppermute | solution.py:405
  22.8 1.5 %collective-permute-start.3 = (bf16[3,40,1024]{2,1,0:T(8,128)(2,1)S(1)}, bf16[3,40,1024]{2,1,0:T(8,128)(2,1)S(1)}, u32[]{:S(2)}, u32[]{:S(2)}) collective-permute-start(bf16[3,40,1024]{2,1,0:T(8,128)(2,1)S(1)} %pad_maximum_fusion.1), channel_id=1, source_target_pairs={{8,0},{16,8},{24,16},{9,1},{17,9},{25,17},{10,2},{18,10},{26,18},{... | collective-permute-start | bytes 737288 | tf_op jit(solution)/shard_map/ppermute | solution.py:405
  24.4 5.0 %middle_attention.1 = (bf16[288,2048]{1,0:T(8,128)(2,1)S(1)}, bf16[288,1024]{1,0:T(8,128)(2,1)S(1)}) custom-call(bf16[18,8,1024]{2,1,0:T(8,128)(2,1)S(1)} %collective-permute-done.west_ref, bf16[18,8,1024]{2,1,0:T(8,128)(2,1)S(1)} %collective-permute-done.1.east_ref, bf16[448,3072]{1,0:T(8,128)(2,1)S(1)} %get-tuple-element.53.own_ref, ...), custom_call_target="tpu_custom_call" | custom-call | flops 5000000000 | bytes 1048576 | tf_op jit(solution)/shard_map/middle_attention/pallas_call | solution.py:348
  29.4 1.4 %collective-permute-done.3.south_ref = bf16[3,40,1024]{2,1,0:T(8,128)(2,1)S(1)} collective-permute-done((bf16[3,40,1024]{2,1,0:T(8,128)(2,1)S(1)}, bf16[3,40,1024]{2,1,0:T(8,128)(2,1)S(1)}, u32[]{:S(2)}, u32[]{:S(2)}) %collective-permute-start.3) | collective-permute-done | bytes 245792 | tf_op jit(solution)/shard_map/ppermute | solution.py:405
  30.9 6.8 %edge_attention.1 = (bf16[18,24,1024]{2,1,0:T(8,128)(2,1)}, bf16[112,2048]{1,0:T(8,128)(2,1)}, bf16[112,2048]{1,0:T(8,128)(2,1)}) custom-call(bf16[18,24,1024]{2,1,0:T(8,128)(2,1)S(1)} %copy-done.4, bf16[3,40,1024]{2,1,0:T(8,128)(2,1)S(1)} %collective-permute-done.2.north_ref, bf16[3,40,1024]{2,1,0:T(8,128)(2,1)S(1)} %collective-permute-done.3.south_ref, ...), custom_call_target="tpu_custom_call" | custom-call | flops 6000000000 | bytes 1048576 | tf_op jit(solution)/shard_map/edge_attention/pallas_call | solution.py:348
  37.7 0.3 collective-permute-done.6.refs_4_
  38.0 0.3 collective-permute-start.7
  38.3 0.2 collective-permute-start.8
  38.5 1.8 %collective-permute-start.9 = (bf16[112,2048]{1,0:T(8,128)(2,1)}, bf16[112,2048]{1,0:T(8,128)(2,1)}, u32[]{:S(2)}, u32[]{:S(2)}) collective-permute-start(bf16[112,2048]{1,0:T(8,128)(2,1)} %get-tuple-element.58.upper_ref), channel_id=1, source_target_pairs={{0,4},{1,5},{2,6},{3,7},{4,0},{5,1},{6,2},{7,3},{8,12},{9,13},{10,... | collective-permute-start | bytes 1376264 | tf_op jit(solution)/shard_map/ppermute | solution.py:570
  40.3 2.1 %collective-permute-start.10 = (bf16[112,2048]{1,0:T(8,128)(2,1)}, bf16[112,2048]{1,0:T(8,128)(2,1)}, u32[]{:S(2)}, u32[]{:S(2)}) collective-permute-start(bf16[112,2048]{1,0:T(8,128)(2,1)} %get-tuple-element.59.lower_ref), channel_id=1, source_target_pairs={{0,2},{1,3},{2,0},{3,1},{4,6},{5,7},{6,4},{7,5},{8,10},{9,11},{10,... | collective-permute-start | bytes 1376264 | tf_op jit(solution)/shard_map/ppermute | solution.py:570
  42.4 0.1 pad_add_fusion.place_ref
  42.5 4.7 %merge_own.1 = (f32[112,512]{1,0:T(8,128)S(1)}, f32[112,512]{1,0:T(8,128)S(1)}, f32[112,512]{1,0:T(8,128)S(1)}, bf16[4096,256]{1,0:T(8,128)(2,1)S(1)}, bf16[4096...) custom-call(s32[2]{0:T(128)S(1)} %pad_add_fusion.place_ref, ...), custom_call_target="tpu_custom_call" | custom-call | flops 939524096 | bytes 1048576 | tf_op jit(solution)/shard_map/merge_own/pallas_call | solution.py:483
  47.1 4.6 %collective-permute-done.9.upper_ref = bf16[112,2048]{1,0:T(8,128)(2,1)} collective-permute-done((bf16[112,2048]{1,0:T(8,128)(2,1)}, bf16[112,2048]{1,0:T(8,128)(2,1)}, u32[]{:S(2)}, u32[]{:S(2)}) %collective-permute-start.9) | collective-permute-done | bytes 458784 | tf_op jit(solution)/shard_map/ppermute | solution.py:570
  51.8 1.5 %collective-permute-done.10.lower_ref = bf16[112,2048]{1,0:T(8,128)(2,1)} collective-permute-done((bf16[112,2048]{1,0:T(8,128)(2,1)}, bf16[112,2048]{1,0:T(8,128)(2,1)}, u32[]{:S(2)}, u32[]{:S(2)}) %collective-permute-start.10) | collective-permute-done | bytes 458784 | tf_op jit(solution)/shard_map/ppermute | solution.py:570
  53.3 2.9 %merge_other.1 = (bf16[112,1024]{1,0:T(8,128)(2,1)S(1)}, bf16[112,1024]{1,0:T(8,128)(2,1)S(1)}) custom-call(s32[2]{0:T(128)S(1)} %pad_add_fusion.place_ref, bf16[112,2048]{1,0:T(8,128)(2,1)} %collective-permute-done.9.upper_ref, bf16[112,2048]{1,0:T(8,128)(2,1)} %collective-permute-done.10.lower_ref, bf16[4096,256]{1,0:T(8,128)(2,1)S(1)} %get-tuple-element.67.refs_0_, ...), custom_call_target="tpu_custom_call" | custom-call | flops 939524096 | bytes 1048576 | tf_op jit(solution)/shard_map/merge_other/pallas_call | solution.py:483
  56.1 0.3 collective-permute-start.11
  56.5 1.7 %collective-permute-start.12 = (bf16[112,1024]{1,0:T(8,128)(2,1)S(1)}, bf16[112,1024]{1,0:T(8,128)(2,1)S(1)}, u32[]{:S(2)}, u32[]{:S(2)}) collective-permute-start(bf16[112,1024]{1,0:T(8,128)(2,1)S(1)} %get-tuple-element.74), channel_id=1, source_target_pairs={{0,2},{1,3},{2,0},{3,1},{4,6},{5,7},{6,4},{7,5},{8,10},{9,11},{10,... | collective-permute-start | bytes 688136 | tf_op jit(solution)/shard_map/ppermute | solution.py:570
  58.2 4.8 %collective-permute-done.11.from_y_ref = bf16[112,1024]{1,0:T(8,128)(2,1)S(1)} collective-permute-done((bf16[112,1024]{1,0:T(8,128)(2,1)S(1)}, bf16[112,1024]{1,0:T(8,128)(2,1)S(1)}, u32[]{:S(2)}, u32[]{:S(2)}) %collective-permute-start.11) | collective-permute-done | bytes 229408 | tf_op jit(solution)/shard_map/ppermute | solution.py:570
  63.0 0.4 collective-permute-done.12.from_x_ref
  63.4 0.6 combine.1.mine_ref
  64.1 0.1 collective-permute-start.15
  64.1 1.3 %collective-permute-start.13 = (bf16[112,2048]{1,0:T(8,128)(2,1)S(1)}, bf16[112,2048]{1,0:T(8,128)(2,1)S(1)}, u32[]{:S(2)}, u32[]{:S(2)}) collective-permute-start(bf16[112,2048]{1,0:T(8,128)(2,1)S(1)} %combine.1.mine_ref), channel_id=1, source_target_pairs={{0,2},{1,5},{2,0},{3,7},{4,6},{5,1},{6,4},{7,3},{8,10},{9,13},{10,... | collective-permute-start | bytes 1376264 | tf_op jit(solution)/shard_map/ppermute | solution.py:575
  65.5 1.4 %collective-permute-start.14 = (bf16[112,2048]{1,0:T(8,128)(2,1)S(1)}, bf16[112,2048]{1,0:T(8,128)(2,1)S(1)}, u32[]{:S(2)}, u32[]{:S(2)}) collective-permute-start(bf16[112,2048]{1,0:T(8,128)(2,1)S(1)} %combine.1.mine_ref), channel_id=1, source_target_pairs={{0,4},{1,3},{2,6},{3,1},{4,0},{5,7},{6,2},{7,5},{8,12},{9,11},{10,... | collective-permute-start | bytes 1376264 | tf_op jit(solution)/shard_map/ppermute | solution.py:575
  66.9 2.6 %feed_forward.4 = (bf16[112,2048]{1,0:T(8,128)(2,1)S(1)}, bf16[112,1024]{1,0:T(8,128)(2,1)S(1)}, bf16[112,1024]{1,0:T(8,128)(2,1)S(1)}) custom-call(bf16[112,2048]{1,0:T(8,128)(2,1)S(1)} %combine.1.mine_ref, bf16[112,2048]{1,0:T(8,128)(2,1)S(1)} %collective-permute-done.15.theirs_ref, bf16[2048,1024]{1,0:T(8,128)(2,1)S(1)} %copy-done, ...), custom_call_target="tpu_custom_call" | custom-call | flops 1879048192 | bytes 8388608 | tf_op jit(solution)/shard_map/feed_forward/pallas_call | solution.py:541
  69.5 7.6 %collective-permute-done.13.mine_ref = bf16[112,2048]{1,0:T(8,128)(2,1)S(1)} collective-permute-done((bf16[112,2048]{1,0:T(8,128)(2,1)S(1)}, bf16[112,2048]{1,0:T(8,128)(2,1)S(1)}, u32[]{:S(2)}, u32[]{:S(2)}) %collective-permute-start.13) | collective-permute-done | bytes 458784 | tf_op jit(solution)/shard_map/ppermute | solution.py:575
  77.1 0.3 collective-permute-start.20
  77.4 0.2 collective-permute-start.19
  77.7 0.3 collective-permute-start.18
  77.9 1.4 %collective-permute-start.16 = (bf16[112,2048]{1,0:T(8,128)(2,1)S(1)}, bf16[112,2048]{1,0:T(8,128)(2,1)S(1)}, u32[]{:S(2)}, u32[]{:S(2)}) collective-permute-start(bf16[112,2048]{1,0:T(8,128)(2,1)S(1)} %collective-permute-done.13.mine_ref), channel_id=1, source_target_pairs={{0,4},{1,3},{2,6},{3,1},{4,0},{5,7},{6,2},{7,5},{8,12},{9,11},{10,... | collective-permute-start | bytes 1376264 | tf_op jit(solution)/shard_map/ppermute | solution.py:575
  79.3 2.6 %feed_forward.5 = (bf16[112,2048]{1,0:T(8,128)(2,1)S(1)}, bf16[112,1024]{1,0:T(8,128)(2,1)S(1)}, bf16[112,1024]{1,0:T(8,128)(2,1)S(1)}) custom-call(bf16[112,2048]{1,0:T(8,128)(2,1)S(1)} %collective-permute-done.13.mine_ref, bf16[112,2048]{1,0:T(8,128)(2,1)S(1)} %collective-permute-done.20.theirs_ref, bf16[2048,1024]{1,0:T(8,128)(2,1)S(1)} %copy-done, ...), custom_call_target="tpu_custom_call" | custom-call | flops 1879048192 | bytes 8388608 | tf_op jit(solution)/shard_map/feed_forward/pallas_call | solution.py:541
  81.9 0.6 collective-permute-start.22
  82.5 0.1 collective-permute-start.21
  82.6 0.1 add_convert_fusion.4
  82.7 2.6 %feed_forward.6 = (bf16[112,2048]{1,0:T(8,128)(2,1)S(1)}, bf16[112,1024]{1,0:T(8,128)(2,1)S(1)}, bf16[112,1024]{1,0:T(8,128)(2,1)S(1)}) custom-call(bf16[112,2048]{1,0:T(8,128)(2,1)S(1)} %collective-permute-done.14.mine_ref, bf16[112,2048]{1,0:T(8,128)(2,1)S(1)} %collective-permute-done.23.theirs_ref, bf16[2048,1024]{1,0:T(8,128)(2,1)S(1)} %copy-done, ...), custom_call_target="tpu_custom_call" | custom-call | flops 1879048192 | bytes 8388608 | tf_op jit(solution)/shard_map/feed_forward/pallas_call | solution.py:541
  85.4 0.5 collective-permute-start.25
  85.9 0.1 collective-permute-start.24
  85.9 0.5 collective-permute-done.16.mine_ref
  86.4 0.1 add_convert_fusion.3
  86.5 0.4 collective-permute-done.25
  87.0 0.4 collective-permute-done.24
  87.3 0.1 add_convert_fusion.2
  87.5 0.8 collective-permute-done.17.theirs_ref
  88.2 1.3 %collective-permute-start.28 = (bf16[112,2048]{1,0:T(8,128)(2,1)S(1)}, bf16[112,2048]{1,0:T(8,128)(2,1)S(1)}, u32[]{:S(2)}, u32[]{:S(2)}) collective-permute-start(bf16[112,2048]{1,0:T(8,128)(2,1)S(1)} %add_convert_fusion.3), channel_id=1, source_target_pairs={{0,2},{1,5},{2,0},{3,7},{4,6},{5,1},{6,4},{7,3},{8,10},{9,13},{10,... | collective-permute-start | bytes 1376264 | tf_op jit(solution)/shard_map/ppermute | solution.py:575
  89.5 1.4 %collective-permute-start.29 = (bf16[112,2048]{1,0:T(8,128)(2,1)S(1)}, bf16[112,2048]{1,0:T(8,128)(2,1)S(1)}, u32[]{:S(2)}, u32[]{:S(2)}) collective-permute-start(bf16[112,2048]{1,0:T(8,128)(2,1)S(1)} %add_convert_fusion.2), channel_id=1, source_target_pairs={{0,4},{1,3},{2,6},{3,1},{4,0},{5,7},{6,2},{7,5},{8,12},{9,11},{10,... | collective-permute-start | bytes 1376264 | tf_op jit(solution)/shard_map/ppermute | solution.py:575
  90.9 2.6 %feed_forward.7 = (bf16[112,2048]{1,0:T(8,128)(2,1)S(1)}, bf16[112,1024]{1,0:T(8,128)(2,1)S(1)}, bf16[112,1024]{1,0:T(8,128)(2,1)S(1)}) custom-call(bf16[112,2048]{1,0:T(8,128)(2,1)S(1)} %collective-permute-done.16.mine_ref, bf16[112,2048]{1,0:T(8,128)(2,1)S(1)} %collective-permute-done.17.theirs_ref, bf16[2048,1024]{1,0:T(8,128)(2,1)S(1)} %copy-done, ...), custom_call_target="tpu_custom_call" | custom-call | flops 1879048192 | bytes 8388608 | tf_op jit(solution)/shard_map/feed_forward/pallas_call | solution.py:541
  93.5 0.1 collective-permute-start.26
  93.6 0.5 collective-permute-start.27
  94.1 1.0 collective-permute-done.26
  95.1 0.3 collective-permute-done.27
  95.4 5.9 %collective-permute-done.28 = bf16[112,2048]{1,0:T(8,128)(2,1)S(1)} collective-permute-done((bf16[112,2048]{1,0:T(8,128)(2,1)S(1)}, bf16[112,2048]{1,0:T(8,128)(2,1)S(1)}, u32[]{:S(2)}, u32[]{:S(2)}) %collective-permute-start.28) | collective-permute-done | bytes 458784 | tf_op jit(solution)/shard_map/ppermute | solution.py:575
  101.3 0.1 add_convert_fusion.1
  101.5 2.0 %collective-permute-start.30 = (bf16[112,2048]{1,0:T(8,128)(2,1)S(1)}, bf16[112,2048]{1,0:T(8,128)(2,1)S(1)}, u32[]{:S(2)}, u32[]{:S(2)}) collective-permute-start(bf16[112,2048]{1,0:T(8,128)(2,1)S(1)} %add_convert_fusion.1), channel_id=1, source_target_pairs={{0,6},{1,7},{2,4},{3,5},{4,2},{5,3},{6,0},{7,1},{8,14},{9,15},{10,... | collective-permute-start | bytes 1376264 | tf_op jit(solution)/shard_map/ppermute | solution.py:570
  103.4 11.5 %collective-permute-done.30 = bf16[112,2048]{1,0:T(8,128)(2,1)S(1)} collective-permute-done((bf16[112,2048]{1,0:T(8,128)(2,1)S(1)}, bf16[112,2048]{1,0:T(8,128)(2,1)S(1)}, u32[]{:S(2)}, u32[]{:S(2)}) %collective-permute-start.30) | collective-permute-done | bytes 458784 | tf_op jit(solution)/shard_map/ppermute | solution.py:570
  115.0 0.4 add_convert_fusion
  115.3 0.9 reshape.45
  (56 shorter events, 0.2 us)
Async XLA Ops:
  0.6 41.8 %collective-permute-start.4 = (bf16[4096,256]{1,0:T(8,128)(2,1)}, bf16[4096,256]{1,0:T(8,128)(2,1)}, u32[]{:S(2)}, u32[]{:S(2)}) collective-permute-start(bf16[4096,256]{1,0:T(8,128)(2,1)} %refs_0_.1), channel_id=1, source_target_pairs={{0,1},{1,0},{2,3},{3,2},{4,5},{5,4},{6,7},{7,6},{8,9},{9,8},{10,11... | collective-permute-start | bytes 6291464 | tf_op jit(solution)/shard_map/ppermute | solution.py:565
  1.1 1.2 %copy-start.3 = (bf16[18,24,1024]{2,1,0:T(8,128)(2,1)S(1)}, bf16[18,24,1024]{2,1,0:T(8,128)(2,1)}, u32[]{:S(2)}) copy-start(bf16[18,24,1024]{2,1,0:T(8,128)(2,1)} %tokens_ref.5) | copy-start | bytes 2654212
  2.3 7.8 %copy-start.4 = (bf16[18,24,1024]{2,1,0:T(8,128)(2,1)S(1)}, bf16[18,24,1024]{2,1,0:T(8,128)(2,1)}, u32[]{:S(2)}) copy-start(bf16[18,24,1024]{2,1,0:T(8,128)(2,1)} %tokens_ref.5) | copy-start | bytes 2654212
  5.3 11.1 %collective-permute-start.1 = (bf16[18,8,1024]{2,1,0:T(8,128)(2,1)S(1)}, bf16[18,8,1024]{2,1,0:T(8,128)(2,1)S(1)}, u32[]{:S(2)}, u32[]{:S(2)}) collective-permute-start(bf16[18,8,1024]{2,1,0:T(8,128)(2,1)S(1)} %get-tuple-element.52), channel_id=1, source_target_pairs={{0,7},{1,0},{2,1},{3,2},{4,3},{5,4},{6,5},{7,6},{8,15},{9,8},{10,9... | collective-permute-start | bytes 884744 | tf_op jit(solution)/shard_map/ppermute | solution.py:405
  8.9 10.3 %collective-permute-start = (bf16[18,8,1024]{2,1,0:T(8,128)(2,1)S(1)}, bf16[18,8,1024]{2,1,0:T(8,128)(2,1)S(1)}, u32[]{:S(2)}, u32[]{:S(2)}) collective-permute-start(bf16[18,8,1024]{2,1,0:T(8,128)(2,1)S(1)} %get-tuple-element.51), channel_id=1, source_target_pairs={{0,1},{1,2},{2,3},{3,4},{4,5},{5,6},{6,7},{7,0},{8,9},{9,10},{10,1... | collective-permute-start | bytes 884744 | tf_op jit(solution)/shard_map/ppermute | solution.py:405
  8.9 28.8 %collective-permute-start.5 = (bf16[2048,256]{1,0:T(8,128)(2,1)}, bf16[2048,256]{1,0:T(8,128)(2,1)}, u32[]{:S(2)}, u32[]{:S(2)}) collective-permute-start(bf16[2048,256]{1,0:T(8,128)(2,1)} %get-tuple-element.60), channel_id=1, source_target_pairs={{0,2},{1,3},{2,0},{3,1},{4,6},{5,7},{6,4},{7,5},{8,10},{9,11},{10,... | collective-permute-start | bytes 3145736 | tf_op jit(solution)/shard_map/ppermute | solution.py:570
  8.9 29.0 %collective-permute-start.6 = (bf16[2048,256]{1,0:T(8,128)(2,1)}, bf16[2048,256]{1,0:T(8,128)(2,1)}, u32[]{:S(2)}, u32[]{:S(2)}) collective-permute-start(bf16[2048,256]{1,0:T(8,128)(2,1)} %get-tuple-element.61), channel_id=1, source_target_pairs={{0,4},{1,5},{2,6},{3,7},{4,0},{5,1},{6,2},{7,3},{8,12},{9,13},{10,... | collective-permute-start | bytes 3145736 | tf_op jit(solution)/shard_map/ppermute | solution.py:570
  10.1 14.1 %copy-start.7 = (bf16[576,144]{1,0:T(8,128)(2,1)S(1)}, bf16[576,144]{1,0:T(8,128)(2,1)}, u32[]{:S(2)}) copy-start(bf16[576,144]{1,0:T(8,128)(2,1)} %constant.71.clone.rest_1_) | copy-start | bytes 497668
  10.1 14.1 %copy-start.8 = (bf16[576,256]{1,0:T(8,128)(2,1)S(1)}, bf16[576,256]{1,0:T(8,128)(2,1)}, u32[]{:S(2)}) copy-start(bf16[576,256]{1,0:T(8,128)(2,1)} %constant.72.clone.rest_2_) | copy-start | bytes 884740
  10.1 14.1 %copy-start.9 = (bf16[144,576]{1,0:T(8,128)(2,1)S(1)}, bf16[144,576]{1,0:T(8,128)(2,1)}, u32[]{:S(2)}) copy-start(bf16[144,576]{1,0:T(8,128)(2,1)} %constant.73.clone.rest_3_) | copy-start | bytes 497668
  10.2 14.1 %copy-start.13 = (bf16[240,240]{1,0:T(8,128)(2,1)S(1)}, bf16[240,240]{1,0:T(8,128)(2,1)}, u32[]{:S(2)}) copy-start(bf16[240,240]{1,0:T(8,128)(2,1)} %constant.70.clone.rest_0_) | copy-start | bytes 345604
  19.2 10.2 %collective-permute-start.2 = (bf16[3,40,1024]{2,1,0:T(8,128)(2,1)S(1)}, bf16[3,40,1024]{2,1,0:T(8,128)(2,1)S(1)}, u32[]{:S(2)}, u32[]{:S(2)}) collective-permute-start(bf16[3,40,1024]{2,1,0:T(8,128)(2,1)S(1)} %pad_maximum_fusion), channel_id=1, source_target_pairs={{0,8},{8,16},{16,24},{1,9},{9,17},{17,25},{2,10},{10,18},{18,26},{... | collective-permute-start | bytes 737288 | tf_op jit(solution)/shard_map/ppermute | solution.py:405
  22.8 8.1 %collective-permute-start.3 = (bf16[3,40,1024]{2,1,0:T(8,128)(2,1)S(1)}, bf16[3,40,1024]{2,1,0:T(8,128)(2,1)S(1)}, u32[]{:S(2)}, u32[]{:S(2)}) collective-permute-start(bf16[3,40,1024]{2,1,0:T(8,128)(2,1)S(1)} %pad_maximum_fusion.1), channel_id=1, source_target_pairs={{8,0},{16,8},{24,16},{9,1},{17,9},{25,17},{10,2},{18,10},{26,18},{... | collective-permute-start | bytes 737288 | tf_op jit(solution)/shard_map/ppermute | solution.py:405
  24.3 6.6 %copy-start.5 = (bf16[1024,1024]{1,0:T(8,128)(2,1)S(1)}, bf16[1024,1024]{1,0:T(8,128)(2,1)}, u32[]{:S(2)}) copy-start(bf16[1024,1024]{1,0:T(8,128)(2,1)} %out_w_ref.1) | copy-start | bytes 6291460
  24.3 6.6 %copy-start.6 = (bf16[448,432]{1,0:T(8,128)(2,1)S(1)}, bf16[448,432]{1,0:T(8,128)(2,1)}, u32[]{:S(2)}) copy-start(bf16[448,432]{1,0:T(8,128)(2,1)} %constant.74.clone.patch_ref) | copy-start | bytes 1161220
  24.3 6.6 %copy-start.10 = (bf16[304,256]{1,0:T(8,128)(2,1)S(1)}, bf16[304,256]{1,0:T(8,128)(2,1)}, u32[]{:S(2)}) copy-start(bf16[304,256]{1,0:T(8,128)(2,1)} %constant.77.clone.rest_2_.rest_6_) | copy-start | bytes 466948
  24.3 6.5 %copy-start.11 = (bf16[240,256]{1,0:T(8,128)(2,1)S(1)}, bf16[240,256]{1,0:T(8,128)(2,1)}, u32[]{:S(2)}) copy-start(bf16[240,256]{1,0:T(8,128)(2,1)} %constant.75.clone.rest_0_) | copy-start | bytes 368644
  24.3 6.5 %copy-start.12 = (bf16[240,256]{1,0:T(8,128)(2,1)S(1)}, bf16[240,256]{1,0:T(8,128)(2,1)}, u32[]{:S(2)}) copy-start(bf16[240,256]{1,0:T(8,128)(2,1)} %constant.79.clone.rest_4_) | copy-start | bytes 368644
  24.3 6.5 %copy-start.14 = (bf16[304,80]{1,0:T(8,128)(2,1)S(1)}, bf16[304,80]{1,0:T(8,128)(2,1)}, u32[]{:S(2)}) copy-start(bf16[304,80]{1,0:T(8,128)(2,1)} %constant.76.clone.rest_1_.rest_5_) | copy-start | bytes 145924
  24.4 6.5 %copy-start.15 = (bf16[80,304]{1,0:T(8,128)(2,1)S(1)}, bf16[80,304]{1,0:T(8,128)(2,1)}, u32[]{:S(2)}) copy-start(bf16[80,304]{1,0:T(8,128)(2,1)} %constant.78.clone.rest_3_.rest_7_) | copy-start | bytes 145924
  30.9 11.6 %copy-start.2 = (bf16[4096,256]{1,0:T(8,128)(2,1)S(1)}, bf16[4096,256]{1,0:T(8,128)(2,1)}, u32[]{:S(2)}) copy-start(bf16[4096,256]{1,0:T(8,128)(2,1)} %refs_0_.1) | copy-start | bytes 6291460
  38.0 4.5 %collective-permute-start.7 = (bf16[2048,256]{1,0:T(8,128)(2,1)}, bf16[2048,256]{1,0:T(8,128)(2,1)S(1)}, u32[]{:S(2)}, u32[]{:S(2)}) collective-permute-start(bf16[2048,256]{1,0:T(8,128)(2,1)} %collective-permute-done.5.refs_2_), channel_id=1, source_target_pairs={{0,1},{1,0},{2,3},{3,2},{4,5},{5,4},{6,7},{7,6},{8,9},{9,8},{10,11... | collective-permute-start | bytes 3145736 | tf_op jit(solution)/shard_map/ppermute | solution.py:565
  38.3 4.2 %collective-permute-start.8 = (bf16[2048,256]{1,0:T(8,128)(2,1)}, bf16[2048,256]{1,0:T(8,128)(2,1)}, u32[]{:S(2)}, u32[]{:S(2)}) collective-permute-start(bf16[2048,256]{1,0:T(8,128)(2,1)} %collective-permute-done.6.refs_4_), channel_id=1, source_target_pairs={{0,1},{1,0},{2,3},{3,2},{4,5},{5,4},{6,7},{7,6},{8,9},{9,8},{10,11... | collective-permute-start | bytes 3145736 | tf_op jit(solution)/shard_map/ppermute | solution.py:565
  38.5 13.3 %collective-permute-start.9 = (bf16[112,2048]{1,0:T(8,128)(2,1)}, bf16[112,2048]{1,0:T(8,128)(2,1)}, u32[]{:S(2)}, u32[]{:S(2)}) collective-permute-start(bf16[112,2048]{1,0:T(8,128)(2,1)} %get-tuple-element.58.upper_ref), channel_id=1, source_target_pairs={{0,4},{1,5},{2,6},{3,7},{4,0},{5,1},{6,2},{7,3},{8,12},{9,13},{10,... | collective-permute-start | bytes 1376264 | tf_op jit(solution)/shard_map/ppermute | solution.py:570
  40.3 13.0 %collective-permute-start.10 = (bf16[112,2048]{1,0:T(8,128)(2,1)}, bf16[112,2048]{1,0:T(8,128)(2,1)}, u32[]{:S(2)}, u32[]{:S(2)}) collective-permute-start(bf16[112,2048]{1,0:T(8,128)(2,1)} %get-tuple-element.59.lower_ref), channel_id=1, source_target_pairs={{0,2},{1,3},{2,0},{3,1},{4,6},{5,7},{6,4},{7,5},{8,10},{9,11},{10,... | collective-permute-start | bytes 1376264 | tf_op jit(solution)/shard_map/ppermute | solution.py:570
  53.3 13.6 %copy-start = (bf16[2048,1024]{1,0:T(8,128)(2,1)S(1)}, bf16[2048,1024]{1,0:T(8,128)(2,1)}, u32[]{:S(2)}) copy-start(bf16[2048,1024]{1,0:T(8,128)(2,1)} %up_ref.7) | copy-start | bytes 12582916
  53.3 13.6 %copy-start.1 = (bf16[1024,2048]{1,0:T(8,128)(2,1)S(1)}, bf16[1024,2048]{1,0:T(8,128)(2,1)}, u32[]{:S(2)}) copy-start(bf16[1024,2048]{1,0:T(8,128)(2,1)} %down_ref.7) | copy-start | bytes 12582916
  56.1 6.9 %collective-permute-start.11 = (bf16[112,1024]{1,0:T(8,128)(2,1)S(1)}, bf16[112,1024]{1,0:T(8,128)(2,1)S(1)}, u32[]{:S(2)}, u32[]{:S(2)}) collective-permute-start(bf16[112,1024]{1,0:T(8,128)(2,1)S(1)} %get-tuple-element.73), channel_id=1, source_target_pairs={{0,4},{1,5},{2,6},{3,7},{4,0},{5,1},{6,2},{7,3},{8,12},{9,13},{10,... | collective-permute-start | bytes 688136 | tf_op jit(solution)/shard_map/ppermute | solution.py:570
  56.5 7.0 %collective-permute-start.12 = (bf16[112,1024]{1,0:T(8,128)(2,1)S(1)}, bf16[112,1024]{1,0:T(8,128)(2,1)S(1)}, u32[]{:S(2)}, u32[]{:S(2)}) collective-permute-start(bf16[112,1024]{1,0:T(8,128)(2,1)S(1)} %get-tuple-element.74), channel_id=1, source_target_pairs={{0,2},{1,3},{2,0},{3,1},{4,6},{5,7},{6,4},{7,5},{8,10},{9,11},{10,... | collective-permute-start | bytes 688136 | tf_op jit(solution)/shard_map/ppermute | solution.py:570
  64.1 2.8 %collective-permute-start.15 = (bf16[112,2048]{1,0:T(8,128)(2,1)S(1)}, bf16[112,2048]{1,0:T(8,128)(2,1)S(1)}, u32[]{:S(2)}, u32[]{:S(2)}) collective-permute-start(bf16[112,2048]{1,0:T(8,128)(2,1)S(1)} %combine.1.mine_ref), channel_id=1, source_target_pairs={{0,1},{1,0},{2,3},{3,2},{4,5},{5,4},{6,7},{7,6},{8,9},{9,8},{10,11... | collective-permute-start | bytes 1376264 | tf_op jit(solution)/shard_map/ppermute | solution.py:565
  64.1 13.0 %collective-permute-start.13 = (bf16[112,2048]{1,0:T(8,128)(2,1)S(1)}, bf16[112,2048]{1,0:T(8,128)(2,1)S(1)}, u32[]{:S(2)}, u32[]{:S(2)}) collective-permute-start(bf16[112,2048]{1,0:T(8,128)(2,1)S(1)} %combine.1.mine_ref), channel_id=1, source_target_pairs={{0,2},{1,5},{2,0},{3,7},{4,6},{5,1},{6,4},{7,3},{8,10},{9,13},{10,... | collective-permute-start | bytes 1376264 | tf_op jit(solution)/shard_map/ppermute | solution.py:575
  65.5 11.7 %collective-permute-start.14 = (bf16[112,2048]{1,0:T(8,128)(2,1)S(1)}, bf16[112,2048]{1,0:T(8,128)(2,1)S(1)}, u32[]{:S(2)}, u32[]{:S(2)}) collective-permute-start(bf16[112,2048]{1,0:T(8,128)(2,1)S(1)} %combine.1.mine_ref), channel_id=1, source_target_pairs={{0,4},{1,3},{2,6},{3,1},{4,0},{5,7},{6,2},{7,5},{8,12},{9,11},{10,... | collective-permute-start | bytes 1376264 | tf_op jit(solution)/shard_map/ppermute | solution.py:575
  77.1 2.2 %collective-permute-start.20 = (bf16[112,2048]{1,0:T(8,128)(2,1)S(1)}, bf16[112,2048]{1,0:T(8,128)(2,1)S(1)}, u32[]{:S(2)}, u32[]{:S(2)}) collective-permute-start(bf16[112,2048]{1,0:T(8,128)(2,1)S(1)} %collective-permute-done.13.mine_ref), channel_id=1, source_target_pairs={{0,1},{1,0},{2,3},{3,2},{4,5},{5,4},{6,7},{7,6},{8,9},{9,8},{10,11... | collective-permute-start | bytes 1376264 | tf_op jit(solution)/shard_map/ppermute | solution.py:565
  77.4 5.1 %collective-permute-start.19 = (bf16[112,1024]{1,0:T(8,128)(2,1)S(1)}, bf16[112,1024]{1,0:T(8,128)(2,1)S(1)}, u32[]{:S(2)}, u32[]{:S(2)}) collective-permute-start(bf16[112,1024]{1,0:T(8,128)(2,1)S(1)} %get-tuple-element.81), channel_id=1, source_target_pairs={{0,1},{1,0},{2,3},{3,2},{4,5},{5,4},{6,7},{7,6},{8,9},{9,8},{10,11... | collective-permute-start | bytes 688136 | tf_op jit(solution)/shard_map/ppermute | solution.py:565
  77.7 5.0 %collective-permute-start.18 = (bf16[112,1024]{1,0:T(8,128)(2,1)S(1)}, bf16[112,1024]{1,0:T(8,128)(2,1)S(1)}, u32[]{:S(2)}, u32[]{:S(2)}) collective-permute-start(bf16[112,1024]{1,0:T(8,128)(2,1)S(1)} %get-tuple-element.80), channel_id=1, source_target_pairs={{0,1},{1,0},{2,3},{3,2},{4,5},{5,4},{6,7},{7,6},{8,9},{9,8},{10,11... | collective-permute-start | bytes 688136 | tf_op jit(solution)/shard_map/ppermute | solution.py:565
  77.9 8.5 %collective-permute-start.16 = (bf16[112,2048]{1,0:T(8,128)(2,1)S(1)}, bf16[112,2048]{1,0:T(8,128)(2,1)S(1)}, u32[]{:S(2)}, u32[]{:S(2)}) collective-permute-start(bf16[112,2048]{1,0:T(8,128)(2,1)S(1)} %collective-permute-done.13.mine_ref), channel_id=1, source_target_pairs={{0,4},{1,3},{2,6},{3,1},{4,0},{5,7},{6,2},{7,5},{8,12},{9,11},{10,... | collective-permute-start | bytes 1376264 | tf_op jit(solution)/shard_map/ppermute | solution.py:575
  79.3 3.4 %collective-permute-start.23 = (bf16[112,2048]{1,0:T(8,128)(2,1)S(1)}, bf16[112,2048]{1,0:T(8,128)(2,1)S(1)}, u32[]{:S(2)}, u32[]{:S(2)}) collective-permute-start(bf16[112,2048]{1,0:T(8,128)(2,1)S(1)} %collective-permute-done.14.mine_ref), channel_id=1, source_target_pairs={{0,1},{1,0},{2,3},{3,2},{4,5},{5,4},{6,7},{7,6},{8,9},{9,8},{10,11... | collective-permute-start | bytes 1376264 | tf_op jit(solution)/shard_map/ppermute | solution.py:565
  81.9 4.5 %collective-permute-start.22 = (bf16[112,1024]{1,0:T(8,128)(2,1)S(1)}, bf16[112,1024]{1,0:T(8,128)(2,1)S(1)}, u32[]{:S(2)}, u32[]{:S(2)}) collective-permute-start(bf16[112,1024]{1,0:T(8,128)(2,1)S(1)} %get-tuple-element.84), channel_id=1, source_target_pairs={{0,1},{1,0},{2,3},{3,2},{4,5},{5,4},{6,7},{7,6},{8,9},{9,8},{10,11... | collective-permute-start | bytes 688136 | tf_op jit(solution)/shard_map/ppermute | solution.py:565
  82.5 3.9 %collective-permute-start.21 = (bf16[112,1024]{1,0:T(8,128)(2,1)S(1)}, bf16[112,1024]{1,0:T(8,128)(2,1)S(1)}, u32[]{:S(2)}, u32[]{:S(2)}) collective-permute-start(bf16[112,1024]{1,0:T(8,128)(2,1)S(1)} %get-tuple-element.83), channel_id=1, source_target_pairs={{0,1},{1,0},{2,3},{3,2},{4,5},{5,4},{6,7},{7,6},{8,9},{9,8},{10,11... | collective-permute-start | bytes 688136 | tf_op jit(solution)/shard_map/ppermute | solution.py:565
  85.4 1.6 %collective-permute-start.25 = (bf16[112,1024]{1,0:T(8,128)(2,1)S(1)}, bf16[112,1024]{1,0:T(8,128)(2,1)S(1)}, u32[]{:S(2)}, u32[]{:S(2)}) collective-permute-start(bf16[112,1024]{1,0:T(8,128)(2,1)S(1)} %get-tuple-element.88), channel_id=1, source_target_pairs={{0,1},{1,0},{2,3},{3,2},{4,5},{5,4},{6,7},{7,6},{8,9},{9,8},{10,11... | collective-permute-start | bytes 688136 | tf_op jit(solution)/shard_map/ppermute | solution.py:565
  85.9 1.5 %collective-permute-start.24 = (bf16[112,1024]{1,0:T(8,128)(2,1)S(1)}, bf16[112,1024]{1,0:T(8,128)(2,1)S(1)}, u32[]{:S(2)}, u32[]{:S(2)}) collective-permute-start(bf16[112,1024]{1,0:T(8,128)(2,1)S(1)} %get-tuple-element.87), channel_id=1, source_target_pairs={{0,1},{1,0},{2,3},{3,2},{4,5},{5,4},{6,7},{7,6},{8,9},{9,8},{10,11... | collective-permute-start | bytes 688136 | tf_op jit(solution)/shard_map/ppermute | solution.py:565
  86.4 1.8 %collective-permute-start.17 = (bf16[112,2048]{1,0:T(8,128)(2,1)S(1)}, bf16[112,2048]{1,0:T(8,128)(2,1)S(1)}, u32[]{:S(2)}, u32[]{:S(2)}) collective-permute-start(bf16[112,2048]{1,0:T(8,128)(2,1)S(1)} %collective-permute-done.16.mine_ref), channel_id=1, source_target_pairs={{0,1},{1,0},{2,3},{3,2},{4,5},{5,4},{6,7},{7,6},{8,9},{9,8},{10,11... | collective-permute-start | bytes 1376264 | tf_op jit(solution)/shard_map/ppermute | solution.py:565
  88.2 13.1 %collective-permute-start.28 = (bf16[112,2048]{1,0:T(8,128)(2,1)S(1)}, bf16[112,2048]{1,0:T(8,128)(2,1)S(1)}, u32[]{:S(2)}, u32[]{:S(2)}) collective-permute-start(bf16[112,2048]{1,0:T(8,128)(2,1)S(1)} %add_convert_fusion.3), channel_id=1, source_target_pairs={{0,2},{1,5},{2,0},{3,7},{4,6},{5,1},{6,4},{7,3},{8,10},{9,13},{10,... | collective-permute-start | bytes 1376264 | tf_op jit(solution)/shard_map/ppermute | solution.py:575
  89.5 11.9 %collective-permute-start.29 = (bf16[112,2048]{1,0:T(8,128)(2,1)S(1)}, bf16[112,2048]{1,0:T(8,128)(2,1)S(1)}, u32[]{:S(2)}, u32[]{:S(2)}) collective-permute-start(bf16[112,2048]{1,0:T(8,128)(2,1)S(1)} %add_convert_fusion.2), channel_id=1, source_target_pairs={{0,4},{1,3},{2,6},{3,1},{4,0},{5,7},{6,2},{7,5},{8,12},{9,11},{10,... | collective-permute-start | bytes 1376264 | tf_op jit(solution)/shard_map/ppermute | solution.py:575
  93.5 1.6 %collective-permute-start.26 = (bf16[112,1024]{1,0:T(8,128)(2,1)S(1)}, bf16[112,1024]{1,0:T(8,128)(2,1)S(1)}, u32[]{:S(2)}, u32[]{:S(2)}) collective-permute-start(bf16[112,1024]{1,0:T(8,128)(2,1)S(1)} %get-tuple-element.91), channel_id=1, source_target_pairs={{0,1},{1,0},{2,3},{3,2},{4,5},{5,4},{6,7},{7,6},{8,9},{9,8},{10,11... | collective-permute-start | bytes 688136 | tf_op jit(solution)/shard_map/ppermute | solution.py:565
  93.6 1.8 %collective-permute-start.27 = (bf16[112,1024]{1,0:T(8,128)(2,1)S(1)}, bf16[112,1024]{1,0:T(8,128)(2,1)S(1)}, u32[]{:S(2)}, u32[]{:S(2)}) collective-permute-start(bf16[112,1024]{1,0:T(8,128)(2,1)S(1)} %get-tuple-element.92), channel_id=1, source_target_pairs={{0,1},{1,0},{2,3},{3,2},{4,5},{5,4},{6,7},{7,6},{8,9},{9,8},{10,11... | collective-permute-start | bytes 688136 | tf_op jit(solution)/shard_map/ppermute | solution.py:565
  101.5 13.5 %collective-permute-start.30 = (bf16[112,2048]{1,0:T(8,128)(2,1)S(1)}, bf16[112,2048]{1,0:T(8,128)(2,1)S(1)}, u32[]{:S(2)}, u32[]{:S(2)}) collective-permute-start(bf16[112,2048]{1,0:T(8,128)(2,1)S(1)} %add_convert_fusion.1), channel_id=1, source_target_pairs={{0,6},{1,7},{2,4},{3,5},{4,2},{5,3},{6,0},{7,1},{8,14},{9,15},{10,... | collective-permute-start | bytes 1376264 | tf_op jit(solution)/shard_map/ppermute | solution.py:570

commit v7 on v6

--- a/solution.py
+++ b/solution.py
@@ -552,8 +552,9 @@
     )(mine, theirs, up, down)
 
 
-def added(mine, low, high):
-    return (mine.astype(F32) + jnp.concatenate([low, high], axis=1).astype(F32)).astype(BF16)
+def added(mine, low, high, more=None):
+    total = mine.astype(F32) + jnp.concatenate([low, high], axis=1).astype(F32)
+    return (total if more is None else total + more.astype(F32)).astype(BF16)
 
 
 def summed(mine, low, high):
@@ -578,19 +579,18 @@
 def coarse_by_squares(upper, lower, merge_weight, halves, up, down):
     own = merge_by_squares(upper, lower, merge_weight, halves)
     near = cross(own, 1, 2)
-    next_near = cross(own, 2, 1)
     first = feed_forward(own, core_swap(own), up, down)
-    near, next_near, *first = lax.optimization_barrier((near, next_near, *first))
+    near, *first = lax.optimization_barrier((near, *first))
     far = cross(near, 2, 1)
-    sums = [summed(*first)]
-    for chunk in (near, next_near):
-        sums.append(summed(*feed_forward(chunk, core_swap(chunk), up, down)))
-    pair, *sums = lax.optimization_barrier((core_swap(far), *sums))
-    back = [cross(sums[1], 1, 2), cross(sums[2], 2, 1)]
-    mine, low, high = feed_forward(far, pair, up, down)
-    low, high, *back = lax.optimization_barrier((core_swap(low), core_swap(high), *back))
-    back.append(chip_swap(added(mine, low, high), 3))
-    return sum(part.astype(F32) for part in (own, sums[0], *back))
+    near_sums = feed_forward(near, core_swap(near), up, down)
+    later, *near_sums = lax.optimization_barrier((own, *near_sums))
+    other = cross(later, 2, 1)
+    far_sums = feed_forward(far, core_swap(far), up, down)
+    other, *far_sums = lax.optimization_barrier((other, *far_sums))
+    relayed = cross(summed(*far_sums), 2, 1)
+    other_back = cross(summed(*feed_forward(other, core_swap(other), up, down)), 2, 1)
+    near_back = cross(added(*near_sums[:1], core_swap(near_sums[1]), core_swap(near_sums[2]), relayed), 1, 2)
+    return sum(part.astype(F32) for part in (own, summed(*first), other_back, near_back))
 
 
 def coarse_by_chips(upper, lower, merge_weight, halves, up, down):

time: 116 us -> 117 us (level)
  waiting for transfers between devices: 45.1 us -> 47.1 us
    ppermute x5 -> x6, waiting for transfers between devices: 14 us -> 28.7 us  [cross(): lax.ppermute(value, 'lon', [(i, i ^ 2 * (second if i % 2 else first)) for...]
    ppermute x7 -> x6, waiting for transfers between devices: 23.2 us -> 11.6 us  [chip_swap(): lax.ppermute(value, 'lon', [(i, i ^ 2 * offset) for i in range(size)])]
    ppermute x7 -> x6, starting transfers between devices: 9.04 us -> 7.08 us  [chip_swap(): lax.ppermute(value, 'lon', [(i, i ^ 2 * offset) for i in range(size)])]
    ppermute x5 -> x6, starting transfers between devices: 6.81 us -> 8.33 us  [cross(): lax.ppermute(value, 'lon', [(i, i ^ 2 * (second if i % 2 else first)) for...]
  transfers between devices with their start and end apart: 31 -> 31, of which waited for: 17 -> 16; matrix products, arithmetic and copies ran while one was open for 0% -> 1% of each run, Pallas kernels for 30% -> 30%
where the time goes in v7:
time: 117 us
  waiting for transfers between devices  47.1 us (40%)
  Pallas kernels  38.7 us (33%)
  starting transfers between devices  27.2 us (23%)
  local copies, waits for them, and re-layouts  2.2 us (2%)
    ppermute x6, waiting for transfers between devices, cross(): lax.ppermute(value, 'lon', [(i, i ^ 2 * (second if i % 2 else first)) for...  28.7 us
    pallas_call x2, Pallas kernels, vmem_call(): pl.pallas_call(kernel, in_specs=[vmem] * len(args), out_specs=[vmem] * le...  11.8 us
    ppermute x6, waiting for transfers between devices, chip_swap(): lax.ppermute(value, 'lon', [(i, i ^ 2 * offset) for i in range(size)])  11.6 us
    pallas_call x4, Pallas kernels, feed_forward(): pl.pallas_call(ffn_kernel, in_specs=[vmem] * 4, out_specs=[vmem] * 3, out...  10.4 us
    ppermute x4, starting transfers between devices, shift(): return lax.ppermute(part, axis, pairs)  8.58 us
    ppermute x6, starting transfers between devices, cross(): lax.ppermute(value, 'lon', [(i, i ^ 2 * (second if i % 2 else first)) for...  8.33 us
    pallas_call x3, Pallas kernels, local_call(): pl.pallas_call(kernel, in_specs=[pl.BlockSpec(memory_space=pltpu.SMEM)] +...  8.15 us
    ppermute x6, starting transfers between devices, chip_swap(): lax.ppermute(value, 'lon', [(i, i ^ 2 * offset) for i in range(size)])  7.08 us
  transfers between devices with their start and end apart: 31, of which 16 were waited for; matrix products, arithmetic and copies ran while one was open for 1% of the time, Pallas kernels for 30%

profile of v7, /device:TPU:0, one launch (start us, length us, event | category | flops | bytes accessed | tf_op | source)
XLA Modules:
  0.0 117.3 jit_solution(8203048858419694393)
XLA Ops:
  0.6 0.5 collective-permute-start.4
  1.1 1.2 copy-done.3
  2.3 3.0 %prepare.1 = (bf16[18,8,1024]{2,1,0:T(8,128)(2,1)S(1)}, bf16[18,8,1024]{2,1,0:T(8,128)(2,1)S(1)}, bf16[2048,256]{1,0:T(8,128)(2,1)}, bf16[2048,256]{1,0:T(8,128)(2,1)}) custom-call(bf16[18,24,1024]{2,1,0:T(8,128)(2,1)S(1)} %copy-done.3, bf16[4096,256]{1,0:T(8,128)(2,1)} %refs_0_.1), custom_call_target="tpu_custom_call" | custom-call | tf_op jit(solution)/shard_map/prepare/pallas_call | solution.py:169
  5.3 3.6 %collective-permute-start.1 = (bf16[18,8,1024]{2,1,0:T(8,128)(2,1)S(1)}, bf16[18,8,1024]{2,1,0:T(8,128)(2,1)S(1)}, u32[]{:S(2)}, u32[]{:S(2)}) collective-permute-start(bf16[18,8,1024]{2,1,0:T(8,128)(2,1)S(1)} %get-tuple-element.51), channel_id=1, source_target_pairs={{0,7},{1,0},{2,1},{3,2},{4,3},{5,4},{6,5},{7,6},{8,15},{9,8},{10,9... | collective-permute-start | bytes 884744 | tf_op jit(solution)/shard_map/ppermute | solution.py:405
  8.9 1.1 collective-permute-start.6
  10.1 0.0 copy-start.8
  10.1 0.0 copy-start.9
  10.2 0.0 copy-start.13
  10.2 5.4 %own_projection.1 = (bf16[448,3072]{1,0:T(8,128)(2,1)S(1)}, bf16[1024,2048]{1,0:T(8,128)(2,1)S(1)}) custom-call(bf16[18,24,1024]{2,1,0:T(8,128)(2,1)S(1)} %copy-done.4, bf16[1024,3072]{1,0:T(8,128)(2,1)} %weight_ref.3), custom_call_target="tpu_custom_call" | custom-call | flops 2818572288 | bytes 6291456 | tf_op jit(solution)/shard_map/own_projection/pallas_call | solution.py:210
  15.5 0.1 or_select_fusion.bias_ref
  15.6 0.8 collective-permute-done.1.east_ref
  16.4 2.8 %collective-permute-done.west_ref = bf16[18,8,1024]{2,1,0:T(8,128)(2,1)S(1)} collective-permute-done((bf16[18,8,1024]{2,1,0:T(8,128)(2,1)S(1)}, bf16[18,8,1024]{2,1,0:T(8,128)(2,1)S(1)}, u32[]{:S(2)}, u32[]{:S(2)}) %collective-permute-start) | collective-permute-done | bytes 294944 | tf_op jit(solution)/shard_map/ppermute | solution.py:405
  19.2 3.5 %collective-permute-start.2 = (bf16[3,40,1024]{2,1,0:T(8,128)(2,1)S(1)}, bf16[3,40,1024]{2,1,0:T(8,128)(2,1)S(1)}, u32[]{:S(2)}, u32[]{:S(2)}) collective-permute-start(bf16[3,40,1024]{2,1,0:T(8,128)(2,1)S(1)} %pad_maximum_fusion), channel_id=1, source_target_pairs={{0,8},{8,16},{16,24},{1,9},{9,17},{17,25},{2,10},{10,18},{18,26},{... | collective-permute-start | bytes 737288 | tf_op jit(solution)/shard_map/ppermute | solution.py:405
  22.8 1.5 %collective-permute-start.3 = (bf16[3,40,1024]{2,1,0:T(8,128)(2,1)S(1)}, bf16[3,40,1024]{2,1,0:T(8,128)(2,1)S(1)}, u32[]{:S(2)}, u32[]{:S(2)}) collective-permute-start(bf16[3,40,1024]{2,1,0:T(8,128)(2,1)S(1)} %pad_maximum_fusion.1), channel_id=1, source_target_pairs={{8,0},{16,8},{24,16},{9,1},{17,9},{25,17},{10,2},{18,10},{26,18},{... | collective-permute-start | bytes 737288 | tf_op jit(solution)/shard_map/ppermute | solution.py:405
  24.3 0.0 copy-start.6
  24.3 0.0 copy-start.11
  24.4 5.0 %middle_attention.1 = (bf16[288,2048]{1,0:T(8,128)(2,1)S(1)}, bf16[288,1024]{1,0:T(8,128)(2,1)S(1)}) custom-call(bf16[18,8,1024]{2,1,0:T(8,128)(2,1)S(1)} %collective-permute-done.west_ref, bf16[18,8,1024]{2,1,0:T(8,128)(2,1)S(1)} %collective-permute-done.1.east_ref, bf16[448,3072]{1,0:T(8,128)(2,1)S(1)} %get-tuple-element.52.own_ref, ...), custom_call_target="tpu_custom_call" | custom-call | flops 5000000000 | bytes 1048576 | tf_op jit(solution)/shard_map/middle_attention/pallas_call | solution.py:348
  29.4 1.4 %collective-permute-done.3.south_ref = bf16[3,40,1024]{2,1,0:T(8,128)(2,1)S(1)} collective-permute-done((bf16[3,40,1024]{2,1,0:T(8,128)(2,1)S(1)}, bf16[3,40,1024]{2,1,0:T(8,128)(2,1)S(1)}, u32[]{:S(2)}, u32[]{:S(2)}) %collective-permute-start.3) | collective-permute-done | bytes 245792 | tf_op jit(solution)/shard_map/ppermute | solution.py:405
  30.9 6.8 %edge_attention.1 = (bf16[18,24,1024]{2,1,0:T(8,128)(2,1)}, bf16[112,2048]{1,0:T(8,128)(2,1)}, bf16[112,2048]{1,0:T(8,128)(2,1)}) custom-call(bf16[18,24,1024]{2,1,0:T(8,128)(2,1)S(1)} %copy-done.4, bf16[3,40,1024]{2,1,0:T(8,128)(2,1)S(1)} %collective-permute-done.2.north_ref, bf16[3,40,1024]{2,1,0:T(8,128)(2,1)S(1)} %collective-permute-done.3.south_ref, ...), custom_call_target="tpu_custom_call" | custom-call | flops 6000000000 | bytes 1048576 | tf_op jit(solution)/shard_map/edge_attention/pallas_call | solution.py:348
  37.7 0.3 collective-permute-done.6.refs_4_
  38.0 0.3 collective-permute-start.7
  38.3 0.2 collective-permute-start.8
  38.5 1.8 %collective-permute-start.9 = (bf16[112,2048]{1,0:T(8,128)(2,1)}, bf16[112,2048]{1,0:T(8,128)(2,1)}, u32[]{:S(2)}, u32[]{:S(2)}) collective-permute-start(bf16[112,2048]{1,0:T(8,128)(2,1)} %get-tuple-element.57.upper_ref), channel_id=1, source_target_pairs={{0,4},{1,5},{2,6},{3,7},{4,0},{5,1},{6,2},{7,3},{8,12},{9,13},{10,... | collective-permute-start | bytes 1376264 | tf_op jit(solution)/shard_map/ppermute | solution.py:571
  40.3 2.1 %collective-permute-start.10 = (bf16[112,2048]{1,0:T(8,128)(2,1)}, bf16[112,2048]{1,0:T(8,128)(2,1)}, u32[]{:S(2)}, u32[]{:S(2)}) collective-permute-start(bf16[112,2048]{1,0:T(8,128)(2,1)} %get-tuple-element.58.lower_ref), channel_id=1, source_target_pairs={{0,2},{1,3},{2,0},{3,1},{4,6},{5,7},{6,4},{7,5},{8,10},{9,11},{10,... | collective-permute-start | bytes 1376264 | tf_op jit(solution)/shard_map/ppermute | solution.py:571
  42.4 0.1 pad_add_fusion.place_ref
  42.5 4.7 %merge_own.1 = (f32[112,512]{1,0:T(8,128)S(1)}, f32[112,512]{1,0:T(8,128)S(1)}, f32[112,512]{1,0:T(8,128)S(1)}, bf16[4096,256]{1,0:T(8,128)(2,1)S(1)}, bf16[4096...) custom-call(s32[2]{0:T(128)S(1)} %pad_add_fusion.place_ref, ...), custom_call_target="tpu_custom_call" | custom-call | flops 939524096 | bytes 1048576 | tf_op jit(solution)/shard_map/merge_own/pallas_call | solution.py:483
  47.1 4.6 %collective-permute-done.9.upper_ref = bf16[112,2048]{1,0:T(8,128)(2,1)} collective-permute-done((bf16[112,2048]{1,0:T(8,128)(2,1)}, bf16[112,2048]{1,0:T(8,128)(2,1)}, u32[]{:S(2)}, u32[]{:S(2)}) %collective-permute-start.9) | collective-permute-done | bytes 458784 | tf_op jit(solution)/shard_map/ppermute | solution.py:571
  51.8 1.5 %collective-permute-done.10.lower_ref = bf16[112,2048]{1,0:T(8,128)(2,1)} collective-permute-done((bf16[112,2048]{1,0:T(8,128)(2,1)}, bf16[112,2048]{1,0:T(8,128)(2,1)}, u32[]{:S(2)}, u32[]{:S(2)}) %collective-permute-start.10) | collective-permute-done | bytes 458784 | tf_op jit(solution)/shard_map/ppermute | solution.py:571
  53.3 2.9 %merge_other.1 = (bf16[112,1024]{1,0:T(8,128)(2,1)S(1)}, bf16[112,1024]{1,0:T(8,128)(2,1)S(1)}) custom-call(s32[2]{0:T(128)S(1)} %pad_add_fusion.place_ref, bf16[112,2048]{1,0:T(8,128)(2,1)} %collective-permute-done.9.upper_ref, bf16[112,2048]{1,0:T(8,128)(2,1)} %collective-permute-done.10.lower_ref, bf16[4096,256]{1,0:T(8,128)(2,1)S(1)} %get-tuple-element.66.refs_0_, ...), custom_call_target="tpu_custom_call" | custom-call | flops 939524096 | bytes 1048576 | tf_op jit(solution)/shard_map/merge_other/pallas_call | solution.py:483
  56.1 0.3 collective-permute-start.11
  56.5 1.7 %collective-permute-start.12 = (bf16[112,1024]{1,0:T(8,128)(2,1)S(1)}, bf16[112,1024]{1,0:T(8,128)(2,1)S(1)}, u32[]{:S(2)}, u32[]{:S(2)}) collective-permute-start(bf16[112,1024]{1,0:T(8,128)(2,1)S(1)} %get-tuple-element.73), channel_id=1, source_target_pairs={{0,2},{1,3},{2,0},{3,1},{4,6},{5,7},{6,4},{7,5},{8,10},{9,11},{10,... | collective-permute-start | bytes 688136 | tf_op jit(solution)/shard_map/ppermute | solution.py:571
  58.2 4.8 %collective-permute-done.11.from_y_ref = bf16[112,1024]{1,0:T(8,128)(2,1)S(1)} collective-permute-done((bf16[112,1024]{1,0:T(8,128)(2,1)S(1)}, bf16[112,1024]{1,0:T(8,128)(2,1)S(1)}, u32[]{:S(2)}, u32[]{:S(2)}) %collective-permute-start.11) | collective-permute-done | bytes 229408 | tf_op jit(solution)/shard_map/ppermute | solution.py:571
  63.0 0.4 collective-permute-done.12.from_x_ref
  63.4 0.6 combine.1.mine_ref
  64.1 0.1 collective-permute-start.14
  64.1 1.3 %collective-permute-start.13 = (bf16[112,2048]{1,0:T(8,128)(2,1)S(1)}, bf16[112,2048]{1,0:T(8,128)(2,1)S(1)}, u32[]{:S(2)}, u32[]{:S(2)}) collective-permute-start(bf16[112,2048]{1,0:T(8,128)(2,1)S(1)} %combine.1.mine_ref), channel_id=1, source_target_pairs={{0,2},{1,5},{2,0},{3,7},{4,6},{5,1},{6,4},{7,3},{8,10},{9,13},{10,... | collective-permute-start | bytes 1376264 | tf_op jit(solution)/shard_map/ppermute | solution.py:576
  65.5 0.5 collective-permute-done.14.theirs_ref
  65.9 2.6 %feed_forward.4 = (bf16[112,2048]{1,0:T(8,128)(2,1)S(1)}, bf16[112,1024]{1,0:T(8,128)(2,1)S(1)}, bf16[112,1024]{1,0:T(8,128)(2,1)S(1)}) custom-call(bf16[112,2048]{1,0:T(8,128)(2,1)S(1)} %combine.1.mine_ref, bf16[112,2048]{1,0:T(8,128)(2,1)S(1)} %collective-permute-done.14.theirs_ref, bf16[2048,1024]{1,0:T(8,128)(2,1)S(1)} %copy-done, ...), custom_call_target="tpu_custom_call" | custom-call | flops 1879048192 | bytes 8388608 | tf_op jit(solution)/shard_map/feed_forward/pallas_call | solution.py:541
  68.6 4.1 %collective-permute-done.13.mine_ref = bf16[112,2048]{1,0:T(8,128)(2,1)S(1)} collective-permute-done((bf16[112,2048]{1,0:T(8,128)(2,1)S(1)}, bf16[112,2048]{1,0:T(8,128)(2,1)S(1)}, u32[]{:S(2)}, u32[]{:S(2)}) %collective-permute-start.13) | collective-permute-done | bytes 458784 | tf_op jit(solution)/shard_map/ppermute | solution.py:576
  72.7 1.3 %collective-permute-start.19 = (bf16[112,2048]{1,0:T(8,128)(2,1)S(1)}, bf16[112,2048]{1,0:T(8,128)(2,1)S(1)}, u32[]{:S(2)}, u32[]{:S(2)}) collective-permute-start(bf16[112,2048]{1,0:T(8,128)(2,1)S(1)} %collective-permute-done.13.mine_ref), channel_id=1, source_target_pairs={{0,4},{1,3},{2,6},{3,1},{4,0},{5,7},{6,2},{7,5},{8,12},{9,11},{10,... | collective-permute-start | bytes 1376264 | tf_op jit(solution)/shard_map/ppermute | solution.py:576
  74.0 7.1 %collective-permute-done.19.mine_ref = bf16[112,2048]{1,0:T(8,128)(2,1)S(1)} collective-permute-done((bf16[112,2048]{1,0:T(8,128)(2,1)S(1)}, bf16[112,2048]{1,0:T(8,128)(2,1)S(1)}, u32[]{:S(2)}, u32[]{:S(2)}) %collective-permute-start.19) | collective-permute-done | bytes 458784 | tf_op jit(solution)/shard_map/ppermute | solution.py:576
  81.2 2.6 %feed_forward.5 = (bf16[112,2048]{1,0:T(8,128)(2,1)S(1)}, bf16[112,1024]{1,0:T(8,128)(2,1)S(1)}, bf16[112,1024]{1,0:T(8,128)(2,1)S(1)}) custom-call(bf16[112,2048]{1,0:T(8,128)(2,1)S(1)} %collective-permute-done.13.mine_ref, bf16[112,2048]{1,0:T(8,128)(2,1)S(1)} %collective-permute-done.17.theirs_ref, bf16[2048,1024]{1,0:T(8,128)(2,1)S(1)} %copy-done, ...), custom_call_target="tpu_custom_call" | custom-call | flops 1879048192 | bytes 8388608 | tf_op jit(solution)/shard_map/feed_forward/pallas_call | solution.py:541
  83.8 1.4 %collective-permute-start.18 = (bf16[112,2048]{1,0:T(8,128)(2,1)S(1)}, bf16[112,2048]{1,0:T(8,128)(2,1)S(1)}, u32[]{:S(2)}, u32[]{:S(2)}) collective-permute-start(bf16[112,2048]{1,0:T(8,128)(2,1)S(1)} %combine.1.mine_ref), channel_id=1, source_target_pairs={{0,4},{1,3},{2,6},{3,1},{4,0},{5,7},{6,2},{7,5},{8,12},{9,11},{10,... | collective-permute-start | bytes 1376264 | tf_op jit(solution)/shard_map/ppermute | solution.py:576
  85.2 2.6 %feed_forward.6 = (bf16[112,2048]{1,0:T(8,128)(2,1)S(1)}, bf16[112,1024]{1,0:T(8,128)(2,1)S(1)}, bf16[112,1024]{1,0:T(8,128)(2,1)S(1)}) custom-call(bf16[112,2048]{1,0:T(8,128)(2,1)S(1)} %collective-permute-done.19.mine_ref, bf16[112,2048]{1,0:T(8,128)(2,1)S(1)} %collective-permute-done.20.theirs_ref, bf16[2048,1024]{1,0:T(8,128)(2,1)S(1)} %copy-done, ...), custom_call_target="tpu_custom_call" | custom-call | flops 1879048192 | bytes 8388608 | tf_op jit(solution)/shard_map/feed_forward/pallas_call | solution.py:541
  87.8 4.5 %collective-permute-done.18.mine_ref = bf16[112,2048]{1,0:T(8,128)(2,1)S(1)} collective-permute-done((bf16[112,2048]{1,0:T(8,128)(2,1)S(1)}, bf16[112,2048]{1,0:T(8,128)(2,1)S(1)}, u32[]{:S(2)}, u32[]{:S(2)}) %collective-permute-start.18) | collective-permute-done | bytes 458784 | tf_op jit(solution)/shard_map/ppermute | solution.py:576
  92.3 0.5 collective-permute-start.27
  92.8 1.0 collective-permute-done.28
  93.8 0.3 collective-permute-done.27
  94.1 0.1 add_convert_fusion.2
  94.2 1.4 %collective-permute-start.29 = (bf16[112,2048]{1,0:T(8,128)(2,1)S(1)}, bf16[112,2048]{1,0:T(8,128)(2,1)S(1)}, u32[]{:S(2)}, u32[]{:S(2)}) collective-permute-start(bf16[112,2048]{1,0:T(8,128)(2,1)S(1)} %add_convert_fusion.2), channel_id=1, source_target_pairs={{0,4},{1,3},{2,6},{3,1},{4,0},{5,7},{6,2},{7,5},{8,12},{9,11},{10,... | collective-permute-start | bytes 1376264 | tf_op jit(solution)/shard_map/ppermute | solution.py:576
  95.7 0.5 collective-permute-start.25
  96.2 0.5 collective-permute-start.15
  96.7 2.6 %feed_forward.7 = (bf16[112,2048]{1,0:T(8,128)(2,1)S(1)}, bf16[112,1024]{1,0:T(8,128)(2,1)S(1)}, bf16[112,1024]{1,0:T(8,128)(2,1)S(1)}) custom-call(bf16[112,2048]{1,0:T(8,128)(2,1)S(1)} %collective-permute-done.18.mine_ref, bf16[112,2048]{1,0:T(8,128)(2,1)S(1)} %collective-permute-done.21.theirs_ref, bf16[2048,1024]{1,0:T(8,128)(2,1)S(1)} %copy-done, ...), custom_call_target="tpu_custom_call" | custom-call | flops 1879048192 | bytes 8388608 | tf_op jit(solution)/shard_map/feed_forward/pallas_call | solution.py:541
  99.3 0.1 collective-permute-start.23
  99.4 0.5 collective-permute-start.22
  99.9 2.9 %collective-permute-done.29 = bf16[112,2048]{1,0:T(8,128)(2,1)S(1)} collective-permute-done((bf16[112,2048]{1,0:T(8,128)(2,1)S(1)}, bf16[112,2048]{1,0:T(8,128)(2,1)S(1)}, u32[]{:S(2)}, u32[]{:S(2)}) %collective-permute-start.29) | collective-permute-done | bytes 458784 | tf_op jit(solution)/shard_map/ppermute | solution.py:576
  102.8 0.2 add_convert_fusion.1
  103.0 1.3 %collective-permute-start.30 = (bf16[112,2048]{1,0:T(8,128)(2,1)S(1)}, bf16[112,2048]{1,0:T(8,128)(2,1)S(1)}, u32[]{:S(2)}, u32[]{:S(2)}) collective-permute-start(bf16[112,2048]{1,0:T(8,128)(2,1)S(1)} %add_convert_fusion.1), channel_id=1, source_target_pairs={{0,2},{1,5},{2,0},{3,7},{4,6},{5,1},{6,4},{7,3},{8,10},{9,13},{10,... | collective-permute-start | bytes 1376264 | tf_op jit(solution)/shard_map/ppermute | solution.py:576
  104.3 0.1 add_convert_fusion.3
  104.4 1.5 %collective-permute-start.24 = (bf16[112,2048]{1,0:T(8,128)(2,1)S(1)}, bf16[112,2048]{1,0:T(8,128)(2,1)S(1)}, u32[]{:S(2)}, u32[]{:S(2)}) collective-permute-start(bf16[112,2048]{1,0:T(8,128)(2,1)S(1)} %add_convert_fusion.3), channel_id=1, source_target_pairs={{0,4},{1,3},{2,6},{3,1},{4,0},{5,7},{6,2},{7,5},{8,12},{9,11},{10,... | collective-permute-start | bytes 1376264 | tf_op jit(solution)/shard_map/ppermute | solution.py:576
  105.9 0.1 convert_add_fusion
  106.1 10.0 %collective-permute-done.30 = bf16[112,2048]{1,0:T(8,128)(2,1)S(1)} collective-permute-done((bf16[112,2048]{1,0:T(8,128)(2,1)S(1)}, bf16[112,2048]{1,0:T(8,128)(2,1)S(1)}, u32[]{:S(2)}, u32[]{:S(2)}) %collective-permute-start.30) | collective-permute-done | bytes 458784 | tf_op jit(solution)/shard_map/ppermute | solution.py:576
  116.1 0.3 add_convert_fusion
  116.3 0.9 reshape.45
  (56 shorter events, 0.2 us)
Async XLA Ops:
  0.6 41.8 %collective-permute-start.4 = (bf16[4096,256]{1,0:T(8,128)(2,1)}, bf16[4096,256]{1,0:T(8,128)(2,1)}, u32[]{:S(2)}, u32[]{:S(2)}) collective-permute-start(bf16[4096,256]{1,0:T(8,128)(2,1)} %refs_0_.1), channel_id=1, source_target_pairs={{0,1},{1,0},{2,3},{3,2},{4,5},{5,4},{6,7},{7,6},{8,9},{9,8},{10,11... | collective-permute-start | bytes 6291464 | tf_op jit(solution)/shard_map/ppermute | solution.py:566
  1.1 1.2 copy-start.3
  2.3 7.8 %copy-start.4 = (bf16[18,24,1024]{2,1,0:T(8,128)(2,1)S(1)}, bf16[18,24,1024]{2,1,0:T(8,128)(2,1)}, u32[]{:S(2)}) copy-start(bf16[18,24,1024]{2,1,0:T(8,128)(2,1)} %tokens_ref.5) | copy-start | bytes 2654212
  5.3 11.1 %collective-permute-start.1 = (bf16[18,8,1024]{2,1,0:T(8,128)(2,1)S(1)}, bf16[18,8,1024]{2,1,0:T(8,128)(2,1)S(1)}, u32[]{:S(2)}, u32[]{:S(2)}) collective-permute-start(bf16[18,8,1024]{2,1,0:T(8,128)(2,1)S(1)} %get-tuple-element.51), channel_id=1, source_target_pairs={{0,7},{1,0},{2,1},{3,2},{4,3},{5,4},{6,5},{7,6},{8,15},{9,8},{10,9... | collective-permute-start | bytes 884744 | tf_op jit(solution)/shard_map/ppermute | solution.py:405
  8.9 10.3 %collective-permute-start = (bf16[18,8,1024]{2,1,0:T(8,128)(2,1)S(1)}, bf16[18,8,1024]{2,1,0:T(8,128)(2,1)S(1)}, u32[]{:S(2)}, u32[]{:S(2)}) collective-permute-start(bf16[18,8,1024]{2,1,0:T(8,128)(2,1)S(1)} %get-tuple-element.50), channel_id=1, source_target_pairs={{0,1},{1,2},{2,3},{3,4},{4,5},{5,6},{6,7},{7,0},{8,9},{9,10},{10,1... | collective-permute-start | bytes 884744 | tf_op jit(solution)/shard_map/ppermute | solution.py:405
  8.9 28.8 %collective-permute-start.5 = (bf16[2048,256]{1,0:T(8,128)(2,1)}, bf16[2048,256]{1,0:T(8,128)(2,1)}, u32[]{:S(2)}, u32[]{:S(2)}) collective-permute-start(bf16[2048,256]{1,0:T(8,128)(2,1)} %get-tuple-element.59), channel_id=1, source_target_pairs={{0,2},{1,3},{2,0},{3,1},{4,6},{5,7},{6,4},{7,5},{8,10},{9,11},{10,... | collective-permute-start | bytes 3145736 | tf_op jit(solution)/shard_map/ppermute | solution.py:571
  8.9 29.0 %collective-permute-start.6 = (bf16[2048,256]{1,0:T(8,128)(2,1)}, bf16[2048,256]{1,0:T(8,128)(2,1)}, u32[]{:S(2)}, u32[]{:S(2)}) collective-permute-start(bf16[2048,256]{1,0:T(8,128)(2,1)} %get-tuple-element.60), channel_id=1, source_target_pairs={{0,4},{1,5},{2,6},{3,7},{4,0},{5,1},{6,2},{7,3},{8,12},{9,13},{10,... | collective-permute-start | bytes 3145736 | tf_op jit(solution)/shard_map/ppermute | solution.py:571
  10.1 14.1 %copy-start.7 = (bf16[576,144]{1,0:T(8,128)(2,1)S(1)}, bf16[576,144]{1,0:T(8,128)(2,1)}, u32[]{:S(2)}) copy-start(bf16[576,144]{1,0:T(8,128)(2,1)} %constant.71.clone.rest_1_) | copy-start | bytes 497668
  10.1 14.1 %copy-start.8 = (bf16[576,256]{1,0:T(8,128)(2,1)S(1)}, bf16[576,256]{1,0:T(8,128)(2,1)}, u32[]{:S(2)}) copy-start(bf16[576,256]{1,0:T(8,128)(2,1)} %constant.72.clone.rest_2_) | copy-start | bytes 884740
  10.1 14.1 %copy-start.9 = (bf16[144,576]{1,0:T(8,128)(2,1)S(1)}, bf16[144,576]{1,0:T(8,128)(2,1)}, u32[]{:S(2)}) copy-start(bf16[144,576]{1,0:T(8,128)(2,1)} %constant.73.clone.rest_3_) | copy-start | bytes 497668
  10.2 14.1 %copy-start.13 = (bf16[240,240]{1,0:T(8,128)(2,1)S(1)}, bf16[240,240]{1,0:T(8,128)(2,1)}, u32[]{:S(2)}) copy-start(bf16[240,240]{1,0:T(8,128)(2,1)} %constant.70.clone.rest_0_) | copy-start | bytes 345604
  19.2 10.2 %collective-permute-start.2 = (bf16[3,40,1024]{2,1,0:T(8,128)(2,1)S(1)}, bf16[3,40,1024]{2,1,0:T(8,128)(2,1)S(1)}, u32[]{:S(2)}, u32[]{:S(2)}) collective-permute-start(bf16[3,40,1024]{2,1,0:T(8,128)(2,1)S(1)} %pad_maximum_fusion), channel_id=1, source_target_pairs={{0,8},{8,16},{16,24},{1,9},{9,17},{17,25},{2,10},{10,18},{18,26},{... | collective-permute-start | bytes 737288 | tf_op jit(solution)/shard_map/ppermute | solution.py:405
  22.8 8.1 %collective-permute-start.3 = (bf16[3,40,1024]{2,1,0:T(8,128)(2,1)S(1)}, bf16[3,40,1024]{2,1,0:T(8,128)(2,1)S(1)}, u32[]{:S(2)}, u32[]{:S(2)}) collective-permute-start(bf16[3,40,1024]{2,1,0:T(8,128)(2,1)S(1)} %pad_maximum_fusion.1), channel_id=1, source_target_pairs={{8,0},{16,8},{24,16},{9,1},{17,9},{25,17},{10,2},{18,10},{26,18},{... | collective-permute-start | bytes 737288 | tf_op jit(solution)/shard_map/ppermute | solution.py:405
  24.3 6.6 %copy-start.5 = (bf16[1024,1024]{1,0:T(8,128)(2,1)S(1)}, bf16[1024,1024]{1,0:T(8,128)(2,1)}, u32[]{:S(2)}) copy-start(bf16[1024,1024]{1,0:T(8,128)(2,1)} %out_w_ref.1) | copy-start | bytes 6291460
  24.3 6.6 %copy-start.6 = (bf16[448,432]{1,0:T(8,128)(2,1)S(1)}, bf16[448,432]{1,0:T(8,128)(2,1)}, u32[]{:S(2)}) copy-start(bf16[448,432]{1,0:T(8,128)(2,1)} %constant.74.clone.patch_ref) | copy-start | bytes 1161220
  24.3 6.6 %copy-start.10 = (bf16[304,256]{1,0:T(8,128)(2,1)S(1)}, bf16[304,256]{1,0:T(8,128)(2,1)}, u32[]{:S(2)}) copy-start(bf16[304,256]{1,0:T(8,128)(2,1)} %constant.77.clone.rest_2_.rest_6_) | copy-start | bytes 466948
  24.3 6.5 %copy-start.11 = (bf16[240,256]{1,0:T(8,128)(2,1)S(1)}, bf16[240,256]{1,0:T(8,128)(2,1)}, u32[]{:S(2)}) copy-start(bf16[240,256]{1,0:T(8,128)(2,1)} %constant.75.clone.rest_0_) | copy-start | bytes 368644
  24.3 6.5 %copy-start.12 = (bf16[240,256]{1,0:T(8,128)(2,1)S(1)}, bf16[240,256]{1,0:T(8,128)(2,1)}, u32[]{:S(2)}) copy-start(bf16[240,256]{1,0:T(8,128)(2,1)} %constant.79.clone.rest_4_) | copy-start | bytes 368644
  24.3 6.5 %copy-start.14 = (bf16[304,80]{1,0:T(8,128)(2,1)S(1)}, bf16[304,80]{1,0:T(8,128)(2,1)}, u32[]{:S(2)}) copy-start(bf16[304,80]{1,0:T(8,128)(2,1)} %constant.76.clone.rest_1_.rest_5_) | copy-start | bytes 145924
  24.4 6.5 %copy-start.15 = (bf16[80,304]{1,0:T(8,128)(2,1)S(1)}, bf16[80,304]{1,0:T(8,128)(2,1)}, u32[]{:S(2)}) copy-start(bf16[80,304]{1,0:T(8,128)(2,1)} %constant.78.clone.rest_3_.rest_7_) | copy-start | bytes 145924
  30.9 11.6 %copy-start.2 = (bf16[4096,256]{1,0:T(8,128)(2,1)S(1)}, bf16[4096,256]{1,0:T(8,128)(2,1)}, u32[]{:S(2)}) copy-start(bf16[4096,256]{1,0:T(8,128)(2,1)} %refs_0_.1) | copy-start | bytes 6291460
  38.0 4.5 %collective-permute-start.7 = (bf16[2048,256]{1,0:T(8,128)(2,1)}, bf16[2048,256]{1,0:T(8,128)(2,1)S(1)}, u32[]{:S(2)}, u32[]{:S(2)}) collective-permute-start(bf16[2048,256]{1,0:T(8,128)(2,1)} %collective-permute-done.5.refs_2_), channel_id=1, source_target_pairs={{0,1},{1,0},{2,3},{3,2},{4,5},{5,4},{6,7},{7,6},{8,9},{9,8},{10,11... | collective-permute-start | bytes 3145736 | tf_op jit(solution)/shard_map/ppermute | solution.py:566
  38.3 4.2 %collective-permute-start.8 = (bf16[2048,256]{1,0:T(8,128)(2,1)}, bf16[2048,256]{1,0:T(8,128)(2,1)}, u32[]{:S(2)}, u32[]{:S(2)}) collective-permute-start(bf16[2048,256]{1,0:T(8,128)(2,1)} %collective-permute-done.6.refs_4_), channel_id=1, source_target_pairs={{0,1},{1,0},{2,3},{3,2},{4,5},{5,4},{6,7},{7,6},{8,9},{9,8},{10,11... | collective-permute-start | bytes 3145736 | tf_op jit(solution)/shard_map/ppermute | solution.py:566
  38.5 13.3 %collective-permute-start.9 = (bf16[112,2048]{1,0:T(8,128)(2,1)}, bf16[112,2048]{1,0:T(8,128)(2,1)}, u32[]{:S(2)}, u32[]{:S(2)}) collective-permute-start(bf16[112,2048]{1,0:T(8,128)(2,1)} %get-tuple-element.57.upper_ref), channel_id=1, source_target_pairs={{0,4},{1,5},{2,6},{3,7},{4,0},{5,1},{6,2},{7,3},{8,12},{9,13},{10,... | collective-permute-start | bytes 1376264 | tf_op jit(solution)/shard_map/ppermute | solution.py:571
  40.3 13.0 %collective-permute-start.10 = (bf16[112,2048]{1,0:T(8,128)(2,1)}, bf16[112,2048]{1,0:T(8,128)(2,1)}, u32[]{:S(2)}, u32[]{:S(2)}) collective-permute-start(bf16[112,2048]{1,0:T(8,128)(2,1)} %get-tuple-element.58.lower_ref), channel_id=1, source_target_pairs={{0,2},{1,3},{2,0},{3,1},{4,6},{5,7},{6,4},{7,5},{8,10},{9,11},{10,... | collective-permute-start | bytes 1376264 | tf_op jit(solution)/shard_map/ppermute | solution.py:571
  53.3 12.7 %copy-start = (bf16[2048,1024]{1,0:T(8,128)(2,1)S(1)}, bf16[2048,1024]{1,0:T(8,128)(2,1)}, u32[]{:S(2)}) copy-start(bf16[2048,1024]{1,0:T(8,128)(2,1)} %up_ref.7) | copy-start | bytes 12582916
  53.3 12.7 %copy-start.1 = (bf16[1024,2048]{1,0:T(8,128)(2,1)S(1)}, bf16[1024,2048]{1,0:T(8,128)(2,1)}, u32[]{:S(2)}) copy-start(bf16[1024,2048]{1,0:T(8,128)(2,1)} %down_ref.7) | copy-start | bytes 12582916
  56.1 6.9 %collective-permute-start.11 = (bf16[112,1024]{1,0:T(8,128)(2,1)S(1)}, bf16[112,1024]{1,0:T(8,128)(2,1)S(1)}, u32[]{:S(2)}, u32[]{:S(2)}) collective-permute-start(bf16[112,1024]{1,0:T(8,128)(2,1)S(1)} %get-tuple-element.72), channel_id=1, source_target_pairs={{0,4},{1,5},{2,6},{3,7},{4,0},{5,1},{6,2},{7,3},{8,12},{9,13},{10,... | collective-permute-start | bytes 688136 | tf_op jit(solution)/shard_map/ppermute | solution.py:571
  56.5 7.0 %collective-permute-start.12 = (bf16[112,1024]{1,0:T(8,128)(2,1)S(1)}, bf16[112,1024]{1,0:T(8,128)(2,1)S(1)}, u32[]{:S(2)}, u32[]{:S(2)}) collective-permute-start(bf16[112,1024]{1,0:T(8,128)(2,1)S(1)} %get-tuple-element.73), channel_id=1, source_target_pairs={{0,2},{1,3},{2,0},{3,1},{4,6},{5,7},{6,4},{7,5},{8,10},{9,11},{10,... | collective-permute-start | bytes 688136 | tf_op jit(solution)/shard_map/ppermute | solution.py:571
  64.1 1.9 %collective-permute-start.14 = (bf16[112,2048]{1,0:T(8,128)(2,1)S(1)}, bf16[112,2048]{1,0:T(8,128)(2,1)S(1)}, u32[]{:S(2)}, u32[]{:S(2)}) collective-permute-start(bf16[112,2048]{1,0:T(8,128)(2,1)S(1)} %combine.1.mine_ref), channel_id=1, source_target_pairs={{0,1},{1,0},{2,3},{3,2},{4,5},{5,4},{6,7},{7,6},{8,9},{9,8},{10,11... | collective-permute-start | bytes 1376264 | tf_op jit(solution)/shard_map/ppermute | solution.py:566
  64.1 8.5 %collective-permute-start.13 = (bf16[112,2048]{1,0:T(8,128)(2,1)S(1)}, bf16[112,2048]{1,0:T(8,128)(2,1)S(1)}, u32[]{:S(2)}, u32[]{:S(2)}) collective-permute-start(bf16[112,2048]{1,0:T(8,128)(2,1)S(1)} %combine.1.mine_ref), channel_id=1, source_target_pairs={{0,2},{1,5},{2,0},{3,7},{4,6},{5,1},{6,4},{7,3},{8,10},{9,13},{10,... | collective-permute-start | bytes 1376264 | tf_op jit(solution)/shard_map/ppermute | solution.py:576
  72.7 8.5 %collective-permute-start.19 = (bf16[112,2048]{1,0:T(8,128)(2,1)S(1)}, bf16[112,2048]{1,0:T(8,128)(2,1)S(1)}, u32[]{:S(2)}, u32[]{:S(2)}) collective-permute-start(bf16[112,2048]{1,0:T(8,128)(2,1)S(1)} %collective-permute-done.13.mine_ref), channel_id=1, source_target_pairs={{0,4},{1,3},{2,6},{3,1},{4,0},{5,7},{6,2},{7,5},{8,12},{9,11},{10,... | collective-permute-start | bytes 1376264 | tf_op jit(solution)/shard_map/ppermute | solution.py:576
  74.0 7.1 %collective-permute-start.17 = (bf16[112,2048]{1,0:T(8,128)(2,1)S(1)}, bf16[112,2048]{1,0:T(8,128)(2,1)S(1)}, u32[]{:S(2)}, u32[]{:S(2)}) collective-permute-start(bf16[112,2048]{1,0:T(8,128)(2,1)S(1)} %collective-permute-done.13.mine_ref), channel_id=1, source_target_pairs={{0,1},{1,0},{2,3},{3,2},{4,5},{5,4},{6,7},{7,6},{8,9},{9,8},{10,11... | collective-permute-start | bytes 1376264 | tf_op jit(solution)/shard_map/ppermute | solution.py:566
  81.2 4.0 %collective-permute-start.20 = (bf16[112,2048]{1,0:T(8,128)(2,1)S(1)}, bf16[112,2048]{1,0:T(8,128)(2,1)S(1)}, u32[]{:S(2)}, u32[]{:S(2)}) collective-permute-start(bf16[112,2048]{1,0:T(8,128)(2,1)S(1)} %collective-permute-done.19.mine_ref), channel_id=1, source_target_pairs={{0,1},{1,0},{2,3},{3,2},{4,5},{5,4},{6,7},{7,6},{8,9},{9,8},{10,11... | collective-permute-start | bytes 1376264 | tf_op jit(solution)/shard_map/ppermute | solution.py:566
  83.8 8.5 %collective-permute-start.18 = (bf16[112,2048]{1,0:T(8,128)(2,1)S(1)}, bf16[112,2048]{1,0:T(8,128)(2,1)S(1)}, u32[]{:S(2)}, u32[]{:S(2)}) collective-permute-start(bf16[112,2048]{1,0:T(8,128)(2,1)S(1)} %combine.1.mine_ref), channel_id=1, source_target_pairs={{0,4},{1,3},{2,6},{3,1},{4,0},{5,7},{6,2},{7,5},{8,12},{9,11},{10,... | collective-permute-start | bytes 1376264 | tf_op jit(solution)/shard_map/ppermute | solution.py:576
  92.3 1.5 %collective-permute-start.28 = (bf16[112,1024]{1,0:T(8,128)(2,1)S(1)}, bf16[112,1024]{1,0:T(8,128)(2,1)S(1)}, u32[]{:S(2)}, u32[]{:S(2)}) collective-permute-start(bf16[112,1024]{1,0:T(8,128)(2,1)S(1)} %get-tuple-element.97), channel_id=1, source_target_pairs={{0,1},{1,0},{2,3},{3,2},{4,5},{5,4},{6,7},{7,6},{8,9},{9,8},{10,11... | collective-permute-start | bytes 688136 | tf_op jit(solution)/shard_map/ppermute | solution.py:566
  92.3 1.8 %collective-permute-start.27 = (bf16[112,1024]{1,0:T(8,128)(2,1)S(1)}, bf16[112,1024]{1,0:T(8,128)(2,1)S(1)}, u32[]{:S(2)}, u32[]{:S(2)}) collective-permute-start(bf16[112,1024]{1,0:T(8,128)(2,1)S(1)} %get-tuple-element.96), channel_id=1, source_target_pairs={{0,1},{1,0},{2,3},{3,2},{4,5},{5,4},{6,7},{7,6},{8,9},{9,8},{10,11... | collective-permute-start | bytes 688136 | tf_op jit(solution)/shard_map/ppermute | solution.py:566
  92.8 3.4 %collective-permute-start.21 = (bf16[112,2048]{1,0:T(8,128)(2,1)S(1)}, bf16[112,2048]{1,0:T(8,128)(2,1)S(1)}, u32[]{:S(2)}, u32[]{:S(2)}) collective-permute-start(bf16[112,2048]{1,0:T(8,128)(2,1)S(1)} %collective-permute-done.18.mine_ref), channel_id=1, source_target_pairs={{0,1},{1,0},{2,3},{3,2},{4,5},{5,4},{6,7},{7,6},{8,9},{9,8},{10,11... | collective-permute-start | bytes 1376264 | tf_op jit(solution)/shard_map/ppermute | solution.py:566
  94.2 8.5 %collective-permute-start.29 = (bf16[112,2048]{1,0:T(8,128)(2,1)S(1)}, bf16[112,2048]{1,0:T(8,128)(2,1)S(1)}, u32[]{:S(2)}, u32[]{:S(2)}) collective-permute-start(bf16[112,2048]{1,0:T(8,128)(2,1)S(1)} %add_convert_fusion.2), channel_id=1, source_target_pairs={{0,4},{1,3},{2,6},{3,1},{4,0},{5,7},{6,2},{7,5},{8,12},{9,11},{10,... | collective-permute-start | bytes 1376264 | tf_op jit(solution)/shard_map/ppermute | solution.py:576
  95.7 3.6 %collective-permute-start.26 = (bf16[112,1024]{1,0:T(8,128)(2,1)S(1)}, bf16[112,1024]{1,0:T(8,128)(2,1)S(1)}, u32[]{:S(2)}, u32[]{:S(2)}) collective-permute-start(bf16[112,1024]{1,0:T(8,128)(2,1)S(1)} %get-tuple-element.94), channel_id=1, source_target_pairs={{0,1},{1,0},{2,3},{3,2},{4,5},{5,4},{6,7},{7,6},{8,9},{9,8},{10,11... | collective-permute-start | bytes 688136 | tf_op jit(solution)/shard_map/ppermute | solution.py:566
  95.7 3.7 %collective-permute-start.25 = (bf16[112,1024]{1,0:T(8,128)(2,1)S(1)}, bf16[112,1024]{1,0:T(8,128)(2,1)S(1)}, u32[]{:S(2)}, u32[]{:S(2)}) collective-permute-start(bf16[112,1024]{1,0:T(8,128)(2,1)S(1)} %get-tuple-element.93), channel_id=1, source_target_pairs={{0,1},{1,0},{2,3},{3,2},{4,5},{5,4},{6,7},{7,6},{8,9},{9,8},{10,11... | collective-permute-start | bytes 688136 | tf_op jit(solution)/shard_map/ppermute | solution.py:566
  96.2 9.8 %collective-permute-start.16 = (bf16[112,1024]{1,0:T(8,128)(2,1)S(1)}, bf16[112,1024]{1,0:T(8,128)(2,1)S(1)}, u32[]{:S(2)}, u32[]{:S(2)}) collective-permute-start(bf16[112,1024]{1,0:T(8,128)(2,1)S(1)} %get-tuple-element.79), channel_id=1, source_target_pairs={{0,1},{1,0},{2,3},{3,2},{4,5},{5,4},{6,7},{7,6},{8,9},{9,8},{10,11... | collective-permute-start | bytes 688136 | tf_op jit(solution)/shard_map/ppermute | solution.py:566
  96.2 9.8 %collective-permute-start.15 = (bf16[112,1024]{1,0:T(8,128)(2,1)S(1)}, bf16[112,1024]{1,0:T(8,128)(2,1)S(1)}, u32[]{:S(2)}, u32[]{:S(2)}) collective-permute-start(bf16[112,1024]{1,0:T(8,128)(2,1)S(1)} %get-tuple-element.78), channel_id=1, source_target_pairs={{0,1},{1,0},{2,3},{3,2},{4,5},{5,4},{6,7},{7,6},{8,9},{9,8},{10,11... | collective-permute-start | bytes 688136 | tf_op jit(solution)/shard_map/ppermute | solution.py:566
  99.3 5.0 %collective-permute-start.23 = (bf16[112,1024]{1,0:T(8,128)(2,1)S(1)}, bf16[112,1024]{1,0:T(8,128)(2,1)S(1)}, u32[]{:S(2)}, u32[]{:S(2)}) collective-permute-start(bf16[112,1024]{1,0:T(8,128)(2,1)S(1)} %get-tuple-element.91), channel_id=1, source_target_pairs={{0,1},{1,0},{2,3},{3,2},{4,5},{5,4},{6,7},{7,6},{8,9},{9,8},{10,11... | collective-permute-start | bytes 688136 | tf_op jit(solution)/shard_map/ppermute | solution.py:566
  99.4 4.9 %collective-permute-start.22 = (bf16[112,1024]{1,0:T(8,128)(2,1)S(1)}, bf16[112,1024]{1,0:T(8,128)(2,1)S(1)}, u32[]{:S(2)}, u32[]{:S(2)}) collective-permute-start(bf16[112,1024]{1,0:T(8,128)(2,1)S(1)} %get-tuple-element.90), channel_id=1, source_target_pairs={{0,1},{1,0},{2,3},{3,2},{4,5},{5,4},{6,7},{7,6},{8,9},{9,8},{10,11... | collective-permute-start | bytes 688136 | tf_op jit(solution)/shard_map/ppermute | solution.py:566
  103.0 13.1 %collective-permute-start.30 = (bf16[112,2048]{1,0:T(8,128)(2,1)S(1)}, bf16[112,2048]{1,0:T(8,128)(2,1)S(1)}, u32[]{:S(2)}, u32[]{:S(2)}) collective-permute-start(bf16[112,2048]{1,0:T(8,128)(2,1)S(1)} %add_convert_fusion.1), channel_id=1, source_target_pairs={{0,2},{1,5},{2,0},{3,7},{4,6},{5,1},{6,4},{7,3},{8,10},{9,13},{10,... | collective-permute-start | bytes 1376264 | tf_op jit(solution)/shard_map/ppermute | solution.py:576
  104.4 11.6 %collective-permute-start.24 = (bf16[112,2048]{1,0:T(8,128)(2,1)S(1)}, bf16[112,2048]{1,0:T(8,128)(2,1)S(1)}, u32[]{:S(2)}, u32[]{:S(2)}) collective-permute-start(bf16[112,2048]{1,0:T(8,128)(2,1)S(1)} %add_convert_fusion.3), channel_id=1, source_target_pairs={{0,4},{1,3},{2,6},{3,1},{4,0},{5,7},{6,2},{7,5},{8,12},{9,11},{10,... | collective-permute-start | bytes 1376264 | tf_op jit(solution)/shard_map/ppermute | solution.py:576

commit v8 on v7

--- a/solution.py
+++ b/solution.py
@@ -552,9 +552,8 @@
     )(mine, theirs, up, down)
 
 
-def added(mine, low, high, more=None):
-    total = mine.astype(F32) + jnp.concatenate([low, high], axis=1).astype(F32)
-    return (total if more is None else total + more.astype(F32)).astype(BF16)
+def added(mine, low, high):
+    return (mine.astype(F32) + jnp.concatenate([low, high], axis=1).astype(F32)).astype(BF16)
 
 
 def summed(mine, low, high):
@@ -582,14 +581,21 @@
     first = feed_forward(own, core_swap(own), up, down)
     near, *first = lax.optimization_barrier((near, *first))
     far = cross(near, 2, 1)
-    near_sums = feed_forward(near, core_swap(near), up, down)
-    later, *near_sums = lax.optimization_barrier((own, *near_sums))
+    near_mine, near_low, near_high = feed_forward(near, core_swap(near), up, down)
+    later, near_mine = lax.optimization_barrier((own, near_mine))
     other = cross(later, 2, 1)
-    far_sums = feed_forward(far, core_swap(far), up, down)
-    other, *far_sums = lax.optimization_barrier((other, *far_sums))
-    relayed = cross(summed(*far_sums), 2, 1)
+    near_low, far = lax.optimization_barrier((core_swap(near_low), far))
+    mine, low, high = feed_forward(far, core_swap(far), up, down)
+    low, other = lax.optimization_barrier((core_swap(low), other))
+    relayed = cross(added(mine, low, core_swap(high)), 2, 1)
     other_back = cross(summed(*feed_forward(other, core_swap(other), up, down)), 2, 1)
-    near_back = cross(added(*near_sums[:1], core_swap(near_sums[1]), core_swap(near_sums[2]), relayed), 1, 2)
+    half = low.shape[1]
+    near_back = []
+    for part, at in ((near_low, 0), (core_swap(near_high), half)):
+        columns = slice(at, at + half)
+        total = near_mine[:, columns].astype(F32) + part.astype(F32) + relayed[:, columns].astype(F32)
+        near_back.append(cross(total.astype(BF16), 1, 2))
+    near_back = jnp.concatenate(near_back, axis=1)
     return sum(part.astype(F32) for part in (own, summed(*first), other_back, near_back))
 
 

time: 117 us -> 113 us (0.966)
  waiting for transfers between devices: 47.1 us -> 42.3 us
    ppermute x6 -> x7, waiting for transfers between devices: 28.7 us -> 24.1 us  [cross(): lax.ppermute(value, 'lon', [(i, i ^ 2 * (second if i % 2 else first)) for...]
    ppermute x6 -> x7, starting transfers between devices: 8.33 us -> 8.89 us  [cross(): lax.ppermute(value, 'lon', [(i, i ^ 2 * (second if i % 2 else first)) for...]
  transfers between devices with their start and end apart: 31 -> 32, of which waited for: 16 -> 17; matrix products, arithmetic and copies ran while one was open for 1% -> 1% of each run, Pallas kernels for 30% -> 31%
where the time goes in v8:
time: 113 us
  waiting for transfers between devices  42.3 us (37%)
  Pallas kernels  38.7 us (34%)
  starting transfers between devices  27.7 us (25%)
  local copies, waits for them, and re-layouts  2.2 us (2%)
    ppermute x7, waiting for transfers between devices, cross(): lax.ppermute(value, 'lon', [(i, i ^ 2 * (second if i % 2 else first)) for...  24.1 us
    pallas_call x2, Pallas kernels, vmem_call(): pl.pallas_call(kernel, in_specs=[vmem] * len(args), out_specs=[vmem] * le...  11.8 us
    ppermute x6, waiting for transfers between devices, chip_swap(): lax.ppermute(value, 'lon', [(i, i ^ 2 * offset) for i in range(size)])  11.7 us
    pallas_call x4, Pallas kernels, feed_forward(): pl.pallas_call(ffn_kernel, in_specs=[vmem] * 4, out_specs=[vmem] * 3, out...  10.4 us
    ppermute x7, starting transfers between devices, cross(): lax.ppermute(value, 'lon', [(i, i ^ 2 * (second if i % 2 else first)) for...  8.89 us
    ppermute x4, starting transfers between devices, shift(): return lax.ppermute(part, axis, pairs)  8.58 us
    pallas_call x3, Pallas kernels, local_call(): pl.pallas_call(kernel, in_specs=[pl.BlockSpec(memory_space=pltpu.SMEM)] +...  8.15 us
    ppermute x6, starting transfers between devices, chip_swap(): lax.ppermute(value, 'lon', [(i, i ^ 2 * offset) for i in range(size)])  7.08 us
  transfers between devices with their start and end apart: 32, of which 17 were waited for; matrix products, arithmetic and copies ran while one was open for 1% of the time, Pallas kernels for 31%

profile of v8, /device:TPU:0, one launch (start us, length us, event | category | flops | bytes accessed | tf_op | source)
XLA Modules:
  0.0 112.9 jit_solution(10579005209541648423)
XLA Ops:
  0.6 0.5 collective-permute-start.4
  1.1 1.2 %copy-done.3 = bf16[18,24,1024]{2,1,0:T(8,128)(2,1)S(1)} copy-done((bf16[18,24,1024]{2,1,0:T(8,128)(2,1)S(1)}, bf16[18,24,1024]{2,1,0:T(8,128)(2,1)}, u32[]{:S(2)}) %copy-start.3) | copy-done | bytes 884760
  2.3 3.0 %prepare.1 = (bf16[18,8,1024]{2,1,0:T(8,128)(2,1)S(1)}, bf16[18,8,1024]{2,1,0:T(8,128)(2,1)S(1)}, bf16[2048,256]{1,0:T(8,128)(2,1)}, bf16[2048,256]{1,0:T(8,128)(2,1)}) custom-call(bf16[18,24,1024]{2,1,0:T(8,128)(2,1)S(1)} %copy-done.3, bf16[4096,256]{1,0:T(8,128)(2,1)} %refs_0_.1), custom_call_target="tpu_custom_call" | custom-call | tf_op jit(solution)/shard_map/prepare/pallas_call | solution.py:169
  5.3 3.6 %collective-permute-start.1 = (bf16[18,8,1024]{2,1,0:T(8,128)(2,1)S(1)}, bf16[18,8,1024]{2,1,0:T(8,128)(2,1)S(1)}, u32[]{:S(2)}, u32[]{:S(2)}) collective-permute-start(bf16[18,8,1024]{2,1,0:T(8,128)(2,1)S(1)} %get-tuple-element.49), channel_id=1, source_target_pairs={{0,7},{1,0},{2,1},{3,2},{4,3},{5,4},{6,5},{7,6},{8,15},{9,8},{10,9... | collective-permute-start | bytes 884744 | tf_op jit(solution)/shard_map/ppermute | solution.py:405
  8.9 1.1 collective-permute-start.6
  10.2 5.4 %own_projection.1 = (bf16[448,3072]{1,0:T(8,128)(2,1)S(1)}, bf16[1024,2048]{1,0:T(8,128)(2,1)S(1)}) custom-call(bf16[18,24,1024]{2,1,0:T(8,128)(2,1)S(1)} %copy-done.4, bf16[1024,3072]{1,0:T(8,128)(2,1)} %weight_ref.3), custom_call_target="tpu_custom_call" | custom-call | flops 2818572288 | bytes 6291456 | tf_op jit(solution)/shard_map/own_projection/pallas_call | solution.py:210
  15.6 0.1 or_select_fusion.bias_ref
  15.6 0.8 collective-permute-done.1.east_ref
  16.4 2.8 %collective-permute-done.west_ref = bf16[18,8,1024]{2,1,0:T(8,128)(2,1)S(1)} collective-permute-done((bf16[18,8,1024]{2,1,0:T(8,128)(2,1)S(1)}, bf16[18,8,1024]{2,1,0:T(8,128)(2,1)S(1)}, u32[]{:S(2)}, u32[]{:S(2)}) %collective-permute-start) | collective-permute-done | bytes 294944 | tf_op jit(solution)/shard_map/ppermute | solution.py:405
  19.2 3.5 %collective-permute-start.2 = (bf16[3,40,1024]{2,1,0:T(8,128)(2,1)S(1)}, bf16[3,40,1024]{2,1,0:T(8,128)(2,1)S(1)}, u32[]{:S(2)}, u32[]{:S(2)}) collective-permute-start(bf16[3,40,1024]{2,1,0:T(8,128)(2,1)S(1)} %pad_maximum_fusion.1), channel_id=1, source_target_pairs={{0,8},{8,16},{16,24},{1,9},{9,17},{17,25},{2,10},{10,18},{18,26},{... | collective-permute-start | bytes 737288 | tf_op jit(solution)/shard_map/ppermute | solution.py:405
  22.8 1.5 %collective-permute-start.3 = (bf16[3,40,1024]{2,1,0:T(8,128)(2,1)S(1)}, bf16[3,40,1024]{2,1,0:T(8,128)(2,1)S(1)}, u32[]{:S(2)}, u32[]{:S(2)}) collective-permute-start(bf16[3,40,1024]{2,1,0:T(8,128)(2,1)S(1)} %pad_maximum_fusion.2), channel_id=1, source_target_pairs={{8,0},{16,8},{24,16},{9,1},{17,9},{25,17},{10,2},{18,10},{26,18},{... | collective-permute-start | bytes 737288 | tf_op jit(solution)/shard_map/ppermute | solution.py:405
  24.4 5.0 %middle_attention.1 = (bf16[288,2048]{1,0:T(8,128)(2,1)S(1)}, bf16[288,1024]{1,0:T(8,128)(2,1)S(1)}) custom-call(bf16[18,8,1024]{2,1,0:T(8,128)(2,1)S(1)} %collective-permute-done.west_ref, bf16[18,8,1024]{2,1,0:T(8,128)(2,1)S(1)} %collective-permute-done.1.east_ref, bf16[448,3072]{1,0:T(8,128)(2,1)S(1)} %get-tuple-element.50.own_ref, ...), custom_call_target="tpu_custom_call" | custom-call | flops 5000000000 | bytes 1048576 | tf_op jit(solution)/shard_map/middle_attention/pallas_call | solution.py:348
  29.4 1.4 %collective-permute-done.3.south_ref = bf16[3,40,1024]{2,1,0:T(8,128)(2,1)S(1)} collective-permute-done((bf16[3,40,1024]{2,1,0:T(8,128)(2,1)S(1)}, bf16[3,40,1024]{2,1,0:T(8,128)(2,1)S(1)}, u32[]{:S(2)}, u32[]{:S(2)}) %collective-permute-start.3) | collective-permute-done | bytes 245792 | tf_op jit(solution)/shard_map/ppermute | solution.py:405
  30.9 6.7 %edge_attention.1 = (bf16[18,24,1024]{2,1,0:T(8,128)(2,1)}, bf16[112,2048]{1,0:T(8,128)(2,1)}, bf16[112,2048]{1,0:T(8,128)(2,1)}) custom-call(bf16[18,24,1024]{2,1,0:T(8,128)(2,1)S(1)} %copy-done.4, bf16[3,40,1024]{2,1,0:T(8,128)(2,1)S(1)} %collective-permute-done.2.north_ref, bf16[3,40,1024]{2,1,0:T(8,128)(2,1)S(1)} %collective-permute-done.3.south_ref, ...), custom_call_target="tpu_custom_call" | custom-call | flops 6000000000 | bytes 1048576 | tf_op jit(solution)/shard_map/edge_attention/pallas_call | solution.py:348
  37.7 0.3 collective-permute-done.6.refs_4_
  38.0 0.3 collective-permute-start.7
  38.3 0.2 collective-permute-start.8
  38.5 1.8 %collective-permute-start.9 = (bf16[112,2048]{1,0:T(8,128)(2,1)}, bf16[112,2048]{1,0:T(8,128)(2,1)}, u32[]{:S(2)}, u32[]{:S(2)}) collective-permute-start(bf16[112,2048]{1,0:T(8,128)(2,1)} %get-tuple-element.55.upper_ref), channel_id=1, source_target_pairs={{0,4},{1,5},{2,6},{3,7},{4,0},{5,1},{6,2},{7,3},{8,12},{9,13},{10,... | collective-permute-start | bytes 1376264 | tf_op jit(solution)/shard_map/ppermute | solution.py:570
  40.3 2.1 %collective-permute-start.10 = (bf16[112,2048]{1,0:T(8,128)(2,1)}, bf16[112,2048]{1,0:T(8,128)(2,1)}, u32[]{:S(2)}, u32[]{:S(2)}) collective-permute-start(bf16[112,2048]{1,0:T(8,128)(2,1)} %get-tuple-element.56.lower_ref), channel_id=1, source_target_pairs={{0,2},{1,3},{2,0},{3,1},{4,6},{5,7},{6,4},{7,5},{8,10},{9,11},{10,... | collective-permute-start | bytes 1376264 | tf_op jit(solution)/shard_map/ppermute | solution.py:570
  42.4 0.1 pad_add_fusion.place_ref
  42.5 4.7 %merge_own.1 = (f32[112,512]{1,0:T(8,128)S(1)}, f32[112,512]{1,0:T(8,128)S(1)}, f32[112,512]{1,0:T(8,128)S(1)}, bf16[4096,256]{1,0:T(8,128)(2,1)S(1)}, bf16[4096...) custom-call(s32[2]{0:T(128)S(1)} %pad_add_fusion.place_ref, ...), custom_call_target="tpu_custom_call" | custom-call | flops 939524096 | bytes 1048576 | tf_op jit(solution)/shard_map/merge_own/pallas_call | solution.py:483
  47.2 4.6 %collective-permute-done.9.upper_ref = bf16[112,2048]{1,0:T(8,128)(2,1)} collective-permute-done((bf16[112,2048]{1,0:T(8,128)(2,1)}, bf16[112,2048]{1,0:T(8,128)(2,1)}, u32[]{:S(2)}, u32[]{:S(2)}) %collective-permute-start.9) | collective-permute-done | bytes 458784 | tf_op jit(solution)/shard_map/ppermute | solution.py:570
  51.8 1.5 %collective-permute-done.10.lower_ref = bf16[112,2048]{1,0:T(8,128)(2,1)} collective-permute-done((bf16[112,2048]{1,0:T(8,128)(2,1)}, bf16[112,2048]{1,0:T(8,128)(2,1)}, u32[]{:S(2)}, u32[]{:S(2)}) %collective-permute-start.10) | collective-permute-done | bytes 458784 | tf_op jit(solution)/shard_map/ppermute | solution.py:570
  53.3 2.9 %merge_other.1 = (bf16[112,1024]{1,0:T(8,128)(2,1)S(1)}, bf16[112,1024]{1,0:T(8,128)(2,1)S(1)}) custom-call(s32[2]{0:T(128)S(1)} %pad_add_fusion.place_ref, bf16[112,2048]{1,0:T(8,128)(2,1)} %collective-permute-done.9.upper_ref, bf16[112,2048]{1,0:T(8,128)(2,1)} %collective-permute-done.10.lower_ref, bf16[4096,256]{1,0:T(8,128)(2,1)S(1)} %get-tuple-element.64.refs_0_, ...), custom_call_target="tpu_custom_call" | custom-call | flops 939524096 | bytes 1048576 | tf_op jit(solution)/shard_map/merge_other/pallas_call | solution.py:483
  56.1 0.3 collective-permute-start.11
  56.5 1.7 %collective-permute-start.12 = (bf16[112,1024]{1,0:T(8,128)(2,1)S(1)}, bf16[112,1024]{1,0:T(8,128)(2,1)S(1)}, u32[]{:S(2)}, u32[]{:S(2)}) collective-permute-start(bf16[112,1024]{1,0:T(8,128)(2,1)S(1)} %get-tuple-element.71), channel_id=1, source_target_pairs={{0,2},{1,3},{2,0},{3,1},{4,6},{5,7},{6,4},{7,5},{8,10},{9,11},{10,... | collective-permute-start | bytes 688136 | tf_op jit(solution)/shard_map/ppermute | solution.py:570
  58.2 4.8 %collective-permute-done.11.from_y_ref = bf16[112,1024]{1,0:T(8,128)(2,1)S(1)} collective-permute-done((bf16[112,1024]{1,0:T(8,128)(2,1)S(1)}, bf16[112,1024]{1,0:T(8,128)(2,1)S(1)}, u32[]{:S(2)}, u32[]{:S(2)}) %collective-permute-start.11) | collective-permute-done | bytes 229408 | tf_op jit(solution)/shard_map/ppermute | solution.py:570
  63.0 0.4 collective-permute-done.12.from_x_ref
  63.4 0.6 combine.1.mine_ref
  64.1 0.1 collective-permute-start.14
  64.1 1.3 %collective-permute-start.13 = (bf16[112,2048]{1,0:T(8,128)(2,1)S(1)}, bf16[112,2048]{1,0:T(8,128)(2,1)S(1)}, u32[]{:S(2)}, u32[]{:S(2)}) collective-permute-start(bf16[112,2048]{1,0:T(8,128)(2,1)S(1)} %combine.1.mine_ref), channel_id=1, source_target_pairs={{0,2},{1,5},{2,0},{3,7},{4,6},{5,1},{6,4},{7,3},{8,10},{9,13},{10,... | collective-permute-start | bytes 1376264 | tf_op jit(solution)/shard_map/ppermute | solution.py:575
  65.5 0.5 collective-permute-done.14.theirs_ref
  66.0 2.6 %feed_forward.4 = (bf16[112,2048]{1,0:T(8,128)(2,1)S(1)}, bf16[112,1024]{1,0:T(8,128)(2,1)S(1)}, bf16[112,1024]{1,0:T(8,128)(2,1)S(1)}) custom-call(bf16[112,2048]{1,0:T(8,128)(2,1)S(1)} %combine.1.mine_ref, bf16[112,2048]{1,0:T(8,128)(2,1)S(1)} %collective-permute-done.14.theirs_ref, bf16[2048,1024]{1,0:T(8,128)(2,1)S(1)} %copy-done, ...), custom_call_target="tpu_custom_call" | custom-call | flops 1879048192 | bytes 8388608 | tf_op jit(solution)/shard_map/feed_forward/pallas_call | solution.py:541
  68.6 4.1 %collective-permute-done.13.mine_ref = bf16[112,2048]{1,0:T(8,128)(2,1)S(1)} collective-permute-done((bf16[112,2048]{1,0:T(8,128)(2,1)S(1)}, bf16[112,2048]{1,0:T(8,128)(2,1)S(1)}, u32[]{:S(2)}, u32[]{:S(2)}) %collective-permute-start.13) | collective-permute-done | bytes 458784 | tf_op jit(solution)/shard_map/ppermute | solution.py:575
  72.7 1.3 %collective-permute-start.19 = (bf16[112,2048]{1,0:T(8,128)(2,1)S(1)}, bf16[112,2048]{1,0:T(8,128)(2,1)S(1)}, u32[]{:S(2)}, u32[]{:S(2)}) collective-permute-start(bf16[112,2048]{1,0:T(8,128)(2,1)S(1)} %collective-permute-done.13.mine_ref), channel_id=1, source_target_pairs={{0,4},{1,3},{2,6},{3,1},{4,0},{5,7},{6,2},{7,5},{8,12},{9,11},{10,... | collective-permute-start | bytes 1376264 | tf_op jit(solution)/shard_map/ppermute | solution.py:575
  74.0 0.5 collective-permute-done.17.theirs_ref
  74.5 2.6 %feed_forward.5 = (bf16[112,2048]{1,0:T(8,128)(2,1)S(1)}, bf16[112,1024]{1,0:T(8,128)(2,1)S(1)}, bf16[112,1024]{1,0:T(8,128)(2,1)S(1)}) custom-call(bf16[112,2048]{1,0:T(8,128)(2,1)S(1)} %collective-permute-done.13.mine_ref, bf16[112,2048]{1,0:T(8,128)(2,1)S(1)} %collective-permute-done.17.theirs_ref, bf16[2048,1024]{1,0:T(8,128)(2,1)S(1)} %copy-done, ...), custom_call_target="tpu_custom_call" | custom-call | flops 1879048192 | bytes 8388608 | tf_op jit(solution)/shard_map/feed_forward/pallas_call | solution.py:541
  77.1 0.2 collective-permute-start.18
  77.3 3.8 %collective-permute-done.19.mine_ref = bf16[112,2048]{1,0:T(8,128)(2,1)S(1)} collective-permute-done((bf16[112,2048]{1,0:T(8,128)(2,1)S(1)}, bf16[112,2048]{1,0:T(8,128)(2,1)S(1)}, u32[]{:S(2)}, u32[]{:S(2)}) %collective-permute-start.19) | collective-permute-done | bytes 458784 | tf_op jit(solution)/shard_map/ppermute | solution.py:575
  81.2 1.3 %collective-permute-start.22 = (bf16[112,2048]{1,0:T(8,128)(2,1)S(1)}, bf16[112,2048]{1,0:T(8,128)(2,1)S(1)}, u32[]{:S(2)}, u32[]{:S(2)}) collective-permute-start(bf16[112,2048]{1,0:T(8,128)(2,1)S(1)} %combine.1.mine_ref), channel_id=1, source_target_pairs={{0,4},{1,3},{2,6},{3,1},{4,0},{5,7},{6,2},{7,5},{8,12},{9,11},{10,... | collective-permute-start | bytes 1376264 | tf_op jit(solution)/shard_map/ppermute | solution.py:575
  82.5 0.5 collective-permute-done.20.theirs_ref
  83.0 2.6 %feed_forward.6 = (bf16[112,2048]{1,0:T(8,128)(2,1)S(1)}, bf16[112,1024]{1,0:T(8,128)(2,1)S(1)}, bf16[112,1024]{1,0:T(8,128)(2,1)S(1)}) custom-call(bf16[112,2048]{1,0:T(8,128)(2,1)S(1)} %collective-permute-done.19.mine_ref, bf16[112,2048]{1,0:T(8,128)(2,1)S(1)} %collective-permute-done.20.theirs_ref, bf16[2048,1024]{1,0:T(8,128)(2,1)S(1)} %copy-done, ...), custom_call_target="tpu_custom_call" | custom-call | flops 1879048192 | bytes 8388608 | tf_op jit(solution)/shard_map/feed_forward/pallas_call | solution.py:541
  85.6 0.2 collective-permute-start.21
  85.8 0.4 collective-permute-start.27
  86.2 3.5 %collective-permute-done.22.mine_ref = bf16[112,2048]{1,0:T(8,128)(2,1)S(1)} collective-permute-done((bf16[112,2048]{1,0:T(8,128)(2,1)S(1)}, bf16[112,2048]{1,0:T(8,128)(2,1)S(1)}, u32[]{:S(2)}, u32[]{:S(2)}) %collective-permute-start.22) | collective-permute-done | bytes 458784 | tf_op jit(solution)/shard_map/ppermute | solution.py:575
  89.7 0.1 add_convert_fusion.1
  89.8 1.4 %collective-permute-start.28 = (bf16[112,2048]{1,0:T(8,128)(2,1)S(1)}, bf16[112,2048]{1,0:T(8,128)(2,1)S(1)}, u32[]{:S(2)}, u32[]{:S(2)}) collective-permute-start(bf16[112,2048]{1,0:T(8,128)(2,1)S(1)} %add_convert_fusion.1), channel_id=1, source_target_pairs={{0,4},{1,3},{2,6},{3,1},{4,0},{5,7},{6,2},{7,5},{8,12},{9,11},{10,... | collective-permute-start | bytes 1376264 | tf_op jit(solution)/shard_map/ppermute | solution.py:575
  91.2 0.1 collective-permute-start.30
  91.3 0.4 collective-permute-start.16
  91.7 0.1 collective-permute-start.15
  91.9 2.6 %feed_forward.7 = (bf16[112,2048]{1,0:T(8,128)(2,1)S(1)}, bf16[112,1024]{1,0:T(8,128)(2,1)S(1)}, bf16[112,1024]{1,0:T(8,128)(2,1)S(1)}) custom-call(bf16[112,2048]{1,0:T(8,128)(2,1)S(1)} %collective-permute-done.22.mine_ref, bf16[112,2048]{1,0:T(8,128)(2,1)S(1)} %collective-permute-done.23.theirs_ref, bf16[2048,1024]{1,0:T(8,128)(2,1)S(1)} %copy-done, ...), custom_call_target="tpu_custom_call" | custom-call | flops 1879048192 | bytes 8388608 | tf_op jit(solution)/shard_map/feed_forward/pallas_call | solution.py:541
  94.5 0.4 collective-permute-start.25
  94.9 0.1 collective-permute-start.24
  95.0 3.3 %collective-permute-done.28 = bf16[112,2048]{1,0:T(8,128)(2,1)S(1)} collective-permute-done((bf16[112,2048]{1,0:T(8,128)(2,1)S(1)}, bf16[112,2048]{1,0:T(8,128)(2,1)S(1)}, u32[]{:S(2)}, u32[]{:S(2)}) %collective-permute-start.28) | collective-permute-done | bytes 458784 | tf_op jit(solution)/shard_map/ppermute | solution.py:575
  98.3 0.2 add_convert_fusion.4
  98.6 1.3 %collective-permute-start.31 = (bf16[112,1024]{1,0:T(8,128)(2,1)S(1)}, bf16[112,1024]{1,0:T(8,128)(2,1)S(1)}, u32[]{:S(2)}, u32[]{:S(2)}) collective-permute-start(bf16[112,1024]{1,0:T(8,128)(2,1)S(1)} %get-tuple-element.95), channel_id=1, source_target_pairs={{0,2},{1,5},{2,0},{3,7},{4,6},{5,1},{6,4},{7,3},{8,10},{9,13},{10,... | collective-permute-start | bytes 688136 | tf_op jit(solution)/shard_map/ppermute | solution.py:575
  99.9 0.8 collective-permute-start.29
  100.7 0.1 add_convert_fusion.2
  100.8 1.4 %collective-permute-start.26 = (bf16[112,2048]{1,0:T(8,128)(2,1)S(1)}, bf16[112,2048]{1,0:T(8,128)(2,1)S(1)}, u32[]{:S(2)}, u32[]{:S(2)}) collective-permute-start(bf16[112,2048]{1,0:T(8,128)(2,1)S(1)} %add_convert_fusion.2), channel_id=1, source_target_pairs={{0,4},{1,3},{2,6},{3,1},{4,0},{5,7},{6,2},{7,5},{8,12},{9,11},{10,... | collective-permute-start | bytes 1376264 | tf_op jit(solution)/shard_map/ppermute | solution.py:575
  102.2 0.1 convert_add_fusion
  102.3 4.5 %collective-permute-done.31 = bf16[112,1024]{1,0:T(8,128)(2,1)S(1)} collective-permute-done((bf16[112,1024]{1,0:T(8,128)(2,1)S(1)}, bf16[112,1024]{1,0:T(8,128)(2,1)S(1)}, u32[]{:S(2)}, u32[]{:S(2)}) %collective-permute-start.31) | collective-permute-done | bytes 229408 | tf_op jit(solution)/shard_map/ppermute | solution.py:575
  106.8 4.9 %collective-permute-done.29 = bf16[112,1024]{1,0:T(8,128)(2,1)S(1)} collective-permute-done((bf16[112,1024]{1,0:T(8,128)(2,1)S(1)}, bf16[112,1024]{1,0:T(8,128)(2,1)S(1)}, u32[]{:S(2)}, u32[]{:S(2)}) %collective-permute-start.29) | collective-permute-done | bytes 229408 | tf_op jit(solution)/shard_map/ppermute | solution.py:575
  111.7 0.3 add_convert_fusion
  112.0 0.9 reshape.45
  (58 shorter events, 0.2 us)
Async XLA Ops:
  0.6 41.8 %collective-permute-start.4 = (bf16[4096,256]{1,0:T(8,128)(2,1)}, bf16[4096,256]{1,0:T(8,128)(2,1)}, u32[]{:S(2)}, u32[]{:S(2)}) collective-permute-start(bf16[4096,256]{1,0:T(8,128)(2,1)} %refs_0_.1), channel_id=1, source_target_pairs={{0,1},{1,0},{2,3},{3,2},{4,5},{5,4},{6,7},{7,6},{8,9},{9,8},{10,11... | collective-permute-start | bytes 6291464 | tf_op jit(solution)/shard_map/ppermute | solution.py:565
  1.1 1.2 %copy-start.3 = (bf16[18,24,1024]{2,1,0:T(8,128)(2,1)S(1)}, bf16[18,24,1024]{2,1,0:T(8,128)(2,1)}, u32[]{:S(2)}) copy-start(bf16[18,24,1024]{2,1,0:T(8,128)(2,1)} %tokens_ref.5) | copy-start | bytes 2654212
  2.3 7.8 %copy-start.4 = (bf16[18,24,1024]{2,1,0:T(8,128)(2,1)S(1)}, bf16[18,24,1024]{2,1,0:T(8,128)(2,1)}, u32[]{:S(2)}) copy-start(bf16[18,24,1024]{2,1,0:T(8,128)(2,1)} %tokens_ref.5) | copy-start | bytes 2654212
  5.3 11.1 %collective-permute-start.1 = (bf16[18,8,1024]{2,1,0:T(8,128)(2,1)S(1)}, bf16[18,8,1024]{2,1,0:T(8,128)(2,1)S(1)}, u32[]{:S(2)}, u32[]{:S(2)}) collective-permute-start(bf16[18,8,1024]{2,1,0:T(8,128)(2,1)S(1)} %get-tuple-element.49), channel_id=1, source_target_pairs={{0,7},{1,0},{2,1},{3,2},{4,3},{5,4},{6,5},{7,6},{8,15},{9,8},{10,9... | collective-permute-start | bytes 884744 | tf_op jit(solution)/shard_map/ppermute | solution.py:405
  8.9 10.3 %collective-permute-start = (bf16[18,8,1024]{2,1,0:T(8,128)(2,1)S(1)}, bf16[18,8,1024]{2,1,0:T(8,128)(2,1)S(1)}, u32[]{:S(2)}, u32[]{:S(2)}) collective-permute-start(bf16[18,8,1024]{2,1,0:T(8,128)(2,1)S(1)} %get-tuple-element.48), channel_id=1, source_target_pairs={{0,1},{1,2},{2,3},{3,4},{4,5},{5,6},{6,7},{7,0},{8,9},{9,10},{10,1... | collective-permute-start | bytes 884744 | tf_op jit(solution)/shard_map/ppermute | solution.py:405
  8.9 28.7 %collective-permute-start.5 = (bf16[2048,256]{1,0:T(8,128)(2,1)}, bf16[2048,256]{1,0:T(8,128)(2,1)}, u32[]{:S(2)}, u32[]{:S(2)}) collective-permute-start(bf16[2048,256]{1,0:T(8,128)(2,1)} %get-tuple-element.57), channel_id=1, source_target_pairs={{0,2},{1,3},{2,0},{3,1},{4,6},{5,7},{6,4},{7,5},{8,10},{9,11},{10,... | collective-permute-start | bytes 3145736 | tf_op jit(solution)/shard_map/ppermute | solution.py:570
  8.9 29.0 %collective-permute-start.6 = (bf16[2048,256]{1,0:T(8,128)(2,1)}, bf16[2048,256]{1,0:T(8,128)(2,1)}, u32[]{:S(2)}, u32[]{:S(2)}) collective-permute-start(bf16[2048,256]{1,0:T(8,128)(2,1)} %get-tuple-element.58), channel_id=1, source_target_pairs={{0,4},{1,5},{2,6},{3,7},{4,0},{5,1},{6,2},{7,3},{8,12},{9,13},{10,... | collective-permute-start | bytes 3145736 | tf_op jit(solution)/shard_map/ppermute | solution.py:570
  10.1 14.1 %copy-start.7 = (bf16[576,144]{1,0:T(8,128)(2,1)S(1)}, bf16[576,144]{1,0:T(8,128)(2,1)}, u32[]{:S(2)}) copy-start(bf16[576,144]{1,0:T(8,128)(2,1)} %constant.71.clone.rest_1_) | copy-start | bytes 497668
  10.1 14.1 %copy-start.8 = (bf16[576,256]{1,0:T(8,128)(2,1)S(1)}, bf16[576,256]{1,0:T(8,128)(2,1)}, u32[]{:S(2)}) copy-start(bf16[576,256]{1,0:T(8,128)(2,1)} %constant.72.clone.rest_2_) | copy-start | bytes 884740
  10.2 14.1 %copy-start.9 = (bf16[144,576]{1,0:T(8,128)(2,1)S(1)}, bf16[144,576]{1,0:T(8,128)(2,1)}, u32[]{:S(2)}) copy-start(bf16[144,576]{1,0:T(8,128)(2,1)} %constant.73.clone.rest_3_) | copy-start | bytes 497668
  10.2 14.1 %copy-start.13 = (bf16[240,240]{1,0:T(8,128)(2,1)S(1)}, bf16[240,240]{1,0:T(8,128)(2,1)}, u32[]{:S(2)}) copy-start(bf16[240,240]{1,0:T(8,128)(2,1)} %constant.70.clone.rest_0_) | copy-start | bytes 345604
  19.2 10.2 %collective-permute-start.2 = (bf16[3,40,1024]{2,1,0:T(8,128)(2,1)S(1)}, bf16[3,40,1024]{2,1,0:T(8,128)(2,1)S(1)}, u32[]{:S(2)}, u32[]{:S(2)}) collective-permute-start(bf16[3,40,1024]{2,1,0:T(8,128)(2,1)S(1)} %pad_maximum_fusion.1), channel_id=1, source_target_pairs={{0,8},{8,16},{16,24},{1,9},{9,17},{17,25},{2,10},{10,18},{18,26},{... | collective-permute-start | bytes 737288 | tf_op jit(solution)/shard_map/ppermute | solution.py:405
  22.8 8.1 %collective-permute-start.3 = (bf16[3,40,1024]{2,1,0:T(8,128)(2,1)S(1)}, bf16[3,40,1024]{2,1,0:T(8,128)(2,1)S(1)}, u32[]{:S(2)}, u32[]{:S(2)}) collective-permute-start(bf16[3,40,1024]{2,1,0:T(8,128)(2,1)S(1)} %pad_maximum_fusion.2), channel_id=1, source_target_pairs={{8,0},{16,8},{24,16},{9,1},{17,9},{25,17},{10,2},{18,10},{26,18},{... | collective-permute-start | bytes 737288 | tf_op jit(solution)/shard_map/ppermute | solution.py:405
  24.3 6.6 %copy-start.5 = (bf16[1024,1024]{1,0:T(8,128)(2,1)S(1)}, bf16[1024,1024]{1,0:T(8,128)(2,1)}, u32[]{:S(2)}) copy-start(bf16[1024,1024]{1,0:T(8,128)(2,1)} %out_w_ref.1) | copy-start | bytes 6291460
  24.3 6.6 %copy-start.6 = (bf16[448,432]{1,0:T(8,128)(2,1)S(1)}, bf16[448,432]{1,0:T(8,128)(2,1)}, u32[]{:S(2)}) copy-start(bf16[448,432]{1,0:T(8,128)(2,1)} %constant.74.clone.patch_ref) | copy-start | bytes 1161220
  24.3 6.6 %copy-start.10 = (bf16[304,256]{1,0:T(8,128)(2,1)S(1)}, bf16[304,256]{1,0:T(8,128)(2,1)}, u32[]{:S(2)}) copy-start(bf16[304,256]{1,0:T(8,128)(2,1)} %constant.77.clone.rest_2_.rest_6_) | copy-start | bytes 466948
  24.3 6.5 %copy-start.11 = (bf16[240,256]{1,0:T(8,128)(2,1)S(1)}, bf16[240,256]{1,0:T(8,128)(2,1)}, u32[]{:S(2)}) copy-start(bf16[240,256]{1,0:T(8,128)(2,1)} %constant.75.clone.rest_0_) | copy-start | bytes 368644
  24.3 6.5 %copy-start.12 = (bf16[240,256]{1,0:T(8,128)(2,1)S(1)}, bf16[240,256]{1,0:T(8,128)(2,1)}, u32[]{:S(2)}) copy-start(bf16[240,256]{1,0:T(8,128)(2,1)} %constant.79.clone.rest_4_) | copy-start | bytes 368644
  24.4 6.5 %copy-start.14 = (bf16[304,80]{1,0:T(8,128)(2,1)S(1)}, bf16[304,80]{1,0:T(8,128)(2,1)}, u32[]{:S(2)}) copy-start(bf16[304,80]{1,0:T(8,128)(2,1)} %constant.76.clone.rest_1_.rest_5_) | copy-start | bytes 145924
  24.4 6.5 %copy-start.15 = (bf16[80,304]{1,0:T(8,128)(2,1)S(1)}, bf16[80,304]{1,0:T(8,128)(2,1)}, u32[]{:S(2)}) copy-start(bf16[80,304]{1,0:T(8,128)(2,1)} %constant.78.clone.rest_3_.rest_7_) | copy-start | bytes 145924
  30.9 11.6 %copy-start.2 = (bf16[4096,256]{1,0:T(8,128)(2,1)S(1)}, bf16[4096,256]{1,0:T(8,128)(2,1)}, u32[]{:S(2)}) copy-start(bf16[4096,256]{1,0:T(8,128)(2,1)} %refs_0_.1) | copy-start | bytes 6291460
  38.0 4.5 %collective-permute-start.7 = (bf16[2048,256]{1,0:T(8,128)(2,1)}, bf16[2048,256]{1,0:T(8,128)(2,1)S(1)}, u32[]{:S(2)}, u32[]{:S(2)}) collective-permute-start(bf16[2048,256]{1,0:T(8,128)(2,1)} %collective-permute-done.5.refs_2_), channel_id=1, source_target_pairs={{0,1},{1,0},{2,3},{3,2},{4,5},{5,4},{6,7},{7,6},{8,9},{9,8},{10,11... | collective-permute-start | bytes 3145736 | tf_op jit(solution)/shard_map/ppermute | solution.py:565
  38.3 4.2 %collective-permute-start.8 = (bf16[2048,256]{1,0:T(8,128)(2,1)}, bf16[2048,256]{1,0:T(8,128)(2,1)}, u32[]{:S(2)}, u32[]{:S(2)}) collective-permute-start(bf16[2048,256]{1,0:T(8,128)(2,1)} %collective-permute-done.6.refs_4_), channel_id=1, source_target_pairs={{0,1},{1,0},{2,3},{3,2},{4,5},{5,4},{6,7},{7,6},{8,9},{9,8},{10,11... | collective-permute-start | bytes 3145736 | tf_op jit(solution)/shard_map/ppermute | solution.py:565
  38.5 13.3 %collective-permute-start.9 = (bf16[112,2048]{1,0:T(8,128)(2,1)}, bf16[112,2048]{1,0:T(8,128)(2,1)}, u32[]{:S(2)}, u32[]{:S(2)}) collective-permute-start(bf16[112,2048]{1,0:T(8,128)(2,1)} %get-tuple-element.55.upper_ref), channel_id=1, source_target_pairs={{0,4},{1,5},{2,6},{3,7},{4,0},{5,1},{6,2},{7,3},{8,12},{9,13},{10,... | collective-permute-start | bytes 1376264 | tf_op jit(solution)/shard_map/ppermute | solution.py:570
  40.3 13.0 %collective-permute-start.10 = (bf16[112,2048]{1,0:T(8,128)(2,1)}, bf16[112,2048]{1,0:T(8,128)(2,1)}, u32[]{:S(2)}, u32[]{:S(2)}) collective-permute-start(bf16[112,2048]{1,0:T(8,128)(2,1)} %get-tuple-element.56.lower_ref), channel_id=1, source_target_pairs={{0,2},{1,3},{2,0},{3,1},{4,6},{5,7},{6,4},{7,5},{8,10},{9,11},{10,... | collective-permute-start | bytes 1376264 | tf_op jit(solution)/shard_map/ppermute | solution.py:570
  53.3 12.7 %copy-start = (bf16[2048,1024]{1,0:T(8,128)(2,1)S(1)}, bf16[2048,1024]{1,0:T(8,128)(2,1)}, u32[]{:S(2)}) copy-start(bf16[2048,1024]{1,0:T(8,128)(2,1)} %up_ref.7) | copy-start | bytes 12582916
  53.3 12.7 %copy-start.1 = (bf16[1024,2048]{1,0:T(8,128)(2,1)S(1)}, bf16[1024,2048]{1,0:T(8,128)(2,1)}, u32[]{:S(2)}) copy-start(bf16[1024,2048]{1,0:T(8,128)(2,1)} %down_ref.7) | copy-start | bytes 12582916
  56.1 6.9 %collective-permute-start.11 = (bf16[112,1024]{1,0:T(8,128)(2,1)S(1)}, bf16[112,1024]{1,0:T(8,128)(2,1)S(1)}, u32[]{:S(2)}, u32[]{:S(2)}) collective-permute-start(bf16[112,1024]{1,0:T(8,128)(2,1)S(1)} %get-tuple-element.70), channel_id=1, source_target_pairs={{0,4},{1,5},{2,6},{3,7},{4,0},{5,1},{6,2},{7,3},{8,12},{9,13},{10,... | collective-permute-start | bytes 688136 | tf_op jit(solution)/shard_map/ppermute | solution.py:570
  56.5 7.0 %collective-permute-start.12 = (bf16[112,1024]{1,0:T(8,128)(2,1)S(1)}, bf16[112,1024]{1,0:T(8,128)(2,1)S(1)}, u32[]{:S(2)}, u32[]{:S(2)}) collective-permute-start(bf16[112,1024]{1,0:T(8,128)(2,1)S(1)} %get-tuple-element.71), channel_id=1, source_target_pairs={{0,2},{1,3},{2,0},{3,1},{4,6},{5,7},{6,4},{7,5},{8,10},{9,11},{10,... | collective-permute-start | bytes 688136 | tf_op jit(solution)/shard_map/ppermute | solution.py:570
  64.1 1.9 %collective-permute-start.14 = (bf16[112,2048]{1,0:T(8,128)(2,1)S(1)}, bf16[112,2048]{1,0:T(8,128)(2,1)S(1)}, u32[]{:S(2)}, u32[]{:S(2)}) collective-permute-start(bf16[112,2048]{1,0:T(8,128)(2,1)S(1)} %combine.1.mine_ref), channel_id=1, source_target_pairs={{0,1},{1,0},{2,3},{3,2},{4,5},{5,4},{6,7},{7,6},{8,9},{9,8},{10,11... | collective-permute-start | bytes 1376264 | tf_op jit(solution)/shard_map/ppermute | solution.py:565
  64.1 8.5 %collective-permute-start.13 = (bf16[112,2048]{1,0:T(8,128)(2,1)S(1)}, bf16[112,2048]{1,0:T(8,128)(2,1)S(1)}, u32[]{:S(2)}, u32[]{:S(2)}) collective-permute-start(bf16[112,2048]{1,0:T(8,128)(2,1)S(1)} %combine.1.mine_ref), channel_id=1, source_target_pairs={{0,2},{1,5},{2,0},{3,7},{4,6},{5,1},{6,4},{7,3},{8,10},{9,13},{10,... | collective-permute-start | bytes 1376264 | tf_op jit(solution)/shard_map/ppermute | solution.py:575
  72.7 1.8 %collective-permute-start.17 = (bf16[112,2048]{1,0:T(8,128)(2,1)S(1)}, bf16[112,2048]{1,0:T(8,128)(2,1)S(1)}, u32[]{:S(2)}, u32[]{:S(2)}) collective-permute-start(bf16[112,2048]{1,0:T(8,128)(2,1)S(1)} %collective-permute-done.13.mine_ref), channel_id=1, source_target_pairs={{0,1},{1,0},{2,3},{3,2},{4,5},{5,4},{6,7},{7,6},{8,9},{9,8},{10,11... | collective-permute-start | bytes 1376264 | tf_op jit(solution)/shard_map/ppermute | solution.py:565
  72.7 8.5 %collective-permute-start.19 = (bf16[112,2048]{1,0:T(8,128)(2,1)S(1)}, bf16[112,2048]{1,0:T(8,128)(2,1)S(1)}, u32[]{:S(2)}, u32[]{:S(2)}) collective-permute-start(bf16[112,2048]{1,0:T(8,128)(2,1)S(1)} %collective-permute-done.13.mine_ref), channel_id=1, source_target_pairs={{0,4},{1,3},{2,6},{3,1},{4,0},{5,7},{6,2},{7,5},{8,12},{9,11},{10,... | collective-permute-start | bytes 1376264 | tf_op jit(solution)/shard_map/ppermute | solution.py:575
  77.1 4.1 %collective-permute-start.18 = (bf16[112,1024]{1,0:T(8,128)(2,1)S(1)}, bf16[112,1024]{1,0:T(8,128)(2,1)S(1)}, u32[]{:S(2)}, u32[]{:S(2)}) collective-permute-start(bf16[112,1024]{1,0:T(8,128)(2,1)S(1)} %get-tuple-element.79), channel_id=1, source_target_pairs={{0,1},{1,0},{2,3},{3,2},{4,5},{5,4},{6,7},{7,6},{8,9},{9,8},{10,11... | collective-permute-start | bytes 688136 | tf_op jit(solution)/shard_map/ppermute | solution.py:565
  81.2 1.8 %collective-permute-start.20 = (bf16[112,2048]{1,0:T(8,128)(2,1)S(1)}, bf16[112,2048]{1,0:T(8,128)(2,1)S(1)}, u32[]{:S(2)}, u32[]{:S(2)}) collective-permute-start(bf16[112,2048]{1,0:T(8,128)(2,1)S(1)} %collective-permute-done.19.mine_ref), channel_id=1, source_target_pairs={{0,1},{1,0},{2,3},{3,2},{4,5},{5,4},{6,7},{7,6},{8,9},{9,8},{10,11... | collective-permute-start | bytes 1376264 | tf_op jit(solution)/shard_map/ppermute | solution.py:565
  81.2 8.5 %collective-permute-start.22 = (bf16[112,2048]{1,0:T(8,128)(2,1)S(1)}, bf16[112,2048]{1,0:T(8,128)(2,1)S(1)}, u32[]{:S(2)}, u32[]{:S(2)}) collective-permute-start(bf16[112,2048]{1,0:T(8,128)(2,1)S(1)} %combine.1.mine_ref), channel_id=1, source_target_pairs={{0,4},{1,3},{2,6},{3,1},{4,0},{5,7},{6,2},{7,5},{8,12},{9,11},{10,... | collective-permute-start | bytes 1376264 | tf_op jit(solution)/shard_map/ppermute | solution.py:575
  85.6 4.1 %collective-permute-start.21 = (bf16[112,1024]{1,0:T(8,128)(2,1)S(1)}, bf16[112,1024]{1,0:T(8,128)(2,1)S(1)}, u32[]{:S(2)}, u32[]{:S(2)}) collective-permute-start(bf16[112,1024]{1,0:T(8,128)(2,1)S(1)} %get-tuple-element.81), channel_id=1, source_target_pairs={{0,1},{1,0},{2,3},{3,2},{4,5},{5,4},{6,7},{7,6},{8,9},{9,8},{10,11... | collective-permute-start | bytes 688136 | tf_op jit(solution)/shard_map/ppermute | solution.py:565
  85.8 3.8 %collective-permute-start.27 = (bf16[112,1024]{1,0:T(8,128)(2,1)S(1)}, bf16[112,1024]{1,0:T(8,128)(2,1)S(1)}, u32[]{:S(2)}, u32[]{:S(2)}) collective-permute-start(bf16[112,1024]{1,0:T(8,128)(2,1)S(1)} %get-tuple-element.92), channel_id=1, source_target_pairs={{0,1},{1,0},{2,3},{3,2},{4,5},{5,4},{6,7},{7,6},{8,9},{9,8},{10,11... | collective-permute-start | bytes 688136 | tf_op jit(solution)/shard_map/ppermute | solution.py:565
  89.7 2.2 %collective-permute-start.23 = (bf16[112,2048]{1,0:T(8,128)(2,1)S(1)}, bf16[112,2048]{1,0:T(8,128)(2,1)S(1)}, u32[]{:S(2)}, u32[]{:S(2)}) collective-permute-start(bf16[112,2048]{1,0:T(8,128)(2,1)S(1)} %collective-permute-done.22.mine_ref), channel_id=1, source_target_pairs={{0,1},{1,0},{2,3},{3,2},{4,5},{5,4},{6,7},{7,6},{8,9},{9,8},{10,11... | collective-permute-start | bytes 1376264 | tf_op jit(solution)/shard_map/ppermute | solution.py:565
  89.8 8.5 %collective-permute-start.28 = (bf16[112,2048]{1,0:T(8,128)(2,1)S(1)}, bf16[112,2048]{1,0:T(8,128)(2,1)S(1)}, u32[]{:S(2)}, u32[]{:S(2)}) collective-permute-start(bf16[112,2048]{1,0:T(8,128)(2,1)S(1)} %add_convert_fusion.1), channel_id=1, source_target_pairs={{0,4},{1,3},{2,6},{3,1},{4,0},{5,7},{6,2},{7,5},{8,12},{9,11},{10,... | collective-permute-start | bytes 1376264 | tf_op jit(solution)/shard_map/ppermute | solution.py:575
  91.2 3.7 %collective-permute-start.30 = (bf16[112,1024]{1,0:T(8,128)(2,1)S(1)}, bf16[112,1024]{1,0:T(8,128)(2,1)S(1)}, u32[]{:S(2)}, u32[]{:S(2)}) collective-permute-start(bf16[112,1024]{1,0:T(8,128)(2,1)S(1)} %get-tuple-element.93), channel_id=1, source_target_pairs={{0,1},{1,0},{2,3},{3,2},{4,5},{5,4},{6,7},{7,6},{8,9},{9,8},{10,11... | collective-permute-start | bytes 688136 | tf_op jit(solution)/shard_map/ppermute | solution.py:565
  91.3 10.9 %collective-permute-start.16 = (bf16[112,1024]{1,0:T(8,128)(2,1)S(1)}, bf16[112,1024]{1,0:T(8,128)(2,1)S(1)}, u32[]{:S(2)}, u32[]{:S(2)}) collective-permute-start(bf16[112,1024]{1,0:T(8,128)(2,1)S(1)} %get-tuple-element.77), channel_id=1, source_target_pairs={{0,1},{1,0},{2,3},{3,2},{4,5},{5,4},{6,7},{7,6},{8,9},{9,8},{10,11... | collective-permute-start | bytes 688136 | tf_op jit(solution)/shard_map/ppermute | solution.py:565
  91.7 10.5 %collective-permute-start.15 = (bf16[112,1024]{1,0:T(8,128)(2,1)S(1)}, bf16[112,1024]{1,0:T(8,128)(2,1)S(1)}, u32[]{:S(2)}, u32[]{:S(2)}) collective-permute-start(bf16[112,1024]{1,0:T(8,128)(2,1)S(1)} %get-tuple-element.76), channel_id=1, source_target_pairs={{0,1},{1,0},{2,3},{3,2},{4,5},{5,4},{6,7},{7,6},{8,9},{9,8},{10,11... | collective-permute-start | bytes 688136 | tf_op jit(solution)/shard_map/ppermute | solution.py:565
  94.5 5.5 %collective-permute-start.25 = (bf16[112,1024]{1,0:T(8,128)(2,1)S(1)}, bf16[112,1024]{1,0:T(8,128)(2,1)S(1)}, u32[]{:S(2)}, u32[]{:S(2)}) collective-permute-start(bf16[112,1024]{1,0:T(8,128)(2,1)S(1)} %get-tuple-element.87), channel_id=1, source_target_pairs={{0,1},{1,0},{2,3},{3,2},{4,5},{5,4},{6,7},{7,6},{8,9},{9,8},{10,11... | collective-permute-start | bytes 688136 | tf_op jit(solution)/shard_map/ppermute | solution.py:565
  94.9 5.8 %collective-permute-start.24 = (bf16[112,1024]{1,0:T(8,128)(2,1)S(1)}, bf16[112,1024]{1,0:T(8,128)(2,1)S(1)}, u32[]{:S(2)}, u32[]{:S(2)}) collective-permute-start(bf16[112,1024]{1,0:T(8,128)(2,1)S(1)} %get-tuple-element.86), channel_id=1, source_target_pairs={{0,1},{1,0},{2,3},{3,2},{4,5},{5,4},{6,7},{7,6},{8,9},{9,8},{10,11... | collective-permute-start | bytes 688136 | tf_op jit(solution)/shard_map/ppermute | solution.py:565
  98.6 8.2 %collective-permute-start.31 = (bf16[112,1024]{1,0:T(8,128)(2,1)S(1)}, bf16[112,1024]{1,0:T(8,128)(2,1)S(1)}, u32[]{:S(2)}, u32[]{:S(2)}) collective-permute-start(bf16[112,1024]{1,0:T(8,128)(2,1)S(1)} %get-tuple-element.95), channel_id=1, source_target_pairs={{0,2},{1,5},{2,0},{3,7},{4,6},{5,1},{6,4},{7,3},{8,10},{9,13},{10,... | collective-permute-start | bytes 688136 | tf_op jit(solution)/shard_map/ppermute | solution.py:575
  99.9 11.8 %collective-permute-start.29 = (bf16[112,1024]{1,0:T(8,128)(2,1)S(1)}, bf16[112,1024]{1,0:T(8,128)(2,1)S(1)}, u32[]{:S(2)}, u32[]{:S(2)}) collective-permute-start(bf16[112,1024]{1,0:T(8,128)(2,1)S(1)} %get-tuple-element.94), channel_id=1, source_target_pairs={{0,2},{1,5},{2,0},{3,7},{4,6},{5,1},{6,4},{7,3},{8,10},{9,13},{10,... | collective-permute-start | bytes 688136 | tf_op jit(solution)/shard_map/ppermute | solution.py:575
  100.8 10.9 %collective-permute-start.26 = (bf16[112,2048]{1,0:T(8,128)(2,1)S(1)}, bf16[112,2048]{1,0:T(8,128)(2,1)S(1)}, u32[]{:S(2)}, u32[]{:S(2)}) collective-permute-start(bf16[112,2048]{1,0:T(8,128)(2,1)S(1)} %add_convert_fusion.2), channel_id=1, source_target_pairs={{0,4},{1,3},{2,6},{3,1},{4,0},{5,7},{6,2},{7,5},{8,12},{9,11},{10,... | collective-permute-start | bytes 1376264 | tf_op jit(solution)/shard_map/ppermute | solution.py:575

commit v9 on v8

--- a/solution.py
+++ b/solution.py
@@ -147,7 +147,26 @@
     return jnp.concatenate([values, jnp.zeros((total - values.shape[0], values.shape[1]), values.dtype)], axis=0)
 
 
-def prepare_kernel(tokens_ref, weight_ref, east_ref, west_ref, upper_ref, lower_ref, sems):
+def rims_kernel(tokens_ref, east_ref, west_ref):
+    columns = tokens_ref.shape[1]
+    east_ref[...] = tokens_ref[:, columns - SIDE :]
+    west_ref[...] = tokens_ref[:, :SIDE]
+
+
+def rims(tokens):
+    rows, _, width = tokens.shape
+    vmem = pl.BlockSpec(memory_space=pltpu.VMEM)
+    return pl.pallas_call(
+        rims_kernel,
+        in_specs=[vmem],
+        out_specs=[vmem] * 2,
+        out_shape=[jax.ShapeDtypeStruct((rows, SIDE, width), BF16)] * 2,
+        compiler_params=params(16),
+        name="rims",
+    )(tokens)
+
+
+def halves_kernel(weight_ref, upper_ref, lower_ref, sems):
     half = upper_ref.shape[0]
     copies = [
         pltpu.make_async_copy(weight_ref.at[k * half : (k + 1) * half], ref, sems.at[k])
@@ -155,27 +174,21 @@
     ]
     for copy in copies:
         copy.start()
-    columns = tokens_ref.shape[1]
-    east_ref[...] = tokens_ref[:, columns - SIDE :]
-    west_ref[...] = tokens_ref[:, :SIDE]
     for copy in copies:
         copy.wait()
 
 
-def prepare(tokens, merge_weight):
-    rows, _, width = tokens.shape
-    depth, block = merge_weight.shape
-    vmem, anywhere = pl.BlockSpec(memory_space=pltpu.VMEM), pl.BlockSpec(memory_space=pl.ANY)
+def halves_of(weight):
+    depth, block = weight.shape
     return pl.pallas_call(
-        prepare_kernel,
-        in_specs=[vmem, anywhere],
-        out_specs=[vmem] * 4,
-        out_shape=[jax.ShapeDtypeStruct((rows, SIDE, width), BF16)] * 2
-        + [jax.ShapeDtypeStruct((depth // 2, block), BF16)] * 2,
+        halves_kernel,
+        in_specs=[pl.BlockSpec(memory_space=pl.ANY)],
+        out_specs=[pl.BlockSpec(memory_space=pltpu.VMEM)] * 2,
+        out_shape=[jax.ShapeDtypeStruct((depth // 2, block), BF16)] * 2,
         scratch_shapes=[pltpu.SemaphoreType.DMA((2,))],
         compiler_params=params(52),
-        name="prepare",
-    )(tokens, merge_weight)
+        name="halves",
+    )(weight)
 
 
 def own_kernel(bands, tokens_ref, weight_ref, out_ref, kv_ref, normed_ref, q_ref, sems):
@@ -357,11 +370,11 @@
     )(*args)
 
 
-def attention(bands, tokens, rims, qkv_weight, out_weight):
+def attention(bands, tokens, sides, qkv_weight, out_weight):
     rows, columns, width = tokens.shape
     block = width * GROUP // HEADS
-    west = shift(rims[0], "lon", 1, True)
-    east = shift(rims[1], "lon", -1, True)
+    west = shift(sides[0], "lon", 1, True)
+    east = shift(sides[1], "lon", -1, True)
     own, kv_weight = own_projection(bands, tokens, qkv_weight)
 
     def slab(part):
@@ -616,10 +629,11 @@
     rows, columns, width = tokens.shape
     bands = Bands(rows, columns)
     cells = rows * columns // 4
-    *rims, upper_weight, lower_weight = prepare(tokens, merge_weight)
-    middle_out, upper, lower = attention(bands, tokens, rims, qkv_weight, out_weight)
+    sides = rims(tokens)
+    *sides, later = lax.optimization_barrier((*sides, merge_weight))
+    halves = halves_of(later)
+    middle_out, upper, lower = attention(bands, tokens, sides, qkv_weight, out_weight)
     coarse = coarse_by_squares if lax.axis_size("lon") == 8 else coarse_by_chips
-    halves = [upper_weight, lower_weight]
     total = coarse(upper, lower, merge_weight, halves, up_weight, down_weight)
     coarse_out = total[:cells].astype(jnp.bfloat16)
     return (middle_out, coarse_out.reshape(rows // 2, columns // 2, -1))

time: 113 us -> 111 us (0.982)
  starting transfers between devices: 27.7 us -> 22 us
  waiting for transfers between devices: 42.3 us -> 46.3 us
    ppermute x15, waiting for transfers between devices: 1.46 us -> 6.13 us  [core_swap(): return lax.ppermute(value, 'lon', [(i, i ^ 1) for i in range(size)])]
    ppermute x7, starting transfers between devices: 8.89 us -> 5.27 us  [cross(): lax.ppermute(value, 'lon', [(i, i ^ 2 * (second if i % 2 else first)) for...]
    ppermute x6, starting transfers between devices: 7.08 us -> 5.16 us  [chip_swap(): lax.ppermute(value, 'lon', [(i, i ^ 2 * offset) for i in range(size)])]
    pallas_call x1 -> x2, Pallas kernels: 3 us -> 2.96 us  [the longest x1 2.92 us: halves_of(): pl.pallas_call(halves_kernel, in_specs=[pl.BlockSpec(memory_space=pl.ANY)...]
  transfers between devices with their start and end apart: 32 -> 32, of which waited for: 17 -> 18; matrix products, arithmetic and copies ran while one was open for 1% -> 1% of each run, Pallas kernels for 31% -> 32%
where the time goes in v9:
time: 111 us
  waiting for transfers between devices  46.3 us (42%)
  Pallas kernels  38.7 us (35%)
  starting transfers between devices  22 us (20%)
  local copies, waits for them, and re-layouts  2.2 us (2%)
    ppermute x7, waiting for transfers between devices, cross(): lax.ppermute(value, 'lon', [(i, i ^ 2 * (second if i % 2 else first)) for...  25.2 us
    pallas_call x2, Pallas kernels, vmem_call(): pl.pallas_call(kernel, in_specs=[vmem] * len(args), out_specs=[vmem] * le...  11.8 us
    ppermute x6, waiting for transfers between devices, chip_swap(): lax.ppermute(value, 'lon', [(i, i ^ 2 * offset) for i in range(size)])  10.9 us
    pallas_call x4, Pallas kernels, feed_forward(): pl.pallas_call(ffn_kernel, in_specs=[vmem] * 4, out_specs=[vmem] * 3, out...  10.4 us
    ppermute x4, starting transfers between devices, shift(): return lax.ppermute(part, axis, pairs)  8.58 us
    pallas_call x3, Pallas kernels, local_call(): pl.pallas_call(kernel, in_specs=[pl.BlockSpec(memory_space=pltpu.SMEM)] +...  8.14 us
    ppermute x15, waiting for transfers between devices, core_swap(): return lax.ppermute(value, 'lon', [(i, i ^ 1) for i in range(size)])  6.13 us
    pallas_call x1, Pallas kernels, own_projection(): pl.pallas_call(functools.partial(own_kernel, bands), in_specs=[vmem, pl.B...  5.35 us
  transfers between devices with their start and end apart: 32, of which 18 were waited for; matrix products, arithmetic and copies ran while one was open for 1% of the time, Pallas kernels for 32%

profile of v9, /device:TPU:0, one launch (start us, length us, event | category | flops | bytes accessed | tf_op | source)
XLA Modules:
  0.0 111.3 jit_solution(15614581074014869627)
XLA Ops:
  0.6 0.5 collective-permute-start.4
  1.1 1.2 %copy-done.3 = bf16[18,24,1024]{2,1,0:T(8,128)(2,1)S(1)} copy-done((bf16[18,24,1024]{2,1,0:T(8,128)(2,1)S(1)}, bf16[18,24,1024]{2,1,0:T(8,128)(2,1)}, u32[]{:S(2)}) %copy-start.3) | copy-done | bytes 884760
  2.4 3.6 %collective-permute-start.1 = (bf16[18,8,1024]{2,1,0:T(8,128)(2,1)S(1)}, bf16[18,8,1024]{2,1,0:T(8,128)(2,1)S(1)}, u32[]{:S(2)}, u32[]{:S(2)}) collective-permute-start(bf16[18,8,1024]{2,1,0:T(8,128)(2,1)S(1)} %get-tuple-element.54), channel_id=1, source_target_pairs={{0,7},{1,0},{2,1},{3,2},{4,3},{5,4},{6,5},{7,6},{8,15},{9,8},{10,9... | collective-permute-start | bytes 884744 | tf_op jit(solution)/shard_map/ppermute | solution.py:418
  6.0 2.9 %halves.1 = (bf16[2048,256]{1,0:T(8,128)(2,1)}, bf16[2048,256]{1,0:T(8,128)(2,1)}) custom-call(bf16[4096,256]{1,0:T(8,128)(2,1)} %refs_0_.1), custom_call_target="tpu_custom_call" | custom-call | tf_op jit(solution)/shard_map/halves/pallas_call | solution.py:183
  8.9 0.1 collective-permute-start.5
  9.0 1.1 collective-permute-start.6
  10.2 5.4 %own_projection.1 = (bf16[448,3072]{1,0:T(8,128)(2,1)S(1)}, bf16[1024,2048]{1,0:T(8,128)(2,1)S(1)}) custom-call(bf16[18,24,1024]{2,1,0:T(8,128)(2,1)S(1)} %copy-done.4, bf16[1024,3072]{1,0:T(8,128)(2,1)} %weight_ref.1), custom_call_target="tpu_custom_call" | custom-call | flops 2818572288 | bytes 6291456 | tf_op jit(solution)/shard_map/own_projection/pallas_call | solution.py:223
  15.5 0.1 or_select_fusion.bias_ref
  15.6 0.3 collective-permute-done.west_ref
  16.0 3.5 %collective-permute-start.2 = (bf16[3,40,1024]{2,1,0:T(8,128)(2,1)S(1)}, bf16[3,40,1024]{2,1,0:T(8,128)(2,1)S(1)}, u32[]{:S(2)}, u32[]{:S(2)}) collective-permute-start(bf16[3,40,1024]{2,1,0:T(8,128)(2,1)S(1)} %pad_maximum_fusion.1), channel_id=1, source_target_pairs={{0,8},{8,16},{16,24},{1,9},{9,17},{17,25},{2,10},{10,18},{18,26},{... | collective-permute-start | bytes 737288 | tf_op jit(solution)/shard_map/ppermute | solution.py:418
  19.5 1.5 %collective-permute-start.3 = (bf16[3,40,1024]{2,1,0:T(8,128)(2,1)S(1)}, bf16[3,40,1024]{2,1,0:T(8,128)(2,1)S(1)}, u32[]{:S(2)}, u32[]{:S(2)}) collective-permute-start(bf16[3,40,1024]{2,1,0:T(8,128)(2,1)S(1)} %pad_maximum_fusion.2), channel_id=1, source_target_pairs={{8,0},{16,8},{24,16},{9,1},{17,9},{25,17},{10,2},{18,10},{26,18},{... | collective-permute-start | bytes 737288 | tf_op jit(solution)/shard_map/ppermute | solution.py:418
  21.2 5.0 %middle_attention.1 = (bf16[288,2048]{1,0:T(8,128)(2,1)S(1)}, bf16[288,1024]{1,0:T(8,128)(2,1)S(1)}) custom-call(bf16[18,8,1024]{2,1,0:T(8,128)(2,1)S(1)} %collective-permute-done.west_ref, bf16[18,8,1024]{2,1,0:T(8,128)(2,1)S(1)} %collective-permute-done.1.east_ref, bf16[448,3072]{1,0:T(8,128)(2,1)S(1)} %get-tuple-element.55.own_ref, ...), custom_call_target="tpu_custom_call" | custom-call | flops 5000000000 | bytes 1048576 | tf_op jit(solution)/shard_map/middle_attention/pallas_call | solution.py:361
  26.2 3.8 %collective-permute-done.3.south_ref = bf16[3,40,1024]{2,1,0:T(8,128)(2,1)S(1)} collective-permute-done((bf16[3,40,1024]{2,1,0:T(8,128)(2,1)S(1)}, bf16[3,40,1024]{2,1,0:T(8,128)(2,1)S(1)}, u32[]{:S(2)}, u32[]{:S(2)}) %collective-permute-start.3) | collective-permute-done | bytes 245792 | tf_op jit(solution)/shard_map/ppermute | solution.py:418
  30.1 6.8 %edge_attention.1 = (bf16[18,24,1024]{2,1,0:T(8,128)(2,1)}, bf16[112,2048]{1,0:T(8,128)(2,1)}, bf16[112,2048]{1,0:T(8,128)(2,1)}) custom-call(bf16[18,24,1024]{2,1,0:T(8,128)(2,1)S(1)} %copy-done.4, bf16[3,40,1024]{2,1,0:T(8,128)(2,1)S(1)} %collective-permute-done.2.north_ref, bf16[3,40,1024]{2,1,0:T(8,128)(2,1)S(1)} %collective-permute-done.3.south_ref, ...), custom_call_target="tpu_custom_call" | custom-call | flops 6000000000 | bytes 1048576 | tf_op jit(solution)/shard_map/edge_attention/pallas_call | solution.py:361
  36.8 0.5 collective-permute-start.7
  37.3 0.1 collective-permute-start.8
  37.4 0.7 collective-permute-start.9
  38.1 1.3 %collective-permute-start.10 = (bf16[112,2048]{1,0:T(8,128)(2,1)}, bf16[112,2048]{1,0:T(8,128)(2,1)}, u32[]{:S(2)}, u32[]{:S(2)}) collective-permute-start(bf16[112,2048]{1,0:T(8,128)(2,1)} %get-tuple-element.61.lower_ref), channel_id=1, source_target_pairs={{0,2},{1,3},{2,0},{3,1},{4,6},{5,7},{6,4},{7,5},{8,10},{9,11},{10,... | collective-permute-start | bytes 1376264 | tf_op jit(solution)/shard_map/ppermute | solution.py:583
  39.4 0.1 pad_add_fusion.place_ref
  39.5 1.1 collective-permute-done.7.refs_3_
  40.6 0.9 collective-permute-done.8.refs_5_
  41.5 4.7 %merge_own.1 = (f32[112,512]{1,0:T(8,128)S(1)}, f32[112,512]{1,0:T(8,128)S(1)}, f32[112,512]{1,0:T(8,128)S(1)}, bf16[4096,256]{1,0:T(8,128)(2,1)S(1)}, bf16[4096...) custom-call(s32[2]{0:T(128)S(1)} %pad_add_fusion.place_ref, ...), custom_call_target="tpu_custom_call" | custom-call | flops 939524096 | bytes 1048576 | tf_op jit(solution)/shard_map/merge_own/pallas_call | solution.py:496
  46.1 4.4 %collective-permute-done.9.upper_ref = bf16[112,2048]{1,0:T(8,128)(2,1)} collective-permute-done((bf16[112,2048]{1,0:T(8,128)(2,1)}, bf16[112,2048]{1,0:T(8,128)(2,1)}, u32[]{:S(2)}, u32[]{:S(2)}) %collective-permute-start.9) | collective-permute-done | bytes 458784 | tf_op jit(solution)/shard_map/ppermute | solution.py:583
  50.6 0.4 collective-permute-done.10.lower_ref
  51.0 2.8 %merge_other.1 = (bf16[112,1024]{1,0:T(8,128)(2,1)S(1)}, bf16[112,1024]{1,0:T(8,128)(2,1)S(1)}) custom-call(s32[2]{0:T(128)S(1)} %pad_add_fusion.place_ref, bf16[112,2048]{1,0:T(8,128)(2,1)} %collective-permute-done.9.upper_ref, bf16[112,2048]{1,0:T(8,128)(2,1)} %collective-permute-done.10.lower_ref, bf16[4096,256]{1,0:T(8,128)(2,1)S(1)} %get-tuple-element.70.refs_0_, ...), custom_call_target="tpu_custom_call" | custom-call | flops 939524096 | bytes 1048576 | tf_op jit(solution)/shard_map/merge_other/pallas_call | solution.py:496
  53.8 1.4 %collective-permute-start.11 = (bf16[112,1024]{1,0:T(8,128)(2,1)S(1)}, bf16[112,1024]{1,0:T(8,128)(2,1)S(1)}, u32[]{:S(2)}, u32[]{:S(2)}) collective-permute-start(bf16[112,1024]{1,0:T(8,128)(2,1)S(1)} %get-tuple-element.76), channel_id=1, source_target_pairs={{0,4},{1,5},{2,6},{3,7},{4,0},{5,1},{6,2},{7,3},{8,12},{9,13},{10,... | collective-permute-start | bytes 688136 | tf_op jit(solution)/shard_map/ppermute | solution.py:583
  55.2 0.6 collective-permute-start.12
  55.8 4.9 %collective-permute-done.11.from_y_ref = bf16[112,1024]{1,0:T(8,128)(2,1)S(1)} collective-permute-done((bf16[112,1024]{1,0:T(8,128)(2,1)S(1)}, bf16[112,1024]{1,0:T(8,128)(2,1)S(1)}, u32[]{:S(2)}, u32[]{:S(2)}) %collective-permute-start.11) | collective-permute-done | bytes 229408 | tf_op jit(solution)/shard_map/ppermute | solution.py:583
  60.7 1.1 collective-permute-done.12.from_x_ref
  61.8 0.6 combine.1.mine_ref
  62.4 0.1 collective-permute-start.14
  62.5 0.3 collective-permute-start.13
  62.9 1.5 %collective-permute-done.14.theirs_ref = bf16[112,2048]{1,0:T(8,128)(2,1)S(1)} collective-permute-done((bf16[112,2048]{1,0:T(8,128)(2,1)S(1)}, bf16[112,2048]{1,0:T(8,128)(2,1)S(1)}, u32[]{:S(2)}, u32[]{:S(2)}) %collective-permute-start.14) | collective-permute-done | bytes 458784 | tf_op jit(solution)/shard_map/ppermute | solution.py:578
  64.3 2.6 %feed_forward.4 = (bf16[112,2048]{1,0:T(8,128)(2,1)S(1)}, bf16[112,1024]{1,0:T(8,128)(2,1)S(1)}, bf16[112,1024]{1,0:T(8,128)(2,1)S(1)}) custom-call(bf16[112,2048]{1,0:T(8,128)(2,1)S(1)} %combine.1.mine_ref, bf16[112,2048]{1,0:T(8,128)(2,1)S(1)} %collective-permute-done.14.theirs_ref, bf16[2048,1024]{1,0:T(8,128)(2,1)S(1)} %copy-done, ...), custom_call_target="tpu_custom_call" | custom-call | flops 1879048192 | bytes 8388608 | tf_op jit(solution)/shard_map/feed_forward/pallas_call | solution.py:554
  66.9 4.1 %collective-permute-done.13.mine_ref = bf16[112,2048]{1,0:T(8,128)(2,1)S(1)} collective-permute-done((bf16[112,2048]{1,0:T(8,128)(2,1)S(1)}, bf16[112,2048]{1,0:T(8,128)(2,1)S(1)}, u32[]{:S(2)}, u32[]{:S(2)}) %collective-permute-start.13) | collective-permute-done | bytes 458784 | tf_op jit(solution)/shard_map/ppermute | solution.py:588
  71.1 0.7 collective-permute-start.19
  71.7 1.1 %collective-permute-done.17.theirs_ref = bf16[112,2048]{1,0:T(8,128)(2,1)S(1)} collective-permute-done((bf16[112,2048]{1,0:T(8,128)(2,1)S(1)}, bf16[112,2048]{1,0:T(8,128)(2,1)S(1)}, u32[]{:S(2)}, u32[]{:S(2)}) %collective-permute-start.17) | collective-permute-done | bytes 458784 | tf_op jit(solution)/shard_map/ppermute | solution.py:578
  72.9 2.6 %feed_forward.5 = (bf16[112,2048]{1,0:T(8,128)(2,1)S(1)}, bf16[112,1024]{1,0:T(8,128)(2,1)S(1)}, bf16[112,1024]{1,0:T(8,128)(2,1)S(1)}) custom-call(bf16[112,2048]{1,0:T(8,128)(2,1)S(1)} %collective-permute-done.13.mine_ref, bf16[112,2048]{1,0:T(8,128)(2,1)S(1)} %collective-permute-done.17.theirs_ref, bf16[2048,1024]{1,0:T(8,128)(2,1)S(1)} %copy-done, ...), custom_call_target="tpu_custom_call" | custom-call | flops 1879048192 | bytes 8388608 | tf_op jit(solution)/shard_map/feed_forward/pallas_call | solution.py:554
  75.5 0.2 collective-permute-start.18
  75.7 3.9 %collective-permute-done.19.mine_ref = bf16[112,2048]{1,0:T(8,128)(2,1)S(1)} collective-permute-done((bf16[112,2048]{1,0:T(8,128)(2,1)S(1)}, bf16[112,2048]{1,0:T(8,128)(2,1)S(1)}, u32[]{:S(2)}, u32[]{:S(2)}) %collective-permute-start.19) | collective-permute-done | bytes 458784 | tf_op jit(solution)/shard_map/ppermute | solution.py:588
  79.5 0.7 collective-permute-start.22
  80.2 1.1 %collective-permute-done.20.theirs_ref = bf16[112,2048]{1,0:T(8,128)(2,1)S(1)} collective-permute-done((bf16[112,2048]{1,0:T(8,128)(2,1)S(1)}, bf16[112,2048]{1,0:T(8,128)(2,1)S(1)}, u32[]{:S(2)}, u32[]{:S(2)}) %collective-permute-start.20) | collective-permute-done | bytes 458784 | tf_op jit(solution)/shard_map/ppermute | solution.py:578
  81.4 2.6 %feed_forward.6 = (bf16[112,2048]{1,0:T(8,128)(2,1)S(1)}, bf16[112,1024]{1,0:T(8,128)(2,1)S(1)}, bf16[112,1024]{1,0:T(8,128)(2,1)S(1)}) custom-call(bf16[112,2048]{1,0:T(8,128)(2,1)S(1)} %collective-permute-done.19.mine_ref, bf16[112,2048]{1,0:T(8,128)(2,1)S(1)} %collective-permute-done.20.theirs_ref, bf16[2048,1024]{1,0:T(8,128)(2,1)S(1)} %copy-done, ...), custom_call_target="tpu_custom_call" | custom-call | flops 1879048192 | bytes 8388608 | tf_op jit(solution)/shard_map/feed_forward/pallas_call | solution.py:554
  84.0 0.2 collective-permute-start.21
  84.2 0.4 collective-permute-start.27
  84.5 3.5 %collective-permute-done.22.mine_ref = bf16[112,2048]{1,0:T(8,128)(2,1)S(1)} collective-permute-done((bf16[112,2048]{1,0:T(8,128)(2,1)S(1)}, bf16[112,2048]{1,0:T(8,128)(2,1)S(1)}, u32[]{:S(2)}, u32[]{:S(2)}) %collective-permute-start.22) | collective-permute-done | bytes 458784 | tf_op jit(solution)/shard_map/ppermute | solution.py:588
  88.0 0.1 add_convert_fusion.1
  88.2 0.7 collective-permute-start.28
  88.9 0.5 collective-permute-start.16
  89.4 0.4 collective-permute-done.23.theirs_ref
  89.8 2.6 %feed_forward.7 = (bf16[112,2048]{1,0:T(8,128)(2,1)S(1)}, bf16[112,1024]{1,0:T(8,128)(2,1)S(1)}, bf16[112,1024]{1,0:T(8,128)(2,1)S(1)}) custom-call(bf16[112,2048]{1,0:T(8,128)(2,1)S(1)} %collective-permute-done.22.mine_ref, bf16[112,2048]{1,0:T(8,128)(2,1)S(1)} %collective-permute-done.23.theirs_ref, bf16[2048,1024]{1,0:T(8,128)(2,1)S(1)} %copy-done, ...), custom_call_target="tpu_custom_call" | custom-call | flops 1879048192 | bytes 8388608 | tf_op jit(solution)/shard_map/feed_forward/pallas_call | solution.py:554
  92.4 0.2 collective-permute-start.25
  92.7 0.4 collective-permute-start.24
  93.0 3.7 %collective-permute-done.28 = bf16[112,2048]{1,0:T(8,128)(2,1)S(1)} collective-permute-done((bf16[112,2048]{1,0:T(8,128)(2,1)S(1)}, bf16[112,2048]{1,0:T(8,128)(2,1)S(1)}, u32[]{:S(2)}, u32[]{:S(2)}) %collective-permute-start.28) | collective-permute-done | bytes 458784 | tf_op jit(solution)/shard_map/ppermute | solution.py:588
  96.7 0.2 add_convert_fusion.4
  96.9 0.3 collective-permute-start.31
  97.3 1.7 %collective-permute-start.29 = (bf16[112,1024]{1,0:T(8,128)(2,1)S(1)}, bf16[112,1024]{1,0:T(8,128)(2,1)S(1)}, u32[]{:S(2)}, u32[]{:S(2)}) collective-permute-start(bf16[112,1024]{1,0:T(8,128)(2,1)S(1)} %get-tuple-element.100), channel_id=1, source_target_pairs={{0,2},{1,5},{2,0},{3,7},{4,6},{5,1},{6,4},{7,3},{8,10},{9,13},{10,... | collective-permute-start | bytes 688136 | tf_op jit(solution)/shard_map/ppermute | solution.py:588
  99.0 0.1 add_convert_fusion.2
  99.2 0.7 collective-permute-start.26
  99.9 0.1 convert_add_fusion
  100.0 5.1 %collective-permute-done.31 = bf16[112,1024]{1,0:T(8,128)(2,1)S(1)} collective-permute-done((bf16[112,1024]{1,0:T(8,128)(2,1)S(1)}, bf16[112,1024]{1,0:T(8,128)(2,1)S(1)}, u32[]{:S(2)}, u32[]{:S(2)}) %collective-permute-start.31) | collective-permute-done | bytes 229408 | tf_op jit(solution)/shard_map/ppermute | solution.py:588
  105.2 4.9 %collective-permute-done.29 = bf16[112,1024]{1,0:T(8,128)(2,1)S(1)} collective-permute-done((bf16[112,1024]{1,0:T(8,128)(2,1)S(1)}, bf16[112,1024]{1,0:T(8,128)(2,1)S(1)}, u32[]{:S(2)}, u32[]{:S(2)}) %collective-permute-start.29) | collective-permute-done | bytes 229408 | tf_op jit(solution)/shard_map/ppermute | solution.py:588
  110.1 0.3 add_convert_fusion
  110.4 0.9 reshape.45
  (59 shorter events, 0.3 us)
Async XLA Ops:
  0.6 38.9 %collective-permute-start.4 = (bf16[4096,256]{1,0:T(8,128)(2,1)}, bf16[4096,256]{1,0:T(8,128)(2,1)}, u32[]{:S(2)}, u32[]{:S(2)}) collective-permute-start(bf16[4096,256]{1,0:T(8,128)(2,1)} %refs_0_.1), channel_id=1, source_target_pairs={{0,1},{1,0},{2,3},{3,2},{4,5},{5,4},{6,7},{7,6},{8,9},{9,8},{10,11... | collective-permute-start | bytes 6291464 | tf_op jit(solution)/shard_map/ppermute | solution.py:578
  1.1 1.2 %copy-start.3 = (bf16[18,24,1024]{2,1,0:T(8,128)(2,1)S(1)}, bf16[18,24,1024]{2,1,0:T(8,128)(2,1)}, u32[]{:S(2)}) copy-start(bf16[18,24,1024]{2,1,0:T(8,128)(2,1)} %tokens_ref.5) | copy-start | bytes 2654212
  2.3 7.7 %copy-start.4 = (bf16[18,24,1024]{2,1,0:T(8,128)(2,1)S(1)}, bf16[18,24,1024]{2,1,0:T(8,128)(2,1)}, u32[]{:S(2)}) copy-start(bf16[18,24,1024]{2,1,0:T(8,128)(2,1)} %tokens_ref.5) | copy-start | bytes 2654212
  2.4 13.3 %collective-permute-start.1 = (bf16[18,8,1024]{2,1,0:T(8,128)(2,1)S(1)}, bf16[18,8,1024]{2,1,0:T(8,128)(2,1)S(1)}, u32[]{:S(2)}, u32[]{:S(2)}) collective-permute-start(bf16[18,8,1024]{2,1,0:T(8,128)(2,1)S(1)} %get-tuple-element.54), channel_id=1, source_target_pairs={{0,7},{1,0},{2,1},{3,2},{4,3},{5,4},{6,5},{7,6},{8,15},{9,8},{10,9... | collective-permute-start | bytes 884744 | tf_op jit(solution)/shard_map/ppermute | solution.py:418
  6.0 10.0 %collective-permute-start = (bf16[18,8,1024]{2,1,0:T(8,128)(2,1)S(1)}, bf16[18,8,1024]{2,1,0:T(8,128)(2,1)S(1)}, u32[]{:S(2)}, u32[]{:S(2)}) collective-permute-start(bf16[18,8,1024]{2,1,0:T(8,128)(2,1)S(1)} %get-tuple-element.53), channel_id=1, source_target_pairs={{0,1},{1,2},{2,3},{3,4},{4,5},{5,6},{6,7},{7,0},{8,9},{9,10},{10,1... | collective-permute-start | bytes 884744 | tf_op jit(solution)/shard_map/ppermute | solution.py:418
  8.9 27.9 %collective-permute-start.5 = (bf16[2048,256]{1,0:T(8,128)(2,1)}, bf16[2048,256]{1,0:T(8,128)(2,1)}, u32[]{:S(2)}, u32[]{:S(2)}) collective-permute-start(bf16[2048,256]{1,0:T(8,128)(2,1)} %get-tuple-element.63), channel_id=1, source_target_pairs={{0,2},{1,3},{2,0},{3,1},{4,6},{5,7},{6,4},{7,5},{8,10},{9,11},{10,... | collective-permute-start | bytes 3145736 | tf_op jit(solution)/shard_map/ppermute | solution.py:583
  9.0 27.8 %collective-permute-start.6 = (bf16[2048,256]{1,0:T(8,128)(2,1)}, bf16[2048,256]{1,0:T(8,128)(2,1)}, u32[]{:S(2)}, u32[]{:S(2)}) collective-permute-start(bf16[2048,256]{1,0:T(8,128)(2,1)} %get-tuple-element.64), channel_id=1, source_target_pairs={{0,4},{1,5},{2,6},{3,7},{4,0},{5,1},{6,2},{7,3},{8,12},{9,13},{10,... | collective-permute-start | bytes 3145736 | tf_op jit(solution)/shard_map/ppermute | solution.py:583
  10.1 10.9 %copy-start.7 = (bf16[576,144]{1,0:T(8,128)(2,1)S(1)}, bf16[576,144]{1,0:T(8,128)(2,1)}, u32[]{:S(2)}) copy-start(bf16[576,144]{1,0:T(8,128)(2,1)} %constant.71.clone.rest_1_) | copy-start | bytes 497668
  10.1 10.9 %copy-start.8 = (bf16[576,256]{1,0:T(8,128)(2,1)S(1)}, bf16[576,256]{1,0:T(8,128)(2,1)}, u32[]{:S(2)}) copy-start(bf16[576,256]{1,0:T(8,128)(2,1)} %constant.72.clone.rest_2_) | copy-start | bytes 884740
  10.1 10.9 %copy-start.9 = (bf16[144,576]{1,0:T(8,128)(2,1)S(1)}, bf16[144,576]{1,0:T(8,128)(2,1)}, u32[]{:S(2)}) copy-start(bf16[144,576]{1,0:T(8,128)(2,1)} %constant.73.clone.rest_3_) | copy-start | bytes 497668
  10.2 10.9 %copy-start.13 = (bf16[240,240]{1,0:T(8,128)(2,1)S(1)}, bf16[240,240]{1,0:T(8,128)(2,1)}, u32[]{:S(2)}) copy-start(bf16[240,240]{1,0:T(8,128)(2,1)} %constant.70.clone.rest_0_) | copy-start | bytes 345604
  16.0 10.2 %collective-permute-start.2 = (bf16[3,40,1024]{2,1,0:T(8,128)(2,1)S(1)}, bf16[3,40,1024]{2,1,0:T(8,128)(2,1)S(1)}, u32[]{:S(2)}, u32[]{:S(2)}) collective-permute-start(bf16[3,40,1024]{2,1,0:T(8,128)(2,1)S(1)} %pad_maximum_fusion.1), channel_id=1, source_target_pairs={{0,8},{8,16},{16,24},{1,9},{9,17},{17,25},{2,10},{10,18},{18,26},{... | collective-permute-start | bytes 737288 | tf_op jit(solution)/shard_map/ppermute | solution.py:418
  19.5 10.4 %collective-permute-start.3 = (bf16[3,40,1024]{2,1,0:T(8,128)(2,1)S(1)}, bf16[3,40,1024]{2,1,0:T(8,128)(2,1)S(1)}, u32[]{:S(2)}, u32[]{:S(2)}) collective-permute-start(bf16[3,40,1024]{2,1,0:T(8,128)(2,1)S(1)} %pad_maximum_fusion.2), channel_id=1, source_target_pairs={{8,0},{16,8},{24,16},{9,1},{17,9},{25,17},{10,2},{18,10},{26,18},{... | collective-permute-start | bytes 737288 | tf_op jit(solution)/shard_map/ppermute | solution.py:418
  21.1 8.9 %copy-start.5 = (bf16[1024,1024]{1,0:T(8,128)(2,1)S(1)}, bf16[1024,1024]{1,0:T(8,128)(2,1)}, u32[]{:S(2)}) copy-start(bf16[1024,1024]{1,0:T(8,128)(2,1)} %out_w_ref.1) | copy-start | bytes 6291460
  21.1 8.9 %copy-start.6 = (bf16[448,432]{1,0:T(8,128)(2,1)S(1)}, bf16[448,432]{1,0:T(8,128)(2,1)}, u32[]{:S(2)}) copy-start(bf16[448,432]{1,0:T(8,128)(2,1)} %constant.74.clone.patch_ref) | copy-start | bytes 1161220
  21.1 8.9 %copy-start.10 = (bf16[304,256]{1,0:T(8,128)(2,1)S(1)}, bf16[304,256]{1,0:T(8,128)(2,1)}, u32[]{:S(2)}) copy-start(bf16[304,256]{1,0:T(8,128)(2,1)} %constant.77.clone.rest_2_.rest_6_) | copy-start | bytes 466948
  21.1 8.9 %copy-start.11 = (bf16[240,256]{1,0:T(8,128)(2,1)S(1)}, bf16[240,256]{1,0:T(8,128)(2,1)}, u32[]{:S(2)}) copy-start(bf16[240,256]{1,0:T(8,128)(2,1)} %constant.75.clone.rest_0_) | copy-start | bytes 368644
  21.1 8.9 %copy-start.12 = (bf16[240,256]{1,0:T(8,128)(2,1)S(1)}, bf16[240,256]{1,0:T(8,128)(2,1)}, u32[]{:S(2)}) copy-start(bf16[240,256]{1,0:T(8,128)(2,1)} %constant.79.clone.rest_4_) | copy-start | bytes 368644
  21.1 8.9 %copy-start.14 = (bf16[304,80]{1,0:T(8,128)(2,1)S(1)}, bf16[304,80]{1,0:T(8,128)(2,1)}, u32[]{:S(2)}) copy-start(bf16[304,80]{1,0:T(8,128)(2,1)} %constant.76.clone.rest_1_.rest_5_) | copy-start | bytes 145924
  21.1 8.9 %copy-start.15 = (bf16[80,304]{1,0:T(8,128)(2,1)S(1)}, bf16[80,304]{1,0:T(8,128)(2,1)}, u32[]{:S(2)}) copy-start(bf16[80,304]{1,0:T(8,128)(2,1)} %constant.78.clone.rest_3_.rest_7_) | copy-start | bytes 145924
  30.0 11.4 %copy-start.2 = (bf16[4096,256]{1,0:T(8,128)(2,1)S(1)}, bf16[4096,256]{1,0:T(8,128)(2,1)}, u32[]{:S(2)}) copy-start(bf16[4096,256]{1,0:T(8,128)(2,1)} %refs_0_.1) | copy-start | bytes 6291460
  36.8 3.8 %collective-permute-start.7 = (bf16[2048,256]{1,0:T(8,128)(2,1)}, bf16[2048,256]{1,0:T(8,128)(2,1)S(1)}, u32[]{:S(2)}, u32[]{:S(2)}) collective-permute-start(bf16[2048,256]{1,0:T(8,128)(2,1)} %collective-permute-done.5.refs_2_), channel_id=1, source_target_pairs={{0,1},{1,0},{2,3},{3,2},{4,5},{5,4},{6,7},{7,6},{8,9},{9,8},{10,11... | collective-permute-start | bytes 3145736 | tf_op jit(solution)/shard_map/ppermute | solution.py:578
  37.3 4.1 %collective-permute-start.8 = (bf16[2048,256]{1,0:T(8,128)(2,1)}, bf16[2048,256]{1,0:T(8,128)(2,1)}, u32[]{:S(2)}, u32[]{:S(2)}) collective-permute-start(bf16[2048,256]{1,0:T(8,128)(2,1)} %collective-permute-done.6.refs_4_), channel_id=1, source_target_pairs={{0,1},{1,0},{2,3},{3,2},{4,5},{5,4},{6,7},{7,6},{8,9},{9,8},{10,11... | collective-permute-start | bytes 3145736 | tf_op jit(solution)/shard_map/ppermute | solution.py:578
  37.4 13.2 %collective-permute-start.9 = (bf16[112,2048]{1,0:T(8,128)(2,1)}, bf16[112,2048]{1,0:T(8,128)(2,1)}, u32[]{:S(2)}, u32[]{:S(2)}) collective-permute-start(bf16[112,2048]{1,0:T(8,128)(2,1)} %get-tuple-element.60.upper_ref), channel_id=1, source_target_pairs={{0,4},{1,5},{2,6},{3,7},{4,0},{5,1},{6,2},{7,3},{8,12},{9,13},{10,... | collective-permute-start | bytes 1376264 | tf_op jit(solution)/shard_map/ppermute | solution.py:583
  38.1 12.9 %collective-permute-start.10 = (bf16[112,2048]{1,0:T(8,128)(2,1)}, bf16[112,2048]{1,0:T(8,128)(2,1)}, u32[]{:S(2)}, u32[]{:S(2)}) collective-permute-start(bf16[112,2048]{1,0:T(8,128)(2,1)} %get-tuple-element.61.lower_ref), channel_id=1, source_target_pairs={{0,2},{1,3},{2,0},{3,1},{4,6},{5,7},{6,4},{7,5},{8,10},{9,11},{10,... | collective-permute-start | bytes 1376264 | tf_op jit(solution)/shard_map/ppermute | solution.py:583
  51.0 13.3 %copy-start = (bf16[2048,1024]{1,0:T(8,128)(2,1)S(1)}, bf16[2048,1024]{1,0:T(8,128)(2,1)}, u32[]{:S(2)}) copy-start(bf16[2048,1024]{1,0:T(8,128)(2,1)} %up_ref.7) | copy-start | bytes 12582916
  51.0 13.3 %copy-start.1 = (bf16[1024,2048]{1,0:T(8,128)(2,1)S(1)}, bf16[1024,2048]{1,0:T(8,128)(2,1)}, u32[]{:S(2)}) copy-start(bf16[1024,2048]{1,0:T(8,128)(2,1)} %down_ref.7) | copy-start | bytes 12582916
  53.8 6.9 %collective-permute-start.11 = (bf16[112,1024]{1,0:T(8,128)(2,1)S(1)}, bf16[112,1024]{1,0:T(8,128)(2,1)S(1)}, u32[]{:S(2)}, u32[]{:S(2)}) collective-permute-start(bf16[112,1024]{1,0:T(8,128)(2,1)S(1)} %get-tuple-element.76), channel_id=1, source_target_pairs={{0,4},{1,5},{2,6},{3,7},{4,0},{5,1},{6,2},{7,3},{8,12},{9,13},{10,... | collective-permute-start | bytes 688136 | tf_op jit(solution)/shard_map/ppermute | solution.py:583
  55.2 6.6 %collective-permute-start.12 = (bf16[112,1024]{1,0:T(8,128)(2,1)S(1)}, bf16[112,1024]{1,0:T(8,128)(2,1)S(1)}, u32[]{:S(2)}, u32[]{:S(2)}) collective-permute-start(bf16[112,1024]{1,0:T(8,128)(2,1)S(1)} %get-tuple-element.77), channel_id=1, source_target_pairs={{0,2},{1,3},{2,0},{3,1},{4,6},{5,7},{6,4},{7,5},{8,10},{9,11},{10,... | collective-permute-start | bytes 688136 | tf_op jit(solution)/shard_map/ppermute | solution.py:583
  62.4 1.9 %collective-permute-start.14 = (bf16[112,2048]{1,0:T(8,128)(2,1)S(1)}, bf16[112,2048]{1,0:T(8,128)(2,1)S(1)}, u32[]{:S(2)}, u32[]{:S(2)}) collective-permute-start(bf16[112,2048]{1,0:T(8,128)(2,1)S(1)} %combine.1.mine_ref), channel_id=1, source_target_pairs={{0,1},{1,0},{2,3},{3,2},{4,5},{5,4},{6,7},{7,6},{8,9},{9,8},{10,11... | collective-permute-start | bytes 1376264 | tf_op jit(solution)/shard_map/ppermute | solution.py:578
  62.5 8.5 %collective-permute-start.13 = (bf16[112,2048]{1,0:T(8,128)(2,1)S(1)}, bf16[112,2048]{1,0:T(8,128)(2,1)S(1)}, u32[]{:S(2)}, u32[]{:S(2)}) collective-permute-start(bf16[112,2048]{1,0:T(8,128)(2,1)S(1)} %combine.1.mine_ref), channel_id=1, source_target_pairs={{0,2},{1,5},{2,0},{3,7},{4,6},{5,1},{6,4},{7,3},{8,10},{9,13},{10,... | collective-permute-start | bytes 1376264 | tf_op jit(solution)/shard_map/ppermute | solution.py:588
  71.1 1.8 %collective-permute-start.17 = (bf16[112,2048]{1,0:T(8,128)(2,1)S(1)}, bf16[112,2048]{1,0:T(8,128)(2,1)S(1)}, u32[]{:S(2)}, u32[]{:S(2)}) collective-permute-start(bf16[112,2048]{1,0:T(8,128)(2,1)S(1)} %collective-permute-done.13.mine_ref), channel_id=1, source_target_pairs={{0,1},{1,0},{2,3},{3,2},{4,5},{5,4},{6,7},{7,6},{8,9},{9,8},{10,11... | collective-permute-start | bytes 1376264 | tf_op jit(solution)/shard_map/ppermute | solution.py:578
  71.1 8.5 %collective-permute-start.19 = (bf16[112,2048]{1,0:T(8,128)(2,1)S(1)}, bf16[112,2048]{1,0:T(8,128)(2,1)S(1)}, u32[]{:S(2)}, u32[]{:S(2)}) collective-permute-start(bf16[112,2048]{1,0:T(8,128)(2,1)S(1)} %collective-permute-done.13.mine_ref), channel_id=1, source_target_pairs={{0,4},{1,3},{2,6},{3,1},{4,0},{5,7},{6,2},{7,5},{8,12},{9,11},{10,... | collective-permute-start | bytes 1376264 | tf_op jit(solution)/shard_map/ppermute | solution.py:588
  75.5 4.0 %collective-permute-start.18 = (bf16[112,1024]{1,0:T(8,128)(2,1)S(1)}, bf16[112,1024]{1,0:T(8,128)(2,1)S(1)}, u32[]{:S(2)}, u32[]{:S(2)}) collective-permute-start(bf16[112,1024]{1,0:T(8,128)(2,1)S(1)} %get-tuple-element.85), channel_id=1, source_target_pairs={{0,1},{1,0},{2,3},{3,2},{4,5},{5,4},{6,7},{7,6},{8,9},{9,8},{10,11... | collective-permute-start | bytes 688136 | tf_op jit(solution)/shard_map/ppermute | solution.py:578
  79.5 1.8 %collective-permute-start.20 = (bf16[112,2048]{1,0:T(8,128)(2,1)S(1)}, bf16[112,2048]{1,0:T(8,128)(2,1)S(1)}, u32[]{:S(2)}, u32[]{:S(2)}) collective-permute-start(bf16[112,2048]{1,0:T(8,128)(2,1)S(1)} %collective-permute-done.19.mine_ref), channel_id=1, source_target_pairs={{0,1},{1,0},{2,3},{3,2},{4,5},{5,4},{6,7},{7,6},{8,9},{9,8},{10,11... | collective-permute-start | bytes 1376264 | tf_op jit(solution)/shard_map/ppermute | solution.py:578
  79.5 8.5 %collective-permute-start.22 = (bf16[112,2048]{1,0:T(8,128)(2,1)S(1)}, bf16[112,2048]{1,0:T(8,128)(2,1)S(1)}, u32[]{:S(2)}, u32[]{:S(2)}) collective-permute-start(bf16[112,2048]{1,0:T(8,128)(2,1)S(1)} %combine.1.mine_ref), channel_id=1, source_target_pairs={{0,4},{1,3},{2,6},{3,1},{4,0},{5,7},{6,2},{7,5},{8,12},{9,11},{10,... | collective-permute-start | bytes 1376264 | tf_op jit(solution)/shard_map/ppermute | solution.py:588
  84.0 4.1 %collective-permute-start.21 = (bf16[112,1024]{1,0:T(8,128)(2,1)S(1)}, bf16[112,1024]{1,0:T(8,128)(2,1)S(1)}, u32[]{:S(2)}, u32[]{:S(2)}) collective-permute-start(bf16[112,1024]{1,0:T(8,128)(2,1)S(1)} %get-tuple-element.87), channel_id=1, source_target_pairs={{0,1},{1,0},{2,3},{3,2},{4,5},{5,4},{6,7},{7,6},{8,9},{9,8},{10,11... | collective-permute-start | bytes 688136 | tf_op jit(solution)/shard_map/ppermute | solution.py:578
  84.2 3.9 %collective-permute-start.27 = (bf16[112,1024]{1,0:T(8,128)(2,1)S(1)}, bf16[112,1024]{1,0:T(8,128)(2,1)S(1)}, u32[]{:S(2)}, u32[]{:S(2)}) collective-permute-start(bf16[112,1024]{1,0:T(8,128)(2,1)S(1)} %get-tuple-element.98), channel_id=1, source_target_pairs={{0,1},{1,0},{2,3},{3,2},{4,5},{5,4},{6,7},{7,6},{8,9},{9,8},{10,11... | collective-permute-start | bytes 688136 | tf_op jit(solution)/shard_map/ppermute | solution.py:578
  88.0 1.8 %collective-permute-start.23 = (bf16[112,2048]{1,0:T(8,128)(2,1)S(1)}, bf16[112,2048]{1,0:T(8,128)(2,1)S(1)}, u32[]{:S(2)}, u32[]{:S(2)}) collective-permute-start(bf16[112,2048]{1,0:T(8,128)(2,1)S(1)} %collective-permute-done.22.mine_ref), channel_id=1, source_target_pairs={{0,1},{1,0},{2,3},{3,2},{4,5},{5,4},{6,7},{7,6},{8,9},{9,8},{10,11... | collective-permute-start | bytes 1376264 | tf_op jit(solution)/shard_map/ppermute | solution.py:578
  88.2 8.5 %collective-permute-start.28 = (bf16[112,2048]{1,0:T(8,128)(2,1)S(1)}, bf16[112,2048]{1,0:T(8,128)(2,1)S(1)}, u32[]{:S(2)}, u32[]{:S(2)}) collective-permute-start(bf16[112,2048]{1,0:T(8,128)(2,1)S(1)} %add_convert_fusion.1), channel_id=1, source_target_pairs={{0,4},{1,3},{2,6},{3,1},{4,0},{5,7},{6,2},{7,5},{8,12},{9,11},{10,... | collective-permute-start | bytes 1376264 | tf_op jit(solution)/shard_map/ppermute | solution.py:588
  88.9 3.8 %collective-permute-start.30 = (bf16[112,1024]{1,0:T(8,128)(2,1)S(1)}, bf16[112,1024]{1,0:T(8,128)(2,1)S(1)}, u32[]{:S(2)}, u32[]{:S(2)}) collective-permute-start(bf16[112,1024]{1,0:T(8,128)(2,1)S(1)} %get-tuple-element.99), channel_id=1, source_target_pairs={{0,1},{1,0},{2,3},{3,2},{4,5},{5,4},{6,7},{7,6},{8,9},{9,8},{10,11... | collective-permute-start | bytes 688136 | tf_op jit(solution)/shard_map/ppermute | solution.py:578
  88.9 11.0 %collective-permute-start.16 = (bf16[112,1024]{1,0:T(8,128)(2,1)S(1)}, bf16[112,1024]{1,0:T(8,128)(2,1)S(1)}, u32[]{:S(2)}, u32[]{:S(2)}) collective-permute-start(bf16[112,1024]{1,0:T(8,128)(2,1)S(1)} %get-tuple-element.83), channel_id=1, source_target_pairs={{0,1},{1,0},{2,3},{3,2},{4,5},{5,4},{6,7},{7,6},{8,9},{9,8},{10,11... | collective-permute-start | bytes 688136 | tf_op jit(solution)/shard_map/ppermute | solution.py:578
  89.4 10.5 %collective-permute-start.15 = (bf16[112,1024]{1,0:T(8,128)(2,1)S(1)}, bf16[112,1024]{1,0:T(8,128)(2,1)S(1)}, u32[]{:S(2)}, u32[]{:S(2)}) collective-permute-start(bf16[112,1024]{1,0:T(8,128)(2,1)S(1)} %get-tuple-element.82), channel_id=1, source_target_pairs={{0,1},{1,0},{2,3},{3,2},{4,5},{5,4},{6,7},{7,6},{8,9},{9,8},{10,11... | collective-permute-start | bytes 688136 | tf_op jit(solution)/shard_map/ppermute | solution.py:578
  92.4 4.8 %collective-permute-start.25 = (bf16[112,1024]{1,0:T(8,128)(2,1)S(1)}, bf16[112,1024]{1,0:T(8,128)(2,1)S(1)}, u32[]{:S(2)}, u32[]{:S(2)}) collective-permute-start(bf16[112,1024]{1,0:T(8,128)(2,1)S(1)} %get-tuple-element.93), channel_id=1, source_target_pairs={{0,1},{1,0},{2,3},{3,2},{4,5},{5,4},{6,7},{7,6},{8,9},{9,8},{10,11... | collective-permute-start | bytes 688136 | tf_op jit(solution)/shard_map/ppermute | solution.py:578
  92.7 6.4 %collective-permute-start.24 = (bf16[112,1024]{1,0:T(8,128)(2,1)S(1)}, bf16[112,1024]{1,0:T(8,128)(2,1)S(1)}, u32[]{:S(2)}, u32[]{:S(2)}) collective-permute-start(bf16[112,1024]{1,0:T(8,128)(2,1)S(1)} %get-tuple-element.92), channel_id=1, source_target_pairs={{0,1},{1,0},{2,3},{3,2},{4,5},{5,4},{6,7},{7,6},{8,9},{9,8},{10,11... | collective-permute-start | bytes 688136 | tf_op jit(solution)/shard_map/ppermute | solution.py:578
  96.9 8.2 %collective-permute-start.31 = (bf16[112,1024]{1,0:T(8,128)(2,1)S(1)}, bf16[112,1024]{1,0:T(8,128)(2,1)S(1)}, u32[]{:S(2)}, u32[]{:S(2)}) collective-permute-start(bf16[112,1024]{1,0:T(8,128)(2,1)S(1)} %get-tuple-element.101), channel_id=1, source_target_pairs={{0,2},{1,5},{2,0},{3,7},{4,6},{5,1},{6,4},{7,3},{8,10},{9,13},{10,... | collective-permute-start | bytes 688136 | tf_op jit(solution)/shard_map/ppermute | solution.py:588
  97.3 12.8 %collective-permute-start.29 = (bf16[112,1024]{1,0:T(8,128)(2,1)S(1)}, bf16[112,1024]{1,0:T(8,128)(2,1)S(1)}, u32[]{:S(2)}, u32[]{:S(2)}) collective-permute-start(bf16[112,1024]{1,0:T(8,128)(2,1)S(1)} %get-tuple-element.100), channel_id=1, source_target_pairs={{0,2},{1,5},{2,0},{3,7},{4,6},{5,1},{6,4},{7,3},{8,10},{9,13},{10,... | collective-permute-start | bytes 688136 | tf_op jit(solution)/shard_map/ppermute | solution.py:588
  99.2 10.9 %collective-permute-start.26 = (bf16[112,2048]{1,0:T(8,128)(2,1)S(1)}, bf16[112,2048]{1,0:T(8,128)(2,1)S(1)}, u32[]{:S(2)}, u32[]{:S(2)}) collective-permute-start(bf16[112,2048]{1,0:T(8,128)(2,1)S(1)} %add_convert_fusion.2), channel_id=1, source_target_pairs={{0,4},{1,3},{2,6},{3,1},{4,0},{5,7},{6,2},{7,5},{8,12},{9,11},{10,... | collective-permute-start | bytes 1376264 | tf_op jit(solution)/shard_map/ppermute | solution.py:588

commit v10 on v9

--- a/solution.py
+++ b/solution.py
@@ -168,10 +168,14 @@
 
 def halves_kernel(weight_ref, upper_ref, lower_ref, sems):
     half = upper_ref.shape[0]
-    copies = [
-        pltpu.make_async_copy(weight_ref.at[k * half : (k + 1) * half], ref, sems.at[k])
-        for k, ref in enumerate((upper_ref, lower_ref))
-    ]
+    pieces = sems.shape[0] // 2
+    size = half // pieces
+    copies = []
+    for k, ref in enumerate((upper_ref, lower_ref)):
+        for n in range(pieces):
+            rows = weight_ref.at[k * half + n * size : k * half + (n + 1) * size]
+            to = ref.at[n * size : (n + 1) * size]
+            copies.append(pltpu.make_async_copy(rows, to, sems.at[k * pieces + n]))
     for copy in copies:
         copy.start()
     for copy in copies:
@@ -185,7 +189,7 @@
         in_specs=[pl.BlockSpec(memory_space=pl.ANY)],
         out_specs=[pl.BlockSpec(memory_space=pltpu.VMEM)] * 2,
         out_shape=[jax.ShapeDtypeStruct((depth // 2, block), BF16)] * 2,
-        scratch_shapes=[pltpu.SemaphoreType.DMA((2,))],
+        scratch_shapes=[pltpu.SemaphoreType.DMA((8,))],
         compiler_params=params(52),
         name="halves",
     )(weight)
@@ -231,7 +235,7 @@
         scratch_shapes=[
             pltpu.VMEM((bands.own_total, width), BF16),
             pltpu.VMEM((width, width), BF16),
-            pltpu.SemaphoreType.DMA((6,)),
+            pltpu.SemaphoreType.DMA((12,)),
         ],
         compiler_params=params(42),
         cost_estimate=pl.CostEstimate(
@@ -599,8 +603,8 @@
     other = cross(later, 2, 1)
     near_low, far = lax.optimization_barrier((core_swap(near_low), far))
     mine, low, high = feed_forward(far, core_swap(far), up, down)
-    low, other = lax.optimization_barrier((core_swap(low), other))
-    relayed = cross(added(mine, low, core_swap(high)), 2, 1)
+    low, high, other = lax.optimization_barrier((core_swap(low), core_swap(high), other))
+    relayed = cross(added(mine, low, high), 2, 1)
     other_back = cross(summed(*feed_forward(other, core_swap(other), up, down)), 2, 1)
     half = low.shape[1]
     near_back = []

time: 111 us -> 115 us (1.036)
  Pallas kernels: 38.7 us -> 42.1 us
  waiting for transfers between devices: 46.3 us -> 44.4 us
  starting transfers between devices: 22 us -> 23.7 us
    pallas_call x1, Pallas kernels: 5.35 us -> 8.86 us  [own_projection(): pl.pallas_call(functools.partial(own_kernel, bands), in_specs=[vmem, pl.B...]
    ppermute x7, starting transfers between devices: 5.27 us -> 6.82 us  [cross(): lax.ppermute(value, 'lon', [(i, i ^ 2 * (second if i % 2 else first)) for...]
  transfers between devices with their start and end apart: 32 -> 32, of which waited for: 18 -> 17; matrix products, arithmetic and copies ran while one was open for 1% -> 1% of each run, Pallas kernels for 32% -> 34%
where the time goes in v10:
time: 115 us; the launch traced here: 114 us
  waiting for transfers between devices  44.4 us (39%)
  Pallas kernels  42.1 us (37%)
  starting transfers between devices  23.7 us (21%)
  local copies, waits for them, and re-layouts  2.2 us (2%)
    ppermute x7, waiting for transfers between devices, cross(): lax.ppermute(value, 'lon', [(i, i ^ 2 * (second if i % 2 else first)) for...  24.8 us
    pallas_call x2, Pallas kernels, vmem_call(): pl.pallas_call(kernel, in_specs=[vmem] * len(args), out_specs=[vmem] * le...  11.8 us
    ppermute x6, waiting for transfers between devices, chip_swap(): lax.ppermute(value, 'lon', [(i, i ^ 2 * offset) for i in range(size)])  10.9 us
    pallas_call x4, Pallas kernels, feed_forward(): pl.pallas_call(ffn_kernel, in_specs=[vmem] * 4, out_specs=[vmem] * 3, out...  10.4 us
    pallas_call x1, Pallas kernels, own_projection(): pl.pallas_call(functools.partial(own_kernel, bands), in_specs=[vmem, pl.B...  8.86 us
    ppermute x4, starting transfers between devices, shift(): return lax.ppermute(part, axis, pairs)  8.58 us
    pallas_call x3, Pallas kernels, local_call(): pl.pallas_call(kernel, in_specs=[pl.BlockSpec(memory_space=pltpu.SMEM)] +...  8.05 us
    ppermute x7, starting transfers between devices, cross(): lax.ppermute(value, 'lon', [(i, i ^ 2 * (second if i % 2 else first)) for...  6.82 us
  transfers between devices with their start and end apart: 32, of which 17 were waited for; matrix products, arithmetic and copies ran while one was open for 1% of the time, Pallas kernels for 34%

profile of v10, /device:TPU:0, one launch (start us, length us, event | category | flops | bytes accessed | tf_op | source)
XLA Modules:
  0.0 114.5 jit_solution(14223926851869452274)
XLA Ops:
  0.6 0.5 collective-permute-start.4
  1.1 1.2 %copy-done.3 = bf16[18,24,1024]{2,1,0:T(8,128)(2,1)S(1)} copy-done((bf16[18,24,1024]{2,1,0:T(8,128)(2,1)S(1)}, bf16[18,24,1024]{2,1,0:T(8,128)(2,1)}, u32[]{:S(2)}) %copy-start.3) | copy-done | bytes 884760
  2.4 3.6 %collective-permute-start.1 = (bf16[18,8,1024]{2,1,0:T(8,128)(2,1)S(1)}, bf16[18,8,1024]{2,1,0:T(8,128)(2,1)S(1)}, u32[]{:S(2)}, u32[]{:S(2)}) collective-permute-start(bf16[18,8,1024]{2,1,0:T(8,128)(2,1)S(1)} %get-tuple-element.55), channel_id=1, source_target_pairs={{0,7},{1,0},{2,1},{3,2},{4,3},{5,4},{6,5},{7,6},{8,15},{9,8},{10,9... | collective-permute-start | bytes 884744 | tf_op jit(solution)/shard_map/ppermute | solution.py:422
  6.0 2.9 %halves.1 = (bf16[2048,256]{1,0:T(8,128)(2,1)}, bf16[2048,256]{1,0:T(8,128)(2,1)}) custom-call(bf16[4096,256]{1,0:T(8,128)(2,1)} %refs_0_.1), custom_call_target="tpu_custom_call" | custom-call | tf_op jit(solution)/shard_map/halves/pallas_call | solution.py:187
  8.9 0.1 collective-permute-start.5
  9.0 1.1 collective-permute-start.6
  10.1 0.0 copy-start.7
  10.2 8.9 %own_projection.1 = (bf16[448,3072]{1,0:T(8,128)(2,1)S(1)}, bf16[1024,2048]{1,0:T(8,128)(2,1)S(1)}) custom-call(bf16[18,24,1024]{2,1,0:T(8,128)(2,1)S(1)} %copy-done.4, bf16[1024,3072]{1,0:T(8,128)(2,1)} %weight_ref.1), custom_call_target="tpu_custom_call" | custom-call | flops 2818572288 | bytes 6291456 | tf_op jit(solution)/shard_map/own_projection/pallas_call | solution.py:227
  19.1 0.1 or_select_fusion.bias_ref
  19.2 3.5 %collective-permute-start.2 = (bf16[3,40,1024]{2,1,0:T(8,128)(2,1)S(1)}, bf16[3,40,1024]{2,1,0:T(8,128)(2,1)S(1)}, u32[]{:S(2)}, u32[]{:S(2)}) collective-permute-start(bf16[3,40,1024]{2,1,0:T(8,128)(2,1)S(1)} %pad_maximum_fusion.1), channel_id=1, source_target_pairs={{0,8},{8,16},{16,24},{1,9},{9,17},{17,25},{2,10},{10,18},{18,26},{... | collective-permute-start | bytes 737288 | tf_op jit(solution)/shard_map/ppermute | solution.py:422
  22.7 1.5 %collective-permute-start.3 = (bf16[3,40,1024]{2,1,0:T(8,128)(2,1)S(1)}, bf16[3,40,1024]{2,1,0:T(8,128)(2,1)S(1)}, u32[]{:S(2)}, u32[]{:S(2)}) collective-permute-start(bf16[3,40,1024]{2,1,0:T(8,128)(2,1)S(1)} %pad_maximum_fusion.2), channel_id=1, source_target_pairs={{8,0},{16,8},{24,16},{9,1},{17,9},{25,17},{10,2},{18,10},{26,18},{... | collective-permute-start | bytes 737288 | tf_op jit(solution)/shard_map/ppermute | solution.py:422
  24.3 5.0 %middle_attention.1 = (bf16[288,2048]{1,0:T(8,128)(2,1)S(1)}, bf16[288,1024]{1,0:T(8,128)(2,1)S(1)}) custom-call(bf16[18,8,1024]{2,1,0:T(8,128)(2,1)S(1)} %collective-permute-done.west_ref, bf16[18,8,1024]{2,1,0:T(8,128)(2,1)S(1)} %collective-permute-done.1.east_ref, bf16[448,3072]{1,0:T(8,128)(2,1)S(1)} %get-tuple-element.56.own_ref, ...), custom_call_target="tpu_custom_call" | custom-call | flops 5000000000 | bytes 1048576 | tf_op jit(solution)/shard_map/middle_attention/pallas_call | solution.py:365
  29.4 3.4 %collective-permute-done.3.south_ref = bf16[3,40,1024]{2,1,0:T(8,128)(2,1)S(1)} collective-permute-done((bf16[3,40,1024]{2,1,0:T(8,128)(2,1)S(1)}, bf16[3,40,1024]{2,1,0:T(8,128)(2,1)S(1)}, u32[]{:S(2)}, u32[]{:S(2)}) %collective-permute-start.3) | collective-permute-done | bytes 245792 | tf_op jit(solution)/shard_map/ppermute | solution.py:422
  32.9 6.8 %edge_attention.1 = (bf16[18,24,1024]{2,1,0:T(8,128)(2,1)}, bf16[112,2048]{1,0:T(8,128)(2,1)}, bf16[112,2048]{1,0:T(8,128)(2,1)}) custom-call(bf16[18,24,1024]{2,1,0:T(8,128)(2,1)S(1)} %copy-done.4, bf16[3,40,1024]{2,1,0:T(8,128)(2,1)S(1)} %collective-permute-done.2.north_ref, bf16[3,40,1024]{2,1,0:T(8,128)(2,1)S(1)} %collective-permute-done.3.south_ref, ...), custom_call_target="tpu_custom_call" | custom-call | flops 6000000000 | bytes 1048576 | tf_op jit(solution)/shard_map/edge_attention/pallas_call | solution.py:365
  39.6 0.9 collective-permute-start.7
  40.5 0.1 collective-permute-start.8
  40.6 1.0 collective-permute-start.9
  41.6 0.7 collective-permute-start.10
  42.4 0.1 pad_add_fusion.place_ref
  42.4 1.3 %collective-permute-done.7.refs_3_ = bf16[2048,256]{1,0:T(8,128)(2,1)S(1)} collective-permute-done((bf16[2048,256]{1,0:T(8,128)(2,1)}, bf16[2048,256]{1,0:T(8,128)(2,1)S(1)}, u32[]{:S(2)}, u32[]{:S(2)}) %collective-permute-start.7) | collective-permute-done | bytes 1048608 | tf_op jit(solution)/shard_map/ppermute | solution.py:582
  43.8 0.9 collective-permute-done.8.refs_5_
  44.6 4.6 %merge_own.1 = (f32[112,512]{1,0:T(8,128)S(1)}, f32[112,512]{1,0:T(8,128)S(1)}, f32[112,512]{1,0:T(8,128)S(1)}, bf16[4096,256]{1,0:T(8,128)(2,1)S(1)}, bf16[4096...) custom-call(s32[2]{0:T(128)S(1)} %pad_add_fusion.place_ref, ...), custom_call_target="tpu_custom_call" | custom-call | flops 939524096 | bytes 1048576 | tf_op jit(solution)/shard_map/merge_own/pallas_call | solution.py:500
  49.2 4.5 %collective-permute-done.9.upper_ref = bf16[112,2048]{1,0:T(8,128)(2,1)} collective-permute-done((bf16[112,2048]{1,0:T(8,128)(2,1)}, bf16[112,2048]{1,0:T(8,128)(2,1)}, u32[]{:S(2)}, u32[]{:S(2)}) %collective-permute-start.9) | collective-permute-done | bytes 458784 | tf_op jit(solution)/shard_map/ppermute | solution.py:587
  53.8 0.7 collective-permute-done.10.lower_ref
  54.5 2.8 %merge_other.1 = (bf16[112,1024]{1,0:T(8,128)(2,1)S(1)}, bf16[112,1024]{1,0:T(8,128)(2,1)S(1)}) custom-call(s32[2]{0:T(128)S(1)} %pad_add_fusion.place_ref, bf16[112,2048]{1,0:T(8,128)(2,1)} %collective-permute-done.9.upper_ref, bf16[112,2048]{1,0:T(8,128)(2,1)} %collective-permute-done.10.lower_ref, bf16[4096,256]{1,0:T(8,128)(2,1)S(1)} %get-tuple-element.71.refs_0_, ...), custom_call_target="tpu_custom_call" | custom-call | flops 939524096 | bytes 1048576 | tf_op jit(solution)/shard_map/merge_other/pallas_call | solution.py:500
  57.4 1.1 collective-permute-start.11
  58.4 0.9 collective-permute-start.12
  59.3 4.9 %collective-permute-done.11.from_y_ref = bf16[112,1024]{1,0:T(8,128)(2,1)S(1)} collective-permute-done((bf16[112,1024]{1,0:T(8,128)(2,1)S(1)}, bf16[112,1024]{1,0:T(8,128)(2,1)S(1)}, u32[]{:S(2)}, u32[]{:S(2)}) %collective-permute-start.11) | collective-permute-done | bytes 229408 | tf_op jit(solution)/shard_map/ppermute | solution.py:587
  64.3 0.7 collective-permute-done.12.from_x_ref
  65.0 0.6 combine.1.mine_ref
  65.6 0.1 collective-permute-start.14
  65.7 0.6 collective-permute-start.13
  66.3 1.3 %collective-permute-done.14.theirs_ref = bf16[112,2048]{1,0:T(8,128)(2,1)S(1)} collective-permute-done((bf16[112,2048]{1,0:T(8,128)(2,1)S(1)}, bf16[112,2048]{1,0:T(8,128)(2,1)S(1)}, u32[]{:S(2)}, u32[]{:S(2)}) %collective-permute-start.14) | collective-permute-done | bytes 458784 | tf_op jit(solution)/shard_map/ppermute | solution.py:582
  67.5 2.6 %feed_forward.4 = (bf16[112,2048]{1,0:T(8,128)(2,1)S(1)}, bf16[112,1024]{1,0:T(8,128)(2,1)S(1)}, bf16[112,1024]{1,0:T(8,128)(2,1)S(1)}) custom-call(bf16[112,2048]{1,0:T(8,128)(2,1)S(1)} %combine.1.mine_ref, bf16[112,2048]{1,0:T(8,128)(2,1)S(1)} %collective-permute-done.14.theirs_ref, bf16[2048,1024]{1,0:T(8,128)(2,1)S(1)} %copy-done, ...), custom_call_target="tpu_custom_call" | custom-call | flops 1879048192 | bytes 8388608 | tf_op jit(solution)/shard_map/feed_forward/pallas_call | solution.py:558
  70.1 4.1 %collective-permute-done.13.mine_ref = bf16[112,2048]{1,0:T(8,128)(2,1)S(1)} collective-permute-done((bf16[112,2048]{1,0:T(8,128)(2,1)S(1)}, bf16[112,2048]{1,0:T(8,128)(2,1)S(1)}, u32[]{:S(2)}, u32[]{:S(2)}) %collective-permute-start.13) | collective-permute-done | bytes 458784 | tf_op jit(solution)/shard_map/ppermute | solution.py:592
  74.3 1.0 collective-permute-start.19
  75.3 0.8 collective-permute-done.17.theirs_ref
  76.1 2.6 %feed_forward.5 = (bf16[112,2048]{1,0:T(8,128)(2,1)S(1)}, bf16[112,1024]{1,0:T(8,128)(2,1)S(1)}, bf16[112,1024]{1,0:T(8,128)(2,1)S(1)}) custom-call(bf16[112,2048]{1,0:T(8,128)(2,1)S(1)} %collective-permute-done.13.mine_ref, bf16[112,2048]{1,0:T(8,128)(2,1)S(1)} %collective-permute-done.17.theirs_ref, bf16[2048,1024]{1,0:T(8,128)(2,1)S(1)} %copy-done, ...), custom_call_target="tpu_custom_call" | custom-call | flops 1879048192 | bytes 8388608 | tf_op jit(solution)/shard_map/feed_forward/pallas_call | solution.py:558
  78.7 0.2 collective-permute-start.18
  78.9 3.9 %collective-permute-done.19.mine_ref = bf16[112,2048]{1,0:T(8,128)(2,1)S(1)} collective-permute-done((bf16[112,2048]{1,0:T(8,128)(2,1)S(1)}, bf16[112,2048]{1,0:T(8,128)(2,1)S(1)}, u32[]{:S(2)}, u32[]{:S(2)}) %collective-permute-start.19) | collective-permute-done | bytes 458784 | tf_op jit(solution)/shard_map/ppermute | solution.py:592
  82.7 1.0 collective-permute-start.23
  83.8 0.8 collective-permute-done.20.theirs_ref
  84.6 2.6 %feed_forward.6 = (bf16[112,2048]{1,0:T(8,128)(2,1)S(1)}, bf16[112,1024]{1,0:T(8,128)(2,1)S(1)}, bf16[112,1024]{1,0:T(8,128)(2,1)S(1)}) custom-call(bf16[112,2048]{1,0:T(8,128)(2,1)S(1)} %collective-permute-done.19.mine_ref, bf16[112,2048]{1,0:T(8,128)(2,1)S(1)} %collective-permute-done.20.theirs_ref, bf16[2048,1024]{1,0:T(8,128)(2,1)S(1)} %copy-done, ...), custom_call_target="tpu_custom_call" | custom-call | flops 1879048192 | bytes 8388608 | tf_op jit(solution)/shard_map/feed_forward/pallas_call | solution.py:558
  87.2 0.2 collective-permute-start.21
  87.4 0.4 collective-permute-start.22
  87.7 3.5 %collective-permute-done.23.mine_ref = bf16[112,2048]{1,0:T(8,128)(2,1)S(1)} collective-permute-done((bf16[112,2048]{1,0:T(8,128)(2,1)S(1)}, bf16[112,2048]{1,0:T(8,128)(2,1)S(1)}, u32[]{:S(2)}, u32[]{:S(2)}) %collective-permute-start.23) | collective-permute-done | bytes 458784 | tf_op jit(solution)/shard_map/ppermute | solution.py:592
  91.2 0.1 add_convert_fusion.1
  91.4 1.1 collective-permute-start.28
  92.4 0.5 collective-permute-start.16
  92.9 0.1 collective-permute-done.24.theirs_ref
  93.0 2.6 %feed_forward.7 = (bf16[112,2048]{1,0:T(8,128)(2,1)S(1)}, bf16[112,1024]{1,0:T(8,128)(2,1)S(1)}, bf16[112,1024]{1,0:T(8,128)(2,1)S(1)}) custom-call(bf16[112,2048]{1,0:T(8,128)(2,1)S(1)} %collective-permute-done.23.mine_ref, bf16[112,2048]{1,0:T(8,128)(2,1)S(1)} %collective-permute-done.24.theirs_ref, bf16[2048,1024]{1,0:T(8,128)(2,1)S(1)} %copy-done, ...), custom_call_target="tpu_custom_call" | custom-call | flops 1879048192 | bytes 8388608 | tf_op jit(solution)/shard_map/feed_forward/pallas_call | solution.py:558
  95.7 0.5 collective-permute-start.26
  96.1 0.1 collective-permute-start.25
  96.2 3.6 %collective-permute-done.28 = bf16[112,2048]{1,0:T(8,128)(2,1)S(1)} collective-permute-done((bf16[112,2048]{1,0:T(8,128)(2,1)S(1)}, bf16[112,2048]{1,0:T(8,128)(2,1)S(1)}, u32[]{:S(2)}, u32[]{:S(2)}) %collective-permute-start.28) | collective-permute-done | bytes 458784 | tf_op jit(solution)/shard_map/ppermute | solution.py:592
  99.9 0.2 add_convert_fusion.4
  100.1 0.6 collective-permute-start.31
  100.7 1.5 %collective-permute-start.29 = (bf16[112,1024]{1,0:T(8,128)(2,1)S(1)}, bf16[112,1024]{1,0:T(8,128)(2,1)S(1)}, u32[]{:S(2)}, u32[]{:S(2)}) collective-permute-start(bf16[112,1024]{1,0:T(8,128)(2,1)S(1)} %get-tuple-element.102), channel_id=1, source_target_pairs={{0,2},{1,5},{2,0},{3,7},{4,6},{5,1},{6,4},{7,3},{8,10},{9,13},{10,... | collective-permute-start | bytes 688136 | tf_op jit(solution)/shard_map/ppermute | solution.py:592
  102.2 0.1 add_convert_fusion.2
  102.4 1.1 collective-permute-start.27
  103.4 0.1 convert_add_fusion
  103.6 4.8 %collective-permute-done.31 = bf16[112,1024]{1,0:T(8,128)(2,1)S(1)} collective-permute-done((bf16[112,1024]{1,0:T(8,128)(2,1)S(1)}, bf16[112,1024]{1,0:T(8,128)(2,1)S(1)}, u32[]{:S(2)}, u32[]{:S(2)}) %collective-permute-start.31) | collective-permute-done | bytes 229408 | tf_op jit(solution)/shard_map/ppermute | solution.py:592
  108.3 4.9 %collective-permute-done.29 = bf16[112,1024]{1,0:T(8,128)(2,1)S(1)} collective-permute-done((bf16[112,1024]{1,0:T(8,128)(2,1)S(1)}, bf16[112,1024]{1,0:T(8,128)(2,1)S(1)}, u32[]{:S(2)}, u32[]{:S(2)}) %collective-permute-start.29) | collective-permute-done | bytes 229408 | tf_op jit(solution)/shard_map/ppermute | solution.py:592
  113.3 0.3 add_convert_fusion
  113.6 0.9 reshape.45
  (59 shorter events, 0.3 us)
Async XLA Ops:
  0.6 41.8 %collective-permute-start.4 = (bf16[4096,256]{1,0:T(8,128)(2,1)}, bf16[4096,256]{1,0:T(8,128)(2,1)}, u32[]{:S(2)}, u32[]{:S(2)}) collective-permute-start(bf16[4096,256]{1,0:T(8,128)(2,1)} %refs_0_.1), channel_id=1, source_target_pairs={{0,1},{1,0},{2,3},{3,2},{4,5},{5,4},{6,7},{7,6},{8,9},{9,8},{10,11... | collective-permute-start | bytes 6291464 | tf_op jit(solution)/shard_map/ppermute | solution.py:582
  1.1 1.2 %copy-start.3 = (bf16[18,24,1024]{2,1,0:T(8,128)(2,1)S(1)}, bf16[18,24,1024]{2,1,0:T(8,128)(2,1)}, u32[]{:S(2)}) copy-start(bf16[18,24,1024]{2,1,0:T(8,128)(2,1)} %tokens_ref.5) | copy-start | bytes 2654212
  2.3 7.8 %copy-start.4 = (bf16[18,24,1024]{2,1,0:T(8,128)(2,1)S(1)}, bf16[18,24,1024]{2,1,0:T(8,128)(2,1)}, u32[]{:S(2)}) copy-start(bf16[18,24,1024]{2,1,0:T(8,128)(2,1)} %tokens_ref.5) | copy-start | bytes 2654212
  2.4 16.8 %collective-permute-start.1 = (bf16[18,8,1024]{2,1,0:T(8,128)(2,1)S(1)}, bf16[18,8,1024]{2,1,0:T(8,128)(2,1)S(1)}, u32[]{:S(2)}, u32[]{:S(2)}) collective-permute-start(bf16[18,8,1024]{2,1,0:T(8,128)(2,1)S(1)} %get-tuple-element.55), channel_id=1, source_target_pairs={{0,7},{1,0},{2,1},{3,2},{4,3},{5,4},{6,5},{7,6},{8,15},{9,8},{10,9... | collective-permute-start | bytes 884744 | tf_op jit(solution)/shard_map/ppermute | solution.py:422
  6.0 13.2 %collective-permute-start = (bf16[18,8,1024]{2,1,0:T(8,128)(2,1)S(1)}, bf16[18,8,1024]{2,1,0:T(8,128)(2,1)S(1)}, u32[]{:S(2)}, u32[]{:S(2)}) collective-permute-start(bf16[18,8,1024]{2,1,0:T(8,128)(2,1)S(1)} %get-tuple-element.54), channel_id=1, source_target_pairs={{0,1},{1,2},{2,3},{3,4},{4,5},{5,6},{6,7},{7,0},{8,9},{9,10},{10,1... | collective-permute-start | bytes 884744 | tf_op jit(solution)/shard_map/ppermute | solution.py:422
  8.9 30.7 %collective-permute-start.5 = (bf16[2048,256]{1,0:T(8,128)(2,1)}, bf16[2048,256]{1,0:T(8,128)(2,1)}, u32[]{:S(2)}, u32[]{:S(2)}) collective-permute-start(bf16[2048,256]{1,0:T(8,128)(2,1)} %get-tuple-element.64), channel_id=1, source_target_pairs={{0,2},{1,3},{2,0},{3,1},{4,6},{5,7},{6,4},{7,5},{8,10},{9,11},{10,... | collective-permute-start | bytes 3145736 | tf_op jit(solution)/shard_map/ppermute | solution.py:587
  9.0 30.6 %collective-permute-start.6 = (bf16[2048,256]{1,0:T(8,128)(2,1)}, bf16[2048,256]{1,0:T(8,128)(2,1)}, u32[]{:S(2)}, u32[]{:S(2)}) collective-permute-start(bf16[2048,256]{1,0:T(8,128)(2,1)} %get-tuple-element.65), channel_id=1, source_target_pairs={{0,4},{1,5},{2,6},{3,7},{4,0},{5,1},{6,2},{7,3},{8,12},{9,13},{10,... | collective-permute-start | bytes 3145736 | tf_op jit(solution)/shard_map/ppermute | solution.py:587
  10.1 14.1 %copy-start.7 = (bf16[576,144]{1,0:T(8,128)(2,1)S(1)}, bf16[576,144]{1,0:T(8,128)(2,1)}, u32[]{:S(2)}) copy-start(bf16[576,144]{1,0:T(8,128)(2,1)} %constant.71.clone.rest_1_) | copy-start | bytes 497668
  10.1 14.1 %copy-start.8 = (bf16[576,256]{1,0:T(8,128)(2,1)S(1)}, bf16[576,256]{1,0:T(8,128)(2,1)}, u32[]{:S(2)}) copy-start(bf16[576,256]{1,0:T(8,128)(2,1)} %constant.72.clone.rest_2_) | copy-start | bytes 884740
  10.2 14.1 %copy-start.9 = (bf16[144,576]{1,0:T(8,128)(2,1)S(1)}, bf16[144,576]{1,0:T(8,128)(2,1)}, u32[]{:S(2)}) copy-start(bf16[144,576]{1,0:T(8,128)(2,1)} %constant.73.clone.rest_3_) | copy-start | bytes 497668
  10.2 14.1 %copy-start.13 = (bf16[240,240]{1,0:T(8,128)(2,1)S(1)}, bf16[240,240]{1,0:T(8,128)(2,1)}, u32[]{:S(2)}) copy-start(bf16[240,240]{1,0:T(8,128)(2,1)} %constant.70.clone.rest_0_) | copy-start | bytes 345604
  19.2 10.2 %collective-permute-start.2 = (bf16[3,40,1024]{2,1,0:T(8,128)(2,1)S(1)}, bf16[3,40,1024]{2,1,0:T(8,128)(2,1)S(1)}, u32[]{:S(2)}, u32[]{:S(2)}) collective-permute-start(bf16[3,40,1024]{2,1,0:T(8,128)(2,1)S(1)} %pad_maximum_fusion.1), channel_id=1, source_target_pairs={{0,8},{8,16},{16,24},{1,9},{9,17},{17,25},{2,10},{10,18},{18,26},{... | collective-permute-start | bytes 737288 | tf_op jit(solution)/shard_map/ppermute | solution.py:422
  22.7 10.1 %collective-permute-start.3 = (bf16[3,40,1024]{2,1,0:T(8,128)(2,1)S(1)}, bf16[3,40,1024]{2,1,0:T(8,128)(2,1)S(1)}, u32[]{:S(2)}, u32[]{:S(2)}) collective-permute-start(bf16[3,40,1024]{2,1,0:T(8,128)(2,1)S(1)} %pad_maximum_fusion.2), channel_id=1, source_target_pairs={{8,0},{16,8},{24,16},{9,1},{17,9},{25,17},{10,2},{18,10},{26,18},{... | collective-permute-start | bytes 737288 | tf_op jit(solution)/shard_map/ppermute | solution.py:422
  24.3 8.6 %copy-start.5 = (bf16[1024,1024]{1,0:T(8,128)(2,1)S(1)}, bf16[1024,1024]{1,0:T(8,128)(2,1)}, u32[]{:S(2)}) copy-start(bf16[1024,1024]{1,0:T(8,128)(2,1)} %out_w_ref.1) | copy-start | bytes 6291460
  24.3 8.5 %copy-start.6 = (bf16[448,432]{1,0:T(8,128)(2,1)S(1)}, bf16[448,432]{1,0:T(8,128)(2,1)}, u32[]{:S(2)}) copy-start(bf16[448,432]{1,0:T(8,128)(2,1)} %constant.74.clone.patch_ref) | copy-start | bytes 1161220
  24.3 8.5 %copy-start.10 = (bf16[304,256]{1,0:T(8,128)(2,1)S(1)}, bf16[304,256]{1,0:T(8,128)(2,1)}, u32[]{:S(2)}) copy-start(bf16[304,256]{1,0:T(8,128)(2,1)} %constant.77.clone.rest_2_.rest_6_) | copy-start | bytes 466948
  24.3 8.5 %copy-start.11 = (bf16[240,256]{1,0:T(8,128)(2,1)S(1)}, bf16[240,256]{1,0:T(8,128)(2,1)}, u32[]{:S(2)}) copy-start(bf16[240,256]{1,0:T(8,128)(2,1)} %constant.75.clone.rest_0_) | copy-start | bytes 368644
  24.3 8.5 %copy-start.12 = (bf16[240,256]{1,0:T(8,128)(2,1)S(1)}, bf16[240,256]{1,0:T(8,128)(2,1)}, u32[]{:S(2)}) copy-start(bf16[240,256]{1,0:T(8,128)(2,1)} %constant.79.clone.rest_4_) | copy-start | bytes 368644
  24.3 8.5 %copy-start.14 = (bf16[304,80]{1,0:T(8,128)(2,1)S(1)}, bf16[304,80]{1,0:T(8,128)(2,1)}, u32[]{:S(2)}) copy-start(bf16[304,80]{1,0:T(8,128)(2,1)} %constant.76.clone.rest_1_.rest_5_) | copy-start | bytes 145924
  24.3 8.5 %copy-start.15 = (bf16[80,304]{1,0:T(8,128)(2,1)S(1)}, bf16[80,304]{1,0:T(8,128)(2,1)}, u32[]{:S(2)}) copy-start(bf16[80,304]{1,0:T(8,128)(2,1)} %constant.78.clone.rest_3_.rest_7_) | copy-start | bytes 145924
  32.9 11.8 %copy-start.2 = (bf16[4096,256]{1,0:T(8,128)(2,1)S(1)}, bf16[4096,256]{1,0:T(8,128)(2,1)}, u32[]{:S(2)}) copy-start(bf16[4096,256]{1,0:T(8,128)(2,1)} %refs_0_.1) | copy-start | bytes 6291460
  39.6 4.1 %collective-permute-start.7 = (bf16[2048,256]{1,0:T(8,128)(2,1)}, bf16[2048,256]{1,0:T(8,128)(2,1)S(1)}, u32[]{:S(2)}, u32[]{:S(2)}) collective-permute-start(bf16[2048,256]{1,0:T(8,128)(2,1)} %collective-permute-done.5.refs_2_), channel_id=1, source_target_pairs={{0,1},{1,0},{2,3},{3,2},{4,5},{5,4},{6,7},{7,6},{8,9},{9,8},{10,11... | collective-permute-start | bytes 3145736 | tf_op jit(solution)/shard_map/ppermute | solution.py:582
  40.5 4.1 %collective-permute-start.8 = (bf16[2048,256]{1,0:T(8,128)(2,1)}, bf16[2048,256]{1,0:T(8,128)(2,1)}, u32[]{:S(2)}, u32[]{:S(2)}) collective-permute-start(bf16[2048,256]{1,0:T(8,128)(2,1)} %collective-permute-done.6.refs_4_), channel_id=1, source_target_pairs={{0,1},{1,0},{2,3},{3,2},{4,5},{5,4},{6,7},{7,6},{8,9},{9,8},{10,11... | collective-permute-start | bytes 3145736 | tf_op jit(solution)/shard_map/ppermute | solution.py:582
  40.6 13.2 %collective-permute-start.9 = (bf16[112,2048]{1,0:T(8,128)(2,1)}, bf16[112,2048]{1,0:T(8,128)(2,1)}, u32[]{:S(2)}, u32[]{:S(2)}) collective-permute-start(bf16[112,2048]{1,0:T(8,128)(2,1)} %get-tuple-element.61.upper_ref), channel_id=1, source_target_pairs={{0,4},{1,5},{2,6},{3,7},{4,0},{5,1},{6,2},{7,3},{8,12},{9,13},{10,... | collective-permute-start | bytes 1376264 | tf_op jit(solution)/shard_map/ppermute | solution.py:587
  41.6 12.9 %collective-permute-start.10 = (bf16[112,2048]{1,0:T(8,128)(2,1)}, bf16[112,2048]{1,0:T(8,128)(2,1)}, u32[]{:S(2)}, u32[]{:S(2)}) collective-permute-start(bf16[112,2048]{1,0:T(8,128)(2,1)} %get-tuple-element.62.lower_ref), channel_id=1, source_target_pairs={{0,2},{1,3},{2,0},{3,1},{4,6},{5,7},{6,4},{7,5},{8,10},{9,11},{10,... | collective-permute-start | bytes 1376264 | tf_op jit(solution)/shard_map/ppermute | solution.py:587
  54.5 13.0 %copy-start = (bf16[2048,1024]{1,0:T(8,128)(2,1)S(1)}, bf16[2048,1024]{1,0:T(8,128)(2,1)}, u32[]{:S(2)}) copy-start(bf16[2048,1024]{1,0:T(8,128)(2,1)} %up_ref.7) | copy-start | bytes 12582916
  54.5 13.0 %copy-start.1 = (bf16[1024,2048]{1,0:T(8,128)(2,1)S(1)}, bf16[1024,2048]{1,0:T(8,128)(2,1)}, u32[]{:S(2)}) copy-start(bf16[1024,2048]{1,0:T(8,128)(2,1)} %down_ref.7) | copy-start | bytes 12582916
  57.4 6.9 %collective-permute-start.11 = (bf16[112,1024]{1,0:T(8,128)(2,1)S(1)}, bf16[112,1024]{1,0:T(8,128)(2,1)S(1)}, u32[]{:S(2)}, u32[]{:S(2)}) collective-permute-start(bf16[112,1024]{1,0:T(8,128)(2,1)S(1)} %get-tuple-element.77), channel_id=1, source_target_pairs={{0,4},{1,5},{2,6},{3,7},{4,0},{5,1},{6,2},{7,3},{8,12},{9,13},{10,... | collective-permute-start | bytes 688136 | tf_op jit(solution)/shard_map/ppermute | solution.py:587
  58.4 6.6 %collective-permute-start.12 = (bf16[112,1024]{1,0:T(8,128)(2,1)S(1)}, bf16[112,1024]{1,0:T(8,128)(2,1)S(1)}, u32[]{:S(2)}, u32[]{:S(2)}) collective-permute-start(bf16[112,1024]{1,0:T(8,128)(2,1)S(1)} %get-tuple-element.78), channel_id=1, source_target_pairs={{0,2},{1,3},{2,0},{3,1},{4,6},{5,7},{6,4},{7,5},{8,10},{9,11},{10,... | collective-permute-start | bytes 688136 | tf_op jit(solution)/shard_map/ppermute | solution.py:587
  65.6 1.9 %collective-permute-start.14 = (bf16[112,2048]{1,0:T(8,128)(2,1)S(1)}, bf16[112,2048]{1,0:T(8,128)(2,1)S(1)}, u32[]{:S(2)}, u32[]{:S(2)}) collective-permute-start(bf16[112,2048]{1,0:T(8,128)(2,1)S(1)} %combine.1.mine_ref), channel_id=1, source_target_pairs={{0,1},{1,0},{2,3},{3,2},{4,5},{5,4},{6,7},{7,6},{8,9},{9,8},{10,11... | collective-permute-start | bytes 1376264 | tf_op jit(solution)/shard_map/ppermute | solution.py:582
  65.7 8.5 %collective-permute-start.13 = (bf16[112,2048]{1,0:T(8,128)(2,1)S(1)}, bf16[112,2048]{1,0:T(8,128)(2,1)S(1)}, u32[]{:S(2)}, u32[]{:S(2)}) collective-permute-start(bf16[112,2048]{1,0:T(8,128)(2,1)S(1)} %combine.1.mine_ref), channel_id=1, source_target_pairs={{0,2},{1,5},{2,0},{3,7},{4,6},{5,1},{6,4},{7,3},{8,10},{9,13},{10,... | collective-permute-start | bytes 1376264 | tf_op jit(solution)/shard_map/ppermute | solution.py:592
  74.2 1.8 %collective-permute-start.17 = (bf16[112,2048]{1,0:T(8,128)(2,1)S(1)}, bf16[112,2048]{1,0:T(8,128)(2,1)S(1)}, u32[]{:S(2)}, u32[]{:S(2)}) collective-permute-start(bf16[112,2048]{1,0:T(8,128)(2,1)S(1)} %collective-permute-done.13.mine_ref), channel_id=1, source_target_pairs={{0,1},{1,0},{2,3},{3,2},{4,5},{5,4},{6,7},{7,6},{8,9},{9,8},{10,11... | collective-permute-start | bytes 1376264 | tf_op jit(solution)/shard_map/ppermute | solution.py:582
  74.3 8.5 %collective-permute-start.19 = (bf16[112,2048]{1,0:T(8,128)(2,1)S(1)}, bf16[112,2048]{1,0:T(8,128)(2,1)S(1)}, u32[]{:S(2)}, u32[]{:S(2)}) collective-permute-start(bf16[112,2048]{1,0:T(8,128)(2,1)S(1)} %collective-permute-done.13.mine_ref), channel_id=1, source_target_pairs={{0,4},{1,3},{2,6},{3,1},{4,0},{5,7},{6,2},{7,5},{8,12},{9,11},{10,... | collective-permute-start | bytes 1376264 | tf_op jit(solution)/shard_map/ppermute | solution.py:592
  78.7 4.0 %collective-permute-start.18 = (bf16[112,1024]{1,0:T(8,128)(2,1)S(1)}, bf16[112,1024]{1,0:T(8,128)(2,1)S(1)}, u32[]{:S(2)}, u32[]{:S(2)}) collective-permute-start(bf16[112,1024]{1,0:T(8,128)(2,1)S(1)} %get-tuple-element.86), channel_id=1, source_target_pairs={{0,1},{1,0},{2,3},{3,2},{4,5},{5,4},{6,7},{7,6},{8,9},{9,8},{10,11... | collective-permute-start | bytes 688136 | tf_op jit(solution)/shard_map/ppermute | solution.py:582
  82.7 1.8 %collective-permute-start.20 = (bf16[112,2048]{1,0:T(8,128)(2,1)S(1)}, bf16[112,2048]{1,0:T(8,128)(2,1)S(1)}, u32[]{:S(2)}, u32[]{:S(2)}) collective-permute-start(bf16[112,2048]{1,0:T(8,128)(2,1)S(1)} %collective-permute-done.19.mine_ref), channel_id=1, source_target_pairs={{0,1},{1,0},{2,3},{3,2},{4,5},{5,4},{6,7},{7,6},{8,9},{9,8},{10,11... | collective-permute-start | bytes 1376264 | tf_op jit(solution)/shard_map/ppermute | solution.py:582
  82.7 8.5 %collective-permute-start.23 = (bf16[112,2048]{1,0:T(8,128)(2,1)S(1)}, bf16[112,2048]{1,0:T(8,128)(2,1)S(1)}, u32[]{:S(2)}, u32[]{:S(2)}) collective-permute-start(bf16[112,2048]{1,0:T(8,128)(2,1)S(1)} %combine.1.mine_ref), channel_id=1, source_target_pairs={{0,4},{1,3},{2,6},{3,1},{4,0},{5,7},{6,2},{7,5},{8,12},{9,11},{10,... | collective-permute-start | bytes 1376264 | tf_op jit(solution)/shard_map/ppermute | solution.py:592
  87.2 4.0 %collective-permute-start.21 = (bf16[112,1024]{1,0:T(8,128)(2,1)S(1)}, bf16[112,1024]{1,0:T(8,128)(2,1)S(1)}, u32[]{:S(2)}, u32[]{:S(2)}) collective-permute-start(bf16[112,1024]{1,0:T(8,128)(2,1)S(1)} %get-tuple-element.88), channel_id=1, source_target_pairs={{0,1},{1,0},{2,3},{3,2},{4,5},{5,4},{6,7},{7,6},{8,9},{9,8},{10,11... | collective-permute-start | bytes 688136 | tf_op jit(solution)/shard_map/ppermute | solution.py:582
  87.4 3.9 %collective-permute-start.22 = (bf16[112,1024]{1,0:T(8,128)(2,1)S(1)}, bf16[112,1024]{1,0:T(8,128)(2,1)S(1)}, u32[]{:S(2)}, u32[]{:S(2)}) collective-permute-start(bf16[112,1024]{1,0:T(8,128)(2,1)S(1)} %get-tuple-element.89), channel_id=1, source_target_pairs={{0,1},{1,0},{2,3},{3,2},{4,5},{5,4},{6,7},{7,6},{8,9},{9,8},{10,11... | collective-permute-start | bytes 688136 | tf_op jit(solution)/shard_map/ppermute | solution.py:582
  91.2 1.8 %collective-permute-start.24 = (bf16[112,2048]{1,0:T(8,128)(2,1)S(1)}, bf16[112,2048]{1,0:T(8,128)(2,1)S(1)}, u32[]{:S(2)}, u32[]{:S(2)}) collective-permute-start(bf16[112,2048]{1,0:T(8,128)(2,1)S(1)} %collective-permute-done.23.mine_ref), channel_id=1, source_target_pairs={{0,1},{1,0},{2,3},{3,2},{4,5},{5,4},{6,7},{7,6},{8,9},{9,8},{10,11... | collective-permute-start | bytes 1376264 | tf_op jit(solution)/shard_map/ppermute | solution.py:582
  91.4 8.5 %collective-permute-start.28 = (bf16[112,2048]{1,0:T(8,128)(2,1)S(1)}, bf16[112,2048]{1,0:T(8,128)(2,1)S(1)}, u32[]{:S(2)}, u32[]{:S(2)}) collective-permute-start(bf16[112,2048]{1,0:T(8,128)(2,1)S(1)} %add_convert_fusion.1), channel_id=1, source_target_pairs={{0,4},{1,3},{2,6},{3,1},{4,0},{5,7},{6,2},{7,5},{8,12},{9,11},{10,... | collective-permute-start | bytes 1376264 | tf_op jit(solution)/shard_map/ppermute | solution.py:592
  92.4 3.7 %collective-permute-start.30 = (bf16[112,1024]{1,0:T(8,128)(2,1)S(1)}, bf16[112,1024]{1,0:T(8,128)(2,1)S(1)}, u32[]{:S(2)}, u32[]{:S(2)}) collective-permute-start(bf16[112,1024]{1,0:T(8,128)(2,1)S(1)} %get-tuple-element.101), channel_id=1, source_target_pairs={{0,1},{1,0},{2,3},{3,2},{4,5},{5,4},{6,7},{7,6},{8,9},{9,8},{10,11... | collective-permute-start | bytes 688136 | tf_op jit(solution)/shard_map/ppermute | solution.py:582
  92.4 11.0 %collective-permute-start.16 = (bf16[112,1024]{1,0:T(8,128)(2,1)S(1)}, bf16[112,1024]{1,0:T(8,128)(2,1)S(1)}, u32[]{:S(2)}, u32[]{:S(2)}) collective-permute-start(bf16[112,1024]{1,0:T(8,128)(2,1)S(1)} %get-tuple-element.84), channel_id=1, source_target_pairs={{0,1},{1,0},{2,3},{3,2},{4,5},{5,4},{6,7},{7,6},{8,9},{9,8},{10,11... | collective-permute-start | bytes 688136 | tf_op jit(solution)/shard_map/ppermute | solution.py:582
  92.9 10.5 %collective-permute-start.15 = (bf16[112,1024]{1,0:T(8,128)(2,1)S(1)}, bf16[112,1024]{1,0:T(8,128)(2,1)S(1)}, u32[]{:S(2)}, u32[]{:S(2)}) collective-permute-start(bf16[112,1024]{1,0:T(8,128)(2,1)S(1)} %get-tuple-element.83), channel_id=1, source_target_pairs={{0,1},{1,0},{2,3},{3,2},{4,5},{5,4},{6,7},{7,6},{8,9},{9,8},{10,11... | collective-permute-start | bytes 688136 | tf_op jit(solution)/shard_map/ppermute | solution.py:582
  95.7 5.0 %collective-permute-start.26 = (bf16[112,1024]{1,0:T(8,128)(2,1)S(1)}, bf16[112,1024]{1,0:T(8,128)(2,1)S(1)}, u32[]{:S(2)}, u32[]{:S(2)}) collective-permute-start(bf16[112,1024]{1,0:T(8,128)(2,1)S(1)} %get-tuple-element.95), channel_id=1, source_target_pairs={{0,1},{1,0},{2,3},{3,2},{4,5},{5,4},{6,7},{7,6},{8,9},{9,8},{10,11... | collective-permute-start | bytes 688136 | tf_op jit(solution)/shard_map/ppermute | solution.py:582
  96.1 6.1 %collective-permute-start.25 = (bf16[112,1024]{1,0:T(8,128)(2,1)S(1)}, bf16[112,1024]{1,0:T(8,128)(2,1)S(1)}, u32[]{:S(2)}, u32[]{:S(2)}) collective-permute-start(bf16[112,1024]{1,0:T(8,128)(2,1)S(1)} %get-tuple-element.94), channel_id=1, source_target_pairs={{0,1},{1,0},{2,3},{3,2},{4,5},{5,4},{6,7},{7,6},{8,9},{9,8},{10,11... | collective-permute-start | bytes 688136 | tf_op jit(solution)/shard_map/ppermute | solution.py:582
  100.1 8.2 %collective-permute-start.31 = (bf16[112,1024]{1,0:T(8,128)(2,1)S(1)}, bf16[112,1024]{1,0:T(8,128)(2,1)S(1)}, u32[]{:S(2)}, u32[]{:S(2)}) collective-permute-start(bf16[112,1024]{1,0:T(8,128)(2,1)S(1)} %get-tuple-element.103), channel_id=1, source_target_pairs={{0,2},{1,5},{2,0},{3,7},{4,6},{5,1},{6,4},{7,3},{8,10},{9,13},{10,... | collective-permute-start | bytes 688136 | tf_op jit(solution)/shard_map/ppermute | solution.py:592
  100.7 12.6 %collective-permute-start.29 = (bf16[112,1024]{1,0:T(8,128)(2,1)S(1)}, bf16[112,1024]{1,0:T(8,128)(2,1)S(1)}, u32[]{:S(2)}, u32[]{:S(2)}) collective-permute-start(bf16[112,1024]{1,0:T(8,128)(2,1)S(1)} %get-tuple-element.102), channel_id=1, source_target_pairs={{0,2},{1,5},{2,0},{3,7},{4,6},{5,1},{6,4},{7,3},{8,10},{9,13},{10,... | collective-permute-start | bytes 688136 | tf_op jit(solution)/shard_map/ppermute | solution.py:592
  102.4 10.9 %collective-permute-start.27 = (bf16[112,2048]{1,0:T(8,128)(2,1)S(1)}, bf16[112,2048]{1,0:T(8,128)(2,1)S(1)}, u32[]{:S(2)}, u32[]{:S(2)}) collective-permute-start(bf16[112,2048]{1,0:T(8,128)(2,1)S(1)} %add_convert_fusion.2), channel_id=1, source_target_pairs={{0,4},{1,3},{2,6},{3,1},{4,0},{5,7},{6,2},{7,5},{8,12},{9,11},{10,... | collective-permute-start | bytes 1376264 | tf_op jit(solution)/shard_map/ppermute | solution.py:592

commit v11 on v9

--- a/solution.py
+++ b/solution.py
@@ -94,16 +94,35 @@
             start += padded
         return g.astype(BF16), head
 
-    def patch_matrix(self):
-        cells = self.rows * self.columns // 4
-        padded = up16(cells)
-        g = np.zeros((4 * padded, self.rows * self.columns), np.float32)
-        for r in range(self.rows // 2):
-            for c in range(self.columns // 2):
+    def inner_patches(self):
+        rows = range(self.rows // 2)
+        inner = [r for r in rows if 2 * r >= RIM_LAT and 2 * r + 1 < self.rows - RIM_LAT]
+        return inner, [r for r in rows if r not in inner]
+
+    def patch_matrix(self, patch_rows, place, sources):
+        half = self.columns // 2
+        padded = up16(len(patch_rows) * half)
+        g = np.zeros((4 * padded, sources), np.float32)
+        for n, r in enumerate(patch_rows):
+            for c in range(half):
                 for k in range(4):
-                    to = k * padded + r * (self.columns // 2) + c
-                    g[to, (2 * r + k // 2) * self.columns + 2 * c + k % 2] = 1
+                    g[k * padded + n * half + c, place(2 * r + k // 2) + 2 * c + k % 2] = 1
         return g.astype(BF16)
+
+    def inner_patch_matrix(self):
+        return self.patch_matrix(
+            self.inner_patches()[0],
+            lambda i: (i - RIM_LAT) * self.columns,
+            (self.rows - 2 * RIM_LAT) * self.columns,
+        )
+
+    def edge_patch_matrix(self):
+        last = self.rows - RIM_LAT - 1
+        return self.patch_matrix(
+            self.inner_patches()[1],
+            lambda i: (i if i <= RIM_LAT else RIM_LAT + 1 + i - last) * self.columns,
+            2 * (RIM_LAT + 1) * self.columns,
+        )
 
     def constants(self, some, block):
         distinct, kinds, consts = [], [], []
@@ -231,7 +250,7 @@
         scratch_shapes=[
             pltpu.VMEM((bands.own_total, width), BF16),
             pltpu.VMEM((width, width), BF16),
-            pltpu.SemaphoreType.DMA((6,)),
+            pltpu.SemaphoreType.DMA((3,)),
         ],
         compiler_params=params(42),
         cost_estimate=pl.CostEstimate(
@@ -298,8 +317,24 @@
     ]
 
 
-def middle_kernel(bands, some, kinds, west_ref, east_ref, own_ref, weight_ref, *rest):
-    consts, (side_ref, out_ref, normed_ref, *scratch) = rest[:-8], rest[-8:]
+def merge_rows(patch_ref, cells, upper_ref, lower_ref, first):
+    width = cells.shape[1]
+    padded = patch_ref.shape[0] // 4
+    parts = [dot(patch_ref[k * padded : (k + 1) * padded, :], cells) for k in range(4)]
+    total = sum(jnp.sum(p, axis=-1, keepdims=True) for p in parts)
+    mean = total * (1.0 / (4 * width))
+    parts = [p - mean for p in parts]
+    spread = sum(jnp.sum(p * p, axis=-1, keepdims=True) for p in parts)
+    factor = lax.rsqrt(spread * (1.0 / (4 * width)) + 1e-05)
+    for k in range(4):
+        ref = (upper_ref, lower_ref)[k // 2]
+        ref[first : first + padded, k % 2 * width : (k % 2 + 1) * width] = (parts[k] * factor).astype(BF16)
+
+
+def middle_kernel(bands, some, kinds, tokens_ref, west_ref, east_ref, own_ref, weight_ref, out_w_ref, patch_ref, *rest):
+    consts, rest = rest[:-11], rest[-11:]
+    side_ref, middle_ref, upper_ref, lower_ref, normed_ref, attended_ref, *scratch = rest
+    rows, columns, width = tokens_ref.shape
     west, east = flat_normed(west_ref), flat_normed(east_ref)
     for b in range(bands.count):
         at, size = bands.first[b] * SIDE, bands.height[b] * SIDE
@@ -313,12 +348,16 @@
     def put(b, g, value):
         at = bands.own_at[b] - bands.own_at[1]
         block = value.shape[1]
-        out_ref[at : at + bands.own_padded[b], g * block : (g + 1) * block] = value
+        attended_ref[at : at + bands.own_padded[b], g * block : (g + 1) * block] = value
 
     attend(bands, some, kinds, consts, own_ref, outer, None, put, scratch)
-
-
-def edge_kernel(bands, some, kinds, tokens_ref, north_ref, south_ref, bias_ref, own_ref, side_ref, inner_ref, weight_ref, out_w_ref, patch_ref, *rest):
+    mixed = dot(attended_ref[...], out_w_ref[...])
+    middle = tokens_ref[RIM_LAT : rows - RIM_LAT].astype(F32) + mixed.reshape(-1, columns, width)
+    middle_ref[...] = middle.astype(BF16)
+    merge_rows(patch_ref, middle.reshape(-1, width).astype(BF16), upper_ref, lower_ref, 0)
+
+
+def edge_kernel(bands, some, kinds, tokens_ref, north_ref, south_ref, bias_ref, own_ref, side_ref, inner_ref, inner_upper_ref, inner_lower_ref, weight_ref, out_w_ref, patch_ref, *rest):
     consts, rest = rest[:-11], rest[-11:]
     middle_ref, upper_ref, lower_ref, normed_ref, slab_ref, attended_ref, *scratch = rest
     rows, columns, width = tokens_ref.shape
@@ -335,25 +374,23 @@
 
     def put(b, g, value):
         block = value.shape[1]
-        attended_ref[bands.own_at[b] : bands.own_at[b] + bands.own_padded[b], g * block : (g + 1) * block] = value
-
-    attended_ref[bands.own_at[1] : bands.own_at[-1], :] = inner_ref[...]
+        at = 0 if b == 0 else bands.own_padded[0]
+        attended_ref[at : at + bands.own_padded[b], g * block : (g + 1) * block] = value
+
     attend(bands, some, kinds, consts, own_ref, outer, bias_ref, put, scratch)
     mixed = dot(attended_ref[...], out_w_ref[...])
-    mixed = jnp.concatenate([mixed[at : at + n] for at, n in zip(bands.own_at, bands.own)], axis=0)
-    middle = tokens_ref[...].astype(F32) + mixed.reshape(rows, columns, width)
-    middle_ref[...] = middle.astype(BF16)
-    middle = middle.reshape(rows * columns, width).astype(BF16)
-    padded = patch_ref.shape[0] // 4
-    parts = [dot(patch_ref[k * padded : (k + 1) * padded, :], middle) for k in range(4)]
-    total = sum(jnp.sum(p, axis=-1, keepdims=True) for p in parts)
-    mean = total * (1.0 / (4 * width))
-    parts = [p - mean for p in parts]
-    spread = sum(jnp.sum(p * p, axis=-1, keepdims=True) for p in parts)
-    factor = lax.rsqrt(spread * (1.0 / (4 * width)) + 1e-05)
-    for k in range(4):
-        ref = (upper_ref, lower_ref)[k // 2]
-        ref[:, k % 2 * width : (k % 2 + 1) * width] = (parts[k] * factor).astype(BF16)
+    low = bands.own_padded[0]
+    top = tokens_ref[:RIM_LAT].astype(F32) + mixed[: bands.own[0]].reshape(-1, columns, width)
+    bottom = tokens_ref[rows - RIM_LAT :].astype(F32) + mixed[low : low + bands.own[-1]].reshape(-1, columns, width)
+    middle_ref[:RIM_LAT] = top.astype(BF16)
+    middle_ref[RIM_LAT : rows - RIM_LAT] = inner_ref[...]
+    middle_ref[rows - RIM_LAT :] = bottom.astype(BF16)
+    first, last = inner_ref[0].astype(F32), inner_ref[rows - 2 * RIM_LAT - 1].astype(F32)
+    cells = jnp.concatenate([top.reshape(-1, width), first, last, bottom.reshape(-1, width)], axis=0)
+    inner_count = inner_upper_ref.shape[0]
+    upper_ref[:inner_count, :] = inner_upper_ref[...]
+    lower_ref[:inner_count, :] = inner_lower_ref[...]
+    merge_rows(patch_ref, cells.astype(BF16), upper_ref, lower_ref, inner_count)
 
 
 def vmem_call(kernel, out, args, scratch, flops, name, mib=24, exps=0):
@@ -385,25 +422,37 @@
     inner = list(range(1, bands.count - 1))
     edges = [0, bands.count - 1]
     kinds, consts = bands.constants(inner, block)
-    side, attended = vmem_call(
+    patch = bands.inner_patch_matrix()
+    inner_count = patch.shape[0] // 4
+    side, middle, upper, lower = vmem_call(
         functools.partial(middle_kernel, bands, inner, kinds),
-        [(bands.side_total, 2 * width), (bands.own_at[-1] - bands.own_at[1], width)],
-        [west, east, own, kv_weight] + consts,
-        [pltpu.VMEM((bands.side_total, width), BF16)] + attend_scratch(bands, inner, block),
+        [
+            (bands.side_total, 2 * width),
+            (rows - 2 * RIM_LAT, columns, width),
+            (inner_count, 2 * width),
+            (inner_count, 2 * width),
+        ],
+        [tokens, west, east, own, kv_weight, out_weight, patch] + consts,
+        [
+            pltpu.VMEM((bands.side_total, width), BF16),
+            pltpu.VMEM((bands.own_at[-1] - bands.own_at[1], width), BF16),
+        ]
+        + attend_scratch(bands, inner, block),
         5 * 10**9,
         "middle_attention",
         exps=500000,
     )
     kinds, consts = bands.constants(edges, block)
-    padded = up16(rows * columns // 4)
+    patch = bands.edge_patch_matrix()
+    count = inner_count + patch.shape[0] // 4
     return vmem_call(
         functools.partial(edge_kernel, bands, edges, kinds),
-        [tokens.shape, (padded, 2 * width), (padded, 2 * width)],
-        [tokens, north, south, key_bias(), own, side, attended, kv_weight, out_weight, bands.patch_matrix()] + consts,
+        [tokens.shape, (count, 2 * width), (count, 2 * width)],
+        [tokens, north, south, key_bias(), own, side, middle, upper, lower, kv_weight, out_weight, patch] + consts,
         [
             pltpu.VMEM((2 * bands.slab_padded, width), BF16),
             pltpu.VMEM((2 * bands.slab_padded, 2 * width), BF16),
-            pltpu.VMEM((bands.own_total, width), BF16),
+            pltpu.VMEM((bands.own_padded[0] + bands.own_padded[-1], width), BF16),
         ]
         + attend_scratch(bands, edges, block),
         6 * 10**9,
@@ -628,14 +677,19 @@
 def per_device(tokens, qkv_weight, out_weight, merge_weight, up_weight, down_weight):
     rows, columns, width = tokens.shape
     bands = Bands(rows, columns)
-    cells = rows * columns // 4
     sides = rims(tokens)
     *sides, later = lax.optimization_barrier((*sides, merge_weight))
     halves = halves_of(later)
     middle_out, upper, lower = attention(bands, tokens, sides, qkv_weight, out_weight)
     coarse = coarse_by_squares if lax.axis_size("lon") == 8 else coarse_by_chips
     total = coarse(upper, lower, merge_weight, halves, up_weight, down_weight)
-    coarse_out = total[:cells].astype(jnp.bfloat16)
+    inner, edge = bands.inner_patches()
+    half = columns // 2
+    above = half * sum(r < inner[0] for r in edge)
+    start = up16(half * len(inner))
+    below = start + half * len(edge)
+    ordered = [total[start : start + above], total[: half * len(inner)], total[start + above : below]]
+    coarse_out = jnp.concatenate(ordered, axis=0).astype(jnp.bfloat16)
     return (middle_out, coarse_out.reshape(rows // 2, columns // 2, -1))
 
 

time: 111 us -> 112 us (level)
  starting transfers between devices: 22 us -> 24.1 us
  waiting for transfers between devices: 46.3 us -> 44.4 us
    ppermute x4, waiting for transfers between devices: 4.13 us -> 2.7 us  [shift(): return lax.ppermute(part, axis, pairs)]
    ppermute x7, starting transfers between devices: 5.27 us -> 6.69 us  [cross(): lax.ppermute(value, 'lon', [(i, i ^ 2 * (second if i % 2 else first)) for...]
  transfers between devices with their start and end apart: 32 -> 32, of which waited for: 18 -> 19; matrix products, arithmetic and copies ran while one was open for 1% -> 1% of each run, Pallas kernels for 32% -> 32%
where the time goes in v11:
time: 112 us
  waiting for transfers between devices  44.4 us (40%)
  Pallas kernels  39.2 us (35%)
  starting transfers between devices  24.1 us (22%)
  local copies, waits for them, and re-layouts  2.24 us (2%)
    ppermute x7, waiting for transfers between devices, cross(): lax.ppermute(value, 'lon', [(i, i ^ 2 * (second if i % 2 else first)) for...  24.7 us
    pallas_call x2, Pallas kernels, vmem_call(): pl.pallas_call(kernel, in_specs=[vmem] * len(args), out_specs=[vmem] * le...  12.5 us
    ppermute x6, waiting for transfers between devices, chip_swap(): lax.ppermute(value, 'lon', [(i, i ^ 2 * offset) for i in range(size)])  10.7 us
    pallas_call x4, Pallas kernels, feed_forward(): pl.pallas_call(ffn_kernel, in_specs=[vmem] * 4, out_specs=[vmem] * 3, out...  10.4 us
    ppermute x4, starting transfers between devices, shift(): return lax.ppermute(part, axis, pairs)  8.58 us
    pallas_call x3, Pallas kernels, local_call(): pl.pallas_call(kernel, in_specs=[pl.BlockSpec(memory_space=pltpu.SMEM)] +...  8.12 us
    ppermute x7, starting transfers between devices, cross(): lax.ppermute(value, 'lon', [(i, i ^ 2 * (second if i % 2 else first)) for...  6.69 us
    ppermute x15, waiting for transfers between devices, core_swap(): return lax.ppermute(value, 'lon', [(i, i ^ 1) for i in range(size)])  6.21 us
  transfers between devices with their start and end apart: 32, of which 19 were waited for; matrix products, arithmetic and copies ran while one was open for 1% of the time, Pallas kernels for 32%

profile of v11, /device:TPU:0, one launch (start us, length us, event | category | flops | bytes accessed | tf_op | source)
XLA Modules:
  0.0 112.0 jit_solution(8681527127416665469)
XLA Ops:
  0.6 0.5 collective-permute-start.4
  1.1 1.2 %copy-done.3 = bf16[18,24,1024]{2,1,0:T(8,128)(2,1)S(1)} copy-done((bf16[18,24,1024]{2,1,0:T(8,128)(2,1)S(1)}, bf16[18,24,1024]{2,1,0:T(8,128)(2,1)}, u32[]{:S(2)}) %copy-start.3) | copy-done | bytes 884760
  2.4 3.6 %collective-permute-start.1 = (bf16[18,8,1024]{2,1,0:T(8,128)(2,1)S(1)}, bf16[18,8,1024]{2,1,0:T(8,128)(2,1)S(1)}, u32[]{:S(2)}, u32[]{:S(2)}) collective-permute-start(bf16[18,8,1024]{2,1,0:T(8,128)(2,1)S(1)} %get-tuple-element.56), channel_id=1, source_target_pairs={{0,7},{1,0},{2,1},{3,2},{4,3},{5,4},{6,5},{7,6},{8,15},{9,8},{10,9... | collective-permute-start | bytes 884744 | tf_op jit(solution)/shard_map/ppermute | solution.py:467
  6.0 2.9 %halves.1 = (bf16[2048,256]{1,0:T(8,128)(2,1)}, bf16[2048,256]{1,0:T(8,128)(2,1)}) custom-call(bf16[4096,256]{1,0:T(8,128)(2,1)} %refs_0_.1), custom_call_target="tpu_custom_call" | custom-call | tf_op jit(solution)/shard_map/halves/pallas_call | solution.py:202
  8.9 0.1 collective-permute-start.5
  9.0 1.1 collective-permute-start.6
  10.2 5.2 %own_projection.1 = (bf16[448,3072]{1,0:T(8,128)(2,1)S(1)}, bf16[1024,2048]{1,0:T(8,128)(2,1)S(1)}) custom-call(bf16[18,24,1024]{2,1,0:T(8,128)(2,1)S(1)} %copy-done.4, bf16[1024,3072]{1,0:T(8,128)(2,1)} %weight_ref.1), custom_call_target="tpu_custom_call" | custom-call | flops 2818572288 | bytes 6291456 | tf_op jit(solution)/shard_map/own_projection/pallas_call | solution.py:242
  15.5 0.1 or_select_fusion.bias_ref
  15.6 0.4 collective-permute-done.west_ref
  16.0 3.5 %collective-permute-start.2 = (bf16[3,40,1024]{2,1,0:T(8,128)(2,1)S(1)}, bf16[3,40,1024]{2,1,0:T(8,128)(2,1)S(1)}, u32[]{:S(2)}, u32[]{:S(2)}) collective-permute-start(bf16[3,40,1024]{2,1,0:T(8,128)(2,1)S(1)} %pad_maximum_fusion.1), channel_id=1, source_target_pairs={{0,8},{8,16},{16,24},{1,9},{9,17},{17,25},{2,10},{10,18},{18,26},{... | collective-permute-start | bytes 737288 | tf_op jit(solution)/shard_map/ppermute | solution.py:467
  19.5 1.5 %collective-permute-start.3 = (bf16[3,40,1024]{2,1,0:T(8,128)(2,1)S(1)}, bf16[3,40,1024]{2,1,0:T(8,128)(2,1)S(1)}, u32[]{:S(2)}, u32[]{:S(2)}) collective-permute-start(bf16[3,40,1024]{2,1,0:T(8,128)(2,1)S(1)} %pad_maximum_fusion.2), channel_id=1, source_target_pairs={{8,0},{16,8},{24,16},{9,1},{17,9},{25,17},{10,2},{18,10},{26,18},{... | collective-permute-start | bytes 737288 | tf_op jit(solution)/shard_map/ppermute | solution.py:467
  21.2 6.5 %middle_attention.1 = (bf16[288,2048]{1,0:T(8,128)(2,1)S(1)}, bf16[12,24,1024]{2,1,0:T(8,128)(2,1)S(1)}, bf16[64,2048]{1,0:T(8,128)(2,1)S(1)}, bf16[64,2048]{1,0:T(8,128)(2,1)S(1)}) custom-call(bf16[18,24,1024]{2,1,0:T(8,128)(2,1)S(1)} %copy-done.4, bf16[18,8,1024]{2,1,0:T(8,128)(2,1)S(1)} %collective-permute-done.west_ref, ...), custom_call_target="tpu_custom_call" | custom-call | flops 5000000000 | bytes 1048576 | tf_op jit(solution)/shard_map/middle_attention/pallas_call | solution.py:398
  27.7 2.3 %collective-permute-done.3.south_ref = bf16[3,40,1024]{2,1,0:T(8,128)(2,1)S(1)} collective-permute-done((bf16[3,40,1024]{2,1,0:T(8,128)(2,1)S(1)}, bf16[3,40,1024]{2,1,0:T(8,128)(2,1)S(1)}, u32[]{:S(2)}, u32[]{:S(2)}) %collective-permute-start.3) | collective-permute-done | bytes 245792 | tf_op jit(solution)/shard_map/ppermute | solution.py:467
  30.0 6.0 %edge_attention.1 = (bf16[18,24,1024]{2,1,0:T(8,128)(2,1)}, bf16[112,2048]{1,0:T(8,128)(2,1)}, bf16[112,2048]{1,0:T(8,128)(2,1)}) custom-call(bf16[18,24,1024]{2,1,0:T(8,128)(2,1)S(1)} %copy-done.4, bf16[3,40,1024]{2,1,0:T(8,128)(2,1)S(1)} %collective-permute-done.2.north_ref, bf16[3,40,1024]{2,1,0:T(8,128)(2,1)S(1)} %collective-permute-done.3.south_ref, ...), custom_call_target="tpu_custom_call" | custom-call | flops 6000000000 | bytes 1048576 | tf_op jit(solution)/shard_map/edge_attention/pallas_call | solution.py:398
  36.0 0.6 collective-permute-done.6.refs_4_
  36.6 0.2 collective-permute-start.7
  36.8 0.3 collective-permute-start.8
  37.1 0.2 collective-permute-start.9
  37.3 2.1 %collective-permute-start.10 = (bf16[112,2048]{1,0:T(8,128)(2,1)}, bf16[112,2048]{1,0:T(8,128)(2,1)}, u32[]{:S(2)}, u32[]{:S(2)}) collective-permute-start(bf16[112,2048]{1,0:T(8,128)(2,1)} %get-tuple-element.65.lower_ref), channel_id=1, source_target_pairs={{0,2},{1,3},{2,0},{3,1},{4,6},{5,7},{6,4},{7,5},{8,10},{9,11},{10,... | collective-permute-start | bytes 1376264 | tf_op jit(solution)/shard_map/ppermute | solution.py:632
  39.4 0.1 pad_add_fusion.place_ref
  39.5 1.6 %collective-permute-done.8.refs_5_ = bf16[2048,256]{1,0:T(8,128)(2,1)} collective-permute-done((bf16[2048,256]{1,0:T(8,128)(2,1)}, bf16[2048,256]{1,0:T(8,128)(2,1)}, u32[]{:S(2)}, u32[]{:S(2)}) %collective-permute-start.8) | collective-permute-done | bytes 1048608 | tf_op jit(solution)/shard_map/ppermute | solution.py:627
  41.1 4.7 %merge_own.1 = (f32[112,512]{1,0:T(8,128)S(1)}, f32[112,512]{1,0:T(8,128)S(1)}, f32[112,512]{1,0:T(8,128)S(1)}, bf16[4096,256]{1,0:T(8,128)(2,1)S(1)}, bf16[4096...) custom-call(s32[2]{0:T(128)S(1)} %pad_add_fusion.place_ref, ...), custom_call_target="tpu_custom_call" | custom-call | flops 939524096 | bytes 1048576 | tf_op jit(solution)/shard_map/merge_own/pallas_call | solution.py:545
  45.8 4.2 %collective-permute-done.9.upper_ref = bf16[112,2048]{1,0:T(8,128)(2,1)} collective-permute-done((bf16[112,2048]{1,0:T(8,128)(2,1)}, bf16[112,2048]{1,0:T(8,128)(2,1)}, u32[]{:S(2)}, u32[]{:S(2)}) %collective-permute-start.9) | collective-permute-done | bytes 458784 | tf_op jit(solution)/shard_map/ppermute | solution.py:632
  50.0 0.3 collective-permute-done.10.lower_ref
  50.3 2.8 %merge_other.1 = (bf16[112,1024]{1,0:T(8,128)(2,1)S(1)}, bf16[112,1024]{1,0:T(8,128)(2,1)S(1)}) custom-call(s32[2]{0:T(128)S(1)} %pad_add_fusion.place_ref, bf16[112,2048]{1,0:T(8,128)(2,1)} %collective-permute-done.9.upper_ref, bf16[112,2048]{1,0:T(8,128)(2,1)} %collective-permute-done.10.lower_ref, bf16[4096,256]{1,0:T(8,128)(2,1)S(1)} %get-tuple-element.74.refs_0_, ...), custom_call_target="tpu_custom_call" | custom-call | flops 939524096 | bytes 1048576 | tf_op jit(solution)/shard_map/merge_other/pallas_call | solution.py:545
  53.1 1.6 %collective-permute-start.11 = (bf16[112,1024]{1,0:T(8,128)(2,1)S(1)}, bf16[112,1024]{1,0:T(8,128)(2,1)S(1)}, u32[]{:S(2)}, u32[]{:S(2)}) collective-permute-start(bf16[112,1024]{1,0:T(8,128)(2,1)S(1)} %get-tuple-element.80), channel_id=1, source_target_pairs={{0,4},{1,5},{2,6},{3,7},{4,0},{5,1},{6,2},{7,3},{8,12},{9,13},{10,... | collective-permute-start | bytes 688136 | tf_op jit(solution)/shard_map/ppermute | solution.py:632
  54.7 0.6 collective-permute-start.12
  55.3 4.7 %collective-permute-done.11.from_y_ref = bf16[112,1024]{1,0:T(8,128)(2,1)S(1)} collective-permute-done((bf16[112,1024]{1,0:T(8,128)(2,1)S(1)}, bf16[112,1024]{1,0:T(8,128)(2,1)S(1)}, u32[]{:S(2)}, u32[]{:S(2)}) %collective-permute-start.11) | collective-permute-done | bytes 229408 | tf_op jit(solution)/shard_map/ppermute | solution.py:632
  60.0 0.9 collective-permute-done.12.from_x_ref
  60.9 0.6 combine.1.mine_ref
  61.6 0.1 collective-permute-start.14
  61.7 0.8 collective-permute-start.13
  62.5 1.0 collective-permute-done.14.theirs_ref
  63.5 2.6 %feed_forward.4 = (bf16[112,2048]{1,0:T(8,128)(2,1)S(1)}, bf16[112,1024]{1,0:T(8,128)(2,1)S(1)}, bf16[112,1024]{1,0:T(8,128)(2,1)S(1)}) custom-call(bf16[112,2048]{1,0:T(8,128)(2,1)S(1)} %combine.1.mine_ref, bf16[112,2048]{1,0:T(8,128)(2,1)S(1)} %collective-permute-done.14.theirs_ref, bf16[2048,1024]{1,0:T(8,128)(2,1)S(1)} %copy-done, ...), custom_call_target="tpu_custom_call" | custom-call | flops 1879048192 | bytes 8388608 | tf_op jit(solution)/shard_map/feed_forward/pallas_call | solution.py:603
  66.1 4.1 %collective-permute-done.13.mine_ref = bf16[112,2048]{1,0:T(8,128)(2,1)S(1)} collective-permute-done((bf16[112,2048]{1,0:T(8,128)(2,1)S(1)}, bf16[112,2048]{1,0:T(8,128)(2,1)S(1)}, u32[]{:S(2)}, u32[]{:S(2)}) %collective-permute-start.13) | collective-permute-done | bytes 458784 | tf_op jit(solution)/shard_map/ppermute | solution.py:637
  70.2 0.8 collective-permute-start.19
  71.0 1.0 collective-permute-done.17.theirs_ref
  72.0 2.6 %feed_forward.5 = (bf16[112,2048]{1,0:T(8,128)(2,1)S(1)}, bf16[112,1024]{1,0:T(8,128)(2,1)S(1)}, bf16[112,1024]{1,0:T(8,128)(2,1)S(1)}) custom-call(bf16[112,2048]{1,0:T(8,128)(2,1)S(1)} %collective-permute-done.13.mine_ref, bf16[112,2048]{1,0:T(8,128)(2,1)S(1)} %collective-permute-done.17.theirs_ref, bf16[2048,1024]{1,0:T(8,128)(2,1)S(1)} %copy-done, ...), custom_call_target="tpu_custom_call" | custom-call | flops 1879048192 | bytes 8388608 | tf_op jit(solution)/shard_map/feed_forward/pallas_call | solution.py:603
  74.6 0.2 collective-permute-start.18
  74.8 3.9 %collective-permute-done.19.mine_ref = bf16[112,2048]{1,0:T(8,128)(2,1)S(1)} collective-permute-done((bf16[112,2048]{1,0:T(8,128)(2,1)S(1)}, bf16[112,2048]{1,0:T(8,128)(2,1)S(1)}, u32[]{:S(2)}, u32[]{:S(2)}) %collective-permute-start.19) | collective-permute-done | bytes 458784 | tf_op jit(solution)/shard_map/ppermute | solution.py:637
  78.7 0.8 collective-permute-start.22
  79.5 1.0 collective-permute-done.20.theirs_ref
  80.5 2.6 %feed_forward.6 = (bf16[112,2048]{1,0:T(8,128)(2,1)S(1)}, bf16[112,1024]{1,0:T(8,128)(2,1)S(1)}, bf16[112,1024]{1,0:T(8,128)(2,1)S(1)}) custom-call(bf16[112,2048]{1,0:T(8,128)(2,1)S(1)} %collective-permute-done.19.mine_ref, bf16[112,2048]{1,0:T(8,128)(2,1)S(1)} %collective-permute-done.20.theirs_ref, bf16[2048,1024]{1,0:T(8,128)(2,1)S(1)} %copy-done, ...), custom_call_target="tpu_custom_call" | custom-call | flops 1879048192 | bytes 8388608 | tf_op jit(solution)/shard_map/feed_forward/pallas_call | solution.py:603
  83.1 0.2 collective-permute-start.21
  83.3 3.8 %collective-permute-done.22.mine_ref = bf16[112,2048]{1,0:T(8,128)(2,1)S(1)} collective-permute-done((bf16[112,2048]{1,0:T(8,128)(2,1)S(1)}, bf16[112,2048]{1,0:T(8,128)(2,1)S(1)}, u32[]{:S(2)}, u32[]{:S(2)}) %collective-permute-start.22) | collective-permute-done | bytes 458784 | tf_op jit(solution)/shard_map/ppermute | solution.py:637
  87.2 0.5 collective-permute-start.27
  87.7 0.5 collective-permute-start.15
  88.2 0.8 collective-permute-done.23.theirs_ref
  89.0 2.6 %feed_forward.7 = (bf16[112,2048]{1,0:T(8,128)(2,1)S(1)}, bf16[112,1024]{1,0:T(8,128)(2,1)S(1)}, bf16[112,1024]{1,0:T(8,128)(2,1)S(1)}) custom-call(bf16[112,2048]{1,0:T(8,128)(2,1)S(1)} %collective-permute-done.22.mine_ref, bf16[112,2048]{1,0:T(8,128)(2,1)S(1)} %collective-permute-done.23.theirs_ref, bf16[2048,1024]{1,0:T(8,128)(2,1)S(1)} %copy-done, ...), custom_call_target="tpu_custom_call" | custom-call | flops 1879048192 | bytes 8388608 | tf_op jit(solution)/shard_map/feed_forward/pallas_call | solution.py:603
  91.6 0.2 collective-permute-start.25
  91.8 0.4 collective-permute-start.24
  92.2 0.1 add_convert_fusion.1
  92.3 0.9 collective-permute-done.25
  93.1 0.9 collective-permute-start.28
  94.0 0.1 add_convert_fusion.2
  94.1 1.2 %collective-permute-start.26 = (bf16[112,2048]{1,0:T(8,128)(2,1)S(1)}, bf16[112,2048]{1,0:T(8,128)(2,1)S(1)}, u32[]{:S(2)}, u32[]{:S(2)}) collective-permute-start(bf16[112,2048]{1,0:T(8,128)(2,1)S(1)} %add_convert_fusion.2), channel_id=1, source_target_pairs={{0,4},{1,3},{2,6},{3,1},{4,0},{5,7},{6,2},{7,5},{8,12},{9,11},{10,... | collective-permute-start | bytes 1376264 | tf_op jit(solution)/shard_map/ppermute | solution.py:637
  95.4 6.3 %collective-permute-done.28 = bf16[112,2048]{1,0:T(8,128)(2,1)S(1)} collective-permute-done((bf16[112,2048]{1,0:T(8,128)(2,1)S(1)}, bf16[112,2048]{1,0:T(8,128)(2,1)S(1)}, u32[]{:S(2)}, u32[]{:S(2)}) %collective-permute-start.28) | collective-permute-done | bytes 458784 | tf_op jit(solution)/shard_map/ppermute | solution.py:637
  101.6 0.2 add_convert_fusion.5
  101.9 0.8 collective-permute-start.31
  102.7 1.3 %collective-permute-start.29 = (bf16[112,1024]{1,0:T(8,128)(2,1)S(1)}, bf16[112,1024]{1,0:T(8,128)(2,1)S(1)}, u32[]{:S(2)}, u32[]{:S(2)}) collective-permute-start(bf16[112,1024]{1,0:T(8,128)(2,1)S(1)} %get-tuple-element.104), channel_id=1, source_target_pairs={{0,2},{1,5},{2,0},{3,7},{4,6},{5,1},{6,4},{7,3},{8,10},{9,13},{10,... | collective-permute-start | bytes 688136 | tf_op jit(solution)/shard_map/ppermute | solution.py:637
  104.0 4.2 %collective-permute-done.31 = bf16[112,1024]{1,0:T(8,128)(2,1)S(1)} collective-permute-done((bf16[112,1024]{1,0:T(8,128)(2,1)S(1)}, bf16[112,1024]{1,0:T(8,128)(2,1)S(1)}, u32[]{:S(2)}, u32[]{:S(2)}) %collective-permute-start.31) | collective-permute-done | bytes 229408 | tf_op jit(solution)/shard_map/ppermute | solution.py:637
  108.2 2.5 %collective-permute-done.29 = bf16[112,1024]{1,0:T(8,128)(2,1)S(1)} collective-permute-done((bf16[112,1024]{1,0:T(8,128)(2,1)S(1)}, bf16[112,1024]{1,0:T(8,128)(2,1)S(1)}, u32[]{:S(2)}, u32[]{:S(2)}) %collective-permute-start.29) | collective-permute-done | bytes 229408 | tf_op jit(solution)/shard_map/ppermute | solution.py:637
  110.6 0.4 add_convert_fusion
  111.1 0.9 convert_element_type.89
  (63 shorter events, 0.4 us)
Async XLA Ops:
  0.6 38.9 %collective-permute-start.4 = (bf16[4096,256]{1,0:T(8,128)(2,1)}, bf16[4096,256]{1,0:T(8,128)(2,1)}, u32[]{:S(2)}, u32[]{:S(2)}) collective-permute-start(bf16[4096,256]{1,0:T(8,128)(2,1)} %refs_0_.1), channel_id=1, source_target_pairs={{0,1},{1,0},{2,3},{3,2},{4,5},{5,4},{6,7},{7,6},{8,9},{9,8},{10,11... | collective-permute-start | bytes 6291464 | tf_op jit(solution)/shard_map/ppermute | solution.py:627
  1.1 1.2 %copy-start.3 = (bf16[18,24,1024]{2,1,0:T(8,128)(2,1)S(1)}, bf16[18,24,1024]{2,1,0:T(8,128)(2,1)}, u32[]{:S(2)}) copy-start(bf16[18,24,1024]{2,1,0:T(8,128)(2,1)} %tokens_ref.7) | copy-start | bytes 2654212
  2.3 7.8 %copy-start.4 = (bf16[18,24,1024]{2,1,0:T(8,128)(2,1)S(1)}, bf16[18,24,1024]{2,1,0:T(8,128)(2,1)}, u32[]{:S(2)}) copy-start(bf16[18,24,1024]{2,1,0:T(8,128)(2,1)} %tokens_ref.7) | copy-start | bytes 2654212
  2.4 13.2 %collective-permute-start.1 = (bf16[18,8,1024]{2,1,0:T(8,128)(2,1)S(1)}, bf16[18,8,1024]{2,1,0:T(8,128)(2,1)S(1)}, u32[]{:S(2)}, u32[]{:S(2)}) collective-permute-start(bf16[18,8,1024]{2,1,0:T(8,128)(2,1)S(1)} %get-tuple-element.56), channel_id=1, source_target_pairs={{0,7},{1,0},{2,1},{3,2},{4,3},{5,4},{6,5},{7,6},{8,15},{9,8},{10,9... | collective-permute-start | bytes 884744 | tf_op jit(solution)/shard_map/ppermute | solution.py:467
  6.0 10.0 %collective-permute-start = (bf16[18,8,1024]{2,1,0:T(8,128)(2,1)S(1)}, bf16[18,8,1024]{2,1,0:T(8,128)(2,1)S(1)}, u32[]{:S(2)}, u32[]{:S(2)}) collective-permute-start(bf16[18,8,1024]{2,1,0:T(8,128)(2,1)S(1)} %get-tuple-element.55), channel_id=1, source_target_pairs={{0,1},{1,2},{2,3},{3,4},{4,5},{5,6},{6,7},{7,0},{8,9},{9,10},{10,1... | collective-permute-start | bytes 884744 | tf_op jit(solution)/shard_map/ppermute | solution.py:467
  8.9 27.1 %collective-permute-start.5 = (bf16[2048,256]{1,0:T(8,128)(2,1)}, bf16[2048,256]{1,0:T(8,128)(2,1)}, u32[]{:S(2)}, u32[]{:S(2)}) collective-permute-start(bf16[2048,256]{1,0:T(8,128)(2,1)} %get-tuple-element.67), channel_id=1, source_target_pairs={{0,2},{1,3},{2,0},{3,1},{4,6},{5,7},{6,4},{7,5},{8,10},{9,11},{10,... | collective-permute-start | bytes 3145736 | tf_op jit(solution)/shard_map/ppermute | solution.py:632
  9.0 27.6 %collective-permute-start.6 = (bf16[2048,256]{1,0:T(8,128)(2,1)}, bf16[2048,256]{1,0:T(8,128)(2,1)}, u32[]{:S(2)}, u32[]{:S(2)}) collective-permute-start(bf16[2048,256]{1,0:T(8,128)(2,1)} %get-tuple-element.68), channel_id=1, source_target_pairs={{0,4},{1,5},{2,6},{3,7},{4,0},{5,1},{6,2},{7,3},{8,12},{9,13},{10,... | collective-permute-start | bytes 3145736 | tf_op jit(solution)/shard_map/ppermute | solution.py:632
  10.1 10.9 %copy-start.5 = (bf16[1024,1024]{1,0:T(8,128)(2,1)S(1)}, bf16[1024,1024]{1,0:T(8,128)(2,1)}, u32[]{:S(2)}) copy-start(bf16[1024,1024]{1,0:T(8,128)(2,1)} %out_w_ref.3) | copy-start | bytes 6291460
  10.1 10.9 %copy-start.6 = (bf16[576,144]{1,0:T(8,128)(2,1)S(1)}, bf16[576,144]{1,0:T(8,128)(2,1)}, u32[]{:S(2)}) copy-start(bf16[576,144]{1,0:T(8,128)(2,1)} %constant.74.clone.rest_1_) | copy-start | bytes 497668
  10.1 10.9 %copy-start.7 = (bf16[576,256]{1,0:T(8,128)(2,1)S(1)}, bf16[576,256]{1,0:T(8,128)(2,1)}, u32[]{:S(2)}) copy-start(bf16[576,256]{1,0:T(8,128)(2,1)} %constant.75.clone.rest_2_) | copy-start | bytes 884740
  10.2 10.9 %copy-start.8 = (bf16[256,288]{1,0:T(8,128)(2,1)S(1)}, bf16[256,288]{1,0:T(8,128)(2,1)}, u32[]{:S(2)}) copy-start(bf16[256,288]{1,0:T(8,128)(2,1)} %constant.72.clone.patch_ref) | copy-start | bytes 442372
  10.2 10.9 %copy-start.9 = (bf16[144,576]{1,0:T(8,128)(2,1)S(1)}, bf16[144,576]{1,0:T(8,128)(2,1)}, u32[]{:S(2)}) copy-start(bf16[144,576]{1,0:T(8,128)(2,1)} %constant.76.clone.rest_3_) | copy-start | bytes 497668
  10.2 10.9 %copy-start.13 = (bf16[240,240]{1,0:T(8,128)(2,1)S(1)}, bf16[240,240]{1,0:T(8,128)(2,1)}, u32[]{:S(2)}) copy-start(bf16[240,240]{1,0:T(8,128)(2,1)} %constant.73.clone.rest_0_) | copy-start | bytes 345604
  16.0 11.7 %collective-permute-start.2 = (bf16[3,40,1024]{2,1,0:T(8,128)(2,1)S(1)}, bf16[3,40,1024]{2,1,0:T(8,128)(2,1)S(1)}, u32[]{:S(2)}, u32[]{:S(2)}) collective-permute-start(bf16[3,40,1024]{2,1,0:T(8,128)(2,1)S(1)} %pad_maximum_fusion.1), channel_id=1, source_target_pairs={{0,8},{8,16},{16,24},{1,9},{9,17},{17,25},{2,10},{10,18},{18,26},{... | collective-permute-start | bytes 737288 | tf_op jit(solution)/shard_map/ppermute | solution.py:467
  19.5 10.4 %collective-permute-start.3 = (bf16[3,40,1024]{2,1,0:T(8,128)(2,1)S(1)}, bf16[3,40,1024]{2,1,0:T(8,128)(2,1)S(1)}, u32[]{:S(2)}, u32[]{:S(2)}) collective-permute-start(bf16[3,40,1024]{2,1,0:T(8,128)(2,1)S(1)} %pad_maximum_fusion.2), channel_id=1, source_target_pairs={{8,0},{16,8},{24,16},{9,1},{17,9},{25,17},{10,2},{18,10},{26,18},{... | collective-permute-start | bytes 737288 | tf_op jit(solution)/shard_map/ppermute | solution.py:467
  21.1 8.9 %copy-start.10 = (bf16[304,256]{1,0:T(8,128)(2,1)S(1)}, bf16[304,256]{1,0:T(8,128)(2,1)}, u32[]{:S(2)}) copy-start(bf16[304,256]{1,0:T(8,128)(2,1)} %constant.80.clone.rest_2_.rest_6_) | copy-start | bytes 466948
  21.1 8.9 %copy-start.11 = (bf16[240,256]{1,0:T(8,128)(2,1)S(1)}, bf16[240,256]{1,0:T(8,128)(2,1)}, u32[]{:S(2)}) copy-start(bf16[240,256]{1,0:T(8,128)(2,1)} %constant.78.clone.rest_0_) | copy-start | bytes 368644
  21.1 8.9 %copy-start.12 = (bf16[240,256]{1,0:T(8,128)(2,1)S(1)}, bf16[240,256]{1,0:T(8,128)(2,1)}, u32[]{:S(2)}) copy-start(bf16[240,256]{1,0:T(8,128)(2,1)} %constant.82.clone.rest_4_) | copy-start | bytes 368644
  21.1 8.9 %copy-start.14 = (bf16[192,192]{1,0:T(8,128)(2,1)S(1)}, bf16[192,192]{1,0:T(8,128)(2,1)}, u32[]{:S(2)}) copy-start(bf16[192,192]{1,0:T(8,128)(2,1)} %constant.77.clone.patch_ref) | copy-start | bytes 221188
  21.1 8.9 %copy-start.15 = (bf16[304,80]{1,0:T(8,128)(2,1)S(1)}, bf16[304,80]{1,0:T(8,128)(2,1)}, u32[]{:S(2)}) copy-start(bf16[304,80]{1,0:T(8,128)(2,1)} %constant.79.clone.rest_1_.rest_5_) | copy-start | bytes 145924
  21.1 8.9 %copy-start.16 = (bf16[80,304]{1,0:T(8,128)(2,1)S(1)}, bf16[80,304]{1,0:T(8,128)(2,1)}, u32[]{:S(2)}) copy-start(bf16[80,304]{1,0:T(8,128)(2,1)} %constant.81.clone.rest_3_.rest_7_) | copy-start | bytes 145924
  30.0 11.1 %copy-start.2 = (bf16[4096,256]{1,0:T(8,128)(2,1)S(1)}, bf16[4096,256]{1,0:T(8,128)(2,1)}, u32[]{:S(2)}) copy-start(bf16[4096,256]{1,0:T(8,128)(2,1)} %refs_0_.1) | copy-start | bytes 6291460
  36.6 2.9 %collective-permute-start.7 = (bf16[2048,256]{1,0:T(8,128)(2,1)}, bf16[2048,256]{1,0:T(8,128)(2,1)S(1)}, u32[]{:S(2)}, u32[]{:S(2)}) collective-permute-start(bf16[2048,256]{1,0:T(8,128)(2,1)} %collective-permute-done.5.refs_2_), channel_id=1, source_target_pairs={{0,1},{1,0},{2,3},{3,2},{4,5},{5,4},{6,7},{7,6},{8,9},{9,8},{10,11... | collective-permute-start | bytes 3145736 | tf_op jit(solution)/shard_map/ppermute | solution.py:627
  36.8 4.3 %collective-permute-start.8 = (bf16[2048,256]{1,0:T(8,128)(2,1)}, bf16[2048,256]{1,0:T(8,128)(2,1)}, u32[]{:S(2)}, u32[]{:S(2)}) collective-permute-start(bf16[2048,256]{1,0:T(8,128)(2,1)} %collective-permute-done.6.refs_4_), channel_id=1, source_target_pairs={{0,1},{1,0},{2,3},{3,2},{4,5},{5,4},{6,7},{7,6},{8,9},{9,8},{10,11... | collective-permute-start | bytes 3145736 | tf_op jit(solution)/shard_map/ppermute | solution.py:627
  37.1 12.9 %collective-permute-start.9 = (bf16[112,2048]{1,0:T(8,128)(2,1)}, bf16[112,2048]{1,0:T(8,128)(2,1)}, u32[]{:S(2)}, u32[]{:S(2)}) collective-permute-start(bf16[112,2048]{1,0:T(8,128)(2,1)} %get-tuple-element.64.upper_ref), channel_id=1, source_target_pairs={{0,4},{1,5},{2,6},{3,7},{4,0},{5,1},{6,2},{7,3},{8,12},{9,13},{10,... | collective-permute-start | bytes 1376264 | tf_op jit(solution)/shard_map/ppermute | solution.py:632
  37.3 13.0 %collective-permute-start.10 = (bf16[112,2048]{1,0:T(8,128)(2,1)}, bf16[112,2048]{1,0:T(8,128)(2,1)}, u32[]{:S(2)}, u32[]{:S(2)}) collective-permute-start(bf16[112,2048]{1,0:T(8,128)(2,1)} %get-tuple-element.65.lower_ref), channel_id=1, source_target_pairs={{0,2},{1,3},{2,0},{3,1},{4,6},{5,7},{6,4},{7,5},{8,10},{9,11},{10,... | collective-permute-start | bytes 1376264 | tf_op jit(solution)/shard_map/ppermute | solution.py:632
  50.3 13.2 %copy-start = (bf16[2048,1024]{1,0:T(8,128)(2,1)S(1)}, bf16[2048,1024]{1,0:T(8,128)(2,1)}, u32[]{:S(2)}) copy-start(bf16[2048,1024]{1,0:T(8,128)(2,1)} %up_ref.7) | copy-start | bytes 12582916
  50.3 13.2 %copy-start.1 = (bf16[1024,2048]{1,0:T(8,128)(2,1)S(1)}, bf16[1024,2048]{1,0:T(8,128)(2,1)}, u32[]{:S(2)}) copy-start(bf16[1024,2048]{1,0:T(8,128)(2,1)} %down_ref.7) | copy-start | bytes 12582916
  53.1 6.9 %collective-permute-start.11 = (bf16[112,1024]{1,0:T(8,128)(2,1)S(1)}, bf16[112,1024]{1,0:T(8,128)(2,1)S(1)}, u32[]{:S(2)}, u32[]{:S(2)}) collective-permute-start(bf16[112,1024]{1,0:T(8,128)(2,1)S(1)} %get-tuple-element.80), channel_id=1, source_target_pairs={{0,4},{1,5},{2,6},{3,7},{4,0},{5,1},{6,2},{7,3},{8,12},{9,13},{10,... | collective-permute-start | bytes 688136 | tf_op jit(solution)/shard_map/ppermute | solution.py:632
  54.7 6.2 %collective-permute-start.12 = (bf16[112,1024]{1,0:T(8,128)(2,1)S(1)}, bf16[112,1024]{1,0:T(8,128)(2,1)S(1)}, u32[]{:S(2)}, u32[]{:S(2)}) collective-permute-start(bf16[112,1024]{1,0:T(8,128)(2,1)S(1)} %get-tuple-element.81), channel_id=1, source_target_pairs={{0,2},{1,3},{2,0},{3,1},{4,6},{5,7},{6,4},{7,5},{8,10},{9,11},{10,... | collective-permute-start | bytes 688136 | tf_op jit(solution)/shard_map/ppermute | solution.py:632
  61.6 1.9 %collective-permute-start.14 = (bf16[112,2048]{1,0:T(8,128)(2,1)S(1)}, bf16[112,2048]{1,0:T(8,128)(2,1)S(1)}, u32[]{:S(2)}, u32[]{:S(2)}) collective-permute-start(bf16[112,2048]{1,0:T(8,128)(2,1)S(1)} %combine.1.mine_ref), channel_id=1, source_target_pairs={{0,1},{1,0},{2,3},{3,2},{4,5},{5,4},{6,7},{7,6},{8,9},{9,8},{10,11... | collective-permute-start | bytes 1376264 | tf_op jit(solution)/shard_map/ppermute | solution.py:627
  61.7 8.5 %collective-permute-start.13 = (bf16[112,2048]{1,0:T(8,128)(2,1)S(1)}, bf16[112,2048]{1,0:T(8,128)(2,1)S(1)}, u32[]{:S(2)}, u32[]{:S(2)}) collective-permute-start(bf16[112,2048]{1,0:T(8,128)(2,1)S(1)} %combine.1.mine_ref), channel_id=1, source_target_pairs={{0,2},{1,5},{2,0},{3,7},{4,6},{5,1},{6,4},{7,3},{8,10},{9,13},{10,... | collective-permute-start | bytes 1376264 | tf_op jit(solution)/shard_map/ppermute | solution.py:637
  70.2 1.8 %collective-permute-start.17 = (bf16[112,2048]{1,0:T(8,128)(2,1)S(1)}, bf16[112,2048]{1,0:T(8,128)(2,1)S(1)}, u32[]{:S(2)}, u32[]{:S(2)}) collective-permute-start(bf16[112,2048]{1,0:T(8,128)(2,1)S(1)} %collective-permute-done.13.mine_ref), channel_id=1, source_target_pairs={{0,1},{1,0},{2,3},{3,2},{4,5},{5,4},{6,7},{7,6},{8,9},{9,8},{10,11... | collective-permute-start | bytes 1376264 | tf_op jit(solution)/shard_map/ppermute | solution.py:627
  70.2 8.5 %collective-permute-start.19 = (bf16[112,2048]{1,0:T(8,128)(2,1)S(1)}, bf16[112,2048]{1,0:T(8,128)(2,1)S(1)}, u32[]{:S(2)}, u32[]{:S(2)}) collective-permute-start(bf16[112,2048]{1,0:T(8,128)(2,1)S(1)} %collective-permute-done.13.mine_ref), channel_id=1, source_target_pairs={{0,4},{1,3},{2,6},{3,1},{4,0},{5,7},{6,2},{7,5},{8,12},{9,11},{10,... | collective-permute-start | bytes 1376264 | tf_op jit(solution)/shard_map/ppermute | solution.py:637
  74.6 4.1 %collective-permute-start.18 = (bf16[112,1024]{1,0:T(8,128)(2,1)S(1)}, bf16[112,1024]{1,0:T(8,128)(2,1)S(1)}, u32[]{:S(2)}, u32[]{:S(2)}) collective-permute-start(bf16[112,1024]{1,0:T(8,128)(2,1)S(1)} %get-tuple-element.89), channel_id=1, source_target_pairs={{0,1},{1,0},{2,3},{3,2},{4,5},{5,4},{6,7},{7,6},{8,9},{9,8},{10,11... | collective-permute-start | bytes 688136 | tf_op jit(solution)/shard_map/ppermute | solution.py:627
  78.7 1.8 %collective-permute-start.20 = (bf16[112,2048]{1,0:T(8,128)(2,1)S(1)}, bf16[112,2048]{1,0:T(8,128)(2,1)S(1)}, u32[]{:S(2)}, u32[]{:S(2)}) collective-permute-start(bf16[112,2048]{1,0:T(8,128)(2,1)S(1)} %collective-permute-done.19.mine_ref), channel_id=1, source_target_pairs={{0,1},{1,0},{2,3},{3,2},{4,5},{5,4},{6,7},{7,6},{8,9},{9,8},{10,11... | collective-permute-start | bytes 1376264 | tf_op jit(solution)/shard_map/ppermute | solution.py:627
  78.7 8.5 %collective-permute-start.22 = (bf16[112,2048]{1,0:T(8,128)(2,1)S(1)}, bf16[112,2048]{1,0:T(8,128)(2,1)S(1)}, u32[]{:S(2)}, u32[]{:S(2)}) collective-permute-start(bf16[112,2048]{1,0:T(8,128)(2,1)S(1)} %combine.1.mine_ref), channel_id=1, source_target_pairs={{0,4},{1,3},{2,6},{3,1},{4,0},{5,7},{6,2},{7,5},{8,12},{9,11},{10,... | collective-permute-start | bytes 1376264 | tf_op jit(solution)/shard_map/ppermute | solution.py:637
  83.1 4.1 %collective-permute-start.21 = (bf16[112,1024]{1,0:T(8,128)(2,1)S(1)}, bf16[112,1024]{1,0:T(8,128)(2,1)S(1)}, u32[]{:S(2)}, u32[]{:S(2)}) collective-permute-start(bf16[112,1024]{1,0:T(8,128)(2,1)S(1)} %get-tuple-element.91), channel_id=1, source_target_pairs={{0,1},{1,0},{2,3},{3,2},{4,5},{5,4},{6,7},{7,6},{8,9},{9,8},{10,11... | collective-permute-start | bytes 688136 | tf_op jit(solution)/shard_map/ppermute | solution.py:627
  87.2 1.8 %collective-permute-start.23 = (bf16[112,2048]{1,0:T(8,128)(2,1)S(1)}, bf16[112,2048]{1,0:T(8,128)(2,1)S(1)}, u32[]{:S(2)}, u32[]{:S(2)}) collective-permute-start(bf16[112,2048]{1,0:T(8,128)(2,1)S(1)} %collective-permute-done.22.mine_ref), channel_id=1, source_target_pairs={{0,1},{1,0},{2,3},{3,2},{4,5},{5,4},{6,7},{7,6},{8,9},{9,8},{10,11... | collective-permute-start | bytes 1376264 | tf_op jit(solution)/shard_map/ppermute | solution.py:627
  87.2 4.6 %collective-permute-start.27 = (bf16[112,1024]{1,0:T(8,128)(2,1)S(1)}, bf16[112,1024]{1,0:T(8,128)(2,1)S(1)}, u32[]{:S(2)}, u32[]{:S(2)}) collective-permute-start(bf16[112,1024]{1,0:T(8,128)(2,1)S(1)} %get-tuple-element.102), channel_id=1, source_target_pairs={{0,1},{1,0},{2,3},{3,2},{4,5},{5,4},{6,7},{7,6},{8,9},{9,8},{10,11... | collective-permute-start | bytes 688136 | tf_op jit(solution)/shard_map/ppermute | solution.py:627
  87.7 16.3 %collective-permute-start.16 = (bf16[112,1024]{1,0:T(8,128)(2,1)S(1)}, bf16[112,1024]{1,0:T(8,128)(2,1)S(1)}, u32[]{:S(2)}, u32[]{:S(2)}) collective-permute-start(bf16[112,1024]{1,0:T(8,128)(2,1)S(1)} %get-tuple-element.87), channel_id=1, source_target_pairs={{0,1},{1,0},{2,3},{3,2},{4,5},{5,4},{6,7},{7,6},{8,9},{9,8},{10,11... | collective-permute-start | bytes 688136 | tf_op jit(solution)/shard_map/ppermute | solution.py:627
  87.7 16.3 %collective-permute-start.15 = (bf16[112,1024]{1,0:T(8,128)(2,1)S(1)}, bf16[112,1024]{1,0:T(8,128)(2,1)S(1)}, u32[]{:S(2)}, u32[]{:S(2)}) collective-permute-start(bf16[112,1024]{1,0:T(8,128)(2,1)S(1)} %get-tuple-element.86), channel_id=1, source_target_pairs={{0,1},{1,0},{2,3},{3,2},{4,5},{5,4},{6,7},{7,6},{8,9},{9,8},{10,11... | collective-permute-start | bytes 688136 | tf_op jit(solution)/shard_map/ppermute | solution.py:627
  88.2 7.2 %collective-permute-start.30 = (bf16[112,1024]{1,0:T(8,128)(2,1)S(1)}, bf16[112,1024]{1,0:T(8,128)(2,1)S(1)}, u32[]{:S(2)}, u32[]{:S(2)}) collective-permute-start(bf16[112,1024]{1,0:T(8,128)(2,1)S(1)} %get-tuple-element.103), channel_id=1, source_target_pairs={{0,1},{1,0},{2,3},{3,2},{4,5},{5,4},{6,7},{7,6},{8,9},{9,8},{10,11... | collective-permute-start | bytes 688136 | tf_op jit(solution)/shard_map/ppermute | solution.py:627
  91.6 1.6 %collective-permute-start.25 = (bf16[112,1024]{1,0:T(8,128)(2,1)S(1)}, bf16[112,1024]{1,0:T(8,128)(2,1)S(1)}, u32[]{:S(2)}, u32[]{:S(2)}) collective-permute-start(bf16[112,1024]{1,0:T(8,128)(2,1)S(1)} %get-tuple-element.97), channel_id=1, source_target_pairs={{0,1},{1,0},{2,3},{3,2},{4,5},{5,4},{6,7},{7,6},{8,9},{9,8},{10,11... | collective-permute-start | bytes 688136 | tf_op jit(solution)/shard_map/ppermute | solution.py:627
  91.8 2.2 %collective-permute-start.24 = (bf16[112,1024]{1,0:T(8,128)(2,1)S(1)}, bf16[112,1024]{1,0:T(8,128)(2,1)S(1)}, u32[]{:S(2)}, u32[]{:S(2)}) collective-permute-start(bf16[112,1024]{1,0:T(8,128)(2,1)S(1)} %get-tuple-element.96), channel_id=1, source_target_pairs={{0,1},{1,0},{2,3},{3,2},{4,5},{5,4},{6,7},{7,6},{8,9},{9,8},{10,11... | collective-permute-start | bytes 688136 | tf_op jit(solution)/shard_map/ppermute | solution.py:627
  93.1 8.5 %collective-permute-start.28 = (bf16[112,2048]{1,0:T(8,128)(2,1)S(1)}, bf16[112,2048]{1,0:T(8,128)(2,1)S(1)}, u32[]{:S(2)}, u32[]{:S(2)}) collective-permute-start(bf16[112,2048]{1,0:T(8,128)(2,1)S(1)} %add_convert_fusion.1), channel_id=1, source_target_pairs={{0,4},{1,3},{2,6},{3,1},{4,0},{5,7},{6,2},{7,5},{8,12},{9,11},{10,... | collective-permute-start | bytes 1376264 | tf_op jit(solution)/shard_map/ppermute | solution.py:637
  94.1 16.5 %collective-permute-start.26 = (bf16[112,2048]{1,0:T(8,128)(2,1)S(1)}, bf16[112,2048]{1,0:T(8,128)(2,1)S(1)}, u32[]{:S(2)}, u32[]{:S(2)}) collective-permute-start(bf16[112,2048]{1,0:T(8,128)(2,1)S(1)} %add_convert_fusion.2), channel_id=1, source_target_pairs={{0,4},{1,3},{2,6},{3,1},{4,0},{5,7},{6,2},{7,5},{8,12},{9,11},{10,... | collective-permute-start | bytes 1376264 | tf_op jit(solution)/shard_map/ppermute | solution.py:637
  101.9 6.3 %collective-permute-start.31 = (bf16[112,1024]{1,0:T(8,128)(2,1)S(1)}, bf16[112,1024]{1,0:T(8,128)(2,1)S(1)}, u32[]{:S(2)}, u32[]{:S(2)}) collective-permute-start(bf16[112,1024]{1,0:T(8,128)(2,1)S(1)} %get-tuple-element.105), channel_id=1, source_target_pairs={{0,2},{1,5},{2,0},{3,7},{4,6},{5,1},{6,4},{7,3},{8,10},{9,13},{10,... | collective-permute-start | bytes 688136 | tf_op jit(solution)/shard_map/ppermute | solution.py:637
  102.7 7.9 %collective-permute-start.29 = (bf16[112,1024]{1,0:T(8,128)(2,1)S(1)}, bf16[112,1024]{1,0:T(8,128)(2,1)S(1)}, u32[]{:S(2)}, u32[]{:S(2)}) collective-permute-start(bf16[112,1024]{1,0:T(8,128)(2,1)S(1)} %get-tuple-element.104), channel_id=1, source_target_pairs={{0,2},{1,5},{2,0},{3,7},{4,6},{5,1},{6,4},{7,3},{8,10},{9,13},{10,... | collective-permute-start | bytes 688136 | tf_op jit(solution)/shard_map/ppermute | solution.py:637

commit v12 on v11

--- a/solution.py
+++ b/solution.py
@@ -649,8 +649,12 @@
     near_low, far = lax.optimization_barrier((core_swap(near_low), far))
     mine, low, high = feed_forward(far, core_swap(far), up, down)
     low, other = lax.optimization_barrier((core_swap(low), other))
-    relayed = cross(added(mine, low, core_swap(high)), 2, 1)
-    other_back = cross(summed(*feed_forward(other, core_swap(other), up, down)), 2, 1)
+    far_sum = added(mine, low, core_swap(high))
+    pair, far_sum = lax.optimization_barrier((core_swap(other), far_sum))
+    relayed = cross(far_sum, 2, 1)
+    mine, low, high = feed_forward(other, pair, up, down)
+    relayed, low = lax.optimization_barrier((relayed, core_swap(low)))
+    other_back = cross(added(mine, low, core_swap(high)), 2, 1)
     half = low.shape[1]
     near_back = []
     for part, at in ((near_low, 0), (core_swap(near_high), half)):

time: 112 us -> 112 us (level)
  transfers between devices with their start and end apart: 32 -> 32, of which waited for: 19 -> 20; matrix products, arithmetic and copies ran while one was open for 1% -> 1% of each run, Pallas kernels for 32% -> 32%
where the time goes in v12:
time: 112 us
  waiting for transfers between devices  44.3 us (40%)
  Pallas kernels  39.2 us (35%)
  starting transfers between devices  23.7 us (21%)
  local copies, waits for them, and re-layouts  2.24 us (2%)
    ppermute x7, waiting for transfers between devices, cross(): lax.ppermute(value, 'lon', [(i, i ^ 2 * (second if i % 2 else first)) for...  24.1 us
    pallas_call x2, Pallas kernels, vmem_call(): pl.pallas_call(kernel, in_specs=[vmem] * len(args), out_specs=[vmem] * le...  12.5 us
    ppermute x6, waiting for transfers between devices, chip_swap(): lax.ppermute(value, 'lon', [(i, i ^ 2 * offset) for i in range(size)])  10.7 us
    pallas_call x4, Pallas kernels, feed_forward(): pl.pallas_call(ffn_kernel, in_specs=[vmem] * 4, out_specs=[vmem] * 3, out...  10.4 us
    ppermute x4, starting transfers between devices, shift(): return lax.ppermute(part, axis, pairs)  8.58 us
    pallas_call x3, Pallas kernels, local_call(): pl.pallas_call(kernel, in_specs=[pl.BlockSpec(memory_space=pltpu.SMEM)] +...  8.12 us
    ppermute x15, waiting for transfers between devices, core_swap(): return lax.ppermute(value, 'lon', [(i, i ^ 1) for i in range(size)])  6.72 us
    ppermute x7, starting transfers between devices, cross(): lax.ppermute(value, 'lon', [(i, i ^ 2 * (second if i % 2 else first)) for...  6.35 us
  transfers between devices with their start and end apart: 32, of which 20 were waited for; matrix products, arithmetic and copies ran while one was open for 1% of the time, Pallas kernels for 32%

profile of v12, /device:TPU:0, one launch (start us, length us, event | category | flops | bytes accessed | tf_op | source)
XLA Modules:
  0.0 111.5 jit_solution(4185556304595451094)
XLA Ops:
  0.6 0.5 collective-permute-start.4
  1.1 1.2 %copy-done.3 = bf16[18,24,1024]{2,1,0:T(8,128)(2,1)S(1)} copy-done((bf16[18,24,1024]{2,1,0:T(8,128)(2,1)S(1)}, bf16[18,24,1024]{2,1,0:T(8,128)(2,1)}, u32[]{:S(2)}) %copy-start.3) | copy-done | bytes 884760
  2.4 3.6 %collective-permute-start.1 = (bf16[18,8,1024]{2,1,0:T(8,128)(2,1)S(1)}, bf16[18,8,1024]{2,1,0:T(8,128)(2,1)S(1)}, u32[]{:S(2)}, u32[]{:S(2)}) collective-permute-start(bf16[18,8,1024]{2,1,0:T(8,128)(2,1)S(1)} %get-tuple-element.60), channel_id=1, source_target_pairs={{0,7},{1,0},{2,1},{3,2},{4,3},{5,4},{6,5},{7,6},{8,15},{9,8},{10,9... | collective-permute-start | bytes 884744 | tf_op jit(solution)/shard_map/ppermute | solution.py:467
  6.0 2.9 %halves.1 = (bf16[2048,256]{1,0:T(8,128)(2,1)}, bf16[2048,256]{1,0:T(8,128)(2,1)}) custom-call(bf16[4096,256]{1,0:T(8,128)(2,1)} %refs_0_.1), custom_call_target="tpu_custom_call" | custom-call | tf_op jit(solution)/shard_map/halves/pallas_call | solution.py:202
  9.0 1.1 collective-permute-start.6
  10.2 5.2 %own_projection.1 = (bf16[448,3072]{1,0:T(8,128)(2,1)S(1)}, bf16[1024,2048]{1,0:T(8,128)(2,1)S(1)}) custom-call(bf16[18,24,1024]{2,1,0:T(8,128)(2,1)S(1)} %copy-done.4, bf16[1024,3072]{1,0:T(8,128)(2,1)} %weight_ref.1), custom_call_target="tpu_custom_call" | custom-call | flops 2818572288 | bytes 6291456 | tf_op jit(solution)/shard_map/own_projection/pallas_call | solution.py:242
  15.5 0.1 or_select_fusion.bias_ref
  15.6 0.4 collective-permute-done.west_ref
  16.0 3.5 %collective-permute-start.2 = (bf16[3,40,1024]{2,1,0:T(8,128)(2,1)S(1)}, bf16[3,40,1024]{2,1,0:T(8,128)(2,1)S(1)}, u32[]{:S(2)}, u32[]{:S(2)}) collective-permute-start(bf16[3,40,1024]{2,1,0:T(8,128)(2,1)S(1)} %pad_maximum_fusion.1), channel_id=1, source_target_pairs={{0,8},{8,16},{16,24},{1,9},{9,17},{17,25},{2,10},{10,18},{18,26},{... | collective-permute-start | bytes 737288 | tf_op jit(solution)/shard_map/ppermute | solution.py:467
  19.5 1.5 %collective-permute-start.3 = (bf16[3,40,1024]{2,1,0:T(8,128)(2,1)S(1)}, bf16[3,40,1024]{2,1,0:T(8,128)(2,1)S(1)}, u32[]{:S(2)}, u32[]{:S(2)}) collective-permute-start(bf16[3,40,1024]{2,1,0:T(8,128)(2,1)S(1)} %pad_maximum_fusion.2), channel_id=1, source_target_pairs={{8,0},{16,8},{24,16},{9,1},{17,9},{25,17},{10,2},{18,10},{26,18},{... | collective-permute-start | bytes 737288 | tf_op jit(solution)/shard_map/ppermute | solution.py:467
  21.2 6.5 %middle_attention.1 = (bf16[288,2048]{1,0:T(8,128)(2,1)S(1)}, bf16[12,24,1024]{2,1,0:T(8,128)(2,1)S(1)}, bf16[64,2048]{1,0:T(8,128)(2,1)S(1)}, bf16[64,2048]{1,0:T(8,128)(2,1)S(1)}) custom-call(bf16[18,24,1024]{2,1,0:T(8,128)(2,1)S(1)} %copy-done.4, bf16[18,8,1024]{2,1,0:T(8,128)(2,1)S(1)} %collective-permute-done.west_ref, ...), custom_call_target="tpu_custom_call" | custom-call | flops 5000000000 | bytes 1048576 | tf_op jit(solution)/shard_map/middle_attention/pallas_call | solution.py:398
  27.7 2.3 %collective-permute-done.3.south_ref = bf16[3,40,1024]{2,1,0:T(8,128)(2,1)S(1)} collective-permute-done((bf16[3,40,1024]{2,1,0:T(8,128)(2,1)S(1)}, bf16[3,40,1024]{2,1,0:T(8,128)(2,1)S(1)}, u32[]{:S(2)}, u32[]{:S(2)}) %collective-permute-start.3) | collective-permute-done | bytes 245792 | tf_op jit(solution)/shard_map/ppermute | solution.py:467
  30.0 6.0 %edge_attention.1 = (bf16[18,24,1024]{2,1,0:T(8,128)(2,1)}, bf16[112,2048]{1,0:T(8,128)(2,1)}, bf16[112,2048]{1,0:T(8,128)(2,1)}) custom-call(bf16[18,24,1024]{2,1,0:T(8,128)(2,1)S(1)} %copy-done.4, bf16[3,40,1024]{2,1,0:T(8,128)(2,1)S(1)} %collective-permute-done.2.north_ref, bf16[3,40,1024]{2,1,0:T(8,128)(2,1)S(1)} %collective-permute-done.3.south_ref, ...), custom_call_target="tpu_custom_call" | custom-call | flops 6000000000 | bytes 1048576 | tf_op jit(solution)/shard_map/edge_attention/pallas_call | solution.py:398
  36.0 0.6 collective-permute-done.6.refs_4_
  36.6 0.2 collective-permute-start.7
  36.8 0.3 collective-permute-start.8
  37.1 0.2 collective-permute-start.9
  37.3 2.1 %collective-permute-start.10 = (bf16[112,2048]{1,0:T(8,128)(2,1)}, bf16[112,2048]{1,0:T(8,128)(2,1)}, u32[]{:S(2)}, u32[]{:S(2)}) collective-permute-start(bf16[112,2048]{1,0:T(8,128)(2,1)} %get-tuple-element.69.lower_ref), channel_id=1, source_target_pairs={{0,2},{1,3},{2,0},{3,1},{4,6},{5,7},{6,4},{7,5},{8,10},{9,11},{10,... | collective-permute-start | bytes 1376264 | tf_op jit(solution)/shard_map/ppermute | solution.py:632
  39.4 0.1 pad_add_fusion.place_ref
  39.5 1.6 %collective-permute-done.8.refs_5_ = bf16[2048,256]{1,0:T(8,128)(2,1)} collective-permute-done((bf16[2048,256]{1,0:T(8,128)(2,1)}, bf16[2048,256]{1,0:T(8,128)(2,1)}, u32[]{:S(2)}, u32[]{:S(2)}) %collective-permute-start.8) | collective-permute-done | bytes 1048608 | tf_op jit(solution)/shard_map/ppermute | solution.py:627
  41.1 4.7 %merge_own.1 = (f32[112,512]{1,0:T(8,128)S(1)}, f32[112,512]{1,0:T(8,128)S(1)}, f32[112,512]{1,0:T(8,128)S(1)}, bf16[4096,256]{1,0:T(8,128)(2,1)S(1)}, bf16[4096...) custom-call(s32[2]{0:T(128)S(1)} %pad_add_fusion.place_ref, ...), custom_call_target="tpu_custom_call" | custom-call | flops 939524096 | bytes 1048576 | tf_op jit(solution)/shard_map/merge_own/pallas_call | solution.py:545
  45.8 4.2 %collective-permute-done.9.upper_ref = bf16[112,2048]{1,0:T(8,128)(2,1)} collective-permute-done((bf16[112,2048]{1,0:T(8,128)(2,1)}, bf16[112,2048]{1,0:T(8,128)(2,1)}, u32[]{:S(2)}, u32[]{:S(2)}) %collective-permute-start.9) | collective-permute-done | bytes 458784 | tf_op jit(solution)/shard_map/ppermute | solution.py:632
  50.0 0.3 collective-permute-done.10.lower_ref
  50.3 2.8 %merge_other.1 = (bf16[112,1024]{1,0:T(8,128)(2,1)S(1)}, bf16[112,1024]{1,0:T(8,128)(2,1)S(1)}) custom-call(s32[2]{0:T(128)S(1)} %pad_add_fusion.place_ref, bf16[112,2048]{1,0:T(8,128)(2,1)} %collective-permute-done.9.upper_ref, bf16[112,2048]{1,0:T(8,128)(2,1)} %collective-permute-done.10.lower_ref, bf16[4096,256]{1,0:T(8,128)(2,1)S(1)} %get-tuple-element.78.refs_0_, ...), custom_call_target="tpu_custom_call" | custom-call | flops 939524096 | bytes 1048576 | tf_op jit(solution)/shard_map/merge_other/pallas_call | solution.py:545
  53.1 1.6 %collective-permute-start.11 = (bf16[112,1024]{1,0:T(8,128)(2,1)S(1)}, bf16[112,1024]{1,0:T(8,128)(2,1)S(1)}, u32[]{:S(2)}, u32[]{:S(2)}) collective-permute-start(bf16[112,1024]{1,0:T(8,128)(2,1)S(1)} %get-tuple-element.84), channel_id=1, source_target_pairs={{0,4},{1,5},{2,6},{3,7},{4,0},{5,1},{6,2},{7,3},{8,12},{9,13},{10,... | collective-permute-start | bytes 688136 | tf_op jit(solution)/shard_map/ppermute | solution.py:632
  54.7 0.6 collective-permute-start.12
  55.3 4.7 %collective-permute-done.11.from_y_ref = bf16[112,1024]{1,0:T(8,128)(2,1)S(1)} collective-permute-done((bf16[112,1024]{1,0:T(8,128)(2,1)S(1)}, bf16[112,1024]{1,0:T(8,128)(2,1)S(1)}, u32[]{:S(2)}, u32[]{:S(2)}) %collective-permute-start.11) | collective-permute-done | bytes 229408 | tf_op jit(solution)/shard_map/ppermute | solution.py:632
  60.0 0.9 collective-permute-done.12.from_x_ref
  60.9 0.6 combine.1.mine_ref
  61.7 0.8 collective-permute-start.13
  62.5 1.0 collective-permute-done.14.theirs_ref
  63.5 2.6 %feed_forward.4 = (bf16[112,2048]{1,0:T(8,128)(2,1)S(1)}, bf16[112,1024]{1,0:T(8,128)(2,1)S(1)}, bf16[112,1024]{1,0:T(8,128)(2,1)S(1)}) custom-call(bf16[112,2048]{1,0:T(8,128)(2,1)S(1)} %combine.1.mine_ref, bf16[112,2048]{1,0:T(8,128)(2,1)S(1)} %collective-permute-done.14.theirs_ref, bf16[2048,1024]{1,0:T(8,128)(2,1)S(1)} %copy-done, ...), custom_call_target="tpu_custom_call" | custom-call | flops 1879048192 | bytes 8388608 | tf_op jit(solution)/shard_map/feed_forward/pallas_call | solution.py:603
  66.1 4.1 %collective-permute-done.13.mine_ref = bf16[112,2048]{1,0:T(8,128)(2,1)S(1)} collective-permute-done((bf16[112,2048]{1,0:T(8,128)(2,1)S(1)}, bf16[112,2048]{1,0:T(8,128)(2,1)S(1)}, u32[]{:S(2)}, u32[]{:S(2)}) %collective-permute-start.13) | collective-permute-done | bytes 458784 | tf_op jit(solution)/shard_map/ppermute | solution.py:637
  70.2 0.8 collective-permute-start.19
  71.0 1.0 collective-permute-done.17.theirs_ref
  72.0 2.6 %feed_forward.5 = (bf16[112,2048]{1,0:T(8,128)(2,1)S(1)}, bf16[112,1024]{1,0:T(8,128)(2,1)S(1)}, bf16[112,1024]{1,0:T(8,128)(2,1)S(1)}) custom-call(bf16[112,2048]{1,0:T(8,128)(2,1)S(1)} %collective-permute-done.13.mine_ref, bf16[112,2048]{1,0:T(8,128)(2,1)S(1)} %collective-permute-done.17.theirs_ref, bf16[2048,1024]{1,0:T(8,128)(2,1)S(1)} %copy-done, ...), custom_call_target="tpu_custom_call" | custom-call | flops 1879048192 | bytes 8388608 | tf_op jit(solution)/shard_map/feed_forward/pallas_call | solution.py:603
  74.6 0.2 collective-permute-start.18
  74.8 3.9 %collective-permute-done.19.mine_ref = bf16[112,2048]{1,0:T(8,128)(2,1)S(1)} collective-permute-done((bf16[112,2048]{1,0:T(8,128)(2,1)S(1)}, bf16[112,2048]{1,0:T(8,128)(2,1)S(1)}, u32[]{:S(2)}, u32[]{:S(2)}) %collective-permute-start.19) | collective-permute-done | bytes 458784 | tf_op jit(solution)/shard_map/ppermute | solution.py:637
  78.7 0.8 collective-permute-start.22
  79.5 1.0 collective-permute-done.20.theirs_ref
  80.5 2.6 %feed_forward.6 = (bf16[112,2048]{1,0:T(8,128)(2,1)S(1)}, bf16[112,1024]{1,0:T(8,128)(2,1)S(1)}, bf16[112,1024]{1,0:T(8,128)(2,1)S(1)}) custom-call(bf16[112,2048]{1,0:T(8,128)(2,1)S(1)} %collective-permute-done.19.mine_ref, bf16[112,2048]{1,0:T(8,128)(2,1)S(1)} %collective-permute-done.20.theirs_ref, bf16[2048,1024]{1,0:T(8,128)(2,1)S(1)} %copy-done, ...), custom_call_target="tpu_custom_call" | custom-call | flops 1879048192 | bytes 8388608 | tf_op jit(solution)/shard_map/feed_forward/pallas_call | solution.py:603
  83.1 0.2 collective-permute-start.21
  83.3 0.4 collective-permute-start.24
  83.7 3.5 %collective-permute-done.22.mine_ref = bf16[112,2048]{1,0:T(8,128)(2,1)S(1)} collective-permute-done((bf16[112,2048]{1,0:T(8,128)(2,1)S(1)}, bf16[112,2048]{1,0:T(8,128)(2,1)S(1)}, u32[]{:S(2)}, u32[]{:S(2)}) %collective-permute-start.22) | collective-permute-done | bytes 458784 | tf_op jit(solution)/shard_map/ppermute | solution.py:637
  87.2 0.1 add_convert_fusion.2
  87.3 1.7 %collective-permute-done.23.theirs_ref = bf16[112,2048]{1,0:T(8,128)(2,1)S(1)} collective-permute-done((bf16[112,2048]{1,0:T(8,128)(2,1)S(1)}, bf16[112,2048]{1,0:T(8,128)(2,1)S(1)}, u32[]{:S(2)}, u32[]{:S(2)}) %collective-permute-start.23) | collective-permute-done | bytes 458784 | tf_op jit(solution)/shard_map/ppermute | solution.py:627
  89.0 0.8 collective-permute-start.25
  89.8 2.6 %feed_forward.7 = (bf16[112,2048]{1,0:T(8,128)(2,1)S(1)}, bf16[112,1024]{1,0:T(8,128)(2,1)S(1)}, bf16[112,1024]{1,0:T(8,128)(2,1)S(1)}) custom-call(bf16[112,2048]{1,0:T(8,128)(2,1)S(1)} %collective-permute-done.22.mine_ref, bf16[112,2048]{1,0:T(8,128)(2,1)S(1)} %collective-permute-done.23.theirs_ref, bf16[2048,1024]{1,0:T(8,128)(2,1)S(1)} %copy-done, ...), custom_call_target="tpu_custom_call" | custom-call | flops 1879048192 | bytes 8388608 | tf_op jit(solution)/shard_map/feed_forward/pallas_call | solution.py:603
  92.5 0.5 collective-permute-start.27
  93.0 0.1 collective-permute-start.16
  93.1 0.4 collective-permute-start.15
  93.5 0.5 collective-permute-done.26
  94.0 0.1 collective-permute-start.30
  94.1 3.3 %collective-permute-done.25 = bf16[112,2048]{1,0:T(8,128)(2,1)S(1)} collective-permute-done((bf16[112,2048]{1,0:T(8,128)(2,1)S(1)}, bf16[112,2048]{1,0:T(8,128)(2,1)S(1)}, u32[]{:S(2)}, u32[]{:S(2)}) %collective-permute-start.25) | collective-permute-done | bytes 458784 | tf_op jit(solution)/shard_map/ppermute | solution.py:637
  97.5 0.1 add_convert_fusion.1
  97.6 0.9 collective-permute-start.28
  98.5 0.2 add_convert_fusion.5
  98.7 1.4 %collective-permute-start.31 = (bf16[112,1024]{1,0:T(8,128)(2,1)S(1)}, bf16[112,1024]{1,0:T(8,128)(2,1)S(1)}, u32[]{:S(2)}, u32[]{:S(2)}) collective-permute-start(bf16[112,1024]{1,0:T(8,128)(2,1)S(1)} %get-tuple-element.113), channel_id=1, source_target_pairs={{0,2},{1,5},{2,0},{3,7},{4,6},{5,1},{6,4},{7,3},{8,10},{9,13},{10,... | collective-permute-start | bytes 688136 | tf_op jit(solution)/shard_map/ppermute | solution.py:637
  100.2 0.7 collective-permute-start.29
  100.8 6.1 %collective-permute-done.31 = bf16[112,1024]{1,0:T(8,128)(2,1)S(1)} collective-permute-done((bf16[112,1024]{1,0:T(8,128)(2,1)S(1)}, bf16[112,1024]{1,0:T(8,128)(2,1)S(1)}, u32[]{:S(2)}, u32[]{:S(2)}) %collective-permute-start.31) | collective-permute-done | bytes 229408 | tf_op jit(solution)/shard_map/ppermute | solution.py:637
  106.9 2.5 %collective-permute-done.29 = bf16[112,1024]{1,0:T(8,128)(2,1)S(1)} collective-permute-done((bf16[112,1024]{1,0:T(8,128)(2,1)S(1)}, bf16[112,1024]{1,0:T(8,128)(2,1)S(1)}, u32[]{:S(2)}, u32[]{:S(2)}) %collective-permute-start.29) | collective-permute-done | bytes 229408 | tf_op jit(solution)/shard_map/ppermute | solution.py:637
  109.4 0.8 collective-permute-done.28
  110.2 0.4 add_convert_fusion
  110.6 0.9 convert_element_type.89
  (63 shorter events, 0.6 us)
Async XLA Ops:
  0.6 38.9 %collective-permute-start.4 = (bf16[4096,256]{1,0:T(8,128)(2,1)}, bf16[4096,256]{1,0:T(8,128)(2,1)}, u32[]{:S(2)}, u32[]{:S(2)}) collective-permute-start(bf16[4096,256]{1,0:T(8,128)(2,1)} %refs_0_.1), channel_id=1, source_target_pairs={{0,1},{1,0},{2,3},{3,2},{4,5},{5,4},{6,7},{7,6},{8,9},{9,8},{10,11... | collective-permute-start | bytes 6291464 | tf_op jit(solution)/shard_map/ppermute | solution.py:627
  1.1 1.2 %copy-start.3 = (bf16[18,24,1024]{2,1,0:T(8,128)(2,1)S(1)}, bf16[18,24,1024]{2,1,0:T(8,128)(2,1)}, u32[]{:S(2)}) copy-start(bf16[18,24,1024]{2,1,0:T(8,128)(2,1)} %tokens_ref.7) | copy-start | bytes 2654212
  2.3 7.8 %copy-start.4 = (bf16[18,24,1024]{2,1,0:T(8,128)(2,1)S(1)}, bf16[18,24,1024]{2,1,0:T(8,128)(2,1)}, u32[]{:S(2)}) copy-start(bf16[18,24,1024]{2,1,0:T(8,128)(2,1)} %tokens_ref.7) | copy-start | bytes 2654212
  2.4 13.2 %collective-permute-start.1 = (bf16[18,8,1024]{2,1,0:T(8,128)(2,1)S(1)}, bf16[18,8,1024]{2,1,0:T(8,128)(2,1)S(1)}, u32[]{:S(2)}, u32[]{:S(2)}) collective-permute-start(bf16[18,8,1024]{2,1,0:T(8,128)(2,1)S(1)} %get-tuple-element.60), channel_id=1, source_target_pairs={{0,7},{1,0},{2,1},{3,2},{4,3},{5,4},{6,5},{7,6},{8,15},{9,8},{10,9... | collective-permute-start | bytes 884744 | tf_op jit(solution)/shard_map/ppermute | solution.py:467
  6.0 10.0 %collective-permute-start = (bf16[18,8,1024]{2,1,0:T(8,128)(2,1)S(1)}, bf16[18,8,1024]{2,1,0:T(8,128)(2,1)S(1)}, u32[]{:S(2)}, u32[]{:S(2)}) collective-permute-start(bf16[18,8,1024]{2,1,0:T(8,128)(2,1)S(1)} %get-tuple-element.59), channel_id=1, source_target_pairs={{0,1},{1,2},{2,3},{3,4},{4,5},{5,6},{6,7},{7,0},{8,9},{9,10},{10,1... | collective-permute-start | bytes 884744 | tf_op jit(solution)/shard_map/ppermute | solution.py:467
  8.9 27.1 %collective-permute-start.5 = (bf16[2048,256]{1,0:T(8,128)(2,1)}, bf16[2048,256]{1,0:T(8,128)(2,1)}, u32[]{:S(2)}, u32[]{:S(2)}) collective-permute-start(bf16[2048,256]{1,0:T(8,128)(2,1)} %get-tuple-element.71), channel_id=1, source_target_pairs={{0,2},{1,3},{2,0},{3,1},{4,6},{5,7},{6,4},{7,5},{8,10},{9,11},{10,... | collective-permute-start | bytes 3145736 | tf_op jit(solution)/shard_map/ppermute | solution.py:632
  9.0 27.6 %collective-permute-start.6 = (bf16[2048,256]{1,0:T(8,128)(2,1)}, bf16[2048,256]{1,0:T(8,128)(2,1)}, u32[]{:S(2)}, u32[]{:S(2)}) collective-permute-start(bf16[2048,256]{1,0:T(8,128)(2,1)} %get-tuple-element.72), channel_id=1, source_target_pairs={{0,4},{1,5},{2,6},{3,7},{4,0},{5,1},{6,2},{7,3},{8,12},{9,13},{10,... | collective-permute-start | bytes 3145736 | tf_op jit(solution)/shard_map/ppermute | solution.py:632
  10.1 10.9 %copy-start.5 = (bf16[1024,1024]{1,0:T(8,128)(2,1)S(1)}, bf16[1024,1024]{1,0:T(8,128)(2,1)}, u32[]{:S(2)}) copy-start(bf16[1024,1024]{1,0:T(8,128)(2,1)} %out_w_ref.3) | copy-start | bytes 6291460
  10.1 10.9 %copy-start.6 = (bf16[576,144]{1,0:T(8,128)(2,1)S(1)}, bf16[576,144]{1,0:T(8,128)(2,1)}, u32[]{:S(2)}) copy-start(bf16[576,144]{1,0:T(8,128)(2,1)} %constant.74.clone.rest_1_) | copy-start | bytes 497668
  10.1 10.9 %copy-start.7 = (bf16[576,256]{1,0:T(8,128)(2,1)S(1)}, bf16[576,256]{1,0:T(8,128)(2,1)}, u32[]{:S(2)}) copy-start(bf16[576,256]{1,0:T(8,128)(2,1)} %constant.75.clone.rest_2_) | copy-start | bytes 884740
  10.2 10.9 %copy-start.8 = (bf16[256,288]{1,0:T(8,128)(2,1)S(1)}, bf16[256,288]{1,0:T(8,128)(2,1)}, u32[]{:S(2)}) copy-start(bf16[256,288]{1,0:T(8,128)(2,1)} %constant.72.clone.patch_ref) | copy-start | bytes 442372
  10.2 10.9 %copy-start.9 = (bf16[144,576]{1,0:T(8,128)(2,1)S(1)}, bf16[144,576]{1,0:T(8,128)(2,1)}, u32[]{:S(2)}) copy-start(bf16[144,576]{1,0:T(8,128)(2,1)} %constant.76.clone.rest_3_) | copy-start | bytes 497668
  10.2 10.9 %copy-start.13 = (bf16[240,240]{1,0:T(8,128)(2,1)S(1)}, bf16[240,240]{1,0:T(8,128)(2,1)}, u32[]{:S(2)}) copy-start(bf16[240,240]{1,0:T(8,128)(2,1)} %constant.73.clone.rest_0_) | copy-start | bytes 345604
  16.0 11.7 %collective-permute-start.2 = (bf16[3,40,1024]{2,1,0:T(8,128)(2,1)S(1)}, bf16[3,40,1024]{2,1,0:T(8,128)(2,1)S(1)}, u32[]{:S(2)}, u32[]{:S(2)}) collective-permute-start(bf16[3,40,1024]{2,1,0:T(8,128)(2,1)S(1)} %pad_maximum_fusion.1), channel_id=1, source_target_pairs={{0,8},{8,16},{16,24},{1,9},{9,17},{17,25},{2,10},{10,18},{18,26},{... | collective-permute-start | bytes 737288 | tf_op jit(solution)/shard_map/ppermute | solution.py:467
  19.5 10.4 %collective-permute-start.3 = (bf16[3,40,1024]{2,1,0:T(8,128)(2,1)S(1)}, bf16[3,40,1024]{2,1,0:T(8,128)(2,1)S(1)}, u32[]{:S(2)}, u32[]{:S(2)}) collective-permute-start(bf16[3,40,1024]{2,1,0:T(8,128)(2,1)S(1)} %pad_maximum_fusion.2), channel_id=1, source_target_pairs={{8,0},{16,8},{24,16},{9,1},{17,9},{25,17},{10,2},{18,10},{26,18},{... | collective-permute-start | bytes 737288 | tf_op jit(solution)/shard_map/ppermute | solution.py:467
  21.1 8.9 %copy-start.10 = (bf16[304,256]{1,0:T(8,128)(2,1)S(1)}, bf16[304,256]{1,0:T(8,128)(2,1)}, u32[]{:S(2)}) copy-start(bf16[304,256]{1,0:T(8,128)(2,1)} %constant.80.clone.rest_2_.rest_6_) | copy-start | bytes 466948
  21.1 8.9 %copy-start.11 = (bf16[240,256]{1,0:T(8,128)(2,1)S(1)}, bf16[240,256]{1,0:T(8,128)(2,1)}, u32[]{:S(2)}) copy-start(bf16[240,256]{1,0:T(8,128)(2,1)} %constant.78.clone.rest_0_) | copy-start | bytes 368644
  21.1 8.9 %copy-start.12 = (bf16[240,256]{1,0:T(8,128)(2,1)S(1)}, bf16[240,256]{1,0:T(8,128)(2,1)}, u32[]{:S(2)}) copy-start(bf16[240,256]{1,0:T(8,128)(2,1)} %constant.82.clone.rest_4_) | copy-start | bytes 368644
  21.1 8.9 %copy-start.14 = (bf16[192,192]{1,0:T(8,128)(2,1)S(1)}, bf16[192,192]{1,0:T(8,128)(2,1)}, u32[]{:S(2)}) copy-start(bf16[192,192]{1,0:T(8,128)(2,1)} %constant.77.clone.patch_ref) | copy-start | bytes 221188
  21.1 8.9 %copy-start.15 = (bf16[304,80]{1,0:T(8,128)(2,1)S(1)}, bf16[304,80]{1,0:T(8,128)(2,1)}, u32[]{:S(2)}) copy-start(bf16[304,80]{1,0:T(8,128)(2,1)} %constant.79.clone.rest_1_.rest_5_) | copy-start | bytes 145924
  21.1 8.9 %copy-start.16 = (bf16[80,304]{1,0:T(8,128)(2,1)S(1)}, bf16[80,304]{1,0:T(8,128)(2,1)}, u32[]{:S(2)}) copy-start(bf16[80,304]{1,0:T(8,128)(2,1)} %constant.81.clone.rest_3_.rest_7_) | copy-start | bytes 145924
  30.0 11.1 %copy-start.2 = (bf16[4096,256]{1,0:T(8,128)(2,1)S(1)}, bf16[4096,256]{1,0:T(8,128)(2,1)}, u32[]{:S(2)}) copy-start(bf16[4096,256]{1,0:T(8,128)(2,1)} %refs_0_.1) | copy-start | bytes 6291460
  36.6 2.9 %collective-permute-start.7 = (bf16[2048,256]{1,0:T(8,128)(2,1)}, bf16[2048,256]{1,0:T(8,128)(2,1)S(1)}, u32[]{:S(2)}, u32[]{:S(2)}) collective-permute-start(bf16[2048,256]{1,0:T(8,128)(2,1)} %collective-permute-done.5.refs_2_), channel_id=1, source_target_pairs={{0,1},{1,0},{2,3},{3,2},{4,5},{5,4},{6,7},{7,6},{8,9},{9,8},{10,11... | collective-permute-start | bytes 3145736 | tf_op jit(solution)/shard_map/ppermute | solution.py:627
  36.8 4.3 %collective-permute-start.8 = (bf16[2048,256]{1,0:T(8,128)(2,1)}, bf16[2048,256]{1,0:T(8,128)(2,1)}, u32[]{:S(2)}, u32[]{:S(2)}) collective-permute-start(bf16[2048,256]{1,0:T(8,128)(2,1)} %collective-permute-done.6.refs_4_), channel_id=1, source_target_pairs={{0,1},{1,0},{2,3},{3,2},{4,5},{5,4},{6,7},{7,6},{8,9},{9,8},{10,11... | collective-permute-start | bytes 3145736 | tf_op jit(solution)/shard_map/ppermute | solution.py:627
  37.1 12.9 %collective-permute-start.9 = (bf16[112,2048]{1,0:T(8,128)(2,1)}, bf16[112,2048]{1,0:T(8,128)(2,1)}, u32[]{:S(2)}, u32[]{:S(2)}) collective-permute-start(bf16[112,2048]{1,0:T(8,128)(2,1)} %get-tuple-element.68.upper_ref), channel_id=1, source_target_pairs={{0,4},{1,5},{2,6},{3,7},{4,0},{5,1},{6,2},{7,3},{8,12},{9,13},{10,... | collective-permute-start | bytes 1376264 | tf_op jit(solution)/shard_map/ppermute | solution.py:632
  37.3 13.0 %collective-permute-start.10 = (bf16[112,2048]{1,0:T(8,128)(2,1)}, bf16[112,2048]{1,0:T(8,128)(2,1)}, u32[]{:S(2)}, u32[]{:S(2)}) collective-permute-start(bf16[112,2048]{1,0:T(8,128)(2,1)} %get-tuple-element.69.lower_ref), channel_id=1, source_target_pairs={{0,2},{1,3},{2,0},{3,1},{4,6},{5,7},{6,4},{7,5},{8,10},{9,11},{10,... | collective-permute-start | bytes 1376264 | tf_op jit(solution)/shard_map/ppermute | solution.py:632
  50.3 13.2 %copy-start = (bf16[2048,1024]{1,0:T(8,128)(2,1)S(1)}, bf16[2048,1024]{1,0:T(8,128)(2,1)}, u32[]{:S(2)}) copy-start(bf16[2048,1024]{1,0:T(8,128)(2,1)} %up_ref.7) | copy-start | bytes 12582916
  50.3 13.2 %copy-start.1 = (bf16[1024,2048]{1,0:T(8,128)(2,1)S(1)}, bf16[1024,2048]{1,0:T(8,128)(2,1)}, u32[]{:S(2)}) copy-start(bf16[1024,2048]{1,0:T(8,128)(2,1)} %down_ref.7) | copy-start | bytes 12582916
  53.1 6.9 %collective-permute-start.11 = (bf16[112,1024]{1,0:T(8,128)(2,1)S(1)}, bf16[112,1024]{1,0:T(8,128)(2,1)S(1)}, u32[]{:S(2)}, u32[]{:S(2)}) collective-permute-start(bf16[112,1024]{1,0:T(8,128)(2,1)S(1)} %get-tuple-element.84), channel_id=1, source_target_pairs={{0,4},{1,5},{2,6},{3,7},{4,0},{5,1},{6,2},{7,3},{8,12},{9,13},{10,... | collective-permute-start | bytes 688136 | tf_op jit(solution)/shard_map/ppermute | solution.py:632
  54.7 6.2 %collective-permute-start.12 = (bf16[112,1024]{1,0:T(8,128)(2,1)S(1)}, bf16[112,1024]{1,0:T(8,128)(2,1)S(1)}, u32[]{:S(2)}, u32[]{:S(2)}) collective-permute-start(bf16[112,1024]{1,0:T(8,128)(2,1)S(1)} %get-tuple-element.85), channel_id=1, source_target_pairs={{0,2},{1,3},{2,0},{3,1},{4,6},{5,7},{6,4},{7,5},{8,10},{9,11},{10,... | collective-permute-start | bytes 688136 | tf_op jit(solution)/shard_map/ppermute | solution.py:632
  61.6 1.9 %collective-permute-start.14 = (bf16[112,2048]{1,0:T(8,128)(2,1)S(1)}, bf16[112,2048]{1,0:T(8,128)(2,1)S(1)}, u32[]{:S(2)}, u32[]{:S(2)}) collective-permute-start(bf16[112,2048]{1,0:T(8,128)(2,1)S(1)} %combine.1.mine_ref), channel_id=1, source_target_pairs={{0,1},{1,0},{2,3},{3,2},{4,5},{5,4},{6,7},{7,6},{8,9},{9,8},{10,11... | collective-permute-start | bytes 1376264 | tf_op jit(solution)/shard_map/ppermute | solution.py:627
  61.7 8.5 %collective-permute-start.13 = (bf16[112,2048]{1,0:T(8,128)(2,1)S(1)}, bf16[112,2048]{1,0:T(8,128)(2,1)S(1)}, u32[]{:S(2)}, u32[]{:S(2)}) collective-permute-start(bf16[112,2048]{1,0:T(8,128)(2,1)S(1)} %combine.1.mine_ref), channel_id=1, source_target_pairs={{0,2},{1,5},{2,0},{3,7},{4,6},{5,1},{6,4},{7,3},{8,10},{9,13},{10,... | collective-permute-start | bytes 1376264 | tf_op jit(solution)/shard_map/ppermute | solution.py:637
  70.2 1.8 %collective-permute-start.17 = (bf16[112,2048]{1,0:T(8,128)(2,1)S(1)}, bf16[112,2048]{1,0:T(8,128)(2,1)S(1)}, u32[]{:S(2)}, u32[]{:S(2)}) collective-permute-start(bf16[112,2048]{1,0:T(8,128)(2,1)S(1)} %collective-permute-done.13.mine_ref), channel_id=1, source_target_pairs={{0,1},{1,0},{2,3},{3,2},{4,5},{5,4},{6,7},{7,6},{8,9},{9,8},{10,11... | collective-permute-start | bytes 1376264 | tf_op jit(solution)/shard_map/ppermute | solution.py:627
  70.2 8.5 %collective-permute-start.19 = (bf16[112,2048]{1,0:T(8,128)(2,1)S(1)}, bf16[112,2048]{1,0:T(8,128)(2,1)S(1)}, u32[]{:S(2)}, u32[]{:S(2)}) collective-permute-start(bf16[112,2048]{1,0:T(8,128)(2,1)S(1)} %collective-permute-done.13.mine_ref), channel_id=1, source_target_pairs={{0,4},{1,3},{2,6},{3,1},{4,0},{5,7},{6,2},{7,5},{8,12},{9,11},{10,... | collective-permute-start | bytes 1376264 | tf_op jit(solution)/shard_map/ppermute | solution.py:637
  74.6 4.1 %collective-permute-start.18 = (bf16[112,1024]{1,0:T(8,128)(2,1)S(1)}, bf16[112,1024]{1,0:T(8,128)(2,1)S(1)}, u32[]{:S(2)}, u32[]{:S(2)}) collective-permute-start(bf16[112,1024]{1,0:T(8,128)(2,1)S(1)} %get-tuple-element.93), channel_id=1, source_target_pairs={{0,1},{1,0},{2,3},{3,2},{4,5},{5,4},{6,7},{7,6},{8,9},{9,8},{10,11... | collective-permute-start | bytes 688136 | tf_op jit(solution)/shard_map/ppermute | solution.py:627
  78.7 1.8 %collective-permute-start.20 = (bf16[112,2048]{1,0:T(8,128)(2,1)S(1)}, bf16[112,2048]{1,0:T(8,128)(2,1)S(1)}, u32[]{:S(2)}, u32[]{:S(2)}) collective-permute-start(bf16[112,2048]{1,0:T(8,128)(2,1)S(1)} %collective-permute-done.19.mine_ref), channel_id=1, source_target_pairs={{0,1},{1,0},{2,3},{3,2},{4,5},{5,4},{6,7},{7,6},{8,9},{9,8},{10,11... | collective-permute-start | bytes 1376264 | tf_op jit(solution)/shard_map/ppermute | solution.py:627
  78.7 8.5 %collective-permute-start.22 = (bf16[112,2048]{1,0:T(8,128)(2,1)S(1)}, bf16[112,2048]{1,0:T(8,128)(2,1)S(1)}, u32[]{:S(2)}, u32[]{:S(2)}) collective-permute-start(bf16[112,2048]{1,0:T(8,128)(2,1)S(1)} %combine.1.mine_ref), channel_id=1, source_target_pairs={{0,4},{1,3},{2,6},{3,1},{4,0},{5,7},{6,2},{7,5},{8,12},{9,11},{10,... | collective-permute-start | bytes 1376264 | tf_op jit(solution)/shard_map/ppermute | solution.py:637
  83.1 4.1 %collective-permute-start.21 = (bf16[112,1024]{1,0:T(8,128)(2,1)S(1)}, bf16[112,1024]{1,0:T(8,128)(2,1)S(1)}, u32[]{:S(2)}, u32[]{:S(2)}) collective-permute-start(bf16[112,1024]{1,0:T(8,128)(2,1)S(1)} %get-tuple-element.95), channel_id=1, source_target_pairs={{0,1},{1,0},{2,3},{3,2},{4,5},{5,4},{6,7},{7,6},{8,9},{9,8},{10,11... | collective-permute-start | bytes 688136 | tf_op jit(solution)/shard_map/ppermute | solution.py:627
  83.3 3.8 %collective-permute-start.24 = (bf16[112,1024]{1,0:T(8,128)(2,1)S(1)}, bf16[112,1024]{1,0:T(8,128)(2,1)S(1)}, u32[]{:S(2)}, u32[]{:S(2)}) collective-permute-start(bf16[112,1024]{1,0:T(8,128)(2,1)S(1)} %get-tuple-element.101), channel_id=1, source_target_pairs={{0,1},{1,0},{2,3},{3,2},{4,5},{5,4},{6,7},{7,6},{8,9},{9,8},{10,11... | collective-permute-start | bytes 688136 | tf_op jit(solution)/shard_map/ppermute | solution.py:627
  87.2 1.8 %collective-permute-start.23 = (bf16[112,2048]{1,0:T(8,128)(2,1)S(1)}, bf16[112,2048]{1,0:T(8,128)(2,1)S(1)}, u32[]{:S(2)}, u32[]{:S(2)}) collective-permute-start(bf16[112,2048]{1,0:T(8,128)(2,1)S(1)} %collective-permute-done.22.mine_ref), channel_id=1, source_target_pairs={{0,1},{1,0},{2,3},{3,2},{4,5},{5,4},{6,7},{7,6},{8,9},{9,8},{10,11... | collective-permute-start | bytes 1376264 | tf_op jit(solution)/shard_map/ppermute | solution.py:627
  89.0 8.5 %collective-permute-start.25 = (bf16[112,2048]{1,0:T(8,128)(2,1)S(1)}, bf16[112,2048]{1,0:T(8,128)(2,1)S(1)}, u32[]{:S(2)}, u32[]{:S(2)}) collective-permute-start(bf16[112,2048]{1,0:T(8,128)(2,1)S(1)} %add_convert_fusion.2), channel_id=1, source_target_pairs={{0,4},{1,3},{2,6},{3,1},{4,0},{5,7},{6,2},{7,5},{8,12},{9,11},{10,... | collective-permute-start | bytes 1376264 | tf_op jit(solution)/shard_map/ppermute | solution.py:637
  92.5 1.6 %collective-permute-start.26 = (bf16[112,1024]{1,0:T(8,128)(2,1)S(1)}, bf16[112,1024]{1,0:T(8,128)(2,1)S(1)}, u32[]{:S(2)}, u32[]{:S(2)}) collective-permute-start(bf16[112,1024]{1,0:T(8,128)(2,1)S(1)} %get-tuple-element.105), channel_id=1, source_target_pairs={{0,1},{1,0},{2,3},{3,2},{4,5},{5,4},{6,7},{7,6},{8,9},{9,8},{10,11... | collective-permute-start | bytes 688136 | tf_op jit(solution)/shard_map/ppermute | solution.py:627
  92.5 4.9 %collective-permute-start.27 = (bf16[112,1024]{1,0:T(8,128)(2,1)S(1)}, bf16[112,1024]{1,0:T(8,128)(2,1)S(1)}, u32[]{:S(2)}, u32[]{:S(2)}) collective-permute-start(bf16[112,1024]{1,0:T(8,128)(2,1)S(1)} %get-tuple-element.107), channel_id=1, source_target_pairs={{0,1},{1,0},{2,3},{3,2},{4,5},{5,4},{6,7},{7,6},{8,9},{9,8},{10,11... | collective-permute-start | bytes 688136 | tf_op jit(solution)/shard_map/ppermute | solution.py:627
  93.0 7.8 %collective-permute-start.16 = (bf16[112,1024]{1,0:T(8,128)(2,1)S(1)}, bf16[112,1024]{1,0:T(8,128)(2,1)S(1)}, u32[]{:S(2)}, u32[]{:S(2)}) collective-permute-start(bf16[112,1024]{1,0:T(8,128)(2,1)S(1)} %get-tuple-element.91), channel_id=1, source_target_pairs={{0,1},{1,0},{2,3},{3,2},{4,5},{5,4},{6,7},{7,6},{8,9},{9,8},{10,11... | collective-permute-start | bytes 688136 | tf_op jit(solution)/shard_map/ppermute | solution.py:627
  93.1 7.7 %collective-permute-start.15 = (bf16[112,1024]{1,0:T(8,128)(2,1)S(1)}, bf16[112,1024]{1,0:T(8,128)(2,1)S(1)}, u32[]{:S(2)}, u32[]{:S(2)}) collective-permute-start(bf16[112,1024]{1,0:T(8,128)(2,1)S(1)} %get-tuple-element.90), channel_id=1, source_target_pairs={{0,1},{1,0},{2,3},{3,2},{4,5},{5,4},{6,7},{7,6},{8,9},{9,8},{10,11... | collective-permute-start | bytes 688136 | tf_op jit(solution)/shard_map/ppermute | solution.py:627
  94.0 4.5 %collective-permute-start.30 = (bf16[112,1024]{1,0:T(8,128)(2,1)S(1)}, bf16[112,1024]{1,0:T(8,128)(2,1)S(1)}, u32[]{:S(2)}, u32[]{:S(2)}) collective-permute-start(bf16[112,1024]{1,0:T(8,128)(2,1)S(1)} %get-tuple-element.111), channel_id=1, source_target_pairs={{0,1},{1,0},{2,3},{3,2},{4,5},{5,4},{6,7},{7,6},{8,9},{9,8},{10,11... | collective-permute-start | bytes 688136 | tf_op jit(solution)/shard_map/ppermute | solution.py:627
  97.6 12.6 %collective-permute-start.28 = (bf16[112,2048]{1,0:T(8,128)(2,1)S(1)}, bf16[112,2048]{1,0:T(8,128)(2,1)S(1)}, u32[]{:S(2)}, u32[]{:S(2)}) collective-permute-start(bf16[112,2048]{1,0:T(8,128)(2,1)S(1)} %add_convert_fusion.1), channel_id=1, source_target_pairs={{0,4},{1,3},{2,6},{3,1},{4,0},{5,7},{6,2},{7,5},{8,12},{9,11},{10,... | collective-permute-start | bytes 1376264 | tf_op jit(solution)/shard_map/ppermute | solution.py:637
  98.7 8.2 %collective-permute-start.31 = (bf16[112,1024]{1,0:T(8,128)(2,1)S(1)}, bf16[112,1024]{1,0:T(8,128)(2,1)S(1)}, u32[]{:S(2)}, u32[]{:S(2)}) collective-permute-start(bf16[112,1024]{1,0:T(8,128)(2,1)S(1)} %get-tuple-element.113), channel_id=1, source_target_pairs={{0,2},{1,5},{2,0},{3,7},{4,6},{5,1},{6,4},{7,3},{8,10},{9,13},{10,... | collective-permute-start | bytes 688136 | tf_op jit(solution)/shard_map/ppermute | solution.py:637
  100.2 9.2 %collective-permute-start.29 = (bf16[112,1024]{1,0:T(8,128)(2,1)S(1)}, bf16[112,1024]{1,0:T(8,128)(2,1)S(1)}, u32[]{:S(2)}, u32[]{:S(2)}) collective-permute-start(bf16[112,1024]{1,0:T(8,128)(2,1)S(1)} %get-tuple-element.112), channel_id=1, source_target_pairs={{0,2},{1,5},{2,0},{3,7},{4,6},{5,1},{6,4},{7,3},{8,10},{9,13},{10,... | collective-permute-start | bytes 688136 | tf_op jit(solution)/shard_map/ppermute | solution.py:637

commit v13 on v12

--- a/solution.py
+++ b/solution.py
@@ -661,8 +661,7 @@
         columns = slice(at, at + half)
         total = near_mine[:, columns].astype(F32) + part.astype(F32) + relayed[:, columns].astype(F32)
         near_back.append(cross(total.astype(BF16), 1, 2))
-    near_back = jnp.concatenate(near_back, axis=1)
-    return sum(part.astype(F32) for part in (own, summed(*first), other_back, near_back))
+    return [own, summed(*first), other_back], near_back
 
 
 def coarse_by_chips(upper, lower, merge_weight, halves, up, down):
@@ -675,7 +674,37 @@
     for m in range(chips):
         part = summed(*feed_forward(arrived[m], core_swap(arrived[m]), up, down))
         total = total + (chip_swap(part, m) if m else part).astype(F32)
-    return total
+    return [total.astype(BF16)], []
+
+
+def finish_kernel(spans, *refs):
+    *parts, low_ref, high_ref, out_ref = refs
+    total = sum(ref[...].astype(F32) for ref in parts)
+    if low_ref is not None:
+        total = total + jnp.concatenate([low_ref[...], high_ref[...]], axis=1).astype(F32)
+    for r, at in enumerate(spans):
+        out_ref[r] = total[at : at + out_ref.shape[1]].astype(BF16)
+
+
+def finish(bands, whole, halves):
+    inner, edge = bands.inner_patches()
+    half = bands.columns // 2
+    start = up16(half * len(inner))
+    place = {r: n * half for n, r in enumerate(inner)} | {r: start + n * half for n, r in enumerate(edge)}
+    spans = [place[r] for r in range(bands.rows // 2)]
+    vmem = pl.BlockSpec(memory_space=pltpu.VMEM)
+
+    def kernel(*refs):
+        finish_kernel(spans, *(refs if halves else (*refs[:-1], None, None, refs[-1])))
+
+    return pl.pallas_call(
+        kernel,
+        in_specs=[vmem] * (len(whole) + len(halves)),
+        out_specs=vmem,
+        out_shape=jax.ShapeDtypeStruct((bands.rows // 2, half, whole[0].shape[1]), BF16),
+        compiler_params=params(16),
+        name="finish",
+    )(*whole, *halves)
 
 
 def per_device(tokens, qkv_weight, out_weight, merge_weight, up_weight, down_weight):
@@ -686,15 +715,8 @@
     halves = halves_of(later)
     middle_out, upper, lower = attention(bands, tokens, sides, qkv_weight, out_weight)
     coarse = coarse_by_squares if lax.axis_size("lon") == 8 else coarse_by_chips
-    total = coarse(upper, lower, merge_weight, halves, up_weight, down_weight)
-    inner, edge = bands.inner_patches()
-    half = columns // 2
-    above = half * sum(r < inner[0] for r in edge)
-    start = up16(half * len(inner))
-    below = start + half * len(edge)
-    ordered = [total[start : start + above], total[: half * len(inner)], total[start + above : below]]
-    coarse_out = jnp.concatenate(ordered, axis=0).astype(jnp.bfloat16)
-    return (middle_out, coarse_out.reshape(rows // 2, columns // 2, -1))
+    parts = coarse(upper, lower, merge_weight, halves, up_weight, down_weight)
+    return (middle_out, finish(bands, *parts))
 
 
 def solution(mesh):

time: 112 us -> 111 us (level)
  no operation moved by 1% of the time
where the time goes in v13:
time: 111 us
  waiting for transfers between devices  44.1 us (40%)
  Pallas kernels  40.3 us (36%)
  starting transfers between devices  23.7 us (21%)
  local copies, waits for them, and re-layouts  1.3 us (1%)
    ppermute x7, waiting for transfers between devices, cross(): lax.ppermute(value, 'lon', [(i, i ^ 2 * (second if i % 2 else first)) for...  24 us
    pallas_call x2, Pallas kernels, vmem_call(): pl.pallas_call(kernel, in_specs=[vmem] * len(args), out_specs=[vmem] * le...  12.5 us
    ppermute x6, waiting for transfers between devices, chip_swap(): lax.ppermute(value, 'lon', [(i, i ^ 2 * offset) for i in range(size)])  10.8 us
    pallas_call x4, Pallas kernels, feed_forward(): pl.pallas_call(ffn_kernel, in_specs=[vmem] * 4, out_specs=[vmem] * 3, out...  10.4 us
    ppermute x4, starting transfers between devices, shift(): return lax.ppermute(part, axis, pairs)  8.58 us
    pallas_call x3, Pallas kernels, local_call(): pl.pallas_call(kernel, in_specs=[pl.BlockSpec(memory_space=pltpu.SMEM)] +...  8.12 us
    ppermute x15, waiting for transfers between devices, core_swap(): return lax.ppermute(value, 'lon', [(i, i ^ 1) for i in range(size)])  6.72 us
    ppermute x7, starting transfers between devices, cross(): lax.ppermute(value, 'lon', [(i, i ^ 2 * (second if i % 2 else first)) for...  6.35 us
  transfers between devices with their start and end apart: 32, of which 20 were waited for; matrix products, arithmetic and copies ran while one was open for 1% of the time, Pallas kernels for 32%

profile of v13, /device:TPU:0, one launch (start us, length us, event | category | flops | bytes accessed | tf_op | source)
XLA Modules:
  0.0 111.2 jit_solution(4063472669084061513)
XLA Ops:
  0.6 0.5 collective-permute-start.4
  1.1 1.2 %copy-done.3 = bf16[18,24,1024]{2,1,0:T(8,128)(2,1)S(1)} copy-done((bf16[18,24,1024]{2,1,0:T(8,128)(2,1)S(1)}, bf16[18,24,1024]{2,1,0:T(8,128)(2,1)}, u32[]{:S(2)}) %copy-start.3) | copy-done | bytes 884760
  2.4 3.6 %collective-permute-start.1 = (bf16[18,8,1024]{2,1,0:T(8,128)(2,1)S(1)}, bf16[18,8,1024]{2,1,0:T(8,128)(2,1)S(1)}, u32[]{:S(2)}, u32[]{:S(2)}) collective-permute-start(bf16[18,8,1024]{2,1,0:T(8,128)(2,1)S(1)} %get-tuple-element.60), channel_id=1, source_target_pairs={{0,7},{1,0},{2,1},{3,2},{4,3},{5,4},{6,5},{7,6},{8,15},{9,8},{10,9... | collective-permute-start | bytes 884744 | tf_op jit(solution)/shard_map/ppermute | solution.py:467
  6.0 2.9 %halves.1 = (bf16[2048,256]{1,0:T(8,128)(2,1)}, bf16[2048,256]{1,0:T(8,128)(2,1)}) custom-call(bf16[4096,256]{1,0:T(8,128)(2,1)} %refs_0_.1), custom_call_target="tpu_custom_call" | custom-call | tf_op jit(solution)/shard_map/halves/pallas_call | solution.py:202
  9.0 1.1 collective-permute-start.6
  10.2 5.2 %own_projection.1 = (bf16[448,3072]{1,0:T(8,128)(2,1)S(1)}, bf16[1024,2048]{1,0:T(8,128)(2,1)S(1)}) custom-call(bf16[18,24,1024]{2,1,0:T(8,128)(2,1)S(1)} %copy-done.4, bf16[1024,3072]{1,0:T(8,128)(2,1)} %weight_ref.1), custom_call_target="tpu_custom_call" | custom-call | flops 2818572288 | bytes 6291456 | tf_op jit(solution)/shard_map/own_projection/pallas_call | solution.py:242
  15.5 0.1 or_select_fusion.bias_ref
  15.6 0.4 collective-permute-done.west_ref
  16.0 3.5 %collective-permute-start.2 = (bf16[3,40,1024]{2,1,0:T(8,128)(2,1)S(1)}, bf16[3,40,1024]{2,1,0:T(8,128)(2,1)S(1)}, u32[]{:S(2)}, u32[]{:S(2)}) collective-permute-start(bf16[3,40,1024]{2,1,0:T(8,128)(2,1)S(1)} %pad_maximum_fusion), channel_id=1, source_target_pairs={{0,8},{8,16},{16,24},{1,9},{9,17},{17,25},{2,10},{10,18},{18,26},{... | collective-permute-start | bytes 737288 | tf_op jit(solution)/shard_map/ppermute | solution.py:467
  19.5 1.5 %collective-permute-start.3 = (bf16[3,40,1024]{2,1,0:T(8,128)(2,1)S(1)}, bf16[3,40,1024]{2,1,0:T(8,128)(2,1)S(1)}, u32[]{:S(2)}, u32[]{:S(2)}) collective-permute-start(bf16[3,40,1024]{2,1,0:T(8,128)(2,1)S(1)} %pad_maximum_fusion.1), channel_id=1, source_target_pairs={{8,0},{16,8},{24,16},{9,1},{17,9},{25,17},{10,2},{18,10},{26,18},{... | collective-permute-start | bytes 737288 | tf_op jit(solution)/shard_map/ppermute | solution.py:467
  21.1 6.5 %middle_attention.1 = (bf16[288,2048]{1,0:T(8,128)(2,1)S(1)}, bf16[12,24,1024]{2,1,0:T(8,128)(2,1)S(1)}, bf16[64,2048]{1,0:T(8,128)(2,1)S(1)}, bf16[64,2048]{1,0:T(8,128)(2,1)S(1)}) custom-call(bf16[18,24,1024]{2,1,0:T(8,128)(2,1)S(1)} %copy-done.4, bf16[18,8,1024]{2,1,0:T(8,128)(2,1)S(1)} %collective-permute-done.west_ref, ...), custom_call_target="tpu_custom_call" | custom-call | flops 5000000000 | bytes 1048576 | tf_op jit(solution)/shard_map/middle_attention/pallas_call | solution.py:398
  27.7 2.3 %collective-permute-done.3.south_ref = bf16[3,40,1024]{2,1,0:T(8,128)(2,1)S(1)} collective-permute-done((bf16[3,40,1024]{2,1,0:T(8,128)(2,1)S(1)}, bf16[3,40,1024]{2,1,0:T(8,128)(2,1)S(1)}, u32[]{:S(2)}, u32[]{:S(2)}) %collective-permute-start.3) | collective-permute-done | bytes 245792 | tf_op jit(solution)/shard_map/ppermute | solution.py:467
  30.0 6.0 %edge_attention.1 = (bf16[18,24,1024]{2,1,0:T(8,128)(2,1)}, bf16[112,2048]{1,0:T(8,128)(2,1)}, bf16[112,2048]{1,0:T(8,128)(2,1)}) custom-call(bf16[18,24,1024]{2,1,0:T(8,128)(2,1)S(1)} %copy-done.4, bf16[3,40,1024]{2,1,0:T(8,128)(2,1)S(1)} %collective-permute-done.2.north_ref, bf16[3,40,1024]{2,1,0:T(8,128)(2,1)S(1)} %collective-permute-done.3.south_ref, ...), custom_call_target="tpu_custom_call" | custom-call | flops 6000000000 | bytes 1048576 | tf_op jit(solution)/shard_map/edge_attention/pallas_call | solution.py:398
  36.0 0.7 collective-permute-done.6.refs_4_
  36.6 0.2 collective-permute-start.7
  36.8 0.3 collective-permute-start.8
  37.1 0.2 collective-permute-start.9
  37.3 2.1 %collective-permute-start.10 = (bf16[112,2048]{1,0:T(8,128)(2,1)}, bf16[112,2048]{1,0:T(8,128)(2,1)}, u32[]{:S(2)}, u32[]{:S(2)}) collective-permute-start(bf16[112,2048]{1,0:T(8,128)(2,1)} %get-tuple-element.69.lower_ref), channel_id=1, source_target_pairs={{0,2},{1,3},{2,0},{3,1},{4,6},{5,7},{6,4},{7,5},{8,10},{9,11},{10,... | collective-permute-start | bytes 1376264 | tf_op jit(solution)/shard_map/ppermute | solution.py:632
  39.4 0.1 pad_add_fusion.place_ref
  39.5 1.6 %collective-permute-done.8.refs_5_ = bf16[2048,256]{1,0:T(8,128)(2,1)} collective-permute-done((bf16[2048,256]{1,0:T(8,128)(2,1)}, bf16[2048,256]{1,0:T(8,128)(2,1)}, u32[]{:S(2)}, u32[]{:S(2)}) %collective-permute-start.8) | collective-permute-done | bytes 1048608 | tf_op jit(solution)/shard_map/ppermute | solution.py:627
  41.1 4.7 %merge_own.1 = (f32[112,512]{1,0:T(8,128)S(1)}, f32[112,512]{1,0:T(8,128)S(1)}, f32[112,512]{1,0:T(8,128)S(1)}, bf16[4096,256]{1,0:T(8,128)(2,1)S(1)}, bf16[4096...) custom-call(s32[2]{0:T(128)S(1)} %pad_add_fusion.place_ref, ...), custom_call_target="tpu_custom_call" | custom-call | flops 939524096 | bytes 1048576 | tf_op jit(solution)/shard_map/merge_own/pallas_call | solution.py:545
  45.8 4.2 %collective-permute-done.9.upper_ref = bf16[112,2048]{1,0:T(8,128)(2,1)} collective-permute-done((bf16[112,2048]{1,0:T(8,128)(2,1)}, bf16[112,2048]{1,0:T(8,128)(2,1)}, u32[]{:S(2)}, u32[]{:S(2)}) %collective-permute-start.9) | collective-permute-done | bytes 458784 | tf_op jit(solution)/shard_map/ppermute | solution.py:632
  50.0 0.3 collective-permute-done.10.lower_ref
  50.3 2.8 %merge_other.1 = (bf16[112,1024]{1,0:T(8,128)(2,1)S(1)}, bf16[112,1024]{1,0:T(8,128)(2,1)S(1)}) custom-call(s32[2]{0:T(128)S(1)} %pad_add_fusion.place_ref, bf16[112,2048]{1,0:T(8,128)(2,1)} %collective-permute-done.9.upper_ref, bf16[112,2048]{1,0:T(8,128)(2,1)} %collective-permute-done.10.lower_ref, bf16[4096,256]{1,0:T(8,128)(2,1)S(1)} %get-tuple-element.78.refs_0_, ...), custom_call_target="tpu_custom_call" | custom-call | flops 939524096 | bytes 1048576 | tf_op jit(solution)/shard_map/merge_other/pallas_call | solution.py:545
  53.1 1.6 %collective-permute-start.11 = (bf16[112,1024]{1,0:T(8,128)(2,1)S(1)}, bf16[112,1024]{1,0:T(8,128)(2,1)S(1)}, u32[]{:S(2)}, u32[]{:S(2)}) collective-permute-start(bf16[112,1024]{1,0:T(8,128)(2,1)S(1)} %get-tuple-element.84), channel_id=1, source_target_pairs={{0,4},{1,5},{2,6},{3,7},{4,0},{5,1},{6,2},{7,3},{8,12},{9,13},{10,... | collective-permute-start | bytes 688136 | tf_op jit(solution)/shard_map/ppermute | solution.py:632
  54.7 0.6 collective-permute-start.12
  55.3 4.7 %collective-permute-done.11.from_y_ref = bf16[112,1024]{1,0:T(8,128)(2,1)S(1)} collective-permute-done((bf16[112,1024]{1,0:T(8,128)(2,1)S(1)}, bf16[112,1024]{1,0:T(8,128)(2,1)S(1)}, u32[]{:S(2)}, u32[]{:S(2)}) %collective-permute-start.11) | collective-permute-done | bytes 229408 | tf_op jit(solution)/shard_map/ppermute | solution.py:632
  60.0 0.9 collective-permute-done.12.from_x_ref
  60.9 0.6 combine.1.mine_ref.refs_0_
  61.7 0.8 collective-permute-start.13
  62.5 1.0 collective-permute-done.14.theirs_ref
  63.5 2.6 %feed_forward.4 = (bf16[112,2048]{1,0:T(8,128)(2,1)S(1)}, bf16[112,1024]{1,0:T(8,128)(2,1)S(1)}, bf16[112,1024]{1,0:T(8,128)(2,1)S(1)}) custom-call(bf16[112,2048]{1,0:T(8,128)(2,1)S(1)} %combine.1.mine_ref.refs_0_, bf16[112,2048]{1,0:T(8,128)(2,1)S(1)} %collective-permute-done.14.theirs_ref, bf16[2048,1024]{1,0:T(8,128)(2,1)S(1)} %copy-done, ...), custom_call_target="tpu_custom_call" | custom-call | flops 1879048192 | bytes 8388608 | tf_op jit(solution)/shard_map/feed_forward/pallas_call | solution.py:603
  66.1 4.1 %collective-permute-done.13.mine_ref = bf16[112,2048]{1,0:T(8,128)(2,1)S(1)} collective-permute-done((bf16[112,2048]{1,0:T(8,128)(2,1)S(1)}, bf16[112,2048]{1,0:T(8,128)(2,1)S(1)}, u32[]{:S(2)}, u32[]{:S(2)}) %collective-permute-start.13) | collective-permute-done | bytes 458784 | tf_op jit(solution)/shard_map/ppermute | solution.py:637
  70.2 0.8 collective-permute-start.19
  71.0 1.0 collective-permute-done.17.theirs_ref
  72.0 2.6 %feed_forward.5 = (bf16[112,2048]{1,0:T(8,128)(2,1)S(1)}, bf16[112,1024]{1,0:T(8,128)(2,1)S(1)}, bf16[112,1024]{1,0:T(8,128)(2,1)S(1)}) custom-call(bf16[112,2048]{1,0:T(8,128)(2,1)S(1)} %collective-permute-done.13.mine_ref, bf16[112,2048]{1,0:T(8,128)(2,1)S(1)} %collective-permute-done.17.theirs_ref, bf16[2048,1024]{1,0:T(8,128)(2,1)S(1)} %copy-done, ...), custom_call_target="tpu_custom_call" | custom-call | flops 1879048192 | bytes 8388608 | tf_op jit(solution)/shard_map/feed_forward/pallas_call | solution.py:603
  74.6 0.2 collective-permute-start.18
  74.8 3.9 %collective-permute-done.19.mine_ref = bf16[112,2048]{1,0:T(8,128)(2,1)S(1)} collective-permute-done((bf16[112,2048]{1,0:T(8,128)(2,1)S(1)}, bf16[112,2048]{1,0:T(8,128)(2,1)S(1)}, u32[]{:S(2)}, u32[]{:S(2)}) %collective-permute-start.19) | collective-permute-done | bytes 458784 | tf_op jit(solution)/shard_map/ppermute | solution.py:637
  78.7 0.8 collective-permute-start.22
  79.5 1.0 collective-permute-done.20.theirs_ref
  80.5 2.6 %feed_forward.6 = (bf16[112,2048]{1,0:T(8,128)(2,1)S(1)}, bf16[112,1024]{1,0:T(8,128)(2,1)S(1)}, bf16[112,1024]{1,0:T(8,128)(2,1)S(1)}) custom-call(bf16[112,2048]{1,0:T(8,128)(2,1)S(1)} %collective-permute-done.19.mine_ref, bf16[112,2048]{1,0:T(8,128)(2,1)S(1)} %collective-permute-done.20.theirs_ref, bf16[2048,1024]{1,0:T(8,128)(2,1)S(1)} %copy-done, ...), custom_call_target="tpu_custom_call" | custom-call | flops 1879048192 | bytes 8388608 | tf_op jit(solution)/shard_map/feed_forward/pallas_call | solution.py:603
  83.1 0.2 collective-permute-start.21
  83.3 0.4 collective-permute-start.24
  83.7 3.5 %collective-permute-done.22.mine_ref = bf16[112,2048]{1,0:T(8,128)(2,1)S(1)} collective-permute-done((bf16[112,2048]{1,0:T(8,128)(2,1)S(1)}, bf16[112,2048]{1,0:T(8,128)(2,1)S(1)}, u32[]{:S(2)}, u32[]{:S(2)}) %collective-permute-start.22) | collective-permute-done | bytes 458784 | tf_op jit(solution)/shard_map/ppermute | solution.py:637
  87.2 0.1 add_convert_fusion.1
  87.3 1.7 %collective-permute-done.23.theirs_ref = bf16[112,2048]{1,0:T(8,128)(2,1)S(1)} collective-permute-done((bf16[112,2048]{1,0:T(8,128)(2,1)S(1)}, bf16[112,2048]{1,0:T(8,128)(2,1)S(1)}, u32[]{:S(2)}, u32[]{:S(2)}) %collective-permute-start.23) | collective-permute-done | bytes 458784 | tf_op jit(solution)/shard_map/ppermute | solution.py:627
  89.0 0.8 collective-permute-start.25
  89.8 2.6 %feed_forward.7 = (bf16[112,2048]{1,0:T(8,128)(2,1)S(1)}, bf16[112,1024]{1,0:T(8,128)(2,1)S(1)}, bf16[112,1024]{1,0:T(8,128)(2,1)S(1)}) custom-call(bf16[112,2048]{1,0:T(8,128)(2,1)S(1)} %collective-permute-done.22.mine_ref, bf16[112,2048]{1,0:T(8,128)(2,1)S(1)} %collective-permute-done.23.theirs_ref, bf16[2048,1024]{1,0:T(8,128)(2,1)S(1)} %copy-done, ...), custom_call_target="tpu_custom_call" | custom-call | flops 1879048192 | bytes 8388608 | tf_op jit(solution)/shard_map/feed_forward/pallas_call | solution.py:603
  92.5 0.5 collective-permute-start.27
  93.0 0.1 collective-permute-start.16
  93.1 0.4 collective-permute-start.15
  93.5 0.5 collective-permute-done.26
  94.0 0.1 collective-permute-start.30
  94.1 3.3 %collective-permute-done.25 = bf16[112,2048]{1,0:T(8,128)(2,1)S(1)} collective-permute-done((bf16[112,2048]{1,0:T(8,128)(2,1)S(1)}, bf16[112,2048]{1,0:T(8,128)(2,1)S(1)}, u32[]{:S(2)}, u32[]{:S(2)}) %collective-permute-start.25) | collective-permute-done | bytes 458784 | tf_op jit(solution)/shard_map/ppermute | solution.py:637
  97.5 0.1 add_convert_fusion
  97.6 0.9 collective-permute-start.28
  98.5 0.2 add_convert_fusion.3
  98.7 1.4 %collective-permute-start.29 = (bf16[112,1024]{1,0:T(8,128)(2,1)S(1)}, bf16[112,1024]{1,0:T(8,128)(2,1)S(1)}, u32[]{:S(2)}, u32[]{:S(2)}) collective-permute-start(bf16[112,1024]{1,0:T(8,128)(2,1)S(1)} %get-tuple-element.113), channel_id=1, source_target_pairs={{0,2},{1,5},{2,0},{3,7},{4,6},{5,1},{6,4},{7,3},{8,10},{9,13},{10,... | collective-permute-start | bytes 688136 | tf_op jit(solution)/shard_map/ppermute | solution.py:637
  100.2 0.7 collective-permute-start.31
  100.8 0.1 add_convert_fusion.2.refs_1_
  101.0 5.9 %collective-permute-done.29.refs_3_ = bf16[112,1024]{1,0:T(8,128)(2,1)S(1)} collective-permute-done((bf16[112,1024]{1,0:T(8,128)(2,1)S(1)}, bf16[112,1024]{1,0:T(8,128)(2,1)S(1)}, u32[]{:S(2)}, u32[]{:S(2)}) %collective-permute-start.29) | collective-permute-done | bytes 229408 | tf_op jit(solution)/shard_map/ppermute | solution.py:637
  106.9 2.5 %collective-permute-done.31.refs_4_ = bf16[112,1024]{1,0:T(8,128)(2,1)S(1)} collective-permute-done((bf16[112,1024]{1,0:T(8,128)(2,1)S(1)}, bf16[112,1024]{1,0:T(8,128)(2,1)S(1)}, u32[]{:S(2)}, u32[]{:S(2)}) %collective-permute-start.31) | collective-permute-done | bytes 229408 | tf_op jit(solution)/shard_map/ppermute | solution.py:637
  109.4 0.8 collective-permute-done.28.refs_2_
  110.2 1.1 finish.1
  (60 shorter events, 0.5 us)
Async XLA Ops:
  0.6 38.9 %collective-permute-start.4 = (bf16[4096,256]{1,0:T(8,128)(2,1)}, bf16[4096,256]{1,0:T(8,128)(2,1)}, u32[]{:S(2)}, u32[]{:S(2)}) collective-permute-start(bf16[4096,256]{1,0:T(8,128)(2,1)} %refs_0_.1), channel_id=1, source_target_pairs={{0,1},{1,0},{2,3},{3,2},{4,5},{5,4},{6,7},{7,6},{8,9},{9,8},{10,11... | collective-permute-start | bytes 6291464 | tf_op jit(solution)/shard_map/ppermute | solution.py:627
  1.1 1.2 %copy-start.3 = (bf16[18,24,1024]{2,1,0:T(8,128)(2,1)S(1)}, bf16[18,24,1024]{2,1,0:T(8,128)(2,1)}, u32[]{:S(2)}) copy-start(bf16[18,24,1024]{2,1,0:T(8,128)(2,1)} %tokens_ref.7) | copy-start | bytes 2654212
  2.3 7.8 %copy-start.4 = (bf16[18,24,1024]{2,1,0:T(8,128)(2,1)S(1)}, bf16[18,24,1024]{2,1,0:T(8,128)(2,1)}, u32[]{:S(2)}) copy-start(bf16[18,24,1024]{2,1,0:T(8,128)(2,1)} %tokens_ref.7) | copy-start | bytes 2654212
  2.4 13.2 %collective-permute-start.1 = (bf16[18,8,1024]{2,1,0:T(8,128)(2,1)S(1)}, bf16[18,8,1024]{2,1,0:T(8,128)(2,1)S(1)}, u32[]{:S(2)}, u32[]{:S(2)}) collective-permute-start(bf16[18,8,1024]{2,1,0:T(8,128)(2,1)S(1)} %get-tuple-element.60), channel_id=1, source_target_pairs={{0,7},{1,0},{2,1},{3,2},{4,3},{5,4},{6,5},{7,6},{8,15},{9,8},{10,9... | collective-permute-start | bytes 884744 | tf_op jit(solution)/shard_map/ppermute | solution.py:467
  6.0 10.0 %collective-permute-start = (bf16[18,8,1024]{2,1,0:T(8,128)(2,1)S(1)}, bf16[18,8,1024]{2,1,0:T(8,128)(2,1)S(1)}, u32[]{:S(2)}, u32[]{:S(2)}) collective-permute-start(bf16[18,8,1024]{2,1,0:T(8,128)(2,1)S(1)} %get-tuple-element.59), channel_id=1, source_target_pairs={{0,1},{1,2},{2,3},{3,4},{4,5},{5,6},{6,7},{7,0},{8,9},{9,10},{10,1... | collective-permute-start | bytes 884744 | tf_op jit(solution)/shard_map/ppermute | solution.py:467
  8.9 27.1 %collective-permute-start.5 = (bf16[2048,256]{1,0:T(8,128)(2,1)}, bf16[2048,256]{1,0:T(8,128)(2,1)}, u32[]{:S(2)}, u32[]{:S(2)}) collective-permute-start(bf16[2048,256]{1,0:T(8,128)(2,1)} %get-tuple-element.71), channel_id=1, source_target_pairs={{0,2},{1,3},{2,0},{3,1},{4,6},{5,7},{6,4},{7,5},{8,10},{9,11},{10,... | collective-permute-start | bytes 3145736 | tf_op jit(solution)/shard_map/ppermute | solution.py:632
  9.0 27.6 %collective-permute-start.6 = (bf16[2048,256]{1,0:T(8,128)(2,1)}, bf16[2048,256]{1,0:T(8,128)(2,1)}, u32[]{:S(2)}, u32[]{:S(2)}) collective-permute-start(bf16[2048,256]{1,0:T(8,128)(2,1)} %get-tuple-element.72), channel_id=1, source_target_pairs={{0,4},{1,5},{2,6},{3,7},{4,0},{5,1},{6,2},{7,3},{8,12},{9,13},{10,... | collective-permute-start | bytes 3145736 | tf_op jit(solution)/shard_map/ppermute | solution.py:632
  10.1 10.9 %copy-start.5 = (bf16[1024,1024]{1,0:T(8,128)(2,1)S(1)}, bf16[1024,1024]{1,0:T(8,128)(2,1)}, u32[]{:S(2)}) copy-start(bf16[1024,1024]{1,0:T(8,128)(2,1)} %out_w_ref.3) | copy-start | bytes 6291460
  10.1 10.9 %copy-start.6 = (bf16[576,144]{1,0:T(8,128)(2,1)S(1)}, bf16[576,144]{1,0:T(8,128)(2,1)}, u32[]{:S(2)}) copy-start(bf16[576,144]{1,0:T(8,128)(2,1)} %constant.74.clone.rest_1_) | copy-start | bytes 497668
  10.2 10.9 %copy-start.7 = (bf16[576,256]{1,0:T(8,128)(2,1)S(1)}, bf16[576,256]{1,0:T(8,128)(2,1)}, u32[]{:S(2)}) copy-start(bf16[576,256]{1,0:T(8,128)(2,1)} %constant.75.clone.rest_2_) | copy-start | bytes 884740
  10.2 10.9 %copy-start.8 = (bf16[256,288]{1,0:T(8,128)(2,1)S(1)}, bf16[256,288]{1,0:T(8,128)(2,1)}, u32[]{:S(2)}) copy-start(bf16[256,288]{1,0:T(8,128)(2,1)} %constant.72.clone.patch_ref) | copy-start | bytes 442372
  10.2 10.9 %copy-start.9 = (bf16[144,576]{1,0:T(8,128)(2,1)S(1)}, bf16[144,576]{1,0:T(8,128)(2,1)}, u32[]{:S(2)}) copy-start(bf16[144,576]{1,0:T(8,128)(2,1)} %constant.76.clone.rest_3_) | copy-start | bytes 497668
  10.2 10.9 %copy-start.13 = (bf16[240,240]{1,0:T(8,128)(2,1)S(1)}, bf16[240,240]{1,0:T(8,128)(2,1)}, u32[]{:S(2)}) copy-start(bf16[240,240]{1,0:T(8,128)(2,1)} %constant.73.clone.rest_0_) | copy-start | bytes 345604
  16.0 11.7 %collective-permute-start.2 = (bf16[3,40,1024]{2,1,0:T(8,128)(2,1)S(1)}, bf16[3,40,1024]{2,1,0:T(8,128)(2,1)S(1)}, u32[]{:S(2)}, u32[]{:S(2)}) collective-permute-start(bf16[3,40,1024]{2,1,0:T(8,128)(2,1)S(1)} %pad_maximum_fusion), channel_id=1, source_target_pairs={{0,8},{8,16},{16,24},{1,9},{9,17},{17,25},{2,10},{10,18},{18,26},{... | collective-permute-start | bytes 737288 | tf_op jit(solution)/shard_map/ppermute | solution.py:467
  19.5 10.4 %collective-permute-start.3 = (bf16[3,40,1024]{2,1,0:T(8,128)(2,1)S(1)}, bf16[3,40,1024]{2,1,0:T(8,128)(2,1)S(1)}, u32[]{:S(2)}, u32[]{:S(2)}) collective-permute-start(bf16[3,40,1024]{2,1,0:T(8,128)(2,1)S(1)} %pad_maximum_fusion.1), channel_id=1, source_target_pairs={{8,0},{16,8},{24,16},{9,1},{17,9},{25,17},{10,2},{18,10},{26,18},{... | collective-permute-start | bytes 737288 | tf_op jit(solution)/shard_map/ppermute | solution.py:467
  21.1 8.9 %copy-start.10 = (bf16[304,256]{1,0:T(8,128)(2,1)S(1)}, bf16[304,256]{1,0:T(8,128)(2,1)}, u32[]{:S(2)}) copy-start(bf16[304,256]{1,0:T(8,128)(2,1)} %constant.80.clone.rest_2_.rest_6_) | copy-start | bytes 466948
  21.1 8.9 %copy-start.11 = (bf16[240,256]{1,0:T(8,128)(2,1)S(1)}, bf16[240,256]{1,0:T(8,128)(2,1)}, u32[]{:S(2)}) copy-start(bf16[240,256]{1,0:T(8,128)(2,1)} %constant.78.clone.rest_0_) | copy-start | bytes 368644
  21.1 8.9 %copy-start.12 = (bf16[240,256]{1,0:T(8,128)(2,1)S(1)}, bf16[240,256]{1,0:T(8,128)(2,1)}, u32[]{:S(2)}) copy-start(bf16[240,256]{1,0:T(8,128)(2,1)} %constant.82.clone.rest_4_) | copy-start | bytes 368644
  21.1 8.8 %copy-start.14 = (bf16[192,192]{1,0:T(8,128)(2,1)S(1)}, bf16[192,192]{1,0:T(8,128)(2,1)}, u32[]{:S(2)}) copy-start(bf16[192,192]{1,0:T(8,128)(2,1)} %constant.77.clone.patch_ref) | copy-start | bytes 221188
  21.1 8.8 %copy-start.15 = (bf16[304,80]{1,0:T(8,128)(2,1)S(1)}, bf16[304,80]{1,0:T(8,128)(2,1)}, u32[]{:S(2)}) copy-start(bf16[304,80]{1,0:T(8,128)(2,1)} %constant.79.clone.rest_1_.rest_5_) | copy-start | bytes 145924
  21.1 8.8 %copy-start.16 = (bf16[80,304]{1,0:T(8,128)(2,1)S(1)}, bf16[80,304]{1,0:T(8,128)(2,1)}, u32[]{:S(2)}) copy-start(bf16[80,304]{1,0:T(8,128)(2,1)} %constant.81.clone.rest_3_.rest_7_) | copy-start | bytes 145924
  30.0 11.2 %copy-start.2 = (bf16[4096,256]{1,0:T(8,128)(2,1)S(1)}, bf16[4096,256]{1,0:T(8,128)(2,1)}, u32[]{:S(2)}) copy-start(bf16[4096,256]{1,0:T(8,128)(2,1)} %refs_0_.1) | copy-start | bytes 6291460
  36.6 2.9 %collective-permute-start.7 = (bf16[2048,256]{1,0:T(8,128)(2,1)}, bf16[2048,256]{1,0:T(8,128)(2,1)S(1)}, u32[]{:S(2)}, u32[]{:S(2)}) collective-permute-start(bf16[2048,256]{1,0:T(8,128)(2,1)} %collective-permute-done.5.refs_2_), channel_id=1, source_target_pairs={{0,1},{1,0},{2,3},{3,2},{4,5},{5,4},{6,7},{7,6},{8,9},{9,8},{10,11... | collective-permute-start | bytes 3145736 | tf_op jit(solution)/shard_map/ppermute | solution.py:627
  36.8 4.3 %collective-permute-start.8 = (bf16[2048,256]{1,0:T(8,128)(2,1)}, bf16[2048,256]{1,0:T(8,128)(2,1)}, u32[]{:S(2)}, u32[]{:S(2)}) collective-permute-start(bf16[2048,256]{1,0:T(8,128)(2,1)} %collective-permute-done.6.refs_4_), channel_id=1, source_target_pairs={{0,1},{1,0},{2,3},{3,2},{4,5},{5,4},{6,7},{7,6},{8,9},{9,8},{10,11... | collective-permute-start | bytes 3145736 | tf_op jit(solution)/shard_map/ppermute | solution.py:627
  37.1 12.9 %collective-permute-start.9 = (bf16[112,2048]{1,0:T(8,128)(2,1)}, bf16[112,2048]{1,0:T(8,128)(2,1)}, u32[]{:S(2)}, u32[]{:S(2)}) collective-permute-start(bf16[112,2048]{1,0:T(8,128)(2,1)} %get-tuple-element.68.upper_ref), channel_id=1, source_target_pairs={{0,4},{1,5},{2,6},{3,7},{4,0},{5,1},{6,2},{7,3},{8,12},{9,13},{10,... | collective-permute-start | bytes 1376264 | tf_op jit(solution)/shard_map/ppermute | solution.py:632
  37.3 13.0 %collective-permute-start.10 = (bf16[112,2048]{1,0:T(8,128)(2,1)}, bf16[112,2048]{1,0:T(8,128)(2,1)}, u32[]{:S(2)}, u32[]{:S(2)}) collective-permute-start(bf16[112,2048]{1,0:T(8,128)(2,1)} %get-tuple-element.69.lower_ref), channel_id=1, source_target_pairs={{0,2},{1,3},{2,0},{3,1},{4,6},{5,7},{6,4},{7,5},{8,10},{9,11},{10,... | collective-permute-start | bytes 1376264 | tf_op jit(solution)/shard_map/ppermute | solution.py:632
  50.3 13.2 %copy-start = (bf16[2048,1024]{1,0:T(8,128)(2,1)S(1)}, bf16[2048,1024]{1,0:T(8,128)(2,1)}, u32[]{:S(2)}) copy-start(bf16[2048,1024]{1,0:T(8,128)(2,1)} %up_ref.7) | copy-start | bytes 12582916
  50.3 13.2 %copy-start.1 = (bf16[1024,2048]{1,0:T(8,128)(2,1)S(1)}, bf16[1024,2048]{1,0:T(8,128)(2,1)}, u32[]{:S(2)}) copy-start(bf16[1024,2048]{1,0:T(8,128)(2,1)} %down_ref.7) | copy-start | bytes 12582916
  53.1 6.9 %collective-permute-start.11 = (bf16[112,1024]{1,0:T(8,128)(2,1)S(1)}, bf16[112,1024]{1,0:T(8,128)(2,1)S(1)}, u32[]{:S(2)}, u32[]{:S(2)}) collective-permute-start(bf16[112,1024]{1,0:T(8,128)(2,1)S(1)} %get-tuple-element.84), channel_id=1, source_target_pairs={{0,4},{1,5},{2,6},{3,7},{4,0},{5,1},{6,2},{7,3},{8,12},{9,13},{10,... | collective-permute-start | bytes 688136 | tf_op jit(solution)/shard_map/ppermute | solution.py:632
  54.7 6.2 %collective-permute-start.12 = (bf16[112,1024]{1,0:T(8,128)(2,1)S(1)}, bf16[112,1024]{1,0:T(8,128)(2,1)S(1)}, u32[]{:S(2)}, u32[]{:S(2)}) collective-permute-start(bf16[112,1024]{1,0:T(8,128)(2,1)S(1)} %get-tuple-element.85), channel_id=1, source_target_pairs={{0,2},{1,3},{2,0},{3,1},{4,6},{5,7},{6,4},{7,5},{8,10},{9,11},{10,... | collective-permute-start | bytes 688136 | tf_op jit(solution)/shard_map/ppermute | solution.py:632
  61.6 1.9 %collective-permute-start.14 = (bf16[112,2048]{1,0:T(8,128)(2,1)S(1)}, bf16[112,2048]{1,0:T(8,128)(2,1)S(1)}, u32[]{:S(2)}, u32[]{:S(2)}) collective-permute-start(bf16[112,2048]{1,0:T(8,128)(2,1)S(1)} %combine.1.mine_ref.refs_0_), channel_id=1, source_target_pairs={{0,1},{1,0},{2,3},{3,2},{4,5},{5,4},{6,7},{7,6},{8,9},{9,8},{10,11... | collective-permute-start | bytes 1376264 | tf_op jit(solution)/shard_map/ppermute | solution.py:627
  61.7 8.5 %collective-permute-start.13 = (bf16[112,2048]{1,0:T(8,128)(2,1)S(1)}, bf16[112,2048]{1,0:T(8,128)(2,1)S(1)}, u32[]{:S(2)}, u32[]{:S(2)}) collective-permute-start(bf16[112,2048]{1,0:T(8,128)(2,1)S(1)} %combine.1.mine_ref.refs_0_), channel_id=1, source_target_pairs={{0,2},{1,5},{2,0},{3,7},{4,6},{5,1},{6,4},{7,3},{8,10},{9,13},{10,... | collective-permute-start | bytes 1376264 | tf_op jit(solution)/shard_map/ppermute | solution.py:637
  70.2 1.8 %collective-permute-start.17 = (bf16[112,2048]{1,0:T(8,128)(2,1)S(1)}, bf16[112,2048]{1,0:T(8,128)(2,1)S(1)}, u32[]{:S(2)}, u32[]{:S(2)}) collective-permute-start(bf16[112,2048]{1,0:T(8,128)(2,1)S(1)} %collective-permute-done.13.mine_ref), channel_id=1, source_target_pairs={{0,1},{1,0},{2,3},{3,2},{4,5},{5,4},{6,7},{7,6},{8,9},{9,8},{10,11... | collective-permute-start | bytes 1376264 | tf_op jit(solution)/shard_map/ppermute | solution.py:627
  70.2 8.5 %collective-permute-start.19 = (bf16[112,2048]{1,0:T(8,128)(2,1)S(1)}, bf16[112,2048]{1,0:T(8,128)(2,1)S(1)}, u32[]{:S(2)}, u32[]{:S(2)}) collective-permute-start(bf16[112,2048]{1,0:T(8,128)(2,1)S(1)} %collective-permute-done.13.mine_ref), channel_id=1, source_target_pairs={{0,4},{1,3},{2,6},{3,1},{4,0},{5,7},{6,2},{7,5},{8,12},{9,11},{10,... | collective-permute-start | bytes 1376264 | tf_op jit(solution)/shard_map/ppermute | solution.py:637
  74.6 4.1 %collective-permute-start.18 = (bf16[112,1024]{1,0:T(8,128)(2,1)S(1)}, bf16[112,1024]{1,0:T(8,128)(2,1)S(1)}, u32[]{:S(2)}, u32[]{:S(2)}) collective-permute-start(bf16[112,1024]{1,0:T(8,128)(2,1)S(1)} %get-tuple-element.93), channel_id=1, source_target_pairs={{0,1},{1,0},{2,3},{3,2},{4,5},{5,4},{6,7},{7,6},{8,9},{9,8},{10,11... | collective-permute-start | bytes 688136 | tf_op jit(solution)/shard_map/ppermute | solution.py:627
  78.7 1.8 %collective-permute-start.20 = (bf16[112,2048]{1,0:T(8,128)(2,1)S(1)}, bf16[112,2048]{1,0:T(8,128)(2,1)S(1)}, u32[]{:S(2)}, u32[]{:S(2)}) collective-permute-start(bf16[112,2048]{1,0:T(8,128)(2,1)S(1)} %collective-permute-done.19.mine_ref), channel_id=1, source_target_pairs={{0,1},{1,0},{2,3},{3,2},{4,5},{5,4},{6,7},{7,6},{8,9},{9,8},{10,11... | collective-permute-start | bytes 1376264 | tf_op jit(solution)/shard_map/ppermute | solution.py:627
  78.7 8.5 %collective-permute-start.22 = (bf16[112,2048]{1,0:T(8,128)(2,1)S(1)}, bf16[112,2048]{1,0:T(8,128)(2,1)S(1)}, u32[]{:S(2)}, u32[]{:S(2)}) collective-permute-start(bf16[112,2048]{1,0:T(8,128)(2,1)S(1)} %combine.1.mine_ref.refs_0_), channel_id=1, source_target_pairs={{0,4},{1,3},{2,6},{3,1},{4,0},{5,7},{6,2},{7,5},{8,12},{9,11},{10,... | collective-permute-start | bytes 1376264 | tf_op jit(solution)/shard_map/ppermute | solution.py:637
  83.1 4.1 %collective-permute-start.21 = (bf16[112,1024]{1,0:T(8,128)(2,1)S(1)}, bf16[112,1024]{1,0:T(8,128)(2,1)S(1)}, u32[]{:S(2)}, u32[]{:S(2)}) collective-permute-start(bf16[112,1024]{1,0:T(8,128)(2,1)S(1)} %get-tuple-element.95), channel_id=1, source_target_pairs={{0,1},{1,0},{2,3},{3,2},{4,5},{5,4},{6,7},{7,6},{8,9},{9,8},{10,11... | collective-permute-start | bytes 688136 | tf_op jit(solution)/shard_map/ppermute | solution.py:627
  83.3 3.8 %collective-permute-start.24 = (bf16[112,1024]{1,0:T(8,128)(2,1)S(1)}, bf16[112,1024]{1,0:T(8,128)(2,1)S(1)}, u32[]{:S(2)}, u32[]{:S(2)}) collective-permute-start(bf16[112,1024]{1,0:T(8,128)(2,1)S(1)} %get-tuple-element.101), channel_id=1, source_target_pairs={{0,1},{1,0},{2,3},{3,2},{4,5},{5,4},{6,7},{7,6},{8,9},{9,8},{10,11... | collective-permute-start | bytes 688136 | tf_op jit(solution)/shard_map/ppermute | solution.py:627
  87.2 1.8 %collective-permute-start.23 = (bf16[112,2048]{1,0:T(8,128)(2,1)S(1)}, bf16[112,2048]{1,0:T(8,128)(2,1)S(1)}, u32[]{:S(2)}, u32[]{:S(2)}) collective-permute-start(bf16[112,2048]{1,0:T(8,128)(2,1)S(1)} %collective-permute-done.22.mine_ref), channel_id=1, source_target_pairs={{0,1},{1,0},{2,3},{3,2},{4,5},{5,4},{6,7},{7,6},{8,9},{9,8},{10,11... | collective-permute-start | bytes 1376264 | tf_op jit(solution)/shard_map/ppermute | solution.py:627
  89.0 8.5 %collective-permute-start.25 = (bf16[112,2048]{1,0:T(8,128)(2,1)S(1)}, bf16[112,2048]{1,0:T(8,128)(2,1)S(1)}, u32[]{:S(2)}, u32[]{:S(2)}) collective-permute-start(bf16[112,2048]{1,0:T(8,128)(2,1)S(1)} %add_convert_fusion.1), channel_id=1, source_target_pairs={{0,4},{1,3},{2,6},{3,1},{4,0},{5,7},{6,2},{7,5},{8,12},{9,11},{10,... | collective-permute-start | bytes 1376264 | tf_op jit(solution)/shard_map/ppermute | solution.py:637
  92.5 1.6 %collective-permute-start.26 = (bf16[112,1024]{1,0:T(8,128)(2,1)S(1)}, bf16[112,1024]{1,0:T(8,128)(2,1)S(1)}, u32[]{:S(2)}, u32[]{:S(2)}) collective-permute-start(bf16[112,1024]{1,0:T(8,128)(2,1)S(1)} %get-tuple-element.105), channel_id=1, source_target_pairs={{0,1},{1,0},{2,3},{3,2},{4,5},{5,4},{6,7},{7,6},{8,9},{9,8},{10,11... | collective-permute-start | bytes 688136 | tf_op jit(solution)/shard_map/ppermute | solution.py:627
  92.5 4.9 %collective-permute-start.27 = (bf16[112,1024]{1,0:T(8,128)(2,1)S(1)}, bf16[112,1024]{1,0:T(8,128)(2,1)S(1)}, u32[]{:S(2)}, u32[]{:S(2)}) collective-permute-start(bf16[112,1024]{1,0:T(8,128)(2,1)S(1)} %get-tuple-element.107), channel_id=1, source_target_pairs={{0,1},{1,0},{2,3},{3,2},{4,5},{5,4},{6,7},{7,6},{8,9},{9,8},{10,11... | collective-permute-start | bytes 688136 | tf_op jit(solution)/shard_map/ppermute | solution.py:627
  93.0 7.8 %collective-permute-start.16 = (bf16[112,1024]{1,0:T(8,128)(2,1)S(1)}, bf16[112,1024]{1,0:T(8,128)(2,1)S(1)}, u32[]{:S(2)}, u32[]{:S(2)}) collective-permute-start(bf16[112,1024]{1,0:T(8,128)(2,1)S(1)} %get-tuple-element.91), channel_id=1, source_target_pairs={{0,1},{1,0},{2,3},{3,2},{4,5},{5,4},{6,7},{7,6},{8,9},{9,8},{10,11... | collective-permute-start | bytes 688136 | tf_op jit(solution)/shard_map/ppermute | solution.py:627
  93.1 7.7 %collective-permute-start.15 = (bf16[112,1024]{1,0:T(8,128)(2,1)S(1)}, bf16[112,1024]{1,0:T(8,128)(2,1)S(1)}, u32[]{:S(2)}, u32[]{:S(2)}) collective-permute-start(bf16[112,1024]{1,0:T(8,128)(2,1)S(1)} %get-tuple-element.90), channel_id=1, source_target_pairs={{0,1},{1,0},{2,3},{3,2},{4,5},{5,4},{6,7},{7,6},{8,9},{9,8},{10,11... | collective-permute-start | bytes 688136 | tf_op jit(solution)/shard_map/ppermute | solution.py:627
  94.0 4.5 %collective-permute-start.30 = (bf16[112,1024]{1,0:T(8,128)(2,1)S(1)}, bf16[112,1024]{1,0:T(8,128)(2,1)S(1)}, u32[]{:S(2)}, u32[]{:S(2)}) collective-permute-start(bf16[112,1024]{1,0:T(8,128)(2,1)S(1)} %get-tuple-element.111), channel_id=1, source_target_pairs={{0,1},{1,0},{2,3},{3,2},{4,5},{5,4},{6,7},{7,6},{8,9},{9,8},{10,11... | collective-permute-start | bytes 688136 | tf_op jit(solution)/shard_map/ppermute | solution.py:627
  97.6 12.6 %collective-permute-start.28 = (bf16[112,2048]{1,0:T(8,128)(2,1)S(1)}, bf16[112,2048]{1,0:T(8,128)(2,1)S(1)}, u32[]{:S(2)}, u32[]{:S(2)}) collective-permute-start(bf16[112,2048]{1,0:T(8,128)(2,1)S(1)} %add_convert_fusion), channel_id=1, source_target_pairs={{0,4},{1,3},{2,6},{3,1},{4,0},{5,7},{6,2},{7,5},{8,12},{9,11},{10,... | collective-permute-start | bytes 1376264 | tf_op jit(solution)/shard_map/ppermute | solution.py:637
  98.7 8.2 %collective-permute-start.29 = (bf16[112,1024]{1,0:T(8,128)(2,1)S(1)}, bf16[112,1024]{1,0:T(8,128)(2,1)S(1)}, u32[]{:S(2)}, u32[]{:S(2)}) collective-permute-start(bf16[112,1024]{1,0:T(8,128)(2,1)S(1)} %get-tuple-element.113), channel_id=1, source_target_pairs={{0,2},{1,5},{2,0},{3,7},{4,6},{5,1},{6,4},{7,3},{8,10},{9,13},{10,... | collective-permute-start | bytes 688136 | tf_op jit(solution)/shard_map/ppermute | solution.py:637
  100.2 9.2 %collective-permute-start.31 = (bf16[112,1024]{1,0:T(8,128)(2,1)S(1)}, bf16[112,1024]{1,0:T(8,128)(2,1)S(1)}, u32[]{:S(2)}, u32[]{:S(2)}) collective-permute-start(bf16[112,1024]{1,0:T(8,128)(2,1)S(1)} %get-tuple-element.112), channel_id=1, source_target_pairs={{0,2},{1,5},{2,0},{3,7},{4,6},{5,1},{6,4},{7,3},{8,10},{9,13},{10,... | collective-permute-start | bytes 688136 | tf_op jit(solution)/shard_map/ppermute | solution.py:637

commit v14 on v13

--- a/solution.py
+++ b/solution.py
@@ -185,27 +185,21 @@
     )(tokens)
 
 
-def halves_kernel(weight_ref, upper_ref, lower_ref, sems):
+def halves_kernel(weight_ref, upper_ref, lower_ref):
     half = upper_ref.shape[0]
-    copies = [
-        pltpu.make_async_copy(weight_ref.at[k * half : (k + 1) * half], ref, sems.at[k])
-        for k, ref in enumerate((upper_ref, lower_ref))
-    ]
-    for copy in copies:
-        copy.start()
-    for copy in copies:
-        copy.wait()
+    upper_ref[...] = weight_ref[:half, :]
+    lower_ref[...] = weight_ref[half:, :]
 
 
 def halves_of(weight):
     depth, block = weight.shape
+    vmem = pl.BlockSpec(memory_space=pltpu.VMEM)
     return pl.pallas_call(
         halves_kernel,
-        in_specs=[pl.BlockSpec(memory_space=pl.ANY)],
-        out_specs=[pl.BlockSpec(memory_space=pltpu.VMEM)] * 2,
+        in_specs=[vmem],
+        out_specs=[vmem] * 2,
         out_shape=[jax.ShapeDtypeStruct((depth // 2, block), BF16)] * 2,
-        scratch_shapes=[pltpu.SemaphoreType.DMA((2,))],
-        compiler_params=params(52),
+        compiler_params=params(16),
         name="halves",
     )(weight)
 

time: 111 us -> 111 us (level)
  local copies, waits for them, and re-layouts: 1.3 us -> 2.89 us
  Pallas kernels: 40.3 us -> 38.9 us
    unnamed x34 -> x36, local copies, waits for them, and re-layouts: 1.27 us -> 2.86 us
    pallas_call x1, Pallas kernels: 2.93 us -> 1.5 us  [halves_of(): pl.pallas_call(halves_kernel, in_specs=[vmem], out_specs=[vmem] * 2, out_...]
  transfers between devices with their start and end apart: 32 -> 32, of which waited for: 20 -> 20; matrix products, arithmetic and copies ran while one was open for 1% -> 1% of each run, Pallas kernels for 32% -> 31%
where the time goes in v14:
time: 111 us
  waiting for transfers between devices  44 us (40%)
  Pallas kernels  38.9 us (35%)
  starting transfers between devices  23.6 us (21%)
  local copies, waits for them, and re-layouts  2.89 us (3%)
    ppermute x7, waiting for transfers between devices, cross(): lax.ppermute(value, 'lon', [(i, i ^ 2 * (second if i % 2 else first)) for...  24 us
    pallas_call x2, Pallas kernels, vmem_call(): pl.pallas_call(kernel, in_specs=[vmem] * len(args), out_specs=[vmem] * le...  12.5 us
    ppermute x6, waiting for transfers between devices, chip_swap(): lax.ppermute(value, 'lon', [(i, i ^ 2 * offset) for i in range(size)])  10.9 us
    pallas_call x4, Pallas kernels, feed_forward(): pl.pallas_call(ffn_kernel, in_specs=[vmem] * 4, out_specs=[vmem] * 3, out...  10.4 us
    ppermute x4, starting transfers between devices, shift(): return lax.ppermute(part, axis, pairs)  8.58 us
    pallas_call x3, Pallas kernels, local_call(): pl.pallas_call(kernel, in_specs=[pl.BlockSpec(memory_space=pltpu.SMEM)] +...  8.13 us
    ppermute x15, waiting for transfers between devices, core_swap(): return lax.ppermute(value, 'lon', [(i, i ^ 1) for i in range(size)])  6.69 us
    ppermute x7, starting transfers between devices, cross(): lax.ppermute(value, 'lon', [(i, i ^ 2 * (second if i % 2 else first)) for...  6.26 us
  transfers between devices with their start and end apart: 32, of which 20 were waited for; matrix products, arithmetic and copies ran while one was open for 1% of the time, Pallas kernels for 31%

profile of v14, /device:TPU:0, one launch (start us, length us, event | category | flops | bytes accessed | tf_op | source)
XLA Modules:
  0.0 111.2 jit_solution(7307811212750496147)
XLA Ops:
  0.6 0.5 collective-permute-start.4
  1.1 1.2 %copy-done.4 = bf16[18,24,1024]{2,1,0:T(8,128)(2,1)S(1)} copy-done((bf16[18,24,1024]{2,1,0:T(8,128)(2,1)S(1)}, bf16[18,24,1024]{2,1,0:T(8,128)(2,1)}, u32[]{:S(2)}) %copy-start.4) | copy-done | bytes 884760
  2.4 3.6 %collective-permute-start.1 = (bf16[18,8,1024]{2,1,0:T(8,128)(2,1)S(1)}, bf16[18,8,1024]{2,1,0:T(8,128)(2,1)S(1)}, u32[]{:S(2)}, u32[]{:S(2)}) collective-permute-start(bf16[18,8,1024]{2,1,0:T(8,128)(2,1)S(1)} %get-tuple-element.60), channel_id=1, source_target_pairs={{0,7},{1,0},{2,1},{3,2},{4,3},{5,4},{6,5},{7,6},{8,15},{9,8},{10,9... | collective-permute-start | bytes 884744 | tf_op jit(solution)/shard_map/ppermute | solution.py:461
  6.0 1.6 %copy-done.2 = bf16[4096,256]{1,0:T(8,128)(2,1)S(1)} copy-done((bf16[4096,256]{1,0:T(8,128)(2,1)S(1)}, bf16[4096,256]{1,0:T(8,128)(2,1)}, u32[]{:S(2)}) %copy-start.2) | copy-done | bytes 2097176
  7.6 1.5 %halves.1 = (bf16[2048,256]{1,0:T(8,128)(2,1)}, bf16[2048,256]{1,0:T(8,128)(2,1)}) custom-call(bf16[4096,256]{1,0:T(8,128)(2,1)S(1)} %copy-done.2), custom_call_target="tpu_custom_call" | custom-call | tf_op jit(solution)/shard_map/halves/pallas_call | solution.py:197
  9.1 1.1 collective-permute-start.6
  10.3 5.2 %own_projection.1 = (bf16[448,3072]{1,0:T(8,128)(2,1)S(1)}, bf16[1024,2048]{1,0:T(8,128)(2,1)S(1)}) custom-call(bf16[18,24,1024]{2,1,0:T(8,128)(2,1)S(1)} %copy-done.5, bf16[1024,3072]{1,0:T(8,128)(2,1)} %weight_ref.1), custom_call_target="tpu_custom_call" | custom-call | flops 2818572288 | bytes 6291456 | tf_op jit(solution)/shard_map/own_projection/pallas_call | solution.py:236
  15.6 0.1 or_select_fusion.bias_ref
  15.7 0.2 collective-permute-done.west_ref
  15.9 3.5 %collective-permute-start.2 = (bf16[3,40,1024]{2,1,0:T(8,128)(2,1)S(1)}, bf16[3,40,1024]{2,1,0:T(8,128)(2,1)S(1)}, u32[]{:S(2)}, u32[]{:S(2)}) collective-permute-start(bf16[3,40,1024]{2,1,0:T(8,128)(2,1)S(1)} %pad_maximum_fusion), channel_id=1, source_target_pairs={{0,8},{8,16},{16,24},{1,9},{9,17},{17,25},{2,10},{10,18},{18,26},{... | collective-permute-start | bytes 737288 | tf_op jit(solution)/shard_map/ppermute | solution.py:461
  19.4 1.5 %collective-permute-start.3 = (bf16[3,40,1024]{2,1,0:T(8,128)(2,1)S(1)}, bf16[3,40,1024]{2,1,0:T(8,128)(2,1)S(1)}, u32[]{:S(2)}, u32[]{:S(2)}) collective-permute-start(bf16[3,40,1024]{2,1,0:T(8,128)(2,1)S(1)} %pad_maximum_fusion.1), channel_id=1, source_target_pairs={{8,0},{16,8},{24,16},{9,1},{17,9},{25,17},{10,2},{18,10},{26,18},{... | collective-permute-start | bytes 737288 | tf_op jit(solution)/shard_map/ppermute | solution.py:461
  21.1 6.5 %middle_attention.1 = (bf16[288,2048]{1,0:T(8,128)(2,1)S(1)}, bf16[12,24,1024]{2,1,0:T(8,128)(2,1)S(1)}, bf16[64,2048]{1,0:T(8,128)(2,1)S(1)}, bf16[64,2048]{1,0:T(8,128)(2,1)S(1)}) custom-call(bf16[18,24,1024]{2,1,0:T(8,128)(2,1)S(1)} %copy-done.5, bf16[18,8,1024]{2,1,0:T(8,128)(2,1)S(1)} %collective-permute-done.west_ref, ...), custom_call_target="tpu_custom_call" | custom-call | flops 5000000000 | bytes 1048576 | tf_op jit(solution)/shard_map/middle_attention/pallas_call | solution.py:392
  27.6 2.2 %collective-permute-done.3.south_ref = bf16[3,40,1024]{2,1,0:T(8,128)(2,1)S(1)} collective-permute-done((bf16[3,40,1024]{2,1,0:T(8,128)(2,1)S(1)}, bf16[3,40,1024]{2,1,0:T(8,128)(2,1)S(1)}, u32[]{:S(2)}, u32[]{:S(2)}) %collective-permute-start.3) | collective-permute-done | bytes 245792 | tf_op jit(solution)/shard_map/ppermute | solution.py:461
  29.8 6.0 %edge_attention.1 = (bf16[18,24,1024]{2,1,0:T(8,128)(2,1)}, bf16[112,2048]{1,0:T(8,128)(2,1)}, bf16[112,2048]{1,0:T(8,128)(2,1)}) custom-call(bf16[18,24,1024]{2,1,0:T(8,128)(2,1)S(1)} %copy-done.5, bf16[3,40,1024]{2,1,0:T(8,128)(2,1)S(1)} %collective-permute-done.2.north_ref, bf16[3,40,1024]{2,1,0:T(8,128)(2,1)S(1)} %collective-permute-done.3.south_ref, ...), custom_call_target="tpu_custom_call" | custom-call | flops 6000000000 | bytes 1048576 | tf_op jit(solution)/shard_map/edge_attention/pallas_call | solution.py:392
  35.8 0.8 collective-permute-done.6.refs_4_
  36.6 0.2 collective-permute-start.7
  36.8 0.3 collective-permute-start.8
  37.1 0.3 collective-permute-start.9
  37.3 2.1 %collective-permute-start.10 = (bf16[112,2048]{1,0:T(8,128)(2,1)}, bf16[112,2048]{1,0:T(8,128)(2,1)}, u32[]{:S(2)}, u32[]{:S(2)}) collective-permute-start(bf16[112,2048]{1,0:T(8,128)(2,1)} %get-tuple-element.69.lower_ref), channel_id=1, source_target_pairs={{0,2},{1,3},{2,0},{3,1},{4,6},{5,7},{6,4},{7,5},{8,10},{9,11},{10,... | collective-permute-start | bytes 1376264 | tf_op jit(solution)/shard_map/ppermute | solution.py:626
  39.5 1.5 %collective-permute-done.8.refs_5_ = bf16[2048,256]{1,0:T(8,128)(2,1)} collective-permute-done((bf16[2048,256]{1,0:T(8,128)(2,1)}, bf16[2048,256]{1,0:T(8,128)(2,1)}, u32[]{:S(2)}, u32[]{:S(2)}) %collective-permute-start.8) | collective-permute-done | bytes 1048608 | tf_op jit(solution)/shard_map/ppermute | solution.py:621
  41.1 4.7 %merge_own.1 = (f32[112,512]{1,0:T(8,128)S(1)}, f32[112,512]{1,0:T(8,128)S(1)}, f32[112,512]{1,0:T(8,128)S(1)}, bf16[4096,256]{1,0:T(8,128)(2,1)S(1)}, bf16[4096...) custom-call(s32[2]{0:T(128)S(1)} %pad_add_fusion.place_ref, ...), custom_call_target="tpu_custom_call" | custom-call | flops 939524096 | bytes 1048576 | tf_op jit(solution)/shard_map/merge_own/pallas_call | solution.py:539
  45.7 4.3 %collective-permute-done.9.upper_ref = bf16[112,2048]{1,0:T(8,128)(2,1)} collective-permute-done((bf16[112,2048]{1,0:T(8,128)(2,1)}, bf16[112,2048]{1,0:T(8,128)(2,1)}, u32[]{:S(2)}, u32[]{:S(2)}) %collective-permute-start.9) | collective-permute-done | bytes 458784 | tf_op jit(solution)/shard_map/ppermute | solution.py:626
  50.0 0.3 collective-permute-done.10.lower_ref
  50.3 2.8 %merge_other.1 = (bf16[112,1024]{1,0:T(8,128)(2,1)S(1)}, bf16[112,1024]{1,0:T(8,128)(2,1)S(1)}) custom-call(s32[2]{0:T(128)S(1)} %pad_add_fusion.place_ref, bf16[112,2048]{1,0:T(8,128)(2,1)} %collective-permute-done.9.upper_ref, bf16[112,2048]{1,0:T(8,128)(2,1)} %collective-permute-done.10.lower_ref, bf16[4096,256]{1,0:T(8,128)(2,1)S(1)} %get-tuple-element.78.refs_0_, ...), custom_call_target="tpu_custom_call" | custom-call | flops 939524096 | bytes 1048576 | tf_op jit(solution)/shard_map/merge_other/pallas_call | solution.py:539
  53.1 1.5 %collective-permute-start.11 = (bf16[112,1024]{1,0:T(8,128)(2,1)S(1)}, bf16[112,1024]{1,0:T(8,128)(2,1)S(1)}, u32[]{:S(2)}, u32[]{:S(2)}) collective-permute-start(bf16[112,1024]{1,0:T(8,128)(2,1)S(1)} %get-tuple-element.84), channel_id=1, source_target_pairs={{0,4},{1,5},{2,6},{3,7},{4,0},{5,1},{6,2},{7,3},{8,12},{9,13},{10,... | collective-permute-start | bytes 688136 | tf_op jit(solution)/shard_map/ppermute | solution.py:626
  54.7 0.7 collective-permute-start.12
  55.3 4.7 %collective-permute-done.11.from_y_ref = bf16[112,1024]{1,0:T(8,128)(2,1)S(1)} collective-permute-done((bf16[112,1024]{1,0:T(8,128)(2,1)S(1)}, bf16[112,1024]{1,0:T(8,128)(2,1)S(1)}, u32[]{:S(2)}, u32[]{:S(2)}) %collective-permute-start.11) | collective-permute-done | bytes 229408 | tf_op jit(solution)/shard_map/ppermute | solution.py:626
  60.0 0.9 collective-permute-done.12.from_x_ref
  61.0 0.6 combine.1.mine_ref.refs_0_
  61.7 0.8 collective-permute-start.13
  62.5 1.0 collective-permute-done.14.theirs_ref
  63.5 2.6 %feed_forward.4 = (bf16[112,2048]{1,0:T(8,128)(2,1)S(1)}, bf16[112,1024]{1,0:T(8,128)(2,1)S(1)}, bf16[112,1024]{1,0:T(8,128)(2,1)S(1)}) custom-call(bf16[112,2048]{1,0:T(8,128)(2,1)S(1)} %combine.1.mine_ref.refs_0_, bf16[112,2048]{1,0:T(8,128)(2,1)S(1)} %collective-permute-done.14.theirs_ref, bf16[2048,1024]{1,0:T(8,128)(2,1)S(1)} %copy-done, ...), custom_call_target="tpu_custom_call" | custom-call | flops 1879048192 | bytes 8388608 | tf_op jit(solution)/shard_map/feed_forward/pallas_call | solution.py:597
  66.1 4.1 %collective-permute-done.13.mine_ref = bf16[112,2048]{1,0:T(8,128)(2,1)S(1)} collective-permute-done((bf16[112,2048]{1,0:T(8,128)(2,1)S(1)}, bf16[112,2048]{1,0:T(8,128)(2,1)S(1)}, u32[]{:S(2)}, u32[]{:S(2)}) %collective-permute-start.13) | collective-permute-done | bytes 458784 | tf_op jit(solution)/shard_map/ppermute | solution.py:631
  70.2 0.8 collective-permute-start.19
  71.0 1.0 collective-permute-done.17.theirs_ref
  72.0 2.6 %feed_forward.5 = (bf16[112,2048]{1,0:T(8,128)(2,1)S(1)}, bf16[112,1024]{1,0:T(8,128)(2,1)S(1)}, bf16[112,1024]{1,0:T(8,128)(2,1)S(1)}) custom-call(bf16[112,2048]{1,0:T(8,128)(2,1)S(1)} %collective-permute-done.13.mine_ref, bf16[112,2048]{1,0:T(8,128)(2,1)S(1)} %collective-permute-done.17.theirs_ref, bf16[2048,1024]{1,0:T(8,128)(2,1)S(1)} %copy-done, ...), custom_call_target="tpu_custom_call" | custom-call | flops 1879048192 | bytes 8388608 | tf_op jit(solution)/shard_map/feed_forward/pallas_call | solution.py:597
  74.6 0.2 collective-permute-start.18
  74.8 3.9 %collective-permute-done.19.mine_ref = bf16[112,2048]{1,0:T(8,128)(2,1)S(1)} collective-permute-done((bf16[112,2048]{1,0:T(8,128)(2,1)S(1)}, bf16[112,2048]{1,0:T(8,128)(2,1)S(1)}, u32[]{:S(2)}, u32[]{:S(2)}) %collective-permute-start.19) | collective-permute-done | bytes 458784 | tf_op jit(solution)/shard_map/ppermute | solution.py:631
  78.7 0.8 collective-permute-start.22
  79.5 1.0 collective-permute-done.20.theirs_ref
  80.5 2.6 %feed_forward.6 = (bf16[112,2048]{1,0:T(8,128)(2,1)S(1)}, bf16[112,1024]{1,0:T(8,128)(2,1)S(1)}, bf16[112,1024]{1,0:T(8,128)(2,1)S(1)}) custom-call(bf16[112,2048]{1,0:T(8,128)(2,1)S(1)} %collective-permute-done.19.mine_ref, bf16[112,2048]{1,0:T(8,128)(2,1)S(1)} %collective-permute-done.20.theirs_ref, bf16[2048,1024]{1,0:T(8,128)(2,1)S(1)} %copy-done, ...), custom_call_target="tpu_custom_call" | custom-call | flops 1879048192 | bytes 8388608 | tf_op jit(solution)/shard_map/feed_forward/pallas_call | solution.py:597
  83.1 0.2 collective-permute-start.21
  83.3 0.4 collective-permute-start.24
  83.7 3.5 %collective-permute-done.22.mine_ref = bf16[112,2048]{1,0:T(8,128)(2,1)S(1)} collective-permute-done((bf16[112,2048]{1,0:T(8,128)(2,1)S(1)}, bf16[112,2048]{1,0:T(8,128)(2,1)S(1)}, u32[]{:S(2)}, u32[]{:S(2)}) %collective-permute-start.22) | collective-permute-done | bytes 458784 | tf_op jit(solution)/shard_map/ppermute | solution.py:631
  87.2 0.1 add_convert_fusion.1
  87.3 1.7 %collective-permute-done.23.theirs_ref = bf16[112,2048]{1,0:T(8,128)(2,1)S(1)} collective-permute-done((bf16[112,2048]{1,0:T(8,128)(2,1)S(1)}, bf16[112,2048]{1,0:T(8,128)(2,1)S(1)}, u32[]{:S(2)}, u32[]{:S(2)}) %collective-permute-start.23) | collective-permute-done | bytes 458784 | tf_op jit(solution)/shard_map/ppermute | solution.py:621
  89.0 0.8 collective-permute-start.25
  89.8 2.6 %feed_forward.7 = (bf16[112,2048]{1,0:T(8,128)(2,1)S(1)}, bf16[112,1024]{1,0:T(8,128)(2,1)S(1)}, bf16[112,1024]{1,0:T(8,128)(2,1)S(1)}) custom-call(bf16[112,2048]{1,0:T(8,128)(2,1)S(1)} %collective-permute-done.22.mine_ref, bf16[112,2048]{1,0:T(8,128)(2,1)S(1)} %collective-permute-done.23.theirs_ref, bf16[2048,1024]{1,0:T(8,128)(2,1)S(1)} %copy-done, ...), custom_call_target="tpu_custom_call" | custom-call | flops 1879048192 | bytes 8388608 | tf_op jit(solution)/shard_map/feed_forward/pallas_call | solution.py:597
  92.5 0.5 collective-permute-start.27
  93.0 0.1 collective-permute-start.16
  93.1 0.4 collective-permute-start.15
  93.5 0.5 collective-permute-done.26
  94.0 0.1 collective-permute-start.30
  94.1 3.3 %collective-permute-done.25 = bf16[112,2048]{1,0:T(8,128)(2,1)S(1)} collective-permute-done((bf16[112,2048]{1,0:T(8,128)(2,1)S(1)}, bf16[112,2048]{1,0:T(8,128)(2,1)S(1)}, u32[]{:S(2)}, u32[]{:S(2)}) %collective-permute-start.25) | collective-permute-done | bytes 458784 | tf_op jit(solution)/shard_map/ppermute | solution.py:631
  97.5 0.1 add_convert_fusion
  97.6 0.9 collective-permute-start.28
  98.5 0.2 add_convert_fusion.3
  98.7 1.4 %collective-permute-start.29 = (bf16[112,1024]{1,0:T(8,128)(2,1)S(1)}, bf16[112,1024]{1,0:T(8,128)(2,1)S(1)}, u32[]{:S(2)}, u32[]{:S(2)}) collective-permute-start(bf16[112,1024]{1,0:T(8,128)(2,1)S(1)} %get-tuple-element.113), channel_id=1, source_target_pairs={{0,2},{1,5},{2,0},{3,7},{4,6},{5,1},{6,4},{7,3},{8,10},{9,13},{10,... | collective-permute-start | bytes 688136 | tf_op jit(solution)/shard_map/ppermute | solution.py:631
  100.2 0.7 collective-permute-start.31
  100.8 0.1 add_convert_fusion.2.refs_1_
  101.0 6.0 %collective-permute-done.29.refs_3_ = bf16[112,1024]{1,0:T(8,128)(2,1)S(1)} collective-permute-done((bf16[112,1024]{1,0:T(8,128)(2,1)S(1)}, bf16[112,1024]{1,0:T(8,128)(2,1)S(1)}, u32[]{:S(2)}, u32[]{:S(2)}) %collective-permute-start.29) | collective-permute-done | bytes 229408 | tf_op jit(solution)/shard_map/ppermute | solution.py:631
  106.9 2.5 %collective-permute-done.31.refs_4_ = bf16[112,1024]{1,0:T(8,128)(2,1)S(1)} collective-permute-done((bf16[112,1024]{1,0:T(8,128)(2,1)S(1)}, bf16[112,1024]{1,0:T(8,128)(2,1)S(1)}, u32[]{:S(2)}, u32[]{:S(2)}) %collective-permute-start.31) | collective-permute-done | bytes 229408 | tf_op jit(solution)/shard_map/ppermute | solution.py:631
  109.4 0.8 collective-permute-done.28.refs_2_
  110.2 1.1 finish.1
  (62 shorter events, 0.5 us)
Async XLA Ops:
  0.6 38.9 %collective-permute-start.4 = (bf16[4096,256]{1,0:T(8,128)(2,1)}, bf16[4096,256]{1,0:T(8,128)(2,1)}, u32[]{:S(2)}, u32[]{:S(2)}) collective-permute-start(bf16[4096,256]{1,0:T(8,128)(2,1)} %refs_0_.1), channel_id=1, source_target_pairs={{0,1},{1,0},{2,3},{3,2},{4,5},{5,4},{6,7},{7,6},{8,9},{9,8},{10,11... | collective-permute-start | bytes 6291464 | tf_op jit(solution)/shard_map/ppermute | solution.py:621
  1.1 1.2 %copy-start.4 = (bf16[18,24,1024]{2,1,0:T(8,128)(2,1)S(1)}, bf16[18,24,1024]{2,1,0:T(8,128)(2,1)}, u32[]{:S(2)}) copy-start(bf16[18,24,1024]{2,1,0:T(8,128)(2,1)} %tokens_ref.7) | copy-start | bytes 2654212
  2.3 7.8 %copy-start.5 = (bf16[18,24,1024]{2,1,0:T(8,128)(2,1)S(1)}, bf16[18,24,1024]{2,1,0:T(8,128)(2,1)}, u32[]{:S(2)}) copy-start(bf16[18,24,1024]{2,1,0:T(8,128)(2,1)} %tokens_ref.7) | copy-start | bytes 2654212
  2.4 13.3 %collective-permute-start.1 = (bf16[18,8,1024]{2,1,0:T(8,128)(2,1)S(1)}, bf16[18,8,1024]{2,1,0:T(8,128)(2,1)S(1)}, u32[]{:S(2)}, u32[]{:S(2)}) collective-permute-start(bf16[18,8,1024]{2,1,0:T(8,128)(2,1)S(1)} %get-tuple-element.60), channel_id=1, source_target_pairs={{0,7},{1,0},{2,1},{3,2},{4,3},{5,4},{6,5},{7,6},{8,15},{9,8},{10,9... | collective-permute-start | bytes 884744 | tf_op jit(solution)/shard_map/ppermute | solution.py:461
  6.0 9.9 %collective-permute-start = (bf16[18,8,1024]{2,1,0:T(8,128)(2,1)S(1)}, bf16[18,8,1024]{2,1,0:T(8,128)(2,1)S(1)}, u32[]{:S(2)}, u32[]{:S(2)}) collective-permute-start(bf16[18,8,1024]{2,1,0:T(8,128)(2,1)S(1)} %get-tuple-element.59), channel_id=1, source_target_pairs={{0,1},{1,2},{2,3},{3,4},{4,5},{5,6},{6,7},{7,0},{8,9},{9,10},{10,1... | collective-permute-start | bytes 884744 | tf_op jit(solution)/shard_map/ppermute | solution.py:461
  6.0 1.6 %copy-start.2 = (bf16[4096,256]{1,0:T(8,128)(2,1)S(1)}, bf16[4096,256]{1,0:T(8,128)(2,1)}, u32[]{:S(2)}) copy-start(bf16[4096,256]{1,0:T(8,128)(2,1)} %refs_0_.1) | copy-start | bytes 6291460
  9.1 26.7 %collective-permute-start.5 = (bf16[2048,256]{1,0:T(8,128)(2,1)}, bf16[2048,256]{1,0:T(8,128)(2,1)}, u32[]{:S(2)}, u32[]{:S(2)}) collective-permute-start(bf16[2048,256]{1,0:T(8,128)(2,1)} %get-tuple-element.71), channel_id=1, source_target_pairs={{0,2},{1,3},{2,0},{3,1},{4,6},{5,7},{6,4},{7,5},{8,10},{9,11},{10,... | collective-permute-start | bytes 3145736 | tf_op jit(solution)/shard_map/ppermute | solution.py:626
  9.1 27.5 %collective-permute-start.6 = (bf16[2048,256]{1,0:T(8,128)(2,1)}, bf16[2048,256]{1,0:T(8,128)(2,1)}, u32[]{:S(2)}, u32[]{:S(2)}) collective-permute-start(bf16[2048,256]{1,0:T(8,128)(2,1)} %get-tuple-element.72), channel_id=1, source_target_pairs={{0,4},{1,5},{2,6},{3,7},{4,0},{5,1},{6,2},{7,3},{8,12},{9,13},{10,... | collective-permute-start | bytes 3145736 | tf_op jit(solution)/shard_map/ppermute | solution.py:626
  10.2 10.7 %copy-start.6 = (bf16[1024,1024]{1,0:T(8,128)(2,1)S(1)}, bf16[1024,1024]{1,0:T(8,128)(2,1)}, u32[]{:S(2)}) copy-start(bf16[1024,1024]{1,0:T(8,128)(2,1)} %out_w_ref.3) | copy-start | bytes 6291460
  10.2 10.7 %copy-start.7 = (bf16[576,144]{1,0:T(8,128)(2,1)S(1)}, bf16[576,144]{1,0:T(8,128)(2,1)}, u32[]{:S(2)}) copy-start(bf16[576,144]{1,0:T(8,128)(2,1)} %constant.74.clone.rest_1_) | copy-start | bytes 497668
  10.2 10.7 %copy-start.8 = (bf16[576,256]{1,0:T(8,128)(2,1)S(1)}, bf16[576,256]{1,0:T(8,128)(2,1)}, u32[]{:S(2)}) copy-start(bf16[576,256]{1,0:T(8,128)(2,1)} %constant.75.clone.rest_2_) | copy-start | bytes 884740
  10.3 10.7 %copy-start.9 = (bf16[256,288]{1,0:T(8,128)(2,1)S(1)}, bf16[256,288]{1,0:T(8,128)(2,1)}, u32[]{:S(2)}) copy-start(bf16[256,288]{1,0:T(8,128)(2,1)} %constant.72.clone.patch_ref) | copy-start | bytes 442372
  10.3 10.7 %copy-start.10 = (bf16[144,576]{1,0:T(8,128)(2,1)S(1)}, bf16[144,576]{1,0:T(8,128)(2,1)}, u32[]{:S(2)}) copy-start(bf16[144,576]{1,0:T(8,128)(2,1)} %constant.76.clone.rest_3_) | copy-start | bytes 497668
  10.3 10.7 %copy-start.14 = (bf16[240,240]{1,0:T(8,128)(2,1)S(1)}, bf16[240,240]{1,0:T(8,128)(2,1)}, u32[]{:S(2)}) copy-start(bf16[240,240]{1,0:T(8,128)(2,1)} %constant.73.clone.rest_0_) | copy-start | bytes 345604
  15.9 11.7 %collective-permute-start.2 = (bf16[3,40,1024]{2,1,0:T(8,128)(2,1)S(1)}, bf16[3,40,1024]{2,1,0:T(8,128)(2,1)S(1)}, u32[]{:S(2)}, u32[]{:S(2)}) collective-permute-start(bf16[3,40,1024]{2,1,0:T(8,128)(2,1)S(1)} %pad_maximum_fusion), channel_id=1, source_target_pairs={{0,8},{8,16},{16,24},{1,9},{9,17},{17,25},{2,10},{10,18},{18,26},{... | collective-permute-start | bytes 737288 | tf_op jit(solution)/shard_map/ppermute | solution.py:461
  19.4 10.3 %collective-permute-start.3 = (bf16[3,40,1024]{2,1,0:T(8,128)(2,1)S(1)}, bf16[3,40,1024]{2,1,0:T(8,128)(2,1)S(1)}, u32[]{:S(2)}, u32[]{:S(2)}) collective-permute-start(bf16[3,40,1024]{2,1,0:T(8,128)(2,1)S(1)} %pad_maximum_fusion.1), channel_id=1, source_target_pairs={{8,0},{16,8},{24,16},{9,1},{17,9},{25,17},{10,2},{18,10},{26,18},{... | collective-permute-start | bytes 737288 | tf_op jit(solution)/shard_map/ppermute | solution.py:461
  21.0 8.8 %copy-start.11 = (bf16[304,256]{1,0:T(8,128)(2,1)S(1)}, bf16[304,256]{1,0:T(8,128)(2,1)}, u32[]{:S(2)}) copy-start(bf16[304,256]{1,0:T(8,128)(2,1)} %constant.80.clone.rest_2_.rest_6_) | copy-start | bytes 466948
  21.0 8.8 %copy-start.12 = (bf16[240,256]{1,0:T(8,128)(2,1)S(1)}, bf16[240,256]{1,0:T(8,128)(2,1)}, u32[]{:S(2)}) copy-start(bf16[240,256]{1,0:T(8,128)(2,1)} %constant.78.clone.rest_0_) | copy-start | bytes 368644
  21.0 8.7 %copy-start.13 = (bf16[240,256]{1,0:T(8,128)(2,1)S(1)}, bf16[240,256]{1,0:T(8,128)(2,1)}, u32[]{:S(2)}) copy-start(bf16[240,256]{1,0:T(8,128)(2,1)} %constant.82.clone.rest_4_) | copy-start | bytes 368644
  21.0 8.7 %copy-start.15 = (bf16[192,192]{1,0:T(8,128)(2,1)S(1)}, bf16[192,192]{1,0:T(8,128)(2,1)}, u32[]{:S(2)}) copy-start(bf16[192,192]{1,0:T(8,128)(2,1)} %constant.77.clone.patch_ref) | copy-start | bytes 221188
  21.0 8.7 %copy-start.16 = (bf16[304,80]{1,0:T(8,128)(2,1)S(1)}, bf16[304,80]{1,0:T(8,128)(2,1)}, u32[]{:S(2)}) copy-start(bf16[304,80]{1,0:T(8,128)(2,1)} %constant.79.clone.rest_1_.rest_5_) | copy-start | bytes 145924
  21.0 8.7 %copy-start.17 = (bf16[80,304]{1,0:T(8,128)(2,1)S(1)}, bf16[80,304]{1,0:T(8,128)(2,1)}, u32[]{:S(2)}) copy-start(bf16[80,304]{1,0:T(8,128)(2,1)} %constant.81.clone.rest_3_.rest_7_) | copy-start | bytes 145924
  29.8 11.3 %copy-start.3 = (bf16[4096,256]{1,0:T(8,128)(2,1)S(1)}, bf16[4096,256]{1,0:T(8,128)(2,1)}, u32[]{:S(2)}) copy-start(bf16[4096,256]{1,0:T(8,128)(2,1)} %refs_0_.1) | copy-start | bytes 6291460
  36.6 3.0 %collective-permute-start.7 = (bf16[2048,256]{1,0:T(8,128)(2,1)}, bf16[2048,256]{1,0:T(8,128)(2,1)S(1)}, u32[]{:S(2)}, u32[]{:S(2)}) collective-permute-start(bf16[2048,256]{1,0:T(8,128)(2,1)} %collective-permute-done.5.refs_2_), channel_id=1, source_target_pairs={{0,1},{1,0},{2,3},{3,2},{4,5},{5,4},{6,7},{7,6},{8,9},{9,8},{10,11... | collective-permute-start | bytes 3145736 | tf_op jit(solution)/shard_map/ppermute | solution.py:621
  36.8 4.3 %collective-permute-start.8 = (bf16[2048,256]{1,0:T(8,128)(2,1)}, bf16[2048,256]{1,0:T(8,128)(2,1)}, u32[]{:S(2)}, u32[]{:S(2)}) collective-permute-start(bf16[2048,256]{1,0:T(8,128)(2,1)} %collective-permute-done.6.refs_4_), channel_id=1, source_target_pairs={{0,1},{1,0},{2,3},{3,2},{4,5},{5,4},{6,7},{7,6},{8,9},{9,8},{10,11... | collective-permute-start | bytes 3145736 | tf_op jit(solution)/shard_map/ppermute | solution.py:621
  37.1 12.9 %collective-permute-start.9 = (bf16[112,2048]{1,0:T(8,128)(2,1)}, bf16[112,2048]{1,0:T(8,128)(2,1)}, u32[]{:S(2)}, u32[]{:S(2)}) collective-permute-start(bf16[112,2048]{1,0:T(8,128)(2,1)} %get-tuple-element.68.upper_ref), channel_id=1, source_target_pairs={{0,4},{1,5},{2,6},{3,7},{4,0},{5,1},{6,2},{7,3},{8,12},{9,13},{10,... | collective-permute-start | bytes 1376264 | tf_op jit(solution)/shard_map/ppermute | solution.py:626
  37.3 13.0 %collective-permute-start.10 = (bf16[112,2048]{1,0:T(8,128)(2,1)}, bf16[112,2048]{1,0:T(8,128)(2,1)}, u32[]{:S(2)}, u32[]{:S(2)}) collective-permute-start(bf16[112,2048]{1,0:T(8,128)(2,1)} %get-tuple-element.69.lower_ref), channel_id=1, source_target_pairs={{0,2},{1,3},{2,0},{3,1},{4,6},{5,7},{6,4},{7,5},{8,10},{9,11},{10,... | collective-permute-start | bytes 1376264 | tf_op jit(solution)/shard_map/ppermute | solution.py:626
  50.3 13.2 %copy-start = (bf16[2048,1024]{1,0:T(8,128)(2,1)S(1)}, bf16[2048,1024]{1,0:T(8,128)(2,1)}, u32[]{:S(2)}) copy-start(bf16[2048,1024]{1,0:T(8,128)(2,1)} %up_ref.7) | copy-start | bytes 12582916
  50.3 13.2 %copy-start.1 = (bf16[1024,2048]{1,0:T(8,128)(2,1)S(1)}, bf16[1024,2048]{1,0:T(8,128)(2,1)}, u32[]{:S(2)}) copy-start(bf16[1024,2048]{1,0:T(8,128)(2,1)} %down_ref.7) | copy-start | bytes 12582916
  53.1 6.9 %collective-permute-start.11 = (bf16[112,1024]{1,0:T(8,128)(2,1)S(1)}, bf16[112,1024]{1,0:T(8,128)(2,1)S(1)}, u32[]{:S(2)}, u32[]{:S(2)}) collective-permute-start(bf16[112,1024]{1,0:T(8,128)(2,1)S(1)} %get-tuple-element.84), channel_id=1, source_target_pairs={{0,4},{1,5},{2,6},{3,7},{4,0},{5,1},{6,2},{7,3},{8,12},{9,13},{10,... | collective-permute-start | bytes 688136 | tf_op jit(solution)/shard_map/ppermute | solution.py:626
  54.7 6.3 %collective-permute-start.12 = (bf16[112,1024]{1,0:T(8,128)(2,1)S(1)}, bf16[112,1024]{1,0:T(8,128)(2,1)S(1)}, u32[]{:S(2)}, u32[]{:S(2)}) collective-permute-start(bf16[112,1024]{1,0:T(8,128)(2,1)S(1)} %get-tuple-element.85), channel_id=1, source_target_pairs={{0,2},{1,3},{2,0},{3,1},{4,6},{5,7},{6,4},{7,5},{8,10},{9,11},{10,... | collective-permute-start | bytes 688136 | tf_op jit(solution)/shard_map/ppermute | solution.py:626
  61.6 1.9 %collective-permute-start.14 = (bf16[112,2048]{1,0:T(8,128)(2,1)S(1)}, bf16[112,2048]{1,0:T(8,128)(2,1)S(1)}, u32[]{:S(2)}, u32[]{:S(2)}) collective-permute-start(bf16[112,2048]{1,0:T(8,128)(2,1)S(1)} %combine.1.mine_ref.refs_0_), channel_id=1, source_target_pairs={{0,1},{1,0},{2,3},{3,2},{4,5},{5,4},{6,7},{7,6},{8,9},{9,8},{10,11... | collective-permute-start | bytes 1376264 | tf_op jit(solution)/shard_map/ppermute | solution.py:621
  61.7 8.5 %collective-permute-start.13 = (bf16[112,2048]{1,0:T(8,128)(2,1)S(1)}, bf16[112,2048]{1,0:T(8,128)(2,1)S(1)}, u32[]{:S(2)}, u32[]{:S(2)}) collective-permute-start(bf16[112,2048]{1,0:T(8,128)(2,1)S(1)} %combine.1.mine_ref.refs_0_), channel_id=1, source_target_pairs={{0,2},{1,5},{2,0},{3,7},{4,6},{5,1},{6,4},{7,3},{8,10},{9,13},{10,... | collective-permute-start | bytes 1376264 | tf_op jit(solution)/shard_map/ppermute | solution.py:631
  70.2 1.8 %collective-permute-start.17 = (bf16[112,2048]{1,0:T(8,128)(2,1)S(1)}, bf16[112,2048]{1,0:T(8,128)(2,1)S(1)}, u32[]{:S(2)}, u32[]{:S(2)}) collective-permute-start(bf16[112,2048]{1,0:T(8,128)(2,1)S(1)} %collective-permute-done.13.mine_ref), channel_id=1, source_target_pairs={{0,1},{1,0},{2,3},{3,2},{4,5},{5,4},{6,7},{7,6},{8,9},{9,8},{10,11... | collective-permute-start | bytes 1376264 | tf_op jit(solution)/shard_map/ppermute | solution.py:621
  70.2 8.5 %collective-permute-start.19 = (bf16[112,2048]{1,0:T(8,128)(2,1)S(1)}, bf16[112,2048]{1,0:T(8,128)(2,1)S(1)}, u32[]{:S(2)}, u32[]{:S(2)}) collective-permute-start(bf16[112,2048]{1,0:T(8,128)(2,1)S(1)} %collective-permute-done.13.mine_ref), channel_id=1, source_target_pairs={{0,4},{1,3},{2,6},{3,1},{4,0},{5,7},{6,2},{7,5},{8,12},{9,11},{10,... | collective-permute-start | bytes 1376264 | tf_op jit(solution)/shard_map/ppermute | solution.py:631
  74.6 4.1 %collective-permute-start.18 = (bf16[112,1024]{1,0:T(8,128)(2,1)S(1)}, bf16[112,1024]{1,0:T(8,128)(2,1)S(1)}, u32[]{:S(2)}, u32[]{:S(2)}) collective-permute-start(bf16[112,1024]{1,0:T(8,128)(2,1)S(1)} %get-tuple-element.93), channel_id=1, source_target_pairs={{0,1},{1,0},{2,3},{3,2},{4,5},{5,4},{6,7},{7,6},{8,9},{9,8},{10,11... | collective-permute-start | bytes 688136 | tf_op jit(solution)/shard_map/ppermute | solution.py:621
  78.7 1.8 %collective-permute-start.20 = (bf16[112,2048]{1,0:T(8,128)(2,1)S(1)}, bf16[112,2048]{1,0:T(8,128)(2,1)S(1)}, u32[]{:S(2)}, u32[]{:S(2)}) collective-permute-start(bf16[112,2048]{1,0:T(8,128)(2,1)S(1)} %collective-permute-done.19.mine_ref), channel_id=1, source_target_pairs={{0,1},{1,0},{2,3},{3,2},{4,5},{5,4},{6,7},{7,6},{8,9},{9,8},{10,11... | collective-permute-start | bytes 1376264 | tf_op jit(solution)/shard_map/ppermute | solution.py:621
  78.7 8.5 %collective-permute-start.22 = (bf16[112,2048]{1,0:T(8,128)(2,1)S(1)}, bf16[112,2048]{1,0:T(8,128)(2,1)S(1)}, u32[]{:S(2)}, u32[]{:S(2)}) collective-permute-start(bf16[112,2048]{1,0:T(8,128)(2,1)S(1)} %combine.1.mine_ref.refs_0_), channel_id=1, source_target_pairs={{0,4},{1,3},{2,6},{3,1},{4,0},{5,7},{6,2},{7,5},{8,12},{9,11},{10,... | collective-permute-start | bytes 1376264 | tf_op jit(solution)/shard_map/ppermute | solution.py:631
  83.1 4.1 %collective-permute-start.21 = (bf16[112,1024]{1,0:T(8,128)(2,1)S(1)}, bf16[112,1024]{1,0:T(8,128)(2,1)S(1)}, u32[]{:S(2)}, u32[]{:S(2)}) collective-permute-start(bf16[112,1024]{1,0:T(8,128)(2,1)S(1)} %get-tuple-element.95), channel_id=1, source_target_pairs={{0,1},{1,0},{2,3},{3,2},{4,5},{5,4},{6,7},{7,6},{8,9},{9,8},{10,11... | collective-permute-start | bytes 688136 | tf_op jit(solution)/shard_map/ppermute | solution.py:621
  83.3 3.8 %collective-permute-start.24 = (bf16[112,1024]{1,0:T(8,128)(2,1)S(1)}, bf16[112,1024]{1,0:T(8,128)(2,1)S(1)}, u32[]{:S(2)}, u32[]{:S(2)}) collective-permute-start(bf16[112,1024]{1,0:T(8,128)(2,1)S(1)} %get-tuple-element.101), channel_id=1, source_target_pairs={{0,1},{1,0},{2,3},{3,2},{4,5},{5,4},{6,7},{7,6},{8,9},{9,8},{10,11... | collective-permute-start | bytes 688136 | tf_op jit(solution)/shard_map/ppermute | solution.py:621
  87.2 1.8 %collective-permute-start.23 = (bf16[112,2048]{1,0:T(8,128)(2,1)S(1)}, bf16[112,2048]{1,0:T(8,128)(2,1)S(1)}, u32[]{:S(2)}, u32[]{:S(2)}) collective-permute-start(bf16[112,2048]{1,0:T(8,128)(2,1)S(1)} %collective-permute-done.22.mine_ref), channel_id=1, source_target_pairs={{0,1},{1,0},{2,3},{3,2},{4,5},{5,4},{6,7},{7,6},{8,9},{9,8},{10,11... | collective-permute-start | bytes 1376264 | tf_op jit(solution)/shard_map/ppermute | solution.py:621
  89.0 8.5 %collective-permute-start.25 = (bf16[112,2048]{1,0:T(8,128)(2,1)S(1)}, bf16[112,2048]{1,0:T(8,128)(2,1)S(1)}, u32[]{:S(2)}, u32[]{:S(2)}) collective-permute-start(bf16[112,2048]{1,0:T(8,128)(2,1)S(1)} %add_convert_fusion.1), channel_id=1, source_target_pairs={{0,4},{1,3},{2,6},{3,1},{4,0},{5,7},{6,2},{7,5},{8,12},{9,11},{10,... | collective-permute-start | bytes 1376264 | tf_op jit(solution)/shard_map/ppermute | solution.py:631
  92.5 1.6 %collective-permute-start.26 = (bf16[112,1024]{1,0:T(8,128)(2,1)S(1)}, bf16[112,1024]{1,0:T(8,128)(2,1)S(1)}, u32[]{:S(2)}, u32[]{:S(2)}) collective-permute-start(bf16[112,1024]{1,0:T(8,128)(2,1)S(1)} %get-tuple-element.105), channel_id=1, source_target_pairs={{0,1},{1,0},{2,3},{3,2},{4,5},{5,4},{6,7},{7,6},{8,9},{9,8},{10,11... | collective-permute-start | bytes 688136 | tf_op jit(solution)/shard_map/ppermute | solution.py:621
  92.5 5.0 %collective-permute-start.27 = (bf16[112,1024]{1,0:T(8,128)(2,1)S(1)}, bf16[112,1024]{1,0:T(8,128)(2,1)S(1)}, u32[]{:S(2)}, u32[]{:S(2)}) collective-permute-start(bf16[112,1024]{1,0:T(8,128)(2,1)S(1)} %get-tuple-element.107), channel_id=1, source_target_pairs={{0,1},{1,0},{2,3},{3,2},{4,5},{5,4},{6,7},{7,6},{8,9},{9,8},{10,11... | collective-permute-start | bytes 688136 | tf_op jit(solution)/shard_map/ppermute | solution.py:621
  93.0 7.8 %collective-permute-start.16 = (bf16[112,1024]{1,0:T(8,128)(2,1)S(1)}, bf16[112,1024]{1,0:T(8,128)(2,1)S(1)}, u32[]{:S(2)}, u32[]{:S(2)}) collective-permute-start(bf16[112,1024]{1,0:T(8,128)(2,1)S(1)} %get-tuple-element.91), channel_id=1, source_target_pairs={{0,1},{1,0},{2,3},{3,2},{4,5},{5,4},{6,7},{7,6},{8,9},{9,8},{10,11... | collective-permute-start | bytes 688136 | tf_op jit(solution)/shard_map/ppermute | solution.py:621
  93.1 7.7 %collective-permute-start.15 = (bf16[112,1024]{1,0:T(8,128)(2,1)S(1)}, bf16[112,1024]{1,0:T(8,128)(2,1)S(1)}, u32[]{:S(2)}, u32[]{:S(2)}) collective-permute-start(bf16[112,1024]{1,0:T(8,128)(2,1)S(1)} %get-tuple-element.90), channel_id=1, source_target_pairs={{0,1},{1,0},{2,3},{3,2},{4,5},{5,4},{6,7},{7,6},{8,9},{9,8},{10,11... | collective-permute-start | bytes 688136 | tf_op jit(solution)/shard_map/ppermute | solution.py:621
  94.0 4.5 %collective-permute-start.30 = (bf16[112,1024]{1,0:T(8,128)(2,1)S(1)}, bf16[112,1024]{1,0:T(8,128)(2,1)S(1)}, u32[]{:S(2)}, u32[]{:S(2)}) collective-permute-start(bf16[112,1024]{1,0:T(8,128)(2,1)S(1)} %get-tuple-element.111), channel_id=1, source_target_pairs={{0,1},{1,0},{2,3},{3,2},{4,5},{5,4},{6,7},{7,6},{8,9},{9,8},{10,11... | collective-permute-start | bytes 688136 | tf_op jit(solution)/shard_map/ppermute | solution.py:621
  97.6 12.6 %collective-permute-start.28 = (bf16[112,2048]{1,0:T(8,128)(2,1)S(1)}, bf16[112,2048]{1,0:T(8,128)(2,1)S(1)}, u32[]{:S(2)}, u32[]{:S(2)}) collective-permute-start(bf16[112,2048]{1,0:T(8,128)(2,1)S(1)} %add_convert_fusion), channel_id=1, source_target_pairs={{0,4},{1,3},{2,6},{3,1},{4,0},{5,7},{6,2},{7,5},{8,12},{9,11},{10,... | collective-permute-start | bytes 1376264 | tf_op jit(solution)/shard_map/ppermute | solution.py:631
  98.7 8.2 %collective-permute-start.29 = (bf16[112,1024]{1,0:T(8,128)(2,1)S(1)}, bf16[112,1024]{1,0:T(8,128)(2,1)S(1)}, u32[]{:S(2)}, u32[]{:S(2)}) collective-permute-start(bf16[112,1024]{1,0:T(8,128)(2,1)S(1)} %get-tuple-element.113), channel_id=1, source_target_pairs={{0,2},{1,5},{2,0},{3,7},{4,6},{5,1},{6,4},{7,3},{8,10},{9,13},{10,... | collective-permute-start | bytes 688136 | tf_op jit(solution)/shard_map/ppermute | solution.py:631
  100.2 9.2 %collective-permute-start.31 = (bf16[112,1024]{1,0:T(8,128)(2,1)S(1)}, bf16[112,1024]{1,0:T(8,128)(2,1)S(1)}, u32[]{:S(2)}, u32[]{:S(2)}) collective-permute-start(bf16[112,1024]{1,0:T(8,128)(2,1)S(1)} %get-tuple-element.112), channel_id=1, source_target_pairs={{0,2},{1,5},{2,0},{3,7},{4,6},{5,1},{6,4},{7,3},{8,10},{9,13},{10,... | collective-permute-start | bytes 688136 | tf_op jit(solution)/shard_map/ppermute | solution.py:631

commit v15 on v13

--- a/solution.py
+++ b/solution.py
@@ -317,7 +317,7 @@
     ]
 
 
-def merge_rows(patch_ref, cells, upper_ref, lower_ref, first):
+def merge_rows(patch_ref, cells, upper_ref, lower_ref):
     width = cells.shape[1]
     padded = patch_ref.shape[0] // 4
     parts = [dot(patch_ref[k * padded : (k + 1) * padded, :], cells) for k in range(4)]
@@ -328,7 +328,7 @@
     factor = lax.rsqrt(spread * (1.0 / (4 * width)) + 1e-05)
     for k in range(4):
         ref = (upper_ref, lower_ref)[k // 2]
-        ref[first : first + padded, k % 2 * width : (k % 2 + 1) * width] = (parts[k] * factor).astype(BF16)
+        ref[:, k % 2 * width : (k % 2 + 1) * width] = (parts[k] * factor).astype(BF16)
 
 
 def middle_kernel(bands, some, kinds, tokens_ref, west_ref, east_ref, own_ref, weight_ref, out_w_ref, patch_ref, *rest):
@@ -354,10 +354,10 @@
     mixed = dot(attended_ref[...], out_w_ref[...])
     middle = tokens_ref[RIM_LAT : rows - RIM_LAT].astype(F32) + mixed.reshape(-1, columns, width)
     middle_ref[...] = middle.astype(BF16)
-    merge_rows(patch_ref, middle.reshape(-1, width).astype(BF16), upper_ref, lower_ref, 0)
-
-
-def edge_kernel(bands, some, kinds, tokens_ref, north_ref, south_ref, bias_ref, own_ref, side_ref, inner_ref, inner_upper_ref, inner_lower_ref, weight_ref, out_w_ref, patch_ref, *rest):
+    merge_rows(patch_ref, middle.reshape(-1, width).astype(BF16), upper_ref, lower_ref)
+
+
+def edge_kernel(bands, some, kinds, tokens_ref, north_ref, south_ref, bias_ref, own_ref, side_ref, inner_ref, weight_ref, out_w_ref, patch_ref, *rest):
     consts, rest = rest[:-11], rest[-11:]
     middle_ref, upper_ref, lower_ref, normed_ref, slab_ref, attended_ref, *scratch = rest
     rows, columns, width = tokens_ref.shape
@@ -387,10 +387,7 @@
     middle_ref[rows - RIM_LAT :] = bottom.astype(BF16)
     first, last = inner_ref[0].astype(F32), inner_ref[rows - 2 * RIM_LAT - 1].astype(F32)
     cells = jnp.concatenate([top.reshape(-1, width), first, last, bottom.reshape(-1, width)], axis=0)
-    inner_count = inner_upper_ref.shape[0]
-    upper_ref[:inner_count, :] = inner_upper_ref[...]
-    lower_ref[:inner_count, :] = inner_lower_ref[...]
-    merge_rows(patch_ref, cells.astype(BF16), upper_ref, lower_ref, inner_count)
+    merge_rows(patch_ref, cells.astype(BF16), upper_ref, lower_ref)
 
 
 def vmem_call(kernel, out, args, scratch, flops, name, mib=24, exps=0):
@@ -444,11 +441,11 @@
     )
     kinds, consts = bands.constants(edges, block)
     patch = bands.edge_patch_matrix()
-    count = inner_count + patch.shape[0] // 4
-    return vmem_call(
+    count = patch.shape[0] // 4
+    middle_out, upper_edge, lower_edge = vmem_call(
         functools.partial(edge_kernel, bands, edges, kinds),
         [tokens.shape, (count, 2 * width), (count, 2 * width)],
-        [tokens, north, south, key_bias(), own, side, middle, upper, lower, kv_weight, out_weight, patch] + consts,
+        [tokens, north, south, key_bias(), own, side, middle, kv_weight, out_weight, patch] + consts,
         [
             pltpu.VMEM((2 * bands.slab_padded, width), BF16),
             pltpu.VMEM((2 * bands.slab_padded, 2 * width), BF16),
@@ -459,6 +456,7 @@
         "edge_attention",
         exps=300000,
     )
+    return middle_out, [upper, upper_edge], [lower, lower_edge]
 
 
 def shift(part, axis, step, wrap):
@@ -492,7 +490,12 @@
         y(at[k], dot(lower, ref[...]))
 
 
-def merge_own_kernel(place_ref, upper_ref, lower_ref, *refs):
+def stacked(refs):
+    return jnp.concatenate([ref[...] for ref in refs], axis=0)
+
+
+def merge_own_kernel(place_ref, *refs):
+    rows, refs = refs[:4], refs[4:]
     weights, (own_ref, x_ref, y_ref), kept = refs[:6], refs[6:9], refs[9:]
     for ref, to in zip(weights, kept):
         to[...] = ref[...]
@@ -506,10 +509,11 @@
     def y(at, b):
         y_ref[:, at] = b
 
-    merge_dots(place_ref, upper_ref[...], lower_ref[...], *weights, (own, x, y))
-
-
-def merge_other_kernel(place_ref, upper_ref, lower_ref, *refs):
+    merge_dots(place_ref, stacked(rows[:2]), stacked(rows[2:]), *weights, (own, x, y))
+
+
+def merge_other_kernel(place_ref, *refs):
+    rows, refs = refs[:4], refs[4:]
     weights, (to_y_ref, to_x_ref) = refs[:6], refs[6:]
     wide = to_x_ref.shape[1] // 2
 
@@ -523,7 +527,7 @@
     def y(at, b):
         to_x_ref[:, pl.ds(pl.multiple_of(wide + at.start, at.size), at.size)] = b.astype(BF16)
 
-    merge_dots(place_ref, upper_ref[...], lower_ref[...], *weights, (own, x, y))
+    merge_dots(place_ref, stacked(rows[:2]), stacked(rows[2:]), *weights, (own, x, y))
 
 
 def combine_kernel(place_ref, own_ref, x_ref, y_ref, from_y_ref, from_x_ref, out_ref):
@@ -556,23 +560,23 @@
 def merge_by_squares(upper, lower, merge_weight, halves):
     half = merge_weight.shape[0] // 2
     block = merge_weight.shape[1]
-    count = upper.shape[0]
+    count = sum(part.shape[0] for part in upper)
     x = chip_swap(halves[0], 1)
     y = chip_swap(halves[1], 2)
-    x_pair, y_pair, _ = lax.optimization_barrier((x, y, upper))
+    from_y = [chip_swap(part, 2) for part in upper]
+    from_x = [chip_swap(part, 1) for part in lower]
+    x_pair, y_pair, from_y[0], from_x[0], _ = lax.optimization_barrier((x, y, from_y[0], from_x[0], upper[1]))
     weights = [merge_weight, core_swap(merge_weight), x, core_swap(x_pair), y, core_swap(y_pair)]
     place = place_index()
-    from_y = chip_swap(upper, 2)
-    from_x = chip_swap(lower, 1)
     flops = 16 * count * half * block
     wide = jax.ShapeDtypeStruct((count, 2 * block), F32)
     kept = [jax.ShapeDtypeStruct(w.shape, BF16) for w in weights]
     *own, a, b, c, d, e, f = local_call(
-        merge_own_kernel, [wide] * 3 + kept, place, [upper, lower] + weights, flops, "merge_own", 28
+        merge_own_kernel, [wide] * 3 + kept, place, [*upper, *lower] + weights, flops, "merge_own", 28
     )
     weights = [a, b, c, d, e, f]
     pair = jax.ShapeDtypeStruct((count, 4 * block), BF16)
-    to_y, to_x = local_call(merge_other_kernel, [pair] * 2, place, [from_y, from_x] + weights, flops, "merge_other")
+    to_y, to_x = local_call(merge_other_kernel, [pair] * 2, place, [*from_y, *from_x] + weights, flops, "merge_other")
     back_y, back_x = chip_swap(to_y, 2), chip_swap(to_x, 1)
     out = jax.ShapeDtypeStruct((count, 8 * block), BF16)
     return local_call(combine_kernel, [out], place, [*own, back_y, back_x], 0, "combine")[0]
@@ -666,7 +670,7 @@
 
 def coarse_by_chips(upper, lower, merge_weight, halves, up, down):
     weight = lax.all_gather(merge_weight, "lon", axis=1, tiled=True)
-    patches = jnp.concatenate([upper, lower], axis=1)
+    patches = jnp.concatenate([jnp.concatenate(upper, axis=0), jnp.concatenate(lower, axis=0)], axis=1)
     coarse = jnp.dot(patches, weight, preferred_element_type=F32).astype(BF16)
     chips = lax.axis_size("lon") // 2
     arrived = [coarse] + [chip_swap(coarse, m) for m in range(1, chips)]

time: 111 us -> 116 us (1.045)
  starting transfers between devices: 23.7 us -> 28 us
  local copies, waits for them, and re-layouts: 1.3 us -> 5.51 us
  waiting for transfers between devices: 44.1 us -> 41.8 us
  Pallas kernels: 40.3 us -> 38.9 us
    unnamed x34 -> x54, local copies, waits for them, and re-layouts: 1.27 us -> 5.48 us
    ppermute x7, starting transfers between devices: 6.35 us -> 10.3 us  [cross(): lax.ppermute(value, 'lon', [(i, i ^ 2 * (second if i % 2 else first)) for...]
    ppermute x15, waiting for transfers between devices: 6.72 us -> 5.09 us  [core_swap(): return lax.ppermute(value, 'lon', [(i, i ^ 1) for i in range(size)])]
    ppermute x6 -> x8, waiting for transfers between devices: 10.8 us -> 11.7 us  [chip_swap(): lax.ppermute(value, 'lon', [(i, i ^ 2 * offset) for i in range(size)])]
    ppermute x6 -> x8, starting transfers between devices: 5.64 us -> 6.03 us  [chip_swap(): lax.ppermute(value, 'lon', [(i, i ^ 2 * offset) for i in range(size)])]
  transfers between devices with their start and end apart: 32 -> 34, of which waited for: 20 -> 19; matrix products, arithmetic and copies ran while one was open for 1% -> 1% of each run, Pallas kernels for 32% -> 30%
where the time goes in v15:
time: 116 us
  waiting for transfers between devices  41.8 us (36%)
  Pallas kernels  38.9 us (34%)
  starting transfers between devices  28 us (24%)
  local copies, waits for them, and re-layouts  5.51 us (5%)
    ppermute x7, waiting for transfers between devices, cross(): lax.ppermute(value, 'lon', [(i, i ^ 2 * (second if i % 2 else first)) for...  23 us
    pallas_call x2, Pallas kernels, vmem_call(): pl.pallas_call(kernel, in_specs=[vmem] * len(args), out_specs=[vmem] * le...  12.1 us
    ppermute x8, waiting for transfers between devices, chip_swap(): lax.ppermute(value, 'lon', [(i, i ^ 2 * offset) for i in range(size)])  11.7 us
    pallas_call x4, Pallas kernels, feed_forward(): pl.pallas_call(ffn_kernel, in_specs=[vmem] * 4, out_specs=[vmem] * 3, out...  10.4 us
    ppermute x7, starting transfers between devices, cross(): lax.ppermute(value, 'lon', [(i, i ^ 2 * (second if i % 2 else first)) for...  10.3 us
    ppermute x4, starting transfers between devices, shift(): return lax.ppermute(part, axis, pairs)  8.58 us
    pallas_call x3, Pallas kernels, local_call(): pl.pallas_call(kernel, in_specs=[pl.BlockSpec(memory_space=pltpu.SMEM)] +...  7.13 us
    ppermute x8, starting transfers between devices, chip_swap(): lax.ppermute(value, 'lon', [(i, i ^ 2 * offset) for i in range(size)])  6.03 us
  transfers between devices with their start and end apart: 34, of which 19 were waited for; matrix products, arithmetic and copies ran while one was open for 1% of the time, Pallas kernels for 30%

profile of v15, /device:TPU:0, one launch (start us, length us, event | category | flops | bytes accessed | tf_op | source)
XLA Modules:
  0.0 116.2 jit_solution(12338264014376529937)
XLA Ops:
  0.6 0.5 collective-permute-start.4
  1.1 1.2 %copy-done.3 = bf16[18,24,1024]{2,1,0:T(8,128)(2,1)S(1)} copy-done((bf16[18,24,1024]{2,1,0:T(8,128)(2,1)S(1)}, bf16[18,24,1024]{2,1,0:T(8,128)(2,1)}, u32[]{:S(2)}) %copy-start.3) | copy-done | bytes 884760
  2.4 3.6 %collective-permute-start.1 = (bf16[18,8,1024]{2,1,0:T(8,128)(2,1)S(1)}, bf16[18,8,1024]{2,1,0:T(8,128)(2,1)S(1)}, u32[]{:S(2)}, u32[]{:S(2)}) collective-permute-start(bf16[18,8,1024]{2,1,0:T(8,128)(2,1)S(1)} %get-tuple-element.62), channel_id=1, source_target_pairs={{0,7},{1,0},{2,1},{3,2},{4,3},{5,4},{6,5},{7,6},{8,15},{9,8},{10,9... | collective-permute-start | bytes 884744 | tf_op jit(solution)/shard_map/ppermute | solution.py:465
  6.0 2.9 %halves.1 = (bf16[2048,256]{1,0:T(8,128)(2,1)}, bf16[2048,256]{1,0:T(8,128)(2,1)}) custom-call(bf16[4096,256]{1,0:T(8,128)(2,1)} %refs_4_.1), custom_call_target="tpu_custom_call" | custom-call | tf_op jit(solution)/shard_map/halves/pallas_call | solution.py:202
  9.0 1.1 collective-permute-start.6
  10.2 5.2 %own_projection.1 = (bf16[448,3072]{1,0:T(8,128)(2,1)S(1)}, bf16[1024,2048]{1,0:T(8,128)(2,1)S(1)}) custom-call(bf16[18,24,1024]{2,1,0:T(8,128)(2,1)S(1)} %copy-done.4, bf16[1024,3072]{1,0:T(8,128)(2,1)} %weight_ref.1), custom_call_target="tpu_custom_call" | custom-call | flops 2818572288 | bytes 6291456 | tf_op jit(solution)/shard_map/own_projection/pallas_call | solution.py:242
  15.6 0.4 collective-permute-done.west_ref
  16.0 3.5 %collective-permute-start.2 = (bf16[3,40,1024]{2,1,0:T(8,128)(2,1)S(1)}, bf16[3,40,1024]{2,1,0:T(8,128)(2,1)S(1)}, u32[]{:S(2)}, u32[]{:S(2)}) collective-permute-start(bf16[3,40,1024]{2,1,0:T(8,128)(2,1)S(1)} %pad_maximum_fusion), channel_id=1, source_target_pairs={{0,8},{8,16},{16,24},{1,9},{9,17},{17,25},{2,10},{10,18},{18,26},{... | collective-permute-start | bytes 737288 | tf_op jit(solution)/shard_map/ppermute | solution.py:465
  19.5 1.5 %collective-permute-start.3 = (bf16[3,40,1024]{2,1,0:T(8,128)(2,1)S(1)}, bf16[3,40,1024]{2,1,0:T(8,128)(2,1)S(1)}, u32[]{:S(2)}, u32[]{:S(2)}) collective-permute-start(bf16[3,40,1024]{2,1,0:T(8,128)(2,1)S(1)} %pad_maximum_fusion.1), channel_id=1, source_target_pairs={{8,0},{16,8},{24,16},{9,1},{17,9},{25,17},{10,2},{18,10},{26,18},{... | collective-permute-start | bytes 737288 | tf_op jit(solution)/shard_map/ppermute | solution.py:465
  21.2 6.5 %middle_attention.1 = (bf16[288,2048]{1,0:T(8,128)(2,1)S(1)}, bf16[12,24,1024]{2,1,0:T(8,128)(2,1)S(1)}, bf16[64,2048]{1,0:T(8,128)(2,1)S(1)}, bf16[64,2048]{1,0:T(8,128)(2,1)S(1)}) custom-call(bf16[18,24,1024]{2,1,0:T(8,128)(2,1)S(1)} %copy-done.4, bf16[18,8,1024]{2,1,0:T(8,128)(2,1)S(1)} %collective-permute-done.west_ref, ...), custom_call_target="tpu_custom_call" | custom-call | flops 5000000000 | bytes 1048576 | tf_op jit(solution)/shard_map/middle_attention/pallas_call | solution.py:395
  27.7 0.7 collective-permute-start.7
  28.4 1.6 %collective-permute-done.3.south_ref = bf16[3,40,1024]{2,1,0:T(8,128)(2,1)S(1)} collective-permute-done((bf16[3,40,1024]{2,1,0:T(8,128)(2,1)S(1)}, bf16[3,40,1024]{2,1,0:T(8,128)(2,1)S(1)}, u32[]{:S(2)}, u32[]{:S(2)}) %collective-permute-start.3) | collective-permute-done | bytes 245792 | tf_op jit(solution)/shard_map/ppermute | solution.py:465
  30.0 0.9 collective-permute-start.8
  31.0 5.6 %edge_attention.1 = (bf16[18,24,1024]{2,1,0:T(8,128)(2,1)}, bf16[48,2048]{1,0:T(8,128)(2,1)S(1)}, bf16[48,2048]{1,0:T(8,128)(2,1)S(1)}) custom-call(bf16[18,24,1024]{2,1,0:T(8,128)(2,1)S(1)} %copy-done.4, bf16[3,40,1024]{2,1,0:T(8,128)(2,1)S(1)} %collective-permute-done.2.north_ref, bf16[3,40,1024]{2,1,0:T(8,128)(2,1)S(1)} %collective-permute-done.3.south_ref, ...), custom_call_target="tpu_custom_call" | custom-call | flops 6000000000 | bytes 1048576 | tf_op jit(solution)/shard_map/edge_attention/pallas_call | solution.py:395
  36.5 5.6 %collective-permute-done.7.refs_0_ = bf16[64,2048]{1,0:T(8,128)(2,1)S(1)} collective-permute-done((bf16[64,2048]{1,0:T(8,128)(2,1)S(1)}, bf16[64,2048]{1,0:T(8,128)(2,1)S(1)}, u32[]{:S(2)}, u32[]{:S(2)}) %collective-permute-start.7) | collective-permute-done | bytes 262176 | tf_op jit(solution)/shard_map/ppermute | solution.py:636
  42.1 0.7 copy-done.7
  42.8 0.7 copy-done.9
  43.6 0.2 collective-permute-start.9
  43.8 0.3 collective-permute-start.10
  44.1 1.7 %collective-permute-start.12 = (bf16[48,2048]{1,0:T(8,128)(2,1)}, bf16[48,2048]{1,0:T(8,128)(2,1)S(1)}, u32[]{:S(2)}, u32[]{:S(2)}) collective-permute-start(bf16[48,2048]{1,0:T(8,128)(2,1)} %copy-done.11), channel_id=1, source_target_pairs={{0,2},{1,3},{2,0},{3,1},{4,6},{5,7},{6,4},{7,5},{8,10},{9,11},{10,... | collective-permute-start | bytes 589832 | tf_op jit(solution)/shard_map/ppermute | solution.py:636
  45.9 0.6 collective-permute-done.9.refs_7_
  46.5 1.6 %collective-permute-done.10.refs_9_ = bf16[2048,256]{1,0:T(8,128)(2,1)} collective-permute-done((bf16[2048,256]{1,0:T(8,128)(2,1)}, bf16[2048,256]{1,0:T(8,128)(2,1)}, u32[]{:S(2)}, u32[]{:S(2)}) %collective-permute-start.10) | collective-permute-done | bytes 1048608 | tf_op jit(solution)/shard_map/ppermute | solution.py:631
  48.1 0.9 copy-done.6
  49.1 0.9 copy-done.12
  50.0 0.9 copy-done.14
  50.9 4.6 %merge_own.1 = (f32[112,512]{1,0:T(8,128)S(1)}, f32[112,512]{1,0:T(8,128)S(1)}, f32[112,512]{1,0:T(8,128)S(1)}, bf16[4096,256]{1,0:T(8,128)(2,1)S(1)}, bf16[4096...) custom-call(s32[2]{0:T(128)S(1)} %pad_add_fusion.place_ref, ...), custom_call_target="tpu_custom_call" | custom-call | flops 939524096 | bytes 1048576 | tf_op jit(solution)/shard_map/merge_own/pallas_call | solution.py:549
  55.6 1.9 %merge_other.1 = (bf16[112,1024]{1,0:T(8,128)(2,1)S(1)}, bf16[112,1024]{1,0:T(8,128)(2,1)S(1)}) custom-call(s32[2]{0:T(128)S(1)} %pad_add_fusion.place_ref, bf16[64,2048]{1,0:T(8,128)(2,1)S(1)} %copy-done.8, bf16[48,2048]{1,0:T(8,128)(2,1)S(1)} %collective-permute-done.11.refs_1_, bf16[64,2048]{1,0:T(8,128)(2,1)S(1)} %copy-done.10, ...), custom_call_target="tpu_custom_call" | custom-call | flops 939524096 | bytes 1048576 | tf_op jit(solution)/shard_map/merge_other/pallas_call | solution.py:549
  57.6 1.6 %collective-permute-start.14 = (bf16[112,1024]{1,0:T(8,128)(2,1)S(1)}, bf16[112,1024]{1,0:T(8,128)(2,1)S(1)}, u32[]{:S(2)}, u32[]{:S(2)}) collective-permute-start(bf16[112,1024]{1,0:T(8,128)(2,1)S(1)} %get-tuple-element.89), channel_id=1, source_target_pairs={{0,2},{1,3},{2,0},{3,1},{4,6},{5,7},{6,4},{7,5},{8,10},{9,11},{10,... | collective-permute-start | bytes 688136 | tf_op jit(solution)/shard_map/ppermute | solution.py:636
  59.2 6.0 %collective-permute-done.13.from_y_ref = bf16[112,1024]{1,0:T(8,128)(2,1)S(1)} collective-permute-done((bf16[112,1024]{1,0:T(8,128)(2,1)S(1)}, bf16[112,1024]{1,0:T(8,128)(2,1)S(1)}, u32[]{:S(2)}, u32[]{:S(2)}) %collective-permute-start.13) | collective-permute-done | bytes 229408 | tf_op jit(solution)/shard_map/ppermute | solution.py:636
  65.3 0.6 combine.1.mine_ref.refs_0_
  66.0 1.4 %collective-permute-start.15 = (bf16[112,2048]{1,0:T(8,128)(2,1)S(1)}, bf16[112,2048]{1,0:T(8,128)(2,1)S(1)}, u32[]{:S(2)}, u32[]{:S(2)}) collective-permute-start(bf16[112,2048]{1,0:T(8,128)(2,1)S(1)} %combine.1.mine_ref.refs_0_), channel_id=1, source_target_pairs={{0,2},{1,5},{2,0},{3,7},{4,6},{5,1},{6,4},{7,3},{8,10},{9,13},{10,... | collective-permute-start | bytes 1376264 | tf_op jit(solution)/shard_map/ppermute | solution.py:641
  67.4 0.4 collective-permute-done.16.theirs_ref
  67.8 2.6 %feed_forward.4 = (bf16[112,2048]{1,0:T(8,128)(2,1)S(1)}, bf16[112,1024]{1,0:T(8,128)(2,1)S(1)}, bf16[112,1024]{1,0:T(8,128)(2,1)S(1)}) custom-call(bf16[112,2048]{1,0:T(8,128)(2,1)S(1)} %combine.1.mine_ref.refs_0_, bf16[112,2048]{1,0:T(8,128)(2,1)S(1)} %collective-permute-done.16.theirs_ref, bf16[2048,1024]{1,0:T(8,128)(2,1)S(1)} %copy-done, ...), custom_call_target="tpu_custom_call" | custom-call | flops 1879048192 | bytes 8388608 | tf_op jit(solution)/shard_map/feed_forward/pallas_call | solution.py:607
  70.4 4.1 %collective-permute-done.15.mine_ref = bf16[112,2048]{1,0:T(8,128)(2,1)S(1)} collective-permute-done((bf16[112,2048]{1,0:T(8,128)(2,1)S(1)}, bf16[112,2048]{1,0:T(8,128)(2,1)S(1)}, u32[]{:S(2)}, u32[]{:S(2)}) %collective-permute-start.15) | collective-permute-done | bytes 458784 | tf_op jit(solution)/shard_map/ppermute | solution.py:641
  74.5 1.7 %collective-permute-start.21 = (bf16[112,2048]{1,0:T(8,128)(2,1)S(1)}, bf16[112,2048]{1,0:T(8,128)(2,1)S(1)}, u32[]{:S(2)}, u32[]{:S(2)}) collective-permute-start(bf16[112,2048]{1,0:T(8,128)(2,1)S(1)} %collective-permute-done.15.mine_ref), channel_id=1, source_target_pairs={{0,4},{1,3},{2,6},{3,1},{4,0},{5,7},{6,2},{7,5},{8,12},{9,11},{10,... | collective-permute-start | bytes 1376264 | tf_op jit(solution)/shard_map/ppermute | solution.py:641
  76.2 0.1 collective-permute-done.19.theirs_ref
  76.3 2.6 %feed_forward.5 = (bf16[112,2048]{1,0:T(8,128)(2,1)S(1)}, bf16[112,1024]{1,0:T(8,128)(2,1)S(1)}, bf16[112,1024]{1,0:T(8,128)(2,1)S(1)}) custom-call(bf16[112,2048]{1,0:T(8,128)(2,1)S(1)} %collective-permute-done.15.mine_ref, bf16[112,2048]{1,0:T(8,128)(2,1)S(1)} %collective-permute-done.19.theirs_ref, bf16[2048,1024]{1,0:T(8,128)(2,1)S(1)} %copy-done, ...), custom_call_target="tpu_custom_call" | custom-call | flops 1879048192 | bytes 8388608 | tf_op jit(solution)/shard_map/feed_forward/pallas_call | solution.py:607
  79.0 0.2 collective-permute-start.20
  79.1 3.9 %collective-permute-done.21.mine_ref = bf16[112,2048]{1,0:T(8,128)(2,1)S(1)} collective-permute-done((bf16[112,2048]{1,0:T(8,128)(2,1)S(1)}, bf16[112,2048]{1,0:T(8,128)(2,1)S(1)}, u32[]{:S(2)}, u32[]{:S(2)}) %collective-permute-start.21) | collective-permute-done | bytes 458784 | tf_op jit(solution)/shard_map/ppermute | solution.py:641
  83.0 1.7 %collective-permute-start.24 = (bf16[112,2048]{1,0:T(8,128)(2,1)S(1)}, bf16[112,2048]{1,0:T(8,128)(2,1)S(1)}, u32[]{:S(2)}, u32[]{:S(2)}) collective-permute-start(bf16[112,2048]{1,0:T(8,128)(2,1)S(1)} %combine.1.mine_ref.refs_0_), channel_id=1, source_target_pairs={{0,4},{1,3},{2,6},{3,1},{4,0},{5,7},{6,2},{7,5},{8,12},{9,11},{10,... | collective-permute-start | bytes 1376264 | tf_op jit(solution)/shard_map/ppermute | solution.py:641
  84.7 0.1 collective-permute-done.22.theirs_ref
  84.8 2.6 %feed_forward.6 = (bf16[112,2048]{1,0:T(8,128)(2,1)S(1)}, bf16[112,1024]{1,0:T(8,128)(2,1)S(1)}, bf16[112,1024]{1,0:T(8,128)(2,1)S(1)}) custom-call(bf16[112,2048]{1,0:T(8,128)(2,1)S(1)} %collective-permute-done.21.mine_ref, bf16[112,2048]{1,0:T(8,128)(2,1)S(1)} %collective-permute-done.22.theirs_ref, bf16[2048,1024]{1,0:T(8,128)(2,1)S(1)} %copy-done, ...), custom_call_target="tpu_custom_call" | custom-call | flops 1879048192 | bytes 8388608 | tf_op jit(solution)/shard_map/feed_forward/pallas_call | solution.py:607
  87.4 0.2 collective-permute-start.23
  87.6 0.4 collective-permute-start.26
  88.0 3.5 %collective-permute-done.24.mine_ref = bf16[112,2048]{1,0:T(8,128)(2,1)S(1)} collective-permute-done((bf16[112,2048]{1,0:T(8,128)(2,1)S(1)}, bf16[112,2048]{1,0:T(8,128)(2,1)S(1)}, u32[]{:S(2)}, u32[]{:S(2)}) %collective-permute-start.24) | collective-permute-done | bytes 458784 | tf_op jit(solution)/shard_map/ppermute | solution.py:641
  91.5 0.1 add_convert_fusion.1
  91.6 1.7 %collective-permute-done.25.theirs_ref = bf16[112,2048]{1,0:T(8,128)(2,1)S(1)} collective-permute-done((bf16[112,2048]{1,0:T(8,128)(2,1)S(1)}, bf16[112,2048]{1,0:T(8,128)(2,1)S(1)}, u32[]{:S(2)}, u32[]{:S(2)}) %collective-permute-start.25) | collective-permute-done | bytes 458784 | tf_op jit(solution)/shard_map/ppermute | solution.py:631
  93.3 1.7 %collective-permute-start.27 = (bf16[112,2048]{1,0:T(8,128)(2,1)S(1)}, bf16[112,2048]{1,0:T(8,128)(2,1)S(1)}, u32[]{:S(2)}, u32[]{:S(2)}) collective-permute-start(bf16[112,2048]{1,0:T(8,128)(2,1)S(1)} %add_convert_fusion.1), channel_id=1, source_target_pairs={{0,4},{1,3},{2,6},{3,1},{4,0},{5,7},{6,2},{7,5},{8,12},{9,11},{10,... | collective-permute-start | bytes 1376264 | tf_op jit(solution)/shard_map/ppermute | solution.py:641
  95.0 2.6 %feed_forward.7 = (bf16[112,2048]{1,0:T(8,128)(2,1)S(1)}, bf16[112,1024]{1,0:T(8,128)(2,1)S(1)}, bf16[112,1024]{1,0:T(8,128)(2,1)S(1)}) custom-call(bf16[112,2048]{1,0:T(8,128)(2,1)S(1)} %collective-permute-done.24.mine_ref, bf16[112,2048]{1,0:T(8,128)(2,1)S(1)} %collective-permute-done.25.theirs_ref, bf16[2048,1024]{1,0:T(8,128)(2,1)S(1)} %copy-done, ...), custom_call_target="tpu_custom_call" | custom-call | flops 1879048192 | bytes 8388608 | tf_op jit(solution)/shard_map/feed_forward/pallas_call | solution.py:607
  97.7 0.5 collective-permute-start.29
  98.2 0.4 collective-permute-start.17
  98.7 0.5 collective-permute-done.28
  99.1 0.1 collective-permute-start.32
  99.3 2.5 %collective-permute-done.27 = bf16[112,2048]{1,0:T(8,128)(2,1)S(1)} collective-permute-done((bf16[112,2048]{1,0:T(8,128)(2,1)S(1)}, bf16[112,2048]{1,0:T(8,128)(2,1)S(1)}, u32[]{:S(2)}, u32[]{:S(2)}) %collective-permute-start.27) | collective-permute-done | bytes 458784 | tf_op jit(solution)/shard_map/ppermute | solution.py:641
  101.8 0.1 add_convert_fusion
  101.9 1.7 %collective-permute-start.30 = (bf16[112,2048]{1,0:T(8,128)(2,1)S(1)}, bf16[112,2048]{1,0:T(8,128)(2,1)S(1)}, u32[]{:S(2)}, u32[]{:S(2)}) collective-permute-start(bf16[112,2048]{1,0:T(8,128)(2,1)S(1)} %add_convert_fusion), channel_id=1, source_target_pairs={{0,4},{1,3},{2,6},{3,1},{4,0},{5,7},{6,2},{7,5},{8,12},{9,11},{10,... | collective-permute-start | bytes 1376264 | tf_op jit(solution)/shard_map/ppermute | solution.py:641
  103.6 0.2 add_convert_fusion.3
  103.9 0.9 collective-permute-start.31
  104.8 1.2 %collective-permute-start.33 = (bf16[112,1024]{1,0:T(8,128)(2,1)S(1)}, bf16[112,1024]{1,0:T(8,128)(2,1)S(1)}, u32[]{:S(2)}, u32[]{:S(2)}) collective-permute-start(bf16[112,1024]{1,0:T(8,128)(2,1)S(1)} %get-tuple-element.116), channel_id=1, source_target_pairs={{0,2},{1,5},{2,0},{3,7},{4,6},{5,1},{6,4},{7,3},{8,10},{9,13},{10,... | collective-permute-start | bytes 688136 | tf_op jit(solution)/shard_map/ppermute | solution.py:641
  106.0 0.1 add_convert_fusion.2.refs_1_
  106.1 5.1 %collective-permute-done.31.refs_3_ = bf16[112,1024]{1,0:T(8,128)(2,1)S(1)} collective-permute-done((bf16[112,1024]{1,0:T(8,128)(2,1)S(1)}, bf16[112,1024]{1,0:T(8,128)(2,1)S(1)}, u32[]{:S(2)}, u32[]{:S(2)}) %collective-permute-start.31) | collective-permute-done | bytes 229408 | tf_op jit(solution)/shard_map/ppermute | solution.py:641
  111.2 2.5 %collective-permute-done.33.refs_4_ = bf16[112,1024]{1,0:T(8,128)(2,1)S(1)} collective-permute-done((bf16[112,1024]{1,0:T(8,128)(2,1)S(1)}, bf16[112,1024]{1,0:T(8,128)(2,1)S(1)}, u32[]{:S(2)}, u32[]{:S(2)}) %collective-permute-start.33) | collective-permute-done | bytes 229408 | tf_op jit(solution)/shard_map/ppermute | solution.py:641
  113.7 1.4 %collective-permute-done.30.refs_2_ = bf16[112,2048]{1,0:T(8,128)(2,1)S(1)} collective-permute-done((bf16[112,2048]{1,0:T(8,128)(2,1)S(1)}, bf16[112,2048]{1,0:T(8,128)(2,1)S(1)}, u32[]{:S(2)}, u32[]{:S(2)}) %collective-permute-start.30) | collective-permute-done | bytes 458784 | tf_op jit(solution)/shard_map/ppermute | solution.py:641
  115.1 1.1 finish.1
  (84 shorter events, 0.9 us)
Async XLA Ops:
  0.6 45.2 %collective-permute-start.4 = (bf16[4096,256]{1,0:T(8,128)(2,1)}, bf16[4096,256]{1,0:T(8,128)(2,1)}, u32[]{:S(2)}, u32[]{:S(2)}) collective-permute-start(bf16[4096,256]{1,0:T(8,128)(2,1)} %refs_4_.1), channel_id=1, source_target_pairs={{0,1},{1,0},{2,3},{3,2},{4,5},{5,4},{6,7},{7,6},{8,9},{9,8},{10,11... | collective-permute-start | bytes 6291464 | tf_op jit(solution)/shard_map/ppermute | solution.py:631
  1.1 1.2 %copy-start.3 = (bf16[18,24,1024]{2,1,0:T(8,128)(2,1)S(1)}, bf16[18,24,1024]{2,1,0:T(8,128)(2,1)}, u32[]{:S(2)}) copy-start(bf16[18,24,1024]{2,1,0:T(8,128)(2,1)} %tokens_ref.7) | copy-start | bytes 2654212
  2.3 7.7 %copy-start.4 = (bf16[18,24,1024]{2,1,0:T(8,128)(2,1)S(1)}, bf16[18,24,1024]{2,1,0:T(8,128)(2,1)}, u32[]{:S(2)}) copy-start(bf16[18,24,1024]{2,1,0:T(8,128)(2,1)} %tokens_ref.7) | copy-start | bytes 2654212
  2.4 13.2 %collective-permute-start.1 = (bf16[18,8,1024]{2,1,0:T(8,128)(2,1)S(1)}, bf16[18,8,1024]{2,1,0:T(8,128)(2,1)S(1)}, u32[]{:S(2)}, u32[]{:S(2)}) collective-permute-start(bf16[18,8,1024]{2,1,0:T(8,128)(2,1)S(1)} %get-tuple-element.62), channel_id=1, source_target_pairs={{0,7},{1,0},{2,1},{3,2},{4,3},{5,4},{6,5},{7,6},{8,15},{9,8},{10,9... | collective-permute-start | bytes 884744 | tf_op jit(solution)/shard_map/ppermute | solution.py:465
  6.0 10.0 %collective-permute-start = (bf16[18,8,1024]{2,1,0:T(8,128)(2,1)S(1)}, bf16[18,8,1024]{2,1,0:T(8,128)(2,1)S(1)}, u32[]{:S(2)}, u32[]{:S(2)}) collective-permute-start(bf16[18,8,1024]{2,1,0:T(8,128)(2,1)S(1)} %get-tuple-element.61), channel_id=1, source_target_pairs={{0,1},{1,2},{2,3},{3,4},{4,5},{5,6},{6,7},{7,0},{8,9},{9,10},{10,1... | collective-permute-start | bytes 884744 | tf_op jit(solution)/shard_map/ppermute | solution.py:465
  8.9 34.6 %collective-permute-start.5 = (bf16[2048,256]{1,0:T(8,128)(2,1)}, bf16[2048,256]{1,0:T(8,128)(2,1)}, u32[]{:S(2)}, u32[]{:S(2)}) collective-permute-start(bf16[2048,256]{1,0:T(8,128)(2,1)} %get-tuple-element.73), channel_id=1, source_target_pairs={{0,2},{1,3},{2,0},{3,1},{4,6},{5,7},{6,4},{7,5},{8,10},{9,11},{10,... | collective-permute-start | bytes 3145736 | tf_op jit(solution)/shard_map/ppermute | solution.py:636
  9.0 34.6 %collective-permute-start.6 = (bf16[2048,256]{1,0:T(8,128)(2,1)}, bf16[2048,256]{1,0:T(8,128)(2,1)}, u32[]{:S(2)}, u32[]{:S(2)}) collective-permute-start(bf16[2048,256]{1,0:T(8,128)(2,1)} %get-tuple-element.74), channel_id=1, source_target_pairs={{0,4},{1,5},{2,6},{3,7},{4,0},{5,1},{6,2},{7,3},{8,12},{9,13},{10,... | collective-permute-start | bytes 3145736 | tf_op jit(solution)/shard_map/ppermute | solution.py:636
  10.1 10.9 %copy-start.15 = (bf16[1024,1024]{1,0:T(8,128)(2,1)S(1)}, bf16[1024,1024]{1,0:T(8,128)(2,1)}, u32[]{:S(2)}) copy-start(bf16[1024,1024]{1,0:T(8,128)(2,1)} %out_w_ref.3) | copy-start | bytes 6291460
  10.1 10.9 %copy-start.16 = (bf16[576,144]{1,0:T(8,128)(2,1)S(1)}, bf16[576,144]{1,0:T(8,128)(2,1)}, u32[]{:S(2)}) copy-start(bf16[576,144]{1,0:T(8,128)(2,1)} %constant.74.clone.rest_1_) | copy-start | bytes 497668
  10.1 10.9 %copy-start.17 = (bf16[576,256]{1,0:T(8,128)(2,1)S(1)}, bf16[576,256]{1,0:T(8,128)(2,1)}, u32[]{:S(2)}) copy-start(bf16[576,256]{1,0:T(8,128)(2,1)} %constant.75.clone.rest_2_) | copy-start | bytes 884740
  10.1 10.9 %copy-start.18 = (bf16[256,288]{1,0:T(8,128)(2,1)S(1)}, bf16[256,288]{1,0:T(8,128)(2,1)}, u32[]{:S(2)}) copy-start(bf16[256,288]{1,0:T(8,128)(2,1)} %constant.72.clone.patch_ref) | copy-start | bytes 442372
  10.2 10.9 %copy-start.19 = (bf16[144,576]{1,0:T(8,128)(2,1)S(1)}, bf16[144,576]{1,0:T(8,128)(2,1)}, u32[]{:S(2)}) copy-start(bf16[144,576]{1,0:T(8,128)(2,1)} %constant.76.clone.rest_3_) | copy-start | bytes 497668
  10.2 10.9 %copy-start.23 = (bf16[240,240]{1,0:T(8,128)(2,1)S(1)}, bf16[240,240]{1,0:T(8,128)(2,1)}, u32[]{:S(2)}) copy-start(bf16[240,240]{1,0:T(8,128)(2,1)} %constant.73.clone.rest_0_) | copy-start | bytes 345604
  16.0 11.7 %collective-permute-start.2 = (bf16[3,40,1024]{2,1,0:T(8,128)(2,1)S(1)}, bf16[3,40,1024]{2,1,0:T(8,128)(2,1)S(1)}, u32[]{:S(2)}, u32[]{:S(2)}) collective-permute-start(bf16[3,40,1024]{2,1,0:T(8,128)(2,1)S(1)} %pad_maximum_fusion), channel_id=1, source_target_pairs={{0,8},{8,16},{16,24},{1,9},{9,17},{17,25},{2,10},{10,18},{18,26},{... | collective-permute-start | bytes 737288 | tf_op jit(solution)/shard_map/ppermute | solution.py:465
  19.5 10.4 %collective-permute-start.3 = (bf16[3,40,1024]{2,1,0:T(8,128)(2,1)S(1)}, bf16[3,40,1024]{2,1,0:T(8,128)(2,1)S(1)}, u32[]{:S(2)}, u32[]{:S(2)}) collective-permute-start(bf16[3,40,1024]{2,1,0:T(8,128)(2,1)S(1)} %pad_maximum_fusion.1), channel_id=1, source_target_pairs={{8,0},{16,8},{24,16},{9,1},{17,9},{25,17},{10,2},{18,10},{26,18},{... | collective-permute-start | bytes 737288 | tf_op jit(solution)/shard_map/ppermute | solution.py:465
  21.1 9.8 %copy-start.20 = (bf16[304,256]{1,0:T(8,128)(2,1)S(1)}, bf16[304,256]{1,0:T(8,128)(2,1)}, u32[]{:S(2)}) copy-start(bf16[304,256]{1,0:T(8,128)(2,1)} %constant.80.clone.rest_2_.rest_6_) | copy-start | bytes 466948
  21.1 9.8 %copy-start.21 = (bf16[240,256]{1,0:T(8,128)(2,1)S(1)}, bf16[240,256]{1,0:T(8,128)(2,1)}, u32[]{:S(2)}) copy-start(bf16[240,256]{1,0:T(8,128)(2,1)} %constant.78.clone.rest_0_) | copy-start | bytes 368644
  21.1 9.8 %copy-start.22 = (bf16[240,256]{1,0:T(8,128)(2,1)S(1)}, bf16[240,256]{1,0:T(8,128)(2,1)}, u32[]{:S(2)}) copy-start(bf16[240,256]{1,0:T(8,128)(2,1)} %constant.82.clone.rest_4_) | copy-start | bytes 368644
  21.1 9.8 %copy-start.24 = (bf16[192,192]{1,0:T(8,128)(2,1)S(1)}, bf16[192,192]{1,0:T(8,128)(2,1)}, u32[]{:S(2)}) copy-start(bf16[192,192]{1,0:T(8,128)(2,1)} %constant.77.clone.patch_ref) | copy-start | bytes 221188
  21.1 9.8 %copy-start.25 = (bf16[304,80]{1,0:T(8,128)(2,1)S(1)}, bf16[304,80]{1,0:T(8,128)(2,1)}, u32[]{:S(2)}) copy-start(bf16[304,80]{1,0:T(8,128)(2,1)} %constant.79.clone.rest_1_.rest_5_) | copy-start | bytes 145924
  21.2 9.8 %copy-start.26 = (bf16[80,304]{1,0:T(8,128)(2,1)S(1)}, bf16[80,304]{1,0:T(8,128)(2,1)}, u32[]{:S(2)}) copy-start(bf16[80,304]{1,0:T(8,128)(2,1)} %constant.81.clone.rest_3_.rest_7_) | copy-start | bytes 145924
  27.7 8.8 %copy-start.5 = (bf16[64,2048]{1,0:T(8,128)(2,1)}, bf16[64,2048]{1,0:T(8,128)(2,1)S(1)}, u32[]{:S(2)}) copy-start(bf16[64,2048]{1,0:T(8,128)(2,1)S(1)} %get-tuple-element.70.refs_2_) | copy-start | bytes 786436
  27.7 14.4 %collective-permute-start.7 = (bf16[64,2048]{1,0:T(8,128)(2,1)S(1)}, bf16[64,2048]{1,0:T(8,128)(2,1)S(1)}, u32[]{:S(2)}, u32[]{:S(2)}) collective-permute-start(bf16[64,2048]{1,0:T(8,128)(2,1)S(1)} %get-tuple-element.68.refs_0_), channel_id=1, source_target_pairs={{0,4},{1,5},{2,6},{3,7},{4,0},{5,1},{6,2},{7,3},{8,12},{9,13},{10,... | collective-permute-start | bytes 786440 | tf_op jit(solution)/shard_map/ppermute | solution.py:636
  30.0 12.8 %collective-permute-start.8 = (bf16[64,2048]{1,0:T(8,128)(2,1)S(1)}, bf16[64,2048]{1,0:T(8,128)(2,1)S(1)}, u32[]{:S(2)}, u32[]{:S(2)}) collective-permute-start(bf16[64,2048]{1,0:T(8,128)(2,1)S(1)} %get-tuple-element.70.refs_2_), channel_id=1, source_target_pairs={{0,2},{1,3},{2,0},{3,1},{4,6},{5,7},{6,4},{7,5},{8,10},{9,11},{10,... | collective-permute-start | bytes 786440 | tf_op jit(solution)/shard_map/ppermute | solution.py:636
  30.9 17.2 %copy-start.2 = (bf16[4096,256]{1,0:T(8,128)(2,1)S(1)}, bf16[4096,256]{1,0:T(8,128)(2,1)}, u32[]{:S(2)}) copy-start(bf16[4096,256]{1,0:T(8,128)(2,1)} %refs_4_.1) | copy-start | bytes 6291460
  36.5 7.0 %copy-start.11 = (bf16[48,2048]{1,0:T(8,128)(2,1)}, bf16[48,2048]{1,0:T(8,128)(2,1)S(1)}, u32[]{:S(2)}) copy-start(bf16[48,2048]{1,0:T(8,128)(2,1)S(1)} %get-tuple-element.71.refs_3_) | copy-start | bytes 589828
  36.5 7.0 %copy-start.13 = (bf16[48,2048]{1,0:T(8,128)(2,1)}, bf16[48,2048]{1,0:T(8,128)(2,1)S(1)}, u32[]{:S(2)}) copy-start(bf16[48,2048]{1,0:T(8,128)(2,1)S(1)} %get-tuple-element.69.refs_1_) | copy-start | bytes 589828
  42.1 0.7 copy-start.7
  42.8 0.7 copy-start.9
  43.6 2.9 %collective-permute-start.9 = (bf16[2048,256]{1,0:T(8,128)(2,1)}, bf16[2048,256]{1,0:T(8,128)(2,1)S(1)}, u32[]{:S(2)}, u32[]{:S(2)}) collective-permute-start(bf16[2048,256]{1,0:T(8,128)(2,1)} %collective-permute-done.5.refs_6_), channel_id=1, source_target_pairs={{0,1},{1,0},{2,3},{3,2},{4,5},{5,4},{6,7},{7,6},{8,9},{9,8},{10,11... | collective-permute-start | bytes 3145736 | tf_op jit(solution)/shard_map/ppermute | solution.py:631
  43.8 4.3 %collective-permute-start.10 = (bf16[2048,256]{1,0:T(8,128)(2,1)}, bf16[2048,256]{1,0:T(8,128)(2,1)}, u32[]{:S(2)}, u32[]{:S(2)}) collective-permute-start(bf16[2048,256]{1,0:T(8,128)(2,1)} %collective-permute-done.6.refs_8_), channel_id=1, source_target_pairs={{0,1},{1,0},{2,3},{3,2},{4,5},{5,4},{6,7},{7,6},{8,9},{9,8},{10,11... | collective-permute-start | bytes 3145736 | tf_op jit(solution)/shard_map/ppermute | solution.py:631
  44.1 11.4 %collective-permute-start.11 = (bf16[48,2048]{1,0:T(8,128)(2,1)}, bf16[48,2048]{1,0:T(8,128)(2,1)S(1)}, u32[]{:S(2)}, u32[]{:S(2)}) collective-permute-start(bf16[48,2048]{1,0:T(8,128)(2,1)} %copy-done.13), channel_id=1, source_target_pairs={{0,4},{1,5},{2,6},{3,7},{4,0},{5,1},{6,2},{7,3},{8,12},{9,13},{10,... | collective-permute-start | bytes 589832 | tf_op jit(solution)/shard_map/ppermute | solution.py:636
  44.1 11.4 %collective-permute-start.12 = (bf16[48,2048]{1,0:T(8,128)(2,1)}, bf16[48,2048]{1,0:T(8,128)(2,1)S(1)}, u32[]{:S(2)}, u32[]{:S(2)}) collective-permute-start(bf16[48,2048]{1,0:T(8,128)(2,1)} %copy-done.11), channel_id=1, source_target_pairs={{0,2},{1,3},{2,0},{3,1},{4,6},{5,7},{6,4},{7,5},{8,10},{9,11},{10,... | collective-permute-start | bytes 589832 | tf_op jit(solution)/shard_map/ppermute | solution.py:636
  48.1 1.0 copy-start.6
  49.1 0.9 copy-start.12
  50.0 0.9 copy-start.14
  50.9 4.6 %copy-start.8 = (bf16[64,2048]{1,0:T(8,128)(2,1)S(1)}, bf16[64,2048]{1,0:T(8,128)(2,1)}, u32[]{:S(2)}) copy-start(bf16[64,2048]{1,0:T(8,128)(2,1)} %copy-done.7) | copy-start | bytes 786436
  50.9 4.6 %copy-start.10 = (bf16[64,2048]{1,0:T(8,128)(2,1)S(1)}, bf16[64,2048]{1,0:T(8,128)(2,1)}, u32[]{:S(2)}) copy-start(bf16[64,2048]{1,0:T(8,128)(2,1)} %copy-done.9) | copy-start | bytes 786436
  55.6 12.2 %copy-start = (bf16[2048,1024]{1,0:T(8,128)(2,1)S(1)}, bf16[2048,1024]{1,0:T(8,128)(2,1)}, u32[]{:S(2)}) copy-start(bf16[2048,1024]{1,0:T(8,128)(2,1)} %up_ref.7) | copy-start | bytes 12582916
  55.6 12.2 %copy-start.1 = (bf16[1024,2048]{1,0:T(8,128)(2,1)S(1)}, bf16[1024,2048]{1,0:T(8,128)(2,1)}, u32[]{:S(2)}) copy-start(bf16[1024,2048]{1,0:T(8,128)(2,1)} %down_ref.7) | copy-start | bytes 12582916
  57.5 7.7 %collective-permute-start.13 = (bf16[112,1024]{1,0:T(8,128)(2,1)S(1)}, bf16[112,1024]{1,0:T(8,128)(2,1)S(1)}, u32[]{:S(2)}, u32[]{:S(2)}) collective-permute-start(bf16[112,1024]{1,0:T(8,128)(2,1)S(1)} %get-tuple-element.88), channel_id=1, source_target_pairs={{0,4},{1,5},{2,6},{3,7},{4,0},{5,1},{6,2},{7,3},{8,12},{9,13},{10,... | collective-permute-start | bytes 688136 | tf_op jit(solution)/shard_map/ppermute | solution.py:636
  57.6 7.7 %collective-permute-start.14 = (bf16[112,1024]{1,0:T(8,128)(2,1)S(1)}, bf16[112,1024]{1,0:T(8,128)(2,1)S(1)}, u32[]{:S(2)}, u32[]{:S(2)}) collective-permute-start(bf16[112,1024]{1,0:T(8,128)(2,1)S(1)} %get-tuple-element.89), channel_id=1, source_target_pairs={{0,2},{1,3},{2,0},{3,1},{4,6},{5,7},{6,4},{7,5},{8,10},{9,11},{10,... | collective-permute-start | bytes 688136 | tf_op jit(solution)/shard_map/ppermute | solution.py:636
  65.9 1.9 %collective-permute-start.16 = (bf16[112,2048]{1,0:T(8,128)(2,1)S(1)}, bf16[112,2048]{1,0:T(8,128)(2,1)S(1)}, u32[]{:S(2)}, u32[]{:S(2)}) collective-permute-start(bf16[112,2048]{1,0:T(8,128)(2,1)S(1)} %combine.1.mine_ref.refs_0_), channel_id=1, source_target_pairs={{0,1},{1,0},{2,3},{3,2},{4,5},{5,4},{6,7},{7,6},{8,9},{9,8},{10,11... | collective-permute-start | bytes 1376264 | tf_op jit(solution)/shard_map/ppermute | solution.py:631
  66.0 8.5 %collective-permute-start.15 = (bf16[112,2048]{1,0:T(8,128)(2,1)S(1)}, bf16[112,2048]{1,0:T(8,128)(2,1)S(1)}, u32[]{:S(2)}, u32[]{:S(2)}) collective-permute-start(bf16[112,2048]{1,0:T(8,128)(2,1)S(1)} %combine.1.mine_ref.refs_0_), channel_id=1, source_target_pairs={{0,2},{1,5},{2,0},{3,7},{4,6},{5,1},{6,4},{7,3},{8,10},{9,13},{10,... | collective-permute-start | bytes 1376264 | tf_op jit(solution)/shard_map/ppermute | solution.py:641
  74.5 1.8 %collective-permute-start.19 = (bf16[112,2048]{1,0:T(8,128)(2,1)S(1)}, bf16[112,2048]{1,0:T(8,128)(2,1)S(1)}, u32[]{:S(2)}, u32[]{:S(2)}) collective-permute-start(bf16[112,2048]{1,0:T(8,128)(2,1)S(1)} %collective-permute-done.15.mine_ref), channel_id=1, source_target_pairs={{0,1},{1,0},{2,3},{3,2},{4,5},{5,4},{6,7},{7,6},{8,9},{9,8},{10,11... | collective-permute-start | bytes 1376264 | tf_op jit(solution)/shard_map/ppermute | solution.py:631
  74.5 8.5 %collective-permute-start.21 = (bf16[112,2048]{1,0:T(8,128)(2,1)S(1)}, bf16[112,2048]{1,0:T(8,128)(2,1)S(1)}, u32[]{:S(2)}, u32[]{:S(2)}) collective-permute-start(bf16[112,2048]{1,0:T(8,128)(2,1)S(1)} %collective-permute-done.15.mine_ref), channel_id=1, source_target_pairs={{0,4},{1,3},{2,6},{3,1},{4,0},{5,7},{6,2},{7,5},{8,12},{9,11},{10,... | collective-permute-start | bytes 1376264 | tf_op jit(solution)/shard_map/ppermute | solution.py:641
  79.0 4.0 %collective-permute-start.20 = (bf16[112,1024]{1,0:T(8,128)(2,1)S(1)}, bf16[112,1024]{1,0:T(8,128)(2,1)S(1)}, u32[]{:S(2)}, u32[]{:S(2)}) collective-permute-start(bf16[112,1024]{1,0:T(8,128)(2,1)S(1)} %get-tuple-element.97), channel_id=1, source_target_pairs={{0,1},{1,0},{2,3},{3,2},{4,5},{5,4},{6,7},{7,6},{8,9},{9,8},{10,11... | collective-permute-start | bytes 688136 | tf_op jit(solution)/shard_map/ppermute | solution.py:631
  83.0 1.8 %collective-permute-start.22 = (bf16[112,2048]{1,0:T(8,128)(2,1)S(1)}, bf16[112,2048]{1,0:T(8,128)(2,1)S(1)}, u32[]{:S(2)}, u32[]{:S(2)}) collective-permute-start(bf16[112,2048]{1,0:T(8,128)(2,1)S(1)} %collective-permute-done.21.mine_ref), channel_id=1, source_target_pairs={{0,1},{1,0},{2,3},{3,2},{4,5},{5,4},{6,7},{7,6},{8,9},{9,8},{10,11... | collective-permute-start | bytes 1376264 | tf_op jit(solution)/shard_map/ppermute | solution.py:631
  83.0 8.5 %collective-permute-start.24 = (bf16[112,2048]{1,0:T(8,128)(2,1)S(1)}, bf16[112,2048]{1,0:T(8,128)(2,1)S(1)}, u32[]{:S(2)}, u32[]{:S(2)}) collective-permute-start(bf16[112,2048]{1,0:T(8,128)(2,1)S(1)} %combine.1.mine_ref.refs_0_), channel_id=1, source_target_pairs={{0,4},{1,3},{2,6},{3,1},{4,0},{5,7},{6,2},{7,5},{8,12},{9,11},{10,... | collective-permute-start | bytes 1376264 | tf_op jit(solution)/shard_map/ppermute | solution.py:641
  87.4 4.0 %collective-permute-start.23 = (bf16[112,1024]{1,0:T(8,128)(2,1)S(1)}, bf16[112,1024]{1,0:T(8,128)(2,1)S(1)}, u32[]{:S(2)}, u32[]{:S(2)}) collective-permute-start(bf16[112,1024]{1,0:T(8,128)(2,1)S(1)} %get-tuple-element.99), channel_id=1, source_target_pairs={{0,1},{1,0},{2,3},{3,2},{4,5},{5,4},{6,7},{7,6},{8,9},{9,8},{10,11... | collective-permute-start | bytes 688136 | tf_op jit(solution)/shard_map/ppermute | solution.py:631
  87.6 3.9 %collective-permute-start.26 = (bf16[112,1024]{1,0:T(8,128)(2,1)S(1)}, bf16[112,1024]{1,0:T(8,128)(2,1)S(1)}, u32[]{:S(2)}, u32[]{:S(2)}) collective-permute-start(bf16[112,1024]{1,0:T(8,128)(2,1)S(1)} %get-tuple-element.105), channel_id=1, source_target_pairs={{0,1},{1,0},{2,3},{3,2},{4,5},{5,4},{6,7},{7,6},{8,9},{9,8},{10,11... | collective-permute-start | bytes 688136 | tf_op jit(solution)/shard_map/ppermute | solution.py:631
  91.5 1.8 %collective-permute-start.25 = (bf16[112,2048]{1,0:T(8,128)(2,1)S(1)}, bf16[112,2048]{1,0:T(8,128)(2,1)S(1)}, u32[]{:S(2)}, u32[]{:S(2)}) collective-permute-start(bf16[112,2048]{1,0:T(8,128)(2,1)S(1)} %collective-permute-done.24.mine_ref), channel_id=1, source_target_pairs={{0,1},{1,0},{2,3},{3,2},{4,5},{5,4},{6,7},{7,6},{8,9},{9,8},{10,11... | collective-permute-start | bytes 1376264 | tf_op jit(solution)/shard_map/ppermute | solution.py:631
  93.3 8.5 %collective-permute-start.27 = (bf16[112,2048]{1,0:T(8,128)(2,1)S(1)}, bf16[112,2048]{1,0:T(8,128)(2,1)S(1)}, u32[]{:S(2)}, u32[]{:S(2)}) collective-permute-start(bf16[112,2048]{1,0:T(8,128)(2,1)S(1)} %add_convert_fusion.1), channel_id=1, source_target_pairs={{0,4},{1,3},{2,6},{3,1},{4,0},{5,7},{6,2},{7,5},{8,12},{9,11},{10,... | collective-permute-start | bytes 1376264 | tf_op jit(solution)/shard_map/ppermute | solution.py:641
  97.6 1.6 %collective-permute-start.28 = (bf16[112,1024]{1,0:T(8,128)(2,1)S(1)}, bf16[112,1024]{1,0:T(8,128)(2,1)S(1)}, u32[]{:S(2)}, u32[]{:S(2)}) collective-permute-start(bf16[112,1024]{1,0:T(8,128)(2,1)S(1)} %get-tuple-element.109), channel_id=1, source_target_pairs={{0,1},{1,0},{2,3},{3,2},{4,5},{5,4},{6,7},{7,6},{8,9},{9,8},{10,11... | collective-permute-start | bytes 688136 | tf_op jit(solution)/shard_map/ppermute | solution.py:631
  97.7 4.1 %collective-permute-start.29 = (bf16[112,1024]{1,0:T(8,128)(2,1)S(1)}, bf16[112,1024]{1,0:T(8,128)(2,1)S(1)}, u32[]{:S(2)}, u32[]{:S(2)}) collective-permute-start(bf16[112,1024]{1,0:T(8,128)(2,1)S(1)} %get-tuple-element.111), channel_id=1, source_target_pairs={{0,1},{1,0},{2,3},{3,2},{4,5},{5,4},{6,7},{7,6},{8,9},{9,8},{10,11... | collective-permute-start | bytes 688136 | tf_op jit(solution)/shard_map/ppermute | solution.py:631
  98.2 7.8 %collective-permute-start.18 = (bf16[112,1024]{1,0:T(8,128)(2,1)S(1)}, bf16[112,1024]{1,0:T(8,128)(2,1)S(1)}, u32[]{:S(2)}, u32[]{:S(2)}) collective-permute-start(bf16[112,1024]{1,0:T(8,128)(2,1)S(1)} %get-tuple-element.95), channel_id=1, source_target_pairs={{0,1},{1,0},{2,3},{3,2},{4,5},{5,4},{6,7},{7,6},{8,9},{9,8},{10,11... | collective-permute-start | bytes 688136 | tf_op jit(solution)/shard_map/ppermute | solution.py:631
  98.2 7.8 %collective-permute-start.17 = (bf16[112,1024]{1,0:T(8,128)(2,1)S(1)}, bf16[112,1024]{1,0:T(8,128)(2,1)S(1)}, u32[]{:S(2)}, u32[]{:S(2)}) collective-permute-start(bf16[112,1024]{1,0:T(8,128)(2,1)S(1)} %get-tuple-element.94), channel_id=1, source_target_pairs={{0,1},{1,0},{2,3},{3,2},{4,5},{5,4},{6,7},{7,6},{8,9},{9,8},{10,11... | collective-permute-start | bytes 688136 | tf_op jit(solution)/shard_map/ppermute | solution.py:631
  99.1 4.5 %collective-permute-start.32 = (bf16[112,1024]{1,0:T(8,128)(2,1)S(1)}, bf16[112,1024]{1,0:T(8,128)(2,1)S(1)}, u32[]{:S(2)}, u32[]{:S(2)}) collective-permute-start(bf16[112,1024]{1,0:T(8,128)(2,1)S(1)} %get-tuple-element.115), channel_id=1, source_target_pairs={{0,1},{1,0},{2,3},{3,2},{4,5},{5,4},{6,7},{7,6},{8,9},{9,8},{10,11... | collective-permute-start | bytes 688136 | tf_op jit(solution)/shard_map/ppermute | solution.py:631
  101.9 13.2 %collective-permute-start.30 = (bf16[112,2048]{1,0:T(8,128)(2,1)S(1)}, bf16[112,2048]{1,0:T(8,128)(2,1)S(1)}, u32[]{:S(2)}, u32[]{:S(2)}) collective-permute-start(bf16[112,2048]{1,0:T(8,128)(2,1)S(1)} %add_convert_fusion), channel_id=1, source_target_pairs={{0,4},{1,3},{2,6},{3,1},{4,0},{5,7},{6,2},{7,5},{8,12},{9,11},{10,... | collective-permute-start | bytes 1376264 | tf_op jit(solution)/shard_map/ppermute | solution.py:641
  103.9 7.3 %collective-permute-start.31 = (bf16[112,1024]{1,0:T(8,128)(2,1)S(1)}, bf16[112,1024]{1,0:T(8,128)(2,1)S(1)}, u32[]{:S(2)}, u32[]{:S(2)}) collective-permute-start(bf16[112,1024]{1,0:T(8,128)(2,1)S(1)} %get-tuple-element.117), channel_id=1, source_target_pairs={{0,2},{1,5},{2,0},{3,7},{4,6},{5,1},{6,4},{7,3},{8,10},{9,13},{10,... | collective-permute-start | bytes 688136 | tf_op jit(solution)/shard_map/ppermute | solution.py:641
  104.8 8.9 %collective-permute-start.33 = (bf16[112,1024]{1,0:T(8,128)(2,1)S(1)}, bf16[112,1024]{1,0:T(8,128)(2,1)S(1)}, u32[]{:S(2)}, u32[]{:S(2)}) collective-permute-start(bf16[112,1024]{1,0:T(8,128)(2,1)S(1)} %get-tuple-element.116), channel_id=1, source_target_pairs={{0,2},{1,5},{2,0},{3,7},{4,6},{5,1},{6,4},{7,3},{8,10},{9,13},{10,... | collective-permute-start | bytes 688136 | tf_op jit(solution)/shard_map/ppermute | solution.py:641

commit v16 on v13

--- a/solution.py
+++ b/solution.py
@@ -540,7 +540,7 @@
         out_ref[:, pl.ds(pl.multiple_of((chip ^ m) * wide, wide), wide)] = part.astype(BF16)
 
 
-def local_call(kernel, out, place, args, flops, name, mib=16):
+def local_call(kernel, out, place, args, flops, name, mib=12):
     vmem = pl.BlockSpec(memory_space=pltpu.VMEM)
     return pl.pallas_call(
         kernel,
@@ -568,7 +568,7 @@
     wide = jax.ShapeDtypeStruct((count, 2 * block), F32)
     kept = [jax.ShapeDtypeStruct(w.shape, BF16) for w in weights]
     *own, a, b, c, d, e, f = local_call(
-        merge_own_kernel, [wide] * 3 + kept, place, [upper, lower] + weights, flops, "merge_own", 28
+        merge_own_kernel, [wide] * 3 + kept, place, [upper, lower] + weights, flops, "merge_own", 20
     )
     weights = [a, b, c, d, e, f]
     pair = jax.ShapeDtypeStruct((count, 4 * block), BF16)

time: 111 us -> 112 us (level)
  no operation moved by 1% of the time
where the time goes in v16:
time: 112 us; the launch traced here: 111 us
  waiting for transfers between devices  44 us (39%)
  Pallas kernels  40.3 us (36%)
  starting transfers between devices  23.8 us (21%)
  local copies, waits for them, and re-layouts  1.3 us (1%)
    ppermute x7, waiting for transfers between devices, cross(): lax.ppermute(value, 'lon', [(i, i ^ 2 * (second if i % 2 else first)) for...  24 us
    pallas_call x2, Pallas kernels, vmem_call(): pl.pallas_call(kernel, in_specs=[vmem] * len(args), out_specs=[vmem] * le...  12.5 us
    ppermute x6, waiting for transfers between devices, chip_swap(): lax.ppermute(value, 'lon', [(i, i ^ 2 * offset) for i in range(size)])  10.8 us
    pallas_call x4, Pallas kernels, feed_forward(): pl.pallas_call(ffn_kernel, in_specs=[vmem] * 4, out_specs=[vmem] * 3, out...  10.4 us
    ppermute x4, starting transfers between devices, shift(): return lax.ppermute(part, axis, pairs)  8.58 us
    pallas_call x3, Pallas kernels, local_call(): pl.pallas_call(kernel, in_specs=[pl.BlockSpec(memory_space=pltpu.SMEM)] +...  8.14 us
    ppermute x15, waiting for transfers between devices, core_swap(): return lax.ppermute(value, 'lon', [(i, i ^ 1) for i in range(size)])  6.61 us
    ppermute x7, starting transfers between devices, cross(): lax.ppermute(value, 'lon', [(i, i ^ 2 * (second if i % 2 else first)) for...  6.51 us
  transfers between devices with their start and end apart: 32, of which 20 were waited for; matrix products, arithmetic and copies ran while one was open for 1% of the time, Pallas kernels for 32%

profile of v16, /device:TPU:0, one launch (start us, length us, event | category | flops | bytes accessed | tf_op | source)
XLA Modules:
  0.0 111.3 jit_solution(7069705278274554449)
XLA Ops:
  0.6 0.5 collective-permute-start.4
  1.1 1.2 %copy-done.3 = bf16[18,24,1024]{2,1,0:T(8,128)(2,1)S(1)} copy-done((bf16[18,24,1024]{2,1,0:T(8,128)(2,1)S(1)}, bf16[18,24,1024]{2,1,0:T(8,128)(2,1)}, u32[]{:S(2)}) %copy-start.3) | copy-done | bytes 884760
  2.4 3.6 %collective-permute-start.1 = (bf16[18,8,1024]{2,1,0:T(8,128)(2,1)S(1)}, bf16[18,8,1024]{2,1,0:T(8,128)(2,1)S(1)}, u32[]{:S(2)}, u32[]{:S(2)}) collective-permute-start(bf16[18,8,1024]{2,1,0:T(8,128)(2,1)S(1)} %get-tuple-element.60), channel_id=1, source_target_pairs={{0,7},{1,0},{2,1},{3,2},{4,3},{5,4},{6,5},{7,6},{8,15},{9,8},{10,9... | collective-permute-start | bytes 884744 | tf_op jit(solution)/shard_map/ppermute | solution.py:467
  6.0 2.9 %halves.1 = (bf16[2048,256]{1,0:T(8,128)(2,1)}, bf16[2048,256]{1,0:T(8,128)(2,1)}) custom-call(bf16[4096,256]{1,0:T(8,128)(2,1)} %refs_0_.1), custom_call_target="tpu_custom_call" | custom-call | tf_op jit(solution)/shard_map/halves/pallas_call | solution.py:202
  9.0 1.1 collective-permute-start.6
  10.2 5.2 %own_projection.1 = (bf16[448,3072]{1,0:T(8,128)(2,1)S(1)}, bf16[1024,2048]{1,0:T(8,128)(2,1)S(1)}) custom-call(bf16[18,24,1024]{2,1,0:T(8,128)(2,1)S(1)} %copy-done.4, bf16[1024,3072]{1,0:T(8,128)(2,1)} %weight_ref.1), custom_call_target="tpu_custom_call" | custom-call | flops 2818572288 | bytes 6291456 | tf_op jit(solution)/shard_map/own_projection/pallas_call | solution.py:242
  15.5 0.1 or_select_fusion.bias_ref
  15.6 0.4 collective-permute-done.west_ref
  16.0 3.5 %collective-permute-start.2 = (bf16[3,40,1024]{2,1,0:T(8,128)(2,1)S(1)}, bf16[3,40,1024]{2,1,0:T(8,128)(2,1)S(1)}, u32[]{:S(2)}, u32[]{:S(2)}) collective-permute-start(bf16[3,40,1024]{2,1,0:T(8,128)(2,1)S(1)} %pad_maximum_fusion), channel_id=1, source_target_pairs={{0,8},{8,16},{16,24},{1,9},{9,17},{17,25},{2,10},{10,18},{18,26},{... | collective-permute-start | bytes 737288 | tf_op jit(solution)/shard_map/ppermute | solution.py:467
  19.5 1.5 %collective-permute-start.3 = (bf16[3,40,1024]{2,1,0:T(8,128)(2,1)S(1)}, bf16[3,40,1024]{2,1,0:T(8,128)(2,1)S(1)}, u32[]{:S(2)}, u32[]{:S(2)}) collective-permute-start(bf16[3,40,1024]{2,1,0:T(8,128)(2,1)S(1)} %pad_maximum_fusion.1), channel_id=1, source_target_pairs={{8,0},{16,8},{24,16},{9,1},{17,9},{25,17},{10,2},{18,10},{26,18},{... | collective-permute-start | bytes 737288 | tf_op jit(solution)/shard_map/ppermute | solution.py:467
  21.1 6.5 %middle_attention.1 = (bf16[288,2048]{1,0:T(8,128)(2,1)S(1)}, bf16[12,24,1024]{2,1,0:T(8,128)(2,1)S(1)}, bf16[64,2048]{1,0:T(8,128)(2,1)S(1)}, bf16[64,2048]{1,0:T(8,128)(2,1)S(1)}) custom-call(bf16[18,24,1024]{2,1,0:T(8,128)(2,1)S(1)} %copy-done.4, bf16[18,8,1024]{2,1,0:T(8,128)(2,1)S(1)} %collective-permute-done.west_ref, ...), custom_call_target="tpu_custom_call" | custom-call | flops 5000000000 | bytes 1048576 | tf_op jit(solution)/shard_map/middle_attention/pallas_call | solution.py:398
  27.7 2.3 %collective-permute-done.3.south_ref = bf16[3,40,1024]{2,1,0:T(8,128)(2,1)S(1)} collective-permute-done((bf16[3,40,1024]{2,1,0:T(8,128)(2,1)S(1)}, bf16[3,40,1024]{2,1,0:T(8,128)(2,1)S(1)}, u32[]{:S(2)}, u32[]{:S(2)}) %collective-permute-start.3) | collective-permute-done | bytes 245792 | tf_op jit(solution)/shard_map/ppermute | solution.py:467
  30.0 6.0 %edge_attention.1 = (bf16[18,24,1024]{2,1,0:T(8,128)(2,1)}, bf16[112,2048]{1,0:T(8,128)(2,1)}, bf16[112,2048]{1,0:T(8,128)(2,1)}) custom-call(bf16[18,24,1024]{2,1,0:T(8,128)(2,1)S(1)} %copy-done.4, bf16[3,40,1024]{2,1,0:T(8,128)(2,1)S(1)} %collective-permute-done.2.north_ref, bf16[3,40,1024]{2,1,0:T(8,128)(2,1)S(1)} %collective-permute-done.3.south_ref, ...), custom_call_target="tpu_custom_call" | custom-call | flops 6000000000 | bytes 1048576 | tf_op jit(solution)/shard_map/edge_attention/pallas_call | solution.py:398
  36.0 0.7 collective-permute-done.6.refs_4_
  36.6 0.2 collective-permute-start.7
  36.8 0.3 collective-permute-start.8
  37.1 0.2 collective-permute-start.9
  37.3 2.1 %collective-permute-start.10 = (bf16[112,2048]{1,0:T(8,128)(2,1)}, bf16[112,2048]{1,0:T(8,128)(2,1)}, u32[]{:S(2)}, u32[]{:S(2)}) collective-permute-start(bf16[112,2048]{1,0:T(8,128)(2,1)} %get-tuple-element.69.lower_ref), channel_id=1, source_target_pairs={{0,2},{1,3},{2,0},{3,1},{4,6},{5,7},{6,4},{7,5},{8,10},{9,11},{10,... | collective-permute-start | bytes 1376264 | tf_op jit(solution)/shard_map/ppermute | solution.py:632
  39.4 0.1 pad_add_fusion.place_ref
  39.5 1.6 %collective-permute-done.8.refs_5_ = bf16[2048,256]{1,0:T(8,128)(2,1)} collective-permute-done((bf16[2048,256]{1,0:T(8,128)(2,1)}, bf16[2048,256]{1,0:T(8,128)(2,1)}, u32[]{:S(2)}, u32[]{:S(2)}) %collective-permute-start.8) | collective-permute-done | bytes 1048608 | tf_op jit(solution)/shard_map/ppermute | solution.py:627
  41.1 4.7 %merge_own.1 = (f32[112,512]{1,0:T(8,128)S(1)}, f32[112,512]{1,0:T(8,128)S(1)}, f32[112,512]{1,0:T(8,128)S(1)}, bf16[4096,256]{1,0:T(8,128)(2,1)S(1)}, bf16[4096...) custom-call(s32[2]{0:T(128)S(1)} %pad_add_fusion.place_ref, ...), custom_call_target="tpu_custom_call" | custom-call | flops 939524096 | bytes 1048576 | tf_op jit(solution)/shard_map/merge_own/pallas_call | solution.py:545
  45.8 4.2 %collective-permute-done.9.upper_ref = bf16[112,2048]{1,0:T(8,128)(2,1)} collective-permute-done((bf16[112,2048]{1,0:T(8,128)(2,1)}, bf16[112,2048]{1,0:T(8,128)(2,1)}, u32[]{:S(2)}, u32[]{:S(2)}) %collective-permute-start.9) | collective-permute-done | bytes 458784 | tf_op jit(solution)/shard_map/ppermute | solution.py:632
  50.0 0.3 collective-permute-done.10.lower_ref
  50.3 2.9 %merge_other.1 = (bf16[112,1024]{1,0:T(8,128)(2,1)S(1)}, bf16[112,1024]{1,0:T(8,128)(2,1)S(1)}) custom-call(s32[2]{0:T(128)S(1)} %pad_add_fusion.place_ref, bf16[112,2048]{1,0:T(8,128)(2,1)} %collective-permute-done.9.upper_ref, bf16[112,2048]{1,0:T(8,128)(2,1)} %collective-permute-done.10.lower_ref, bf16[4096,256]{1,0:T(8,128)(2,1)S(1)} %get-tuple-element.78.refs_0_, ...), custom_call_target="tpu_custom_call" | custom-call | flops 939524096 | bytes 1048576 | tf_op jit(solution)/shard_map/merge_other/pallas_call | solution.py:545
  53.2 1.6 %collective-permute-start.11 = (bf16[112,1024]{1,0:T(8,128)(2,1)S(1)}, bf16[112,1024]{1,0:T(8,128)(2,1)S(1)}, u32[]{:S(2)}, u32[]{:S(2)}) collective-permute-start(bf16[112,1024]{1,0:T(8,128)(2,1)S(1)} %get-tuple-element.84), channel_id=1, source_target_pairs={{0,4},{1,5},{2,6},{3,7},{4,0},{5,1},{6,2},{7,3},{8,12},{9,13},{10,... | collective-permute-start | bytes 688136 | tf_op jit(solution)/shard_map/ppermute | solution.py:632
  54.8 0.6 collective-permute-start.12
  55.4 4.7 %collective-permute-done.11.from_y_ref = bf16[112,1024]{1,0:T(8,128)(2,1)S(1)} collective-permute-done((bf16[112,1024]{1,0:T(8,128)(2,1)S(1)}, bf16[112,1024]{1,0:T(8,128)(2,1)S(1)}, u32[]{:S(2)}, u32[]{:S(2)}) %collective-permute-start.11) | collective-permute-done | bytes 229408 | tf_op jit(solution)/shard_map/ppermute | solution.py:632
  60.1 0.9 collective-permute-done.12.from_x_ref
  61.0 0.6 combine.1.mine_ref.refs_0_
  61.7 0.9 collective-permute-start.13
  62.6 0.9 collective-permute-done.14.theirs_ref
  63.5 2.6 %feed_forward.4 = (bf16[112,2048]{1,0:T(8,128)(2,1)S(1)}, bf16[112,1024]{1,0:T(8,128)(2,1)S(1)}, bf16[112,1024]{1,0:T(8,128)(2,1)S(1)}) custom-call(bf16[112,2048]{1,0:T(8,128)(2,1)S(1)} %combine.1.mine_ref.refs_0_, bf16[112,2048]{1,0:T(8,128)(2,1)S(1)} %collective-permute-done.14.theirs_ref, bf16[2048,1024]{1,0:T(8,128)(2,1)S(1)} %copy-done, ...), custom_call_target="tpu_custom_call" | custom-call | flops 1879048192 | bytes 8388608 | tf_op jit(solution)/shard_map/feed_forward/pallas_call | solution.py:603
  66.1 4.1 %collective-permute-done.13.mine_ref = bf16[112,2048]{1,0:T(8,128)(2,1)S(1)} collective-permute-done((bf16[112,2048]{1,0:T(8,128)(2,1)S(1)}, bf16[112,2048]{1,0:T(8,128)(2,1)S(1)}, u32[]{:S(2)}, u32[]{:S(2)}) %collective-permute-start.13) | collective-permute-done | bytes 458784 | tf_op jit(solution)/shard_map/ppermute | solution.py:637
  70.2 0.9 collective-permute-start.19
  71.1 0.9 collective-permute-done.17.theirs_ref
  72.0 2.6 %feed_forward.5 = (bf16[112,2048]{1,0:T(8,128)(2,1)S(1)}, bf16[112,1024]{1,0:T(8,128)(2,1)S(1)}, bf16[112,1024]{1,0:T(8,128)(2,1)S(1)}) custom-call(bf16[112,2048]{1,0:T(8,128)(2,1)S(1)} %collective-permute-done.13.mine_ref, bf16[112,2048]{1,0:T(8,128)(2,1)S(1)} %collective-permute-done.17.theirs_ref, bf16[2048,1024]{1,0:T(8,128)(2,1)S(1)} %copy-done, ...), custom_call_target="tpu_custom_call" | custom-call | flops 1879048192 | bytes 8388608 | tf_op jit(solution)/shard_map/feed_forward/pallas_call | solution.py:603
  74.7 0.2 collective-permute-start.18
  74.8 3.9 %collective-permute-done.19.mine_ref = bf16[112,2048]{1,0:T(8,128)(2,1)S(1)} collective-permute-done((bf16[112,2048]{1,0:T(8,128)(2,1)S(1)}, bf16[112,2048]{1,0:T(8,128)(2,1)S(1)}, u32[]{:S(2)}, u32[]{:S(2)}) %collective-permute-start.19) | collective-permute-done | bytes 458784 | tf_op jit(solution)/shard_map/ppermute | solution.py:637
  78.7 0.9 collective-permute-start.22
  79.6 0.9 collective-permute-done.20.theirs_ref
  80.5 2.6 %feed_forward.6 = (bf16[112,2048]{1,0:T(8,128)(2,1)S(1)}, bf16[112,1024]{1,0:T(8,128)(2,1)S(1)}, bf16[112,1024]{1,0:T(8,128)(2,1)S(1)}) custom-call(bf16[112,2048]{1,0:T(8,128)(2,1)S(1)} %collective-permute-done.19.mine_ref, bf16[112,2048]{1,0:T(8,128)(2,1)S(1)} %collective-permute-done.20.theirs_ref, bf16[2048,1024]{1,0:T(8,128)(2,1)S(1)} %copy-done, ...), custom_call_target="tpu_custom_call" | custom-call | flops 1879048192 | bytes 8388608 | tf_op jit(solution)/shard_map/feed_forward/pallas_call | solution.py:603
  83.1 0.2 collective-permute-start.21
  83.4 0.3 collective-permute-start.24
  83.7 3.5 %collective-permute-done.22.mine_ref = bf16[112,2048]{1,0:T(8,128)(2,1)S(1)} collective-permute-done((bf16[112,2048]{1,0:T(8,128)(2,1)S(1)}, bf16[112,2048]{1,0:T(8,128)(2,1)S(1)}, u32[]{:S(2)}, u32[]{:S(2)}) %collective-permute-start.22) | collective-permute-done | bytes 458784 | tf_op jit(solution)/shard_map/ppermute | solution.py:637
  87.2 0.1 add_convert_fusion.1
  87.3 1.7 %collective-permute-done.23.theirs_ref = bf16[112,2048]{1,0:T(8,128)(2,1)S(1)} collective-permute-done((bf16[112,2048]{1,0:T(8,128)(2,1)S(1)}, bf16[112,2048]{1,0:T(8,128)(2,1)S(1)}, u32[]{:S(2)}, u32[]{:S(2)}) %collective-permute-start.23) | collective-permute-done | bytes 458784 | tf_op jit(solution)/shard_map/ppermute | solution.py:627
  89.0 0.9 collective-permute-start.25
  89.9 2.6 %feed_forward.7 = (bf16[112,2048]{1,0:T(8,128)(2,1)S(1)}, bf16[112,1024]{1,0:T(8,128)(2,1)S(1)}, bf16[112,1024]{1,0:T(8,128)(2,1)S(1)}) custom-call(bf16[112,2048]{1,0:T(8,128)(2,1)S(1)} %collective-permute-done.22.mine_ref, bf16[112,2048]{1,0:T(8,128)(2,1)S(1)} %collective-permute-done.23.theirs_ref, bf16[2048,1024]{1,0:T(8,128)(2,1)S(1)} %copy-done, ...), custom_call_target="tpu_custom_call" | custom-call | flops 1879048192 | bytes 8388608 | tf_op jit(solution)/shard_map/feed_forward/pallas_call | solution.py:603
  92.6 0.5 collective-permute-start.27
  93.1 0.1 collective-permute-start.16
  93.1 0.4 collective-permute-start.15
  93.6 0.5 collective-permute-done.26
  94.0 0.1 collective-permute-start.30
  94.2 3.3 %collective-permute-done.25 = bf16[112,2048]{1,0:T(8,128)(2,1)S(1)} collective-permute-done((bf16[112,2048]{1,0:T(8,128)(2,1)S(1)}, bf16[112,2048]{1,0:T(8,128)(2,1)S(1)}, u32[]{:S(2)}, u32[]{:S(2)}) %collective-permute-start.25) | collective-permute-done | bytes 458784 | tf_op jit(solution)/shard_map/ppermute | solution.py:637
  97.5 0.1 add_convert_fusion
  97.6 0.9 collective-permute-start.28
  98.5 0.2 add_convert_fusion.3
  98.8 1.4 %collective-permute-start.29 = (bf16[112,1024]{1,0:T(8,128)(2,1)S(1)}, bf16[112,1024]{1,0:T(8,128)(2,1)S(1)}, u32[]{:S(2)}, u32[]{:S(2)}) collective-permute-start(bf16[112,1024]{1,0:T(8,128)(2,1)S(1)} %get-tuple-element.113), channel_id=1, source_target_pairs={{0,2},{1,5},{2,0},{3,7},{4,6},{5,1},{6,4},{7,3},{8,10},{9,13},{10,... | collective-permute-start | bytes 688136 | tf_op jit(solution)/shard_map/ppermute | solution.py:637
  100.2 0.7 collective-permute-start.31
  100.9 0.1 add_convert_fusion.2.refs_1_
  101.0 5.9 %collective-permute-done.29.refs_3_ = bf16[112,1024]{1,0:T(8,128)(2,1)S(1)} collective-permute-done((bf16[112,1024]{1,0:T(8,128)(2,1)S(1)}, bf16[112,1024]{1,0:T(8,128)(2,1)S(1)}, u32[]{:S(2)}, u32[]{:S(2)}) %collective-permute-start.29) | collective-permute-done | bytes 229408 | tf_op jit(solution)/shard_map/ppermute | solution.py:637
  106.9 2.5 %collective-permute-done.31.refs_4_ = bf16[112,1024]{1,0:T(8,128)(2,1)S(1)} collective-permute-done((bf16[112,1024]{1,0:T(8,128)(2,1)S(1)}, bf16[112,1024]{1,0:T(8,128)(2,1)S(1)}, u32[]{:S(2)}, u32[]{:S(2)}) %collective-permute-start.31) | collective-permute-done | bytes 229408 | tf_op jit(solution)/shard_map/ppermute | solution.py:637
  109.4 0.8 collective-permute-done.28.refs_2_
  110.2 1.1 finish.1
  (60 shorter events, 0.5 us)
Async XLA Ops:
  0.6 38.9 %collective-permute-start.4 = (bf16[4096,256]{1,0:T(8,128)(2,1)}, bf16[4096,256]{1,0:T(8,128)(2,1)}, u32[]{:S(2)}, u32[]{:S(2)}) collective-permute-start(bf16[4096,256]{1,0:T(8,128)(2,1)} %refs_0_.1), channel_id=1, source_target_pairs={{0,1},{1,0},{2,3},{3,2},{4,5},{5,4},{6,7},{7,6},{8,9},{9,8},{10,11... | collective-permute-start | bytes 6291464 | tf_op jit(solution)/shard_map/ppermute | solution.py:627
  1.1 1.2 %copy-start.3 = (bf16[18,24,1024]{2,1,0:T(8,128)(2,1)S(1)}, bf16[18,24,1024]{2,1,0:T(8,128)(2,1)}, u32[]{:S(2)}) copy-start(bf16[18,24,1024]{2,1,0:T(8,128)(2,1)} %tokens_ref.7) | copy-start | bytes 2654212
  2.3 7.8 %copy-start.4 = (bf16[18,24,1024]{2,1,0:T(8,128)(2,1)S(1)}, bf16[18,24,1024]{2,1,0:T(8,128)(2,1)}, u32[]{:S(2)}) copy-start(bf16[18,24,1024]{2,1,0:T(8,128)(2,1)} %tokens_ref.7) | copy-start | bytes 2654212
  2.4 13.2 %collective-permute-start.1 = (bf16[18,8,1024]{2,1,0:T(8,128)(2,1)S(1)}, bf16[18,8,1024]{2,1,0:T(8,128)(2,1)S(1)}, u32[]{:S(2)}, u32[]{:S(2)}) collective-permute-start(bf16[18,8,1024]{2,1,0:T(8,128)(2,1)S(1)} %get-tuple-element.60), channel_id=1, source_target_pairs={{0,7},{1,0},{2,1},{3,2},{4,3},{5,4},{6,5},{7,6},{8,15},{9,8},{10,9... | collective-permute-start | bytes 884744 | tf_op jit(solution)/shard_map/ppermute | solution.py:467
  6.0 10.0 %collective-permute-start = (bf16[18,8,1024]{2,1,0:T(8,128)(2,1)S(1)}, bf16[18,8,1024]{2,1,0:T(8,128)(2,1)S(1)}, u32[]{:S(2)}, u32[]{:S(2)}) collective-permute-start(bf16[18,8,1024]{2,1,0:T(8,128)(2,1)S(1)} %get-tuple-element.59), channel_id=1, source_target_pairs={{0,1},{1,2},{2,3},{3,4},{4,5},{5,6},{6,7},{7,0},{8,9},{9,10},{10,1... | collective-permute-start | bytes 884744 | tf_op jit(solution)/shard_map/ppermute | solution.py:467
  8.9 27.1 %collective-permute-start.5 = (bf16[2048,256]{1,0:T(8,128)(2,1)}, bf16[2048,256]{1,0:T(8,128)(2,1)}, u32[]{:S(2)}, u32[]{:S(2)}) collective-permute-start(bf16[2048,256]{1,0:T(8,128)(2,1)} %get-tuple-element.71), channel_id=1, source_target_pairs={{0,2},{1,3},{2,0},{3,1},{4,6},{5,7},{6,4},{7,5},{8,10},{9,11},{10,... | collective-permute-start | bytes 3145736 | tf_op jit(solution)/shard_map/ppermute | solution.py:632
  9.0 27.6 %collective-permute-start.6 = (bf16[2048,256]{1,0:T(8,128)(2,1)}, bf16[2048,256]{1,0:T(8,128)(2,1)}, u32[]{:S(2)}, u32[]{:S(2)}) collective-permute-start(bf16[2048,256]{1,0:T(8,128)(2,1)} %get-tuple-element.72), channel_id=1, source_target_pairs={{0,4},{1,5},{2,6},{3,7},{4,0},{5,1},{6,2},{7,3},{8,12},{9,13},{10,... | collective-permute-start | bytes 3145736 | tf_op jit(solution)/shard_map/ppermute | solution.py:632
  10.1 10.9 %copy-start.5 = (bf16[1024,1024]{1,0:T(8,128)(2,1)S(1)}, bf16[1024,1024]{1,0:T(8,128)(2,1)}, u32[]{:S(2)}) copy-start(bf16[1024,1024]{1,0:T(8,128)(2,1)} %out_w_ref.3) | copy-start | bytes 6291460
  10.1 10.9 %copy-start.6 = (bf16[576,144]{1,0:T(8,128)(2,1)S(1)}, bf16[576,144]{1,0:T(8,128)(2,1)}, u32[]{:S(2)}) copy-start(bf16[576,144]{1,0:T(8,128)(2,1)} %constant.74.clone.rest_1_) | copy-start | bytes 497668
  10.2 10.9 %copy-start.7 = (bf16[576,256]{1,0:T(8,128)(2,1)S(1)}, bf16[576,256]{1,0:T(8,128)(2,1)}, u32[]{:S(2)}) copy-start(bf16[576,256]{1,0:T(8,128)(2,1)} %constant.75.clone.rest_2_) | copy-start | bytes 884740
  10.2 10.9 %copy-start.8 = (bf16[256,288]{1,0:T(8,128)(2,1)S(1)}, bf16[256,288]{1,0:T(8,128)(2,1)}, u32[]{:S(2)}) copy-start(bf16[256,288]{1,0:T(8,128)(2,1)} %constant.72.clone.patch_ref) | copy-start | bytes 442372
  10.2 10.9 %copy-start.9 = (bf16[144,576]{1,0:T(8,128)(2,1)S(1)}, bf16[144,576]{1,0:T(8,128)(2,1)}, u32[]{:S(2)}) copy-start(bf16[144,576]{1,0:T(8,128)(2,1)} %constant.76.clone.rest_3_) | copy-start | bytes 497668
  10.2 10.9 %copy-start.13 = (bf16[240,240]{1,0:T(8,128)(2,1)S(1)}, bf16[240,240]{1,0:T(8,128)(2,1)}, u32[]{:S(2)}) copy-start(bf16[240,240]{1,0:T(8,128)(2,1)} %constant.73.clone.rest_0_) | copy-start | bytes 345604
  16.0 11.7 %collective-permute-start.2 = (bf16[3,40,1024]{2,1,0:T(8,128)(2,1)S(1)}, bf16[3,40,1024]{2,1,0:T(8,128)(2,1)S(1)}, u32[]{:S(2)}, u32[]{:S(2)}) collective-permute-start(bf16[3,40,1024]{2,1,0:T(8,128)(2,1)S(1)} %pad_maximum_fusion), channel_id=1, source_target_pairs={{0,8},{8,16},{16,24},{1,9},{9,17},{17,25},{2,10},{10,18},{18,26},{... | collective-permute-start | bytes 737288 | tf_op jit(solution)/shard_map/ppermute | solution.py:467
  19.5 10.4 %collective-permute-start.3 = (bf16[3,40,1024]{2,1,0:T(8,128)(2,1)S(1)}, bf16[3,40,1024]{2,1,0:T(8,128)(2,1)S(1)}, u32[]{:S(2)}, u32[]{:S(2)}) collective-permute-start(bf16[3,40,1024]{2,1,0:T(8,128)(2,1)S(1)} %pad_maximum_fusion.1), channel_id=1, source_target_pairs={{8,0},{16,8},{24,16},{9,1},{17,9},{25,17},{10,2},{18,10},{26,18},{... | collective-permute-start | bytes 737288 | tf_op jit(solution)/shard_map/ppermute | solution.py:467
  21.1 8.9 %copy-start.10 = (bf16[304,256]{1,0:T(8,128)(2,1)S(1)}, bf16[304,256]{1,0:T(8,128)(2,1)}, u32[]{:S(2)}) copy-start(bf16[304,256]{1,0:T(8,128)(2,1)} %constant.80.clone.rest_2_.rest_6_) | copy-start | bytes 466948
  21.1 8.9 %copy-start.11 = (bf16[240,256]{1,0:T(8,128)(2,1)S(1)}, bf16[240,256]{1,0:T(8,128)(2,1)}, u32[]{:S(2)}) copy-start(bf16[240,256]{1,0:T(8,128)(2,1)} %constant.78.clone.rest_0_) | copy-start | bytes 368644
  21.1 8.9 %copy-start.12 = (bf16[240,256]{1,0:T(8,128)(2,1)S(1)}, bf16[240,256]{1,0:T(8,128)(2,1)}, u32[]{:S(2)}) copy-start(bf16[240,256]{1,0:T(8,128)(2,1)} %constant.82.clone.rest_4_) | copy-start | bytes 368644
  21.1 8.8 %copy-start.14 = (bf16[192,192]{1,0:T(8,128)(2,1)S(1)}, bf16[192,192]{1,0:T(8,128)(2,1)}, u32[]{:S(2)}) copy-start(bf16[192,192]{1,0:T(8,128)(2,1)} %constant.77.clone.patch_ref) | copy-start | bytes 221188
  21.1 8.8 %copy-start.15 = (bf16[304,80]{1,0:T(8,128)(2,1)S(1)}, bf16[304,80]{1,0:T(8,128)(2,1)}, u32[]{:S(2)}) copy-start(bf16[304,80]{1,0:T(8,128)(2,1)} %constant.79.clone.rest_1_.rest_5_) | copy-start | bytes 145924
  21.1 8.8 %copy-start.16 = (bf16[80,304]{1,0:T(8,128)(2,1)S(1)}, bf16[80,304]{1,0:T(8,128)(2,1)}, u32[]{:S(2)}) copy-start(bf16[80,304]{1,0:T(8,128)(2,1)} %constant.81.clone.rest_3_.rest_7_) | copy-start | bytes 145924
  30.0 11.2 %copy-start.2 = (bf16[4096,256]{1,0:T(8,128)(2,1)S(1)}, bf16[4096,256]{1,0:T(8,128)(2,1)}, u32[]{:S(2)}) copy-start(bf16[4096,256]{1,0:T(8,128)(2,1)} %refs_0_.1) | copy-start | bytes 6291460
  36.6 2.9 %collective-permute-start.7 = (bf16[2048,256]{1,0:T(8,128)(2,1)}, bf16[2048,256]{1,0:T(8,128)(2,1)S(1)}, u32[]{:S(2)}, u32[]{:S(2)}) collective-permute-start(bf16[2048,256]{1,0:T(8,128)(2,1)} %collective-permute-done.5.refs_2_), channel_id=1, source_target_pairs={{0,1},{1,0},{2,3},{3,2},{4,5},{5,4},{6,7},{7,6},{8,9},{9,8},{10,11... | collective-permute-start | bytes 3145736 | tf_op jit(solution)/shard_map/ppermute | solution.py:627
  36.8 4.3 %collective-permute-start.8 = (bf16[2048,256]{1,0:T(8,128)(2,1)}, bf16[2048,256]{1,0:T(8,128)(2,1)}, u32[]{:S(2)}, u32[]{:S(2)}) collective-permute-start(bf16[2048,256]{1,0:T(8,128)(2,1)} %collective-permute-done.6.refs_4_), channel_id=1, source_target_pairs={{0,1},{1,0},{2,3},{3,2},{4,5},{5,4},{6,7},{7,6},{8,9},{9,8},{10,11... | collective-permute-start | bytes 3145736 | tf_op jit(solution)/shard_map/ppermute | solution.py:627
  37.1 12.9 %collective-permute-start.9 = (bf16[112,2048]{1,0:T(8,128)(2,1)}, bf16[112,2048]{1,0:T(8,128)(2,1)}, u32[]{:S(2)}, u32[]{:S(2)}) collective-permute-start(bf16[112,2048]{1,0:T(8,128)(2,1)} %get-tuple-element.68.upper_ref), channel_id=1, source_target_pairs={{0,4},{1,5},{2,6},{3,7},{4,0},{5,1},{6,2},{7,3},{8,12},{9,13},{10,... | collective-permute-start | bytes 1376264 | tf_op jit(solution)/shard_map/ppermute | solution.py:632
  37.3 13.0 %collective-permute-start.10 = (bf16[112,2048]{1,0:T(8,128)(2,1)}, bf16[112,2048]{1,0:T(8,128)(2,1)}, u32[]{:S(2)}, u32[]{:S(2)}) collective-permute-start(bf16[112,2048]{1,0:T(8,128)(2,1)} %get-tuple-element.69.lower_ref), channel_id=1, source_target_pairs={{0,2},{1,3},{2,0},{3,1},{4,6},{5,7},{6,4},{7,5},{8,10},{9,11},{10,... | collective-permute-start | bytes 1376264 | tf_op jit(solution)/shard_map/ppermute | solution.py:632
  50.3 13.2 %copy-start = (bf16[2048,1024]{1,0:T(8,128)(2,1)S(1)}, bf16[2048,1024]{1,0:T(8,128)(2,1)}, u32[]{:S(2)}) copy-start(bf16[2048,1024]{1,0:T(8,128)(2,1)} %up_ref.7) | copy-start | bytes 12582916
  50.3 13.2 %copy-start.1 = (bf16[1024,2048]{1,0:T(8,128)(2,1)S(1)}, bf16[1024,2048]{1,0:T(8,128)(2,1)}, u32[]{:S(2)}) copy-start(bf16[1024,2048]{1,0:T(8,128)(2,1)} %down_ref.7) | copy-start | bytes 12582916
  53.2 6.9 %collective-permute-start.11 = (bf16[112,1024]{1,0:T(8,128)(2,1)S(1)}, bf16[112,1024]{1,0:T(8,128)(2,1)S(1)}, u32[]{:S(2)}, u32[]{:S(2)}) collective-permute-start(bf16[112,1024]{1,0:T(8,128)(2,1)S(1)} %get-tuple-element.84), channel_id=1, source_target_pairs={{0,4},{1,5},{2,6},{3,7},{4,0},{5,1},{6,2},{7,3},{8,12},{9,13},{10,... | collective-permute-start | bytes 688136 | tf_op jit(solution)/shard_map/ppermute | solution.py:632
  54.8 6.2 %collective-permute-start.12 = (bf16[112,1024]{1,0:T(8,128)(2,1)S(1)}, bf16[112,1024]{1,0:T(8,128)(2,1)S(1)}, u32[]{:S(2)}, u32[]{:S(2)}) collective-permute-start(bf16[112,1024]{1,0:T(8,128)(2,1)S(1)} %get-tuple-element.85), channel_id=1, source_target_pairs={{0,2},{1,3},{2,0},{3,1},{4,6},{5,7},{6,4},{7,5},{8,10},{9,11},{10,... | collective-permute-start | bytes 688136 | tf_op jit(solution)/shard_map/ppermute | solution.py:632
  61.6 1.9 %collective-permute-start.14 = (bf16[112,2048]{1,0:T(8,128)(2,1)S(1)}, bf16[112,2048]{1,0:T(8,128)(2,1)S(1)}, u32[]{:S(2)}, u32[]{:S(2)}) collective-permute-start(bf16[112,2048]{1,0:T(8,128)(2,1)S(1)} %combine.1.mine_ref.refs_0_), channel_id=1, source_target_pairs={{0,1},{1,0},{2,3},{3,2},{4,5},{5,4},{6,7},{7,6},{8,9},{9,8},{10,11... | collective-permute-start | bytes 1376264 | tf_op jit(solution)/shard_map/ppermute | solution.py:627
  61.7 8.5 %collective-permute-start.13 = (bf16[112,2048]{1,0:T(8,128)(2,1)S(1)}, bf16[112,2048]{1,0:T(8,128)(2,1)S(1)}, u32[]{:S(2)}, u32[]{:S(2)}) collective-permute-start(bf16[112,2048]{1,0:T(8,128)(2,1)S(1)} %combine.1.mine_ref.refs_0_), channel_id=1, source_target_pairs={{0,2},{1,5},{2,0},{3,7},{4,6},{5,1},{6,4},{7,3},{8,10},{9,13},{10,... | collective-permute-start | bytes 1376264 | tf_op jit(solution)/shard_map/ppermute | solution.py:637
  70.2 1.8 %collective-permute-start.17 = (bf16[112,2048]{1,0:T(8,128)(2,1)S(1)}, bf16[112,2048]{1,0:T(8,128)(2,1)S(1)}, u32[]{:S(2)}, u32[]{:S(2)}) collective-permute-start(bf16[112,2048]{1,0:T(8,128)(2,1)S(1)} %collective-permute-done.13.mine_ref), channel_id=1, source_target_pairs={{0,1},{1,0},{2,3},{3,2},{4,5},{5,4},{6,7},{7,6},{8,9},{9,8},{10,11... | collective-permute-start | bytes 1376264 | tf_op jit(solution)/shard_map/ppermute | solution.py:627
  70.2 8.5 %collective-permute-start.19 = (bf16[112,2048]{1,0:T(8,128)(2,1)S(1)}, bf16[112,2048]{1,0:T(8,128)(2,1)S(1)}, u32[]{:S(2)}, u32[]{:S(2)}) collective-permute-start(bf16[112,2048]{1,0:T(8,128)(2,1)S(1)} %collective-permute-done.13.mine_ref), channel_id=1, source_target_pairs={{0,4},{1,3},{2,6},{3,1},{4,0},{5,7},{6,2},{7,5},{8,12},{9,11},{10,... | collective-permute-start | bytes 1376264 | tf_op jit(solution)/shard_map/ppermute | solution.py:637
  74.7 4.0 %collective-permute-start.18 = (bf16[112,1024]{1,0:T(8,128)(2,1)S(1)}, bf16[112,1024]{1,0:T(8,128)(2,1)S(1)}, u32[]{:S(2)}, u32[]{:S(2)}) collective-permute-start(bf16[112,1024]{1,0:T(8,128)(2,1)S(1)} %get-tuple-element.93), channel_id=1, source_target_pairs={{0,1},{1,0},{2,3},{3,2},{4,5},{5,4},{6,7},{7,6},{8,9},{9,8},{10,11... | collective-permute-start | bytes 688136 | tf_op jit(solution)/shard_map/ppermute | solution.py:627
  78.7 1.8 %collective-permute-start.20 = (bf16[112,2048]{1,0:T(8,128)(2,1)S(1)}, bf16[112,2048]{1,0:T(8,128)(2,1)S(1)}, u32[]{:S(2)}, u32[]{:S(2)}) collective-permute-start(bf16[112,2048]{1,0:T(8,128)(2,1)S(1)} %collective-permute-done.19.mine_ref), channel_id=1, source_target_pairs={{0,1},{1,0},{2,3},{3,2},{4,5},{5,4},{6,7},{7,6},{8,9},{9,8},{10,11... | collective-permute-start | bytes 1376264 | tf_op jit(solution)/shard_map/ppermute | solution.py:627
  78.7 8.5 %collective-permute-start.22 = (bf16[112,2048]{1,0:T(8,128)(2,1)S(1)}, bf16[112,2048]{1,0:T(8,128)(2,1)S(1)}, u32[]{:S(2)}, u32[]{:S(2)}) collective-permute-start(bf16[112,2048]{1,0:T(8,128)(2,1)S(1)} %combine.1.mine_ref.refs_0_), channel_id=1, source_target_pairs={{0,4},{1,3},{2,6},{3,1},{4,0},{5,7},{6,2},{7,5},{8,12},{9,11},{10,... | collective-permute-start | bytes 1376264 | tf_op jit(solution)/shard_map/ppermute | solution.py:637
  83.1 4.1 %collective-permute-start.21 = (bf16[112,1024]{1,0:T(8,128)(2,1)S(1)}, bf16[112,1024]{1,0:T(8,128)(2,1)S(1)}, u32[]{:S(2)}, u32[]{:S(2)}) collective-permute-start(bf16[112,1024]{1,0:T(8,128)(2,1)S(1)} %get-tuple-element.95), channel_id=1, source_target_pairs={{0,1},{1,0},{2,3},{3,2},{4,5},{5,4},{6,7},{7,6},{8,9},{9,8},{10,11... | collective-permute-start | bytes 688136 | tf_op jit(solution)/shard_map/ppermute | solution.py:627
  83.4 3.8 %collective-permute-start.24 = (bf16[112,1024]{1,0:T(8,128)(2,1)S(1)}, bf16[112,1024]{1,0:T(8,128)(2,1)S(1)}, u32[]{:S(2)}, u32[]{:S(2)}) collective-permute-start(bf16[112,1024]{1,0:T(8,128)(2,1)S(1)} %get-tuple-element.101), channel_id=1, source_target_pairs={{0,1},{1,0},{2,3},{3,2},{4,5},{5,4},{6,7},{7,6},{8,9},{9,8},{10,11... | collective-permute-start | bytes 688136 | tf_op jit(solution)/shard_map/ppermute | solution.py:627
  87.2 1.8 %collective-permute-start.23 = (bf16[112,2048]{1,0:T(8,128)(2,1)S(1)}, bf16[112,2048]{1,0:T(8,128)(2,1)S(1)}, u32[]{:S(2)}, u32[]{:S(2)}) collective-permute-start(bf16[112,2048]{1,0:T(8,128)(2,1)S(1)} %collective-permute-done.22.mine_ref), channel_id=1, source_target_pairs={{0,1},{1,0},{2,3},{3,2},{4,5},{5,4},{6,7},{7,6},{8,9},{9,8},{10,11... | collective-permute-start | bytes 1376264 | tf_op jit(solution)/shard_map/ppermute | solution.py:627
  89.0 8.5 %collective-permute-start.25 = (bf16[112,2048]{1,0:T(8,128)(2,1)S(1)}, bf16[112,2048]{1,0:T(8,128)(2,1)S(1)}, u32[]{:S(2)}, u32[]{:S(2)}) collective-permute-start(bf16[112,2048]{1,0:T(8,128)(2,1)S(1)} %add_convert_fusion.1), channel_id=1, source_target_pairs={{0,4},{1,3},{2,6},{3,1},{4,0},{5,7},{6,2},{7,5},{8,12},{9,11},{10,... | collective-permute-start | bytes 1376264 | tf_op jit(solution)/shard_map/ppermute | solution.py:637
  92.5 1.6 %collective-permute-start.26 = (bf16[112,1024]{1,0:T(8,128)(2,1)S(1)}, bf16[112,1024]{1,0:T(8,128)(2,1)S(1)}, u32[]{:S(2)}, u32[]{:S(2)}) collective-permute-start(bf16[112,1024]{1,0:T(8,128)(2,1)S(1)} %get-tuple-element.105), channel_id=1, source_target_pairs={{0,1},{1,0},{2,3},{3,2},{4,5},{5,4},{6,7},{7,6},{8,9},{9,8},{10,11... | collective-permute-start | bytes 688136 | tf_op jit(solution)/shard_map/ppermute | solution.py:627
  92.6 4.9 %collective-permute-start.27 = (bf16[112,1024]{1,0:T(8,128)(2,1)S(1)}, bf16[112,1024]{1,0:T(8,128)(2,1)S(1)}, u32[]{:S(2)}, u32[]{:S(2)}) collective-permute-start(bf16[112,1024]{1,0:T(8,128)(2,1)S(1)} %get-tuple-element.107), channel_id=1, source_target_pairs={{0,1},{1,0},{2,3},{3,2},{4,5},{5,4},{6,7},{7,6},{8,9},{9,8},{10,11... | collective-permute-start | bytes 688136 | tf_op jit(solution)/shard_map/ppermute | solution.py:627
  93.1 7.8 %collective-permute-start.16 = (bf16[112,1024]{1,0:T(8,128)(2,1)S(1)}, bf16[112,1024]{1,0:T(8,128)(2,1)S(1)}, u32[]{:S(2)}, u32[]{:S(2)}) collective-permute-start(bf16[112,1024]{1,0:T(8,128)(2,1)S(1)} %get-tuple-element.91), channel_id=1, source_target_pairs={{0,1},{1,0},{2,3},{3,2},{4,5},{5,4},{6,7},{7,6},{8,9},{9,8},{10,11... | collective-permute-start | bytes 688136 | tf_op jit(solution)/shard_map/ppermute | solution.py:627
  93.1 7.8 %collective-permute-start.15 = (bf16[112,1024]{1,0:T(8,128)(2,1)S(1)}, bf16[112,1024]{1,0:T(8,128)(2,1)S(1)}, u32[]{:S(2)}, u32[]{:S(2)}) collective-permute-start(bf16[112,1024]{1,0:T(8,128)(2,1)S(1)} %get-tuple-element.90), channel_id=1, source_target_pairs={{0,1},{1,0},{2,3},{3,2},{4,5},{5,4},{6,7},{7,6},{8,9},{9,8},{10,11... | collective-permute-start | bytes 688136 | tf_op jit(solution)/shard_map/ppermute | solution.py:627
  94.0 4.5 %collective-permute-start.30 = (bf16[112,1024]{1,0:T(8,128)(2,1)S(1)}, bf16[112,1024]{1,0:T(8,128)(2,1)S(1)}, u32[]{:S(2)}, u32[]{:S(2)}) collective-permute-start(bf16[112,1024]{1,0:T(8,128)(2,1)S(1)} %get-tuple-element.111), channel_id=1, source_target_pairs={{0,1},{1,0},{2,3},{3,2},{4,5},{5,4},{6,7},{7,6},{8,9},{9,8},{10,11... | collective-permute-start | bytes 688136 | tf_op jit(solution)/shard_map/ppermute | solution.py:627
  97.6 12.6 %collective-permute-start.28 = (bf16[112,2048]{1,0:T(8,128)(2,1)S(1)}, bf16[112,2048]{1,0:T(8,128)(2,1)S(1)}, u32[]{:S(2)}, u32[]{:S(2)}) collective-permute-start(bf16[112,2048]{1,0:T(8,128)(2,1)S(1)} %add_convert_fusion), channel_id=1, source_target_pairs={{0,4},{1,3},{2,6},{3,1},{4,0},{5,7},{6,2},{7,5},{8,12},{9,11},{10,... | collective-permute-start | bytes 1376264 | tf_op jit(solution)/shard_map/ppermute | solution.py:637
  98.8 8.1 %collective-permute-start.29 = (bf16[112,1024]{1,0:T(8,128)(2,1)S(1)}, bf16[112,1024]{1,0:T(8,128)(2,1)S(1)}, u32[]{:S(2)}, u32[]{:S(2)}) collective-permute-start(bf16[112,1024]{1,0:T(8,128)(2,1)S(1)} %get-tuple-element.113), channel_id=1, source_target_pairs={{0,2},{1,5},{2,0},{3,7},{4,6},{5,1},{6,4},{7,3},{8,10},{9,13},{10,... | collective-permute-start | bytes 688136 | tf_op jit(solution)/shard_map/ppermute | solution.py:637
  100.2 9.2 %collective-permute-start.31 = (bf16[112,1024]{1,0:T(8,128)(2,1)S(1)}, bf16[112,1024]{1,0:T(8,128)(2,1)S(1)}, u32[]{:S(2)}, u32[]{:S(2)}) collective-permute-start(bf16[112,1024]{1,0:T(8,128)(2,1)S(1)} %get-tuple-element.112), channel_id=1, source_target_pairs={{0,2},{1,5},{2,0},{3,7},{4,6},{5,1},{6,4},{7,3},{8,10},{9,13},{10,... | collective-permute-start | bytes 688136 | tf_op jit(solution)/shard_map/ppermute | solution.py:637

commit v17 on v16

--- a/solution.py
+++ b/solution.py
@@ -494,7 +494,7 @@
 
 def merge_own_kernel(place_ref, upper_ref, lower_ref, *refs):
     weights, (own_ref, x_ref, y_ref), kept = refs[:6], refs[6:9], refs[9:]
-    for ref, to in zip(weights, kept):
+    for ref, to in zip(weights[1:], kept):
         to[...] = ref[...]
 
     def own(at, a, b):
@@ -566,11 +566,11 @@
     from_x = chip_swap(lower, 1)
     flops = 16 * count * half * block
     wide = jax.ShapeDtypeStruct((count, 2 * block), F32)
-    kept = [jax.ShapeDtypeStruct(w.shape, BF16) for w in weights]
-    *own, a, b, c, d, e, f = local_call(
+    kept = [jax.ShapeDtypeStruct(w.shape, BF16) for w in weights[1:]]
+    *own, b, c, d, e, f = local_call(
         merge_own_kernel, [wide] * 3 + kept, place, [upper, lower] + weights, flops, "merge_own", 20
     )
-    weights = [a, b, c, d, e, f]
+    weights = [merge_weight, b, c, d, e, f]
     pair = jax.ShapeDtypeStruct((count, 4 * block), BF16)
     to_y, to_x = local_call(merge_other_kernel, [pair] * 2, place, [from_y, from_x] + weights, flops, "merge_other")
     back_y, back_x = chip_swap(to_y, 2), chip_swap(to_x, 1)

time: 112 us -> 112 us (level)
  no operation moved by 1% of the time
where the time goes in v17:
time: 112 us; the launch traced here: 111 us
  waiting for transfers between devices  44.2 us (39%)
  Pallas kernels  40.3 us (36%)
  starting transfers between devices  23.7 us (21%)
  local copies, waits for them, and re-layouts  1.3 us (1%)
    ppermute x7, waiting for transfers between devices, cross(): lax.ppermute(value, 'lon', [(i, i ^ 2 * (second if i % 2 else first)) for...  24 us
    pallas_call x2, Pallas kernels, vmem_call(): pl.pallas_call(kernel, in_specs=[vmem] * len(args), out_specs=[vmem] * le...  12.5 us
    ppermute x6, waiting for transfers between devices, chip_swap(): lax.ppermute(value, 'lon', [(i, i ^ 2 * offset) for i in range(size)])  10.9 us
    pallas_call x4, Pallas kernels, feed_forward(): pl.pallas_call(ffn_kernel, in_specs=[vmem] * 4, out_specs=[vmem] * 3, out...  10.4 us
    ppermute x4, starting transfers between devices, shift(): return lax.ppermute(part, axis, pairs)  8.58 us
    pallas_call x3, Pallas kernels, local_call(): pl.pallas_call(kernel, in_specs=[pl.BlockSpec(memory_space=pltpu.SMEM)] +...  8.05 us
    ppermute x15, waiting for transfers between devices, core_swap(): return lax.ppermute(value, 'lon', [(i, i ^ 1) for i in range(size)])  6.68 us
    ppermute x7, starting transfers between devices, cross(): lax.ppermute(value, 'lon', [(i, i ^ 2 * (second if i % 2 else first)) for...  6.42 us
  transfers between devices with their start and end apart: 32, of which 20 were waited for; matrix products, arithmetic and copies ran while one was open for 1% of the time, Pallas kernels for 32%

profile of v17, /device:TPU:0, one launch (start us, length us, event | category | flops | bytes accessed | tf_op | source)
XLA Modules:
  0.0 111.3 jit_solution(2167238589238136954)
XLA Ops:
  0.6 0.5 collective-permute-start.4
  1.1 1.2 %copy-done.3 = bf16[18,24,1024]{2,1,0:T(8,128)(2,1)S(1)} copy-done((bf16[18,24,1024]{2,1,0:T(8,128)(2,1)S(1)}, bf16[18,24,1024]{2,1,0:T(8,128)(2,1)}, u32[]{:S(2)}) %copy-start.3) | copy-done | bytes 884760
  2.4 3.6 %collective-permute-start.1 = (bf16[18,8,1024]{2,1,0:T(8,128)(2,1)S(1)}, bf16[18,8,1024]{2,1,0:T(8,128)(2,1)S(1)}, u32[]{:S(2)}, u32[]{:S(2)}) collective-permute-start(bf16[18,8,1024]{2,1,0:T(8,128)(2,1)S(1)} %get-tuple-element.59), channel_id=1, source_target_pairs={{0,7},{1,0},{2,1},{3,2},{4,3},{5,4},{6,5},{7,6},{8,15},{9,8},{10,9... | collective-permute-start | bytes 884744 | tf_op jit(solution)/shard_map/ppermute | solution.py:467
  6.0 2.9 %halves.1 = (bf16[2048,256]{1,0:T(8,128)(2,1)}, bf16[2048,256]{1,0:T(8,128)(2,1)}) custom-call(bf16[4096,256]{1,0:T(8,128)(2,1)} %refs_0_.3), custom_call_target="tpu_custom_call" | custom-call | tf_op jit(solution)/shard_map/halves/pallas_call | solution.py:202
  9.0 1.1 collective-permute-start.6
  10.2 5.2 %own_projection.1 = (bf16[448,3072]{1,0:T(8,128)(2,1)S(1)}, bf16[1024,2048]{1,0:T(8,128)(2,1)S(1)}) custom-call(bf16[18,24,1024]{2,1,0:T(8,128)(2,1)S(1)} %copy-done.4, bf16[1024,3072]{1,0:T(8,128)(2,1)} %weight_ref.1), custom_call_target="tpu_custom_call" | custom-call | flops 2818572288 | bytes 6291456 | tf_op jit(solution)/shard_map/own_projection/pallas_call | solution.py:242
  15.5 0.1 or_select_fusion.bias_ref
  15.6 0.4 collective-permute-done.west_ref
  16.0 3.5 %collective-permute-start.2 = (bf16[3,40,1024]{2,1,0:T(8,128)(2,1)S(1)}, bf16[3,40,1024]{2,1,0:T(8,128)(2,1)S(1)}, u32[]{:S(2)}, u32[]{:S(2)}) collective-permute-start(bf16[3,40,1024]{2,1,0:T(8,128)(2,1)S(1)} %pad_maximum_fusion), channel_id=1, source_target_pairs={{0,8},{8,16},{16,24},{1,9},{9,17},{17,25},{2,10},{10,18},{18,26},{... | collective-permute-start | bytes 737288 | tf_op jit(solution)/shard_map/ppermute | solution.py:467
  19.5 1.5 %collective-permute-start.3 = (bf16[3,40,1024]{2,1,0:T(8,128)(2,1)S(1)}, bf16[3,40,1024]{2,1,0:T(8,128)(2,1)S(1)}, u32[]{:S(2)}, u32[]{:S(2)}) collective-permute-start(bf16[3,40,1024]{2,1,0:T(8,128)(2,1)S(1)} %pad_maximum_fusion.1), channel_id=1, source_target_pairs={{8,0},{16,8},{24,16},{9,1},{17,9},{25,17},{10,2},{18,10},{26,18},{... | collective-permute-start | bytes 737288 | tf_op jit(solution)/shard_map/ppermute | solution.py:467
  21.1 6.5 %middle_attention.1 = (bf16[288,2048]{1,0:T(8,128)(2,1)S(1)}, bf16[12,24,1024]{2,1,0:T(8,128)(2,1)S(1)}, bf16[64,2048]{1,0:T(8,128)(2,1)S(1)}, bf16[64,2048]{1,0:T(8,128)(2,1)S(1)}) custom-call(bf16[18,24,1024]{2,1,0:T(8,128)(2,1)S(1)} %copy-done.4, bf16[18,8,1024]{2,1,0:T(8,128)(2,1)S(1)} %collective-permute-done.west_ref, ...), custom_call_target="tpu_custom_call" | custom-call | flops 5000000000 | bytes 1048576 | tf_op jit(solution)/shard_map/middle_attention/pallas_call | solution.py:398
  27.7 2.3 %collective-permute-done.3.south_ref = bf16[3,40,1024]{2,1,0:T(8,128)(2,1)S(1)} collective-permute-done((bf16[3,40,1024]{2,1,0:T(8,128)(2,1)S(1)}, bf16[3,40,1024]{2,1,0:T(8,128)(2,1)S(1)}, u32[]{:S(2)}, u32[]{:S(2)}) %collective-permute-start.3) | collective-permute-done | bytes 245792 | tf_op jit(solution)/shard_map/ppermute | solution.py:467
  30.0 6.0 %edge_attention.1 = (bf16[18,24,1024]{2,1,0:T(8,128)(2,1)}, bf16[112,2048]{1,0:T(8,128)(2,1)}, bf16[112,2048]{1,0:T(8,128)(2,1)}) custom-call(bf16[18,24,1024]{2,1,0:T(8,128)(2,1)S(1)} %copy-done.4, bf16[3,40,1024]{2,1,0:T(8,128)(2,1)S(1)} %collective-permute-done.2.north_ref, bf16[3,40,1024]{2,1,0:T(8,128)(2,1)S(1)} %collective-permute-done.3.south_ref, ...), custom_call_target="tpu_custom_call" | custom-call | flops 6000000000 | bytes 1048576 | tf_op jit(solution)/shard_map/edge_attention/pallas_call | solution.py:398
  36.0 0.7 collective-permute-done.6.refs_4_
  36.6 0.2 collective-permute-start.7
  36.8 0.3 collective-permute-start.8
  37.1 0.2 collective-permute-start.9
  37.3 2.1 %collective-permute-start.10 = (bf16[112,2048]{1,0:T(8,128)(2,1)}, bf16[112,2048]{1,0:T(8,128)(2,1)}, u32[]{:S(2)}, u32[]{:S(2)}) collective-permute-start(bf16[112,2048]{1,0:T(8,128)(2,1)} %get-tuple-element.68.lower_ref), channel_id=1, source_target_pairs={{0,2},{1,3},{2,0},{3,1},{4,6},{5,7},{6,4},{7,5},{8,10},{9,11},{10,... | collective-permute-start | bytes 1376264 | tf_op jit(solution)/shard_map/ppermute | solution.py:632
  39.4 0.1 pad_add_fusion.place_ref
  39.5 1.6 %collective-permute-done.8.refs_5_ = bf16[2048,256]{1,0:T(8,128)(2,1)} collective-permute-done((bf16[2048,256]{1,0:T(8,128)(2,1)}, bf16[2048,256]{1,0:T(8,128)(2,1)}, u32[]{:S(2)}, u32[]{:S(2)}) %collective-permute-start.8) | collective-permute-done | bytes 1048608 | tf_op jit(solution)/shard_map/ppermute | solution.py:627
  41.1 4.5 %merge_own.1 = (f32[112,512]{1,0:T(8,128)S(1)}, f32[112,512]{1,0:T(8,128)S(1)}, f32[112,512]{1,0:T(8,128)S(1)}, bf16[4096,256]{1,0:T(8,128)(2,1)S(1)}, bf16[2048...) custom-call(s32[2]{0:T(128)S(1)} %pad_add_fusion.place_ref, ...), custom_call_target="tpu_custom_call" | custom-call | flops 939524096 | bytes 1048576 | tf_op jit(solution)/shard_map/merge_own/pallas_call | solution.py:545
  45.7 4.4 %collective-permute-done.9.upper_ref = bf16[112,2048]{1,0:T(8,128)(2,1)} collective-permute-done((bf16[112,2048]{1,0:T(8,128)(2,1)}, bf16[112,2048]{1,0:T(8,128)(2,1)}, u32[]{:S(2)}, u32[]{:S(2)}) %collective-permute-start.9) | collective-permute-done | bytes 458784 | tf_op jit(solution)/shard_map/ppermute | solution.py:632
  50.0 0.3 collective-permute-done.10.lower_ref
  50.3 2.9 %merge_other.1 = (bf16[112,1024]{1,0:T(8,128)(2,1)S(1)}, bf16[112,1024]{1,0:T(8,128)(2,1)S(1)}) custom-call(s32[2]{0:T(128)S(1)} %pad_add_fusion.place_ref, bf16[112,2048]{1,0:T(8,128)(2,1)} %collective-permute-done.9.upper_ref, bf16[112,2048]{1,0:T(8,128)(2,1)} %collective-permute-done.10.lower_ref, bf16[4096,256]{1,0:T(8,128)(2,1)S(1)} %copy-done.2, ...), custom_call_target="tpu_custom_call" | custom-call | flops 939524096 | bytes 1048576 | tf_op jit(solution)/shard_map/merge_other/pallas_call | solution.py:545
  53.2 1.6 %collective-permute-start.11 = (bf16[112,1024]{1,0:T(8,128)(2,1)S(1)}, bf16[112,1024]{1,0:T(8,128)(2,1)S(1)}, u32[]{:S(2)}, u32[]{:S(2)}) collective-permute-start(bf16[112,1024]{1,0:T(8,128)(2,1)S(1)} %get-tuple-element.82), channel_id=1, source_target_pairs={{0,4},{1,5},{2,6},{3,7},{4,0},{5,1},{6,2},{7,3},{8,12},{9,13},{10,... | collective-permute-start | bytes 688136 | tf_op jit(solution)/shard_map/ppermute | solution.py:632
  54.8 0.6 collective-permute-start.12
  55.4 4.7 %collective-permute-done.11.from_y_ref = bf16[112,1024]{1,0:T(8,128)(2,1)S(1)} collective-permute-done((bf16[112,1024]{1,0:T(8,128)(2,1)S(1)}, bf16[112,1024]{1,0:T(8,128)(2,1)S(1)}, u32[]{:S(2)}, u32[]{:S(2)}) %collective-permute-start.11) | collective-permute-done | bytes 229408 | tf_op jit(solution)/shard_map/ppermute | solution.py:632
  60.1 0.9 collective-permute-done.12.from_x_ref
  61.0 0.6 combine.1.mine_ref.refs_0_
  61.7 0.8 collective-permute-start.13
  62.6 1.0 collective-permute-done.14.theirs_ref
  63.5 2.6 %feed_forward.4 = (bf16[112,2048]{1,0:T(8,128)(2,1)S(1)}, bf16[112,1024]{1,0:T(8,128)(2,1)S(1)}, bf16[112,1024]{1,0:T(8,128)(2,1)S(1)}) custom-call(bf16[112,2048]{1,0:T(8,128)(2,1)S(1)} %combine.1.mine_ref.refs_0_, bf16[112,2048]{1,0:T(8,128)(2,1)S(1)} %collective-permute-done.14.theirs_ref, bf16[2048,1024]{1,0:T(8,128)(2,1)S(1)} %copy-done, ...), custom_call_target="tpu_custom_call" | custom-call | flops 1879048192 | bytes 8388608 | tf_op jit(solution)/shard_map/feed_forward/pallas_call | solution.py:603
  66.1 4.1 %collective-permute-done.13.mine_ref = bf16[112,2048]{1,0:T(8,128)(2,1)S(1)} collective-permute-done((bf16[112,2048]{1,0:T(8,128)(2,1)S(1)}, bf16[112,2048]{1,0:T(8,128)(2,1)S(1)}, u32[]{:S(2)}, u32[]{:S(2)}) %collective-permute-start.13) | collective-permute-done | bytes 458784 | tf_op jit(solution)/shard_map/ppermute | solution.py:637
  70.3 0.9 collective-permute-start.19
  71.1 1.0 collective-permute-done.17.theirs_ref
  72.1 2.6 %feed_forward.5 = (bf16[112,2048]{1,0:T(8,128)(2,1)S(1)}, bf16[112,1024]{1,0:T(8,128)(2,1)S(1)}, bf16[112,1024]{1,0:T(8,128)(2,1)S(1)}) custom-call(bf16[112,2048]{1,0:T(8,128)(2,1)S(1)} %collective-permute-done.13.mine_ref, bf16[112,2048]{1,0:T(8,128)(2,1)S(1)} %collective-permute-done.17.theirs_ref, bf16[2048,1024]{1,0:T(8,128)(2,1)S(1)} %copy-done, ...), custom_call_target="tpu_custom_call" | custom-call | flops 1879048192 | bytes 8388608 | tf_op jit(solution)/shard_map/feed_forward/pallas_call | solution.py:603
  74.7 0.2 collective-permute-start.18
  74.9 3.9 %collective-permute-done.19.mine_ref = bf16[112,2048]{1,0:T(8,128)(2,1)S(1)} collective-permute-done((bf16[112,2048]{1,0:T(8,128)(2,1)S(1)}, bf16[112,2048]{1,0:T(8,128)(2,1)S(1)}, u32[]{:S(2)}, u32[]{:S(2)}) %collective-permute-start.19) | collective-permute-done | bytes 458784 | tf_op jit(solution)/shard_map/ppermute | solution.py:637
  78.7 0.9 collective-permute-start.22
  79.6 1.0 collective-permute-done.20.theirs_ref
  80.6 2.6 %feed_forward.6 = (bf16[112,2048]{1,0:T(8,128)(2,1)S(1)}, bf16[112,1024]{1,0:T(8,128)(2,1)S(1)}, bf16[112,1024]{1,0:T(8,128)(2,1)S(1)}) custom-call(bf16[112,2048]{1,0:T(8,128)(2,1)S(1)} %collective-permute-done.19.mine_ref, bf16[112,2048]{1,0:T(8,128)(2,1)S(1)} %collective-permute-done.20.theirs_ref, bf16[2048,1024]{1,0:T(8,128)(2,1)S(1)} %copy-done, ...), custom_call_target="tpu_custom_call" | custom-call | flops 1879048192 | bytes 8388608 | tf_op jit(solution)/shard_map/feed_forward/pallas_call | solution.py:603
  83.2 0.2 collective-permute-start.21
  83.4 0.3 collective-permute-start.24
  83.7 3.5 %collective-permute-done.22.mine_ref = bf16[112,2048]{1,0:T(8,128)(2,1)S(1)} collective-permute-done((bf16[112,2048]{1,0:T(8,128)(2,1)S(1)}, bf16[112,2048]{1,0:T(8,128)(2,1)S(1)}, u32[]{:S(2)}, u32[]{:S(2)}) %collective-permute-start.22) | collective-permute-done | bytes 458784 | tf_op jit(solution)/shard_map/ppermute | solution.py:637
  87.2 0.1 add_convert_fusion.1
  87.4 1.7 %collective-permute-done.23.theirs_ref = bf16[112,2048]{1,0:T(8,128)(2,1)S(1)} collective-permute-done((bf16[112,2048]{1,0:T(8,128)(2,1)S(1)}, bf16[112,2048]{1,0:T(8,128)(2,1)S(1)}, u32[]{:S(2)}, u32[]{:S(2)}) %collective-permute-start.23) | collective-permute-done | bytes 458784 | tf_op jit(solution)/shard_map/ppermute | solution.py:627
  89.0 0.9 collective-permute-start.25
  89.9 2.6 %feed_forward.7 = (bf16[112,2048]{1,0:T(8,128)(2,1)S(1)}, bf16[112,1024]{1,0:T(8,128)(2,1)S(1)}, bf16[112,1024]{1,0:T(8,128)(2,1)S(1)}) custom-call(bf16[112,2048]{1,0:T(8,128)(2,1)S(1)} %collective-permute-done.22.mine_ref, bf16[112,2048]{1,0:T(8,128)(2,1)S(1)} %collective-permute-done.23.theirs_ref, bf16[2048,1024]{1,0:T(8,128)(2,1)S(1)} %copy-done, ...), custom_call_target="tpu_custom_call" | custom-call | flops 1879048192 | bytes 8388608 | tf_op jit(solution)/shard_map/feed_forward/pallas_call | solution.py:603
  92.6 0.5 collective-permute-start.27
  93.1 0.1 collective-permute-start.16
  93.2 0.4 collective-permute-start.15
  93.6 0.5 collective-permute-done.26
  94.1 0.1 collective-permute-start.30
  94.2 3.3 %collective-permute-done.25 = bf16[112,2048]{1,0:T(8,128)(2,1)S(1)} collective-permute-done((bf16[112,2048]{1,0:T(8,128)(2,1)S(1)}, bf16[112,2048]{1,0:T(8,128)(2,1)S(1)}, u32[]{:S(2)}, u32[]{:S(2)}) %collective-permute-start.25) | collective-permute-done | bytes 458784 | tf_op jit(solution)/shard_map/ppermute | solution.py:637
  97.5 0.1 add_convert_fusion
  97.6 0.9 collective-permute-start.28
  98.6 0.2 add_convert_fusion.3
  98.8 1.4 %collective-permute-start.29 = (bf16[112,1024]{1,0:T(8,128)(2,1)S(1)}, bf16[112,1024]{1,0:T(8,128)(2,1)S(1)}, u32[]{:S(2)}, u32[]{:S(2)}) collective-permute-start(bf16[112,1024]{1,0:T(8,128)(2,1)S(1)} %get-tuple-element.111), channel_id=1, source_target_pairs={{0,2},{1,5},{2,0},{3,7},{4,6},{5,1},{6,4},{7,3},{8,10},{9,13},{10,... | collective-permute-start | bytes 688136 | tf_op jit(solution)/shard_map/ppermute | solution.py:637
  100.2 0.7 collective-permute-start.31
  100.9 0.1 add_convert_fusion.2.refs_1_
  101.0 5.9 %collective-permute-done.29.refs_3_ = bf16[112,1024]{1,0:T(8,128)(2,1)S(1)} collective-permute-done((bf16[112,1024]{1,0:T(8,128)(2,1)S(1)}, bf16[112,1024]{1,0:T(8,128)(2,1)S(1)}, u32[]{:S(2)}, u32[]{:S(2)}) %collective-permute-start.29) | collective-permute-done | bytes 229408 | tf_op jit(solution)/shard_map/ppermute | solution.py:637
  107.0 2.5 %collective-permute-done.31.refs_4_ = bf16[112,1024]{1,0:T(8,128)(2,1)S(1)} collective-permute-done((bf16[112,1024]{1,0:T(8,128)(2,1)S(1)}, bf16[112,1024]{1,0:T(8,128)(2,1)S(1)}, u32[]{:S(2)}, u32[]{:S(2)}) %collective-permute-start.31) | collective-permute-done | bytes 229408 | tf_op jit(solution)/shard_map/ppermute | solution.py:637
  109.4 0.8 collective-permute-done.28.refs_2_
  110.2 1.1 finish.1
  (60 shorter events, 0.5 us)
Async XLA Ops:
  0.6 38.9 %collective-permute-start.4 = (bf16[4096,256]{1,0:T(8,128)(2,1)}, bf16[4096,256]{1,0:T(8,128)(2,1)}, u32[]{:S(2)}, u32[]{:S(2)}) collective-permute-start(bf16[4096,256]{1,0:T(8,128)(2,1)} %refs_0_.3), channel_id=1, source_target_pairs={{0,1},{1,0},{2,3},{3,2},{4,5},{5,4},{6,7},{7,6},{8,9},{9,8},{10,11... | collective-permute-start | bytes 6291464 | tf_op jit(solution)/shard_map/ppermute | solution.py:627
  1.1 1.2 %copy-start.3 = (bf16[18,24,1024]{2,1,0:T(8,128)(2,1)S(1)}, bf16[18,24,1024]{2,1,0:T(8,128)(2,1)}, u32[]{:S(2)}) copy-start(bf16[18,24,1024]{2,1,0:T(8,128)(2,1)} %tokens_ref.7) | copy-start | bytes 2654212
  2.3 7.8 %copy-start.4 = (bf16[18,24,1024]{2,1,0:T(8,128)(2,1)S(1)}, bf16[18,24,1024]{2,1,0:T(8,128)(2,1)}, u32[]{:S(2)}) copy-start(bf16[18,24,1024]{2,1,0:T(8,128)(2,1)} %tokens_ref.7) | copy-start | bytes 2654212
  2.4 13.2 %collective-permute-start.1 = (bf16[18,8,1024]{2,1,0:T(8,128)(2,1)S(1)}, bf16[18,8,1024]{2,1,0:T(8,128)(2,1)S(1)}, u32[]{:S(2)}, u32[]{:S(2)}) collective-permute-start(bf16[18,8,1024]{2,1,0:T(8,128)(2,1)S(1)} %get-tuple-element.59), channel_id=1, source_target_pairs={{0,7},{1,0},{2,1},{3,2},{4,3},{5,4},{6,5},{7,6},{8,15},{9,8},{10,9... | collective-permute-start | bytes 884744 | tf_op jit(solution)/shard_map/ppermute | solution.py:467
  6.0 10.0 %collective-permute-start = (bf16[18,8,1024]{2,1,0:T(8,128)(2,1)S(1)}, bf16[18,8,1024]{2,1,0:T(8,128)(2,1)S(1)}, u32[]{:S(2)}, u32[]{:S(2)}) collective-permute-start(bf16[18,8,1024]{2,1,0:T(8,128)(2,1)S(1)} %get-tuple-element.58), channel_id=1, source_target_pairs={{0,1},{1,2},{2,3},{3,4},{4,5},{5,6},{6,7},{7,0},{8,9},{9,10},{10,1... | collective-permute-start | bytes 884744 | tf_op jit(solution)/shard_map/ppermute | solution.py:467
  8.9 27.1 %collective-permute-start.5 = (bf16[2048,256]{1,0:T(8,128)(2,1)}, bf16[2048,256]{1,0:T(8,128)(2,1)}, u32[]{:S(2)}, u32[]{:S(2)}) collective-permute-start(bf16[2048,256]{1,0:T(8,128)(2,1)} %get-tuple-element.70), channel_id=1, source_target_pairs={{0,2},{1,3},{2,0},{3,1},{4,6},{5,7},{6,4},{7,5},{8,10},{9,11},{10,... | collective-permute-start | bytes 3145736 | tf_op jit(solution)/shard_map/ppermute | solution.py:632
  9.0 27.6 %collective-permute-start.6 = (bf16[2048,256]{1,0:T(8,128)(2,1)}, bf16[2048,256]{1,0:T(8,128)(2,1)}, u32[]{:S(2)}, u32[]{:S(2)}) collective-permute-start(bf16[2048,256]{1,0:T(8,128)(2,1)} %get-tuple-element.71), channel_id=1, source_target_pairs={{0,4},{1,5},{2,6},{3,7},{4,0},{5,1},{6,2},{7,3},{8,12},{9,13},{10,... | collective-permute-start | bytes 3145736 | tf_op jit(solution)/shard_map/ppermute | solution.py:632
  10.1 10.9 %copy-start.5 = (bf16[1024,1024]{1,0:T(8,128)(2,1)S(1)}, bf16[1024,1024]{1,0:T(8,128)(2,1)}, u32[]{:S(2)}) copy-start(bf16[1024,1024]{1,0:T(8,128)(2,1)} %out_w_ref.3) | copy-start | bytes 6291460
  10.1 10.9 %copy-start.6 = (bf16[576,144]{1,0:T(8,128)(2,1)S(1)}, bf16[576,144]{1,0:T(8,128)(2,1)}, u32[]{:S(2)}) copy-start(bf16[576,144]{1,0:T(8,128)(2,1)} %constant.74.clone.rest_1_) | copy-start | bytes 497668
  10.2 10.9 %copy-start.7 = (bf16[576,256]{1,0:T(8,128)(2,1)S(1)}, bf16[576,256]{1,0:T(8,128)(2,1)}, u32[]{:S(2)}) copy-start(bf16[576,256]{1,0:T(8,128)(2,1)} %constant.75.clone.rest_2_) | copy-start | bytes 884740
  10.2 10.9 %copy-start.8 = (bf16[256,288]{1,0:T(8,128)(2,1)S(1)}, bf16[256,288]{1,0:T(8,128)(2,1)}, u32[]{:S(2)}) copy-start(bf16[256,288]{1,0:T(8,128)(2,1)} %constant.72.clone.patch_ref) | copy-start | bytes 442372
  10.2 10.9 %copy-start.9 = (bf16[144,576]{1,0:T(8,128)(2,1)S(1)}, bf16[144,576]{1,0:T(8,128)(2,1)}, u32[]{:S(2)}) copy-start(bf16[144,576]{1,0:T(8,128)(2,1)} %constant.76.clone.rest_3_) | copy-start | bytes 497668
  10.2 10.9 %copy-start.13 = (bf16[240,240]{1,0:T(8,128)(2,1)S(1)}, bf16[240,240]{1,0:T(8,128)(2,1)}, u32[]{:S(2)}) copy-start(bf16[240,240]{1,0:T(8,128)(2,1)} %constant.73.clone.rest_0_) | copy-start | bytes 345604
  16.0 11.7 %collective-permute-start.2 = (bf16[3,40,1024]{2,1,0:T(8,128)(2,1)S(1)}, bf16[3,40,1024]{2,1,0:T(8,128)(2,1)S(1)}, u32[]{:S(2)}, u32[]{:S(2)}) collective-permute-start(bf16[3,40,1024]{2,1,0:T(8,128)(2,1)S(1)} %pad_maximum_fusion), channel_id=1, source_target_pairs={{0,8},{8,16},{16,24},{1,9},{9,17},{17,25},{2,10},{10,18},{18,26},{... | collective-permute-start | bytes 737288 | tf_op jit(solution)/shard_map/ppermute | solution.py:467
  19.5 10.4 %collective-permute-start.3 = (bf16[3,40,1024]{2,1,0:T(8,128)(2,1)S(1)}, bf16[3,40,1024]{2,1,0:T(8,128)(2,1)S(1)}, u32[]{:S(2)}, u32[]{:S(2)}) collective-permute-start(bf16[3,40,1024]{2,1,0:T(8,128)(2,1)S(1)} %pad_maximum_fusion.1), channel_id=1, source_target_pairs={{8,0},{16,8},{24,16},{9,1},{17,9},{25,17},{10,2},{18,10},{26,18},{... | collective-permute-start | bytes 737288 | tf_op jit(solution)/shard_map/ppermute | solution.py:467
  21.1 8.9 %copy-start.10 = (bf16[304,256]{1,0:T(8,128)(2,1)S(1)}, bf16[304,256]{1,0:T(8,128)(2,1)}, u32[]{:S(2)}) copy-start(bf16[304,256]{1,0:T(8,128)(2,1)} %constant.80.clone.rest_2_.rest_6_) | copy-start | bytes 466948
  21.1 8.9 %copy-start.11 = (bf16[240,256]{1,0:T(8,128)(2,1)S(1)}, bf16[240,256]{1,0:T(8,128)(2,1)}, u32[]{:S(2)}) copy-start(bf16[240,256]{1,0:T(8,128)(2,1)} %constant.78.clone.rest_0_) | copy-start | bytes 368644
  21.1 8.9 %copy-start.12 = (bf16[240,256]{1,0:T(8,128)(2,1)S(1)}, bf16[240,256]{1,0:T(8,128)(2,1)}, u32[]{:S(2)}) copy-start(bf16[240,256]{1,0:T(8,128)(2,1)} %constant.82.clone.rest_4_) | copy-start | bytes 368644
  21.1 8.8 %copy-start.14 = (bf16[192,192]{1,0:T(8,128)(2,1)S(1)}, bf16[192,192]{1,0:T(8,128)(2,1)}, u32[]{:S(2)}) copy-start(bf16[192,192]{1,0:T(8,128)(2,1)} %constant.77.clone.patch_ref) | copy-start | bytes 221188
  21.1 8.8 %copy-start.15 = (bf16[304,80]{1,0:T(8,128)(2,1)S(1)}, bf16[304,80]{1,0:T(8,128)(2,1)}, u32[]{:S(2)}) copy-start(bf16[304,80]{1,0:T(8,128)(2,1)} %constant.79.clone.rest_1_.rest_5_) | copy-start | bytes 145924
  21.1 8.8 %copy-start.16 = (bf16[80,304]{1,0:T(8,128)(2,1)S(1)}, bf16[80,304]{1,0:T(8,128)(2,1)}, u32[]{:S(2)}) copy-start(bf16[80,304]{1,0:T(8,128)(2,1)} %constant.81.clone.rest_3_.rest_7_) | copy-start | bytes 145924
  30.0 11.2 %copy-start.2 = (bf16[4096,256]{1,0:T(8,128)(2,1)S(1)}, bf16[4096,256]{1,0:T(8,128)(2,1)}, u32[]{:S(2)}) copy-start(bf16[4096,256]{1,0:T(8,128)(2,1)} %refs_0_.3) | copy-start | bytes 6291460
  36.6 2.9 %collective-permute-start.7 = (bf16[2048,256]{1,0:T(8,128)(2,1)}, bf16[2048,256]{1,0:T(8,128)(2,1)S(1)}, u32[]{:S(2)}, u32[]{:S(2)}) collective-permute-start(bf16[2048,256]{1,0:T(8,128)(2,1)} %collective-permute-done.5.refs_2_), channel_id=1, source_target_pairs={{0,1},{1,0},{2,3},{3,2},{4,5},{5,4},{6,7},{7,6},{8,9},{9,8},{10,11... | collective-permute-start | bytes 3145736 | tf_op jit(solution)/shard_map/ppermute | solution.py:627
  36.8 4.3 %collective-permute-start.8 = (bf16[2048,256]{1,0:T(8,128)(2,1)}, bf16[2048,256]{1,0:T(8,128)(2,1)}, u32[]{:S(2)}, u32[]{:S(2)}) collective-permute-start(bf16[2048,256]{1,0:T(8,128)(2,1)} %collective-permute-done.6.refs_4_), channel_id=1, source_target_pairs={{0,1},{1,0},{2,3},{3,2},{4,5},{5,4},{6,7},{7,6},{8,9},{9,8},{10,11... | collective-permute-start | bytes 3145736 | tf_op jit(solution)/shard_map/ppermute | solution.py:627
  37.1 12.9 %collective-permute-start.9 = (bf16[112,2048]{1,0:T(8,128)(2,1)}, bf16[112,2048]{1,0:T(8,128)(2,1)}, u32[]{:S(2)}, u32[]{:S(2)}) collective-permute-start(bf16[112,2048]{1,0:T(8,128)(2,1)} %get-tuple-element.67.upper_ref), channel_id=1, source_target_pairs={{0,4},{1,5},{2,6},{3,7},{4,0},{5,1},{6,2},{7,3},{8,12},{9,13},{10,... | collective-permute-start | bytes 1376264 | tf_op jit(solution)/shard_map/ppermute | solution.py:632
  37.3 13.0 %collective-permute-start.10 = (bf16[112,2048]{1,0:T(8,128)(2,1)}, bf16[112,2048]{1,0:T(8,128)(2,1)}, u32[]{:S(2)}, u32[]{:S(2)}) collective-permute-start(bf16[112,2048]{1,0:T(8,128)(2,1)} %get-tuple-element.68.lower_ref), channel_id=1, source_target_pairs={{0,2},{1,3},{2,0},{3,1},{4,6},{5,7},{6,4},{7,5},{8,10},{9,11},{10,... | collective-permute-start | bytes 1376264 | tf_op jit(solution)/shard_map/ppermute | solution.py:632
  50.3 13.2 %copy-start = (bf16[2048,1024]{1,0:T(8,128)(2,1)S(1)}, bf16[2048,1024]{1,0:T(8,128)(2,1)}, u32[]{:S(2)}) copy-start(bf16[2048,1024]{1,0:T(8,128)(2,1)} %up_ref.7) | copy-start | bytes 12582916
  50.3 13.2 %copy-start.1 = (bf16[1024,2048]{1,0:T(8,128)(2,1)S(1)}, bf16[1024,2048]{1,0:T(8,128)(2,1)}, u32[]{:S(2)}) copy-start(bf16[1024,2048]{1,0:T(8,128)(2,1)} %down_ref.7) | copy-start | bytes 12582916
  53.2 6.9 %collective-permute-start.11 = (bf16[112,1024]{1,0:T(8,128)(2,1)S(1)}, bf16[112,1024]{1,0:T(8,128)(2,1)S(1)}, u32[]{:S(2)}, u32[]{:S(2)}) collective-permute-start(bf16[112,1024]{1,0:T(8,128)(2,1)S(1)} %get-tuple-element.82), channel_id=1, source_target_pairs={{0,4},{1,5},{2,6},{3,7},{4,0},{5,1},{6,2},{7,3},{8,12},{9,13},{10,... | collective-permute-start | bytes 688136 | tf_op jit(solution)/shard_map/ppermute | solution.py:632
  54.8 6.2 %collective-permute-start.12 = (bf16[112,1024]{1,0:T(8,128)(2,1)S(1)}, bf16[112,1024]{1,0:T(8,128)(2,1)S(1)}, u32[]{:S(2)}, u32[]{:S(2)}) collective-permute-start(bf16[112,1024]{1,0:T(8,128)(2,1)S(1)} %get-tuple-element.83), channel_id=1, source_target_pairs={{0,2},{1,3},{2,0},{3,1},{4,6},{5,7},{6,4},{7,5},{8,10},{9,11},{10,... | collective-permute-start | bytes 688136 | tf_op jit(solution)/shard_map/ppermute | solution.py:632
  61.6 1.9 %collective-permute-start.14 = (bf16[112,2048]{1,0:T(8,128)(2,1)S(1)}, bf16[112,2048]{1,0:T(8,128)(2,1)S(1)}, u32[]{:S(2)}, u32[]{:S(2)}) collective-permute-start(bf16[112,2048]{1,0:T(8,128)(2,1)S(1)} %combine.1.mine_ref.refs_0_), channel_id=1, source_target_pairs={{0,1},{1,0},{2,3},{3,2},{4,5},{5,4},{6,7},{7,6},{8,9},{9,8},{10,11... | collective-permute-start | bytes 1376264 | tf_op jit(solution)/shard_map/ppermute | solution.py:627
  61.7 8.5 %collective-permute-start.13 = (bf16[112,2048]{1,0:T(8,128)(2,1)S(1)}, bf16[112,2048]{1,0:T(8,128)(2,1)S(1)}, u32[]{:S(2)}, u32[]{:S(2)}) collective-permute-start(bf16[112,2048]{1,0:T(8,128)(2,1)S(1)} %combine.1.mine_ref.refs_0_), channel_id=1, source_target_pairs={{0,2},{1,5},{2,0},{3,7},{4,6},{5,1},{6,4},{7,3},{8,10},{9,13},{10,... | collective-permute-start | bytes 1376264 | tf_op jit(solution)/shard_map/ppermute | solution.py:637
  70.3 1.8 %collective-permute-start.17 = (bf16[112,2048]{1,0:T(8,128)(2,1)S(1)}, bf16[112,2048]{1,0:T(8,128)(2,1)S(1)}, u32[]{:S(2)}, u32[]{:S(2)}) collective-permute-start(bf16[112,2048]{1,0:T(8,128)(2,1)S(1)} %collective-permute-done.13.mine_ref), channel_id=1, source_target_pairs={{0,1},{1,0},{2,3},{3,2},{4,5},{5,4},{6,7},{7,6},{8,9},{9,8},{10,11... | collective-permute-start | bytes 1376264 | tf_op jit(solution)/shard_map/ppermute | solution.py:627
  70.3 8.5 %collective-permute-start.19 = (bf16[112,2048]{1,0:T(8,128)(2,1)S(1)}, bf16[112,2048]{1,0:T(8,128)(2,1)S(1)}, u32[]{:S(2)}, u32[]{:S(2)}) collective-permute-start(bf16[112,2048]{1,0:T(8,128)(2,1)S(1)} %collective-permute-done.13.mine_ref), channel_id=1, source_target_pairs={{0,4},{1,3},{2,6},{3,1},{4,0},{5,7},{6,2},{7,5},{8,12},{9,11},{10,... | collective-permute-start | bytes 1376264 | tf_op jit(solution)/shard_map/ppermute | solution.py:637
  74.7 4.0 %collective-permute-start.18 = (bf16[112,1024]{1,0:T(8,128)(2,1)S(1)}, bf16[112,1024]{1,0:T(8,128)(2,1)S(1)}, u32[]{:S(2)}, u32[]{:S(2)}) collective-permute-start(bf16[112,1024]{1,0:T(8,128)(2,1)S(1)} %get-tuple-element.91), channel_id=1, source_target_pairs={{0,1},{1,0},{2,3},{3,2},{4,5},{5,4},{6,7},{7,6},{8,9},{9,8},{10,11... | collective-permute-start | bytes 688136 | tf_op jit(solution)/shard_map/ppermute | solution.py:627
  78.7 1.8 %collective-permute-start.20 = (bf16[112,2048]{1,0:T(8,128)(2,1)S(1)}, bf16[112,2048]{1,0:T(8,128)(2,1)S(1)}, u32[]{:S(2)}, u32[]{:S(2)}) collective-permute-start(bf16[112,2048]{1,0:T(8,128)(2,1)S(1)} %collective-permute-done.19.mine_ref), channel_id=1, source_target_pairs={{0,1},{1,0},{2,3},{3,2},{4,5},{5,4},{6,7},{7,6},{8,9},{9,8},{10,11... | collective-permute-start | bytes 1376264 | tf_op jit(solution)/shard_map/ppermute | solution.py:627
  78.7 8.5 %collective-permute-start.22 = (bf16[112,2048]{1,0:T(8,128)(2,1)S(1)}, bf16[112,2048]{1,0:T(8,128)(2,1)S(1)}, u32[]{:S(2)}, u32[]{:S(2)}) collective-permute-start(bf16[112,2048]{1,0:T(8,128)(2,1)S(1)} %combine.1.mine_ref.refs_0_), channel_id=1, source_target_pairs={{0,4},{1,3},{2,6},{3,1},{4,0},{5,7},{6,2},{7,5},{8,12},{9,11},{10,... | collective-permute-start | bytes 1376264 | tf_op jit(solution)/shard_map/ppermute | solution.py:637
  83.2 4.1 %collective-permute-start.21 = (bf16[112,1024]{1,0:T(8,128)(2,1)S(1)}, bf16[112,1024]{1,0:T(8,128)(2,1)S(1)}, u32[]{:S(2)}, u32[]{:S(2)}) collective-permute-start(bf16[112,1024]{1,0:T(8,128)(2,1)S(1)} %get-tuple-element.93), channel_id=1, source_target_pairs={{0,1},{1,0},{2,3},{3,2},{4,5},{5,4},{6,7},{7,6},{8,9},{9,8},{10,11... | collective-permute-start | bytes 688136 | tf_op jit(solution)/shard_map/ppermute | solution.py:627
  83.4 3.8 %collective-permute-start.24 = (bf16[112,1024]{1,0:T(8,128)(2,1)S(1)}, bf16[112,1024]{1,0:T(8,128)(2,1)S(1)}, u32[]{:S(2)}, u32[]{:S(2)}) collective-permute-start(bf16[112,1024]{1,0:T(8,128)(2,1)S(1)} %get-tuple-element.99), channel_id=1, source_target_pairs={{0,1},{1,0},{2,3},{3,2},{4,5},{5,4},{6,7},{7,6},{8,9},{9,8},{10,11... | collective-permute-start | bytes 688136 | tf_op jit(solution)/shard_map/ppermute | solution.py:627
  87.2 1.8 %collective-permute-start.23 = (bf16[112,2048]{1,0:T(8,128)(2,1)S(1)}, bf16[112,2048]{1,0:T(8,128)(2,1)S(1)}, u32[]{:S(2)}, u32[]{:S(2)}) collective-permute-start(bf16[112,2048]{1,0:T(8,128)(2,1)S(1)} %collective-permute-done.22.mine_ref), channel_id=1, source_target_pairs={{0,1},{1,0},{2,3},{3,2},{4,5},{5,4},{6,7},{7,6},{8,9},{9,8},{10,11... | collective-permute-start | bytes 1376264 | tf_op jit(solution)/shard_map/ppermute | solution.py:627
  89.0 8.5 %collective-permute-start.25 = (bf16[112,2048]{1,0:T(8,128)(2,1)S(1)}, bf16[112,2048]{1,0:T(8,128)(2,1)S(1)}, u32[]{:S(2)}, u32[]{:S(2)}) collective-permute-start(bf16[112,2048]{1,0:T(8,128)(2,1)S(1)} %add_convert_fusion.1), channel_id=1, source_target_pairs={{0,4},{1,3},{2,6},{3,1},{4,0},{5,7},{6,2},{7,5},{8,12},{9,11},{10,... | collective-permute-start | bytes 1376264 | tf_op jit(solution)/shard_map/ppermute | solution.py:637
  92.5 1.6 %collective-permute-start.26 = (bf16[112,1024]{1,0:T(8,128)(2,1)S(1)}, bf16[112,1024]{1,0:T(8,128)(2,1)S(1)}, u32[]{:S(2)}, u32[]{:S(2)}) collective-permute-start(bf16[112,1024]{1,0:T(8,128)(2,1)S(1)} %get-tuple-element.103), channel_id=1, source_target_pairs={{0,1},{1,0},{2,3},{3,2},{4,5},{5,4},{6,7},{7,6},{8,9},{9,8},{10,11... | collective-permute-start | bytes 688136 | tf_op jit(solution)/shard_map/ppermute | solution.py:627
  92.6 4.9 %collective-permute-start.27 = (bf16[112,1024]{1,0:T(8,128)(2,1)S(1)}, bf16[112,1024]{1,0:T(8,128)(2,1)S(1)}, u32[]{:S(2)}, u32[]{:S(2)}) collective-permute-start(bf16[112,1024]{1,0:T(8,128)(2,1)S(1)} %get-tuple-element.105), channel_id=1, source_target_pairs={{0,1},{1,0},{2,3},{3,2},{4,5},{5,4},{6,7},{7,6},{8,9},{9,8},{10,11... | collective-permute-start | bytes 688136 | tf_op jit(solution)/shard_map/ppermute | solution.py:627
  93.1 7.8 %collective-permute-start.16 = (bf16[112,1024]{1,0:T(8,128)(2,1)S(1)}, bf16[112,1024]{1,0:T(8,128)(2,1)S(1)}, u32[]{:S(2)}, u32[]{:S(2)}) collective-permute-start(bf16[112,1024]{1,0:T(8,128)(2,1)S(1)} %get-tuple-element.89), channel_id=1, source_target_pairs={{0,1},{1,0},{2,3},{3,2},{4,5},{5,4},{6,7},{7,6},{8,9},{9,8},{10,11... | collective-permute-start | bytes 688136 | tf_op jit(solution)/shard_map/ppermute | solution.py:627
  93.2 7.7 %collective-permute-start.15 = (bf16[112,1024]{1,0:T(8,128)(2,1)S(1)}, bf16[112,1024]{1,0:T(8,128)(2,1)S(1)}, u32[]{:S(2)}, u32[]{:S(2)}) collective-permute-start(bf16[112,1024]{1,0:T(8,128)(2,1)S(1)} %get-tuple-element.88), channel_id=1, source_target_pairs={{0,1},{1,0},{2,3},{3,2},{4,5},{5,4},{6,7},{7,6},{8,9},{9,8},{10,11... | collective-permute-start | bytes 688136 | tf_op jit(solution)/shard_map/ppermute | solution.py:627
  94.1 4.5 %collective-permute-start.30 = (bf16[112,1024]{1,0:T(8,128)(2,1)S(1)}, bf16[112,1024]{1,0:T(8,128)(2,1)S(1)}, u32[]{:S(2)}, u32[]{:S(2)}) collective-permute-start(bf16[112,1024]{1,0:T(8,128)(2,1)S(1)} %get-tuple-element.109), channel_id=1, source_target_pairs={{0,1},{1,0},{2,3},{3,2},{4,5},{5,4},{6,7},{7,6},{8,9},{9,8},{10,11... | collective-permute-start | bytes 688136 | tf_op jit(solution)/shard_map/ppermute | solution.py:627
  97.6 12.6 %collective-permute-start.28 = (bf16[112,2048]{1,0:T(8,128)(2,1)S(1)}, bf16[112,2048]{1,0:T(8,128)(2,1)S(1)}, u32[]{:S(2)}, u32[]{:S(2)}) collective-permute-start(bf16[112,2048]{1,0:T(8,128)(2,1)S(1)} %add_convert_fusion), channel_id=1, source_target_pairs={{0,4},{1,3},{2,6},{3,1},{4,0},{5,7},{6,2},{7,5},{8,12},{9,11},{10,... | collective-permute-start | bytes 1376264 | tf_op jit(solution)/shard_map/ppermute | solution.py:637
  98.8 8.1 %collective-permute-start.29 = (bf16[112,1024]{1,0:T(8,128)(2,1)S(1)}, bf16[112,1024]{1,0:T(8,128)(2,1)S(1)}, u32[]{:S(2)}, u32[]{:S(2)}) collective-permute-start(bf16[112,1024]{1,0:T(8,128)(2,1)S(1)} %get-tuple-element.111), channel_id=1, source_target_pairs={{0,2},{1,5},{2,0},{3,7},{4,6},{5,1},{6,4},{7,3},{8,10},{9,13},{10,... | collective-permute-start | bytes 688136 | tf_op jit(solution)/shard_map/ppermute | solution.py:637
  100.2 9.2 %collective-permute-start.31 = (bf16[112,1024]{1,0:T(8,128)(2,1)S(1)}, bf16[112,1024]{1,0:T(8,128)(2,1)S(1)}, u32[]{:S(2)}, u32[]{:S(2)}) collective-permute-start(bf16[112,1024]{1,0:T(8,128)(2,1)S(1)} %get-tuple-element.110), channel_id=1, source_target_pairs={{0,2},{1,5},{2,0},{3,7},{4,6},{5,1},{6,4},{7,3},{8,10},{9,13},{10,... | collective-permute-start | bytes 688136 | tf_op jit(solution)/shard_map/ppermute | solution.py:637
